TPU v7x, 32 devices: a whole 2x2x4 slice. The times are simulated.
32 devices in a mesh: dev: 32 (over z, y, x, core).
Axes of the slice: x: 2, y: 2, z: 4, core: 2. Of those that a mesh axis runs over, the one named last changes fastest.
Arguments:
- master: float32 [2, 3, 1024, 256], P(None, None, 'dev'), may hold values from -0.18 to 0.18
- first_moment: float32 [2, 3, 1024, 256], P(None, None, 'dev'), may hold values from -2 to 2
- second_moment: float32 [2, 3, 1024, 256], P(None, None, 'dev'), may hold values from 0.05 to 2
- old_rows: bfloat16 [32, 256, 1024], P('dev'), may hold values from -6 to 6
- old_cotangent: bfloat16 [32, 256, 1024], P('dev'), may hold values from -0.08984375 to 0.08984375
- new_rows: bfloat16 [32, 256, 1024], P('dev'), may hold values from -6 to 6
- old_slots: int32 [32], replicated, may hold values from 0 to 1
- new_slots: int32 [32], replicated, may hold values from 0 to 1
- live_rows: int32 [32], P('dev'), may hold values from 64 to 256, as said below
Outputs:
- new_master: float32 [2, 3, 1024, 256], P(None, None, 'dev')
- new_first: float32 [2, 3, 1024, 256], P(None, None, 'dev')
- new_second: float32 [2, 3, 1024, 256], P(None, None, 'dev')
- new_outputs: bfloat16 [32, 256, 1024], P('dev')
Inputs may be any that keep to these rules, and one draw needn't show every extreme that they name: `live_rows`: some slot has all 256 rows live in every draw.
All inputs are finite; a program needn't handle non-finite values.
Results may differ from a plain program's by a relative error of at most 0.0059.
The roundings to bfloat16 on the way count: a program that leaves them out, or rounds other values in their place, can miss the bound.
Values may be sent and summed in bfloat16 or wider, within the bound.
No kernel may reach another device: no remote copies, remote signals or barrier semaphores. Data moves between devices by JAX's collectives and lax.ppermute only.
A program may use at most 64 MiB of HBM per device.

v0:
```python
import jax
import jax.numpy as jnp
from jax import lax
from jax.sharding import PartitionSpec as P

beta_one = 0.9
beta_two = 0.95
corr_one = 0.9999734386011124
corr_two = 0.994079470779666
adam_eps = 1e-08
learn_rate = 0.003
decay_rate = 0.1


def from_partner(block, axis, bit):
    count = lax.axis_size(axis)
    route = []
    for low in range(count):
        high = low | 1 << bit
        if high != low and high < count:
            route += [(low, high), (high, low)]
    return lax.ppermute(block, axis, route)


def hidden_terms(tokens, cotangent, weights, live):
    positions = jnp.arange(tokens.shape[0], dtype=jnp.int32)
    cotangent = jnp.where((positions < live)[:, None], cotangent, jnp.zeros_like(cotangent))
    gate_pre = jnp.dot(tokens, weights[0], preferred_element_type=jnp.float32)
    up_pre = jnp.dot(tokens, weights[1], preferred_element_type=jnp.float32)
    gate_sig = jax.nn.sigmoid(gate_pre)
    gate_act = gate_pre * gate_sig
    hidden = (gate_act * up_pre).astype(jnp.bfloat16)
    grad_down = lax.dot_general(
        cotangent, hidden, (((0,), (0,)), ((), ())), preferred_element_type=jnp.float32
    )
    grad_hidden = jnp.dot(cotangent, weights[2], preferred_element_type=jnp.float32)
    grad_up_pre = (grad_hidden * gate_act).astype(jnp.bfloat16)
    grad_gate_pre = (grad_hidden * up_pre * gate_sig * (1.0 + gate_pre * (1.0 - gate_sig))).astype(
        jnp.bfloat16
    )
    grad_gate = lax.dot_general(
        tokens, grad_gate_pre, (((0,), (0,)), ((), ())), preferred_element_type=jnp.float32
    )
    grad_up = lax.dot_general(
        tokens, grad_up_pre, (((0,), (0,)), ((), ())), preferred_element_type=jnp.float32
    )
    return jnp.stack([grad_gate, grad_up, grad_down])


def adam_update(master, first, second, grad):
    first_new = beta_one * first + (1.0 - beta_one) * grad
    second_new = beta_two * second + (1.0 - beta_two) * grad * grad
    direction = first_new / corr_one / (jnp.sqrt(second_new / corr_two) + adam_eps)
    master_new = master - learn_rate * (direction + decay_rate * master)
    return (master_new, first_new, second_new)


def expert_forward(tokens, weights):
    gate_pre = jnp.dot(tokens, weights[0], preferred_element_type=jnp.float32)
    up_pre = jnp.dot(tokens, weights[1], preferred_element_type=jnp.float32)
    activation = (jax.nn.silu(gate_pre) * up_pre).astype(jnp.bfloat16)
    result = lax.dot_general(
        activation, weights[2], (((1,), (1,)), ((), ())), preferred_element_type=jnp.float32
    )
    return result.astype(jnp.bfloat16)


def halving(buffer, first_step, levels, me_index):
    blocks = buffer.shape[0]
    local_rows = buffer.shape[3]
    block_width = buffer.shape[4]
    for step in range(first_step, levels):
        count = buffer.shape[2]
        halves = buffer.reshape(blocks, 3, count // 2, 2, local_rows, block_width)
        split_axis = 3
        own_bit = me_index >> step & 1
        keeping = lax.dynamic_index_in_dim(halves, own_bit, split_axis, keepdims=False)
        sending = lax.dynamic_index_in_dim(halves, 1 - own_bit, split_axis, keepdims=False)
        buffer = keeping + from_partner(sending, "dev", step)
    return buffer


def on_device(
    master,
    first_moment,
    second_moment,
    old_rows,
    old_cotangent,
    new_rows,
    old_slots,
    new_slots,
    live_rows,
):
    blocks = master.shape[0]
    local_rows = master.shape[2]
    block_width = master.shape[3]
    devices = lax.axis_size("dev")
    levels = devices.bit_length() - 1
    me_index = lax.axis_index("dev")
    own_old = lax.dynamic_index_in_dim(old_slots, me_index, 0, keepdims=False)
    own_new = lax.dynamic_index_in_dim(new_slots, me_index, 0, keepdims=False)
    every_block = lax.all_gather(master.astype(jnp.bfloat16), "dev", axis=2, tiled=True)
    weights = lax.dynamic_index_in_dim(every_block, own_old, 0, keepdims=False)
    slot_grad = hidden_terms(old_rows[0], old_cotangent[0], weights, live_rows[0])
    block_ids = jnp.arange(blocks, dtype=jnp.int32)[:, None, None, None, None]
    dense = slot_grad.reshape(3, devices, local_rows, block_width)
    buffer = jnp.where(block_ids == own_old, dense[None], jnp.zeros((), jnp.float32))
    buffer = halving(buffer, 0, levels, me_index)
    grad = buffer.reshape(blocks, 3, local_rows, block_width)
    new_master, new_first, new_second = adam_update(master, first_moment, second_moment, grad)
    updated_blocks = lax.all_gather(new_master.astype(jnp.bfloat16), "dev", axis=2, tiled=True)
    new_weights = lax.dynamic_index_in_dim(updated_blocks, own_new, 0, keepdims=False)
    new_outputs = expert_forward(new_rows[0], new_weights)[None]
    return (new_master, new_first, new_second, new_outputs)


def solution(mesh):
    return jax.shard_map(
        on_device,
        mesh=mesh,
        in_specs=(
            P(None, None, "dev", None),
            P(None, None, "dev", None),
            P(None, None, "dev", None),
            P("dev", None, None),
            P("dev", None, None),
            P("dev", None, None),
            P(),
            P(),
            P("dev"),
        ),
        out_specs=(
            P(None, None, "dev", None),
            P(None, None, "dev", None),
            P(None, None, "dev", None),
            P("dev", None, None),
        ),
        check_vma=False,
    )
```

profile of v0, /device:TPU:0, one launch (start us, length us, event | category | flops | bytes accessed | tf_op | source)
XLA Modules:
  0.0 247.3 jit_solution(6808849697504979850)
XLA Ops:
  7.2 0.0 copy-start
  7.2 0.0 all-gather.3.cloned.1.call-start
  7.2 1.6 convert_element_type.21
  8.9 0.0 all-gather.3.cloned.1.call-update
  8.9 0.0 all-gather.5.cloned.1.call-start
  8.9 1.2 dynamic_slice.45
  12.1 1.2 copy.36
  14.0 0.7 iota_compare_fusion.1
  14.7 0.8 bitcast_select_fusion
  15.5 57.7 %all-gather.3.cloned.1.call-done = bf16[2,3,1024,256]{3,2,1,0:T(8,128)(2,1)} async-done(((bf16[2,3,32,256]{3,2,1,0:T(8,128)(2,1)}), bf16[2,3,1024,256]{3,2,1,0:T(8,128)(2,1)}) %all-gather.3.cloned.1.call-update) | async-done | bytes 3145744 | tf_op jit(solution)/shard_map/all_gather | solution.py:102
  73.3 1.5 fusion.3
  74.8 0.0 copy-done
  74.8 1.3 convolution_bitcast_fusion.5
  76.2 1.4 convolution_bitcast_fusion.1
  77.5 1.3 convolution_bitcast_fusion.6
  78.9 0.4 convolution_bitcast_fusion.2
  79.3 0.3 copy.34
  79.6 1.6 copy.35
  81.2 1.4 convolution_bitcast_fusion
  82.6 1.0 broadcast_select_fusion
  83.5 0.0 copy-start.1
  83.6 2.4 dynamic-slice_bitcast_fusion
  85.9 1.2 copy-done.1
  87.2 0.3 collective-permute-start
  87.4 5.7 %collective-permute-done = f32[2,3,16,32,256]{4,3,2,1,0:T(8,128)} collective-permute-done((f32[2,3,16,32,256]{4,3,2,1,0:T(8,128)}, f32[2,3,16,32,256]{4,3,2,1,0:T(8,128)}, u32[]{:S(2)}, u32[]{:S(2)}) %collective-permute-start) | collective-permute-done | bytes 3145760 | tf_op jit(solution)/shard_map/ppermute | solution.py:22
  93.2 3.8 %bitcast_add_fusion = f32[2,3,16,32,256]{4,3,2,1,0:T(8,128)S(1)} fusion(f32[2,3,16,32,256]{4,3,2,1,0:T(8,128)} %collective-permute-done, f32[2,3,16,2,32,256]{5,4,2,1,0,3:T(8,128)} %copy-done.1, s32[]{:T(128)S(6)} %select_n.67), kind=kLoop, calls=%fused_computation.1 | loop fusion | flops 786432 | bytes 9437188 | tf_op jit(solution)/shard_map/add | solution.py:79
  97.0 0.0 copy-start.2
  97.0 1.6 copy-done.2
  98.6 0.1 dynamic-slice_bitcast_fusion.1
  98.7 1.5 collective-permute-start.1
  100.2 35.2 %collective-permute-done.1 = f32[2,3,8,32,256]{4,3,2,1,0:T(8,128)} collective-permute-done((f32[2,3,8,32,256]{4,3,2,1,0:T(8,128)S(1)}, f32[2,3,8,32,256]{4,3,2,1,0:T(8,128)}, u32[]{:S(2)}, u32[]{:S(2)}) %collective-permute-start.1) | collective-permute-done | bytes 1572896 | tf_op jit(solution)/shard_map/ppermute | solution.py:22
  135.5 2.1 bitcast_add_fusion.1
  137.6 0.0 copy-start.3
  137.6 0.0 copy-start.5
  137.6 0.0 copy-start.6
  137.6 0.1 dynamic-slice_bitcast_fusion.2
  137.7 1.5 collective-permute-start.2
  139.3 0.0 copy-start.7
  139.3 17.5 %collective-permute-done.2 = f32[2,3,4,32,256]{4,3,2,1,0:T(8,128)} collective-permute-done((f32[2,3,4,32,256]{4,3,2,1,0:T(8,128)S(1)}, f32[2,3,4,32,256]{4,3,2,1,0:T(8,128)}, u32[]{:S(2)}, u32[]{:S(2)}) %collective-permute-start.2) | collective-permute-done | bytes 786464 | tf_op jit(solution)/shard_map/ppermute | solution.py:22
  156.8 1.2 bitcast_add_fusion.2
  158.0 0.0 copy-start.4
  158.1 0.8 collective-permute-start.3
  158.9 8.8 %collective-permute-done.3 = f32[2,3,2,32,256]{4,3,2,1,0:T(8,128)S(1)} collective-permute-done((f32[2,3,2,32,256]{4,3,2,1,0:T(8,128)S(1)}, f32[2,3,2,32,256]{4,3,2,1,0:T(8,128)S(1)}, u32[]{:S(2)}, u32[]{:S(2)}) %collective-permute-start.3) | collective-permute-done | bytes 393248 | tf_op jit(solution)/shard_map/ppermute | solution.py:22
  167.7 0.1 bitcast_add_fusion.3
  167.8 1.1 collective-permute-start.4
  168.8 8.5 %collective-permute-done.4 = f32[2,3,1,32,256]{4,3,2,1,0:T(8,128)S(1)} collective-permute-done((f32[2,3,1,32,256]{4,3,2,1,0:T(8,128)S(1)}, f32[2,3,1,32,256]{4,3,2,1,0:T(8,128)S(1)}, u32[]{:S(2)}, u32[]{:S(2)}) %collective-permute-start.4) | collective-permute-done | bytes 196640 | tf_op jit(solution)/shard_map/ppermute | solution.py:22
  177.4 0.0 copy-done.3
  177.4 0.0 copy-done.5
  177.4 0.0 copy-done.6
  177.4 0.9 fusion.40
  178.3 0.0 all-gather.5.cloned.1.call-update
  178.4 0.0 copy-done.7
  178.4 0.6 dynamic_slice.55
  180.6 55.7 %all-gather.5.cloned.1.call-done = bf16[2,3,1024,256]{3,2,1,0:T(8,128)(2,1)} async-done(((bf16[2,3,32,256]{3,2,1,0:T(8,128)(2,1)}), bf16[2,3,1024,256]{3,2,1,0:T(8,128)(2,1)}) %all-gather.5.cloned.1.call-update) | async-done | bytes 3145744 | tf_op jit(solution)/shard_map/all_gather | solution.py:111
  236.4 0.0 copy-done.4
  236.4 1.3 convolution_bitcast_fusion.4
  237.7 2.7 %fusion = bf16[1,256,1024]{2,1,0:T(8,128)(2,1)} fusion(bf16[2,3,1024,256]{3,2,1,0:T(8,128)(2,1)} %all-gather.5.cloned.1.call-done, s32[]{:T(128)S(6)} %select_n.77, s32[]{:T(128)S(6)} %add.118, s32[]{:T(128)S(6)} %add.119, bf16[1,256,1024]{2,1,0:T(8,128)(2,1)S(1)} %copy-done.4, f32[256,256]{1,0:T(8,128)S(1)} %convolution_bitcast_fusion.4), kind=kOutput, calls=%fused_computation.10 | convolution fusion | flops 269090816 | bytes 2361344 | tf_op jit(solution)/shard_map/dot_general | solution.py:62
  (3 shorter events, 0.1 us)
Async XLA Ops:
  7.2 67.7 %copy-start = (bf16[1,256,1024]{2,1,0:T(8,128)(2,1)S(1)}, bf16[1,256,1024]{2,1,0:T(8,128)(2,1)}, u32[]{:S(2)}) copy-start(bf16[1,256,1024]{2,1,0:T(8,128)(2,1)} %param.12) | copy-start | bytes 1572868
  7.2 66.1 %all-gather.3.cloned.1.call-start = ((), (), s32[]{:S(2)}) async-start(), calls=%async_computation | async-start | bytes 3244032 | tf_op jit(solution)/shard_map/all_gather | solution.py:102
  8.9 227.5 %all-gather.5.cloned.1.call-start = ((), (), s32[]{:S(2)}) async-start(), calls=%async_computation.1 | async-start | bytes 3244032 | tf_op jit(solution)/shard_map/all_gather | solution.py:111
  83.5 3.6 %copy-start.1 = (f32[2,3,16,2,32,256]{5,4,2,1,0,3:T(8,128)}, f32[2,3,16,2,32,256]{5,4,2,1,0,3:T(8,128)S(1)}, u32[]{:S(2)}) copy-start(f32[2,3,16,2,32,256]{5,4,2,1,0,3:T(8,128)S(1)} %broadcast_select_fusion) | copy-start | bytes 18874372
  87.2 6.0 %collective-permute-start = (f32[2,3,16,32,256]{4,3,2,1,0:T(8,128)}, f32[2,3,16,32,256]{4,3,2,1,0:T(8,128)}, u32[]{:S(2)}, u32[]{:S(2)}) collective-permute-start(f32[2,3,16,32,256]{4,3,2,1,0:T(8,128)} %dynamic-slice_bitcast_fusion), channel_id=1, source_target_pairs={{0,1},{1,0},{2,3},{3,2},{4,5},{5,4},{6,7},{7,6},{8,9},{9,8},{10,11... | collective-permute-start | bytes 9437192 | tf_op jit(solution)/shard_map/ppermute | solution.py:22
  97.0 1.6 copy-start.2
  98.7 36.7 %collective-permute-start.1 = (f32[2,3,8,32,256]{4,3,2,1,0:T(8,128)S(1)}, f32[2,3,8,32,256]{4,3,2,1,0:T(8,128)}, u32[]{:S(2)}, u32[]{:S(2)}) collective-permute-start(f32[2,3,8,32,256]{4,3,2,1,0:T(8,128)S(1)} %dynamic-slice_bitcast_fusion.1), channel_id=1, source_target_pairs={{0,2},{2,0},{1,3},{3,1},{4,6},{6,4},{5,7},{7,5},{8,10},{10,8},{9,1... | collective-permute-start | bytes 4718600 | tf_op jit(solution)/shard_map/ppermute | solution.py:22
  137.6 39.8 %copy-start.3 = (f32[2,3,32,256]{3,2,1,0:T(8,128)S(1)}, f32[2,3,32,256]{3,2,1,0:T(8,128)}, u32[]{:S(2)}) copy-start(f32[2,3,32,256]{3,2,1,0:T(8,128)} %param.9) | copy-start | bytes 589828
  137.6 39.8 %copy-start.5 = (f32[2,3,32,256]{3,2,1,0:T(8,128)S(1)}, f32[2,3,32,256]{3,2,1,0:T(8,128)}, u32[]{:S(2)}) copy-start(f32[2,3,32,256]{3,2,1,0:T(8,128)} %param.10) | copy-start | bytes 589828
  137.6 39.7 %copy-start.6 = (f32[2,3,32,256]{3,2,1,0:T(8,128)S(1)}, f32[2,3,32,256]{3,2,1,0:T(8,128)}, u32[]{:S(2)}) copy-start(f32[2,3,32,256]{3,2,1,0:T(8,128)} %param.11) | copy-start | bytes 589828
  137.7 19.1 %collective-permute-start.2 = (f32[2,3,4,32,256]{4,3,2,1,0:T(8,128)S(1)}, f32[2,3,4,32,256]{4,3,2,1,0:T(8,128)}, u32[]{:S(2)}, u32[]{:S(2)}) collective-permute-start(f32[2,3,4,32,256]{4,3,2,1,0:T(8,128)S(1)} %dynamic-slice_bitcast_fusion.2), channel_id=1, source_target_pairs={{0,4},{4,0},{1,5},{5,1},{2,6},{6,2},{3,7},{7,3},{8,12},{12,8},{9,1... | collective-permute-start | bytes 2359304 | tf_op jit(solution)/shard_map/ppermute | solution.py:22
  139.3 39.1 %copy-start.7 = (s32[32]{0:T(128)S(1)}, s32[32]{0:T(128)}, u32[]{:S(2)}) copy-start(s32[32]{0:T(128)} %param.16) | copy-start | bytes 388
  158.0 78.3 %copy-start.4 = (bf16[1,256,1024]{2,1,0:T(8,128)(2,1)S(1)}, bf16[1,256,1024]{2,1,0:T(8,128)(2,1)}, u32[]{:S(2)}) copy-start(bf16[1,256,1024]{2,1,0:T(8,128)(2,1)} %param.14) | copy-start | bytes 1572868
  158.1 9.6 %collective-permute-start.3 = (f32[2,3,2,32,256]{4,3,2,1,0:T(8,128)S(1)}, f32[2,3,2,32,256]{4,3,2,1,0:T(8,128)S(1)}, u32[]{:S(2)}, u32[]{:S(2)}) collective-permute-start(f32[2,3,2,32,256]{4,3,2,1,0:T(8,128)S(1)} %dynamic-slice_bitcast_fusion.16), channel_id=1, source_target_pairs={{0,8},{8,0},{1,9},{9,1},{2,10},{10,2},{3,11},{11,3},{4,12},{12,4},... | collective-permute-start | bytes 1179656 | tf_op jit(solution)/shard_map/ppermute | solution.py:22
  167.8 9.6 %collective-permute-start.4 = (f32[2,3,1,32,256]{4,3,2,1,0:T(8,128)S(1)}, f32[2,3,1,32,256]{4,3,2,1,0:T(8,128)S(1)}, u32[]{:S(2)}, u32[]{:S(2)}) collective-permute-start(f32[2,3,1,32,256]{4,3,2,1,0:T(8,128)S(1)} %constant_dynamic-slice_fusion), channel_id=1, source_target_pairs={{0,16},{16,0},{1,17},{17,1},{2,18},{18,2},{3,19},{19,3},{4,20},{20... | collective-permute-start | bytes 589832 | tf_op jit(solution)/shard_map/ppermute | solution.py:22
Sparse Core Ops, SparseCore 0:
  11.5 61.7 all-gather.2
  178.5 57.8 all-gather.4
where the time goes:
time: 248 us; the launch traced here: 247 us
  waiting for transfers between devices  189 us (76%)
  between operations  18.5 us (7%)
  other arithmetic  12.3 us (5%)
  matrix products  11.4 us (5%)
  local copies, waits for them, and re-layouts  10.5 us (4%)
  starting transfers between devices  5.25 us (2%)
    ppermute x5, waiting for transfers between devices, from_partner(): return lax.ppermute(block, axis, route)  75.8 us
    all_gather x1, waiting for transfers between devices, on_device(): lax.all_gather(master.astype(jnp.bfloat16), 'dev', axis=2, tiled=True)  57.7 us
    all_gather x1, waiting for transfers between devices, on_device(): lax.all_gather(new_master.astype(jnp.bfloat16), 'dev', axis=2, tiled=True)  55.7 us
    add x4, other arithmetic, halving(): buffer = keeping + from_partner(sending, 'dev', step)  7.24 us
    ppermute x5, starting transfers between devices, from_partner(): return lax.ppermute(block, axis, route)  5.17 us
  transfers between devices with their start and end apart: 7, of which 7 were waited for; matrix products, arithmetic and copies ran while one was open for 2% of the time, Pallas kernels for 0%

commit v1 on v0

v1 whole, which is shorter than its diff:
```python
import functools

import jax
import jax.numpy as jnp
from jax import lax
from jax.experimental import pallas as pl
from jax.experimental.pallas import tpu as pltpu
from jax.sharding import PartitionSpec as P

beta_one = 0.9
beta_two = 0.95
corr_one = 0.9999734386011124
corr_two = 0.994079470779666
adam_eps = 1e-08
learn_rate = 0.003
decay_rate = 0.1

CORE, X_STEP, Y_STEP, Z_UNIT = 1, 2, 4, 8
VMEM_LIMIT = 48 * 1024 * 1024


def hop(block, mask):
    count = lax.axis_size("dev")
    return lax.ppermute(block, "dev", [(low, low ^ mask) for low in range(count)])


def adam_update(master, first, second, grad):
    first_new = beta_one * first + (1.0 - beta_one) * grad
    second_new = beta_two * second + (1.0 - beta_two) * grad * grad
    direction = first_new / corr_one / (jnp.sqrt(second_new / corr_two) + adam_eps)
    master_new = master - learn_rate * (direction + decay_rate * master)
    return (master_new, first_new, second_new)


def place_pieces(chip, pieces, weights, sems):
    rows = pieces[0].shape[1]
    copies = []
    for j, piece in enumerate(pieces):
        start = pl.multiple_of(lax.bitwise_xor(chip, j) * rows, rows)
        copies.append(pltpu.make_async_copy(piece, weights.at[:, pl.ds(start, rows), :], sems.at[j]))
    for copy in copies:
        copy.start()
    for copy in copies:
        copy.wait()


def transpose_kernel(chip_ref, own_ref, other_ref, out_ref):
    chip = chip_ref[0]
    tokens, width = own_ref.shape
    count = chip_ref.shape[0] - 1
    rows = width // count
    lanes = max(128, rows)
    for part, ref in enumerate((own_ref, other_ref)):
        for at in range(0, width, lanes):
            turned = ref[:, at : at + lanes].T
            for low in range(0, lanes, rows):
                j = lax.bitwise_xor(chip, (at + low) // rows)
                start = pl.multiple_of(j * rows, rows)
                out_ref[pl.ds(start, rows), part * tokens : (part + 1) * tokens] = turned[low : low + rows]


def backward_kernel(count, chip_ref, *refs):
    pieces = refs[:count]
    own_x, other_x, own_c, other_c, x_turned, c_turned = refs[count : count + 6]
    outs = refs[count + 6 : 2 * count + 6]
    weights, gate_grad, up_grad, hidden_all, sems = refs[2 * count + 6 :]
    place_pieces(chip_ref[0], pieces, weights, sems)
    tokens = own_x.shape[0]
    for part, (x_ref, c_ref) in enumerate(((own_x, own_c), (other_x, other_c))):
        span = slice(part * tokens, (part + 1) * tokens)
        gate_pre = jnp.dot(x_ref[...], weights[0], preferred_element_type=jnp.float32)
        up_pre = jnp.dot(x_ref[...], weights[1], preferred_element_type=jnp.float32)
        grad_hidden = jnp.dot(c_ref[...], weights[2], preferred_element_type=jnp.float32)
        gate_sig = jax.nn.sigmoid(gate_pre)
        gate_act = gate_pre * gate_sig
        hidden_all[span] = (gate_act * up_pre).astype(jnp.bfloat16)
        up_grad[span] = (grad_hidden * gate_act).astype(jnp.bfloat16)
        gate_grad[span] = (grad_hidden * up_pre * gate_sig * (1.0 + gate_pre * (1.0 - gate_sig))).astype(
            jnp.bfloat16
        )
    rows = outs[0].shape[1]
    width = count * rows
    tall = min(width, 256)
    for at in range(0, width, tall):
        for kind, (left, right) in enumerate(
            ((x_turned, gate_grad), (x_turned, up_grad), (c_turned, hidden_all))
        ):
            product = jnp.dot(left[at : at + tall], right[...], preferred_element_type=jnp.float32)
            product = product.astype(jnp.bfloat16)
            for low in range(0, tall, rows):
                outs[(at + low) // rows][kind] = product[low : low + rows]


def forward_kernel(count, chip_ref, *refs):
    pieces = refs[:count]
    own_y, other_y, own_out, other_out, weights, sems = refs[count:]
    place_pieces(chip_ref[0], pieces, weights, sems)
    for y_ref, out_ref in ((other_y, other_out), (own_y, own_out)):
        gate_pre = jnp.dot(y_ref[...], weights[0], preferred_element_type=jnp.float32)
        up_pre = jnp.dot(y_ref[...], weights[1], preferred_element_type=jnp.float32)
        act = (gate_pre * jax.nn.sigmoid(gate_pre) * up_pre).astype(jnp.bfloat16)
        result = lax.dot_general(act, weights[2], (((1,), (1,)), ((), ())), preferred_element_type=jnp.float32)
        out_ref[...] = result.astype(jnp.bfloat16)


VMEM = pl.BlockSpec(memory_space=pltpu.VMEM)
SMEM = pl.BlockSpec(memory_space=pltpu.SMEM)
ANY = pl.BlockSpec(memory_space=pl.ANY)


def params():
    return pltpu.CompilerParams(vmem_limit_bytes=VMEM_LIMIT)


def transposed(chip_ids, own, other):
    tokens, width = own.shape
    return pl.pallas_call(
        transpose_kernel,
        out_shape=jax.ShapeDtypeStruct((width, 2 * tokens), own.dtype),
        in_specs=[SMEM, VMEM, VMEM],
        out_specs=VMEM,
        compiler_params=params(),
        cost_estimate=pl.CostEstimate(flops=0, bytes_accessed=8 * tokens * width, transcendentals=0),
        name="transpose_rows",
    )(chip_ids, own, other)


def backward(chip_ids, pieces, own_x, other_x, own_c, other_c, x_turned, c_turned):
    count = len(pieces)
    kinds, rows, units = pieces[0].shape
    tokens, width = own_x.shape
    return pl.pallas_call(
        functools.partial(backward_kernel, count),
        out_shape=[jax.ShapeDtypeStruct((kinds, rows, units), jnp.bfloat16)] * count,
        in_specs=[SMEM] + [ANY] * count + [VMEM] * 6,
        out_specs=[VMEM] * count,
        scratch_shapes=[
            pltpu.VMEM((kinds, width, units), jnp.bfloat16),
            pltpu.VMEM((2 * tokens, units), jnp.bfloat16),
            pltpu.VMEM((2 * tokens, units), jnp.bfloat16),
            pltpu.VMEM((2 * tokens, units), jnp.bfloat16),
            pltpu.SemaphoreType.DMA((count,)),
        ],
        compiler_params=params(),
        cost_estimate=pl.CostEstimate(
            flops=24 * tokens * width * units,
            bytes_accessed=16 * tokens * width + 12 * width * units,
            transcendentals=2 * tokens * units,
        ),
        name="slot_gradients",
    )(chip_ids, *pieces, own_x, other_x, own_c, other_c, x_turned, c_turned)


def forward(chip_ids, pieces, own_y, other_y):
    count = len(pieces)
    kinds, rows, units = pieces[0].shape
    tokens, width = own_y.shape
    return pl.pallas_call(
        functools.partial(forward_kernel, count),
        out_shape=[jax.ShapeDtypeStruct((tokens, width), jnp.bfloat16)] * 2,
        in_specs=[SMEM] + [ANY] * count + [VMEM] * 2,
        out_specs=[VMEM] * 2,
        scratch_shapes=[
            pltpu.VMEM((kinds, width, units), jnp.bfloat16),
            pltpu.SemaphoreType.DMA((count,)),
        ],
        compiler_params=params(),
        cost_estimate=pl.CostEstimate(
            flops=12 * tokens * width * units,
            bytes_accessed=8 * tokens * width + 6 * width * units,
            transcendentals=2 * tokens * units,
        ),
        name="expert_outputs",
    )(chip_ids, *pieces, own_y, other_y)


def gather_chips(piece):
    depth = lax.axis_size("dev") // Z_UNIT
    column = [piece] + [hop(piece, zj * Z_UNIT) for zj in range(1, depth)]
    pieces = []
    for zj, here in enumerate(column):
        along_x = hop(here, X_STEP)
        along_y = hop(here, Y_STEP)
        across = hop(along_x, Y_STEP) if 2 * zj < depth else hop(along_y, X_STEP)
        pieces += [here, along_x, along_y, across]
    return pieces


def add_pair(one, two):
    return (one.astype(jnp.float32) + two.astype(jnp.float32)).astype(jnp.bfloat16)


def reduce_chips(pieces):
    depth = lax.axis_size("dev") // Z_UNIT
    total = None
    for zj in reversed(range(depth)):
        here, along_x, along_y, across = pieces[4 * zj : 4 * zj + 4]
        if 2 * zj < depth:
            along_y = add_pair(along_y, hop(across, X_STEP))
        else:
            along_x = add_pair(along_x, hop(across, Y_STEP))
        column = (
            here.astype(jnp.float32)
            + hop(along_x, X_STEP).astype(jnp.float32)
            + hop(along_y, Y_STEP).astype(jnp.float32)
        )
        if zj:
            column = hop(column.astype(jnp.bfloat16), zj * Z_UNIT).astype(jnp.float32)
        total = column if total is None else total + column
    return total


def block_a_core(master, first, second, old_rows, old_cotangent, new_rows, own_old, own_new, live):
    local_rows = master.shape[2]
    me_index = lax.axis_index("dev")
    core = me_index & CORE
    chips = lax.axis_size("dev") // 2
    chip_ids = jnp.full((chips + 1,), me_index // 2, jnp.int32)

    def mine(state):
        return lax.dynamic_index_in_dim(state, core, 0, keepdims=False)

    def partners(state):
        return lax.dynamic_index_in_dim(state, 1 - core, 0, keepdims=False)

    def both_rows(own, other):
        return jnp.where(
            core == 0, jnp.concatenate([own, other], axis=-2), jnp.concatenate([other, own], axis=-2)
        )

    master_two = both_rows(mine(master), hop(partners(master), CORE))
    pieces = gather_chips(master_two.astype(jnp.bfloat16))

    positions = jnp.arange(old_rows.shape[0], dtype=jnp.int32)[:, None]
    alive = positions < live
    empty = jnp.zeros_like(old_cotangent)
    own_c = jnp.where(alive & (own_old == core), old_cotangent, empty)
    other_c = hop(jnp.where(alive & (own_old != core), old_cotangent, empty), CORE)
    other_x = hop(old_rows, CORE)
    other_y = hop(new_rows, CORE)
    moments = jnp.stack([first, second], axis=1)
    first_two, second_two = both_rows(mine(moments), hop(partners(moments), CORE))

    x_turned = transposed(chip_ids, old_rows, other_x)
    c_turned = transposed(chip_ids, own_c, other_c)
    grads = backward(chip_ids, pieces, old_rows, other_x, own_c, other_c, x_turned, c_turned)
    grad = reduce_chips(grads)
    updated = adam_update(master_two, first_two, second_two, grad)

    new_pieces = gather_chips(updated[0].astype(jnp.bfloat16))
    updated = jnp.stack(updated)
    own_part = lax.dynamic_slice_in_dim(updated, core * local_rows, local_rows, 2)
    other_part = lax.dynamic_slice_in_dim(updated, (1 - core) * local_rows, local_rows, 2)
    from_other = hop(other_part, CORE)
    state = jnp.where(
        core == 0, jnp.stack([own_part, from_other], axis=1), jnp.stack([from_other, own_part], axis=1)
    )
    own_out, other_out = forward(chip_ids, new_pieces, new_rows, other_y)
    new_outputs = jnp.where(own_new == core, own_out, hop(other_out, CORE))
    return (state[0], state[1], state[2], new_outputs[None])


def hidden_terms(tokens, cotangent, weights, live):
    positions = jnp.arange(tokens.shape[0], dtype=jnp.int32)
    cotangent = jnp.where((positions < live)[:, None], cotangent, jnp.zeros_like(cotangent))
    gate_pre = jnp.dot(tokens, weights[0], preferred_element_type=jnp.float32)
    up_pre = jnp.dot(tokens, weights[1], preferred_element_type=jnp.float32)
    gate_sig = jax.nn.sigmoid(gate_pre)
    gate_act = gate_pre * gate_sig
    hidden = (gate_act * up_pre).astype(jnp.bfloat16)
    grad_down = lax.dot_general(
        cotangent, hidden, (((0,), (0,)), ((), ())), preferred_element_type=jnp.float32
    )
    grad_hidden = jnp.dot(cotangent, weights[2], preferred_element_type=jnp.float32)
    grad_up_pre = (grad_hidden * gate_act).astype(jnp.bfloat16)
    grad_gate_pre = (grad_hidden * up_pre * gate_sig * (1.0 + gate_pre * (1.0 - gate_sig))).astype(
        jnp.bfloat16
    )
    grad_gate = lax.dot_general(
        tokens, grad_gate_pre, (((0,), (0,)), ((), ())), preferred_element_type=jnp.float32
    )
    grad_up = lax.dot_general(
        tokens, grad_up_pre, (((0,), (0,)), ((), ())), preferred_element_type=jnp.float32
    )
    return jnp.stack([grad_gate, grad_up, grad_down])


def expert_forward(tokens, weights):
    gate_pre = jnp.dot(tokens, weights[0], preferred_element_type=jnp.float32)
    up_pre = jnp.dot(tokens, weights[1], preferred_element_type=jnp.float32)
    activation = (jax.nn.silu(gate_pre) * up_pre).astype(jnp.bfloat16)
    result = lax.dot_general(
        activation, weights[2], (((1,), (1,)), ((), ())), preferred_element_type=jnp.float32
    )
    return result.astype(jnp.bfloat16)


def halving(buffer, levels, me_index):
    for step in range(levels):
        count = buffer.shape[2]
        halves = buffer.reshape(buffer.shape[:2] + (count // 2, 2) + buffer.shape[3:])
        own_bit = me_index >> step & 1
        keeping = lax.dynamic_index_in_dim(halves, own_bit, 3, keepdims=False)
        sending = lax.dynamic_index_in_dim(halves, 1 - own_bit, 3, keepdims=False)
        buffer = keeping + hop(sending, 1 << step)
    return buffer


def any_shape(master, first, second, old_rows, old_cotangent, new_rows, own_old, own_new, live):
    blocks, kinds, local_rows, block_width = master.shape
    devices = lax.axis_size("dev")
    me_index = lax.axis_index("dev")
    every_block = lax.all_gather(master.astype(jnp.bfloat16), "dev", axis=2, tiled=True)
    weights = lax.dynamic_index_in_dim(every_block, own_old, 0, keepdims=False)
    slot_grad = hidden_terms(old_rows, old_cotangent, weights, live)
    block_ids = jnp.arange(blocks, dtype=jnp.int32)[:, None, None, None, None]
    dense = slot_grad.reshape(kinds, devices, local_rows, block_width)
    buffer = jnp.where(block_ids == own_old, dense[None], jnp.zeros((), jnp.float32))
    buffer = halving(buffer, devices.bit_length() - 1, me_index)
    grad = buffer.reshape(master.shape)
    new_master, new_first, new_second = adam_update(master, first, second, grad)
    updated_blocks = lax.all_gather(new_master.astype(jnp.bfloat16), "dev", axis=2, tiled=True)
    new_weights = lax.dynamic_index_in_dim(updated_blocks, own_new, 0, keepdims=False)
    return (new_master, new_first, new_second, expert_forward(new_rows, new_weights)[None])


def on_device(
    master,
    first_moment,
    second_moment,
    old_rows,
    old_cotangent,
    new_rows,
    old_slots,
    new_slots,
    live_rows,
):
    blocks, kinds, local_rows, units = master.shape
    devices = lax.axis_size("dev")
    me_index = lax.axis_index("dev")
    own_old = lax.dynamic_index_in_dim(old_slots, me_index, 0, keepdims=False)
    own_new = lax.dynamic_index_in_dim(new_slots, me_index, 0, keepdims=False)
    whole_tiles = local_rows % 16 == 0 and units % 128 == 0 and old_rows.shape[1] % 128 == 0
    form = block_a_core if blocks == 2 and devices % Z_UNIT == 0 and whole_tiles else any_shape
    return form(
        master,
        first_moment,
        second_moment,
        old_rows[0],
        old_cotangent[0],
        new_rows[0],
        own_old,
        own_new,
        live_rows[0],
    )


def solution(mesh):
    return jax.shard_map(
        on_device,
        mesh=mesh,
        in_specs=(
            P(None, None, "dev", None),
            P(None, None, "dev", None),
            P(None, None, "dev", None),
            P("dev", None, None),
            P("dev", None, None),
            P("dev", None, None),
            P(),
            P(),
            P("dev"),
        ),
        out_specs=(
            P(None, None, "dev", None),
            P(None, None, "dev", None),
            P(None, None, "dev", None),
            P("dev", None, None),
        ),
        check_vma=False,
    )
```

time: 248 us -> 132 us (0.53)
  waiting for transfers between devices: 189 us -> 46.1 us
  starting transfers between devices: 5.25 us -> 54 us
  between operations: 18.5 us -> 3.78 us
  matrix products: 11.4 us -> 0 us
  Pallas kernels: 0 us -> 10.2 us
  other arithmetic: 12.3 us -> 4.64 us
    all_gather x2 -> x0, waiting for transfers between devices: 113 us -> none  [the longest x1 57.7 us: on_device(): lax.all_gather(master.astype(jnp.bfloat16), 'dev', axis=2, tiled=True)]
    ppermute x5 -> x52, starting transfers between devices: 5.17 us -> 54 us  [hop(): lax.ppermute(block, 'dev', [(low, low ^ mask) for low in range(count)])]
    ppermute x5 -> x52, waiting for transfers between devices: 75.8 us -> 46.1 us  [hop(): lax.ppermute(block, 'dev', [(low, low ^ mask) for low in range(count)])]
    dot_general x8 -> x0, matrix products: 11.4 us -> none  [the longest x1 2.74 us: expert_forward(): lax.dot_general(activation, weights[2], (((1,), (1,)), ((), ())), preferr...]
    pallas_call x0 -> x4, Pallas kernels: none -> 10.2 us  [the longest x1 5.85 us: backward(): pl.pallas_call(functools.partial(backward_kernel, count), out_shape=[jax....]
    add x4 -> x0, other arithmetic: 7.24 us -> none  [halving(): buffer = keeping + from_partner(sending, 'dev', step)]
    unnamed x17 -> x78, local copies, waits for them, and re-layouts: 4.17 us -> 9.33 us
  transfers between devices with their start and end apart: 7 -> 52, of which waited for: 7 -> 19; matrix products, arithmetic and copies ran while one was open for 2% -> 4% of each run, Pallas kernels for 0% -> 3%
where the time goes in v1:
time: 132 us; the launch traced here: 131 us
  starting transfers between devices  54 us (41%)
  waiting for transfers between devices  46.1 us (35%)
  local copies, waits for them, and re-layouts  12.3 us (9%)
  Pallas kernels  10.2 us (8%)
  other arithmetic  4.64 us (4%)
  between operations  3.78 us (3%)
    ppermute x52, starting transfers between devices, hop(): lax.ppermute(block, 'dev', [(low, low ^ mask) for low in range(count)])  54 us
    ppermute x52, waiting for transfers between devices, hop(): lax.ppermute(block, 'dev', [(low, low ^ mask) for low in range(count)])  46.1 us
    unnamed x78, local copies, waits for them, and re-layouts  9.33 us
    pallas_call x1, Pallas kernels, backward(): pl.pallas_call(functools.partial(backward_kernel, count), out_shape=[jax....  5.85 us
    pallas_call x1, Pallas kernels, forward(): pl.pallas_call(functools.partial(forward_kernel, count), out_shape=[jax.S...  2.66 us
  transfers between devices with their start and end apart: 52, of which 19 were waited for; matrix products, arithmetic and copies ran while one was open for 4% of the time, Pallas kernels for 3%

profile of v1, /device:TPU:0, one launch (start us, length us, event | category | flops | bytes accessed | tf_op | source)
XLA Modules:
  0.0 131.1 jit_solution(4758512018435781828)
XLA Ops:
  0.6 1.0 dynamic-slice_bitcast_fusion.1
  5.3 2.0 %bitcast_select_fusion = (bf16[256,1024]{1,0:T(8,128)(2,1)}, bf16[256,1024]{1,0:T(8,128)(2,1)S(1)}) fusion(bf16[1,256,1024]{2,1,0:T(8,128)(2,1)} %param.13, pred[256]{0:T(512)(128)(4,1)S(1)} %get-tuple-element.56, pred[256]{0:T(512)(128)(4,1)S(1)} %get-tuple-element.57), kind=kLoop, calls=%fused_computation.2 | loop fusion | flops 524288 | bytes 1573376 | tf_op jit(solution)/shard_map/jit(_where)/select_n | solution.py:238
  8.5 3.6 %collective-permute-start.9 = (bf16[3,64,256]{2,1,0:T(8,128)(2,1)S(1)}, bf16[3,64,256]{2,1,0:T(8,128)(2,1)S(1)}, u32[]{:S(2)}, u32[]{:S(2)}) collective-permute-start(bf16[3,64,256]{2,1,0:T(8,128)(2,1)S(1)} %fusion.8.refs_0_), channel_id=1, source_target_pairs={{0,16},{1,17},{2,18},{3,19},{4,20},{5,21},{6,22},{7,23},{8,24},{9,... | collective-permute-start | bytes 294920 | tf_op jit(solution)/shard_map/ppermute | solution.py:24
  12.1 1.3 %collective-permute-start.13 = (bf16[3,64,256]{2,1,0:T(8,128)(2,1)S(1)}, bf16[3,64,256]{2,1,0:T(8,128)(2,1)S(1)}, u32[]{:S(2)}, u32[]{:S(2)}) collective-permute-start(bf16[3,64,256]{2,1,0:T(8,128)(2,1)S(1)} %fusion.8.refs_0_), channel_id=1, source_target_pairs={{0,24},{1,25},{2,26},{3,27},{4,28},{5,29},{6,30},{7,31},{8,16},{9,... | collective-permute-start | bytes 294920 | tf_op jit(solution)/shard_map/ppermute | solution.py:24
  13.7 6.3 %collective-permute-done.9.refs_8_ = bf16[3,64,256]{2,1,0:T(8,128)(2,1)S(1)} collective-permute-done((bf16[3,64,256]{2,1,0:T(8,128)(2,1)S(1)}, bf16[3,64,256]{2,1,0:T(8,128)(2,1)S(1)}, u32[]{:S(2)}, u32[]{:S(2)}) %collective-permute-start.9) | collective-permute-done | bytes 98336 | tf_op jit(solution)/shard_map/ppermute | solution.py:24
  20.0 1.7 %collective-permute-start.2 = (bf16[3,64,256]{2,1,0:T(8,128)(2,1)S(1)}, bf16[3,64,256]{2,1,0:T(8,128)(2,1)S(1)}, u32[]{:S(2)}, u32[]{:S(2)}) collective-permute-start(bf16[3,64,256]{2,1,0:T(8,128)(2,1)S(1)} %fusion.8.refs_0_), channel_id=1, source_target_pairs={{0,2},{1,3},{2,0},{3,1},{4,6},{5,7},{6,4},{7,5},{8,10},{9,11},{10,... | collective-permute-start | bytes 294920 | tf_op jit(solution)/shard_map/ppermute | solution.py:24
  21.8 1.5 %collective-permute-start.3 = (bf16[3,64,256]{2,1,0:T(8,128)(2,1)S(1)}, bf16[3,64,256]{2,1,0:T(8,128)(2,1)S(1)}, u32[]{:S(2)}, u32[]{:S(2)}) collective-permute-start(bf16[3,64,256]{2,1,0:T(8,128)(2,1)S(1)} %fusion.8.refs_0_), channel_id=1, source_target_pairs={{0,4},{1,5},{2,6},{3,7},{4,0},{5,1},{6,2},{7,3},{8,12},{9,13},{10,... | collective-permute-start | bytes 294920 | tf_op jit(solution)/shard_map/ppermute | solution.py:24
  23.8 0.8 collective-permute-done.2.refs_1_
  24.6 1.8 %collective-permute-start.15 = (bf16[3,64,256]{2,1,0:T(8,128)(2,1)S(1)}, bf16[3,64,256]{2,1,0:T(8,128)(2,1)S(1)}, u32[]{:S(2)}, u32[]{:S(2)}) collective-permute-start(bf16[3,64,256]{2,1,0:T(8,128)(2,1)S(1)} %collective-permute-done.13.refs_12_), channel_id=1, source_target_pairs={{0,4},{1,5},{2,6},{3,7},{4,0},{5,1},{6,2},{7,3},{8,12},{9,13},{10,... | collective-permute-start | bytes 294920 | tf_op jit(solution)/shard_map/ppermute | solution.py:24
  26.4 1.0 collective-permute-done.3.refs_2_
  27.9 0.9 collective-permute-done.11.refs_10_
  29.8 1.2 collective-permute-start.14
  31.0 1.9 %collective-permute-done.6.refs_5_ = bf16[3,64,256]{2,1,0:T(8,128)(2,1)S(1)} collective-permute-done((bf16[3,64,256]{2,1,0:T(8,128)(2,1)S(1)}, bf16[3,64,256]{2,1,0:T(8,128)(2,1)S(1)}, u32[]{:S(2)}, u32[]{:S(2)}) %collective-permute-start.6) | collective-permute-done | bytes 98336 | tf_op jit(solution)/shard_map/ppermute | solution.py:24
  32.9 1.2 collective-permute-start.7
  34.1 1.0 collective-permute-start.4
  35.7 1.4 %collective-permute-start.16 = (bf16[3,64,256]{2,1,0:T(8,128)(2,1)S(1)}, bf16[3,64,256]{2,1,0:T(8,128)(2,1)}, u32[]{:S(2)}, u32[]{:S(2)}) collective-permute-start(bf16[3,64,256]{2,1,0:T(8,128)(2,1)S(1)} %collective-permute-done.15.refs_14_), channel_id=1, source_target_pairs={{0,2},{1,3},{2,0},{3,1},{4,6},{5,7},{6,4},{7,5},{8,10},{9,11},{10,... | collective-permute-start | bytes 294920 | tf_op jit(solution)/shard_map/ppermute | solution.py:24
  37.1 1.0 collective-permute-start.8
  38.2 0.9 transpose_rows.2.refs_20_
  39.1 0.9 copy-done
  40.1 0.9 transpose_rows.3.refs_21_
  41.0 1.0 copy-done.1
  44.0 0.9 copy-done.21
  44.9 0.9 copy-done.25
  45.8 0.9 copy-done.27
  46.7 5.9 %slot_gradients.1 = (bf16[3,64,256]{2,1,0:T(8,128)(2,1)S(1)}, bf16[3,64,256]{2,1,0:T(8,128)(2,1)S(1)}, bf16[3,64,256]{2,1,0:T(8,128)(2,1)S(1)}, bf16[3,64,256]{2...) custom-call(s32[17]{0:T(128)S(1)} %broadcast_in_dim.23.chip_ref, ...), custom_call_target="tpu_custom_call" | custom-call | flops 1610612736 | bytes 7340032 | tf_op jit(solution)/shard_map/slot_gradients/pallas_call | solution.py:132
  52.6 1.0 collective-permute-start.19
  54.3 1.1 collective-permute-start.21
  55.4 1.0 collective-permute-start.23
  56.3 1.5 %collective-permute-done.19 = bf16[3,64,256]{2,1,0:T(8,128)(2,1)S(1)} collective-permute-done((bf16[3,64,256]{2,1,0:T(8,128)(2,1)}, bf16[3,64,256]{2,1,0:T(8,128)(2,1)S(1)}, u32[]{:S(2)}, u32[]{:S(2)}) %collective-permute-start.19) | collective-permute-done | bytes 98336 | tf_op jit(solution)/shard_map/ppermute | solution.py:24
  57.8 0.9 collective-permute-start.25
  58.7 3.6 %collective-permute-done.23 = bf16[3,64,256]{2,1,0:T(8,128)(2,1)S(1)} collective-permute-done((bf16[3,64,256]{2,1,0:T(8,128)(2,1)}, bf16[3,64,256]{2,1,0:T(8,128)(2,1)S(1)}, u32[]{:S(2)}, u32[]{:S(2)}) %collective-permute-start.23) | collective-permute-done | bytes 98336 | tf_op jit(solution)/shard_map/ppermute | solution.py:24
  63.1 3.8 %collective-permute-done.28 = bf16[3,64,256]{2,1,0:T(8,128)(2,1)S(1)} collective-permute-done((bf16[3,64,256]{2,1,0:T(8,128)(2,1)S(1)}, bf16[3,64,256]{2,1,0:T(8,128)(2,1)S(1)}, u32[]{:S(2)}, u32[]{:S(2)}) %collective-permute-start.28) | collective-permute-done | bytes 98336 | tf_op jit(solution)/shard_map/ppermute | solution.py:24
  67.7 4.5 %collective-permute-done.32 = bf16[3,64,256]{2,1,0:T(8,128)(2,1)S(1)} collective-permute-done((bf16[3,64,256]{2,1,0:T(8,128)(2,1)S(1)}, bf16[3,64,256]{2,1,0:T(8,128)(2,1)S(1)}, u32[]{:S(2)}, u32[]{:S(2)}) %collective-permute-start.32) | collective-permute-done | bytes 98336 | tf_op jit(solution)/shard_map/ppermute | solution.py:24
  72.8 0.9 copy-done.5
  73.6 1.6 %collective-permute-start.27 = (bf16[3,64,256]{2,1,0:T(8,128)(2,1)S(1)}, bf16[3,64,256]{2,1,0:T(8,128)(2,1)S(1)}, u32[]{:S(2)}, u32[]{:S(2)}) collective-permute-start(bf16[3,64,256]{2,1,0:T(8,128)(2,1)S(1)} %copy-done.5), channel_id=1, source_target_pairs={{0,2},{1,3},{2,0},{3,1},{4,6},{5,7},{6,4},{7,5},{8,10},{9,11},{10,... | collective-permute-start | bytes 294920 | tf_op jit(solution)/shard_map/ppermute | solution.py:24
  75.2 2.7 %collective-permute-done.20 = bf16[3,64,256]{2,1,0:T(8,128)(2,1)S(1)} collective-permute-done((bf16[3,64,256]{2,1,0:T(8,128)(2,1)S(1)}, bf16[3,64,256]{2,1,0:T(8,128)(2,1)S(1)}, u32[]{:S(2)}, u32[]{:S(2)}) %collective-permute-start.20) | collective-permute-done | bytes 98336 | tf_op jit(solution)/shard_map/ppermute | solution.py:24
  78.4 1.7 %collective-permute-start.31 = (bf16[3,64,256]{2,1,0:T(8,128)(2,1)S(1)}, bf16[3,64,256]{2,1,0:T(8,128)(2,1)S(1)}, u32[]{:S(2)}, u32[]{:S(2)}) collective-permute-start(bf16[3,64,256]{2,1,0:T(8,128)(2,1)S(1)} %get-tuple-element.35), channel_id=1, source_target_pairs={{0,2},{1,3},{2,0},{3,1},{4,6},{5,7},{6,4},{7,5},{8,10},{9,11},{10,... | collective-permute-start | bytes 294920 | tf_op jit(solution)/shard_map/ppermute | solution.py:24
  80.1 2.5 %collective-permute-done.24 = bf16[3,64,256]{2,1,0:T(8,128)(2,1)S(1)} collective-permute-done((bf16[3,64,256]{2,1,0:T(8,128)(2,1)S(1)}, bf16[3,64,256]{2,1,0:T(8,128)(2,1)S(1)}, u32[]{:S(2)}, u32[]{:S(2)}) %collective-permute-start.24) | collective-permute-done | bytes 98336 | tf_op jit(solution)/shard_map/ppermute | solution.py:24
  82.5 1.2 collective-permute-start.29
  83.8 0.9 collective-permute-start.33
  84.7 2.5 %collective-permute-done.29 = bf16[3,64,256]{2,1,0:T(8,128)(2,1)S(1)} collective-permute-done((bf16[3,64,256]{2,1,0:T(8,128)(2,1)S(1)}, bf16[3,64,256]{2,1,0:T(8,128)(2,1)S(1)}, u32[]{:S(2)}, u32[]{:S(2)}) %collective-permute-start.29) | collective-permute-done | bytes 98336 | tf_op jit(solution)/shard_map/ppermute | solution.py:24
  87.2 3.8 %collective-permute-start.22 = (bf16[3,64,256]{2,1,0:T(8,128)(2,1)S(1)}, bf16[3,64,256]{2,1,0:T(8,128)(2,1)S(1)}, u32[]{:S(2)}, u32[]{:S(2)}) collective-permute-start(bf16[3,64,256]{2,1,0:T(8,128)(2,1)S(1)} %add_convert_fusion.5), channel_id=1, source_target_pairs={{0,24},{1,25},{2,26},{3,27},{4,28},{5,29},{6,30},{7,31},{8,16},{9,... | collective-permute-start | bytes 294920 | tf_op jit(solution)/shard_map/ppermute | solution.py:24
  91.8 2.9 %collective-permute-done.22 = bf16[3,64,256]{2,1,0:T(8,128)(2,1)S(1)} collective-permute-done((bf16[3,64,256]{2,1,0:T(8,128)(2,1)S(1)}, bf16[3,64,256]{2,1,0:T(8,128)(2,1)S(1)}, u32[]{:S(2)}, u32[]{:S(2)}) %collective-permute-start.22) | collective-permute-done | bytes 98336 | tf_op jit(solution)/shard_map/ppermute | solution.py:24
  94.7 6.0 %collective-permute-done.26 = bf16[3,64,256]{2,1,0:T(8,128)(2,1)S(1)} collective-permute-done((bf16[3,64,256]{2,1,0:T(8,128)(2,1)S(1)}, bf16[3,64,256]{2,1,0:T(8,128)(2,1)S(1)}, u32[]{:S(2)}, u32[]{:S(2)}) %collective-permute-start.26) | collective-permute-done | bytes 98336 | tf_op jit(solution)/shard_map/ppermute | solution.py:24
  101.1 3.4 %collective-permute-start.42 = (bf16[3,64,256]{2,1,0:T(8,128)(2,1)S(1)}, bf16[3,64,256]{2,1,0:T(8,128)(2,1)S(1)}, u32[]{:S(2)}, u32[]{:S(2)}) collective-permute-start(bf16[3,64,256]{2,1,0:T(8,128)(2,1)S(1)} %get-tuple-element.40.refs_0_), channel_id=1, source_target_pairs={{0,16},{1,17},{2,18},{3,19},{4,20},{5,21},{6,22},{7,23},{8,24},{9,... | collective-permute-start | bytes 294920 | tf_op jit(solution)/shard_map/ppermute | solution.py:24
  104.5 0.9 collective-permute-start.46
  106.1 2.0 %collective-permute-start.36 = (bf16[3,64,256]{2,1,0:T(8,128)(2,1)S(1)}, bf16[3,64,256]{2,1,0:T(8,128)(2,1)S(1)}, u32[]{:S(2)}, u32[]{:S(2)}) collective-permute-start(bf16[3,64,256]{2,1,0:T(8,128)(2,1)S(1)} %get-tuple-element.40.refs_0_), channel_id=1, source_target_pairs={{0,4},{1,5},{2,6},{3,7},{4,0},{5,1},{6,2},{7,3},{8,12},{9,13},{10,... | collective-permute-start | bytes 294920 | tf_op jit(solution)/shard_map/ppermute | solution.py:24
  108.8 0.8 collective-permute-start.40
  109.6 1.3 collective-permute-done.46.refs_12_
  110.9 1.2 collective-permute-start.44
  112.1 0.8 collective-permute-start.48
  113.0 1.2 collective-permute-start.37
  114.2 1.3 %collective-permute-start.43 = (bf16[3,64,256]{2,1,0:T(8,128)(2,1)S(1)}, bf16[3,64,256]{2,1,0:T(8,128)(2,1)S(1)}, u32[]{:S(2)}, u32[]{:S(2)}) collective-permute-start(bf16[3,64,256]{2,1,0:T(8,128)(2,1)S(1)} %collective-permute-done.42.refs_8_), channel_id=1, source_target_pairs={{0,2},{1,3},{2,0},{3,1},{4,6},{5,7},{6,4},{7,5},{8,10},{9,11},{10,... | collective-permute-start | bytes 294920 | tf_op jit(solution)/shard_map/ppermute | solution.py:24
  115.6 1.5 %collective-permute-start.47 = (bf16[3,64,256]{2,1,0:T(8,128)(2,1)S(1)}, bf16[3,64,256]{2,1,0:T(8,128)(2,1)S(1)}, u32[]{:S(2)}, u32[]{:S(2)}) collective-permute-start(bf16[3,64,256]{2,1,0:T(8,128)(2,1)S(1)} %collective-permute-done.46.refs_12_), channel_id=1, source_target_pairs={{0,2},{1,3},{2,0},{3,1},{4,6},{5,7},{6,4},{7,5},{8,10},{9,11},{10,... | collective-permute-start | bytes 294920 | tf_op jit(solution)/shard_map/ppermute | solution.py:24
  117.0 1.0 collective-permute-start.41
  118.0 1.1 collective-permute-start.45
  119.1 0.9 collective-permute-start.49
  120.2 1.4 %collective-permute-done.41.refs_7_ = bf16[3,64,256]{2,1,0:T(8,128)(2,1)S(1)} collective-permute-done((bf16[3,64,256]{2,1,0:T(8,128)(2,1)S(1)}, bf16[3,64,256]{2,1,0:T(8,128)(2,1)S(1)}, u32[]{:S(2)}, u32[]{:S(2)}) %collective-permute-start.41) | collective-permute-done | bytes 98336 | tf_op jit(solution)/shard_map/ppermute | solution.py:24
  121.6 1.0 collective-permute-done.45.refs_11_
  122.6 1.1 collective-permute-done.49.refs_15_
  123.7 2.7 %expert_outputs.1 = (bf16[256,1024]{1,0:T(8,128)(2,1)S(1)}, bf16[256,1024]{1,0:T(8,128)(2,1)S(1)}) custom-call(s32[17]{0:T(128)S(1)} %broadcast_in_dim.23.chip_ref, bf16[3,64,256]{2,1,0:T(8,128)(2,1)S(1)} %get-tuple-element.40.refs_0_, bf16[3,64,256]{2,1,0:T(8,128)(2,1)S(1)} %collective-permute-done.35.refs_1_, ...), custom_call_target="tpu_custom_call" | custom-call | flops 805306368 | bytes 3670016 | tf_op jit(solution)/shard_map/expert_outputs/pallas_call | solution.py:158
  128.3 1.1 maximum_select_fusion
  129.4 0.8 slice_bitcast_fusion
  130.3 0.8 select_bitcast_fusion
  (145 shorter events, 15.2 us)
Async XLA Ops:
  1.6 6.3 %copy-start.31 = (f32[3,32,256]{2,1,0:T(8,128)}, f32[3,32,256]{2,1,0:T(8,128)S(1)}, u32[]{:S(2)}) copy-start(f32[3,32,256]{2,1,0:T(8,128)S(1)} %get-tuple-element.55) | copy-start | bytes 294916
  1.6 6.3 %collective-permute-start = (f32[3,32,256]{2,1,0:T(8,128)S(1)}, f32[3,32,256]{2,1,0:T(8,128)S(1)}, u32[]{:S(2)}, u32[]{:S(2)}) collective-permute-start(f32[3,32,256]{2,1,0:T(8,128)S(1)} %get-tuple-element.54), channel_id=1, source_target_pairs={{0,1},{1,0},{2,3},{3,2},{4,5},{5,4},{6,7},{7,6},{8,9},{9,8},{10,11... | collective-permute-start | bytes 294920 | tf_op jit(solution)/shard_map/ppermute | solution.py:24
  7.4 28.3 %collective-permute-start.18 = (bf16[256,1024]{1,0:T(8,128)(2,1)}, bf16[256,1024]{1,0:T(8,128)(2,1)S(1)}, u32[]{:S(2)}, u32[]{:S(2)}) collective-permute-start(bf16[256,1024]{1,0:T(8,128)(2,1)} %get-tuple-element.50), channel_id=1, source_target_pairs={{0,1},{1,0},{2,3},{3,2},{4,5},{5,4},{6,7},{7,6},{8,9},{9,8},{10,11... | collective-permute-start | bytes 1572872 | tf_op jit(solution)/shard_map/ppermute | solution.py:24
  7.4 29.7 %collective-permute-start.17 = (bf16[256,1024]{1,0:T(8,128)(2,1)S(1)}, bf16[256,1024]{1,0:T(8,128)(2,1)S(1)}, u32[]{:S(2)}, u32[]{:S(2)}) collective-permute-start(bf16[256,1024]{1,0:T(8,128)(2,1)S(1)} %bitcast.53), channel_id=1, source_target_pairs={{0,1},{1,0},{2,3},{3,2},{4,5},{5,4},{6,7},{7,6},{8,9},{9,8},{10,11... | collective-permute-start | bytes 1572872 | tf_op jit(solution)/shard_map/ppermute | solution.py:24
  8.5 11.5 %collective-permute-start.9 = (bf16[3,64,256]{2,1,0:T(8,128)(2,1)S(1)}, bf16[3,64,256]{2,1,0:T(8,128)(2,1)S(1)}, u32[]{:S(2)}, u32[]{:S(2)}) collective-permute-start(bf16[3,64,256]{2,1,0:T(8,128)(2,1)S(1)} %fusion.8.refs_0_), channel_id=1, source_target_pairs={{0,16},{1,17},{2,18},{3,19},{4,20},{5,21},{6,22},{7,23},{8,24},{9,... | collective-permute-start | bytes 294920 | tf_op jit(solution)/shard_map/ppermute | solution.py:24
  12.1 9.7 %collective-permute-start.13 = (bf16[3,64,256]{2,1,0:T(8,128)(2,1)S(1)}, bf16[3,64,256]{2,1,0:T(8,128)(2,1)S(1)}, u32[]{:S(2)}, u32[]{:S(2)}) collective-permute-start(bf16[3,64,256]{2,1,0:T(8,128)(2,1)S(1)} %fusion.8.refs_0_), channel_id=1, source_target_pairs={{0,24},{1,25},{2,26},{3,27},{4,28},{5,29},{6,30},{7,31},{8,16},{9,... | collective-permute-start | bytes 294920 | tf_op jit(solution)/shard_map/ppermute | solution.py:24
  13.5 9.8 %collective-permute-start.5 = (bf16[3,64,256]{2,1,0:T(8,128)(2,1)S(1)}, bf16[3,64,256]{2,1,0:T(8,128)(2,1)S(1)}, u32[]{:S(2)}, u32[]{:S(2)}) collective-permute-start(bf16[3,64,256]{2,1,0:T(8,128)(2,1)S(1)} %fusion.8.refs_0_), channel_id=1, source_target_pairs={{0,8},{1,9},{2,10},{3,11},{4,12},{5,13},{6,14},{7,15},{8,0},{9,1},... | collective-permute-start | bytes 294920 | tf_op jit(solution)/shard_map/ppermute | solution.py:24
  20.0 4.6 %collective-permute-start.2 = (bf16[3,64,256]{2,1,0:T(8,128)(2,1)S(1)}, bf16[3,64,256]{2,1,0:T(8,128)(2,1)S(1)}, u32[]{:S(2)}, u32[]{:S(2)}) collective-permute-start(bf16[3,64,256]{2,1,0:T(8,128)(2,1)S(1)} %fusion.8.refs_0_), channel_id=1, source_target_pairs={{0,2},{1,3},{2,0},{3,1},{4,6},{5,7},{6,4},{7,5},{8,10},{9,11},{10,... | collective-permute-start | bytes 294920 | tf_op jit(solution)/shard_map/ppermute | solution.py:24
  21.8 5.6 %collective-permute-start.3 = (bf16[3,64,256]{2,1,0:T(8,128)(2,1)S(1)}, bf16[3,64,256]{2,1,0:T(8,128)(2,1)S(1)}, u32[]{:S(2)}, u32[]{:S(2)}) collective-permute-start(bf16[3,64,256]{2,1,0:T(8,128)(2,1)S(1)} %fusion.8.refs_0_), channel_id=1, source_target_pairs={{0,4},{1,5},{2,6},{3,7},{4,0},{5,1},{6,2},{7,3},{8,12},{9,13},{10,... | collective-permute-start | bytes 294920 | tf_op jit(solution)/shard_map/ppermute | solution.py:24
  23.3 5.5 %collective-permute-start.11 = (bf16[3,64,256]{2,1,0:T(8,128)(2,1)S(1)}, bf16[3,64,256]{2,1,0:T(8,128)(2,1)S(1)}, u32[]{:S(2)}, u32[]{:S(2)}) collective-permute-start(bf16[3,64,256]{2,1,0:T(8,128)(2,1)S(1)} %collective-permute-done.9.refs_8_), channel_id=1, source_target_pairs={{0,4},{1,5},{2,6},{3,7},{4,0},{5,1},{6,2},{7,3},{8,12},{9,13},{10,... | collective-permute-start | bytes 294920 | tf_op jit(solution)/shard_map/ppermute | solution.py:24
  24.6 5.2 %collective-permute-start.15 = (bf16[3,64,256]{2,1,0:T(8,128)(2,1)S(1)}, bf16[3,64,256]{2,1,0:T(8,128)(2,1)S(1)}, u32[]{:S(2)}, u32[]{:S(2)}) collective-permute-start(bf16[3,64,256]{2,1,0:T(8,128)(2,1)S(1)} %collective-permute-done.13.refs_12_), channel_id=1, source_target_pairs={{0,4},{1,5},{2,6},{3,7},{4,0},{5,1},{6,2},{7,3},{8,12},{9,13},{10,... | collective-permute-start | bytes 294920 | tf_op jit(solution)/shard_map/ppermute | solution.py:24
  27.4 11.7 %copy-start.6 = (bf16[3,64,256]{2,1,0:T(8,128)(2,1)}, bf16[3,64,256]{2,1,0:T(8,128)(2,1)S(1)}, u32[]{:S(2)}) copy-start(bf16[3,64,256]{2,1,0:T(8,128)(2,1)S(1)} %collective-permute-done.3.refs_2_) | copy-start | bytes 294916
  27.4 5.5 %collective-permute-start.6 = (bf16[3,64,256]{2,1,0:T(8,128)(2,1)S(1)}, bf16[3,64,256]{2,1,0:T(8,128)(2,1)S(1)}, u32[]{:S(2)}, u32[]{:S(2)}) collective-permute-start(bf16[3,64,256]{2,1,0:T(8,128)(2,1)S(1)} %collective-permute-done.5.refs_4_), channel_id=1, source_target_pairs={{0,2},{1,3},{2,0},{3,1},{4,6},{5,7},{6,4},{7,5},{8,10},{9,11},{10,... | collective-permute-start | bytes 294920 | tf_op jit(solution)/shard_map/ppermute | solution.py:24
  28.8 10.3 %copy-start.8 = (bf16[3,64,256]{2,1,0:T(8,128)(2,1)}, bf16[3,64,256]{2,1,0:T(8,128)(2,1)S(1)}, u32[]{:S(2)}) copy-start(bf16[3,64,256]{2,1,0:T(8,128)(2,1)S(1)} %collective-permute-done.11.refs_10_) | copy-start | bytes 294916
  28.8 5.3 %collective-permute-start.10 = (bf16[3,64,256]{2,1,0:T(8,128)(2,1)S(1)}, bf16[3,64,256]{2,1,0:T(8,128)(2,1)S(1)}, u32[]{:S(2)}, u32[]{:S(2)}) collective-permute-start(bf16[3,64,256]{2,1,0:T(8,128)(2,1)S(1)} %collective-permute-done.9.refs_8_), channel_id=1, source_target_pairs={{0,2},{1,3},{2,0},{3,1},{4,6},{5,7},{6,4},{7,5},{8,10},{9,11},{10,... | collective-permute-start | bytes 294920 | tf_op jit(solution)/shard_map/ppermute | solution.py:24
  29.8 9.2 %copy-start.10 = (bf16[3,64,256]{2,1,0:T(8,128)(2,1)}, bf16[3,64,256]{2,1,0:T(8,128)(2,1)S(1)}, u32[]{:S(2)}) copy-start(bf16[3,64,256]{2,1,0:T(8,128)(2,1)S(1)} %collective-permute-done.15.refs_14_) | copy-start | bytes 294916
  29.8 5.3 %collective-permute-start.14 = (bf16[3,64,256]{2,1,0:T(8,128)(2,1)S(1)}, bf16[3,64,256]{2,1,0:T(8,128)(2,1)S(1)}, u32[]{:S(2)}, u32[]{:S(2)}) collective-permute-start(bf16[3,64,256]{2,1,0:T(8,128)(2,1)S(1)} %collective-permute-done.13.refs_12_), channel_id=1, source_target_pairs={{0,2},{1,3},{2,0},{3,1},{4,6},{5,7},{6,4},{7,5},{8,10},{9,11},{10,... | collective-permute-start | bytes 294920 | tf_op jit(solution)/shard_map/ppermute | solution.py:24
  32.9 6.2 %copy-start.13 = (bf16[3,64,256]{2,1,0:T(8,128)(2,1)}, bf16[3,64,256]{2,1,0:T(8,128)(2,1)S(1)}, u32[]{:S(2)}) copy-start(bf16[3,64,256]{2,1,0:T(8,128)(2,1)S(1)} %collective-permute-done.6.refs_5_) | copy-start | bytes 294916
  32.9 9.1 %collective-permute-start.7 = (bf16[3,64,256]{2,1,0:T(8,128)(2,1)S(1)}, bf16[3,64,256]{2,1,0:T(8,128)(2,1)S(1)}, u32[]{:S(2)}, u32[]{:S(2)}) collective-permute-start(bf16[3,64,256]{2,1,0:T(8,128)(2,1)S(1)} %collective-permute-done.5.refs_4_), channel_id=1, source_target_pairs={{0,4},{1,5},{2,6},{3,7},{4,0},{5,1},{6,2},{7,3},{8,12},{9,13},{10,... | collective-permute-start | bytes 294920 | tf_op jit(solution)/shard_map/ppermute | solution.py:24
  34.1 5.1 %copy-start.15 = (bf16[3,64,256]{2,1,0:T(8,128)(2,1)}, bf16[3,64,256]{2,1,0:T(8,128)(2,1)S(1)}, u32[]{:S(2)}) copy-start(bf16[3,64,256]{2,1,0:T(8,128)(2,1)S(1)} %collective-permute-done.10.refs_9_) | copy-start | bytes 294916
  34.1 8.6 %collective-permute-start.4 = (bf16[3,64,256]{2,1,0:T(8,128)(2,1)S(1)}, bf16[3,64,256]{2,1,0:T(8,128)(2,1)S(1)}, u32[]{:S(2)}, u32[]{:S(2)}) collective-permute-start(bf16[3,64,256]{2,1,0:T(8,128)(2,1)S(1)} %collective-permute-done.2.refs_1_), channel_id=1, source_target_pairs={{0,4},{1,5},{2,6},{3,7},{4,0},{5,1},{6,2},{7,3},{8,12},{9,13},{10,... | collective-permute-start | bytes 294920 | tf_op jit(solution)/shard_map/ppermute | solution.py:24
  35.1 4.0 %copy-start.17 = (bf16[3,64,256]{2,1,0:T(8,128)(2,1)}, bf16[3,64,256]{2,1,0:T(8,128)(2,1)S(1)}, u32[]{:S(2)}) copy-start(bf16[3,64,256]{2,1,0:T(8,128)(2,1)S(1)} %collective-permute-done.14.refs_13_) | copy-start | bytes 294916
  35.1 8.2 %collective-permute-start.12 = (bf16[3,64,256]{2,1,0:T(8,128)(2,1)S(1)}, bf16[3,64,256]{2,1,0:T(8,128)(2,1)S(1)}, u32[]{:S(2)}, u32[]{:S(2)}) collective-permute-start(bf16[3,64,256]{2,1,0:T(8,128)(2,1)S(1)} %collective-permute-done.11.refs_10_), channel_id=1, source_target_pairs={{0,2},{1,3},{2,0},{3,1},{4,6},{5,7},{6,4},{7,5},{8,10},{9,11},{10,... | collective-permute-start | bytes 294920 | tf_op jit(solution)/shard_map/ppermute | solution.py:24
  35.7 8.2 %collective-permute-start.16 = (bf16[3,64,256]{2,1,0:T(8,128)(2,1)S(1)}, bf16[3,64,256]{2,1,0:T(8,128)(2,1)}, u32[]{:S(2)}, u32[]{:S(2)}) collective-permute-start(bf16[3,64,256]{2,1,0:T(8,128)(2,1)S(1)} %collective-permute-done.15.refs_14_), channel_id=1, source_target_pairs={{0,2},{1,3},{2,0},{3,1},{4,6},{5,7},{6,4},{7,5},{8,10},{9,11},{10,... | collective-permute-start | bytes 294920 | tf_op jit(solution)/shard_map/ppermute | solution.py:24
  37.1 6.8 %collective-permute-start.8 = (bf16[3,64,256]{2,1,0:T(8,128)(2,1)S(1)}, bf16[3,64,256]{2,1,0:T(8,128)(2,1)}, u32[]{:S(2)}, u32[]{:S(2)}) collective-permute-start(bf16[3,64,256]{2,1,0:T(8,128)(2,1)S(1)} %collective-permute-done.6.refs_5_), channel_id=1, source_target_pairs={{0,4},{1,5},{2,6},{3,7},{4,0},{5,1},{6,2},{7,3},{8,12},{9,13},{10,... | collective-permute-start | bytes 294920 | tf_op jit(solution)/shard_map/ppermute | solution.py:24
  40.1 3.9 %copy-start.16 = (bf16[3,64,256]{2,1,0:T(8,128)(2,1)S(1)}, bf16[3,64,256]{2,1,0:T(8,128)(2,1)}, u32[]{:S(2)}) copy-start(bf16[3,64,256]{2,1,0:T(8,128)(2,1)} %copy-done.15) | copy-start | bytes 294916
  40.1 13.5 %copy-start.35 = (f32[2,3,32,256]{3,2,1,0:T(8,128)S(1)}, f32[2,3,32,256]{3,2,1,0:T(8,128)}, u32[]{:S(2)}) copy-start(f32[2,3,32,256]{3,2,1,0:T(8,128)} %param.10) | copy-start | bytes 589828
  40.1 13.5 %copy-start.36 = (f32[2,3,32,256]{3,2,1,0:T(8,128)S(1)}, f32[2,3,32,256]{3,2,1,0:T(8,128)}, u32[]{:S(2)}) copy-start(f32[2,3,32,256]{3,2,1,0:T(8,128)} %param.11) | copy-start | bytes 589828
  52.6 5.2 %collective-permute-start.19 = (bf16[3,64,256]{2,1,0:T(8,128)(2,1)}, bf16[3,64,256]{2,1,0:T(8,128)(2,1)S(1)}, u32[]{:S(2)}, u32[]{:S(2)}) collective-permute-start(bf16[3,64,256]{2,1,0:T(8,128)(2,1)} %get-tuple-element.24), channel_id=1, source_target_pairs={{0,4},{1,5},{2,6},{3,7},{4,0},{5,1},{6,2},{7,3},{8,12},{9,13},{10,... | collective-permute-start | bytes 294920 | tf_op jit(solution)/shard_map/ppermute | solution.py:24
  53.7 37.2 %collective-permute-start.1 = (f32[2,3,32,256]{3,2,1,0:T(8,128)S(1)}, f32[2,3,32,256]{3,2,1,0:T(8,128)S(1)}, u32[]{:S(2)}, u32[]{:S(2)}) collective-permute-start(f32[2,3,32,256]{3,2,1,0:T(8,128)S(1)} %get-tuple-element.53), channel_id=1, source_target_pairs={{0,1},{1,0},{2,3},{3,2},{4,5},{5,4},{6,7},{7,6},{8,9},{9,8},{10,11... | collective-permute-start | bytes 589832 | tf_op jit(solution)/shard_map/ppermute | solution.py:24
  53.8 52.2 %collective-permute-start.50 = (bf16[256,1024]{1,0:T(8,128)(2,1)S(1)}, bf16[256,1024]{1,0:T(8,128)(2,1)S(1)}, u32[]{:S(2)}, u32[]{:S(2)}) collective-permute-start(bf16[256,1024]{1,0:T(8,128)(2,1)S(1)} %bitcast.56), channel_id=1, source_target_pairs={{0,1},{1,0},{2,3},{3,2},{4,5},{5,4},{6,7},{7,6},{8,9},{9,8},{10,11... | collective-permute-start | bytes 1572872 | tf_op jit(solution)/shard_map/ppermute | solution.py:24
  54.3 18.5 %collective-permute-start.21 = (bf16[3,64,256]{2,1,0:T(8,128)(2,1)}, bf16[3,64,256]{2,1,0:T(8,128)(2,1)S(1)}, u32[]{:S(2)}, u32[]{:S(2)}) collective-permute-start(bf16[3,64,256]{2,1,0:T(8,128)(2,1)} %copy-done.19), channel_id=1, source_target_pairs={{0,4},{1,5},{2,6},{3,7},{4,0},{5,1},{6,2},{7,3},{8,12},{9,13},{10,... | collective-permute-start | bytes 294920 | tf_op jit(solution)/shard_map/ppermute | solution.py:24
  55.4 6.9 %collective-permute-start.23 = (bf16[3,64,256]{2,1,0:T(8,128)(2,1)}, bf16[3,64,256]{2,1,0:T(8,128)(2,1)S(1)}, u32[]{:S(2)}, u32[]{:S(2)}) collective-permute-start(bf16[3,64,256]{2,1,0:T(8,128)(2,1)} %copy-done.30), channel_id=1, source_target_pairs={{0,4},{1,5},{2,6},{3,7},{4,0},{5,1},{6,2},{7,3},{8,12},{9,13},{10,... | collective-permute-start | bytes 294920 | tf_op jit(solution)/shard_map/ppermute | solution.py:24
  57.8 20.6 %collective-permute-start.25 = (bf16[3,64,256]{2,1,0:T(8,128)(2,1)}, bf16[3,64,256]{2,1,0:T(8,128)(2,1)S(1)}, u32[]{:S(2)}, u32[]{:S(2)}) collective-permute-start(bf16[3,64,256]{2,1,0:T(8,128)(2,1)} %copy-done.12), channel_id=1, source_target_pairs={{0,4},{1,5},{2,6},{3,7},{4,0},{5,1},{6,2},{7,3},{8,12},{9,13},{10,... | collective-permute-start | bytes 294920 | tf_op jit(solution)/shard_map/ppermute | solution.py:24
  62.3 4.6 %collective-permute-start.28 = (bf16[3,64,256]{2,1,0:T(8,128)(2,1)S(1)}, bf16[3,64,256]{2,1,0:T(8,128)(2,1)S(1)}, u32[]{:S(2)}, u32[]{:S(2)}) collective-permute-start(bf16[3,64,256]{2,1,0:T(8,128)(2,1)S(1)} %copy-done.29), channel_id=1, source_target_pairs={{0,2},{1,3},{2,0},{3,1},{4,6},{5,7},{6,4},{7,5},{8,10},{9,11},{10,... | collective-permute-start | bytes 294920 | tf_op jit(solution)/shard_map/ppermute | solution.py:24
  66.9 5.4 %collective-permute-start.32 = (bf16[3,64,256]{2,1,0:T(8,128)(2,1)S(1)}, bf16[3,64,256]{2,1,0:T(8,128)(2,1)S(1)}, u32[]{:S(2)}, u32[]{:S(2)}) collective-permute-start(bf16[3,64,256]{2,1,0:T(8,128)(2,1)S(1)} %copy-done.23), channel_id=1, source_target_pairs={{0,2},{1,3},{2,0},{3,1},{4,6},{5,7},{6,4},{7,5},{8,10},{9,11},{10,... | collective-permute-start | bytes 294920 | tf_op jit(solution)/shard_map/ppermute | solution.py:24
  72.3 5.6 %collective-permute-start.20 = (bf16[3,64,256]{2,1,0:T(8,128)(2,1)S(1)}, bf16[3,64,256]{2,1,0:T(8,128)(2,1)S(1)}, u32[]{:S(2)}, u32[]{:S(2)}) collective-permute-start(bf16[3,64,256]{2,1,0:T(8,128)(2,1)S(1)} %add_convert_fusion.6), channel_id=1, source_target_pairs={{0,2},{1,3},{2,0},{3,1},{4,6},{5,7},{6,4},{7,5},{8,10},{9,11},{10,... | collective-permute-start | bytes 294920 | tf_op jit(solution)/shard_map/ppermute | solution.py:24
  73.6 10.1 %collective-permute-start.27 = (bf16[3,64,256]{2,1,0:T(8,128)(2,1)S(1)}, bf16[3,64,256]{2,1,0:T(8,128)(2,1)S(1)}, u32[]{:S(2)}, u32[]{:S(2)}) collective-permute-start(bf16[3,64,256]{2,1,0:T(8,128)(2,1)S(1)} %copy-done.5), channel_id=1, source_target_pairs={{0,2},{1,3},{2,0},{3,1},{4,6},{5,7},{6,4},{7,5},{8,10},{9,11},{10,... | collective-permute-start | bytes 294920 | tf_op jit(solution)/shard_map/ppermute | solution.py:24
  77.9 4.6 %collective-permute-start.24 = (bf16[3,64,256]{2,1,0:T(8,128)(2,1)S(1)}, bf16[3,64,256]{2,1,0:T(8,128)(2,1)S(1)}, u32[]{:S(2)}, u32[]{:S(2)}) collective-permute-start(bf16[3,64,256]{2,1,0:T(8,128)(2,1)S(1)} %add_convert_fusion.4), channel_id=1, source_target_pairs={{0,2},{1,3},{2,0},{3,1},{4,6},{5,7},{6,4},{7,5},{8,10},{9,11},{10,... | collective-permute-start | bytes 294920 | tf_op jit(solution)/shard_map/ppermute | solution.py:24
  78.4 12.7 %collective-permute-start.31 = (bf16[3,64,256]{2,1,0:T(8,128)(2,1)S(1)}, bf16[3,64,256]{2,1,0:T(8,128)(2,1)S(1)}, u32[]{:S(2)}, u32[]{:S(2)}) collective-permute-start(bf16[3,64,256]{2,1,0:T(8,128)(2,1)S(1)} %get-tuple-element.35), channel_id=1, source_target_pairs={{0,2},{1,3},{2,0},{3,1},{4,6},{5,7},{6,4},{7,5},{8,10},{9,11},{10,... | collective-permute-start | bytes 294920 | tf_op jit(solution)/shard_map/ppermute | solution.py:24
  82.5 4.6 %collective-permute-start.29 = (bf16[3,64,256]{2,1,0:T(8,128)(2,1)S(1)}, bf16[3,64,256]{2,1,0:T(8,128)(2,1)S(1)}, u32[]{:S(2)}, u32[]{:S(2)}) collective-permute-start(bf16[3,64,256]{2,1,0:T(8,128)(2,1)S(1)} %add_convert_fusion.2), channel_id=1, source_target_pairs={{0,4},{1,5},{2,6},{3,7},{4,0},{5,1},{6,2},{7,3},{8,12},{9,13},{10,... | collective-permute-start | bytes 294920 | tf_op jit(solution)/shard_map/ppermute | solution.py:24
  83.8 8.0 %collective-permute-start.33 = (bf16[3,64,256]{2,1,0:T(8,128)(2,1)S(1)}, bf16[3,64,256]{2,1,0:T(8,128)(2,1)S(1)}, u32[]{:S(2)}, u32[]{:S(2)}) collective-permute-start(bf16[3,64,256]{2,1,0:T(8,128)(2,1)S(1)} %add_convert_fusion), channel_id=1, source_target_pairs={{0,4},{1,5},{2,6},{3,7},{4,0},{5,1},{6,2},{7,3},{8,12},{9,13},{10,... | collective-permute-start | bytes 294920 | tf_op jit(solution)/shard_map/ppermute | solution.py:24
  87.2 7.6 %collective-permute-start.22 = (bf16[3,64,256]{2,1,0:T(8,128)(2,1)S(1)}, bf16[3,64,256]{2,1,0:T(8,128)(2,1)S(1)}, u32[]{:S(2)}, u32[]{:S(2)}) collective-permute-start(bf16[3,64,256]{2,1,0:T(8,128)(2,1)S(1)} %add_convert_fusion.5), channel_id=1, source_target_pairs={{0,24},{1,25},{2,26},{3,27},{4,28},{5,29},{6,30},{7,31},{8,16},{9,... | collective-permute-start | bytes 294920 | tf_op jit(solution)/shard_map/ppermute | solution.py:24
  91.0 9.7 %collective-permute-start.26 = (bf16[3,64,256]{2,1,0:T(8,128)(2,1)S(1)}, bf16[3,64,256]{2,1,0:T(8,128)(2,1)S(1)}, u32[]{:S(2)}, u32[]{:S(2)}) collective-permute-start(bf16[3,64,256]{2,1,0:T(8,128)(2,1)S(1)} %add_convert_fusion.3), channel_id=1, source_target_pairs={{0,16},{1,17},{2,18},{3,19},{4,20},{5,21},{6,22},{7,23},{8,24},{9,... | collective-permute-start | bytes 294920 | tf_op jit(solution)/shard_map/ppermute | solution.py:24
  91.1 9.6 %collective-permute-start.30 = (bf16[3,64,256]{2,1,0:T(8,128)(2,1)S(1)}, bf16[3,64,256]{2,1,0:T(8,128)(2,1)S(1)}, u32[]{:S(2)}, u32[]{:S(2)}) collective-permute-start(bf16[3,64,256]{2,1,0:T(8,128)(2,1)S(1)} %add_convert_fusion.1), channel_id=1, source_target_pairs={{0,8},{1,9},{2,10},{3,11},{4,12},{5,13},{6,14},{7,15},{8,0},{9,1},... | collective-permute-start | bytes 294920 | tf_op jit(solution)/shard_map/ppermute | solution.py:24
  91.8 8.9 %copy-start.32 = (f32[3,32,256]{2,1,0:T(8,128)S(1)}, f32[3,32,256]{2,1,0:T(8,128)}, u32[]{:S(2)}) copy-start(f32[3,32,256]{2,1,0:T(8,128)} %copy-done.31) | copy-start | bytes 294916
  91.8 8.9 %copy-start.34 = (f32[3,32,256]{2,1,0:T(8,128)S(1)}, f32[3,32,256]{2,1,0:T(8,128)}, u32[]{:S(2)}) copy-start(f32[3,32,256]{2,1,0:T(8,128)} %copy-done.33) | copy-start | bytes 294916
  101.0 7.1 %collective-permute-start.38 = (bf16[3,64,256]{2,1,0:T(8,128)(2,1)S(1)}, bf16[3,64,256]{2,1,0:T(8,128)(2,1)S(1)}, u32[]{:S(2)}, u32[]{:S(2)}) collective-permute-start(bf16[3,64,256]{2,1,0:T(8,128)(2,1)S(1)} %get-tuple-element.40.refs_0_), channel_id=1, source_target_pairs={{0,8},{1,9},{2,10},{3,11},{4,12},{5,13},{6,14},{7,15},{8,0},{9,1},... | collective-permute-start | bytes 294920 | tf_op jit(solution)/shard_map/ppermute | solution.py:24
  101.1 7.7 %collective-permute-start.42 = (bf16[3,64,256]{2,1,0:T(8,128)(2,1)S(1)}, bf16[3,64,256]{2,1,0:T(8,128)(2,1)S(1)}, u32[]{:S(2)}, u32[]{:S(2)}) collective-permute-start(bf16[3,64,256]{2,1,0:T(8,128)(2,1)S(1)} %get-tuple-element.40.refs_0_), channel_id=1, source_target_pairs={{0,16},{1,17},{2,18},{3,19},{4,20},{5,21},{6,22},{7,23},{8,24},{9,... | collective-permute-start | bytes 294920 | tf_op jit(solution)/shard_map/ppermute | solution.py:24
  104.5 6.4 %collective-permute-start.46 = (bf16[3,64,256]{2,1,0:T(8,128)(2,1)S(1)}, bf16[3,64,256]{2,1,0:T(8,128)(2,1)S(1)}, u32[]{:S(2)}, u32[]{:S(2)}) collective-permute-start(bf16[3,64,256]{2,1,0:T(8,128)(2,1)S(1)} %get-tuple-element.40.refs_0_), channel_id=1, source_target_pairs={{0,24},{1,25},{2,26},{3,27},{4,28},{5,29},{6,30},{7,31},{8,16},{9,... | collective-permute-start | bytes 294920 | tf_op jit(solution)/shard_map/ppermute | solution.py:24
  105.4 6.7 %collective-permute-start.35 = (bf16[3,64,256]{2,1,0:T(8,128)(2,1)S(1)}, bf16[3,64,256]{2,1,0:T(8,128)(2,1)S(1)}, u32[]{:S(2)}, u32[]{:S(2)}) collective-permute-start(bf16[3,64,256]{2,1,0:T(8,128)(2,1)S(1)} %get-tuple-element.40.refs_0_), channel_id=1, source_target_pairs={{0,2},{1,3},{2,0},{3,1},{4,6},{5,7},{6,4},{7,5},{8,10},{9,11},{10,... | collective-permute-start | bytes 294920 | tf_op jit(solution)/shard_map/ppermute | solution.py:24
  106.1 6.9 %collective-permute-start.36 = (bf16[3,64,256]{2,1,0:T(8,128)(2,1)S(1)}, bf16[3,64,256]{2,1,0:T(8,128)(2,1)S(1)}, u32[]{:S(2)}, u32[]{:S(2)}) collective-permute-start(bf16[3,64,256]{2,1,0:T(8,128)(2,1)S(1)} %get-tuple-element.40.refs_0_), channel_id=1, source_target_pairs={{0,4},{1,5},{2,6},{3,7},{4,0},{5,1},{6,2},{7,3},{8,12},{9,13},{10,... | collective-permute-start | bytes 294920 | tf_op jit(solution)/shard_map/ppermute | solution.py:24
  108.1 6.1 %collective-permute-start.39 = (bf16[3,64,256]{2,1,0:T(8,128)(2,1)S(1)}, bf16[3,64,256]{2,1,0:T(8,128)(2,1)S(1)}, u32[]{:S(2)}, u32[]{:S(2)}) collective-permute-start(bf16[3,64,256]{2,1,0:T(8,128)(2,1)S(1)} %collective-permute-done.38.refs_4_), channel_id=1, source_target_pairs={{0,2},{1,3},{2,0},{3,1},{4,6},{5,7},{6,4},{7,5},{8,10},{9,11},{10,... | collective-permute-start | bytes 294920 | tf_op jit(solution)/shard_map/ppermute | solution.py:24
  108.8 10.3 %collective-permute-start.40 = (bf16[3,64,256]{2,1,0:T(8,128)(2,1)S(1)}, bf16[3,64,256]{2,1,0:T(8,128)(2,1)S(1)}, u32[]{:S(2)}, u32[]{:S(2)}) collective-permute-start(bf16[3,64,256]{2,1,0:T(8,128)(2,1)S(1)} %collective-permute-done.38.refs_4_), channel_id=1, source_target_pairs={{0,4},{1,5},{2,6},{3,7},{4,0},{5,1},{6,2},{7,3},{8,12},{9,13},{10,... | collective-permute-start | bytes 294920 | tf_op jit(solution)/shard_map/ppermute | solution.py:24
  110.9 4.6 %collective-permute-start.44 = (bf16[3,64,256]{2,1,0:T(8,128)(2,1)S(1)}, bf16[3,64,256]{2,1,0:T(8,128)(2,1)S(1)}, u32[]{:S(2)}, u32[]{:S(2)}) collective-permute-start(bf16[3,64,256]{2,1,0:T(8,128)(2,1)S(1)} %collective-permute-done.42.refs_8_), channel_id=1, source_target_pairs={{0,4},{1,5},{2,6},{3,7},{4,0},{5,1},{6,2},{7,3},{8,12},{9,13},{10,... | collective-permute-start | bytes 294920 | tf_op jit(solution)/shard_map/ppermute | solution.py:24
  112.1 4.9 %collective-permute-start.48 = (bf16[3,64,256]{2,1,0:T(8,128)(2,1)S(1)}, bf16[3,64,256]{2,1,0:T(8,128)(2,1)S(1)}, u32[]{:S(2)}, u32[]{:S(2)}) collective-permute-start(bf16[3,64,256]{2,1,0:T(8,128)(2,1)S(1)} %collective-permute-done.46.refs_12_), channel_id=1, source_target_pairs={{0,4},{1,5},{2,6},{3,7},{4,0},{5,1},{6,2},{7,3},{8,12},{9,13},{10,... | collective-permute-start | bytes 294920 | tf_op jit(solution)/shard_map/ppermute | solution.py:24
  113.0 5.0 %collective-permute-start.37 = (bf16[3,64,256]{2,1,0:T(8,128)(2,1)S(1)}, bf16[3,64,256]{2,1,0:T(8,128)(2,1)S(1)}, u32[]{:S(2)}, u32[]{:S(2)}) collective-permute-start(bf16[3,64,256]{2,1,0:T(8,128)(2,1)S(1)} %collective-permute-done.35.refs_1_), channel_id=1, source_target_pairs={{0,4},{1,5},{2,6},{3,7},{4,0},{5,1},{6,2},{7,3},{8,12},{9,13},{10,... | collective-permute-start | bytes 294920 | tf_op jit(solution)/shard_map/ppermute | solution.py:24
  114.2 5.9 %collective-permute-start.43 = (bf16[3,64,256]{2,1,0:T(8,128)(2,1)S(1)}, bf16[3,64,256]{2,1,0:T(8,128)(2,1)S(1)}, u32[]{:S(2)}, u32[]{:S(2)}) collective-permute-start(bf16[3,64,256]{2,1,0:T(8,128)(2,1)S(1)} %collective-permute-done.42.refs_8_), channel_id=1, source_target_pairs={{0,2},{1,3},{2,0},{3,1},{4,6},{5,7},{6,4},{7,5},{8,10},{9,11},{10,... | collective-permute-start | bytes 294920 | tf_op jit(solution)/shard_map/ppermute | solution.py:24
  115.6 4.6 %collective-permute-start.47 = (bf16[3,64,256]{2,1,0:T(8,128)(2,1)S(1)}, bf16[3,64,256]{2,1,0:T(8,128)(2,1)S(1)}, u32[]{:S(2)}, u32[]{:S(2)}) collective-permute-start(bf16[3,64,256]{2,1,0:T(8,128)(2,1)S(1)} %collective-permute-done.46.refs_12_), channel_id=1, source_target_pairs={{0,2},{1,3},{2,0},{3,1},{4,6},{5,7},{6,4},{7,5},{8,10},{9,11},{10,... | collective-permute-start | bytes 294920 | tf_op jit(solution)/shard_map/ppermute | solution.py:24
  117.0 4.6 %collective-permute-start.41 = (bf16[3,64,256]{2,1,0:T(8,128)(2,1)S(1)}, bf16[3,64,256]{2,1,0:T(8,128)(2,1)S(1)}, u32[]{:S(2)}, u32[]{:S(2)}) collective-permute-start(bf16[3,64,256]{2,1,0:T(8,128)(2,1)S(1)} %collective-permute-done.39.refs_5_), channel_id=1, source_target_pairs={{0,4},{1,5},{2,6},{3,7},{4,0},{5,1},{6,2},{7,3},{8,12},{9,13},{10,... | collective-permute-start | bytes 294920 | tf_op jit(solution)/shard_map/ppermute | solution.py:24
  118.0 4.6 %collective-permute-start.45 = (bf16[3,64,256]{2,1,0:T(8,128)(2,1)S(1)}, bf16[3,64,256]{2,1,0:T(8,128)(2,1)S(1)}, u32[]{:S(2)}, u32[]{:S(2)}) collective-permute-start(bf16[3,64,256]{2,1,0:T(8,128)(2,1)S(1)} %collective-permute-done.44.refs_10_), channel_id=1, source_target_pairs={{0,2},{1,3},{2,0},{3,1},{4,6},{5,7},{6,4},{7,5},{8,10},{9,11},{10,... | collective-permute-start | bytes 294920 | tf_op jit(solution)/shard_map/ppermute | solution.py:24
  119.1 4.6 %collective-permute-start.49 = (bf16[3,64,256]{2,1,0:T(8,128)(2,1)S(1)}, bf16[3,64,256]{2,1,0:T(8,128)(2,1)S(1)}, u32[]{:S(2)}, u32[]{:S(2)}) collective-permute-start(bf16[3,64,256]{2,1,0:T(8,128)(2,1)S(1)} %collective-permute-done.48.refs_14_), channel_id=1, source_target_pairs={{0,2},{1,3},{2,0},{3,1},{4,6},{5,7},{6,4},{7,5},{8,10},{9,11},{10,... | collective-permute-start | bytes 294920 | tf_op jit(solution)/shard_map/ppermute | solution.py:24
  120.1 8.2 %collective-permute-start.34 = (f32[3,3,32,256]{3,2,1,0:T(8,128)S(1)}, f32[3,3,32,256]{3,2,1,0:T(8,128)}, u32[]{:S(2)}, u32[]{:S(2)}) collective-permute-start(f32[3,3,32,256]{3,2,1,0:T(8,128)S(1)} %get-tuple-element.47), channel_id=1, source_target_pairs={{0,1},{1,0},{2,3},{3,2},{4,5},{5,4},{6,7},{7,6},{8,9},{9,8},{10,11... | collective-permute-start | bytes 884744 | tf_op jit(solution)/shard_map/ppermute | solution.py:24
  126.4 3.8 %collective-permute-start.51 = (bf16[256,1024]{1,0:T(8,128)(2,1)S(1)}, bf16[256,1024]{1,0:T(8,128)(2,1)S(1)}, u32[]{:S(2)}, u32[]{:S(2)}) collective-permute-start(bf16[256,1024]{1,0:T(8,128)(2,1)S(1)} %get-tuple-element.39), channel_id=1, source_target_pairs={{0,1},{1,0},{2,3},{3,2},{4,5},{5,4},{6,7},{7,6},{8,9},{9,8},{10,11... | collective-permute-start | bytes 1572872 | tf_op jit(solution)/shard_map/ppermute | solution.py:24
  (27 other events, 46.4 us)

commit v2 on v1

--- a/solution.py
+++ b/solution.py
@@ -16,7 +16,7 @@
 decay_rate = 0.1
 
 CORE, X_STEP, Y_STEP, Z_UNIT = 1, 2, 4, 8
-VMEM_LIMIT = 48 * 1024 * 1024
+VMEM_LIMIT = 16 * 1024 * 1024
 
 
 def hop(block, mask):
@@ -174,78 +174,96 @@
     )(chip_ids, *pieces, own_y, other_y)
 
 
+def after(value, *others):
+    return lax.optimization_barrier((value,) + others)[0]
+
+
 def gather_chips(piece):
     depth = lax.axis_size("dev") // Z_UNIT
-    column = [piece] + [hop(piece, zj * Z_UNIT) for zj in range(1, depth)]
+    column = [piece] * depth
+    for zj in reversed(range(1, depth)):
+        top = 1 << zj.bit_length() - 1
+        if zj == top:
+            column[zj] = hop(piece, zj * Z_UNIT)
+    for zj in range(1, depth):
+        top = 1 << zj.bit_length() - 1
+        if zj != top:
+            column[zj] = hop(column[top], (zj - top) * Z_UNIT)
     pieces = []
     for zj, here in enumerate(column):
         along_x = hop(here, X_STEP)
         along_y = hop(here, Y_STEP)
-        across = hop(along_x, Y_STEP) if 2 * zj < depth else hop(along_y, X_STEP)
+        across = hop(along_y, X_STEP) if zj % 2 else hop(along_x, Y_STEP)
         pieces += [here, along_x, along_y, across]
     return pieces
 
 
-def add_pair(one, two):
-    return (one.astype(jnp.float32) + two.astype(jnp.float32)).astype(jnp.bfloat16)
+def add_all(first, *others):
+    total = first.astype(jnp.float32)
+    for other in others:
+        total = total + other.astype(jnp.float32)
+    return total
 
 
 def reduce_chips(pieces):
     depth = lax.axis_size("dev") // Z_UNIT
-    total = None
-    for zj in reversed(range(depth)):
-        here, along_x, along_y, across = pieces[4 * zj : 4 * zj + 4]
-        if 2 * zj < depth:
-            along_y = add_pair(along_y, hop(across, X_STEP))
+    column = [None] * depth
+    gate = ((), ())
+    for upper in reversed(range(1, depth, 2)):
+        here, along_x, along_y, across = pieces[4 * upper : 4 * upper + 4]
+        below, below_x, below_y, below_across = pieces[4 * upper - 4 : 4 * upper]
+        from_x = hop(after(across, *gate[0]), X_STEP)
+        from_y = hop(after(below_across, *gate[0]), Y_STEP)
+        along_x = hop(after(along_x, *gate[1]), X_STEP)
+        below_y = hop(after(below_y, *gate[1]), Y_STEP)
+        along_y = hop(add_all(along_y, from_x).astype(jnp.bfloat16), Y_STEP)
+        below_x = hop(add_all(below_x, from_y).astype(jnp.bfloat16), X_STEP)
+        column[upper] = [here, along_x, along_y]
+        column[upper - 1] = [below, below_x, below_y]
+        gate = ((from_x, from_y), (along_x, below_y))
+    for zj in reversed(range(1, depth)):
+        top = 1 << zj.bit_length() - 1
+        low = zj - top
+        part = add_all(*column[zj]).astype(jnp.bfloat16)
+        if low:
+            column[top].append(hop(part, low * Z_UNIT))
         else:
-            along_x = add_pair(along_x, hop(across, Y_STEP))
-        column = (
-            here.astype(jnp.float32)
-            + hop(along_x, X_STEP).astype(jnp.float32)
-            + hop(along_y, Y_STEP).astype(jnp.float32)
-        )
-        if zj:
-            column = hop(column.astype(jnp.bfloat16), zj * Z_UNIT).astype(jnp.float32)
-        total = column if total is None else total + column
-    return total
-
-
-def block_a_core(master, first, second, old_rows, old_cotangent, new_rows, own_old, own_new, live):
+            column[0].append(hop(part, top * Z_UNIT))
+    return add_all(*column[0])
+
+
+def block_a_core(master, first, second, old_rows, old_cotangent, new_rows, old_slots, new_slots, live):
     local_rows = master.shape[2]
     me_index = lax.axis_index("dev")
     core = me_index & CORE
     chips = lax.axis_size("dev") // 2
-    chip_ids = jnp.full((chips + 1,), me_index // 2, jnp.int32)
-
-    def mine(state):
-        return lax.dynamic_index_in_dim(state, core, 0, keepdims=False)
-
-    def partners(state):
-        return lax.dynamic_index_in_dim(state, 1 - core, 0, keepdims=False)
-
-    def both_rows(own, other):
-        return jnp.where(
-            core == 0, jnp.concatenate([own, other], axis=-2), jnp.concatenate([other, own], axis=-2)
-        )
-
-    master_two = both_rows(mine(master), hop(partners(master), CORE))
-    pieces = gather_chips(master_two.astype(jnp.bfloat16))
+    own_old = lax.dynamic_index_in_dim(old_slots, me_index, 0, keepdims=False)
+    own_new = lax.dynamic_index_in_dim(new_slots, me_index, 0, keepdims=False)
+    chip_ids = jnp.full((chips + 1,), lax.shift_right_logical(me_index, 1), jnp.int32)
+
+    state = jnp.stack([master, first, second], axis=1)
+    mine = lax.dynamic_index_in_dim(state, core, 0, keepdims=False)
+    theirs = hop(lax.dynamic_index_in_dim(state, 1 - core, 0, keepdims=False), CORE)
 
     positions = jnp.arange(old_rows.shape[0], dtype=jnp.int32)[:, None]
     alive = positions < live
     empty = jnp.zeros_like(old_cotangent)
+    other_x = hop(old_rows, CORE)
+    other_y = hop(new_rows, CORE)
     own_c = jnp.where(alive & (own_old == core), old_cotangent, empty)
     other_c = hop(jnp.where(alive & (own_old != core), old_cotangent, empty), CORE)
-    other_x = hop(old_rows, CORE)
-    other_y = hop(new_rows, CORE)
-    moments = jnp.stack([first, second], axis=1)
-    first_two, second_two = both_rows(mine(moments), hop(partners(moments), CORE))
+
+    theirs, other_x, other_y, other_c = lax.optimization_barrier((theirs, other_x, other_y, other_c))
+    state = jnp.where(
+        core == 0, jnp.concatenate([mine, theirs], axis=-2), jnp.concatenate([theirs, mine], axis=-2)
+    )
+    pieces = gather_chips(state[0].astype(jnp.bfloat16))
 
     x_turned = transposed(chip_ids, old_rows, other_x)
     c_turned = transposed(chip_ids, own_c, other_c)
     grads = backward(chip_ids, pieces, old_rows, other_x, own_c, other_c, x_turned, c_turned)
     grad = reduce_chips(grads)
-    updated = adam_update(master_two, first_two, second_two, grad)
+    updated = adam_update(state[0], state[1], state[2], grad)
 
     new_pieces = gather_chips(updated[0].astype(jnp.bfloat16))
     updated = jnp.stack(updated)
@@ -306,10 +324,12 @@
     return buffer
 
 
-def any_shape(master, first, second, old_rows, old_cotangent, new_rows, own_old, own_new, live):
+def any_shape(master, first, second, old_rows, old_cotangent, new_rows, old_slots, new_slots, live):
     blocks, kinds, local_rows, block_width = master.shape
     devices = lax.axis_size("dev")
     me_index = lax.axis_index("dev")
+    own_old = lax.dynamic_index_in_dim(old_slots, me_index, 0, keepdims=False)
+    own_new = lax.dynamic_index_in_dim(new_slots, me_index, 0, keepdims=False)
     every_block = lax.all_gather(master.astype(jnp.bfloat16), "dev", axis=2, tiled=True)
     weights = lax.dynamic_index_in_dim(every_block, own_old, 0, keepdims=False)
     slot_grad = hidden_terms(old_rows, old_cotangent, weights, live)
@@ -337,11 +357,8 @@
 ):
     blocks, kinds, local_rows, units = master.shape
     devices = lax.axis_size("dev")
-    me_index = lax.axis_index("dev")
-    own_old = lax.dynamic_index_in_dim(old_slots, me_index, 0, keepdims=False)
-    own_new = lax.dynamic_index_in_dim(new_slots, me_index, 0, keepdims=False)
     whole_tiles = local_rows % 16 == 0 and units % 128 == 0 and old_rows.shape[1] % 128 == 0
-    form = block_a_core if blocks == 2 and devices % Z_UNIT == 0 and whole_tiles else any_shape
+    form = block_a_core if blocks == 2 and devices % (2 * Z_UNIT) == 0 and whole_tiles else any_shape
     return form(
         master,
         first_moment,
@@ -349,8 +366,8 @@
         old_rows[0],
         old_cotangent[0],
         new_rows[0],
-        own_old,
-        own_new,
+        old_slots,
+        new_slots,
         live_rows[0],
     )
 

time: 132 us -> 97.4 us (0.74)
  waiting for transfers between devices: 46.1 us -> 18.8 us
  local copies, waits for them, and re-layouts: 12.3 us -> 4.72 us
  starting transfers between devices: 54 us -> 58.8 us
  other arithmetic: 4.64 us -> 2.8 us
  Pallas kernels: 10.2 us -> 8.55 us
    ppermute x52 -> x51, waiting for transfers between devices: 46.1 us -> 18.8 us  [hop(): lax.ppermute(block, 'dev', [(low, low ^ mask) for low in range(count)])]
    unnamed x78 -> x22, local copies, waits for them, and re-layouts: 9.33 us -> 1.91 us
    ppermute x52 -> x51, starting transfers between devices: 54 us -> 58.8 us  [hop(): lax.ppermute(block, 'dev', [(low, low ^ mask) for low in range(count)])]
    pallas_call x1, Pallas kernels: 5.85 us -> 4.14 us  [backward(): pl.pallas_call(functools.partial(backward_kernel, count), out_shape=[jax....]
  transfers between devices with their start and end apart: 52 -> 51, of which waited for: 19 -> 17; matrix products, arithmetic and copies ran while one was open for 4% -> 5% of each run, Pallas kernels for 3% -> 5%
where the time goes in v2:
time: 97.4 us; the launch traced here: 97.1 us
  starting transfers between devices  58.8 us (60%)
  waiting for transfers between devices  18.8 us (19%)
  Pallas kernels  8.55 us (9%)
  local copies, waits for them, and re-layouts  4.72 us (5%)
  between operations  3.54 us (4%)
  other arithmetic  2.8 us (3%)
    ppermute x51, starting transfers between devices, hop(): lax.ppermute(block, 'dev', [(low, low ^ mask) for low in range(count)])  58.8 us
    ppermute x51, waiting for transfers between devices, hop(): lax.ppermute(block, 'dev', [(low, low ^ mask) for low in range(count)])  18.8 us
    pallas_call x1, Pallas kernels, backward(): pl.pallas_call(functools.partial(backward_kernel, count), out_shape=[jax....  4.14 us
    pallas_call x1, Pallas kernels, forward(): pl.pallas_call(functools.partial(forward_kernel, count), out_shape=[jax.S...  2.68 us
  transfers between devices with their start and end apart: 51, of which 17 were waited for; matrix products, arithmetic and copies ran while one was open for 5% of the time, Pallas kernels for 5%

profile of v2, /device:TPU:0, one launch (start us, length us, event | category | flops | bytes accessed | tf_op | source)
XLA Modules:
  0.0 97.1 jit_solution(9574351583037848831)
XLA Ops:
  1.2 0.7 copy-done.9
  1.9 0.6 dynamic_slice.22
  4.5 1.2 %bitcast_select_fusion = (bf16[256,1024]{1,0:T(8,128)(2,1)S(1)}, bf16[256,1024]{1,0:T(8,128)(2,1)S(1)}) fusion(bf16[1,256,1024]{2,1,0:T(8,128)(2,1)} %param.13, pred[256]{0:T(512)(128)(4,1)S(1)} %get-tuple-element.70, pred[256]{0:T(512)(128)(4,1)S(1)} %get-tuple-element.71), kind=kLoop, calls=%fused_computation.4 | loop fusion | flops 524288 | bytes 1573376 | tf_op jit(solution)/shard_map/jit(_where)/select_n | solution.py:253
  6.3 0.8 dynamic-slice_bitcast_fusion.2
  7.1 1.7 %collective-permute-done = f32[3,3,32,256]{3,2,1,0:T(8,128)S(1)} collective-permute-done((f32[3,3,32,256]{3,2,1,0:T(8,128)}, f32[3,3,32,256]{3,2,1,0:T(8,128)S(1)}, u32[]{:S(2)}, u32[]{:S(2)}) %collective-permute-start) | collective-permute-done | bytes 294944 | tf_op jit(solution)/shard_map/ppermute | solution.py:24
  8.9 3.8 %collective-permute-start.11 = (bf16[3,64,256]{2,1,0:T(8,128)(2,1)S(1)}, bf16[3,64,256]{2,1,0:T(8,128)(2,1)S(1)}, u32[]{:S(2)}, u32[]{:S(2)}) collective-permute-start(bf16[3,64,256]{2,1,0:T(8,128)(2,1)S(1)} %fusion.4.refs_0_), channel_id=1, source_target_pairs={{0,16},{1,17},{2,18},{3,19},{4,20},{5,21},{6,22},{7,23},{8,24},{9,... | collective-permute-start | bytes 294920 | tf_op jit(solution)/shard_map/ppermute | solution.py:24
  12.7 1.6 %collective-permute-start.7 = (bf16[3,64,256]{2,1,0:T(8,128)(2,1)S(1)}, bf16[3,64,256]{2,1,0:T(8,128)(2,1)S(1)}, u32[]{:S(2)}, u32[]{:S(2)}) collective-permute-start(bf16[3,64,256]{2,1,0:T(8,128)(2,1)S(1)} %fusion.4.refs_0_), channel_id=1, source_target_pairs={{0,8},{1,9},{2,10},{3,11},{4,12},{5,13},{6,14},{7,15},{8,0},{9,1},... | collective-permute-start | bytes 294920 | tf_op jit(solution)/shard_map/ppermute | solution.py:24
  14.3 1.5 %collective-permute-start.5 = (bf16[3,64,256]{2,1,0:T(8,128)(2,1)S(1)}, bf16[3,64,256]{2,1,0:T(8,128)(2,1)S(1)}, u32[]{:S(2)}, u32[]{:S(2)}) collective-permute-start(bf16[3,64,256]{2,1,0:T(8,128)(2,1)S(1)} %fusion.4.refs_0_), channel_id=1, source_target_pairs={{0,4},{1,5},{2,6},{3,7},{4,0},{5,1},{6,2},{7,3},{8,12},{9,13},{10,... | collective-permute-start | bytes 294920 | tf_op jit(solution)/shard_map/ppermute | solution.py:24
  15.8 1.5 %collective-permute-start.4 = (bf16[3,64,256]{2,1,0:T(8,128)(2,1)S(1)}, bf16[3,64,256]{2,1,0:T(8,128)(2,1)S(1)}, u32[]{:S(2)}, u32[]{:S(2)}) collective-permute-start(bf16[3,64,256]{2,1,0:T(8,128)(2,1)S(1)} %fusion.4.refs_0_), channel_id=1, source_target_pairs={{0,2},{1,3},{2,0},{3,1},{4,6},{5,7},{6,4},{7,5},{8,10},{9,11},{10,... | collective-permute-start | bytes 294920 | tf_op jit(solution)/shard_map/ppermute | solution.py:24
  17.3 0.9 collective-permute-done.11.refs_8_
  18.3 0.6 collective-permute-start.15
  18.9 1.5 %collective-permute-start.13 = (bf16[3,64,256]{2,1,0:T(8,128)(2,1)S(1)}, bf16[3,64,256]{2,1,0:T(8,128)(2,1)S(1)}, u32[]{:S(2)}, u32[]{:S(2)}) collective-permute-start(bf16[3,64,256]{2,1,0:T(8,128)(2,1)S(1)} %collective-permute-done.11.refs_8_), channel_id=1, source_target_pairs={{0,4},{1,5},{2,6},{3,7},{4,0},{5,1},{6,2},{7,3},{8,12},{9,13},{10,... | collective-permute-start | bytes 294920 | tf_op jit(solution)/shard_map/ppermute | solution.py:24
  20.4 1.5 %collective-permute-start.12 = (bf16[3,64,256]{2,1,0:T(8,128)(2,1)S(1)}, bf16[3,64,256]{2,1,0:T(8,128)(2,1)S(1)}, u32[]{:S(2)}, u32[]{:S(2)}) collective-permute-start(bf16[3,64,256]{2,1,0:T(8,128)(2,1)S(1)} %collective-permute-done.11.refs_8_), channel_id=1, source_target_pairs={{0,2},{1,3},{2,0},{3,1},{4,6},{5,7},{6,4},{7,5},{8,10},{9,11},{10,... | collective-permute-start | bytes 294920 | tf_op jit(solution)/shard_map/ppermute | solution.py:24
  23.0 1.5 %collective-permute-start.17 = (bf16[3,64,256]{2,1,0:T(8,128)(2,1)S(1)}, bf16[3,64,256]{2,1,0:T(8,128)(2,1)}, u32[]{:S(2)}, u32[]{:S(2)}) collective-permute-start(bf16[3,64,256]{2,1,0:T(8,128)(2,1)S(1)} %collective-permute-done.15.refs_12_), channel_id=1, source_target_pairs={{0,4},{1,5},{2,6},{3,7},{4,0},{5,1},{6,2},{7,3},{8,12},{9,13},{10,... | collective-permute-start | bytes 294920 | tf_op jit(solution)/shard_map/ppermute | solution.py:24
  24.5 1.4 %collective-permute-start.6 = (bf16[3,64,256]{2,1,0:T(8,128)(2,1)S(1)}, bf16[3,64,256]{2,1,0:T(8,128)(2,1)}, u32[]{:S(2)}, u32[]{:S(2)}) collective-permute-start(bf16[3,64,256]{2,1,0:T(8,128)(2,1)S(1)} %collective-permute-done.4.refs_1_), channel_id=1, source_target_pairs={{0,4},{1,5},{2,6},{3,7},{4,0},{5,1},{6,2},{7,3},{8,12},{9,13},{10,... | collective-permute-start | bytes 294920 | tf_op jit(solution)/shard_map/ppermute | solution.py:24
  26.1 1.6 %collective-permute-start.16 = (bf16[3,64,256]{2,1,0:T(8,128)(2,1)S(1)}, bf16[3,64,256]{2,1,0:T(8,128)(2,1)}, u32[]{:S(2)}, u32[]{:S(2)}) collective-permute-start(bf16[3,64,256]{2,1,0:T(8,128)(2,1)S(1)} %collective-permute-done.15.refs_12_), channel_id=1, source_target_pairs={{0,2},{1,3},{2,0},{3,1},{4,6},{5,7},{6,4},{7,5},{8,10},{9,11},{10,... | collective-permute-start | bytes 294920 | tf_op jit(solution)/shard_map/ppermute | solution.py:24
  28.2 0.6 copy-done.2
  28.8 1.6 %collective-permute-start.10 = (bf16[3,64,256]{2,1,0:T(8,128)(2,1)S(1)}, bf16[3,64,256]{2,1,0:T(8,128)(2,1)}, u32[]{:S(2)}, u32[]{:S(2)}) collective-permute-start(bf16[3,64,256]{2,1,0:T(8,128)(2,1)S(1)} %collective-permute-done.9.refs_6_), channel_id=1, source_target_pairs={{0,2},{1,3},{2,0},{3,1},{4,6},{5,7},{6,4},{7,5},{8,10},{9,11},{10,... | collective-permute-start | bytes 294920 | tf_op jit(solution)/shard_map/ppermute | solution.py:24
  30.8 0.9 transpose_rows.2.refs_20_
  31.7 0.9 transpose_rows.3.refs_21_
  32.6 1.0 %collective-permute-done.10.refs_7_ = bf16[3,64,256]{2,1,0:T(8,128)(2,1)} collective-permute-done((bf16[3,64,256]{2,1,0:T(8,128)(2,1)S(1)}, bf16[3,64,256]{2,1,0:T(8,128)(2,1)}, u32[]{:S(2)}, u32[]{:S(2)}) %collective-permute-start.10) | collective-permute-done | bytes 98336 | tf_op jit(solution)/shard_map/ppermute | solution.py:24
  33.7 1.6 %collective-permute-done.18.refs_15_ = bf16[3,64,256]{2,1,0:T(8,128)(2,1)} collective-permute-done((bf16[3,64,256]{2,1,0:T(8,128)(2,1)}, bf16[3,64,256]{2,1,0:T(8,128)(2,1)}, u32[]{:S(2)}, u32[]{:S(2)}) %collective-permute-start.18) | collective-permute-done | bytes 98336 | tf_op jit(solution)/shard_map/ppermute | solution.py:24
  35.3 4.1 %slot_gradients.1 = (bf16[3,64,256]{2,1,0:T(8,128)(2,1)S(1)}, bf16[3,64,256]{2,1,0:T(8,128)(2,1)S(1)}, bf16[3,64,256]{2,1,0:T(8,128)(2,1)S(1)}, bf16[3,64,256]{2...) custom-call(s32[17]{0:T(128)S(1)} %broadcast_in_dim.25.chip_ref, ...), custom_call_target="tpu_custom_call" | custom-call | flops 1610612736 | bytes 7340032 | tf_op jit(solution)/shard_map/slot_gradients/pallas_call | solution.py:132
  39.5 0.9 collective-permute-start.19
  40.4 1.2 %collective-permute-start.20 = (bf16[3,64,256]{2,1,0:T(8,128)(2,1)S(1)}, bf16[3,64,256]{2,1,0:T(8,128)(2,1)S(1)}, u32[]{:S(2)}, u32[]{:S(2)}) collective-permute-start(bf16[3,64,256]{2,1,0:T(8,128)(2,1)S(1)} %get-tuple-element.37), channel_id=1, source_target_pairs={{0,4},{1,5},{2,6},{3,7},{4,0},{5,1},{6,2},{7,3},{8,12},{9,13},{10,... | collective-permute-start | bytes 294920 | tf_op jit(solution)/shard_map/ppermute | solution.py:24
  41.5 0.9 collective-permute-start.23
  42.4 1.2 %collective-permute-start.24 = (bf16[3,64,256]{2,1,0:T(8,128)(2,1)S(1)}, bf16[3,64,256]{2,1,0:T(8,128)(2,1)S(1)}, u32[]{:S(2)}, u32[]{:S(2)}) collective-permute-start(bf16[3,64,256]{2,1,0:T(8,128)(2,1)S(1)} %get-tuple-element.41), channel_id=1, source_target_pairs={{0,4},{1,5},{2,6},{3,7},{4,0},{5,1},{6,2},{7,3},{8,12},{9,13},{10,... | collective-permute-start | bytes 294920 | tf_op jit(solution)/shard_map/ppermute | solution.py:24
  44.2 0.9 collective-permute-start.27
  45.0 0.9 collective-permute-done.20
  46.0 1.1 %collective-permute-start.21 = (bf16[3,64,256]{2,1,0:T(8,128)(2,1)S(1)}, bf16[3,64,256]{2,1,0:T(8,128)(2,1)S(1)}, u32[]{:S(2)}, u32[]{:S(2)}) collective-permute-start(bf16[3,64,256]{2,1,0:T(8,128)(2,1)S(1)} %get-tuple-element.38), channel_id=1, source_target_pairs={{0,4},{1,5},{2,6},{3,7},{4,0},{5,1},{6,2},{7,3},{8,12},{9,13},{10,... | collective-permute-start | bytes 294920 | tf_op jit(solution)/shard_map/ppermute | solution.py:24
  47.1 0.9 collective-permute-start.31
  48.0 1.2 %collective-permute-start.26 = (bf16[3,64,256]{2,1,0:T(8,128)(2,1)S(1)}, bf16[3,64,256]{2,1,0:T(8,128)(2,1)S(1)}, u32[]{:S(2)}, u32[]{:S(2)}) collective-permute-start(bf16[3,64,256]{2,1,0:T(8,128)(2,1)S(1)} %add_convert_fusion.5), channel_id=1, source_target_pairs={{0,2},{1,3},{2,0},{3,1},{4,6},{5,7},{6,4},{7,5},{8,10},{9,11},{10,... | collective-permute-start | bytes 294920 | tf_op jit(solution)/shard_map/ppermute | solution.py:24
  49.2 0.9 collective-permute-start.25
  50.6 1.5 %collective-permute-start.30 = (bf16[3,64,256]{2,1,0:T(8,128)(2,1)S(1)}, bf16[3,64,256]{2,1,0:T(8,128)(2,1)S(1)}, u32[]{:S(2)}, u32[]{:S(2)}) collective-permute-start(bf16[3,64,256]{2,1,0:T(8,128)(2,1)S(1)} %get-tuple-element.49), channel_id=1, source_target_pairs={{0,2},{1,3},{2,0},{3,1},{4,6},{5,7},{6,4},{7,5},{8,10},{9,11},{10,... | collective-permute-start | bytes 294920 | tf_op jit(solution)/shard_map/ppermute | solution.py:24
  52.5 0.8 collective-permute-start.22
  53.4 1.6 %collective-permute-start.32 = (bf16[3,64,256]{2,1,0:T(8,128)(2,1)S(1)}, bf16[3,64,256]{2,1,0:T(8,128)(2,1)S(1)}, u32[]{:S(2)}, u32[]{:S(2)}) collective-permute-start(bf16[3,64,256]{2,1,0:T(8,128)(2,1)S(1)} %add_convert_fusion.1), channel_id=1, source_target_pairs={{0,4},{1,5},{2,6},{3,7},{4,0},{5,1},{6,2},{7,3},{8,12},{9,13},{10,... | collective-permute-start | bytes 294920 | tf_op jit(solution)/shard_map/ppermute | solution.py:24
  55.2 1.5 %collective-permute-start.28 = (bf16[3,64,256]{2,1,0:T(8,128)(2,1)S(1)}, bf16[3,64,256]{2,1,0:T(8,128)(2,1)S(1)}, u32[]{:S(2)}, u32[]{:S(2)}) collective-permute-start(bf16[3,64,256]{2,1,0:T(8,128)(2,1)S(1)} %add_convert_fusion.3), channel_id=1, source_target_pairs={{0,8},{1,9},{2,10},{3,11},{4,12},{5,13},{6,14},{7,15},{8,0},{9,1},... | collective-permute-start | bytes 294920 | tf_op jit(solution)/shard_map/ppermute | solution.py:24
  56.7 1.3 %collective-permute-done.32 = bf16[3,64,256]{2,1,0:T(8,128)(2,1)S(1)} collective-permute-done((bf16[3,64,256]{2,1,0:T(8,128)(2,1)S(1)}, bf16[3,64,256]{2,1,0:T(8,128)(2,1)S(1)}, u32[]{:S(2)}, u32[]{:S(2)}) %collective-permute-start.32) | collective-permute-done | bytes 98336 | tf_op jit(solution)/shard_map/ppermute | solution.py:24
  58.1 1.0 collective-permute-start.33
  59.0 1.0 %collective-permute-done.28 = bf16[3,64,256]{2,1,0:T(8,128)(2,1)S(1)} collective-permute-done((bf16[3,64,256]{2,1,0:T(8,128)(2,1)S(1)}, bf16[3,64,256]{2,1,0:T(8,128)(2,1)S(1)}, u32[]{:S(2)}, u32[]{:S(2)}) %collective-permute-start.28) | collective-permute-done | bytes 98336 | tf_op jit(solution)/shard_map/ppermute | solution.py:24
  60.1 3.2 %collective-permute-start.29 = (bf16[3,64,256]{2,1,0:T(8,128)(2,1)S(1)}, bf16[3,64,256]{2,1,0:T(8,128)(2,1)S(1)}, u32[]{:S(2)}, u32[]{:S(2)}) collective-permute-start(bf16[3,64,256]{2,1,0:T(8,128)(2,1)S(1)} %add_convert_fusion.2), channel_id=1, source_target_pairs={{0,16},{1,17},{2,18},{3,19},{4,20},{5,21},{6,22},{7,23},{8,24},{9,... | collective-permute-start | bytes 294920 | tf_op jit(solution)/shard_map/ppermute | solution.py:24
  63.3 4.4 %collective-permute-done.29 = bf16[3,64,256]{2,1,0:T(8,128)(2,1)S(1)} collective-permute-done((bf16[3,64,256]{2,1,0:T(8,128)(2,1)S(1)}, bf16[3,64,256]{2,1,0:T(8,128)(2,1)S(1)}, u32[]{:S(2)}, u32[]{:S(2)}) %collective-permute-start.29) | collective-permute-done | bytes 98336 | tf_op jit(solution)/shard_map/ppermute | solution.py:24
  67.9 2.3 %collective-permute-start.42 = (bf16[3,64,256]{2,1,0:T(8,128)(2,1)S(1)}, bf16[3,64,256]{2,1,0:T(8,128)(2,1)S(1)}, u32[]{:S(2)}, u32[]{:S(2)}) collective-permute-start(bf16[3,64,256]{2,1,0:T(8,128)(2,1)S(1)} %get-tuple-element.56.refs_0_), channel_id=1, source_target_pairs={{0,16},{1,17},{2,18},{3,19},{4,20},{5,21},{6,22},{7,23},{8,24},{9,... | collective-permute-start | bytes 294920 | tf_op jit(solution)/shard_map/ppermute | solution.py:24
  70.2 1.7 %collective-permute-start.38 = (bf16[3,64,256]{2,1,0:T(8,128)(2,1)S(1)}, bf16[3,64,256]{2,1,0:T(8,128)(2,1)S(1)}, u32[]{:S(2)}, u32[]{:S(2)}) collective-permute-start(bf16[3,64,256]{2,1,0:T(8,128)(2,1)S(1)} %get-tuple-element.56.refs_0_), channel_id=1, source_target_pairs={{0,8},{1,9},{2,10},{3,11},{4,12},{5,13},{6,14},{7,15},{8,0},{9,1},... | collective-permute-start | bytes 294920 | tf_op jit(solution)/shard_map/ppermute | solution.py:24
  71.9 0.7 collective-permute-start.36
  72.6 2.6 %collective-permute-start.35 = (bf16[3,64,256]{2,1,0:T(8,128)(2,1)S(1)}, bf16[3,64,256]{2,1,0:T(8,128)(2,1)S(1)}, u32[]{:S(2)}, u32[]{:S(2)}) collective-permute-start(bf16[3,64,256]{2,1,0:T(8,128)(2,1)S(1)} %get-tuple-element.56.refs_0_), channel_id=1, source_target_pairs={{0,2},{1,3},{2,0},{3,1},{4,6},{5,7},{6,4},{7,5},{8,10},{9,11},{10,... | collective-permute-start | bytes 294920 | tf_op jit(solution)/shard_map/ppermute | solution.py:24
  75.2 1.4 %collective-permute-start.44 = (bf16[3,64,256]{2,1,0:T(8,128)(2,1)S(1)}, bf16[3,64,256]{2,1,0:T(8,128)(2,1)S(1)}, u32[]{:S(2)}, u32[]{:S(2)}) collective-permute-start(bf16[3,64,256]{2,1,0:T(8,128)(2,1)S(1)} %collective-permute-done.42.refs_8_), channel_id=1, source_target_pairs={{0,4},{1,5},{2,6},{3,7},{4,0},{5,1},{6,2},{7,3},{8,12},{9,13},{10,... | collective-permute-start | bytes 294920 | tf_op jit(solution)/shard_map/ppermute | solution.py:24
  76.6 1.5 %collective-permute-start.43 = (bf16[3,64,256]{2,1,0:T(8,128)(2,1)S(1)}, bf16[3,64,256]{2,1,0:T(8,128)(2,1)S(1)}, u32[]{:S(2)}, u32[]{:S(2)}) collective-permute-start(bf16[3,64,256]{2,1,0:T(8,128)(2,1)S(1)} %collective-permute-done.42.refs_8_), channel_id=1, source_target_pairs={{0,2},{1,3},{2,0},{3,1},{4,6},{5,7},{6,4},{7,5},{8,10},{9,11},{10,... | collective-permute-start | bytes 294920 | tf_op jit(solution)/shard_map/ppermute | solution.py:24
  78.2 1.0 %collective-permute-start.40 = (bf16[3,64,256]{2,1,0:T(8,128)(2,1)S(1)}, bf16[3,64,256]{2,1,0:T(8,128)(2,1)S(1)}, u32[]{:S(2)}, u32[]{:S(2)}) collective-permute-start(bf16[3,64,256]{2,1,0:T(8,128)(2,1)S(1)} %collective-permute-done.38.refs_4_), channel_id=1, source_target_pairs={{0,4},{1,5},{2,6},{3,7},{4,0},{5,1},{6,2},{7,3},{8,12},{9,13},{10,... | collective-permute-start | bytes 294920 | tf_op jit(solution)/shard_map/ppermute | solution.py:24
  79.2 1.7 %collective-permute-start.39 = (bf16[3,64,256]{2,1,0:T(8,128)(2,1)S(1)}, bf16[3,64,256]{2,1,0:T(8,128)(2,1)S(1)}, u32[]{:S(2)}, u32[]{:S(2)}) collective-permute-start(bf16[3,64,256]{2,1,0:T(8,128)(2,1)S(1)} %collective-permute-done.38.refs_4_), channel_id=1, source_target_pairs={{0,2},{1,3},{2,0},{3,1},{4,6},{5,7},{6,4},{7,5},{8,10},{9,11},{10,... | collective-permute-start | bytes 294920 | tf_op jit(solution)/shard_map/ppermute | solution.py:24
  80.9 1.1 %collective-permute-start.48 = (bf16[3,64,256]{2,1,0:T(8,128)(2,1)S(1)}, bf16[3,64,256]{2,1,0:T(8,128)(2,1)S(1)}, u32[]{:S(2)}, u32[]{:S(2)}) collective-permute-start(bf16[3,64,256]{2,1,0:T(8,128)(2,1)S(1)} %collective-permute-done.46.refs_12_), channel_id=1, source_target_pairs={{0,4},{1,5},{2,6},{3,7},{4,0},{5,1},{6,2},{7,3},{8,12},{9,13},{10,... | collective-permute-start | bytes 294920 | tf_op jit(solution)/shard_map/ppermute | solution.py:24
  82.1 1.0 %collective-permute-start.37 = (bf16[3,64,256]{2,1,0:T(8,128)(2,1)S(1)}, bf16[3,64,256]{2,1,0:T(8,128)(2,1)S(1)}, u32[]{:S(2)}, u32[]{:S(2)}) collective-permute-start(bf16[3,64,256]{2,1,0:T(8,128)(2,1)S(1)} %collective-permute-done.35.refs_1_), channel_id=1, source_target_pairs={{0,4},{1,5},{2,6},{3,7},{4,0},{5,1},{6,2},{7,3},{8,12},{9,13},{10,... | collective-permute-start | bytes 294920 | tf_op jit(solution)/shard_map/ppermute | solution.py:24
  83.1 0.7 collective-permute-start.47
  83.8 1.1 %collective-permute-start.45 = (bf16[3,64,256]{2,1,0:T(8,128)(2,1)S(1)}, bf16[3,64,256]{2,1,0:T(8,128)(2,1)S(1)}, u32[]{:S(2)}, u32[]{:S(2)}) collective-permute-start(bf16[3,64,256]{2,1,0:T(8,128)(2,1)S(1)} %collective-permute-done.43.refs_9_), channel_id=1, source_target_pairs={{0,4},{1,5},{2,6},{3,7},{4,0},{5,1},{6,2},{7,3},{8,12},{9,13},{10,... | collective-permute-start | bytes 294920 | tf_op jit(solution)/shard_map/ppermute | solution.py:24
  84.8 1.4 %collective-permute-start.41 = (bf16[3,64,256]{2,1,0:T(8,128)(2,1)S(1)}, bf16[3,64,256]{2,1,0:T(8,128)(2,1)S(1)}, u32[]{:S(2)}, u32[]{:S(2)}) collective-permute-start(bf16[3,64,256]{2,1,0:T(8,128)(2,1)S(1)} %collective-permute-done.40.refs_6_), channel_id=1, source_target_pairs={{0,2},{1,3},{2,0},{3,1},{4,6},{5,7},{6,4},{7,5},{8,10},{9,11},{10,... | collective-permute-start | bytes 294920 | tf_op jit(solution)/shard_map/ppermute | solution.py:24
  86.2 0.7 collective-permute-start.49
  87.0 0.7 collective-permute-done.47.refs_13_
  87.7 0.7 collective-permute-done.45.refs_11_
  88.4 1.1 %collective-permute-done.41.refs_7_ = bf16[3,64,256]{2,1,0:T(8,128)(2,1)S(1)} collective-permute-done((bf16[3,64,256]{2,1,0:T(8,128)(2,1)S(1)}, bf16[3,64,256]{2,1,0:T(8,128)(2,1)S(1)}, u32[]{:S(2)}, u32[]{:S(2)}) %collective-permute-start.41) | collective-permute-done | bytes 98336 | tf_op jit(solution)/shard_map/ppermute | solution.py:24
  89.4 1.4 %collective-permute-done.49.refs_15_ = bf16[3,64,256]{2,1,0:T(8,128)(2,1)S(1)} collective-permute-done((bf16[3,64,256]{2,1,0:T(8,128)(2,1)S(1)}, bf16[3,64,256]{2,1,0:T(8,128)(2,1)S(1)}, u32[]{:S(2)}, u32[]{:S(2)}) %collective-permute-start.49) | collective-permute-done | bytes 98336 | tf_op jit(solution)/shard_map/ppermute | solution.py:24
  90.8 2.7 %expert_outputs.1 = (bf16[256,1024]{1,0:T(8,128)(2,1)S(1)}, bf16[256,1024]{1,0:T(8,128)(2,1)S(1)}) custom-call(s32[17]{0:T(128)S(1)} %broadcast_in_dim.25.chip_ref, bf16[3,64,256]{2,1,0:T(8,128)(2,1)S(1)} %get-tuple-element.56.refs_0_, bf16[3,64,256]{2,1,0:T(8,128)(2,1)S(1)} %collective-permute-done.35.refs_1_, ...), custom_call_target="tpu_custom_call" | custom-call | flops 805306368 | bytes 3670016 | tf_op jit(solution)/shard_map/expert_outputs/pallas_call | solution.py:158
  94.2 0.6 dynamic_slice.25
  95.5 0.8 slice_bitcast_fusion
  96.3 0.8 select_bitcast_fusion
  (87 shorter events, 6.7 us)
Async XLA Ops:
  0.6 8.2 %collective-permute-start.1 = (bf16[256,1024]{1,0:T(8,128)(2,1)}, bf16[256,1024]{1,0:T(8,128)(2,1)S(1)}, u32[]{:S(2)}, u32[]{:S(2)}) collective-permute-start(bf16[256,1024]{1,0:T(8,128)(2,1)} %bitcast.57), channel_id=1, source_target_pairs={{0,1},{1,0},{2,3},{3,2},{4,5},{5,4},{6,7},{7,6},{8,9},{9,8},{10,11... | collective-permute-start | bytes 1572872 | tf_op jit(solution)/shard_map/ppermute | solution.py:24
  1.1 7.7 %collective-permute-start.2 = (bf16[256,1024]{1,0:T(8,128)(2,1)}, bf16[256,1024]{1,0:T(8,128)(2,1)S(1)}, u32[]{:S(2)}, u32[]{:S(2)}) collective-permute-start(bf16[256,1024]{1,0:T(8,128)(2,1)} %bitcast.60), channel_id=1, source_target_pairs={{0,1},{1,0},{2,3},{3,2},{4,5},{5,4},{6,7},{7,6},{8,9},{9,8},{10,11... | collective-permute-start | bytes 1572872 | tf_op jit(solution)/shard_map/ppermute | solution.py:24
  1.2 0.7 copy-start.9
  4.4 1.8 %copy-start.6 = (f32[2,3,32,256]{3,2,1,0:T(8,128)S(1)}, f32[2,3,32,256]{3,2,1,0:T(8,128)}, u32[]{:S(2)}) copy-start(f32[2,3,32,256]{3,2,1,0:T(8,128)} %param.11) | copy-start | bytes 589828
  4.4 1.8 %copy-start.7 = (f32[2,3,32,256]{3,2,1,0:T(8,128)S(1)}, f32[2,3,32,256]{3,2,1,0:T(8,128)}, u32[]{:S(2)}) copy-start(f32[2,3,32,256]{3,2,1,0:T(8,128)} %param.10) | copy-start | bytes 589828
  4.5 1.8 %copy-start.8 = (f32[2,3,32,256]{3,2,1,0:T(8,128)S(1)}, f32[2,3,32,256]{3,2,1,0:T(8,128)}, u32[]{:S(2)}) copy-start(f32[2,3,32,256]{3,2,1,0:T(8,128)} %param.9) | copy-start | bytes 589828
  5.7 3.1 %collective-permute-start.3 = (bf16[256,1024]{1,0:T(8,128)(2,1)S(1)}, bf16[256,1024]{1,0:T(8,128)(2,1)S(1)}, u32[]{:S(2)}, u32[]{:S(2)}) collective-permute-start(bf16[256,1024]{1,0:T(8,128)(2,1)S(1)} %get-tuple-element.69), channel_id=1, source_target_pairs={{0,1},{1,0},{2,3},{3,2},{4,5},{5,4},{6,7},{7,6},{8,9},{9,8},{10,11... | collective-permute-start | bytes 1572872 | tf_op jit(solution)/shard_map/ppermute | solution.py:24
  7.0 1.8 %collective-permute-start = (f32[3,3,32,256]{3,2,1,0:T(8,128)}, f32[3,3,32,256]{3,2,1,0:T(8,128)S(1)}, u32[]{:S(2)}, u32[]{:S(2)}) collective-permute-start(f32[3,3,32,256]{3,2,1,0:T(8,128)} %get-tuple-element.67), channel_id=1, source_target_pairs={{0,1},{1,0},{2,3},{3,2},{4,5},{5,4},{6,7},{7,6},{8,9},{9,8},{10,11... | collective-permute-start | bytes 884744 | tf_op jit(solution)/shard_map/ppermute | solution.py:24
  8.8 22.0 %copy-start = (bf16[1,256,1024]{2,1,0:T(8,128)(2,1)S(1)}, bf16[1,256,1024]{2,1,0:T(8,128)(2,1)}, u32[]{:S(2)}) copy-start(bf16[1,256,1024]{2,1,0:T(8,128)(2,1)} %param.12) | copy-start | bytes 1572868
  8.9 21.5 %copy-start.4 = (f32[3,3,64,256]{3,2,1,0:T(8,128)}, f32[3,3,64,256]{3,2,1,0:T(8,128)S(1)}, u32[]{:S(2)}) copy-start(f32[3,3,64,256]{3,2,1,0:T(8,128)S(1)} %maximum_select_fusion) | copy-start | bytes 1769476
  8.9 9.3 %collective-permute-start.11 = (bf16[3,64,256]{2,1,0:T(8,128)(2,1)S(1)}, bf16[3,64,256]{2,1,0:T(8,128)(2,1)S(1)}, u32[]{:S(2)}, u32[]{:S(2)}) collective-permute-start(bf16[3,64,256]{2,1,0:T(8,128)(2,1)S(1)} %fusion.4.refs_0_), channel_id=1, source_target_pairs={{0,16},{1,17},{2,18},{3,19},{4,20},{5,21},{6,22},{7,23},{8,24},{9,... | collective-permute-start | bytes 294920 | tf_op jit(solution)/shard_map/ppermute | solution.py:24
  12.7 7.7 %collective-permute-start.7 = (bf16[3,64,256]{2,1,0:T(8,128)(2,1)S(1)}, bf16[3,64,256]{2,1,0:T(8,128)(2,1)S(1)}, u32[]{:S(2)}, u32[]{:S(2)}) collective-permute-start(bf16[3,64,256]{2,1,0:T(8,128)(2,1)S(1)} %fusion.4.refs_0_), channel_id=1, source_target_pairs={{0,8},{1,9},{2,10},{3,11},{4,12},{5,13},{6,14},{7,15},{8,0},{9,1},... | collective-permute-start | bytes 294920 | tf_op jit(solution)/shard_map/ppermute | solution.py:24
  14.3 7.6 %collective-permute-start.5 = (bf16[3,64,256]{2,1,0:T(8,128)(2,1)S(1)}, bf16[3,64,256]{2,1,0:T(8,128)(2,1)S(1)}, u32[]{:S(2)}, u32[]{:S(2)}) collective-permute-start(bf16[3,64,256]{2,1,0:T(8,128)(2,1)S(1)} %fusion.4.refs_0_), channel_id=1, source_target_pairs={{0,4},{1,5},{2,6},{3,7},{4,0},{5,1},{6,2},{7,3},{8,12},{9,13},{10,... | collective-permute-start | bytes 294920 | tf_op jit(solution)/shard_map/ppermute | solution.py:24
  15.8 6.6 %collective-permute-start.4 = (bf16[3,64,256]{2,1,0:T(8,128)(2,1)S(1)}, bf16[3,64,256]{2,1,0:T(8,128)(2,1)S(1)}, u32[]{:S(2)}, u32[]{:S(2)}) collective-permute-start(bf16[3,64,256]{2,1,0:T(8,128)(2,1)S(1)} %fusion.4.refs_0_), channel_id=1, source_target_pairs={{0,2},{1,3},{2,0},{3,1},{4,6},{5,7},{6,4},{7,5},{8,10},{9,11},{10,... | collective-permute-start | bytes 294920 | tf_op jit(solution)/shard_map/ppermute | solution.py:24
  18.3 4.7 %collective-permute-start.15 = (bf16[3,64,256]{2,1,0:T(8,128)(2,1)S(1)}, bf16[3,64,256]{2,1,0:T(8,128)(2,1)S(1)}, u32[]{:S(2)}, u32[]{:S(2)}) collective-permute-start(bf16[3,64,256]{2,1,0:T(8,128)(2,1)S(1)} %collective-permute-done.11.refs_8_), channel_id=1, source_target_pairs={{0,8},{1,9},{2,10},{3,11},{4,12},{5,13},{6,14},{7,15},{8,0},{9,1},... | collective-permute-start | bytes 294920 | tf_op jit(solution)/shard_map/ppermute | solution.py:24
  18.9 5.6 %collective-permute-start.13 = (bf16[3,64,256]{2,1,0:T(8,128)(2,1)S(1)}, bf16[3,64,256]{2,1,0:T(8,128)(2,1)S(1)}, u32[]{:S(2)}, u32[]{:S(2)}) collective-permute-start(bf16[3,64,256]{2,1,0:T(8,128)(2,1)S(1)} %collective-permute-done.11.refs_8_), channel_id=1, source_target_pairs={{0,4},{1,5},{2,6},{3,7},{4,0},{5,1},{6,2},{7,3},{8,12},{9,13},{10,... | collective-permute-start | bytes 294920 | tf_op jit(solution)/shard_map/ppermute | solution.py:24
  20.4 5.6 %collective-permute-start.12 = (bf16[3,64,256]{2,1,0:T(8,128)(2,1)S(1)}, bf16[3,64,256]{2,1,0:T(8,128)(2,1)S(1)}, u32[]{:S(2)}, u32[]{:S(2)}) collective-permute-start(bf16[3,64,256]{2,1,0:T(8,128)(2,1)S(1)} %collective-permute-done.11.refs_8_), channel_id=1, source_target_pairs={{0,2},{1,3},{2,0},{3,1},{4,6},{5,7},{6,4},{7,5},{8,10},{9,11},{10,... | collective-permute-start | bytes 294920 | tf_op jit(solution)/shard_map/ppermute | solution.py:24
  21.9 5.7 %collective-permute-start.9 = (bf16[3,64,256]{2,1,0:T(8,128)(2,1)S(1)}, bf16[3,64,256]{2,1,0:T(8,128)(2,1)S(1)}, u32[]{:S(2)}, u32[]{:S(2)}) collective-permute-start(bf16[3,64,256]{2,1,0:T(8,128)(2,1)S(1)} %collective-permute-done.7.refs_4_), channel_id=1, source_target_pairs={{0,4},{1,5},{2,6},{3,7},{4,0},{5,1},{6,2},{7,3},{8,12},{9,13},{10,... | collective-permute-start | bytes 294920 | tf_op jit(solution)/shard_map/ppermute | solution.py:24
  22.4 5.7 %collective-permute-start.8 = (bf16[3,64,256]{2,1,0:T(8,128)(2,1)S(1)}, bf16[3,64,256]{2,1,0:T(8,128)(2,1)S(1)}, u32[]{:S(2)}, u32[]{:S(2)}) collective-permute-start(bf16[3,64,256]{2,1,0:T(8,128)(2,1)S(1)} %collective-permute-done.7.refs_4_), channel_id=1, source_target_pairs={{0,2},{1,3},{2,0},{3,1},{4,6},{5,7},{6,4},{7,5},{8,10},{9,11},{10,... | collective-permute-start | bytes 294920 | tf_op jit(solution)/shard_map/ppermute | solution.py:24
  23.0 7.4 %collective-permute-start.17 = (bf16[3,64,256]{2,1,0:T(8,128)(2,1)S(1)}, bf16[3,64,256]{2,1,0:T(8,128)(2,1)}, u32[]{:S(2)}, u32[]{:S(2)}) collective-permute-start(bf16[3,64,256]{2,1,0:T(8,128)(2,1)S(1)} %collective-permute-done.15.refs_12_), channel_id=1, source_target_pairs={{0,4},{1,5},{2,6},{3,7},{4,0},{5,1},{6,2},{7,3},{8,12},{9,13},{10,... | collective-permute-start | bytes 294920 | tf_op jit(solution)/shard_map/ppermute | solution.py:24
  24.5 8.1 %collective-permute-start.6 = (bf16[3,64,256]{2,1,0:T(8,128)(2,1)S(1)}, bf16[3,64,256]{2,1,0:T(8,128)(2,1)}, u32[]{:S(2)}, u32[]{:S(2)}) collective-permute-start(bf16[3,64,256]{2,1,0:T(8,128)(2,1)S(1)} %collective-permute-done.4.refs_1_), channel_id=1, source_target_pairs={{0,4},{1,5},{2,6},{3,7},{4,0},{5,1},{6,2},{7,3},{8,12},{9,13},{10,... | collective-permute-start | bytes 294920 | tf_op jit(solution)/shard_map/ppermute | solution.py:24
  26.1 6.6 %collective-permute-start.16 = (bf16[3,64,256]{2,1,0:T(8,128)(2,1)S(1)}, bf16[3,64,256]{2,1,0:T(8,128)(2,1)}, u32[]{:S(2)}, u32[]{:S(2)}) collective-permute-start(bf16[3,64,256]{2,1,0:T(8,128)(2,1)S(1)} %collective-permute-done.15.refs_12_), channel_id=1, source_target_pairs={{0,2},{1,3},{2,0},{3,1},{4,6},{5,7},{6,4},{7,5},{8,10},{9,11},{10,... | collective-permute-start | bytes 294920 | tf_op jit(solution)/shard_map/ppermute | solution.py:24
  27.7 5.0 %collective-permute-start.14 = (bf16[3,64,256]{2,1,0:T(8,128)(2,1)S(1)}, bf16[3,64,256]{2,1,0:T(8,128)(2,1)}, u32[]{:S(2)}, u32[]{:S(2)}) collective-permute-start(bf16[3,64,256]{2,1,0:T(8,128)(2,1)S(1)} %collective-permute-done.12.refs_9_), channel_id=1, source_target_pairs={{0,4},{1,5},{2,6},{3,7},{4,0},{5,1},{6,2},{7,3},{8,12},{9,13},{10,... | collective-permute-start | bytes 294920 | tf_op jit(solution)/shard_map/ppermute | solution.py:24
  28.2 0.6 copy-start.2
  28.8 4.9 %collective-permute-start.10 = (bf16[3,64,256]{2,1,0:T(8,128)(2,1)S(1)}, bf16[3,64,256]{2,1,0:T(8,128)(2,1)}, u32[]{:S(2)}, u32[]{:S(2)}) collective-permute-start(bf16[3,64,256]{2,1,0:T(8,128)(2,1)S(1)} %collective-permute-done.9.refs_6_), channel_id=1, source_target_pairs={{0,2},{1,3},{2,0},{3,1},{4,6},{5,7},{6,4},{7,5},{8,10},{9,11},{10,... | collective-permute-start | bytes 294920 | tf_op jit(solution)/shard_map/ppermute | solution.py:24
  30.4 4.9 %collective-permute-start.18 = (bf16[3,64,256]{2,1,0:T(8,128)(2,1)}, bf16[3,64,256]{2,1,0:T(8,128)(2,1)}, u32[]{:S(2)}, u32[]{:S(2)}) collective-permute-start(bf16[3,64,256]{2,1,0:T(8,128)(2,1)} %collective-permute-done.17.refs_14_), channel_id=1, source_target_pairs={{0,2},{1,3},{2,0},{3,1},{4,6},{5,7},{6,4},{7,5},{8,10},{9,11},{10,... | collective-permute-start | bytes 294920 | tf_op jit(solution)/shard_map/ppermute | solution.py:24
  31.7 3.6 %copy-start.3 = (bf16[3,64,256]{2,1,0:T(8,128)(2,1)S(1)}, bf16[3,64,256]{2,1,0:T(8,128)(2,1)}, u32[]{:S(2)}) copy-start(bf16[3,64,256]{2,1,0:T(8,128)(2,1)} %copy-done.2) | copy-start | bytes 294916
  39.5 4.7 %collective-permute-start.19 = (bf16[3,64,256]{2,1,0:T(8,128)(2,1)S(1)}, bf16[3,64,256]{2,1,0:T(8,128)(2,1)S(1)}, u32[]{:S(2)}, u32[]{:S(2)}) collective-permute-start(bf16[3,64,256]{2,1,0:T(8,128)(2,1)S(1)} %get-tuple-element.36), channel_id=1, source_target_pairs={{0,2},{1,3},{2,0},{3,1},{4,6},{5,7},{6,4},{7,5},{8,10},{9,11},{10,... | collective-permute-start | bytes 294920 | tf_op jit(solution)/shard_map/ppermute | solution.py:24
  40.4 5.6 %collective-permute-start.20 = (bf16[3,64,256]{2,1,0:T(8,128)(2,1)S(1)}, bf16[3,64,256]{2,1,0:T(8,128)(2,1)S(1)}, u32[]{:S(2)}, u32[]{:S(2)}) collective-permute-start(bf16[3,64,256]{2,1,0:T(8,128)(2,1)S(1)} %get-tuple-element.37), channel_id=1, source_target_pairs={{0,4},{1,5},{2,6},{3,7},{4,0},{5,1},{6,2},{7,3},{8,12},{9,13},{10,... | collective-permute-start | bytes 294920 | tf_op jit(solution)/shard_map/ppermute | solution.py:24
  41.5 6.5 %collective-permute-start.23 = (bf16[3,64,256]{2,1,0:T(8,128)(2,1)S(1)}, bf16[3,64,256]{2,1,0:T(8,128)(2,1)S(1)}, u32[]{:S(2)}, u32[]{:S(2)}) collective-permute-start(bf16[3,64,256]{2,1,0:T(8,128)(2,1)S(1)} %get-tuple-element.40), channel_id=1, source_target_pairs={{0,2},{1,3},{2,0},{3,1},{4,6},{5,7},{6,4},{7,5},{8,10},{9,11},{10,... | collective-permute-start | bytes 294920 | tf_op jit(solution)/shard_map/ppermute | solution.py:24
  42.4 6.8 %collective-permute-start.24 = (bf16[3,64,256]{2,1,0:T(8,128)(2,1)S(1)}, bf16[3,64,256]{2,1,0:T(8,128)(2,1)S(1)}, u32[]{:S(2)}, u32[]{:S(2)}) collective-permute-start(bf16[3,64,256]{2,1,0:T(8,128)(2,1)S(1)} %get-tuple-element.41), channel_id=1, source_target_pairs={{0,4},{1,5},{2,6},{3,7},{4,0},{5,1},{6,2},{7,3},{8,12},{9,13},{10,... | collective-permute-start | bytes 294920 | tf_op jit(solution)/shard_map/ppermute | solution.py:24
  44.2 9.2 %collective-permute-start.27 = (bf16[3,64,256]{2,1,0:T(8,128)(2,1)S(1)}, bf16[3,64,256]{2,1,0:T(8,128)(2,1)S(1)}, u32[]{:S(2)}, u32[]{:S(2)}) collective-permute-start(bf16[3,64,256]{2,1,0:T(8,128)(2,1)S(1)} %add_convert_fusion.4), channel_id=1, source_target_pairs={{0,4},{1,5},{2,6},{3,7},{4,0},{5,1},{6,2},{7,3},{8,12},{9,13},{10,... | collective-permute-start | bytes 294920 | tf_op jit(solution)/shard_map/ppermute | solution.py:24
  46.0 4.6 %collective-permute-start.21 = (bf16[3,64,256]{2,1,0:T(8,128)(2,1)S(1)}, bf16[3,64,256]{2,1,0:T(8,128)(2,1)S(1)}, u32[]{:S(2)}, u32[]{:S(2)}) collective-permute-start(bf16[3,64,256]{2,1,0:T(8,128)(2,1)S(1)} %get-tuple-element.38), channel_id=1, source_target_pairs={{0,4},{1,5},{2,6},{3,7},{4,0},{5,1},{6,2},{7,3},{8,12},{9,13},{10,... | collective-permute-start | bytes 294920 | tf_op jit(solution)/shard_map/ppermute | solution.py:24
  47.1 5.5 %collective-permute-start.31 = (bf16[3,64,256]{2,1,0:T(8,128)(2,1)S(1)}, bf16[3,64,256]{2,1,0:T(8,128)(2,1)S(1)}, u32[]{:S(2)}, u32[]{:S(2)}) collective-permute-start(bf16[3,64,256]{2,1,0:T(8,128)(2,1)S(1)} %get-tuple-element.52), channel_id=1, source_target_pairs={{0,2},{1,3},{2,0},{3,1},{4,6},{5,7},{6,4},{7,5},{8,10},{9,11},{10,... | collective-permute-start | bytes 294920 | tf_op jit(solution)/shard_map/ppermute | solution.py:24
  48.0 11.0 %collective-permute-start.26 = (bf16[3,64,256]{2,1,0:T(8,128)(2,1)S(1)}, bf16[3,64,256]{2,1,0:T(8,128)(2,1)S(1)}, u32[]{:S(2)}, u32[]{:S(2)}) collective-permute-start(bf16[3,64,256]{2,1,0:T(8,128)(2,1)S(1)} %add_convert_fusion.5), channel_id=1, source_target_pairs={{0,2},{1,3},{2,0},{3,1},{4,6},{5,7},{6,4},{7,5},{8,10},{9,11},{10,... | collective-permute-start | bytes 294920 | tf_op jit(solution)/shard_map/ppermute | solution.py:24
  49.2 14.1 %collective-permute-start.25 = (bf16[3,64,256]{2,1,0:T(8,128)(2,1)S(1)}, bf16[3,64,256]{2,1,0:T(8,128)(2,1)S(1)}, u32[]{:S(2)}, u32[]{:S(2)}) collective-permute-start(bf16[3,64,256]{2,1,0:T(8,128)(2,1)S(1)} %get-tuple-element.42), channel_id=1, source_target_pairs={{0,4},{1,5},{2,6},{3,7},{4,0},{5,1},{6,2},{7,3},{8,12},{9,13},{10,... | collective-permute-start | bytes 294920 | tf_op jit(solution)/shard_map/ppermute | solution.py:24
  50.6 4.6 %collective-permute-start.30 = (bf16[3,64,256]{2,1,0:T(8,128)(2,1)S(1)}, bf16[3,64,256]{2,1,0:T(8,128)(2,1)S(1)}, u32[]{:S(2)}, u32[]{:S(2)}) collective-permute-start(bf16[3,64,256]{2,1,0:T(8,128)(2,1)S(1)} %get-tuple-element.49), channel_id=1, source_target_pairs={{0,2},{1,3},{2,0},{3,1},{4,6},{5,7},{6,4},{7,5},{8,10},{9,11},{10,... | collective-permute-start | bytes 294920 | tf_op jit(solution)/shard_map/ppermute | solution.py:24
  52.5 10.8 %collective-permute-start.22 = (bf16[3,64,256]{2,1,0:T(8,128)(2,1)S(1)}, bf16[3,64,256]{2,1,0:T(8,128)(2,1)S(1)}, u32[]{:S(2)}, u32[]{:S(2)}) collective-permute-start(bf16[3,64,256]{2,1,0:T(8,128)(2,1)S(1)} %add_convert_fusion.6), channel_id=1, source_target_pairs={{0,2},{1,3},{2,0},{3,1},{4,6},{5,7},{6,4},{7,5},{8,10},{9,11},{10,... | collective-permute-start | bytes 294920 | tf_op jit(solution)/shard_map/ppermute | solution.py:24
  53.4 4.7 %collective-permute-start.32 = (bf16[3,64,256]{2,1,0:T(8,128)(2,1)S(1)}, bf16[3,64,256]{2,1,0:T(8,128)(2,1)S(1)}, u32[]{:S(2)}, u32[]{:S(2)}) collective-permute-start(bf16[3,64,256]{2,1,0:T(8,128)(2,1)S(1)} %add_convert_fusion.1), channel_id=1, source_target_pairs={{0,4},{1,5},{2,6},{3,7},{4,0},{5,1},{6,2},{7,3},{8,12},{9,13},{10,... | collective-permute-start | bytes 294920 | tf_op jit(solution)/shard_map/ppermute | solution.py:24
  55.0 12.7 %copy-start.5 = (f32[3,3,64,256]{3,2,1,0:T(8,128)S(1)}, f32[3,3,64,256]{3,2,1,0:T(8,128)}, u32[]{:S(2)}) copy-start(f32[3,3,64,256]{3,2,1,0:T(8,128)} %copy-done.4) | copy-start | bytes 1769476
  55.2 4.8 %collective-permute-start.28 = (bf16[3,64,256]{2,1,0:T(8,128)(2,1)S(1)}, bf16[3,64,256]{2,1,0:T(8,128)(2,1)S(1)}, u32[]{:S(2)}, u32[]{:S(2)}) collective-permute-start(bf16[3,64,256]{2,1,0:T(8,128)(2,1)S(1)} %add_convert_fusion.3), channel_id=1, source_target_pairs={{0,8},{1,9},{2,10},{3,11},{4,12},{5,13},{6,14},{7,15},{8,0},{9,1},... | collective-permute-start | bytes 294920 | tf_op jit(solution)/shard_map/ppermute | solution.py:24
  58.1 5.3 %collective-permute-start.33 = (bf16[3,64,256]{2,1,0:T(8,128)(2,1)S(1)}, bf16[3,64,256]{2,1,0:T(8,128)(2,1)S(1)}, u32[]{:S(2)}, u32[]{:S(2)}) collective-permute-start(bf16[3,64,256]{2,1,0:T(8,128)(2,1)S(1)} %add_convert_fusion), channel_id=1, source_target_pairs={{0,8},{1,9},{2,10},{3,11},{4,12},{5,13},{6,14},{7,15},{8,0},{9,1},... | collective-permute-start | bytes 294920 | tf_op jit(solution)/shard_map/ppermute | solution.py:24
  60.1 7.6 %collective-permute-start.29 = (bf16[3,64,256]{2,1,0:T(8,128)(2,1)S(1)}, bf16[3,64,256]{2,1,0:T(8,128)(2,1)S(1)}, u32[]{:S(2)}, u32[]{:S(2)}) collective-permute-start(bf16[3,64,256]{2,1,0:T(8,128)(2,1)S(1)} %add_convert_fusion.2), channel_id=1, source_target_pairs={{0,16},{1,17},{2,18},{3,19},{4,20},{5,21},{6,22},{7,23},{8,24},{9,... | collective-permute-start | bytes 294920 | tf_op jit(solution)/shard_map/ppermute | solution.py:24
  67.9 7.2 %collective-permute-start.42 = (bf16[3,64,256]{2,1,0:T(8,128)(2,1)S(1)}, bf16[3,64,256]{2,1,0:T(8,128)(2,1)S(1)}, u32[]{:S(2)}, u32[]{:S(2)}) collective-permute-start(bf16[3,64,256]{2,1,0:T(8,128)(2,1)S(1)} %get-tuple-element.56.refs_0_), channel_id=1, source_target_pairs={{0,16},{1,17},{2,18},{3,19},{4,20},{5,21},{6,22},{7,23},{8,24},{9,... | collective-permute-start | bytes 294920 | tf_op jit(solution)/shard_map/ppermute | solution.py:24
  70.2 6.5 %collective-permute-start.38 = (bf16[3,64,256]{2,1,0:T(8,128)(2,1)S(1)}, bf16[3,64,256]{2,1,0:T(8,128)(2,1)S(1)}, u32[]{:S(2)}, u32[]{:S(2)}) collective-permute-start(bf16[3,64,256]{2,1,0:T(8,128)(2,1)S(1)} %get-tuple-element.56.refs_0_), channel_id=1, source_target_pairs={{0,8},{1,9},{2,10},{3,11},{4,12},{5,13},{6,14},{7,15},{8,0},{9,1},... | collective-permute-start | bytes 294920 | tf_op jit(solution)/shard_map/ppermute | solution.py:24
  71.9 6.3 %collective-permute-start.36 = (bf16[3,64,256]{2,1,0:T(8,128)(2,1)S(1)}, bf16[3,64,256]{2,1,0:T(8,128)(2,1)S(1)}, u32[]{:S(2)}, u32[]{:S(2)}) collective-permute-start(bf16[3,64,256]{2,1,0:T(8,128)(2,1)S(1)} %get-tuple-element.56.refs_0_), channel_id=1, source_target_pairs={{0,4},{1,5},{2,6},{3,7},{4,0},{5,1},{6,2},{7,3},{8,12},{9,13},{10,... | collective-permute-start | bytes 294920 | tf_op jit(solution)/shard_map/ppermute | solution.py:24
  72.6 6.6 %collective-permute-start.35 = (bf16[3,64,256]{2,1,0:T(8,128)(2,1)S(1)}, bf16[3,64,256]{2,1,0:T(8,128)(2,1)S(1)}, u32[]{:S(2)}, u32[]{:S(2)}) collective-permute-start(bf16[3,64,256]{2,1,0:T(8,128)(2,1)S(1)} %get-tuple-element.56.refs_0_), channel_id=1, source_target_pairs={{0,2},{1,3},{2,0},{3,1},{4,6},{5,7},{6,4},{7,5},{8,10},{9,11},{10,... | collective-permute-start | bytes 294920 | tf_op jit(solution)/shard_map/ppermute | solution.py:24
  75.2 5.7 %collective-permute-start.46 = (bf16[3,64,256]{2,1,0:T(8,128)(2,1)S(1)}, bf16[3,64,256]{2,1,0:T(8,128)(2,1)S(1)}, u32[]{:S(2)}, u32[]{:S(2)}) collective-permute-start(bf16[3,64,256]{2,1,0:T(8,128)(2,1)S(1)} %collective-permute-done.42.refs_8_), channel_id=1, source_target_pairs={{0,8},{1,9},{2,10},{3,11},{4,12},{5,13},{6,14},{7,15},{8,0},{9,1},... | collective-permute-start | bytes 294920 | tf_op jit(solution)/shard_map/ppermute | solution.py:24
  75.2 6.8 %collective-permute-start.44 = (bf16[3,64,256]{2,1,0:T(8,128)(2,1)S(1)}, bf16[3,64,256]{2,1,0:T(8,128)(2,1)S(1)}, u32[]{:S(2)}, u32[]{:S(2)}) collective-permute-start(bf16[3,64,256]{2,1,0:T(8,128)(2,1)S(1)} %collective-permute-done.42.refs_8_), channel_id=1, source_target_pairs={{0,4},{1,5},{2,6},{3,7},{4,0},{5,1},{6,2},{7,3},{8,12},{9,13},{10,... | collective-permute-start | bytes 294920 | tf_op jit(solution)/shard_map/ppermute | solution.py:24
  76.6 6.4 %collective-permute-start.43 = (bf16[3,64,256]{2,1,0:T(8,128)(2,1)S(1)}, bf16[3,64,256]{2,1,0:T(8,128)(2,1)S(1)}, u32[]{:S(2)}, u32[]{:S(2)}) collective-permute-start(bf16[3,64,256]{2,1,0:T(8,128)(2,1)S(1)} %collective-permute-done.42.refs_8_), channel_id=1, source_target_pairs={{0,2},{1,3},{2,0},{3,1},{4,6},{5,7},{6,4},{7,5},{8,10},{9,11},{10,... | collective-permute-start | bytes 294920 | tf_op jit(solution)/shard_map/ppermute | solution.py:24
  78.2 5.6 %collective-permute-start.40 = (bf16[3,64,256]{2,1,0:T(8,128)(2,1)S(1)}, bf16[3,64,256]{2,1,0:T(8,128)(2,1)S(1)}, u32[]{:S(2)}, u32[]{:S(2)}) collective-permute-start(bf16[3,64,256]{2,1,0:T(8,128)(2,1)S(1)} %collective-permute-done.38.refs_4_), channel_id=1, source_target_pairs={{0,4},{1,5},{2,6},{3,7},{4,0},{5,1},{6,2},{7,3},{8,12},{9,13},{10,... | collective-permute-start | bytes 294920 | tf_op jit(solution)/shard_map/ppermute | solution.py:24
  79.2 5.6 %collective-permute-start.39 = (bf16[3,64,256]{2,1,0:T(8,128)(2,1)S(1)}, bf16[3,64,256]{2,1,0:T(8,128)(2,1)S(1)}, u32[]{:S(2)}, u32[]{:S(2)}) collective-permute-start(bf16[3,64,256]{2,1,0:T(8,128)(2,1)S(1)} %collective-permute-done.38.refs_4_), channel_id=1, source_target_pairs={{0,2},{1,3},{2,0},{3,1},{4,6},{5,7},{6,4},{7,5},{8,10},{9,11},{10,... | collective-permute-start | bytes 294920 | tf_op jit(solution)/shard_map/ppermute | solution.py:24
  80.9 5.3 %collective-permute-start.48 = (bf16[3,64,256]{2,1,0:T(8,128)(2,1)S(1)}, bf16[3,64,256]{2,1,0:T(8,128)(2,1)S(1)}, u32[]{:S(2)}, u32[]{:S(2)}) collective-permute-start(bf16[3,64,256]{2,1,0:T(8,128)(2,1)S(1)} %collective-permute-done.46.refs_12_), channel_id=1, source_target_pairs={{0,4},{1,5},{2,6},{3,7},{4,0},{5,1},{6,2},{7,3},{8,12},{9,13},{10,... | collective-permute-start | bytes 294920 | tf_op jit(solution)/shard_map/ppermute | solution.py:24
  82.0 8.8 %copy-start.1 = (bf16[1,256,1024]{2,1,0:T(8,128)(2,1)S(1)}, bf16[1,256,1024]{2,1,0:T(8,128)(2,1)}, u32[]{:S(2)}) copy-start(bf16[1,256,1024]{2,1,0:T(8,128)(2,1)} %param.14) | copy-start | bytes 1572868
  82.1 4.8 %collective-permute-start.37 = (bf16[3,64,256]{2,1,0:T(8,128)(2,1)S(1)}, bf16[3,64,256]{2,1,0:T(8,128)(2,1)S(1)}, u32[]{:S(2)}, u32[]{:S(2)}) collective-permute-start(bf16[3,64,256]{2,1,0:T(8,128)(2,1)S(1)} %collective-permute-done.35.refs_1_), channel_id=1, source_target_pairs={{0,4},{1,5},{2,6},{3,7},{4,0},{5,1},{6,2},{7,3},{8,12},{9,13},{10,... | collective-permute-start | bytes 294920 | tf_op jit(solution)/shard_map/ppermute | solution.py:24
  83.1 4.6 %collective-permute-start.47 = (bf16[3,64,256]{2,1,0:T(8,128)(2,1)S(1)}, bf16[3,64,256]{2,1,0:T(8,128)(2,1)S(1)}, u32[]{:S(2)}, u32[]{:S(2)}) collective-permute-start(bf16[3,64,256]{2,1,0:T(8,128)(2,1)S(1)} %collective-permute-done.46.refs_12_), channel_id=1, source_target_pairs={{0,2},{1,3},{2,0},{3,1},{4,6},{5,7},{6,4},{7,5},{8,10},{9,11},{10,... | collective-permute-start | bytes 294920 | tf_op jit(solution)/shard_map/ppermute | solution.py:24
  83.8 4.6 %collective-permute-start.45 = (bf16[3,64,256]{2,1,0:T(8,128)(2,1)S(1)}, bf16[3,64,256]{2,1,0:T(8,128)(2,1)S(1)}, u32[]{:S(2)}, u32[]{:S(2)}) collective-permute-start(bf16[3,64,256]{2,1,0:T(8,128)(2,1)S(1)} %collective-permute-done.43.refs_9_), channel_id=1, source_target_pairs={{0,4},{1,5},{2,6},{3,7},{4,0},{5,1},{6,2},{7,3},{8,12},{9,13},{10,... | collective-permute-start | bytes 294920 | tf_op jit(solution)/shard_map/ppermute | solution.py:24
  84.8 4.6 %collective-permute-start.41 = (bf16[3,64,256]{2,1,0:T(8,128)(2,1)S(1)}, bf16[3,64,256]{2,1,0:T(8,128)(2,1)S(1)}, u32[]{:S(2)}, u32[]{:S(2)}) collective-permute-start(bf16[3,64,256]{2,1,0:T(8,128)(2,1)S(1)} %collective-permute-done.40.refs_6_), channel_id=1, source_target_pairs={{0,2},{1,3},{2,0},{3,1},{4,6},{5,7},{6,4},{7,5},{8,10},{9,11},{10,... | collective-permute-start | bytes 294920 | tf_op jit(solution)/shard_map/ppermute | solution.py:24
  86.2 4.6 %collective-permute-start.49 = (bf16[3,64,256]{2,1,0:T(8,128)(2,1)S(1)}, bf16[3,64,256]{2,1,0:T(8,128)(2,1)S(1)}, u32[]{:S(2)}, u32[]{:S(2)}) collective-permute-start(bf16[3,64,256]{2,1,0:T(8,128)(2,1)S(1)} %collective-permute-done.48.refs_14_), channel_id=1, source_target_pairs={{0,2},{1,3},{2,0},{3,1},{4,6},{5,7},{6,4},{7,5},{8,10},{9,11},{10,... | collective-permute-start | bytes 294920 | tf_op jit(solution)/shard_map/ppermute | solution.py:24
  86.9 8.5 %collective-permute-start.34 = (f32[3,3,32,256]{3,2,1,0:T(8,128)S(1)}, f32[3,3,32,256]{3,2,1,0:T(8,128)S(1)}, u32[]{:S(2)}, u32[]{:S(2)}) collective-permute-start(f32[3,3,32,256]{3,2,1,0:T(8,128)S(1)} %get-tuple-element.65), channel_id=1, source_target_pairs={{0,1},{1,0},{2,3},{3,2},{4,5},{5,4},{6,7},{7,6},{8,9},{9,8},{10,11... | collective-permute-start | bytes 884744 | tf_op jit(solution)/shard_map/ppermute | solution.py:24
  93.5 0.7 copy-start.10
  93.5 2.8 %collective-permute-start.50 = (bf16[256,1024]{1,0:T(8,128)(2,1)S(1)}, bf16[256,1024]{1,0:T(8,128)(2,1)S(1)}, u32[]{:S(2)}, u32[]{:S(2)}) collective-permute-start(bf16[256,1024]{1,0:T(8,128)(2,1)S(1)} %get-tuple-element.55), channel_id=1, source_target_pairs={{0,1},{1,0},{2,3},{3,2},{4,5},{5,4},{6,7},{7,6},{8,9},{9,8},{10,11... | collective-permute-start | bytes 1572872 | tf_op jit(solution)/shard_map/ppermute | solution.py:24

commit v3 on v2

--- a/solution.py
+++ b/solution.py
@@ -44,40 +44,45 @@
         copy.wait()
 
 
-def transpose_kernel(chip_ref, own_ref, other_ref, out_ref):
-    chip = chip_ref[0]
-    tokens, width = own_ref.shape
-    count = chip_ref.shape[0] - 1
-    rows = width // count
+def transpose_kernel(own_x, other_x, own_c, other_c, x_turned, c_turned):
+    chip = lax.axis_index("dev") // 2
+    tokens, width = own_x.shape
+    rows = 2 * width // lax.axis_size("dev")
     lanes = max(128, rows)
-    for part, ref in enumerate((own_ref, other_ref)):
-        for at in range(0, width, lanes):
-            turned = ref[:, at : at + lanes].T
-            for low in range(0, lanes, rows):
-                j = lax.bitwise_xor(chip, (at + low) // rows)
-                start = pl.multiple_of(j * rows, rows)
-                out_ref[pl.ds(start, rows), part * tokens : (part + 1) * tokens] = turned[low : low + rows]
-
-
-def backward_kernel(count, chip_ref, *refs):
+    for out, pair in ((x_turned, (own_x, other_x)), (c_turned, (own_c, other_c))):
+        for part, ref in enumerate(pair):
+            for at in range(0, width, lanes):
+                turned = ref[:, at : at + lanes].T
+                for low in range(0, lanes, rows):
+                    j = lax.bitwise_xor(chip, (at + low) // rows)
+                    start = pl.multiple_of(j * rows, rows)
+                    out[pl.ds(start, rows), part * tokens : (part + 1) * tokens] = turned[low : low + rows]
+
+
+def backward_kernel(count, slots, own_live, other_live, *refs):
     pieces = refs[:count]
     own_x, other_x, own_c, other_c, x_turned, c_turned = refs[count : count + 6]
     outs = refs[count + 6 : 2 * count + 6]
     weights, gate_grad, up_grad, hidden_all, sems = refs[2 * count + 6 :]
-    place_pieces(chip_ref[0], pieces, weights, sems)
+    me_index = lax.axis_index("dev")
+    core = me_index & CORE
+    place_pieces(me_index // 2, pieces, weights, sems)
     tokens = own_x.shape[0]
-    for part, (x_ref, c_ref) in enumerate(((own_x, own_c), (other_x, other_c))):
+    sides = ((own_x, own_c, me_index, own_live), (other_x, other_c, me_index ^ CORE, other_live))
+    for part, (x_ref, c_ref, slot, live) in enumerate(sides):
         span = slice(part * tokens, (part + 1) * tokens)
         gate_pre = jnp.dot(x_ref[...], weights[0], preferred_element_type=jnp.float32)
         up_pre = jnp.dot(x_ref[...], weights[1], preferred_element_type=jnp.float32)
         grad_hidden = jnp.dot(c_ref[...], weights[2], preferred_element_type=jnp.float32)
         gate_sig = jax.nn.sigmoid(gate_pre)
         gate_act = gate_pre * gate_sig
-        hidden_all[span] = (gate_act * up_pre).astype(jnp.bfloat16)
-        up_grad[span] = (grad_hidden * gate_act).astype(jnp.bfloat16)
-        gate_grad[span] = (grad_hidden * up_pre * gate_sig * (1.0 + gate_pre * (1.0 - gate_sig))).astype(
-            jnp.bfloat16
-        )
+        alive = jnp.where(slots[slot] == core, live[0], 0)
+        keep = lax.broadcasted_iota(jnp.int32, gate_pre.shape, 0) < alive
+        grad_up = grad_hidden * gate_act
+        grad_gate = grad_hidden * up_pre * gate_sig * (1.0 + gate_pre * (1.0 - gate_sig))
+        hidden_all[span] = jnp.where(keep, gate_act * up_pre, 0.0).astype(jnp.bfloat16)
+        up_grad[span] = jnp.where(keep, grad_up, 0.0).astype(jnp.bfloat16)
+        gate_grad[span] = jnp.where(keep, grad_gate, 0.0).astype(jnp.bfloat16)
     rows = outs[0].shape[1]
     width = count * rows
     tall = min(width, 256)
@@ -91,10 +96,10 @@
                 outs[(at + low) // rows][kind] = product[low : low + rows]
 
 
-def forward_kernel(count, chip_ref, *refs):
+def forward_kernel(count, *refs):
     pieces = refs[:count]
     own_y, other_y, own_out, other_out, weights, sems = refs[count:]
-    place_pieces(chip_ref[0], pieces, weights, sems)
+    place_pieces(lax.axis_index("dev") // 2, pieces, weights, sems)
     for y_ref, out_ref in ((other_y, other_out), (own_y, own_out)):
         gate_pre = jnp.dot(y_ref[...], weights[0], preferred_element_type=jnp.float32)
         up_pre = jnp.dot(y_ref[...], weights[1], preferred_element_type=jnp.float32)
@@ -112,27 +117,27 @@
     return pltpu.CompilerParams(vmem_limit_bytes=VMEM_LIMIT)
 
 
-def transposed(chip_ids, own, other):
-    tokens, width = own.shape
+def transposed(own_x, other_x, own_c, other_c):
+    tokens, width = own_x.shape
     return pl.pallas_call(
         transpose_kernel,
-        out_shape=jax.ShapeDtypeStruct((width, 2 * tokens), own.dtype),
-        in_specs=[SMEM, VMEM, VMEM],
-        out_specs=VMEM,
+        out_shape=[jax.ShapeDtypeStruct((width, 2 * tokens), own_x.dtype)] * 2,
+        in_specs=[VMEM] * 4,
+        out_specs=[VMEM] * 2,
         compiler_params=params(),
-        cost_estimate=pl.CostEstimate(flops=0, bytes_accessed=8 * tokens * width, transcendentals=0),
+        cost_estimate=pl.CostEstimate(flops=0, bytes_accessed=16 * tokens * width, transcendentals=0),
         name="transpose_rows",
-    )(chip_ids, own, other)
-
-
-def backward(chip_ids, pieces, own_x, other_x, own_c, other_c, x_turned, c_turned):
+    )(own_x, other_x, own_c, other_c)
+
+
+def backward(slots, own_live, other_live, pieces, own_x, other_x, own_c, other_c, x_turned, c_turned):
     count = len(pieces)
     kinds, rows, units = pieces[0].shape
     tokens, width = own_x.shape
     return pl.pallas_call(
         functools.partial(backward_kernel, count),
         out_shape=[jax.ShapeDtypeStruct((kinds, rows, units), jnp.bfloat16)] * count,
-        in_specs=[SMEM] + [ANY] * count + [VMEM] * 6,
+        in_specs=[SMEM] * 3 + [ANY] * count + [VMEM] * 6,
         out_specs=[VMEM] * count,
         scratch_shapes=[
             pltpu.VMEM((kinds, width, units), jnp.bfloat16),
@@ -148,17 +153,17 @@
             transcendentals=2 * tokens * units,
         ),
         name="slot_gradients",
-    )(chip_ids, *pieces, own_x, other_x, own_c, other_c, x_turned, c_turned)
-
-
-def forward(chip_ids, pieces, own_y, other_y):
+    )(slots, own_live, other_live, *pieces, own_x, other_x, own_c, other_c, x_turned, c_turned)
+
+
+def forward(pieces, own_y, other_y):
     count = len(pieces)
     kinds, rows, units = pieces[0].shape
     tokens, width = own_y.shape
     return pl.pallas_call(
         functools.partial(forward_kernel, count),
         out_shape=[jax.ShapeDtypeStruct((tokens, width), jnp.bfloat16)] * 2,
-        in_specs=[SMEM] + [ANY] * count + [VMEM] * 2,
+        in_specs=[ANY] * count + [VMEM] * 2,
         out_specs=[VMEM] * 2,
         scratch_shapes=[
             pltpu.VMEM((kinds, width, units), jnp.bfloat16),
@@ -171,7 +176,7 @@
             transcendentals=2 * tokens * units,
         ),
         name="expert_outputs",
-    )(chip_ids, *pieces, own_y, other_y)
+    )(*pieces, own_y, other_y)
 
 
 def after(value, *others):
@@ -180,22 +185,28 @@
 
 def gather_chips(piece):
     depth = lax.axis_size("dev") // Z_UNIT
-    column = [piece] * depth
-    for zj in reversed(range(1, depth)):
-        top = 1 << zj.bit_length() - 1
-        if zj == top:
-            column[zj] = hop(piece, zj * Z_UNIT)
-    for zj in range(1, depth):
+    column = [piece] + [None] * (depth - 1)
+    for top in reversed([1 << bit for bit in range(depth.bit_length() - 1)]):
+        column[top] = hop(piece, top * Z_UNIT)
+    along_x, along_y, across = [None] * depth, [None] * depth, [None] * depth
+    along_x[0] = hop(piece, X_STEP)
+    along_y[0] = hop(piece, Y_STEP)
+    along_x[1] = hop(column[1], X_STEP)
+    for zj in range(2, depth):
         top = 1 << zj.bit_length() - 1
         if zj != top:
             column[zj] = hop(column[top], (zj - top) * Z_UNIT)
-    pieces = []
-    for zj, here in enumerate(column):
-        along_x = hop(here, X_STEP)
-        along_y = hop(here, Y_STEP)
-        across = hop(along_y, X_STEP) if zj % 2 else hop(along_x, Y_STEP)
-        pieces += [here, along_x, along_y, across]
-    return pieces
+    along_y[1] = hop(after(column[1], along_x[0]), Y_STEP)
+    for zj in range(2, depth, 2):
+        along_x[zj] = hop(after(column[zj], along_x[zj - 2], along_y[zj - 2]), X_STEP)
+        across[zj - 2] = hop(after(along_x[zj - 2], along_y[zj - 2]), Y_STEP)
+        along_x[zj + 1] = hop(after(column[zj + 1], along_x[zj - 1]), X_STEP)
+        along_y[zj + 1] = hop(after(column[zj + 1], along_x[zj - 1]), Y_STEP)
+        along_y[zj] = hop(after(column[zj], along_y[zj - 1]), Y_STEP)
+        across[zj - 1] = hop(after(along_y[zj - 1], along_x[zj]), X_STEP)
+    across[-2] = hop(after(along_x[-2], along_x[-1]), Y_STEP)
+    across[-1] = hop(along_y[-1], X_STEP)
+    return [part for group in zip(column, along_x, along_y, across) for part in group]
 
 
 def add_all(first, *others):
@@ -207,28 +218,28 @@
 
 def reduce_chips(pieces):
     depth = lax.axis_size("dev") // Z_UNIT
-    column = [None] * depth
-    gate = ((), ())
+    column = [[pieces[4 * zj]] for zj in range(depth)]
+    crossed, full, risen = (), (), ()
     for upper in reversed(range(1, depth, 2)):
-        here, along_x, along_y, across = pieces[4 * upper : 4 * upper + 4]
-        below, below_x, below_y, below_across = pieces[4 * upper - 4 : 4 * upper]
-        from_x = hop(after(across, *gate[0]), X_STEP)
-        from_y = hop(after(below_across, *gate[0]), Y_STEP)
-        along_x = hop(after(along_x, *gate[1]), X_STEP)
-        below_y = hop(after(below_y, *gate[1]), Y_STEP)
+        along_x, along_y, across = pieces[4 * upper + 1 : 4 * upper + 4]
+        below_x, below_y, below_across = pieces[4 * upper - 3 : 4 * upper]
+        from_x = hop(after(across, *crossed), X_STEP)
+        from_y = hop(after(below_across, *full), Y_STEP)
+        along_x = hop(after(along_x, *full), X_STEP)
         along_y = hop(add_all(along_y, from_x).astype(jnp.bfloat16), Y_STEP)
-        below_x = hop(add_all(below_x, from_y).astype(jnp.bfloat16), X_STEP)
-        column[upper] = [here, along_x, along_y]
-        column[upper - 1] = [below, below_x, below_y]
-        gate = ((from_x, from_y), (along_x, below_y))
-    for zj in reversed(range(1, depth)):
-        top = 1 << zj.bit_length() - 1
-        low = zj - top
-        part = add_all(*column[zj]).astype(jnp.bfloat16)
-        if low:
-            column[top].append(hop(part, low * Z_UNIT))
-        else:
-            column[0].append(hop(part, top * Z_UNIT))
+        column[upper] += [along_x, along_y]
+        below_x = hop(after(add_all(below_x, from_y).astype(jnp.bfloat16), *risen), X_STEP)
+        below_y = hop(after(below_y, from_x, *risen), Y_STEP)
+        column[upper - 1] += [below_x, below_y]
+        crossed, full = (from_y,), (along_x, along_y)
+        for zj in (upper, upper - 1):
+            top = 1 << zj.bit_length() - 1 if zj else 0
+            low = zj - top
+            if zj:
+                part = add_all(*column[zj]).astype(jnp.bfloat16)
+                risen += (hop(part, low * Z_UNIT if low else top * Z_UNIT),)
+                column[top if low else 0].append(risen[-1])
+        risen = risen[:1] + (below_x, below_y)
     return add_all(*column[0])
 
 
@@ -236,32 +247,36 @@
     local_rows = master.shape[2]
     me_index = lax.axis_index("dev")
     core = me_index & CORE
-    chips = lax.axis_size("dev") // 2
-    own_old = lax.dynamic_index_in_dim(old_slots, me_index, 0, keepdims=False)
     own_new = lax.dynamic_index_in_dim(new_slots, me_index, 0, keepdims=False)
-    chip_ids = jnp.full((chips + 1,), lax.shift_right_logical(me_index, 1), jnp.int32)
-
+
+    other_x = hop(old_rows, CORE)
+    other_c = hop(old_cotangent, CORE)
     state = jnp.stack([master, first, second], axis=1)
     mine = lax.dynamic_index_in_dim(state, core, 0, keepdims=False)
     theirs = hop(lax.dynamic_index_in_dim(state, 1 - core, 0, keepdims=False), CORE)
-
-    positions = jnp.arange(old_rows.shape[0], dtype=jnp.int32)[:, None]
-    alive = positions < live
-    empty = jnp.zeros_like(old_cotangent)
-    other_x = hop(old_rows, CORE)
     other_y = hop(new_rows, CORE)
-    own_c = jnp.where(alive & (own_old == core), old_cotangent, empty)
-    other_c = hop(jnp.where(alive & (own_old != core), old_cotangent, empty), CORE)
-
-    theirs, other_x, other_y, other_c = lax.optimization_barrier((theirs, other_x, other_y, other_c))
+    other_live = hop(live, CORE)
+    x_turned, c_turned = transposed(old_rows, other_x, old_cotangent, other_c)
+
+    theirs, other_y, other_live, x_turned, c_turned, is_own = lax.optimization_barrier(
+        (theirs, other_y, other_live, x_turned, c_turned, own_new == core)
+    )
     state = jnp.where(
         core == 0, jnp.concatenate([mine, theirs], axis=-2), jnp.concatenate([theirs, mine], axis=-2)
     )
     pieces = gather_chips(state[0].astype(jnp.bfloat16))
-
-    x_turned = transposed(chip_ids, old_rows, other_x)
-    c_turned = transposed(chip_ids, own_c, other_c)
-    grads = backward(chip_ids, pieces, old_rows, other_x, own_c, other_c, x_turned, c_turned)
+    grads = backward(
+        old_slots,
+        live,
+        other_live,
+        pieces,
+        old_rows,
+        other_x,
+        old_cotangent,
+        other_c,
+        x_turned,
+        c_turned,
+    )
     grad = reduce_chips(grads)
     updated = adam_update(state[0], state[1], state[2], grad)
 
@@ -273,8 +288,8 @@
     state = jnp.where(
         core == 0, jnp.stack([own_part, from_other], axis=1), jnp.stack([from_other, own_part], axis=1)
     )
-    own_out, other_out = forward(chip_ids, new_pieces, new_rows, other_y)
-    new_outputs = jnp.where(own_new == core, own_out, hop(other_out, CORE))
+    own_out, other_out = forward(new_pieces, new_rows, other_y)
+    new_outputs = jnp.where(is_own, own_out, hop(other_out, CORE))
     return (state[0], state[1], state[2], new_outputs[None])
 
 
@@ -332,7 +347,7 @@
     own_new = lax.dynamic_index_in_dim(new_slots, me_index, 0, keepdims=False)
     every_block = lax.all_gather(master.astype(jnp.bfloat16), "dev", axis=2, tiled=True)
     weights = lax.dynamic_index_in_dim(every_block, own_old, 0, keepdims=False)
-    slot_grad = hidden_terms(old_rows, old_cotangent, weights, live)
+    slot_grad = hidden_terms(old_rows, old_cotangent, weights, live[0])
     block_ids = jnp.arange(blocks, dtype=jnp.int32)[:, None, None, None, None]
     dense = slot_grad.reshape(kinds, devices, local_rows, block_width)
     buffer = jnp.where(block_ids == own_old, dense[None], jnp.zeros((), jnp.float32))
@@ -368,7 +383,7 @@
         new_rows[0],
         old_slots,
         new_slots,
-        live_rows[0],
+        live_rows,
     )
 
 

time: 97.4 us -> 98.8 us (1.014)
  waiting for transfers between devices: 18.8 us -> 25 us
  local copies, waits for them, and re-layouts: 4.72 us -> 2.88 us
  Pallas kernels: 8.55 us -> 6.79 us
  between operations: 3.54 us -> 2.23 us
    ppermute x51 -> x52, waiting for transfers between devices: 18.8 us -> 25 us  [hop(): lax.ppermute(block, 'dev', [(low, low ^ mask) for low in range(count)])]
    select_n x1 -> x0, other arithmetic: 1.24 us -> none  [block_a_core(): own_c = jnp.where(alive & (own_old == core), old_cotangent, empty)]
    pallas_call x2 -> x1, Pallas kernels: 1.73 us -> 0.59 us  [transposed(): pl.pallas_call(transpose_kernel, out_shape=[jax.ShapeDtypeStruct((width,...]
    another operation x1, other arithmetic: 0.05 us -> 1.15 us  [block_a_core(): state = jnp.stack([master, first, second], axis=1)]
    select_n x1, other arithmetic: 0.05 us -> 1.14 us  [block_a_core(): jnp.where(core == 0, jnp.concatenate([mine, theirs], axis=-2), jnp.concat...]
    ppermute x51 -> x52, starting transfers between devices: 58.8 us -> 57.9 us  [hop(): lax.ppermute(block, 'dev', [(low, low ^ mask) for low in range(count)])]
  transfers between devices with their start and end apart: 51 -> 52, of which waited for: 17 -> 23; matrix products, arithmetic and copies ran while one was open for 5% -> 3% of each run, Pallas kernels for 5% -> 3%
where the time goes in v3:
time: 98.8 us; the launch traced here: 98.6 us
  starting transfers between devices  57.9 us (59%)
  waiting for transfers between devices  25 us (25%)
  Pallas kernels  6.79 us (7%)
  other arithmetic  3.76 us (4%)
  local copies, waits for them, and re-layouts  2.88 us (3%)
  between operations  2.23 us (2%)
    ppermute x52, starting transfers between devices, hop(): lax.ppermute(block, 'dev', [(low, low ^ mask) for low in range(count)])  57.9 us
    ppermute x52, waiting for transfers between devices, hop(): lax.ppermute(block, 'dev', [(low, low ^ mask) for low in range(count)])  25 us
    pallas_call x1, Pallas kernels, backward(): pl.pallas_call(functools.partial(backward_kernel, count), out_shape=[jax....  4.09 us
    pallas_call x1, Pallas kernels, forward(): pl.pallas_call(functools.partial(forward_kernel, count), out_shape=[jax.S...  2.1 us
  transfers between devices with their start and end apart: 52, of which 23 were waited for; matrix products, arithmetic and copies ran while one was open for 3% of the time, Pallas kernels for 3%

profile of v3, /device:TPU:0, one launch (start us, length us, event | category | flops | bytes accessed | tf_op | source)
XLA Modules:
  0.0 98.6 jit_solution(6411522813481277641)
XLA Ops:
  1.7 1.2 %pad_maximum_fusion = f32[2,3,3,32,256]{4,3,2,0,1:T(8,128)S(1)} fusion(f32[2,1,3,32,256]{4,3,2,0,1:T(8,128)} %bitcast.62, f32[2,1,3,32,256]{4,3,2,0,1:T(8,128)} %bitcast.63, f32[2,1,3,32,256]{4,3,2,0,1:T(8,128)} %bitcast.64), kind=kLoop, calls=%fused_computation | loop fusion | flops 294912 | bytes 1179648 | tf_op jit(solution)/shard_map/stack | solution.py:254
  3.5 0.7 copy-done.5
  6.1 0.7 copy-done.4
  6.7 1.1 %maximum_select_fusion = f32[3,3,64,256]{3,2,1,0:T(8,128)S(1)} fusion(f32[3,3,32,256]{3,2,1,0:T(8,128)} %copy-done.4, f32[3,3,32,256]{3,2,1,0:T(8,128)S(1)} %get-tuple-element.106, pred[]{:T(512)S(6)} %eq.7), kind=kLoop, calls=%fused_computation.1 | loop fusion | flops 442368 | bytes 1179649 | tf_op jit(solution)/shard_map/jit(_where)/select_n | solution.py:264
  7.9 3.7 %collective-permute-start.11 = (bf16[3,64,256]{2,1,0:T(8,128)(2,1)S(1)}, bf16[3,64,256]{2,1,0:T(8,128)(2,1)S(1)}, u32[]{:S(2)}, u32[]{:S(2)}) collective-permute-start(bf16[3,64,256]{2,1,0:T(8,128)(2,1)S(1)} %fusion.4.refs_0_), channel_id=1, source_target_pairs={{0,16},{1,17},{2,18},{3,19},{4,20},{5,21},{6,22},{7,23},{8,24},{9,... | collective-permute-start | bytes 294920 | tf_op jit(solution)/shard_map/ppermute | solution.py:24
  11.7 1.6 %collective-permute-start.8 = (bf16[3,64,256]{2,1,0:T(8,128)(2,1)S(1)}, bf16[3,64,256]{2,1,0:T(8,128)(2,1)S(1)}, u32[]{:S(2)}, u32[]{:S(2)}) collective-permute-start(bf16[3,64,256]{2,1,0:T(8,128)(2,1)S(1)} %fusion.4.refs_0_), channel_id=1, source_target_pairs={{0,8},{1,9},{2,10},{3,11},{4,12},{5,13},{6,14},{7,15},{8,0},{9,1},... | collective-permute-start | bytes 294920 | tf_op jit(solution)/shard_map/ppermute | solution.py:24
  13.2 1.5 %collective-permute-start.5 = (bf16[3,64,256]{2,1,0:T(8,128)(2,1)S(1)}, bf16[3,64,256]{2,1,0:T(8,128)(2,1)S(1)}, u32[]{:S(2)}, u32[]{:S(2)}) collective-permute-start(bf16[3,64,256]{2,1,0:T(8,128)(2,1)S(1)} %fusion.4.refs_0_), channel_id=1, source_target_pairs={{0,2},{1,3},{2,0},{3,1},{4,6},{5,7},{6,4},{7,5},{8,10},{9,11},{10,... | collective-permute-start | bytes 294920 | tf_op jit(solution)/shard_map/ppermute | solution.py:24
  14.7 1.5 %collective-permute-start.6 = (bf16[3,64,256]{2,1,0:T(8,128)(2,1)S(1)}, bf16[3,64,256]{2,1,0:T(8,128)(2,1)S(1)}, u32[]{:S(2)}, u32[]{:S(2)}) collective-permute-start(bf16[3,64,256]{2,1,0:T(8,128)(2,1)S(1)} %fusion.4.refs_0_), channel_id=1, source_target_pairs={{0,4},{1,5},{2,6},{3,7},{4,0},{5,1},{6,2},{7,3},{8,12},{9,13},{10,... | collective-permute-start | bytes 294920 | tf_op jit(solution)/shard_map/ppermute | solution.py:24
  16.2 1.0 %collective-permute-done.11.refs_8_ = bf16[3,64,256]{2,1,0:T(8,128)(2,1)S(1)} collective-permute-done((bf16[3,64,256]{2,1,0:T(8,128)(2,1)S(1)}, bf16[3,64,256]{2,1,0:T(8,128)(2,1)S(1)}, u32[]{:S(2)}, u32[]{:S(2)}) %collective-permute-start.11) | collective-permute-done | bytes 98336 | tf_op jit(solution)/shard_map/ppermute | solution.py:24
  17.3 0.6 collective-permute-start.15
  17.9 1.5 %collective-permute-start.9 = (bf16[3,64,256]{2,1,0:T(8,128)(2,1)S(1)}, bf16[3,64,256]{2,1,0:T(8,128)(2,1)S(1)}, u32[]{:S(2)}, u32[]{:S(2)}) collective-permute-start(bf16[3,64,256]{2,1,0:T(8,128)(2,1)S(1)} %collective-permute-done.8.refs_4_), channel_id=1, source_target_pairs={{0,2},{1,3},{2,0},{3,1},{4,6},{5,7},{6,4},{7,5},{8,10},{9,11},{10,... | collective-permute-start | bytes 294920 | tf_op jit(solution)/shard_map/ppermute | solution.py:24
  19.4 1.5 %collective-permute-start.10 = (bf16[3,64,256]{2,1,0:T(8,128)(2,1)S(1)}, bf16[3,64,256]{2,1,0:T(8,128)(2,1)S(1)}, u32[]{:S(2)}, u32[]{:S(2)}) collective-permute-start(bf16[3,64,256]{2,1,0:T(8,128)(2,1)S(1)} %collective-permute-done.8.refs_4_), channel_id=1, source_target_pairs={{0,4},{1,5},{2,6},{3,7},{4,0},{5,1},{6,2},{7,3},{8,12},{9,13},{10,... | collective-permute-start | bytes 294920 | tf_op jit(solution)/shard_map/ppermute | solution.py:24
  21.9 0.6 collective-permute-done.9.refs_5_
  22.5 2.2 %collective-permute-start.16 = (bf16[3,64,256]{2,1,0:T(8,128)(2,1)S(1)}, bf16[3,64,256]{2,1,0:T(8,128)(2,1)S(1)}, u32[]{:S(2)}, u32[]{:S(2)}) collective-permute-start(bf16[3,64,256]{2,1,0:T(8,128)(2,1)S(1)} %collective-permute-done.15.refs_12_), channel_id=1, source_target_pairs={{0,2},{1,3},{2,0},{3,1},{4,6},{5,7},{6,4},{7,5},{8,10},{9,11},{10,... | collective-permute-start | bytes 294920 | tf_op jit(solution)/shard_map/ppermute | solution.py:24
  24.8 1.7 %collective-permute-start.18 = (bf16[3,64,256]{2,1,0:T(8,128)(2,1)S(1)}, bf16[3,64,256]{2,1,0:T(8,128)(2,1)S(1)}, u32[]{:S(2)}, u32[]{:S(2)}) collective-permute-start(bf16[3,64,256]{2,1,0:T(8,128)(2,1)S(1)} %collective-permute-done.15.refs_12_), channel_id=1, source_target_pairs={{0,4},{1,5},{2,6},{3,7},{4,0},{5,1},{6,2},{7,3},{8,12},{9,13},{10,... | collective-permute-start | bytes 294920 | tf_op jit(solution)/shard_map/ppermute | solution.py:24
  26.8 1.7 %collective-permute-start.14 = (bf16[3,64,256]{2,1,0:T(8,128)(2,1)S(1)}, bf16[3,64,256]{2,1,0:T(8,128)(2,1)S(1)}, u32[]{:S(2)}, u32[]{:S(2)}) collective-permute-start(bf16[3,64,256]{2,1,0:T(8,128)(2,1)S(1)} %collective-permute-done.11.refs_8_), channel_id=1, source_target_pairs={{0,4},{1,5},{2,6},{3,7},{4,0},{5,1},{6,2},{7,3},{8,12},{9,13},{10,... | collective-permute-start | bytes 294920 | tf_op jit(solution)/shard_map/ppermute | solution.py:24
  28.9 0.9 collective-permute-done.18.refs_14_
  29.8 0.7 collective-permute-start.19
  30.5 1.0 %collective-permute-start.17 = (bf16[3,64,256]{2,1,0:T(8,128)(2,1)S(1)}, bf16[3,64,256]{2,1,0:T(8,128)(2,1)S(1)}, u32[]{:S(2)}, u32[]{:S(2)}) collective-permute-start(bf16[3,64,256]{2,1,0:T(8,128)(2,1)S(1)} %collective-permute-done.12.refs_9_), channel_id=1, source_target_pairs={{0,4},{1,5},{2,6},{3,7},{4,0},{5,1},{6,2},{7,3},{8,12},{9,13},{10,... | collective-permute-start | bytes 294920 | tf_op jit(solution)/shard_map/ppermute | solution.py:24
  33.1 1.3 %collective-permute-done.19.refs_15_ = bf16[3,64,256]{2,1,0:T(8,128)(2,1)S(1)} collective-permute-done((bf16[3,64,256]{2,1,0:T(8,128)(2,1)S(1)}, bf16[3,64,256]{2,1,0:T(8,128)(2,1)S(1)}, u32[]{:S(2)}, u32[]{:S(2)}) %collective-permute-start.19) | collective-permute-done | bytes 98336 | tf_op jit(solution)/shard_map/ppermute | solution.py:24
  34.4 0.7 collective-permute-done.17.refs_11_
  35.1 4.1 %slot_gradients.1 = (bf16[3,64,256]{2,1,0:T(8,128)(2,1)S(1)}, bf16[3,64,256]{2,1,0:T(8,128)(2,1)S(1)}, bf16[3,64,256]{2,1,0:T(8,128)(2,1)S(1)}, bf16[3,64,256]{2...) custom-call(s32[32]{0:T(128)S(1)} %copy-done.3, ...), custom_call_target="tpu_custom_call" | custom-call | flops 1610612736 | bytes 7340032 | tf_op jit(solution)/shard_map/slot_gradients/pallas_call | solution.py:137
  39.2 1.1 %collective-permute-start.20 = (bf16[3,64,256]{2,1,0:T(8,128)(2,1)S(1)}, bf16[3,64,256]{2,1,0:T(8,128)(2,1)S(1)}, u32[]{:S(2)}, u32[]{:S(2)}) collective-permute-start(bf16[3,64,256]{2,1,0:T(8,128)(2,1)S(1)} %get-tuple-element.66), channel_id=1, source_target_pairs={{0,4},{1,5},{2,6},{3,7},{4,0},{5,1},{6,2},{7,3},{8,12},{9,13},{10,... | collective-permute-start | bytes 294920 | tf_op jit(solution)/shard_map/ppermute | solution.py:24
  40.3 2.0 %collective-permute-start.22 = (bf16[3,64,256]{2,1,0:T(8,128)(2,1)S(1)}, bf16[3,64,256]{2,1,0:T(8,128)(2,1)S(1)}, u32[]{:S(2)}, u32[]{:S(2)}) collective-permute-start(bf16[3,64,256]{2,1,0:T(8,128)(2,1)S(1)} %get-tuple-element.68), channel_id=1, source_target_pairs={{0,2},{1,3},{2,0},{3,1},{4,6},{5,7},{6,4},{7,5},{8,10},{9,11},{10,... | collective-permute-start | bytes 294920 | tf_op jit(solution)/shard_map/ppermute | solution.py:24
  42.3 2.2 %collective-permute-done.20 = bf16[3,64,256]{2,1,0:T(8,128)(2,1)S(1)} collective-permute-done((bf16[3,64,256]{2,1,0:T(8,128)(2,1)S(1)}, bf16[3,64,256]{2,1,0:T(8,128)(2,1)S(1)}, u32[]{:S(2)}, u32[]{:S(2)}) %collective-permute-start.20) | collective-permute-done | bytes 98336 | tf_op jit(solution)/shard_map/ppermute | solution.py:24
  44.6 1.4 %collective-permute-start.30 = (bf16[3,64,256]{2,1,0:T(8,128)(2,1)S(1)}, bf16[3,64,256]{2,1,0:T(8,128)(2,1)S(1)}, u32[]{:S(2)}, u32[]{:S(2)}) collective-permute-start(bf16[3,64,256]{2,1,0:T(8,128)(2,1)S(1)} %get-tuple-element.79), channel_id=1, source_target_pairs={{0,2},{1,3},{2,0},{3,1},{4,6},{5,7},{6,4},{7,5},{8,10},{9,11},{10,... | collective-permute-start | bytes 294920 | tf_op jit(solution)/shard_map/ppermute | solution.py:24
  46.0 0.6 collective-permute-start.21
  46.7 1.3 %collective-permute-start.23 = (bf16[3,64,256]{2,1,0:T(8,128)(2,1)S(1)}, bf16[3,64,256]{2,1,0:T(8,128)(2,1)S(1)}, u32[]{:S(2)}, u32[]{:S(2)}) collective-permute-start(bf16[3,64,256]{2,1,0:T(8,128)(2,1)S(1)} %get-tuple-element.69), channel_id=1, source_target_pairs={{0,4},{1,5},{2,6},{3,7},{4,0},{5,1},{6,2},{7,3},{8,12},{9,13},{10,... | collective-permute-start | bytes 294920 | tf_op jit(solution)/shard_map/ppermute | solution.py:24
  48.0 0.8 collective-permute-start.25
  49.3 1.5 %collective-permute-start.33 = (bf16[3,64,256]{2,1,0:T(8,128)(2,1)S(1)}, bf16[3,64,256]{2,1,0:T(8,128)(2,1)S(1)}, u32[]{:S(2)}, u32[]{:S(2)}) collective-permute-start(bf16[3,64,256]{2,1,0:T(8,128)(2,1)S(1)} %add_convert_fusion.1), channel_id=1, source_target_pairs={{0,4},{1,5},{2,6},{3,7},{4,0},{5,1},{6,2},{7,3},{8,12},{9,13},{10,... | collective-permute-start | bytes 294920 | tf_op jit(solution)/shard_map/ppermute | solution.py:24
  50.8 1.8 %collective-permute-done.25 = bf16[3,64,256]{2,1,0:T(8,128)(2,1)S(1)} collective-permute-done((bf16[3,64,256]{2,1,0:T(8,128)(2,1)S(1)}, bf16[3,64,256]{2,1,0:T(8,128)(2,1)S(1)}, u32[]{:S(2)}, u32[]{:S(2)}) %collective-permute-start.25) | collective-permute-done | bytes 98336 | tf_op jit(solution)/shard_map/ppermute | solution.py:24
  52.6 1.0 collective-permute-start.28
  53.6 1.9 %collective-permute-start.32 = (bf16[3,64,256]{2,1,0:T(8,128)(2,1)S(1)}, bf16[3,64,256]{2,1,0:T(8,128)(2,1)S(1)}, u32[]{:S(2)}, u32[]{:S(2)}) collective-permute-start(bf16[3,64,256]{2,1,0:T(8,128)(2,1)S(1)} %get-tuple-element.83), channel_id=1, source_target_pairs={{0,2},{1,3},{2,0},{3,1},{4,6},{5,7},{6,4},{7,5},{8,10},{9,11},{10,... | collective-permute-start | bytes 294920 | tf_op jit(solution)/shard_map/ppermute | solution.py:24
  55.6 1.1 %collective-permute-start.26 = (bf16[3,64,256]{2,1,0:T(8,128)(2,1)S(1)}, bf16[3,64,256]{2,1,0:T(8,128)(2,1)S(1)}, u32[]{:S(2)}, u32[]{:S(2)}) collective-permute-start(bf16[3,64,256]{2,1,0:T(8,128)(2,1)S(1)} %add_convert_fusion.4), channel_id=1, source_target_pairs={{0,8},{1,9},{2,10},{3,11},{4,12},{5,13},{6,14},{7,15},{8,0},{9,1},... | collective-permute-start | bytes 294920 | tf_op jit(solution)/shard_map/ppermute | solution.py:24
  56.7 1.5 %collective-permute-done.32 = bf16[3,64,256]{2,1,0:T(8,128)(2,1)S(1)} collective-permute-done((bf16[3,64,256]{2,1,0:T(8,128)(2,1)S(1)}, bf16[3,64,256]{2,1,0:T(8,128)(2,1)S(1)}, u32[]{:S(2)}, u32[]{:S(2)}) %collective-permute-start.32) | collective-permute-done | bytes 98336 | tf_op jit(solution)/shard_map/ppermute | solution.py:24
  58.3 1.3 %collective-permute-start.34 = (bf16[3,64,256]{2,1,0:T(8,128)(2,1)S(1)}, bf16[3,64,256]{2,1,0:T(8,128)(2,1)S(1)}, u32[]{:S(2)}, u32[]{:S(2)}) collective-permute-start(bf16[3,64,256]{2,1,0:T(8,128)(2,1)S(1)} %add_convert_fusion), channel_id=1, source_target_pairs={{0,8},{1,9},{2,10},{3,11},{4,12},{5,13},{6,14},{7,15},{8,0},{9,1},... | collective-permute-start | bytes 294920 | tf_op jit(solution)/shard_map/ppermute | solution.py:24
  59.6 1.0 %collective-permute-done.26 = bf16[3,64,256]{2,1,0:T(8,128)(2,1)S(1)} collective-permute-done((bf16[3,64,256]{2,1,0:T(8,128)(2,1)S(1)}, bf16[3,64,256]{2,1,0:T(8,128)(2,1)S(1)}, u32[]{:S(2)}, u32[]{:S(2)}) %collective-permute-start.26) | collective-permute-done | bytes 98336 | tf_op jit(solution)/shard_map/ppermute | solution.py:24
  60.7 0.7 collective-permute-start.29
  61.4 1.6 %collective-permute-start.31 = (bf16[3,64,256]{2,1,0:T(8,128)(2,1)S(1)}, bf16[3,64,256]{2,1,0:T(8,128)(2,1)S(1)}, u32[]{:S(2)}, u32[]{:S(2)}) collective-permute-start(bf16[3,64,256]{2,1,0:T(8,128)(2,1)S(1)} %get-tuple-element.80), channel_id=1, source_target_pairs={{0,4},{1,5},{2,6},{3,7},{4,0},{5,1},{6,2},{7,3},{8,12},{9,13},{10,... | collective-permute-start | bytes 294920 | tf_op jit(solution)/shard_map/ppermute | solution.py:24
  63.0 4.3 %collective-permute-start.27 = (bf16[3,64,256]{2,1,0:T(8,128)(2,1)S(1)}, bf16[3,64,256]{2,1,0:T(8,128)(2,1)S(1)}, u32[]{:S(2)}, u32[]{:S(2)}) collective-permute-start(bf16[3,64,256]{2,1,0:T(8,128)(2,1)S(1)} %add_convert_fusion.3), channel_id=1, source_target_pairs={{0,16},{1,17},{2,18},{3,19},{4,20},{5,21},{6,22},{7,23},{8,24},{9,... | collective-permute-start | bytes 294920 | tf_op jit(solution)/shard_map/ppermute | solution.py:24
  67.3 3.2 %collective-permute-done.27 = bf16[3,64,256]{2,1,0:T(8,128)(2,1)S(1)} collective-permute-done((bf16[3,64,256]{2,1,0:T(8,128)(2,1)S(1)}, bf16[3,64,256]{2,1,0:T(8,128)(2,1)S(1)}, u32[]{:S(2)}, u32[]{:S(2)}) %collective-permute-start.27) | collective-permute-done | bytes 98336 | tf_op jit(solution)/shard_map/ppermute | solution.py:24
  70.8 2.3 %collective-permute-start.42 = (bf16[3,64,256]{2,1,0:T(8,128)(2,1)S(1)}, bf16[3,64,256]{2,1,0:T(8,128)(2,1)S(1)}, u32[]{:S(2)}, u32[]{:S(2)}) collective-permute-start(bf16[3,64,256]{2,1,0:T(8,128)(2,1)S(1)} %get-tuple-element.96.refs_0_), channel_id=1, source_target_pairs={{0,16},{1,17},{2,18},{3,19},{4,20},{5,21},{6,22},{7,23},{8,24},{9,... | collective-permute-start | bytes 294920 | tf_op jit(solution)/shard_map/ppermute | solution.py:24
  73.4 1.1 %collective-permute-start.37 = (bf16[3,64,256]{2,1,0:T(8,128)(2,1)S(1)}, bf16[3,64,256]{2,1,0:T(8,128)(2,1)S(1)}, u32[]{:S(2)}, u32[]{:S(2)}) collective-permute-start(bf16[3,64,256]{2,1,0:T(8,128)(2,1)S(1)} %get-tuple-element.96.refs_0_), channel_id=1, source_target_pairs={{0,4},{1,5},{2,6},{3,7},{4,0},{5,1},{6,2},{7,3},{8,12},{9,13},{10,... | collective-permute-start | bytes 294920 | tf_op jit(solution)/shard_map/ppermute | solution.py:24
  74.5 1.3 %collective-permute-start.36 = (bf16[3,64,256]{2,1,0:T(8,128)(2,1)S(1)}, bf16[3,64,256]{2,1,0:T(8,128)(2,1)S(1)}, u32[]{:S(2)}, u32[]{:S(2)}) collective-permute-start(bf16[3,64,256]{2,1,0:T(8,128)(2,1)S(1)} %get-tuple-element.96.refs_0_), channel_id=1, source_target_pairs={{0,2},{1,3},{2,0},{3,1},{4,6},{5,7},{6,4},{7,5},{8,10},{9,11},{10,... | collective-permute-start | bytes 294920 | tf_op jit(solution)/shard_map/ppermute | solution.py:24
  75.7 0.7 collective-permute-done.42.refs_8_
  76.4 1.3 %collective-permute-done.39.refs_4_ = bf16[3,64,256]{2,1,0:T(8,128)(2,1)S(1)} collective-permute-done((bf16[3,64,256]{2,1,0:T(8,128)(2,1)S(1)}, bf16[3,64,256]{2,1,0:T(8,128)(2,1)S(1)}, u32[]{:S(2)}, u32[]{:S(2)}) %collective-permute-start.39) | collective-permute-done | bytes 98336 | tf_op jit(solution)/shard_map/ppermute | solution.py:24
  77.7 0.9 collective-permute-start.40
  79.0 0.8 collective-permute-done.36.refs_1_
  79.7 1.0 collective-permute-start.41
  80.7 1.0 %collective-permute-start.43 = (bf16[3,64,256]{2,1,0:T(8,128)(2,1)S(1)}, bf16[3,64,256]{2,1,0:T(8,128)(2,1)S(1)}, u32[]{:S(2)}, u32[]{:S(2)}) collective-permute-start(bf16[3,64,256]{2,1,0:T(8,128)(2,1)S(1)} %collective-permute-done.42.refs_8_), channel_id=1, source_target_pairs={{0,2},{1,3},{2,0},{3,1},{4,6},{5,7},{6,4},{7,5},{8,10},{9,11},{10,... | collective-permute-start | bytes 294920 | tf_op jit(solution)/shard_map/ppermute | solution.py:24
  81.7 0.6 collective-permute-done.40.refs_5_
  82.3 0.9 collective-permute-start.49
  83.2 1.0 %collective-permute-start.47 = (bf16[3,64,256]{2,1,0:T(8,128)(2,1)S(1)}, bf16[3,64,256]{2,1,0:T(8,128)(2,1)S(1)}, u32[]{:S(2)}, u32[]{:S(2)}) collective-permute-start(bf16[3,64,256]{2,1,0:T(8,128)(2,1)S(1)} %collective-permute-done.46.refs_12_), channel_id=1, source_target_pairs={{0,2},{1,3},{2,0},{3,1},{4,6},{5,7},{6,4},{7,5},{8,10},{9,11},{10,... | collective-permute-start | bytes 294920 | tf_op jit(solution)/shard_map/ppermute | solution.py:24
  84.3 1.1 %collective-permute-start.38 = (bf16[3,64,256]{2,1,0:T(8,128)(2,1)S(1)}, bf16[3,64,256]{2,1,0:T(8,128)(2,1)S(1)}, u32[]{:S(2)}, u32[]{:S(2)}) collective-permute-start(bf16[3,64,256]{2,1,0:T(8,128)(2,1)S(1)} %collective-permute-done.36.refs_1_), channel_id=1, source_target_pairs={{0,4},{1,5},{2,6},{3,7},{4,0},{5,1},{6,2},{7,3},{8,12},{9,13},{10,... | collective-permute-start | bytes 294920 | tf_op jit(solution)/shard_map/ppermute | solution.py:24
  85.4 1.0 collective-permute-start.45
  86.4 1.0 %collective-permute-start.44 = (bf16[3,64,256]{2,1,0:T(8,128)(2,1)S(1)}, bf16[3,64,256]{2,1,0:T(8,128)(2,1)S(1)}, u32[]{:S(2)}, u32[]{:S(2)}) collective-permute-start(bf16[3,64,256]{2,1,0:T(8,128)(2,1)S(1)} %collective-permute-done.41.refs_6_), channel_id=1, source_target_pairs={{0,2},{1,3},{2,0},{3,1},{4,6},{5,7},{6,4},{7,5},{8,10},{9,11},{10,... | collective-permute-start | bytes 294920 | tf_op jit(solution)/shard_map/ppermute | solution.py:24
  87.8 1.2 %collective-permute-start.48 = (bf16[3,64,256]{2,1,0:T(8,128)(2,1)S(1)}, bf16[3,64,256]{2,1,0:T(8,128)(2,1)S(1)}, u32[]{:S(2)}, u32[]{:S(2)}) collective-permute-start(bf16[3,64,256]{2,1,0:T(8,128)(2,1)S(1)} %collective-permute-done.43.refs_9_), channel_id=1, source_target_pairs={{0,4},{1,5},{2,6},{3,7},{4,0},{5,1},{6,2},{7,3},{8,12},{9,13},{10,... | collective-permute-start | bytes 294920 | tf_op jit(solution)/shard_map/ppermute | solution.py:24
  89.0 0.9 collective-permute-start.50
  90.0 1.0 collective-permute-done.44.refs_7_
  91.0 2.6 %collective-permute-done.50.refs_15_ = bf16[3,64,256]{2,1,0:T(8,128)(2,1)S(1)} collective-permute-done((bf16[3,64,256]{2,1,0:T(8,128)(2,1)S(1)}, bf16[3,64,256]{2,1,0:T(8,128)(2,1)S(1)}, u32[]{:S(2)}, u32[]{:S(2)}) %collective-permute-start.50) | collective-permute-done | bytes 98336 | tf_op jit(solution)/shard_map/ppermute | solution.py:24
  93.6 2.1 %expert_outputs.1 = (bf16[256,1024]{1,0:T(8,128)(2,1)S(1)}, bf16[256,1024]{1,0:T(8,128)(2,1)S(1)}) custom-call(bf16[3,64,256]{2,1,0:T(8,128)(2,1)S(1)} %get-tuple-element.96.refs_0_, bf16[3,64,256]{2,1,0:T(8,128)(2,1)S(1)} %collective-permute-done.36.refs_1_, bf16[3,64,256]{2,1,0:T(8,128)(2,1)S(1)} %collective-permute-done.37.refs_2_, ...), custom_call_target="tpu_custom_call" | custom-call | flops 805306368 | bytes 3670016 | tf_op jit(solution)/shard_map/expert_outputs/pallas_call | solution.py:163
  95.9 0.8 slice_bitcast_fusion
  96.7 1.0 %collective-permute-done.51 = bf16[256,1024]{1,0:T(8,128)(2,1)S(1)} collective-permute-done((bf16[256,1024]{1,0:T(8,128)(2,1)S(1)}, bf16[256,1024]{1,0:T(8,128)(2,1)S(1)}, u32[]{:S(2)}, u32[]{:S(2)}) %collective-permute-start.51) | collective-permute-done | bytes 524320 | tf_op jit(solution)/shard_map/ppermute | solution.py:24
  97.7 0.8 select_bitcast_fusion
  (74 shorter events, 7.9 us)
Async XLA Ops:
  0.6 4.7 %collective-permute-start.3 = (bf16[256,1024]{1,0:T(8,128)(2,1)}, bf16[256,1024]{1,0:T(8,128)(2,1)S(1)}, u32[]{:S(2)}, u32[]{:S(2)}) collective-permute-start(bf16[256,1024]{1,0:T(8,128)(2,1)} %bitcast.52), channel_id=1, source_target_pairs={{0,1},{1,0},{2,3},{3,2},{4,5},{5,4},{6,7},{7,6},{8,9},{9,8},{10,11... | collective-permute-start | bytes 1572872 | tf_op jit(solution)/shard_map/ppermute | solution.py:24
  1.1 4.2 %collective-permute-start.4 = (bf16[256,1024]{1,0:T(8,128)(2,1)}, bf16[256,1024]{1,0:T(8,128)(2,1)S(1)}, u32[]{:S(2)}, u32[]{:S(2)}) collective-permute-start(bf16[256,1024]{1,0:T(8,128)(2,1)} %bitcast.55), channel_id=1, source_target_pairs={{0,1},{1,0},{2,3},{3,2},{4,5},{5,4},{6,7},{7,6},{8,9},{9,8},{10,11... | collective-permute-start | bytes 1572872 | tf_op jit(solution)/shard_map/ppermute | solution.py:24
  1.2 4.8 %collective-permute-start.1 = (bf16[256,1024]{1,0:T(8,128)(2,1)}, bf16[256,1024]{1,0:T(8,128)(2,1)S(1)}, u32[]{:S(2)}, u32[]{:S(2)}) collective-permute-start(bf16[256,1024]{1,0:T(8,128)(2,1)} %bitcast.58), channel_id=1, source_target_pairs={{0,1},{1,0},{2,3},{3,2},{4,5},{5,4},{6,7},{7,6},{8,9},{9,8},{10,11... | collective-permute-start | bytes 1572872 | tf_op jit(solution)/shard_map/ppermute | solution.py:24
  2.8 2.6 %copy-start = (bf16[1,256,1024]{2,1,0:T(8,128)(2,1)S(1)}, bf16[1,256,1024]{2,1,0:T(8,128)(2,1)}, u32[]{:S(2)}) copy-start(bf16[1,256,1024]{2,1,0:T(8,128)(2,1)} %param.12) | copy-start | bytes 1572868
  2.8 2.6 %copy-start.1 = (bf16[1,256,1024]{2,1,0:T(8,128)(2,1)S(1)}, bf16[1,256,1024]{2,1,0:T(8,128)(2,1)}, u32[]{:S(2)}) copy-start(bf16[1,256,1024]{2,1,0:T(8,128)(2,1)} %param.13) | copy-start | bytes 1572868
  2.9 3.1 %collective-permute-start = (f32[3,3,32,256]{3,2,1,0:T(8,128)S(1)}, f32[3,3,32,256]{3,2,1,0:T(8,128)S(1)}, u32[]{:S(2)}, u32[]{:S(2)}) collective-permute-start(f32[3,3,32,256]{3,2,1,0:T(8,128)S(1)} %get-tuple-element.107), channel_id=1, source_target_pairs={{0,1},{1,0},{2,3},{3,2},{4,5},{5,4},{6,7},{7,6},{8,9},{9,8},{10,11... | collective-permute-start | bytes 884744 | tf_op jit(solution)/shard_map/ppermute | solution.py:24
  3.0 3.0 %collective-permute-start.2 = (s32[1]{0:T(128)}, s32[1]{0:T(128)}, u32[]{:S(2)}, u32[]{:S(2)}) collective-permute-start(s32[1]{0:T(128)} %param.17), channel_id=1, source_target_pairs={{0,1},{1,0},{2,3},{3,2},{4,5},{5,4},{6,7},{7,6},{8,9},{9,8},{10,11... | collective-permute-start | bytes 20 | tf_op jit(solution)/shard_map/ppermute | solution.py:24
  3.5 0.7 copy-start.5
  6.0 0.7 copy-start.4
  7.9 27.2 %copy-start.3 = (s32[32]{0:T(128)S(1)}, s32[32]{0:T(128)}, u32[]{:S(2)}) copy-start(s32[32]{0:T(128)} %slots.1) | copy-start | bytes 388
  7.9 9.3 %collective-permute-start.11 = (bf16[3,64,256]{2,1,0:T(8,128)(2,1)S(1)}, bf16[3,64,256]{2,1,0:T(8,128)(2,1)S(1)}, u32[]{:S(2)}, u32[]{:S(2)}) collective-permute-start(bf16[3,64,256]{2,1,0:T(8,128)(2,1)S(1)} %fusion.4.refs_0_), channel_id=1, source_target_pairs={{0,16},{1,17},{2,18},{3,19},{4,20},{5,21},{6,22},{7,23},{8,24},{9,... | collective-permute-start | bytes 294920 | tf_op jit(solution)/shard_map/ppermute | solution.py:24
  11.7 6.3 %collective-permute-start.8 = (bf16[3,64,256]{2,1,0:T(8,128)(2,1)S(1)}, bf16[3,64,256]{2,1,0:T(8,128)(2,1)S(1)}, u32[]{:S(2)}, u32[]{:S(2)}) collective-permute-start(bf16[3,64,256]{2,1,0:T(8,128)(2,1)S(1)} %fusion.4.refs_0_), channel_id=1, source_target_pairs={{0,8},{1,9},{2,10},{3,11},{4,12},{5,13},{6,14},{7,15},{8,0},{9,1},... | collective-permute-start | bytes 294920 | tf_op jit(solution)/shard_map/ppermute | solution.py:24
  13.2 6.2 %collective-permute-start.5 = (bf16[3,64,256]{2,1,0:T(8,128)(2,1)S(1)}, bf16[3,64,256]{2,1,0:T(8,128)(2,1)S(1)}, u32[]{:S(2)}, u32[]{:S(2)}) collective-permute-start(bf16[3,64,256]{2,1,0:T(8,128)(2,1)S(1)} %fusion.4.refs_0_), channel_id=1, source_target_pairs={{0,2},{1,3},{2,0},{3,1},{4,6},{5,7},{6,4},{7,5},{8,10},{9,11},{10,... | collective-permute-start | bytes 294920 | tf_op jit(solution)/shard_map/ppermute | solution.py:24
  14.7 6.2 %collective-permute-start.6 = (bf16[3,64,256]{2,1,0:T(8,128)(2,1)S(1)}, bf16[3,64,256]{2,1,0:T(8,128)(2,1)S(1)}, u32[]{:S(2)}, u32[]{:S(2)}) collective-permute-start(bf16[3,64,256]{2,1,0:T(8,128)(2,1)S(1)} %fusion.4.refs_0_), channel_id=1, source_target_pairs={{0,4},{1,5},{2,6},{3,7},{4,0},{5,1},{6,2},{7,3},{8,12},{9,13},{10,... | collective-permute-start | bytes 294920 | tf_op jit(solution)/shard_map/ppermute | solution.py:24
  17.3 4.6 %collective-permute-start.15 = (bf16[3,64,256]{2,1,0:T(8,128)(2,1)S(1)}, bf16[3,64,256]{2,1,0:T(8,128)(2,1)S(1)}, u32[]{:S(2)}, u32[]{:S(2)}) collective-permute-start(bf16[3,64,256]{2,1,0:T(8,128)(2,1)S(1)} %collective-permute-done.11.refs_8_), channel_id=1, source_target_pairs={{0,8},{1,9},{2,10},{3,11},{4,12},{5,13},{6,14},{7,15},{8,0},{9,1},... | collective-permute-start | bytes 294920 | tf_op jit(solution)/shard_map/ppermute | solution.py:24
  17.9 4.6 %collective-permute-start.9 = (bf16[3,64,256]{2,1,0:T(8,128)(2,1)S(1)}, bf16[3,64,256]{2,1,0:T(8,128)(2,1)S(1)}, u32[]{:S(2)}, u32[]{:S(2)}) collective-permute-start(bf16[3,64,256]{2,1,0:T(8,128)(2,1)S(1)} %collective-permute-done.8.refs_4_), channel_id=1, source_target_pairs={{0,2},{1,3},{2,0},{3,1},{4,6},{5,7},{6,4},{7,5},{8,10},{9,11},{10,... | collective-permute-start | bytes 294920 | tf_op jit(solution)/shard_map/ppermute | solution.py:24
  19.4 7.4 %collective-permute-start.10 = (bf16[3,64,256]{2,1,0:T(8,128)(2,1)S(1)}, bf16[3,64,256]{2,1,0:T(8,128)(2,1)S(1)}, u32[]{:S(2)}, u32[]{:S(2)}) collective-permute-start(bf16[3,64,256]{2,1,0:T(8,128)(2,1)S(1)} %collective-permute-done.8.refs_4_), channel_id=1, source_target_pairs={{0,4},{1,5},{2,6},{3,7},{4,0},{5,1},{6,2},{7,3},{8,12},{9,13},{10,... | collective-permute-start | bytes 294920 | tf_op jit(solution)/shard_map/ppermute | solution.py:24
  20.9 7.6 %collective-permute-start.12 = (bf16[3,64,256]{2,1,0:T(8,128)(2,1)S(1)}, bf16[3,64,256]{2,1,0:T(8,128)(2,1)S(1)}, u32[]{:S(2)}, u32[]{:S(2)}) collective-permute-start(bf16[3,64,256]{2,1,0:T(8,128)(2,1)S(1)} %collective-permute-done.11.refs_8_), channel_id=1, source_target_pairs={{0,2},{1,3},{2,0},{3,1},{4,6},{5,7},{6,4},{7,5},{8,10},{9,11},{10,... | collective-permute-start | bytes 294920 | tf_op jit(solution)/shard_map/ppermute | solution.py:24
  22.5 6.4 %collective-permute-start.16 = (bf16[3,64,256]{2,1,0:T(8,128)(2,1)S(1)}, bf16[3,64,256]{2,1,0:T(8,128)(2,1)S(1)}, u32[]{:S(2)}, u32[]{:S(2)}) collective-permute-start(bf16[3,64,256]{2,1,0:T(8,128)(2,1)S(1)} %collective-permute-done.15.refs_12_), channel_id=1, source_target_pairs={{0,2},{1,3},{2,0},{3,1},{4,6},{5,7},{6,4},{7,5},{8,10},{9,11},{10,... | collective-permute-start | bytes 294920 | tf_op jit(solution)/shard_map/ppermute | solution.py:24
  24.8 5.0 %collective-permute-start.18 = (bf16[3,64,256]{2,1,0:T(8,128)(2,1)S(1)}, bf16[3,64,256]{2,1,0:T(8,128)(2,1)S(1)}, u32[]{:S(2)}, u32[]{:S(2)}) collective-permute-start(bf16[3,64,256]{2,1,0:T(8,128)(2,1)S(1)} %collective-permute-done.15.refs_12_), channel_id=1, source_target_pairs={{0,4},{1,5},{2,6},{3,7},{4,0},{5,1},{6,2},{7,3},{8,12},{9,13},{10,... | collective-permute-start | bytes 294920 | tf_op jit(solution)/shard_map/ppermute | solution.py:24
  26.4 5.7 %collective-permute-start.7 = (bf16[3,64,256]{2,1,0:T(8,128)(2,1)S(1)}, bf16[3,64,256]{2,1,0:T(8,128)(2,1)S(1)}, u32[]{:S(2)}, u32[]{:S(2)}) collective-permute-start(bf16[3,64,256]{2,1,0:T(8,128)(2,1)S(1)} %collective-permute-done.5.refs_1_), channel_id=1, source_target_pairs={{0,4},{1,5},{2,6},{3,7},{4,0},{5,1},{6,2},{7,3},{8,12},{9,13},{10,... | collective-permute-start | bytes 294920 | tf_op jit(solution)/shard_map/ppermute | solution.py:24
  26.8 6.0 %collective-permute-start.14 = (bf16[3,64,256]{2,1,0:T(8,128)(2,1)S(1)}, bf16[3,64,256]{2,1,0:T(8,128)(2,1)S(1)}, u32[]{:S(2)}, u32[]{:S(2)}) collective-permute-start(bf16[3,64,256]{2,1,0:T(8,128)(2,1)S(1)} %collective-permute-done.11.refs_8_), channel_id=1, source_target_pairs={{0,4},{1,5},{2,6},{3,7},{4,0},{5,1},{6,2},{7,3},{8,12},{9,13},{10,... | collective-permute-start | bytes 294920 | tf_op jit(solution)/shard_map/ppermute | solution.py:24
  28.5 4.6 %collective-permute-start.13 = (bf16[3,64,256]{2,1,0:T(8,128)(2,1)S(1)}, bf16[3,64,256]{2,1,0:T(8,128)(2,1)S(1)}, u32[]{:S(2)}, u32[]{:S(2)}) collective-permute-start(bf16[3,64,256]{2,1,0:T(8,128)(2,1)S(1)} %collective-permute-done.10.refs_6_), channel_id=1, source_target_pairs={{0,2},{1,3},{2,0},{3,1},{4,6},{5,7},{6,4},{7,5},{8,10},{9,11},{10,... | collective-permute-start | bytes 294920 | tf_op jit(solution)/shard_map/ppermute | solution.py:24
  29.8 4.6 %collective-permute-start.19 = (bf16[3,64,256]{2,1,0:T(8,128)(2,1)S(1)}, bf16[3,64,256]{2,1,0:T(8,128)(2,1)S(1)}, u32[]{:S(2)}, u32[]{:S(2)}) collective-permute-start(bf16[3,64,256]{2,1,0:T(8,128)(2,1)S(1)} %collective-permute-done.18.refs_14_), channel_id=1, source_target_pairs={{0,2},{1,3},{2,0},{3,1},{4,6},{5,7},{6,4},{7,5},{8,10},{9,11},{10,... | collective-permute-start | bytes 294920 | tf_op jit(solution)/shard_map/ppermute | solution.py:24
  30.5 4.6 %collective-permute-start.17 = (bf16[3,64,256]{2,1,0:T(8,128)(2,1)S(1)}, bf16[3,64,256]{2,1,0:T(8,128)(2,1)S(1)}, u32[]{:S(2)}, u32[]{:S(2)}) collective-permute-start(bf16[3,64,256]{2,1,0:T(8,128)(2,1)S(1)} %collective-permute-done.12.refs_9_), channel_id=1, source_target_pairs={{0,4},{1,5},{2,6},{3,7},{4,0},{5,1},{6,2},{7,3},{8,12},{9,13},{10,... | collective-permute-start | bytes 294920 | tf_op jit(solution)/shard_map/ppermute | solution.py:24
  39.2 5.3 %collective-permute-start.20 = (bf16[3,64,256]{2,1,0:T(8,128)(2,1)S(1)}, bf16[3,64,256]{2,1,0:T(8,128)(2,1)S(1)}, u32[]{:S(2)}, u32[]{:S(2)}) collective-permute-start(bf16[3,64,256]{2,1,0:T(8,128)(2,1)S(1)} %get-tuple-element.66), channel_id=1, source_target_pairs={{0,4},{1,5},{2,6},{3,7},{4,0},{5,1},{6,2},{7,3},{8,12},{9,13},{10,... | collective-permute-start | bytes 294920 | tf_op jit(solution)/shard_map/ppermute | solution.py:24
  40.3 6.4 %collective-permute-start.22 = (bf16[3,64,256]{2,1,0:T(8,128)(2,1)S(1)}, bf16[3,64,256]{2,1,0:T(8,128)(2,1)S(1)}, u32[]{:S(2)}, u32[]{:S(2)}) collective-permute-start(bf16[3,64,256]{2,1,0:T(8,128)(2,1)S(1)} %get-tuple-element.68), channel_id=1, source_target_pairs={{0,2},{1,3},{2,0},{3,1},{4,6},{5,7},{6,4},{7,5},{8,10},{9,11},{10,... | collective-permute-start | bytes 294920 | tf_op jit(solution)/shard_map/ppermute | solution.py:24
  42.3 8.5 %collective-permute-start.24 = (bf16[3,64,256]{2,1,0:T(8,128)(2,1)S(1)}, bf16[3,64,256]{2,1,0:T(8,128)(2,1)S(1)}, u32[]{:S(2)}, u32[]{:S(2)}) collective-permute-start(bf16[3,64,256]{2,1,0:T(8,128)(2,1)S(1)} %get-tuple-element.71), channel_id=1, source_target_pairs={{0,2},{1,3},{2,0},{3,1},{4,6},{5,7},{6,4},{7,5},{8,10},{9,11},{10,... | collective-permute-start | bytes 294920 | tf_op jit(solution)/shard_map/ppermute | solution.py:24
  44.6 4.7 %collective-permute-start.30 = (bf16[3,64,256]{2,1,0:T(8,128)(2,1)S(1)}, bf16[3,64,256]{2,1,0:T(8,128)(2,1)S(1)}, u32[]{:S(2)}, u32[]{:S(2)}) collective-permute-start(bf16[3,64,256]{2,1,0:T(8,128)(2,1)S(1)} %get-tuple-element.79), channel_id=1, source_target_pairs={{0,2},{1,3},{2,0},{3,1},{4,6},{5,7},{6,4},{7,5},{8,10},{9,11},{10,... | collective-permute-start | bytes 294920 | tf_op jit(solution)/shard_map/ppermute | solution.py:24
  46.0 13.6 %collective-permute-start.21 = (bf16[3,64,256]{2,1,0:T(8,128)(2,1)S(1)}, bf16[3,64,256]{2,1,0:T(8,128)(2,1)S(1)}, u32[]{:S(2)}, u32[]{:S(2)}) collective-permute-start(bf16[3,64,256]{2,1,0:T(8,128)(2,1)S(1)} %add_convert_fusion.6), channel_id=1, source_target_pairs={{0,2},{1,3},{2,0},{3,1},{4,6},{5,7},{6,4},{7,5},{8,10},{9,11},{10,... | collective-permute-start | bytes 294920 | tf_op jit(solution)/shard_map/ppermute | solution.py:24
  46.7 12.9 %collective-permute-start.23 = (bf16[3,64,256]{2,1,0:T(8,128)(2,1)S(1)}, bf16[3,64,256]{2,1,0:T(8,128)(2,1)S(1)}, u32[]{:S(2)}, u32[]{:S(2)}) collective-permute-start(bf16[3,64,256]{2,1,0:T(8,128)(2,1)S(1)} %get-tuple-element.69), channel_id=1, source_target_pairs={{0,4},{1,5},{2,6},{3,7},{4,0},{5,1},{6,2},{7,3},{8,12},{9,13},{10,... | collective-permute-start | bytes 294920 | tf_op jit(solution)/shard_map/ppermute | solution.py:24
  48.0 4.7 %collective-permute-start.25 = (bf16[3,64,256]{2,1,0:T(8,128)(2,1)S(1)}, bf16[3,64,256]{2,1,0:T(8,128)(2,1)S(1)}, u32[]{:S(2)}, u32[]{:S(2)}) collective-permute-start(bf16[3,64,256]{2,1,0:T(8,128)(2,1)S(1)} %add_convert_fusion.5), channel_id=1, source_target_pairs={{0,4},{1,5},{2,6},{3,7},{4,0},{5,1},{6,2},{7,3},{8,12},{9,13},{10,... | collective-permute-start | bytes 294920 | tf_op jit(solution)/shard_map/ppermute | solution.py:24
  49.3 6.3 %collective-permute-start.33 = (bf16[3,64,256]{2,1,0:T(8,128)(2,1)S(1)}, bf16[3,64,256]{2,1,0:T(8,128)(2,1)S(1)}, u32[]{:S(2)}, u32[]{:S(2)}) collective-permute-start(bf16[3,64,256]{2,1,0:T(8,128)(2,1)S(1)} %add_convert_fusion.1), channel_id=1, source_target_pairs={{0,4},{1,5},{2,6},{3,7},{4,0},{5,1},{6,2},{7,3},{8,12},{9,13},{10,... | collective-permute-start | bytes 294920 | tf_op jit(solution)/shard_map/ppermute | solution.py:24
  52.6 8.0 %collective-permute-start.28 = (bf16[3,64,256]{2,1,0:T(8,128)(2,1)S(1)}, bf16[3,64,256]{2,1,0:T(8,128)(2,1)S(1)}, u32[]{:S(2)}, u32[]{:S(2)}) collective-permute-start(bf16[3,64,256]{2,1,0:T(8,128)(2,1)S(1)} %get-tuple-element.75), channel_id=1, source_target_pairs={{0,4},{1,5},{2,6},{3,7},{4,0},{5,1},{6,2},{7,3},{8,12},{9,13},{10,... | collective-permute-start | bytes 294920 | tf_op jit(solution)/shard_map/ppermute | solution.py:24
  53.6 4.6 %collective-permute-start.32 = (bf16[3,64,256]{2,1,0:T(8,128)(2,1)S(1)}, bf16[3,64,256]{2,1,0:T(8,128)(2,1)S(1)}, u32[]{:S(2)}, u32[]{:S(2)}) collective-permute-start(bf16[3,64,256]{2,1,0:T(8,128)(2,1)S(1)} %get-tuple-element.83), channel_id=1, source_target_pairs={{0,2},{1,3},{2,0},{3,1},{4,6},{5,7},{6,4},{7,5},{8,10},{9,11},{10,... | collective-permute-start | bytes 294920 | tf_op jit(solution)/shard_map/ppermute | solution.py:24
  55.6 5.0 %collective-permute-start.26 = (bf16[3,64,256]{2,1,0:T(8,128)(2,1)S(1)}, bf16[3,64,256]{2,1,0:T(8,128)(2,1)S(1)}, u32[]{:S(2)}, u32[]{:S(2)}) collective-permute-start(bf16[3,64,256]{2,1,0:T(8,128)(2,1)S(1)} %add_convert_fusion.4), channel_id=1, source_target_pairs={{0,8},{1,9},{2,10},{3,11},{4,12},{5,13},{6,14},{7,15},{8,0},{9,1},... | collective-permute-start | bytes 294920 | tf_op jit(solution)/shard_map/ppermute | solution.py:24
  58.3 9.1 %collective-permute-start.34 = (bf16[3,64,256]{2,1,0:T(8,128)(2,1)S(1)}, bf16[3,64,256]{2,1,0:T(8,128)(2,1)S(1)}, u32[]{:S(2)}, u32[]{:S(2)}) collective-permute-start(bf16[3,64,256]{2,1,0:T(8,128)(2,1)S(1)} %add_convert_fusion), channel_id=1, source_target_pairs={{0,8},{1,9},{2,10},{3,11},{4,12},{5,13},{6,14},{7,15},{8,0},{9,1},... | collective-permute-start | bytes 294920 | tf_op jit(solution)/shard_map/ppermute | solution.py:24
  60.7 6.6 %collective-permute-start.29 = (bf16[3,64,256]{2,1,0:T(8,128)(2,1)S(1)}, bf16[3,64,256]{2,1,0:T(8,128)(2,1)S(1)}, u32[]{:S(2)}, u32[]{:S(2)}) collective-permute-start(bf16[3,64,256]{2,1,0:T(8,128)(2,1)S(1)} %add_convert_fusion.2), channel_id=1, source_target_pairs={{0,2},{1,3},{2,0},{3,1},{4,6},{5,7},{6,4},{7,5},{8,10},{9,11},{10,... | collective-permute-start | bytes 294920 | tf_op jit(solution)/shard_map/ppermute | solution.py:24
  61.4 5.9 %collective-permute-start.31 = (bf16[3,64,256]{2,1,0:T(8,128)(2,1)S(1)}, bf16[3,64,256]{2,1,0:T(8,128)(2,1)S(1)}, u32[]{:S(2)}, u32[]{:S(2)}) collective-permute-start(bf16[3,64,256]{2,1,0:T(8,128)(2,1)S(1)} %get-tuple-element.80), channel_id=1, source_target_pairs={{0,4},{1,5},{2,6},{3,7},{4,0},{5,1},{6,2},{7,3},{8,12},{9,13},{10,... | collective-permute-start | bytes 294920 | tf_op jit(solution)/shard_map/ppermute | solution.py:24
  63.0 7.5 %collective-permute-start.27 = (bf16[3,64,256]{2,1,0:T(8,128)(2,1)S(1)}, bf16[3,64,256]{2,1,0:T(8,128)(2,1)S(1)}, u32[]{:S(2)}, u32[]{:S(2)}) collective-permute-start(bf16[3,64,256]{2,1,0:T(8,128)(2,1)S(1)} %add_convert_fusion.3), channel_id=1, source_target_pairs={{0,16},{1,17},{2,18},{3,19},{4,20},{5,21},{6,22},{7,23},{8,24},{9,... | collective-permute-start | bytes 294920 | tf_op jit(solution)/shard_map/ppermute | solution.py:24
  70.8 5.7 %collective-permute-start.42 = (bf16[3,64,256]{2,1,0:T(8,128)(2,1)S(1)}, bf16[3,64,256]{2,1,0:T(8,128)(2,1)S(1)}, u32[]{:S(2)}, u32[]{:S(2)}) collective-permute-start(bf16[3,64,256]{2,1,0:T(8,128)(2,1)S(1)} %get-tuple-element.96.refs_0_), channel_id=1, source_target_pairs={{0,16},{1,17},{2,18},{3,19},{4,20},{5,21},{6,22},{7,23},{8,24},{9,... | collective-permute-start | bytes 294920 | tf_op jit(solution)/shard_map/ppermute | solution.py:24
  73.1 4.6 %collective-permute-start.39 = (bf16[3,64,256]{2,1,0:T(8,128)(2,1)S(1)}, bf16[3,64,256]{2,1,0:T(8,128)(2,1)S(1)}, u32[]{:S(2)}, u32[]{:S(2)}) collective-permute-start(bf16[3,64,256]{2,1,0:T(8,128)(2,1)S(1)} %get-tuple-element.96.refs_0_), channel_id=1, source_target_pairs={{0,8},{1,9},{2,10},{3,11},{4,12},{5,13},{6,14},{7,15},{8,0},{9,1},... | collective-permute-start | bytes 294920 | tf_op jit(solution)/shard_map/ppermute | solution.py:24
  73.4 5.6 %collective-permute-start.37 = (bf16[3,64,256]{2,1,0:T(8,128)(2,1)S(1)}, bf16[3,64,256]{2,1,0:T(8,128)(2,1)S(1)}, u32[]{:S(2)}, u32[]{:S(2)}) collective-permute-start(bf16[3,64,256]{2,1,0:T(8,128)(2,1)S(1)} %get-tuple-element.96.refs_0_), channel_id=1, source_target_pairs={{0,4},{1,5},{2,6},{3,7},{4,0},{5,1},{6,2},{7,3},{8,12},{9,13},{10,... | collective-permute-start | bytes 294920 | tf_op jit(solution)/shard_map/ppermute | solution.py:24
  74.5 5.3 %collective-permute-start.36 = (bf16[3,64,256]{2,1,0:T(8,128)(2,1)S(1)}, bf16[3,64,256]{2,1,0:T(8,128)(2,1)S(1)}, u32[]{:S(2)}, u32[]{:S(2)}) collective-permute-start(bf16[3,64,256]{2,1,0:T(8,128)(2,1)S(1)} %get-tuple-element.96.refs_0_), channel_id=1, source_target_pairs={{0,2},{1,3},{2,0},{3,1},{4,6},{5,7},{6,4},{7,5},{8,10},{9,11},{10,... | collective-permute-start | bytes 294920 | tf_op jit(solution)/shard_map/ppermute | solution.py:24
  76.4 5.3 %collective-permute-start.46 = (bf16[3,64,256]{2,1,0:T(8,128)(2,1)S(1)}, bf16[3,64,256]{2,1,0:T(8,128)(2,1)S(1)}, u32[]{:S(2)}, u32[]{:S(2)}) collective-permute-start(bf16[3,64,256]{2,1,0:T(8,128)(2,1)S(1)} %collective-permute-done.42.refs_8_), channel_id=1, source_target_pairs={{0,8},{1,9},{2,10},{3,11},{4,12},{5,13},{6,14},{7,15},{8,0},{9,1},... | collective-permute-start | bytes 294920 | tf_op jit(solution)/shard_map/ppermute | solution.py:24
  77.7 4.6 %collective-permute-start.40 = (bf16[3,64,256]{2,1,0:T(8,128)(2,1)S(1)}, bf16[3,64,256]{2,1,0:T(8,128)(2,1)S(1)}, u32[]{:S(2)}, u32[]{:S(2)}) collective-permute-start(bf16[3,64,256]{2,1,0:T(8,128)(2,1)S(1)} %collective-permute-done.39.refs_4_), channel_id=1, source_target_pairs={{0,2},{1,3},{2,0},{3,1},{4,6},{5,7},{6,4},{7,5},{8,10},{9,11},{10,... | collective-permute-start | bytes 294920 | tf_op jit(solution)/shard_map/ppermute | solution.py:24
  79.7 5.6 %collective-permute-start.41 = (bf16[3,64,256]{2,1,0:T(8,128)(2,1)S(1)}, bf16[3,64,256]{2,1,0:T(8,128)(2,1)S(1)}, u32[]{:S(2)}, u32[]{:S(2)}) collective-permute-start(bf16[3,64,256]{2,1,0:T(8,128)(2,1)S(1)} %collective-permute-done.39.refs_4_), channel_id=1, source_target_pairs={{0,4},{1,5},{2,6},{3,7},{4,0},{5,1},{6,2},{7,3},{8,12},{9,13},{10,... | collective-permute-start | bytes 294920 | tf_op jit(solution)/shard_map/ppermute | solution.py:24
  80.7 5.7 %collective-permute-start.43 = (bf16[3,64,256]{2,1,0:T(8,128)(2,1)S(1)}, bf16[3,64,256]{2,1,0:T(8,128)(2,1)S(1)}, u32[]{:S(2)}, u32[]{:S(2)}) collective-permute-start(bf16[3,64,256]{2,1,0:T(8,128)(2,1)S(1)} %collective-permute-done.42.refs_8_), channel_id=1, source_target_pairs={{0,2},{1,3},{2,0},{3,1},{4,6},{5,7},{6,4},{7,5},{8,10},{9,11},{10,... | collective-permute-start | bytes 294920 | tf_op jit(solution)/shard_map/ppermute | solution.py:24
  82.3 6.6 %collective-permute-start.49 = (bf16[3,64,256]{2,1,0:T(8,128)(2,1)S(1)}, bf16[3,64,256]{2,1,0:T(8,128)(2,1)S(1)}, u32[]{:S(2)}, u32[]{:S(2)}) collective-permute-start(bf16[3,64,256]{2,1,0:T(8,128)(2,1)S(1)} %collective-permute-done.46.refs_12_), channel_id=1, source_target_pairs={{0,4},{1,5},{2,6},{3,7},{4,0},{5,1},{6,2},{7,3},{8,12},{9,13},{10,... | collective-permute-start | bytes 294920 | tf_op jit(solution)/shard_map/ppermute | solution.py:24
  83.2 4.6 %collective-permute-start.47 = (bf16[3,64,256]{2,1,0:T(8,128)(2,1)S(1)}, bf16[3,64,256]{2,1,0:T(8,128)(2,1)S(1)}, u32[]{:S(2)}, u32[]{:S(2)}) collective-permute-start(bf16[3,64,256]{2,1,0:T(8,128)(2,1)S(1)} %collective-permute-done.46.refs_12_), channel_id=1, source_target_pairs={{0,2},{1,3},{2,0},{3,1},{4,6},{5,7},{6,4},{7,5},{8,10},{9,11},{10,... | collective-permute-start | bytes 294920 | tf_op jit(solution)/shard_map/ppermute | solution.py:24
  84.3 9.4 %copy-start.2 = (bf16[1,256,1024]{2,1,0:T(8,128)(2,1)S(1)}, bf16[1,256,1024]{2,1,0:T(8,128)(2,1)}, u32[]{:S(2)}) copy-start(bf16[1,256,1024]{2,1,0:T(8,128)(2,1)} %param.14) | copy-start | bytes 1572868
  84.3 5.7 %collective-permute-start.38 = (bf16[3,64,256]{2,1,0:T(8,128)(2,1)S(1)}, bf16[3,64,256]{2,1,0:T(8,128)(2,1)S(1)}, u32[]{:S(2)}, u32[]{:S(2)}) collective-permute-start(bf16[3,64,256]{2,1,0:T(8,128)(2,1)S(1)} %collective-permute-done.36.refs_1_), channel_id=1, source_target_pairs={{0,4},{1,5},{2,6},{3,7},{4,0},{5,1},{6,2},{7,3},{8,12},{9,13},{10,... | collective-permute-start | bytes 294920 | tf_op jit(solution)/shard_map/ppermute | solution.py:24
  85.4 4.6 %collective-permute-start.45 = (bf16[3,64,256]{2,1,0:T(8,128)(2,1)S(1)}, bf16[3,64,256]{2,1,0:T(8,128)(2,1)S(1)}, u32[]{:S(2)}, u32[]{:S(2)}) collective-permute-start(bf16[3,64,256]{2,1,0:T(8,128)(2,1)S(1)} %collective-permute-done.42.refs_8_), channel_id=1, source_target_pairs={{0,4},{1,5},{2,6},{3,7},{4,0},{5,1},{6,2},{7,3},{8,12},{9,13},{10,... | collective-permute-start | bytes 294920 | tf_op jit(solution)/shard_map/ppermute | solution.py:24
  86.4 4.6 %collective-permute-start.44 = (bf16[3,64,256]{2,1,0:T(8,128)(2,1)S(1)}, bf16[3,64,256]{2,1,0:T(8,128)(2,1)S(1)}, u32[]{:S(2)}, u32[]{:S(2)}) collective-permute-start(bf16[3,64,256]{2,1,0:T(8,128)(2,1)S(1)} %collective-permute-done.41.refs_6_), channel_id=1, source_target_pairs={{0,2},{1,3},{2,0},{3,1},{4,6},{5,7},{6,4},{7,5},{8,10},{9,11},{10,... | collective-permute-start | bytes 294920 | tf_op jit(solution)/shard_map/ppermute | solution.py:24
  87.8 5.8 %collective-permute-start.48 = (bf16[3,64,256]{2,1,0:T(8,128)(2,1)S(1)}, bf16[3,64,256]{2,1,0:T(8,128)(2,1)S(1)}, u32[]{:S(2)}, u32[]{:S(2)}) collective-permute-start(bf16[3,64,256]{2,1,0:T(8,128)(2,1)S(1)} %collective-permute-done.43.refs_9_), channel_id=1, source_target_pairs={{0,4},{1,5},{2,6},{3,7},{4,0},{5,1},{6,2},{7,3},{8,12},{9,13},{10,... | collective-permute-start | bytes 294920 | tf_op jit(solution)/shard_map/ppermute | solution.py:24
  89.0 4.6 %collective-permute-start.50 = (bf16[3,64,256]{2,1,0:T(8,128)(2,1)S(1)}, bf16[3,64,256]{2,1,0:T(8,128)(2,1)S(1)}, u32[]{:S(2)}, u32[]{:S(2)}) collective-permute-start(bf16[3,64,256]{2,1,0:T(8,128)(2,1)S(1)} %collective-permute-done.49.refs_14_), channel_id=1, source_target_pairs={{0,2},{1,3},{2,0},{3,1},{4,6},{5,7},{6,4},{7,5},{8,10},{9,11},{10,... | collective-permute-start | bytes 294920 | tf_op jit(solution)/shard_map/ppermute | solution.py:24
  89.9 5.9 %collective-permute-start.35 = (f32[3,3,32,256]{3,2,1,0:T(8,128)S(1)}, f32[3,3,32,256]{3,2,1,0:T(8,128)S(1)}, u32[]{:S(2)}, u32[]{:S(2)}) collective-permute-start(f32[3,3,32,256]{3,2,1,0:T(8,128)S(1)} %get-tuple-element.105), channel_id=1, source_target_pairs={{0,1},{1,0},{2,3},{3,2},{4,5},{5,4},{6,7},{7,6},{8,9},{9,8},{10,11... | collective-permute-start | bytes 884744 | tf_op jit(solution)/shard_map/ppermute | solution.py:24
  95.7 2.0 %collective-permute-start.51 = (bf16[256,1024]{1,0:T(8,128)(2,1)S(1)}, bf16[256,1024]{1,0:T(8,128)(2,1)S(1)}, u32[]{:S(2)}, u32[]{:S(2)}) collective-permute-start(bf16[256,1024]{1,0:T(8,128)(2,1)S(1)} %get-tuple-element.95), channel_id=1, source_target_pairs={{0,1},{1,0},{2,3},{3,2},{4,5},{5,4},{6,7},{7,6},{8,9},{9,8},{10,11... | collective-permute-start | bytes 1572872 | tf_op jit(solution)/shard_map/ppermute | solution.py:24

commit v4 on v3

--- a/solution.py
+++ b/solution.py
@@ -59,11 +59,20 @@
                     out[pl.ds(start, rows), part * tokens : (part + 1) * tokens] = turned[low : low + rows]
 
 
+def places(outs):
+    found = []
+    for zj in range(len(outs) // 3):
+        own, later, pair = outs[3 * zj : 3 * zj + 3]
+        by_x, by_y = ((pair, (1,)), (later, ())) if zj % 2 else ((later, ()), (pair, (1,)))
+        found += [(own, ()), by_x, by_y, (pair, (0,))]
+    return found
+
+
 def backward_kernel(count, slots, own_live, other_live, *refs):
     pieces = refs[:count]
     own_x, other_x, own_c, other_c, x_turned, c_turned = refs[count : count + 6]
-    outs = refs[count + 6 : 2 * count + 6]
-    weights, gate_grad, up_grad, hidden_all, sems = refs[2 * count + 6 :]
+    weights, gate_grad, up_grad, hidden_all, sems = refs[-5:]
+    outs = places(refs[count + 6 : -5])
     me_index = lax.axis_index("dev")
     core = me_index & CORE
     place_pieces(me_index // 2, pieces, weights, sems)
@@ -83,7 +92,7 @@
         hidden_all[span] = jnp.where(keep, gate_act * up_pre, 0.0).astype(jnp.bfloat16)
         up_grad[span] = jnp.where(keep, grad_up, 0.0).astype(jnp.bfloat16)
         gate_grad[span] = jnp.where(keep, grad_gate, 0.0).astype(jnp.bfloat16)
-    rows = outs[0].shape[1]
+    rows = pieces[0].shape[1]
     width = count * rows
     tall = min(width, 256)
     for at in range(0, width, tall):
@@ -93,19 +102,31 @@
             product = jnp.dot(left[at : at + tall], right[...], preferred_element_type=jnp.float32)
             product = product.astype(jnp.bfloat16)
             for low in range(0, tall, rows):
-                outs[(at + low) // rows][kind] = product[low : low + rows]
-
-
-def forward_kernel(count, *refs):
+                out, before = outs[(at + low) // rows]
+                out[before + (kind,)] = product[low : low + rows]
+
+
+def forward_kernel(count, slots, *refs):
     pieces = refs[:count]
-    own_y, other_y, own_out, other_out, weights, sems = refs[count:]
-    place_pieces(lax.axis_index("dev") // 2, pieces, weights, sems)
-    for y_ref, out_ref in ((other_y, other_out), (own_y, own_out)):
-        gate_pre = jnp.dot(y_ref[...], weights[0], preferred_element_type=jnp.float32)
-        up_pre = jnp.dot(y_ref[...], weights[1], preferred_element_type=jnp.float32)
-        act = (gate_pre * jax.nn.sigmoid(gate_pre) * up_pre).astype(jnp.bfloat16)
-        result = lax.dot_general(act, weights[2], (((1,), (1,)), ((), ())), preferred_element_type=jnp.float32)
-        out_ref[...] = result.astype(jnp.bfloat16)
+    y_ref, out_ref, matches, weights, sems = refs[count:]
+    me_index = lax.axis_index("dev")
+    place_pieces(me_index // 2, pieces, weights, sems)
+    matches[0] = jnp.where(slots[me_index] == (me_index & CORE), 1, 0)
+    gate_pre = jnp.dot(y_ref[...], weights[0], preferred_element_type=jnp.float32)
+    up_pre = jnp.dot(y_ref[...], weights[1], preferred_element_type=jnp.float32)
+    act = (gate_pre * jax.nn.sigmoid(gate_pre) * up_pre).astype(jnp.bfloat16)
+    result = lax.dot_general(act, weights[2], (((1,), (1,)), ((), ())), preferred_element_type=jnp.float32)
+    out_ref[...] = result.astype(jnp.bfloat16)
+
+
+def choose_kernel(matches, own_out, other_out, out, sem):
+    for wanted, source in ((1, own_out), (0, other_out)):
+
+        @pl.when(matches[0] == wanted)
+        def move():
+            copy = pltpu.make_async_copy(source, out, sem)
+            copy.start()
+            copy.wait()
 
 
 VMEM = pl.BlockSpec(memory_space=pltpu.VMEM)
@@ -134,11 +155,13 @@
     count = len(pieces)
     kinds, rows, units = pieces[0].shape
     tokens, width = own_x.shape
+    one = jax.ShapeDtypeStruct((kinds, rows, units), jnp.bfloat16)
+    two = jax.ShapeDtypeStruct((2, kinds, rows, units), jnp.bfloat16)
     return pl.pallas_call(
         functools.partial(backward_kernel, count),
-        out_shape=[jax.ShapeDtypeStruct((kinds, rows, units), jnp.bfloat16)] * count,
+        out_shape=[one, one, two] * (count // 4),
         in_specs=[SMEM] * 3 + [ANY] * count + [VMEM] * 6,
-        out_specs=[VMEM] * count,
+        out_specs=[VMEM] * (3 * count // 4),
         scratch_shapes=[
             pltpu.VMEM((kinds, width, units), jnp.bfloat16),
             pltpu.VMEM((2 * tokens, units), jnp.bfloat16),
@@ -156,27 +179,42 @@
     )(slots, own_live, other_live, *pieces, own_x, other_x, own_c, other_c, x_turned, c_turned)
 
 
-def forward(pieces, own_y, other_y):
+def forward(slots, pieces, rows_in):
     count = len(pieces)
     kinds, rows, units = pieces[0].shape
-    tokens, width = own_y.shape
+    tokens, width = rows_in.shape
     return pl.pallas_call(
         functools.partial(forward_kernel, count),
-        out_shape=[jax.ShapeDtypeStruct((tokens, width), jnp.bfloat16)] * 2,
-        in_specs=[ANY] * count + [VMEM] * 2,
-        out_specs=[VMEM] * 2,
+        out_shape=[
+            jax.ShapeDtypeStruct((tokens, width), jnp.bfloat16),
+            jax.ShapeDtypeStruct((1,), jnp.int32),
+        ],
+        in_specs=[SMEM] + [ANY] * count + [VMEM],
+        out_specs=[VMEM, SMEM],
         scratch_shapes=[
             pltpu.VMEM((kinds, width, units), jnp.bfloat16),
             pltpu.SemaphoreType.DMA((count,)),
         ],
         compiler_params=params(),
         cost_estimate=pl.CostEstimate(
-            flops=12 * tokens * width * units,
-            bytes_accessed=8 * tokens * width + 6 * width * units,
-            transcendentals=2 * tokens * units,
+            flops=6 * tokens * width * units,
+            bytes_accessed=4 * tokens * width + 6 * width * units,
+            transcendentals=tokens * units,
         ),
         name="expert_outputs",
-    )(*pieces, own_y, other_y)
+    )(slots, *pieces, rows_in)
+
+
+def choose(matches, own_out, other_out):
+    return pl.pallas_call(
+        choose_kernel,
+        out_shape=jax.ShapeDtypeStruct(own_out.shape, own_out.dtype),
+        in_specs=[SMEM, ANY, ANY],
+        out_specs=ANY,
+        scratch_shapes=[pltpu.SemaphoreType.DMA],
+        compiler_params=params(),
+        name="choose_outputs",
+    )(matches, own_out, other_out)
 
 
 def after(value, *others):
@@ -218,53 +256,51 @@
 
 def reduce_chips(pieces):
     depth = lax.axis_size("dev") // Z_UNIT
-    column = [[pieces[4 * zj]] for zj in range(depth)]
-    crossed, full, risen = (), (), ()
+    column = [[pieces[3 * zj]] for zj in range(depth)]
+    crossed, turned = (), ()
     for upper in reversed(range(1, depth, 2)):
-        along_x, along_y, across = pieces[4 * upper + 1 : 4 * upper + 4]
-        below_x, below_y, below_across = pieces[4 * upper - 3 : 4 * upper]
-        from_x = hop(after(across, *crossed), X_STEP)
-        from_y = hop(after(below_across, *full), Y_STEP)
-        along_x = hop(after(along_x, *full), X_STEP)
-        along_y = hop(add_all(along_y, from_x).astype(jnp.bfloat16), Y_STEP)
-        column[upper] += [along_x, along_y]
-        below_x = hop(after(add_all(below_x, from_y).astype(jnp.bfloat16), *risen), X_STEP)
-        below_y = hop(after(below_y, from_x, *risen), Y_STEP)
-        column[upper - 1] += [below_x, below_y]
-        crossed, full = (from_y,), (along_x, along_y)
+        up_y, pair_x = pieces[3 * upper + 1 : 3 * upper + 3]
+        below_x, pair_y = pieces[3 * upper - 2 : 3 * upper]
+        got_x = hop(after(pair_x, *crossed), X_STEP)
+        got_y = hop(after(pair_y, *turned), Y_STEP)
+        column[upper] += [got_x[1], hop(add_all(up_y, got_x[0]).astype(jnp.bfloat16), Y_STEP)]
+        column[upper - 1] += [got_y[1], hop(add_all(below_x, got_y[0]).astype(jnp.bfloat16), X_STEP)]
+        crossed, turned = (got_x,), (got_y,)
         for zj in (upper, upper - 1):
             top = 1 << zj.bit_length() - 1 if zj else 0
             low = zj - top
             if zj:
                 part = add_all(*column[zj]).astype(jnp.bfloat16)
-                risen += (hop(part, low * Z_UNIT if low else top * Z_UNIT),)
-                column[top if low else 0].append(risen[-1])
-        risen = risen[:1] + (below_x, below_y)
+                column[top if low else 0].append(hop(part, (low or top) * Z_UNIT))
     return add_all(*column[0])
 
 
 def block_a_core(master, first, second, old_rows, old_cotangent, new_rows, old_slots, new_slots, live):
     local_rows = master.shape[2]
-    me_index = lax.axis_index("dev")
-    core = me_index & CORE
-    own_new = lax.dynamic_index_in_dim(new_slots, me_index, 0, keepdims=False)
+    core = lax.axis_index("dev") & CORE
+
+    def mine(state):
+        return lax.dynamic_index_in_dim(state, core, 0, keepdims=False)
+
+    def partners(state):
+        return lax.dynamic_index_in_dim(state, 1 - core, 0, keepdims=False)
+
+    def both_rows(own, other):
+        return jnp.where(
+            core == 0, jnp.concatenate([own, other], axis=-2), jnp.concatenate([other, own], axis=-2)
+        )
 
     other_x = hop(old_rows, CORE)
     other_c = hop(old_cotangent, CORE)
-    state = jnp.stack([master, first, second], axis=1)
-    mine = lax.dynamic_index_in_dim(state, core, 0, keepdims=False)
-    theirs = hop(lax.dynamic_index_in_dim(state, 1 - core, 0, keepdims=False), CORE)
+    theirs = hop(jnp.stack([partners(master), partners(first), partners(second)]), CORE)
     other_y = hop(new_rows, CORE)
     other_live = hop(live, CORE)
     x_turned, c_turned = transposed(old_rows, other_x, old_cotangent, other_c)
-
-    theirs, other_y, other_live, x_turned, c_turned, is_own = lax.optimization_barrier(
-        (theirs, other_y, other_live, x_turned, c_turned, own_new == core)
-    )
-    state = jnp.where(
-        core == 0, jnp.concatenate([mine, theirs], axis=-2), jnp.concatenate([theirs, mine], axis=-2)
-    )
-    pieces = gather_chips(state[0].astype(jnp.bfloat16))
+    theirs, other_y, other_live, x_turned, c_turned = lax.optimization_barrier(
+        (theirs, other_y, other_live, x_turned, c_turned)
+    )
+    master_two = both_rows(mine(master), theirs[0])
+    pieces = gather_chips(master_two.astype(jnp.bfloat16))
     grads = backward(
         old_slots,
         live,
@@ -277,20 +313,26 @@
         x_turned,
         c_turned,
     )
+    theirs = after(theirs, grads[0])
+    first_two = both_rows(mine(first), theirs[1])
+    second_two = both_rows(mine(second), theirs[2])
     grad = reduce_chips(grads)
-    updated = adam_update(state[0], state[1], state[2], grad)
+    updated = adam_update(master_two, first_two, second_two, grad)
 
     new_pieces = gather_chips(updated[0].astype(jnp.bfloat16))
     updated = jnp.stack(updated)
     own_part = lax.dynamic_slice_in_dim(updated, core * local_rows, local_rows, 2)
     other_part = lax.dynamic_slice_in_dim(updated, (1 - core) * local_rows, local_rows, 2)
-    from_other = hop(other_part, CORE)
+    from_other = hop(after(other_part, new_pieces[-3]), CORE)
     state = jnp.where(
         core == 0, jnp.stack([own_part, from_other], axis=1), jnp.stack([from_other, own_part], axis=1)
     )
-    own_out, other_out = forward(new_pieces, new_rows, other_y)
-    new_outputs = jnp.where(is_own, own_out, hop(other_out, CORE))
-    return (state[0], state[1], state[2], new_outputs[None])
+    state = (state[0], state[1], state[2])
+    other_y, *state = lax.optimization_barrier((other_y,) + state)
+    other_out, matches = forward(new_slots, new_pieces, other_y)
+    own_out, matches = forward(new_slots, new_pieces, after(new_rows, other_out))
+    new_outputs = choose(matches, own_out, hop(other_out, CORE))
+    return (*state, new_outputs[None])
 
 
 def hidden_terms(tokens, cotangent, weights, live):

time: 98.8 us -> 107 us (1.083)
  waiting for transfers between devices: 25 us -> 36 us
  Pallas kernels: 6.79 us -> 10.6 us
  starting transfers between devices: 57.9 us -> 55 us
  other arithmetic: 3.76 us -> 1.35 us
    ppermute x52 -> x48, waiting for transfers between devices: 25 us -> 36 us  [hop(): lax.ppermute(block, 'dev', [(low, low ^ mask) for low in range(count)])]
    ppermute x52 -> x48, starting transfers between devices: 57.9 us -> 55 us  [hop(): lax.ppermute(block, 'dev', [(low, low ^ mask) for low in range(count)])]
    pallas_call x1 -> x2, Pallas kernels: 2.1 us -> 4.41 us  [forward(): pl.pallas_call(functools.partial(forward_kernel, count), out_shape=[jax.S...]
    pallas_call x1 -> x2, Pallas kernels: 4.09 us -> 5.63 us  [the longest x1 4.14 us: backward(): pl.pallas_call(functools.partial(backward_kernel, count), out_shape=[one,...]
    unnamed x12, local copies, waits for them, and re-layouts: 1.38 us -> 0.03 us
    select_n x1 -> x0, other arithmetic: 1.14 us -> none  [block_a_core(): jnp.where(core == 0, jnp.concatenate([mine, theirs], axis=-2), jnp.concat...]
    squeeze x2 -> x5, local copies, waits for them, and re-layouts: 0.87 us -> 2 us  [the longest x2 1.15 us: mine(): return lax.dynamic_index_in_dim(state, core, 0, keepdims=False)]
  transfers between devices with their start and end apart: 52 -> 48, of which waited for: 23 -> 25; matrix products, arithmetic and copies ran while one was open for 3% -> 3% of each run, Pallas kernels for 3% -> 3%
where the time goes in v4:
time: 107 us
  starting transfers between devices  55 us (51%)
  waiting for transfers between devices  36 us (34%)
  Pallas kernels  10.6 us (10%)
  local copies, waits for them, and re-layouts  2.06 us (2%)
  between operations  1.51 us (1%)
  other arithmetic  1.35 us (1%)
    ppermute x48, starting transfers between devices, hop(): lax.ppermute(block, 'dev', [(low, low ^ mask) for low in range(count)])  55 us
    ppermute x48, waiting for transfers between devices, hop(): lax.ppermute(block, 'dev', [(low, low ^ mask) for low in range(count)])  36 us
    pallas_call x2, Pallas kernels, forward(): pl.pallas_call(functools.partial(forward_kernel, count), out_shape=[jax.S...  4.41 us
    pallas_call x1, Pallas kernels, backward(): pl.pallas_call(functools.partial(backward_kernel, count), out_shape=[one,...  4.14 us
  transfers between devices with their start and end apart: 48, of which 25 were waited for; matrix products, arithmetic and copies ran while one was open for 3% of the time, Pallas kernels for 3%

profile of v4, /device:TPU:0, one launch (start us, length us, event | category | flops | bytes accessed | tf_op | source)
XLA Modules:
  0.0 106.5 jit_solution(9006382578421411162)
XLA Ops:
  0.6 0.5 collective-permute-start.3
  1.2 0.4 collective-permute-start.1
  1.7 1.1 %dynamic-slice_bitcast_fusion.1 = (f32[3,32,256]{2,1,0:T(8,128)S(1)}, f32[1,3,32,256]{3,2,1,0:T(8,128)S(1)}, f32[1,3,32,256]{3,2,1,0:T(8,128)S(1)}, f32[3,32,256]{2,1,0:T(8,128)S(1)}) fusion(f32[2,3,32,256]{3,2,1,0:T(8,128)} %param.11, s32[]{:T(128)S(6)} %select_n.44, s32[]{:T(128)S(6)} %select_n.41, f32[2,3,32,256]{3,2,1,0:T(8,128)} %param.10), kind=kLoop, calls=%fused_computation.47 | loop fusion | bytes 786440 | tf_op jit(solution)/shard_map/jit(dynamic_index_in_dim)/squeeze | solution.py:283
  2.9 0.7 pad_maximum_fusion.1
  3.7 0.4 collective-permute-start.2
  4.1 0.6 transpose_rows.1
  4.7 0.5 collective-permute-done.2.other_live
  5.4 3.8 %collective-permute-start.11 = (bf16[3,64,256]{2,1,0:T(8,128)(2,1)S(1)}, bf16[3,64,256]{2,1,0:T(8,128)(2,1)S(1)}, u32[]{:S(2)}, u32[]{:S(2)}) collective-permute-start(bf16[3,64,256]{2,1,0:T(8,128)(2,1)S(1)} %fusion.17.refs_0_), channel_id=1, source_target_pairs={{0,16},{1,17},{2,18},{3,19},{4,20},{5,21},{6,22},{7,23},{8,24},{9,... | collective-permute-start | bytes 294920 | tf_op jit(solution)/shard_map/ppermute | solution.py:24
  9.2 1.6 %collective-permute-start.8 = (bf16[3,64,256]{2,1,0:T(8,128)(2,1)S(1)}, bf16[3,64,256]{2,1,0:T(8,128)(2,1)S(1)}, u32[]{:S(2)}, u32[]{:S(2)}) collective-permute-start(bf16[3,64,256]{2,1,0:T(8,128)(2,1)S(1)} %fusion.17.refs_0_), channel_id=1, source_target_pairs={{0,8},{1,9},{2,10},{3,11},{4,12},{5,13},{6,14},{7,15},{8,0},{9,1},... | collective-permute-start | bytes 294920 | tf_op jit(solution)/shard_map/ppermute | solution.py:24
  10.8 1.5 %collective-permute-start.5 = (bf16[3,64,256]{2,1,0:T(8,128)(2,1)S(1)}, bf16[3,64,256]{2,1,0:T(8,128)(2,1)S(1)}, u32[]{:S(2)}, u32[]{:S(2)}) collective-permute-start(bf16[3,64,256]{2,1,0:T(8,128)(2,1)S(1)} %fusion.17.refs_0_), channel_id=1, source_target_pairs={{0,2},{1,3},{2,0},{3,1},{4,6},{5,7},{6,4},{7,5},{8,10},{9,11},{10,... | collective-permute-start | bytes 294920 | tf_op jit(solution)/shard_map/ppermute | solution.py:24
  12.3 1.5 %collective-permute-start.6 = (bf16[3,64,256]{2,1,0:T(8,128)(2,1)S(1)}, bf16[3,64,256]{2,1,0:T(8,128)(2,1)S(1)}, u32[]{:S(2)}, u32[]{:S(2)}) collective-permute-start(bf16[3,64,256]{2,1,0:T(8,128)(2,1)S(1)} %fusion.17.refs_0_), channel_id=1, source_target_pairs={{0,4},{1,5},{2,6},{3,7},{4,0},{5,1},{6,2},{7,3},{8,12},{9,13},{10,... | collective-permute-start | bytes 294920 | tf_op jit(solution)/shard_map/ppermute | solution.py:24
  13.8 0.9 collective-permute-done.11.refs_8_
  14.8 0.6 collective-permute-start.15
  15.4 1.5 %collective-permute-start.9 = (bf16[3,64,256]{2,1,0:T(8,128)(2,1)S(1)}, bf16[3,64,256]{2,1,0:T(8,128)(2,1)S(1)}, u32[]{:S(2)}, u32[]{:S(2)}) collective-permute-start(bf16[3,64,256]{2,1,0:T(8,128)(2,1)S(1)} %collective-permute-done.8.refs_4_), channel_id=1, source_target_pairs={{0,2},{1,3},{2,0},{3,1},{4,6},{5,7},{6,4},{7,5},{8,10},{9,11},{10,... | collective-permute-start | bytes 294920 | tf_op jit(solution)/shard_map/ppermute | solution.py:24
  16.9 1.5 %collective-permute-start.10 = (bf16[3,64,256]{2,1,0:T(8,128)(2,1)S(1)}, bf16[3,64,256]{2,1,0:T(8,128)(2,1)S(1)}, u32[]{:S(2)}, u32[]{:S(2)}) collective-permute-start(bf16[3,64,256]{2,1,0:T(8,128)(2,1)S(1)} %collective-permute-done.8.refs_4_), channel_id=1, source_target_pairs={{0,4},{1,5},{2,6},{3,7},{4,0},{5,1},{6,2},{7,3},{8,12},{9,13},{10,... | collective-permute-start | bytes 294920 | tf_op jit(solution)/shard_map/ppermute | solution.py:24
  18.4 0.5 collective-permute-start.12
  19.4 0.6 collective-permute-done.9.refs_5_
  20.0 2.3 %collective-permute-start.16 = (bf16[3,64,256]{2,1,0:T(8,128)(2,1)S(1)}, bf16[3,64,256]{2,1,0:T(8,128)(2,1)S(1)}, u32[]{:S(2)}, u32[]{:S(2)}) collective-permute-start(bf16[3,64,256]{2,1,0:T(8,128)(2,1)S(1)} %collective-permute-done.15.refs_12_), channel_id=1, source_target_pairs={{0,2},{1,3},{2,0},{3,1},{4,6},{5,7},{6,4},{7,5},{8,10},{9,11},{10,... | collective-permute-start | bytes 294920 | tf_op jit(solution)/shard_map/ppermute | solution.py:24
  22.3 1.6 %collective-permute-start.18 = (bf16[3,64,256]{2,1,0:T(8,128)(2,1)S(1)}, bf16[3,64,256]{2,1,0:T(8,128)(2,1)S(1)}, u32[]{:S(2)}, u32[]{:S(2)}) collective-permute-start(bf16[3,64,256]{2,1,0:T(8,128)(2,1)S(1)} %collective-permute-done.15.refs_12_), channel_id=1, source_target_pairs={{0,4},{1,5},{2,6},{3,7},{4,0},{5,1},{6,2},{7,3},{8,12},{9,13},{10,... | collective-permute-start | bytes 294920 | tf_op jit(solution)/shard_map/ppermute | solution.py:24
  24.3 1.6 %collective-permute-start.14 = (bf16[3,64,256]{2,1,0:T(8,128)(2,1)S(1)}, bf16[3,64,256]{2,1,0:T(8,128)(2,1)S(1)}, u32[]{:S(2)}, u32[]{:S(2)}) collective-permute-start(bf16[3,64,256]{2,1,0:T(8,128)(2,1)S(1)} %collective-permute-done.11.refs_8_), channel_id=1, source_target_pairs={{0,4},{1,5},{2,6},{3,7},{4,0},{5,1},{6,2},{7,3},{8,12},{9,13},{10,... | collective-permute-start | bytes 294920 | tf_op jit(solution)/shard_map/ppermute | solution.py:24
  26.0 0.5 collective-permute-start.13
  26.4 0.9 collective-permute-done.18.refs_14_
  27.3 0.7 collective-permute-start.19
  28.0 1.0 collective-permute-start.17
  29.7 0.6 collective-permute-done.14.refs_10_
  30.6 1.3 %collective-permute-done.19.refs_15_ = bf16[3,64,256]{2,1,0:T(8,128)(2,1)S(1)} collective-permute-done((bf16[3,64,256]{2,1,0:T(8,128)(2,1)S(1)}, bf16[3,64,256]{2,1,0:T(8,128)(2,1)S(1)}, u32[]{:S(2)}, u32[]{:S(2)}) %collective-permute-start.19) | collective-permute-done | bytes 98336 | tf_op jit(solution)/shard_map/ppermute | solution.py:24
  31.9 0.7 collective-permute-done.17.refs_11_
  32.6 4.1 %slot_gradients.1 = (bf16[3,64,256]{2,1,0:T(8,128)(2,1)S(1)}, bf16[3,64,256]{2,1,0:T(8,128)(2,1)S(1)}, bf16[2,3,64,256]{3,2,1,0:T(8,128)(2,1)S(1)}, bf16[3,64,25...) custom-call(s32[32]{0:T(128)S(1)} %copy-done.4, ...), custom_call_target="tpu_custom_call" | custom-call | flops 1610612736 | bytes 7340032 | tf_op jit(solution)/shard_map/slot_gradients/pallas_call | solution.py:160
  36.8 1.4 %collective-permute-start.22 = (bf16[2,3,64,256]{3,2,1,0:T(8,128)(2,1)S(1)}, bf16[2,3,64,256]{3,2,1,0:T(8,128)(2,1)S(1)}, u32[]{:S(2)}, u32[]{:S(2)}) collective-permute-start(bf16[2,3,64,256]{3,2,1,0:T(8,128)(2,1)S(1)} %get-tuple-element.69), channel_id=1, source_target_pairs={{0,2},{1,3},{2,0},{3,1},{4,6},{5,7},{6,4},{7,5},{8,10},{9,11},{10,... | collective-permute-start | bytes 589832 | tf_op jit(solution)/shard_map/ppermute | solution.py:24
  38.1 1.7 %collective-permute-start.20 = (bf16[2,3,64,256]{3,2,1,0:T(8,128)(2,1)S(1)}, bf16[2,3,64,256]{3,2,1,0:T(8,128)(2,1)S(1)}, u32[]{:S(2)}, u32[]{:S(2)}) collective-permute-start(bf16[2,3,64,256]{3,2,1,0:T(8,128)(2,1)S(1)} %get-tuple-element.66), channel_id=1, source_target_pairs={{0,4},{1,5},{2,6},{3,7},{4,0},{5,1},{6,2},{7,3},{8,12},{9,13},{10,... | collective-permute-start | bytes 589832 | tf_op jit(solution)/shard_map/ppermute | solution.py:24
  39.8 3.6 %collective-permute-done.22 = bf16[2,3,64,256]{3,2,1,0:T(8,128)(2,1)S(1)} collective-permute-done((bf16[2,3,64,256]{3,2,1,0:T(8,128)(2,1)S(1)}, bf16[2,3,64,256]{3,2,1,0:T(8,128)(2,1)S(1)}, u32[]{:S(2)}, u32[]{:S(2)}) %collective-permute-start.22) | collective-permute-done | bytes 196640 | tf_op jit(solution)/shard_map/ppermute | solution.py:24
  43.4 1.6 %collective-permute-start.23 = (bf16[3,64,256]{2,1,0:T(8,128)(2,1)S(1)}, bf16[3,64,256]{2,1,0:T(8,128)(2,1)S(1)}, u32[]{:S(2)}, u32[]{:S(2)}) collective-permute-start(bf16[3,64,256]{2,1,0:T(8,128)(2,1)S(1)} %fusion.10), channel_id=1, source_target_pairs={{0,4},{1,5},{2,6},{3,7},{4,0},{5,1},{6,2},{7,3},{8,12},{9,13},{10,... | collective-permute-start | bytes 294920 | tf_op jit(solution)/shard_map/ppermute | solution.py:24
  45.1 2.5 %collective-permute-start.21 = (bf16[3,64,256]{2,1,0:T(8,128)(2,1)S(1)}, bf16[3,64,256]{2,1,0:T(8,128)(2,1)S(1)}, u32[]{:S(2)}, u32[]{:S(2)}) collective-permute-start(bf16[3,64,256]{2,1,0:T(8,128)(2,1)S(1)} %fusion.13), channel_id=1, source_target_pairs={{0,2},{1,3},{2,0},{3,1},{4,6},{5,7},{6,4},{7,5},{8,10},{9,11},{10,... | collective-permute-start | bytes 294920 | tf_op jit(solution)/shard_map/ppermute | solution.py:24
  47.8 1.9 %collective-permute-start.28 = (bf16[2,3,64,256]{3,2,1,0:T(8,128)(2,1)S(1)}, bf16[2,3,64,256]{3,2,1,0:T(8,128)(2,1)S(1)}, u32[]{:S(2)}, u32[]{:S(2)}) collective-permute-start(bf16[2,3,64,256]{3,2,1,0:T(8,128)(2,1)S(1)} %get-tuple-element.76), channel_id=1, source_target_pairs={{0,2},{1,3},{2,0},{3,1},{4,6},{5,7},{6,4},{7,5},{8,10},{9,11},{10,... | collective-permute-start | bytes 589832 | tf_op jit(solution)/shard_map/ppermute | solution.py:24
  49.7 0.8 collective-permute-start.24
  50.5 2.8 %collective-permute-done.26 = bf16[2,3,64,256]{3,2,1,0:T(8,128)(2,1)S(1)} collective-permute-done((bf16[2,3,64,256]{3,2,1,0:T(8,128)(2,1)S(1)}, bf16[2,3,64,256]{3,2,1,0:T(8,128)(2,1)S(1)}, u32[]{:S(2)}, u32[]{:S(2)}) %collective-permute-start.26) | collective-permute-done | bytes 196640 | tf_op jit(solution)/shard_map/ppermute | solution.py:24
  53.6 1.9 %collective-permute-start.29 = (bf16[3,64,256]{2,1,0:T(8,128)(2,1)S(1)}, bf16[3,64,256]{2,1,0:T(8,128)(2,1)S(1)}, u32[]{:S(2)}, u32[]{:S(2)}) collective-permute-start(bf16[3,64,256]{2,1,0:T(8,128)(2,1)S(1)} %fusion.4), channel_id=1, source_target_pairs={{0,4},{1,5},{2,6},{3,7},{4,0},{5,1},{6,2},{7,3},{8,12},{9,13},{10,... | collective-permute-start | bytes 294920 | tf_op jit(solution)/shard_map/ppermute | solution.py:24
  55.5 0.6 collective-permute-done.24
  56.2 2.9 %collective-permute-start.25 = (bf16[3,64,256]{2,1,0:T(8,128)(2,1)S(1)}, bf16[3,64,256]{2,1,0:T(8,128)(2,1)S(1)}, u32[]{:S(2)}, u32[]{:S(2)}) collective-permute-start(bf16[3,64,256]{2,1,0:T(8,128)(2,1)S(1)} %fusion.16), channel_id=1, source_target_pairs={{0,16},{1,17},{2,18},{3,19},{4,20},{5,21},{6,22},{7,23},{8,24},{9,... | collective-permute-start | bytes 294920 | tf_op jit(solution)/shard_map/ppermute | solution.py:24
  59.1 0.4 collective-permute-start.30
  59.5 5.0 %collective-permute-done.25 = bf16[3,64,256]{2,1,0:T(8,128)(2,1)S(1)} collective-permute-done((bf16[3,64,256]{2,1,0:T(8,128)(2,1)S(1)}, bf16[3,64,256]{2,1,0:T(8,128)(2,1)S(1)}, u32[]{:S(2)}, u32[]{:S(2)}) %collective-permute-start.25) | collective-permute-done | bytes 98336 | tf_op jit(solution)/shard_map/ppermute | solution.py:24
  65.3 3.4 %collective-permute-start.31 = (bf16[3,64,256]{2,1,0:T(8,128)(2,1)S(1)}, bf16[3,64,256]{2,1,0:T(8,128)(2,1)S(1)}, u32[]{:S(2)}, u32[]{:S(2)}) collective-permute-start(bf16[3,64,256]{2,1,0:T(8,128)(2,1)S(1)} %get-tuple-element.94.refs_0_), channel_id=1, source_target_pairs={{0,16},{1,17},{2,18},{3,19},{4,20},{5,21},{6,22},{7,23},{8,24},{9,... | collective-permute-start | bytes 294920 | tf_op jit(solution)/shard_map/ppermute | solution.py:24
  68.7 0.9 collective-permute-done.33.refs_4_
  69.6 1.0 collective-permute-start.34
  70.6 1.8 %collective-permute-done.31.refs_8_ = bf16[3,64,256]{2,1,0:T(8,128)(2,1)S(1)} collective-permute-done((bf16[3,64,256]{2,1,0:T(8,128)(2,1)S(1)}, bf16[3,64,256]{2,1,0:T(8,128)(2,1)S(1)}, u32[]{:S(2)}, u32[]{:S(2)}) %collective-permute-start.31) | collective-permute-done | bytes 98336 | tf_op jit(solution)/shard_map/ppermute | solution.py:24
  72.7 1.5 %collective-permute-done.34.refs_5_ = bf16[3,64,256]{2,1,0:T(8,128)(2,1)S(1)} collective-permute-done((bf16[3,64,256]{2,1,0:T(8,128)(2,1)S(1)}, bf16[3,64,256]{2,1,0:T(8,128)(2,1)S(1)}, u32[]{:S(2)}, u32[]{:S(2)}) %collective-permute-start.34) | collective-permute-done | bytes 98336 | tf_op jit(solution)/shard_map/ppermute | solution.py:24
  74.3 2.8 %collective-permute-done.32.refs_12_ = bf16[3,64,256]{2,1,0:T(8,128)(2,1)S(1)} collective-permute-done((bf16[3,64,256]{2,1,0:T(8,128)(2,1)S(1)}, bf16[3,64,256]{2,1,0:T(8,128)(2,1)S(1)}, u32[]{:S(2)}, u32[]{:S(2)}) %collective-permute-start.32) | collective-permute-done | bytes 98336 | tf_op jit(solution)/shard_map/ppermute | solution.py:24
  77.4 4.2 %collective-permute-done.35.refs_13_ = bf16[3,64,256]{2,1,0:T(8,128)(2,1)S(1)} collective-permute-done((bf16[3,64,256]{2,1,0:T(8,128)(2,1)S(1)}, bf16[3,64,256]{2,1,0:T(8,128)(2,1)S(1)}, u32[]{:S(2)}, u32[]{:S(2)}) %collective-permute-start.35) | collective-permute-done | bytes 98336 | tf_op jit(solution)/shard_map/ppermute | solution.py:24
  82.0 2.0 %collective-permute-start.38 = (bf16[3,64,256]{2,1,0:T(8,128)(2,1)S(1)}, bf16[3,64,256]{2,1,0:T(8,128)(2,1)S(1)}, u32[]{:S(2)}, u32[]{:S(2)}) collective-permute-start(bf16[3,64,256]{2,1,0:T(8,128)(2,1)S(1)} %get-tuple-element.94.refs_0_), channel_id=1, source_target_pairs={{0,4},{1,5},{2,6},{3,7},{4,0},{5,1},{6,2},{7,3},{8,12},{9,13},{10,... | collective-permute-start | bytes 294920 | tf_op jit(solution)/shard_map/ppermute | solution.py:24
  84.0 2.8 %collective-permute-done.37.refs_1_ = bf16[3,64,256]{2,1,0:T(8,128)(2,1)S(1)} collective-permute-done((bf16[3,64,256]{2,1,0:T(8,128)(2,1)S(1)}, bf16[3,64,256]{2,1,0:T(8,128)(2,1)S(1)}, u32[]{:S(2)}, u32[]{:S(2)}) %collective-permute-start.37) | collective-permute-done | bytes 98336 | tf_op jit(solution)/shard_map/ppermute | solution.py:24
  86.8 0.7 collective-permute-start.40
  87.5 1.7 %collective-permute-start.41 = (bf16[3,64,256]{2,1,0:T(8,128)(2,1)S(1)}, bf16[3,64,256]{2,1,0:T(8,128)(2,1)S(1)}, u32[]{:S(2)}, u32[]{:S(2)}) collective-permute-start(bf16[3,64,256]{2,1,0:T(8,128)(2,1)S(1)} %collective-permute-done.31.refs_8_), channel_id=1, source_target_pairs={{0,2},{1,3},{2,0},{3,1},{4,6},{5,7},{6,4},{7,5},{8,10},{9,11},{10,... | collective-permute-start | bytes 294920 | tf_op jit(solution)/shard_map/ppermute | solution.py:24
  89.3 2.0 %collective-permute-start.39 = (bf16[3,64,256]{2,1,0:T(8,128)(2,1)S(1)}, bf16[3,64,256]{2,1,0:T(8,128)(2,1)S(1)}, u32[]{:S(2)}, u32[]{:S(2)}) collective-permute-start(bf16[3,64,256]{2,1,0:T(8,128)(2,1)S(1)} %collective-permute-done.37.refs_1_), channel_id=1, source_target_pairs={{0,4},{1,5},{2,6},{3,7},{4,0},{5,1},{6,2},{7,3},{8,12},{9,13},{10,... | collective-permute-start | bytes 294920 | tf_op jit(solution)/shard_map/ppermute | solution.py:24
  91.3 0.7 collective-permute-done.40.refs_6_
  92.1 1.7 %collective-permute-start.42 = (bf16[3,64,256]{2,1,0:T(8,128)(2,1)S(1)}, bf16[3,64,256]{2,1,0:T(8,128)(2,1)S(1)}, u32[]{:S(2)}, u32[]{:S(2)}) collective-permute-start(bf16[3,64,256]{2,1,0:T(8,128)(2,1)S(1)} %collective-permute-done.40.refs_6_), channel_id=1, source_target_pairs={{0,2},{1,3},{2,0},{3,1},{4,6},{5,7},{6,4},{7,5},{8,10},{9,11},{10,... | collective-permute-start | bytes 294920 | tf_op jit(solution)/shard_map/ppermute | solution.py:24
  93.9 1.1 collective-permute-start.43
  94.9 1.0 collective-permute-start.44
  95.9 1.1 %collective-permute-start.46 = (bf16[3,64,256]{2,1,0:T(8,128)(2,1)S(1)}, bf16[3,64,256]{2,1,0:T(8,128)(2,1)S(1)}, u32[]{:S(2)}, u32[]{:S(2)}) collective-permute-start(bf16[3,64,256]{2,1,0:T(8,128)(2,1)S(1)} %collective-permute-done.45.refs_14_), channel_id=1, source_target_pairs={{0,2},{1,3},{2,0},{3,1},{4,6},{5,7},{6,4},{7,5},{8,10},{9,11},{10,... | collective-permute-start | bytes 294920 | tf_op jit(solution)/shard_map/ppermute | solution.py:24
  97.1 0.8 slice_bitcast_fusion
  97.9 0.9 collective-permute-done.43.refs_10_
  98.8 1.7 %collective-permute-done.46.refs_15_ = bf16[3,64,256]{2,1,0:T(8,128)(2,1)S(1)} collective-permute-done((bf16[3,64,256]{2,1,0:T(8,128)(2,1)S(1)}, bf16[3,64,256]{2,1,0:T(8,128)(2,1)S(1)}, u32[]{:S(2)}, u32[]{:S(2)}) %collective-permute-start.46) | collective-permute-done | bytes 98336 | tf_op jit(solution)/shard_map/ppermute | solution.py:24
  100.5 2.2 %expert_outputs.2 = (bf16[256,1024]{1,0:T(8,128)(2,1)S(1)}, s32[1]{0:T(128)}) custom-call(s32[32]{0:T(128)S(1)} %copy-done.3, bf16[3,64,256]{2,1,0:T(8,128)(2,1)S(1)} %get-tuple-element.94.refs_0_, bf16[3,64,256]{2,1,0:T(8,128)(2,1)S(1)} %collective-permute-done.37.refs_1_, bf16[3,64,256]{2,1,0:T(8,128)(2,1)S(1)} %collective-permute-done.38.refs_2_, ...), custom_call_target="tpu_custom_call" | custom-call | flops 402653184 | bytes 2621440 | tf_op jit(solution)/shard_map/expert_outputs/pallas_call | solution.py:186
  102.8 2.2 %expert_outputs.3 = (bf16[256,1024]{1,0:T(8,128)(2,1)S(1)}, s32[1]{0:T(128)}) custom-call(s32[32]{0:T(128)S(1)} %copy-done.3, bf16[3,64,256]{2,1,0:T(8,128)(2,1)S(1)} %get-tuple-element.94.refs_0_, bf16[3,64,256]{2,1,0:T(8,128)(2,1)S(1)} %collective-permute-done.37.refs_1_, bf16[3,64,256]{2,1,0:T(8,128)(2,1)S(1)} %collective-permute-done.38.refs_2_, ...), custom_call_target="tpu_custom_call" | custom-call | flops 402653184 | bytes 2621440 | tf_op jit(solution)/shard_map/expert_outputs/pallas_call | solution.py:186
  105.0 1.5 %choose_outputs.1 = bf16[256,1024]{1,0:T(8,128)(2,1)} custom-call(s32[1]{0:T(128)} %get-tuple-element.92.matches, bf16[256,1024]{1,0:T(8,128)(2,1)S(1)} %get-tuple-element.93.own_out, bf16[256,1024]{1,0:T(8,128)(2,1)S(1)} %collective-permute-done.47.other_out), custom_call_target="tpu_custom_call" | custom-call | tf_op jit(solution)/shard_map/choose_outputs/pallas_call | solution.py:209
  (67 shorter events, 4.4 us)
Async XLA Ops:
  0.6 3.5 %collective-permute-start.3 = (bf16[256,1024]{1,0:T(8,128)(2,1)}, bf16[256,1024]{1,0:T(8,128)(2,1)S(1)}, u32[]{:S(2)}, u32[]{:S(2)}) collective-permute-start(bf16[256,1024]{1,0:T(8,128)(2,1)} %bitcast.76), channel_id=1, source_target_pairs={{0,1},{1,0},{2,3},{3,2},{4,5},{5,4},{6,7},{7,6},{8,9},{9,8},{10,11... | collective-permute-start | bytes 1572872 | tf_op jit(solution)/shard_map/ppermute | solution.py:24
  1.1 3.0 %collective-permute-start.4 = (bf16[256,1024]{1,0:T(8,128)(2,1)}, bf16[256,1024]{1,0:T(8,128)(2,1)S(1)}, u32[]{:S(2)}, u32[]{:S(2)}) collective-permute-start(bf16[256,1024]{1,0:T(8,128)(2,1)} %bitcast.79), channel_id=1, source_target_pairs={{0,1},{1,0},{2,3},{3,2},{4,5},{5,4},{6,7},{7,6},{8,9},{9,8},{10,11... | collective-permute-start | bytes 1572872 | tf_op jit(solution)/shard_map/ppermute | solution.py:24
  1.2 4.2 %collective-permute-start.1 = (bf16[256,1024]{1,0:T(8,128)(2,1)}, bf16[256,1024]{1,0:T(8,128)(2,1)S(1)}, u32[]{:S(2)}, u32[]{:S(2)}) collective-permute-start(bf16[256,1024]{1,0:T(8,128)(2,1)} %bitcast.74), channel_id=1, source_target_pairs={{0,1},{1,0},{2,3},{3,2},{4,5},{5,4},{6,7},{7,6},{8,9},{9,8},{10,11... | collective-permute-start | bytes 1572872 | tf_op jit(solution)/shard_map/ppermute | solution.py:24
  1.7 1.1 %copy-start.5 = (f32[2,3,32,256]{3,2,1,0:T(8,128)S(1)}, f32[2,3,32,256]{3,2,1,0:T(8,128)}, u32[]{:S(2)}) copy-start(f32[2,3,32,256]{3,2,1,0:T(8,128)} %param.9) | copy-start | bytes 589828
  1.7 2.4 %copy-start.2 = (bf16[1,256,1024]{2,1,0:T(8,128)(2,1)S(1)}, bf16[1,256,1024]{2,1,0:T(8,128)(2,1)}, u32[]{:S(2)}) copy-start(bf16[1,256,1024]{2,1,0:T(8,128)(2,1)} %param.13) | copy-start | bytes 1572868
  2.8 1.3 %copy-start.1 = (bf16[1,256,1024]{2,1,0:T(8,128)(2,1)S(1)}, bf16[1,256,1024]{2,1,0:T(8,128)(2,1)}, u32[]{:S(2)}) copy-start(bf16[1,256,1024]{2,1,0:T(8,128)(2,1)} %param.12) | copy-start | bytes 1572868
  3.6 1.8 %collective-permute-start = (f32[3,3,32,256]{3,2,1,0:T(8,128)}, f32[3,3,32,256]{3,2,1,0:T(8,128)S(1)}, u32[]{:S(2)}, u32[]{:S(2)}) collective-permute-start(f32[3,3,32,256]{3,2,1,0:T(8,128)} %pad_maximum_fusion.1), channel_id=1, source_target_pairs={{0,1},{1,0},{2,3},{3,2},{4,5},{5,4},{6,7},{7,6},{8,9},{9,8},{10,11... | collective-permute-start | bytes 884744 | tf_op jit(solution)/shard_map/ppermute | solution.py:24
  3.7 1.6 %collective-permute-start.2 = (s32[1]{0:T(128)}, s32[1]{0:T(128)}, u32[]{:S(2)}, u32[]{:S(2)}) collective-permute-start(s32[1]{0:T(128)} %param.17), channel_id=1, source_target_pairs={{0,1},{1,0},{2,3},{3,2},{4,5},{5,4},{6,7},{7,6},{8,9},{9,8},{10,11... | collective-permute-start | bytes 20 | tf_op jit(solution)/shard_map/ppermute | solution.py:24
  5.4 27.2 %copy-start.4 = (s32[32]{0:T(128)S(1)}, s32[32]{0:T(128)}, u32[]{:S(2)}) copy-start(s32[32]{0:T(128)} %slots.3) | copy-start | bytes 388
  5.4 9.3 %collective-permute-start.11 = (bf16[3,64,256]{2,1,0:T(8,128)(2,1)S(1)}, bf16[3,64,256]{2,1,0:T(8,128)(2,1)S(1)}, u32[]{:S(2)}, u32[]{:S(2)}) collective-permute-start(bf16[3,64,256]{2,1,0:T(8,128)(2,1)S(1)} %fusion.17.refs_0_), channel_id=1, source_target_pairs={{0,16},{1,17},{2,18},{3,19},{4,20},{5,21},{6,22},{7,23},{8,24},{9,... | collective-permute-start | bytes 294920 | tf_op jit(solution)/shard_map/ppermute | solution.py:24
  9.2 6.2 %collective-permute-start.8 = (bf16[3,64,256]{2,1,0:T(8,128)(2,1)S(1)}, bf16[3,64,256]{2,1,0:T(8,128)(2,1)S(1)}, u32[]{:S(2)}, u32[]{:S(2)}) collective-permute-start(bf16[3,64,256]{2,1,0:T(8,128)(2,1)S(1)} %fusion.17.refs_0_), channel_id=1, source_target_pairs={{0,8},{1,9},{2,10},{3,11},{4,12},{5,13},{6,14},{7,15},{8,0},{9,1},... | collective-permute-start | bytes 294920 | tf_op jit(solution)/shard_map/ppermute | solution.py:24
  10.8 6.1 %collective-permute-start.5 = (bf16[3,64,256]{2,1,0:T(8,128)(2,1)S(1)}, bf16[3,64,256]{2,1,0:T(8,128)(2,1)S(1)}, u32[]{:S(2)}, u32[]{:S(2)}) collective-permute-start(bf16[3,64,256]{2,1,0:T(8,128)(2,1)S(1)} %fusion.17.refs_0_), channel_id=1, source_target_pairs={{0,2},{1,3},{2,0},{3,1},{4,6},{5,7},{6,4},{7,5},{8,10},{9,11},{10,... | collective-permute-start | bytes 294920 | tf_op jit(solution)/shard_map/ppermute | solution.py:24
  12.3 6.1 %collective-permute-start.6 = (bf16[3,64,256]{2,1,0:T(8,128)(2,1)S(1)}, bf16[3,64,256]{2,1,0:T(8,128)(2,1)S(1)}, u32[]{:S(2)}, u32[]{:S(2)}) collective-permute-start(bf16[3,64,256]{2,1,0:T(8,128)(2,1)S(1)} %fusion.17.refs_0_), channel_id=1, source_target_pairs={{0,4},{1,5},{2,6},{3,7},{4,0},{5,1},{6,2},{7,3},{8,12},{9,13},{10,... | collective-permute-start | bytes 294920 | tf_op jit(solution)/shard_map/ppermute | solution.py:24
  14.8 4.6 %collective-permute-start.15 = (bf16[3,64,256]{2,1,0:T(8,128)(2,1)S(1)}, bf16[3,64,256]{2,1,0:T(8,128)(2,1)S(1)}, u32[]{:S(2)}, u32[]{:S(2)}) collective-permute-start(bf16[3,64,256]{2,1,0:T(8,128)(2,1)S(1)} %collective-permute-done.11.refs_8_), channel_id=1, source_target_pairs={{0,8},{1,9},{2,10},{3,11},{4,12},{5,13},{6,14},{7,15},{8,0},{9,1},... | collective-permute-start | bytes 294920 | tf_op jit(solution)/shard_map/ppermute | solution.py:24
  15.4 4.6 %collective-permute-start.9 = (bf16[3,64,256]{2,1,0:T(8,128)(2,1)S(1)}, bf16[3,64,256]{2,1,0:T(8,128)(2,1)S(1)}, u32[]{:S(2)}, u32[]{:S(2)}) collective-permute-start(bf16[3,64,256]{2,1,0:T(8,128)(2,1)S(1)} %collective-permute-done.8.refs_4_), channel_id=1, source_target_pairs={{0,2},{1,3},{2,0},{3,1},{4,6},{5,7},{6,4},{7,5},{8,10},{9,11},{10,... | collective-permute-start | bytes 294920 | tf_op jit(solution)/shard_map/ppermute | solution.py:24
  16.9 7.4 %collective-permute-start.10 = (bf16[3,64,256]{2,1,0:T(8,128)(2,1)S(1)}, bf16[3,64,256]{2,1,0:T(8,128)(2,1)S(1)}, u32[]{:S(2)}, u32[]{:S(2)}) collective-permute-start(bf16[3,64,256]{2,1,0:T(8,128)(2,1)S(1)} %collective-permute-done.8.refs_4_), channel_id=1, source_target_pairs={{0,4},{1,5},{2,6},{3,7},{4,0},{5,1},{6,2},{7,3},{8,12},{9,13},{10,... | collective-permute-start | bytes 294920 | tf_op jit(solution)/shard_map/ppermute | solution.py:24
  18.4 7.5 %collective-permute-start.12 = (bf16[3,64,256]{2,1,0:T(8,128)(2,1)S(1)}, bf16[3,64,256]{2,1,0:T(8,128)(2,1)S(1)}, u32[]{:S(2)}, u32[]{:S(2)}) collective-permute-start(bf16[3,64,256]{2,1,0:T(8,128)(2,1)S(1)} %collective-permute-done.11.refs_8_), channel_id=1, source_target_pairs={{0,2},{1,3},{2,0},{3,1},{4,6},{5,7},{6,4},{7,5},{8,10},{9,11},{10,... | collective-permute-start | bytes 294920 | tf_op jit(solution)/shard_map/ppermute | solution.py:24
  20.0 6.4 %collective-permute-start.16 = (bf16[3,64,256]{2,1,0:T(8,128)(2,1)S(1)}, bf16[3,64,256]{2,1,0:T(8,128)(2,1)S(1)}, u32[]{:S(2)}, u32[]{:S(2)}) collective-permute-start(bf16[3,64,256]{2,1,0:T(8,128)(2,1)S(1)} %collective-permute-done.15.refs_12_), channel_id=1, source_target_pairs={{0,2},{1,3},{2,0},{3,1},{4,6},{5,7},{6,4},{7,5},{8,10},{9,11},{10,... | collective-permute-start | bytes 294920 | tf_op jit(solution)/shard_map/ppermute | solution.py:24
  22.3 5.0 %collective-permute-start.18 = (bf16[3,64,256]{2,1,0:T(8,128)(2,1)S(1)}, bf16[3,64,256]{2,1,0:T(8,128)(2,1)S(1)}, u32[]{:S(2)}, u32[]{:S(2)}) collective-permute-start(bf16[3,64,256]{2,1,0:T(8,128)(2,1)S(1)} %collective-permute-done.15.refs_12_), channel_id=1, source_target_pairs={{0,4},{1,5},{2,6},{3,7},{4,0},{5,1},{6,2},{7,3},{8,12},{9,13},{10,... | collective-permute-start | bytes 294920 | tf_op jit(solution)/shard_map/ppermute | solution.py:24
  23.9 5.7 %collective-permute-start.7 = (bf16[3,64,256]{2,1,0:T(8,128)(2,1)S(1)}, bf16[3,64,256]{2,1,0:T(8,128)(2,1)S(1)}, u32[]{:S(2)}, u32[]{:S(2)}) collective-permute-start(bf16[3,64,256]{2,1,0:T(8,128)(2,1)S(1)} %collective-permute-done.5.refs_1_), channel_id=1, source_target_pairs={{0,4},{1,5},{2,6},{3,7},{4,0},{5,1},{6,2},{7,3},{8,12},{9,13},{10,... | collective-permute-start | bytes 294920 | tf_op jit(solution)/shard_map/ppermute | solution.py:24
  24.3 6.0 %collective-permute-start.14 = (bf16[3,64,256]{2,1,0:T(8,128)(2,1)S(1)}, bf16[3,64,256]{2,1,0:T(8,128)(2,1)S(1)}, u32[]{:S(2)}, u32[]{:S(2)}) collective-permute-start(bf16[3,64,256]{2,1,0:T(8,128)(2,1)S(1)} %collective-permute-done.11.refs_8_), channel_id=1, source_target_pairs={{0,4},{1,5},{2,6},{3,7},{4,0},{5,1},{6,2},{7,3},{8,12},{9,13},{10,... | collective-permute-start | bytes 294920 | tf_op jit(solution)/shard_map/ppermute | solution.py:24
  26.0 4.6 %collective-permute-start.13 = (bf16[3,64,256]{2,1,0:T(8,128)(2,1)S(1)}, bf16[3,64,256]{2,1,0:T(8,128)(2,1)S(1)}, u32[]{:S(2)}, u32[]{:S(2)}) collective-permute-start(bf16[3,64,256]{2,1,0:T(8,128)(2,1)S(1)} %collective-permute-done.10.refs_6_), channel_id=1, source_target_pairs={{0,2},{1,3},{2,0},{3,1},{4,6},{5,7},{6,4},{7,5},{8,10},{9,11},{10,... | collective-permute-start | bytes 294920 | tf_op jit(solution)/shard_map/ppermute | solution.py:24
  27.3 4.6 %collective-permute-start.19 = (bf16[3,64,256]{2,1,0:T(8,128)(2,1)S(1)}, bf16[3,64,256]{2,1,0:T(8,128)(2,1)S(1)}, u32[]{:S(2)}, u32[]{:S(2)}) collective-permute-start(bf16[3,64,256]{2,1,0:T(8,128)(2,1)S(1)} %collective-permute-done.18.refs_14_), channel_id=1, source_target_pairs={{0,2},{1,3},{2,0},{3,1},{4,6},{5,7},{6,4},{7,5},{8,10},{9,11},{10,... | collective-permute-start | bytes 294920 | tf_op jit(solution)/shard_map/ppermute | solution.py:24
  28.0 4.6 %collective-permute-start.17 = (bf16[3,64,256]{2,1,0:T(8,128)(2,1)S(1)}, bf16[3,64,256]{2,1,0:T(8,128)(2,1)S(1)}, u32[]{:S(2)}, u32[]{:S(2)}) collective-permute-start(bf16[3,64,256]{2,1,0:T(8,128)(2,1)S(1)} %collective-permute-done.12.refs_9_), channel_id=1, source_target_pairs={{0,4},{1,5},{2,6},{3,7},{4,0},{5,1},{6,2},{7,3},{8,12},{9,13},{10,... | collective-permute-start | bytes 294920 | tf_op jit(solution)/shard_map/ppermute | solution.py:24
  36.8 6.6 %collective-permute-start.22 = (bf16[2,3,64,256]{3,2,1,0:T(8,128)(2,1)S(1)}, bf16[2,3,64,256]{3,2,1,0:T(8,128)(2,1)S(1)}, u32[]{:S(2)}, u32[]{:S(2)}) collective-permute-start(bf16[2,3,64,256]{3,2,1,0:T(8,128)(2,1)S(1)} %get-tuple-element.69), channel_id=1, source_target_pairs={{0,2},{1,3},{2,0},{3,1},{4,6},{5,7},{6,4},{7,5},{8,10},{9,11},{10,... | collective-permute-start | bytes 589832 | tf_op jit(solution)/shard_map/ppermute | solution.py:24
  38.1 6.9 %collective-permute-start.20 = (bf16[2,3,64,256]{3,2,1,0:T(8,128)(2,1)S(1)}, bf16[2,3,64,256]{3,2,1,0:T(8,128)(2,1)S(1)}, u32[]{:S(2)}, u32[]{:S(2)}) collective-permute-start(bf16[2,3,64,256]{3,2,1,0:T(8,128)(2,1)S(1)} %get-tuple-element.66), channel_id=1, source_target_pairs={{0,4},{1,5},{2,6},{3,7},{4,0},{5,1},{6,2},{7,3},{8,12},{9,13},{10,... | collective-permute-start | bytes 589832 | tf_op jit(solution)/shard_map/ppermute | solution.py:24
  43.4 6.2 %collective-permute-start.23 = (bf16[3,64,256]{2,1,0:T(8,128)(2,1)S(1)}, bf16[3,64,256]{2,1,0:T(8,128)(2,1)S(1)}, u32[]{:S(2)}, u32[]{:S(2)}) collective-permute-start(bf16[3,64,256]{2,1,0:T(8,128)(2,1)S(1)} %fusion.10), channel_id=1, source_target_pairs={{0,4},{1,5},{2,6},{3,7},{4,0},{5,1},{6,2},{7,3},{8,12},{9,13},{10,... | collective-permute-start | bytes 294920 | tf_op jit(solution)/shard_map/ppermute | solution.py:24
  45.1 10.4 %collective-permute-start.21 = (bf16[3,64,256]{2,1,0:T(8,128)(2,1)S(1)}, bf16[3,64,256]{2,1,0:T(8,128)(2,1)S(1)}, u32[]{:S(2)}, u32[]{:S(2)}) collective-permute-start(bf16[3,64,256]{2,1,0:T(8,128)(2,1)S(1)} %fusion.13), channel_id=1, source_target_pairs={{0,2},{1,3},{2,0},{3,1},{4,6},{5,7},{6,4},{7,5},{8,10},{9,11},{10,... | collective-permute-start | bytes 294920 | tf_op jit(solution)/shard_map/ppermute | solution.py:24
  47.6 5.7 %collective-permute-start.26 = (bf16[2,3,64,256]{3,2,1,0:T(8,128)(2,1)S(1)}, bf16[2,3,64,256]{3,2,1,0:T(8,128)(2,1)S(1)}, u32[]{:S(2)}, u32[]{:S(2)}) collective-permute-start(bf16[2,3,64,256]{3,2,1,0:T(8,128)(2,1)S(1)} %get-tuple-element.72), channel_id=1, source_target_pairs={{0,4},{1,5},{2,6},{3,7},{4,0},{5,1},{6,2},{7,3},{8,12},{9,13},{10,... | collective-permute-start | bytes 589832 | tf_op jit(solution)/shard_map/ppermute | solution.py:24
  47.8 5.8 %collective-permute-start.28 = (bf16[2,3,64,256]{3,2,1,0:T(8,128)(2,1)S(1)}, bf16[2,3,64,256]{3,2,1,0:T(8,128)(2,1)S(1)}, u32[]{:S(2)}, u32[]{:S(2)}) collective-permute-start(bf16[2,3,64,256]{3,2,1,0:T(8,128)(2,1)S(1)} %get-tuple-element.76), channel_id=1, source_target_pairs={{0,2},{1,3},{2,0},{3,1},{4,6},{5,7},{6,4},{7,5},{8,10},{9,11},{10,... | collective-permute-start | bytes 589832 | tf_op jit(solution)/shard_map/ppermute | solution.py:24
  49.7 6.5 %collective-permute-start.24 = (bf16[3,64,256]{2,1,0:T(8,128)(2,1)S(1)}, bf16[3,64,256]{2,1,0:T(8,128)(2,1)S(1)}, u32[]{:S(2)}, u32[]{:S(2)}) collective-permute-start(bf16[3,64,256]{2,1,0:T(8,128)(2,1)S(1)} %fusion.12), channel_id=1, source_target_pairs={{0,8},{1,9},{2,10},{3,11},{4,12},{5,13},{6,14},{7,15},{8,0},{9,1},... | collective-permute-start | bytes 294920 | tf_op jit(solution)/shard_map/ppermute | solution.py:24
  53.3 6.2 %collective-permute-start.27 = (bf16[3,64,256]{2,1,0:T(8,128)(2,1)S(1)}, bf16[3,64,256]{2,1,0:T(8,128)(2,1)S(1)}, u32[]{:S(2)}, u32[]{:S(2)}) collective-permute-start(bf16[3,64,256]{2,1,0:T(8,128)(2,1)S(1)} %fusion.7), channel_id=1, source_target_pairs={{0,2},{1,3},{2,0},{3,1},{4,6},{5,7},{6,4},{7,5},{8,10},{9,11},{10,... | collective-permute-start | bytes 294920 | tf_op jit(solution)/shard_map/ppermute | solution.py:24
  53.6 5.4 %collective-permute-start.29 = (bf16[3,64,256]{2,1,0:T(8,128)(2,1)S(1)}, bf16[3,64,256]{2,1,0:T(8,128)(2,1)S(1)}, u32[]{:S(2)}, u32[]{:S(2)}) collective-permute-start(bf16[3,64,256]{2,1,0:T(8,128)(2,1)S(1)} %fusion.4), channel_id=1, source_target_pairs={{0,4},{1,5},{2,6},{3,7},{4,0},{5,1},{6,2},{7,3},{8,12},{9,13},{10,... | collective-permute-start | bytes 294920 | tf_op jit(solution)/shard_map/ppermute | solution.py:24
  56.2 8.3 %collective-permute-start.25 = (bf16[3,64,256]{2,1,0:T(8,128)(2,1)S(1)}, bf16[3,64,256]{2,1,0:T(8,128)(2,1)S(1)}, u32[]{:S(2)}, u32[]{:S(2)}) collective-permute-start(bf16[3,64,256]{2,1,0:T(8,128)(2,1)S(1)} %fusion.16), channel_id=1, source_target_pairs={{0,16},{1,17},{2,18},{3,19},{4,20},{5,21},{6,22},{7,23},{8,24},{9,... | collective-permute-start | bytes 294920 | tf_op jit(solution)/shard_map/ppermute | solution.py:24
  59.1 5.6 %collective-permute-start.30 = (bf16[3,64,256]{2,1,0:T(8,128)(2,1)S(1)}, bf16[3,64,256]{2,1,0:T(8,128)(2,1)S(1)}, u32[]{:S(2)}, u32[]{:S(2)}) collective-permute-start(bf16[3,64,256]{2,1,0:T(8,128)(2,1)S(1)} %fusion.6), channel_id=1, source_target_pairs={{0,8},{1,9},{2,10},{3,11},{4,12},{5,13},{6,14},{7,15},{8,0},{9,1},... | collective-permute-start | bytes 294920 | tf_op jit(solution)/shard_map/ppermute | solution.py:24
  65.0 4.7 %collective-permute-start.33 = (bf16[3,64,256]{2,1,0:T(8,128)(2,1)S(1)}, bf16[3,64,256]{2,1,0:T(8,128)(2,1)S(1)}, u32[]{:S(2)}, u32[]{:S(2)}) collective-permute-start(bf16[3,64,256]{2,1,0:T(8,128)(2,1)S(1)} %get-tuple-element.94.refs_0_), channel_id=1, source_target_pairs={{0,8},{1,9},{2,10},{3,11},{4,12},{5,13},{6,14},{7,15},{8,0},{9,1},... | collective-permute-start | bytes 294920 | tf_op jit(solution)/shard_map/ppermute | solution.py:24
  65.3 7.1 %collective-permute-start.31 = (bf16[3,64,256]{2,1,0:T(8,128)(2,1)S(1)}, bf16[3,64,256]{2,1,0:T(8,128)(2,1)S(1)}, u32[]{:S(2)}, u32[]{:S(2)}) collective-permute-start(bf16[3,64,256]{2,1,0:T(8,128)(2,1)S(1)} %get-tuple-element.94.refs_0_), channel_id=1, source_target_pairs={{0,16},{1,17},{2,18},{3,19},{4,20},{5,21},{6,22},{7,23},{8,24},{9,... | collective-permute-start | bytes 294920 | tf_op jit(solution)/shard_map/ppermute | solution.py:24
  69.6 4.6 %collective-permute-start.34 = (bf16[3,64,256]{2,1,0:T(8,128)(2,1)S(1)}, bf16[3,64,256]{2,1,0:T(8,128)(2,1)S(1)}, u32[]{:S(2)}, u32[]{:S(2)}) collective-permute-start(bf16[3,64,256]{2,1,0:T(8,128)(2,1)S(1)} %collective-permute-done.33.refs_4_), channel_id=1, source_target_pairs={{0,2},{1,3},{2,0},{3,1},{4,6},{5,7},{6,4},{7,5},{8,10},{9,11},{10,... | collective-permute-start | bytes 294920 | tf_op jit(solution)/shard_map/ppermute | solution.py:24
  72.4 4.6 %collective-permute-start.32 = (bf16[3,64,256]{2,1,0:T(8,128)(2,1)S(1)}, bf16[3,64,256]{2,1,0:T(8,128)(2,1)S(1)}, u32[]{:S(2)}, u32[]{:S(2)}) collective-permute-start(bf16[3,64,256]{2,1,0:T(8,128)(2,1)S(1)} %collective-permute-done.31.refs_8_), channel_id=1, source_target_pairs={{0,8},{1,9},{2,10},{3,11},{4,12},{5,13},{6,14},{7,15},{8,0},{9,1},... | collective-permute-start | bytes 294920 | tf_op jit(solution)/shard_map/ppermute | solution.py:24
  77.0 4.6 %collective-permute-start.35 = (bf16[3,64,256]{2,1,0:T(8,128)(2,1)S(1)}, bf16[3,64,256]{2,1,0:T(8,128)(2,1)S(1)}, u32[]{:S(2)}, u32[]{:S(2)}) collective-permute-start(bf16[3,64,256]{2,1,0:T(8,128)(2,1)S(1)} %collective-permute-done.32.refs_12_), channel_id=1, source_target_pairs={{0,2},{1,3},{2,0},{3,1},{4,6},{5,7},{6,4},{7,5},{8,10},{9,11},{10,... | collective-permute-start | bytes 294920 | tf_op jit(solution)/shard_map/ppermute | solution.py:24
  81.6 14.3 %collective-permute-start.36 = (f32[3,3,32,256]{3,2,1,0:T(8,128)S(1)}, f32[3,3,32,256]{3,2,1,0:T(8,128)S(1)}, u32[]{:S(2)}, u32[]{:S(2)}) collective-permute-start(f32[3,3,32,256]{3,2,1,0:T(8,128)S(1)} %get-tuple-element.79), channel_id=1, source_target_pairs={{0,1},{1,0},{2,3},{3,2},{4,5},{5,4},{6,7},{7,6},{8,9},{9,8},{10,11... | collective-permute-start | bytes 884744 | tf_op jit(solution)/shard_map/ppermute | solution.py:24
  81.6 5.2 %collective-permute-start.37 = (bf16[3,64,256]{2,1,0:T(8,128)(2,1)S(1)}, bf16[3,64,256]{2,1,0:T(8,128)(2,1)S(1)}, u32[]{:S(2)}, u32[]{:S(2)}) collective-permute-start(bf16[3,64,256]{2,1,0:T(8,128)(2,1)S(1)} %get-tuple-element.94.refs_0_), channel_id=1, source_target_pairs={{0,2},{1,3},{2,0},{3,1},{4,6},{5,7},{6,4},{7,5},{8,10},{9,11},{10,... | collective-permute-start | bytes 294920 | tf_op jit(solution)/shard_map/ppermute | solution.py:24
  82.0 5.5 %collective-permute-start.38 = (bf16[3,64,256]{2,1,0:T(8,128)(2,1)S(1)}, bf16[3,64,256]{2,1,0:T(8,128)(2,1)S(1)}, u32[]{:S(2)}, u32[]{:S(2)}) collective-permute-start(bf16[3,64,256]{2,1,0:T(8,128)(2,1)S(1)} %get-tuple-element.94.refs_0_), channel_id=1, source_target_pairs={{0,4},{1,5},{2,6},{3,7},{4,0},{5,1},{6,2},{7,3},{8,12},{9,13},{10,... | collective-permute-start | bytes 294920 | tf_op jit(solution)/shard_map/ppermute | solution.py:24
  86.8 5.1 %collective-permute-start.40 = (bf16[3,64,256]{2,1,0:T(8,128)(2,1)S(1)}, bf16[3,64,256]{2,1,0:T(8,128)(2,1)S(1)}, u32[]{:S(2)}, u32[]{:S(2)}) collective-permute-start(bf16[3,64,256]{2,1,0:T(8,128)(2,1)S(1)} %collective-permute-done.33.refs_4_), channel_id=1, source_target_pairs={{0,4},{1,5},{2,6},{3,7},{4,0},{5,1},{6,2},{7,3},{8,12},{9,13},{10,... | collective-permute-start | bytes 294920 | tf_op jit(solution)/shard_map/ppermute | solution.py:24
  87.5 4.6 %collective-permute-start.41 = (bf16[3,64,256]{2,1,0:T(8,128)(2,1)S(1)}, bf16[3,64,256]{2,1,0:T(8,128)(2,1)S(1)}, u32[]{:S(2)}, u32[]{:S(2)}) collective-permute-start(bf16[3,64,256]{2,1,0:T(8,128)(2,1)S(1)} %collective-permute-done.31.refs_8_), channel_id=1, source_target_pairs={{0,2},{1,3},{2,0},{3,1},{4,6},{5,7},{6,4},{7,5},{8,10},{9,11},{10,... | collective-permute-start | bytes 294920 | tf_op jit(solution)/shard_map/ppermute | solution.py:24
  89.2 5.7 %collective-permute-start.45 = (bf16[3,64,256]{2,1,0:T(8,128)(2,1)S(1)}, bf16[3,64,256]{2,1,0:T(8,128)(2,1)S(1)}, u32[]{:S(2)}, u32[]{:S(2)}) collective-permute-start(bf16[3,64,256]{2,1,0:T(8,128)(2,1)S(1)} %collective-permute-done.32.refs_12_), channel_id=1, source_target_pairs={{0,4},{1,5},{2,6},{3,7},{4,0},{5,1},{6,2},{7,3},{8,12},{9,13},{10,... | collective-permute-start | bytes 294920 | tf_op jit(solution)/shard_map/ppermute | solution.py:24
  89.3 8.7 %collective-permute-start.39 = (bf16[3,64,256]{2,1,0:T(8,128)(2,1)S(1)}, bf16[3,64,256]{2,1,0:T(8,128)(2,1)S(1)}, u32[]{:S(2)}, u32[]{:S(2)}) collective-permute-start(bf16[3,64,256]{2,1,0:T(8,128)(2,1)S(1)} %collective-permute-done.37.refs_1_), channel_id=1, source_target_pairs={{0,4},{1,5},{2,6},{3,7},{4,0},{5,1},{6,2},{7,3},{8,12},{9,13},{10,... | collective-permute-start | bytes 294920 | tf_op jit(solution)/shard_map/ppermute | solution.py:24
  92.1 5.8 %collective-permute-start.42 = (bf16[3,64,256]{2,1,0:T(8,128)(2,1)S(1)}, bf16[3,64,256]{2,1,0:T(8,128)(2,1)S(1)}, u32[]{:S(2)}, u32[]{:S(2)}) collective-permute-start(bf16[3,64,256]{2,1,0:T(8,128)(2,1)S(1)} %collective-permute-done.40.refs_6_), channel_id=1, source_target_pairs={{0,2},{1,3},{2,0},{3,1},{4,6},{5,7},{6,4},{7,5},{8,10},{9,11},{10,... | collective-permute-start | bytes 294920 | tf_op jit(solution)/shard_map/ppermute | solution.py:24
  93.9 5.0 %collective-permute-start.43 = (bf16[3,64,256]{2,1,0:T(8,128)(2,1)S(1)}, bf16[3,64,256]{2,1,0:T(8,128)(2,1)S(1)}, u32[]{:S(2)}, u32[]{:S(2)}) collective-permute-start(bf16[3,64,256]{2,1,0:T(8,128)(2,1)S(1)} %collective-permute-done.31.refs_8_), channel_id=1, source_target_pairs={{0,4},{1,5},{2,6},{3,7},{4,0},{5,1},{6,2},{7,3},{8,12},{9,13},{10,... | collective-permute-start | bytes 294920 | tf_op jit(solution)/shard_map/ppermute | solution.py:24
  94.9 5.6 %collective-permute-start.44 = (bf16[3,64,256]{2,1,0:T(8,128)(2,1)S(1)}, bf16[3,64,256]{2,1,0:T(8,128)(2,1)S(1)}, u32[]{:S(2)}, u32[]{:S(2)}) collective-permute-start(bf16[3,64,256]{2,1,0:T(8,128)(2,1)S(1)} %collective-permute-done.41.refs_9_), channel_id=1, source_target_pairs={{0,4},{1,5},{2,6},{3,7},{4,0},{5,1},{6,2},{7,3},{8,12},{9,13},{10,... | collective-permute-start | bytes 294920 | tf_op jit(solution)/shard_map/ppermute | solution.py:24
  95.9 4.6 %collective-permute-start.46 = (bf16[3,64,256]{2,1,0:T(8,128)(2,1)S(1)}, bf16[3,64,256]{2,1,0:T(8,128)(2,1)S(1)}, u32[]{:S(2)}, u32[]{:S(2)}) collective-permute-start(bf16[3,64,256]{2,1,0:T(8,128)(2,1)S(1)} %collective-permute-done.45.refs_14_), channel_id=1, source_target_pairs={{0,2},{1,3},{2,0},{3,1},{4,6},{5,7},{6,4},{7,5},{8,10},{9,11},{10,... | collective-permute-start | bytes 294920 | tf_op jit(solution)/shard_map/ppermute | solution.py:24
  97.9 2.6 %copy-start.3 = (s32[32]{0:T(128)S(1)}, s32[32]{0:T(128)}, u32[]{:S(2)}) copy-start(s32[32]{0:T(128)} %slots.5) | copy-start | bytes 388
  97.9 4.9 %copy-start = (bf16[1,256,1024]{2,1,0:T(8,128)(2,1)S(1)}, bf16[1,256,1024]{2,1,0:T(8,128)(2,1)}, u32[]{:S(2)}) copy-start(bf16[1,256,1024]{2,1,0:T(8,128)(2,1)} %param.14) | copy-start | bytes 1572868
  102.7 2.3 %collective-permute-start.47 = (bf16[256,1024]{1,0:T(8,128)(2,1)S(1)}, bf16[256,1024]{1,0:T(8,128)(2,1)S(1)}, u32[]{:S(2)}, u32[]{:S(2)}) collective-permute-start(bf16[256,1024]{1,0:T(8,128)(2,1)S(1)} %get-tuple-element.90), channel_id=1, source_target_pairs={{0,1},{1,0},{2,3},{3,2},{4,5},{5,4},{6,7},{7,6},{8,9},{9,8},{10,11... | collective-permute-start | bytes 1572872 | tf_op jit(solution)/shard_map/ppermute | solution.py:24

commit v5 on v4

--- a/solution.py
+++ b/solution.py
@@ -32,16 +32,11 @@
     return (master_new, first_new, second_new)
 
 
-def place_pieces(chip, pieces, weights, sems):
+def place_pieces(chip, pieces, weights):
     rows = pieces[0].shape[1]
-    copies = []
     for j, piece in enumerate(pieces):
         start = pl.multiple_of(lax.bitwise_xor(chip, j) * rows, rows)
-        copies.append(pltpu.make_async_copy(piece, weights.at[:, pl.ds(start, rows), :], sems.at[j]))
-    for copy in copies:
-        copy.start()
-    for copy in copies:
-        copy.wait()
+        weights[:, pl.ds(start, rows), :] = piece[...]
 
 
 def transpose_kernel(own_x, other_x, own_c, other_c, x_turned, c_turned):
@@ -61,21 +56,20 @@
 
 def places(outs):
     found = []
-    for zj in range(len(outs) // 3):
-        own, later, pair = outs[3 * zj : 3 * zj + 3]
-        by_x, by_y = ((pair, (1,)), (later, ())) if zj % 2 else ((later, ()), (pair, (1,)))
-        found += [(own, ()), by_x, by_y, (pair, (0,))]
+    for zj in range(2 * len(outs) // 5):
+        here = outs[5 * (zj // 2) : 5 * (zj // 2) + 5]
+        found += [(here[zj % 2], ())] + [(pair, (zj % 2,)) for pair in here[2:]]
     return found
 
 
 def backward_kernel(count, slots, own_live, other_live, *refs):
     pieces = refs[:count]
     own_x, other_x, own_c, other_c, x_turned, c_turned = refs[count : count + 6]
-    weights, gate_grad, up_grad, hidden_all, sems = refs[-5:]
-    outs = places(refs[count + 6 : -5])
+    weights, gate_grad, up_grad, hidden_all = refs[-4:]
+    outs = places(refs[count + 6 : -4])
     me_index = lax.axis_index("dev")
     core = me_index & CORE
-    place_pieces(me_index // 2, pieces, weights, sems)
+    place_pieces(me_index // 2, pieces, weights)
     tokens = own_x.shape[0]
     sides = ((own_x, own_c, me_index, own_live), (other_x, other_c, me_index ^ CORE, other_live))
     for part, (x_ref, c_ref, slot, live) in enumerate(sides):
@@ -108,30 +102,20 @@
 
 def forward_kernel(count, slots, *refs):
     pieces = refs[:count]
-    y_ref, out_ref, matches, weights, sems = refs[count:]
+    own_y, other_y, own_out, other_out, matches, weights = refs[count:]
     me_index = lax.axis_index("dev")
-    place_pieces(me_index // 2, pieces, weights, sems)
+    place_pieces(me_index // 2, pieces, weights)
     matches[0] = jnp.where(slots[me_index] == (me_index & CORE), 1, 0)
-    gate_pre = jnp.dot(y_ref[...], weights[0], preferred_element_type=jnp.float32)
-    up_pre = jnp.dot(y_ref[...], weights[1], preferred_element_type=jnp.float32)
-    act = (gate_pre * jax.nn.sigmoid(gate_pre) * up_pre).astype(jnp.bfloat16)
-    result = lax.dot_general(act, weights[2], (((1,), (1,)), ((), ())), preferred_element_type=jnp.float32)
-    out_ref[...] = result.astype(jnp.bfloat16)
-
-
-def choose_kernel(matches, own_out, other_out, out, sem):
-    for wanted, source in ((1, own_out), (0, other_out)):
-
-        @pl.when(matches[0] == wanted)
-        def move():
-            copy = pltpu.make_async_copy(source, out, sem)
-            copy.start()
-            copy.wait()
+    for y_ref, out_ref in ((other_y, other_out), (own_y, own_out)):
+        gate_pre = jnp.dot(y_ref[...], weights[0], preferred_element_type=jnp.float32)
+        up_pre = jnp.dot(y_ref[...], weights[1], preferred_element_type=jnp.float32)
+        act = (gate_pre * jax.nn.sigmoid(gate_pre) * up_pre).astype(jnp.bfloat16)
+        result = lax.dot_general(act, weights[2], (((1,), (1,)), ((), ())), preferred_element_type=jnp.float32)
+        out_ref[...] = result.astype(jnp.bfloat16)
 
 
 VMEM = pl.BlockSpec(memory_space=pltpu.VMEM)
 SMEM = pl.BlockSpec(memory_space=pltpu.SMEM)
-ANY = pl.BlockSpec(memory_space=pl.ANY)
 
 
 def params():
@@ -159,15 +143,14 @@
     two = jax.ShapeDtypeStruct((2, kinds, rows, units), jnp.bfloat16)
     return pl.pallas_call(
         functools.partial(backward_kernel, count),
-        out_shape=[one, one, two] * (count // 4),
-        in_specs=[SMEM] * 3 + [ANY] * count + [VMEM] * 6,
-        out_specs=[VMEM] * (3 * count // 4),
+        out_shape=[one, one, two, two, two] * (count // 8),
+        in_specs=[SMEM] * 3 + [VMEM] * (count + 6),
+        out_specs=[VMEM] * (5 * count // 8),
         scratch_shapes=[
             pltpu.VMEM((kinds, width, units), jnp.bfloat16),
             pltpu.VMEM((2 * tokens, units), jnp.bfloat16),
             pltpu.VMEM((2 * tokens, units), jnp.bfloat16),
             pltpu.VMEM((2 * tokens, units), jnp.bfloat16),
-            pltpu.SemaphoreType.DMA((count,)),
         ],
         compiler_params=params(),
         cost_estimate=pl.CostEstimate(
@@ -179,42 +162,25 @@
     )(slots, own_live, other_live, *pieces, own_x, other_x, own_c, other_c, x_turned, c_turned)
 
 
-def forward(slots, pieces, rows_in):
+def forward(slots, pieces, own_y, other_y):
     count = len(pieces)
     kinds, rows, units = pieces[0].shape
-    tokens, width = rows_in.shape
+    tokens, width = own_y.shape
+    one = jax.ShapeDtypeStruct((tokens, width), jnp.bfloat16)
     return pl.pallas_call(
         functools.partial(forward_kernel, count),
-        out_shape=[
-            jax.ShapeDtypeStruct((tokens, width), jnp.bfloat16),
-            jax.ShapeDtypeStruct((1,), jnp.int32),
-        ],
-        in_specs=[SMEM] + [ANY] * count + [VMEM],
-        out_specs=[VMEM, SMEM],
-        scratch_shapes=[
-            pltpu.VMEM((kinds, width, units), jnp.bfloat16),
-            pltpu.SemaphoreType.DMA((count,)),
-        ],
+        out_shape=[one, one, jax.ShapeDtypeStruct((1,), jnp.int32)],
+        in_specs=[SMEM] + [VMEM] * (count + 2),
+        out_specs=[VMEM, VMEM, SMEM],
+        scratch_shapes=[pltpu.VMEM((kinds, width, units), jnp.bfloat16)],
         compiler_params=params(),
         cost_estimate=pl.CostEstimate(
-            flops=6 * tokens * width * units,
-            bytes_accessed=4 * tokens * width + 6 * width * units,
-            transcendentals=tokens * units,
+            flops=12 * tokens * width * units,
+            bytes_accessed=8 * tokens * width + 6 * width * units,
+            transcendentals=2 * tokens * units,
         ),
         name="expert_outputs",
-    )(slots, *pieces, rows_in)
-
-
-def choose(matches, own_out, other_out):
-    return pl.pallas_call(
-        choose_kernel,
-        out_shape=jax.ShapeDtypeStruct(own_out.shape, own_out.dtype),
-        in_specs=[SMEM, ANY, ANY],
-        out_specs=ANY,
-        scratch_shapes=[pltpu.SemaphoreType.DMA],
-        compiler_params=params(),
-        name="choose_outputs",
-    )(matches, own_out, other_out)
+    )(slots, *pieces, own_y, other_y)
 
 
 def after(value, *others):
@@ -255,24 +221,19 @@
 
 
 def reduce_chips(pieces):
-    depth = lax.axis_size("dev") // Z_UNIT
-    column = [[pieces[3 * zj]] for zj in range(depth)]
-    crossed, turned = (), ()
-    for upper in reversed(range(1, depth, 2)):
-        up_y, pair_x = pieces[3 * upper + 1 : 3 * upper + 3]
-        below_x, pair_y = pieces[3 * upper - 2 : 3 * upper]
-        got_x = hop(after(pair_x, *crossed), X_STEP)
-        got_y = hop(after(pair_y, *turned), Y_STEP)
-        column[upper] += [got_x[1], hop(add_all(up_y, got_x[0]).astype(jnp.bfloat16), Y_STEP)]
-        column[upper - 1] += [got_y[1], hop(add_all(below_x, got_y[0]).astype(jnp.bfloat16), X_STEP)]
-        crossed, turned = (got_x,), (got_y,)
-        for zj in (upper, upper - 1):
-            top = 1 << zj.bit_length() - 1 if zj else 0
-            low = zj - top
+    total, arrived = None, ()
+    for pair in reversed(range(len(pieces) // 5)):
+        low, high, by_x, by_y, across = pieces[5 * pair : 5 * pair + 5]
+        across = hop(after(across, *arrived), X_STEP | Y_STEP)
+        by_x = hop(after(by_x, *arrived), X_STEP)
+        by_y = hop(after(by_y, *arrived), Y_STEP)
+        arrived = (by_x,)
+        for zj, own in ((2 * pair + 1, high), (2 * pair, low)):
+            column = add_all(own, by_x[zj % 2], by_y[zj % 2], across[zj % 2])
             if zj:
-                part = add_all(*column[zj]).astype(jnp.bfloat16)
-                column[top if low else 0].append(hop(part, (low or top) * Z_UNIT))
-    return add_all(*column[0])
+                column = hop(column.astype(jnp.bfloat16), zj * Z_UNIT).astype(jnp.float32)
+            total = column if total is None else total + column
+    return total
 
 
 def block_a_core(master, first, second, old_rows, old_cotangent, new_rows, old_slots, new_slots, live):
@@ -323,16 +284,13 @@
     updated = jnp.stack(updated)
     own_part = lax.dynamic_slice_in_dim(updated, core * local_rows, local_rows, 2)
     other_part = lax.dynamic_slice_in_dim(updated, (1 - core) * local_rows, local_rows, 2)
-    from_other = hop(after(other_part, new_pieces[-3]), CORE)
+    from_other = hop(other_part, CORE)
     state = jnp.where(
         core == 0, jnp.stack([own_part, from_other], axis=1), jnp.stack([from_other, own_part], axis=1)
     )
-    state = (state[0], state[1], state[2])
-    other_y, *state = lax.optimization_barrier((other_y,) + state)
-    other_out, matches = forward(new_slots, new_pieces, other_y)
-    own_out, matches = forward(new_slots, new_pieces, after(new_rows, other_out))
-    new_outputs = choose(matches, own_out, hop(other_out, CORE))
-    return (*state, new_outputs[None])
+    own_out, other_out, matches = forward(new_slots, new_pieces, new_rows, other_y)
+    new_outputs = jnp.where(matches[0] == 1, own_out, hop(other_out, CORE))
+    return (state[0], state[1], state[2], new_outputs[None])
 
 
 def hidden_terms(tokens, cotangent, weights, live):

time: 107 us -> 91 us (0.85)
  starting transfers between devices: 55 us -> 46.6 us
  Pallas kernels: 10.6 us -> 5.74 us
  waiting for transfers between devices: 36 us -> 32.4 us
    ppermute x48 -> x46, starting transfers between devices: 55 us -> 46.6 us  [hop(): lax.ppermute(block, 'dev', [(low, low ^ mask) for low in range(count)])]
    pallas_call x3 -> x1, Pallas kernels: 5.91 us -> 1.85 us  [forward(): pl.pallas_call(functools.partial(forward_kernel, count), out_shape=[one,...]
    ppermute x48 -> x46, waiting for transfers between devices: 36 us -> 32.4 us  [hop(): lax.ppermute(block, 'dev', [(low, low ^ mask) for low in range(count)])]
  transfers between devices with their start and end apart: 48 -> 46, of which waited for: 25 -> 25; matrix products, arithmetic and copies ran while one was open for 3% -> 3% of each run, Pallas kernels for 3% -> 3%
where the time goes in v5:
time: 91 us; the launch traced here: 90.8 us
  starting transfers between devices  46.6 us (51%)
  waiting for transfers between devices  32.4 us (36%)
  Pallas kernels  5.74 us (6%)
  local copies, waits for them, and re-layouts  2.31 us (3%)
  between operations  2.16 us (2%)
  other arithmetic  1.49 us (2%)
    ppermute x46, starting transfers between devices, hop(): lax.ppermute(block, 'dev', [(low, low ^ mask) for low in range(count)])  46.6 us
    ppermute x46, waiting for transfers between devices, hop(): lax.ppermute(block, 'dev', [(low, low ^ mask) for low in range(count)])  32.4 us
    pallas_call x1, Pallas kernels, backward(): pl.pallas_call(functools.partial(backward_kernel, count), out_shape=[one,...  3.3 us
    pallas_call x1, Pallas kernels, forward(): pl.pallas_call(functools.partial(forward_kernel, count), out_shape=[one,...  1.85 us
  transfers between devices with their start and end apart: 46, of which 25 were waited for; matrix products, arithmetic and copies ran while one was open for 3% of the time, Pallas kernels for 3%

profile of v5, /device:TPU:0, one launch (start us, length us, event | category | flops | bytes accessed | tf_op | source)
XLA Modules:
  0.0 90.8 jit_solution(2786701058324944198)
XLA Ops:
  0.6 0.5 collective-permute-start.3
  1.2 0.4 collective-permute-start.1
  1.7 1.1 %dynamic-slice_bitcast_fusion.2 = (f32[3,32,256]{2,1,0:T(8,128)S(1)}, f32[1,3,32,256]{3,2,1,0:T(8,128)S(1)}, f32[1,3,32,256]{3,2,1,0:T(8,128)S(1)}, f32[3,32,256]{2,1,0:T(8,128)S(1)}) fusion(f32[2,3,32,256]{3,2,1,0:T(8,128)} %param.10, s32[]{:T(128)S(6)} %select_n.51, s32[]{:T(128)S(6)} %select_n.52, f32[2,3,32,256]{3,2,1,0:T(8,128)} %param.9), kind=kLoop, calls=%fused_computation.49 | loop fusion | bytes 786440 | tf_op jit(solution)/shard_map/jit(dynamic_index_in_dim)/squeeze | solution.py:244
  3.0 0.4 collective-permute-start.2
  3.7 0.2 copy-done
  3.9 0.6 transpose_rows.1
  4.5 0.3 collective-permute-done.2.other_live
  4.8 4.0 %collective-permute-start.11 = (bf16[3,64,256]{2,1,0:T(8,128)(2,1)S(1)}, bf16[3,64,256]{2,1,0:T(8,128)(2,1)S(1)}, u32[]{:S(2)}, u32[]{:S(2)}) collective-permute-start(bf16[3,64,256]{2,1,0:T(8,128)(2,1)S(1)} %fusion.8.refs_0_), channel_id=1, source_target_pairs={{0,16},{1,17},{2,18},{3,19},{4,20},{5,21},{6,22},{7,23},{8,24},{9,... | collective-permute-start | bytes 294920 | tf_op jit(solution)/shard_map/ppermute | solution.py:24
  8.8 1.6 %collective-permute-start.8 = (bf16[3,64,256]{2,1,0:T(8,128)(2,1)S(1)}, bf16[3,64,256]{2,1,0:T(8,128)(2,1)S(1)}, u32[]{:S(2)}, u32[]{:S(2)}) collective-permute-start(bf16[3,64,256]{2,1,0:T(8,128)(2,1)S(1)} %fusion.8.refs_0_), channel_id=1, source_target_pairs={{0,8},{1,9},{2,10},{3,11},{4,12},{5,13},{6,14},{7,15},{8,0},{9,1},... | collective-permute-start | bytes 294920 | tf_op jit(solution)/shard_map/ppermute | solution.py:24
  10.3 1.5 %collective-permute-start.5 = (bf16[3,64,256]{2,1,0:T(8,128)(2,1)S(1)}, bf16[3,64,256]{2,1,0:T(8,128)(2,1)S(1)}, u32[]{:S(2)}, u32[]{:S(2)}) collective-permute-start(bf16[3,64,256]{2,1,0:T(8,128)(2,1)S(1)} %fusion.8.refs_0_), channel_id=1, source_target_pairs={{0,2},{1,3},{2,0},{3,1},{4,6},{5,7},{6,4},{7,5},{8,10},{9,11},{10,... | collective-permute-start | bytes 294920 | tf_op jit(solution)/shard_map/ppermute | solution.py:24
  11.8 1.5 %collective-permute-start.6 = (bf16[3,64,256]{2,1,0:T(8,128)(2,1)S(1)}, bf16[3,64,256]{2,1,0:T(8,128)(2,1)S(1)}, u32[]{:S(2)}, u32[]{:S(2)}) collective-permute-start(bf16[3,64,256]{2,1,0:T(8,128)(2,1)S(1)} %fusion.8.refs_0_), channel_id=1, source_target_pairs={{0,4},{1,5},{2,6},{3,7},{4,0},{5,1},{6,2},{7,3},{8,12},{9,13},{10,... | collective-permute-start | bytes 294920 | tf_op jit(solution)/shard_map/ppermute | solution.py:24
  13.3 0.8 collective-permute-done.11.refs_8_
  14.1 0.6 collective-permute-start.15
  14.8 1.5 %collective-permute-start.9 = (bf16[3,64,256]{2,1,0:T(8,128)(2,1)S(1)}, bf16[3,64,256]{2,1,0:T(8,128)(2,1)S(1)}, u32[]{:S(2)}, u32[]{:S(2)}) collective-permute-start(bf16[3,64,256]{2,1,0:T(8,128)(2,1)S(1)} %collective-permute-done.8.refs_4_), channel_id=1, source_target_pairs={{0,2},{1,3},{2,0},{3,1},{4,6},{5,7},{6,4},{7,5},{8,10},{9,11},{10,... | collective-permute-start | bytes 294920 | tf_op jit(solution)/shard_map/ppermute | solution.py:24
  16.3 1.5 %collective-permute-start.10 = (bf16[3,64,256]{2,1,0:T(8,128)(2,1)S(1)}, bf16[3,64,256]{2,1,0:T(8,128)(2,1)S(1)}, u32[]{:S(2)}, u32[]{:S(2)}) collective-permute-start(bf16[3,64,256]{2,1,0:T(8,128)(2,1)S(1)} %collective-permute-done.8.refs_4_), channel_id=1, source_target_pairs={{0,4},{1,5},{2,6},{3,7},{4,0},{5,1},{6,2},{7,3},{8,12},{9,13},{10,... | collective-permute-start | bytes 294920 | tf_op jit(solution)/shard_map/ppermute | solution.py:24
  17.8 0.5 collective-permute-start.12
  18.3 0.4 collective-permute-done.15.refs_12_
  18.7 0.6 collective-permute-done.9.refs_5_
  19.4 2.3 %collective-permute-start.16 = (bf16[3,64,256]{2,1,0:T(8,128)(2,1)S(1)}, bf16[3,64,256]{2,1,0:T(8,128)(2,1)S(1)}, u32[]{:S(2)}, u32[]{:S(2)}) collective-permute-start(bf16[3,64,256]{2,1,0:T(8,128)(2,1)S(1)} %collective-permute-done.15.refs_12_), channel_id=1, source_target_pairs={{0,2},{1,3},{2,0},{3,1},{4,6},{5,7},{6,4},{7,5},{8,10},{9,11},{10,... | collective-permute-start | bytes 294920 | tf_op jit(solution)/shard_map/ppermute | solution.py:24
  21.6 1.6 %collective-permute-start.18 = (bf16[3,64,256]{2,1,0:T(8,128)(2,1)S(1)}, bf16[3,64,256]{2,1,0:T(8,128)(2,1)S(1)}, u32[]{:S(2)}, u32[]{:S(2)}) collective-permute-start(bf16[3,64,256]{2,1,0:T(8,128)(2,1)S(1)} %collective-permute-done.15.refs_12_), channel_id=1, source_target_pairs={{0,4},{1,5},{2,6},{3,7},{4,0},{5,1},{6,2},{7,3},{8,12},{9,13},{10,... | collective-permute-start | bytes 294920 | tf_op jit(solution)/shard_map/ppermute | solution.py:24
  23.3 0.4 collective-permute-start.7
  23.7 1.6 %collective-permute-start.14 = (bf16[3,64,256]{2,1,0:T(8,128)(2,1)S(1)}, bf16[3,64,256]{2,1,0:T(8,128)(2,1)S(1)}, u32[]{:S(2)}, u32[]{:S(2)}) collective-permute-start(bf16[3,64,256]{2,1,0:T(8,128)(2,1)S(1)} %collective-permute-done.11.refs_8_), channel_id=1, source_target_pairs={{0,4},{1,5},{2,6},{3,7},{4,0},{5,1},{6,2},{7,3},{8,12},{9,13},{10,... | collective-permute-start | bytes 294920 | tf_op jit(solution)/shard_map/ppermute | solution.py:24
  25.3 0.5 collective-permute-start.13
  25.8 0.8 collective-permute-done.18.refs_14_
  26.6 0.7 collective-permute-start.19
  27.3 1.0 %collective-permute-start.17 = (bf16[3,64,256]{2,1,0:T(8,128)(2,1)S(1)}, bf16[3,64,256]{2,1,0:T(8,128)(2,1)S(1)}, u32[]{:S(2)}, u32[]{:S(2)}) collective-permute-start(bf16[3,64,256]{2,1,0:T(8,128)(2,1)S(1)} %collective-permute-done.12.refs_9_), channel_id=1, source_target_pairs={{0,4},{1,5},{2,6},{3,7},{4,0},{5,1},{6,2},{7,3},{8,12},{9,13},{10,... | collective-permute-start | bytes 294920 | tf_op jit(solution)/shard_map/ppermute | solution.py:24
  29.0 0.6 collective-permute-done.14.refs_10_
  29.6 0.3 collective-permute-done.13.refs_7_
  29.9 1.3 %collective-permute-done.19.refs_15_ = bf16[3,64,256]{2,1,0:T(8,128)(2,1)S(1)} collective-permute-done((bf16[3,64,256]{2,1,0:T(8,128)(2,1)S(1)}, bf16[3,64,256]{2,1,0:T(8,128)(2,1)S(1)}, u32[]{:S(2)}, u32[]{:S(2)}) %collective-permute-start.19) | collective-permute-done | bytes 98336 | tf_op jit(solution)/shard_map/ppermute | solution.py:24
  31.3 0.7 collective-permute-done.17.refs_11_
  32.0 3.3 %slot_gradients.1 = (bf16[3,64,256]{2,1,0:T(8,128)(2,1)S(1)}, bf16[3,64,256]{2,1,0:T(8,128)(2,1)S(1)}, bf16[2,3,64,256]{3,2,1,0:T(8,128)(2,1)S(1)}, bf16[2,3,64,...) custom-call(s32[32]{0:T(128)S(1)} %copy-done.3, ...), custom_call_target="tpu_custom_call" | custom-call | flops 1610612736 | bytes 7340032 | tf_op jit(solution)/shard_map/slot_gradients/pallas_call | solution.py:144
  35.3 1.4 %collective-permute-start.20 = (bf16[2,3,64,256]{3,2,1,0:T(8,128)(2,1)S(1)}, bf16[2,3,64,256]{3,2,1,0:T(8,128)(2,1)S(1)}, u32[]{:S(2)}, u32[]{:S(2)}) collective-permute-start(bf16[2,3,64,256]{3,2,1,0:T(8,128)(2,1)S(1)} %get-tuple-element.58), channel_id=1, source_target_pairs={{0,2},{1,3},{2,0},{3,1},{4,6},{5,7},{6,4},{7,5},{8,10},{9,11},{10,... | collective-permute-start | bytes 589832 | tf_op jit(solution)/shard_map/ppermute | solution.py:24
  36.7 1.7 %collective-permute-start.21 = (bf16[2,3,64,256]{3,2,1,0:T(8,128)(2,1)S(1)}, bf16[2,3,64,256]{3,2,1,0:T(8,128)(2,1)S(1)}, u32[]{:S(2)}, u32[]{:S(2)}) collective-permute-start(bf16[2,3,64,256]{3,2,1,0:T(8,128)(2,1)S(1)} %get-tuple-element.59), channel_id=1, source_target_pairs={{0,4},{1,5},{2,6},{3,7},{4,0},{5,1},{6,2},{7,3},{8,12},{9,13},{10,... | collective-permute-start | bytes 589832 | tf_op jit(solution)/shard_map/ppermute | solution.py:24
  38.3 0.5 collective-permute-start.22
  38.8 3.6 %collective-permute-done.20 = bf16[2,3,64,256]{3,2,1,0:T(8,128)(2,1)S(1)} collective-permute-done((bf16[2,3,64,256]{3,2,1,0:T(8,128)(2,1)S(1)}, bf16[2,3,64,256]{3,2,1,0:T(8,128)(2,1)S(1)}, u32[]{:S(2)}, u32[]{:S(2)}) %collective-permute-start.20) | collective-permute-done | bytes 196640 | tf_op jit(solution)/shard_map/ppermute | solution.py:24
  42.4 3.1 %collective-permute-start.27 = (bf16[2,3,64,256]{3,2,1,0:T(8,128)(2,1)S(1)}, bf16[2,3,64,256]{3,2,1,0:T(8,128)(2,1)S(1)}, u32[]{:S(2)}, u32[]{:S(2)}) collective-permute-start(bf16[2,3,64,256]{3,2,1,0:T(8,128)(2,1)S(1)} %get-tuple-element.68), channel_id=1, source_target_pairs={{0,6},{1,7},{2,4},{3,5},{4,2},{5,3},{6,0},{7,1},{8,14},{9,15},{10,... | collective-permute-start | bytes 589832 | tf_op jit(solution)/shard_map/ppermute | solution.py:24
  45.5 0.6 collective-permute-start.26
  46.1 4.0 %collective-permute-done.21 = bf16[2,3,64,256]{3,2,1,0:T(8,128)(2,1)S(1)} collective-permute-done((bf16[2,3,64,256]{3,2,1,0:T(8,128)(2,1)S(1)}, bf16[2,3,64,256]{3,2,1,0:T(8,128)(2,1)S(1)}, u32[]{:S(2)}, u32[]{:S(2)}) %collective-permute-start.21) | collective-permute-done | bytes 196640 | tf_op jit(solution)/shard_map/ppermute | solution.py:24
  50.2 3.4 %collective-permute-start.23 = (bf16[3,64,256]{2,1,0:T(8,128)(2,1)S(1)}, bf16[3,64,256]{2,1,0:T(8,128)(2,1)S(1)}, u32[]{:S(2)}, u32[]{:S(2)}) collective-permute-start(bf16[3,64,256]{2,1,0:T(8,128)(2,1)S(1)} %get-tuple-element.88), channel_id=1, source_target_pairs={{0,24},{1,25},{2,26},{3,27},{4,28},{5,29},{6,30},{7,31},{8,16},{9,... | collective-permute-start | bytes 294920 | tf_op jit(solution)/shard_map/ppermute | solution.py:24
  53.7 1.1 %collective-permute-start.28 = (bf16[3,64,256]{2,1,0:T(8,128)(2,1)S(1)}, bf16[3,64,256]{2,1,0:T(8,128)(2,1)S(1)}, u32[]{:S(2)}, u32[]{:S(2)}) collective-permute-start(bf16[3,64,256]{2,1,0:T(8,128)(2,1)S(1)} %fusion.5), channel_id=1, source_target_pairs={{0,8},{1,9},{2,10},{3,11},{4,12},{5,13},{6,14},{7,15},{8,0},{9,1},... | collective-permute-start | bytes 294920 | tf_op jit(solution)/shard_map/ppermute | solution.py:24
  54.9 2.6 %collective-permute-done.23 = bf16[3,64,256]{2,1,0:T(8,128)(2,1)S(1)} collective-permute-done((bf16[3,64,256]{2,1,0:T(8,128)(2,1)S(1)}, bf16[3,64,256]{2,1,0:T(8,128)(2,1)S(1)}, u32[]{:S(2)}, u32[]{:S(2)}) %collective-permute-start.23) | collective-permute-done | bytes 98336 | tf_op jit(solution)/shard_map/ppermute | solution.py:24
  57.5 4.3 %collective-permute-done.24 = bf16[3,64,256]{2,1,0:T(8,128)(2,1)S(1)} collective-permute-done((bf16[3,64,256]{2,1,0:T(8,128)(2,1)S(1)}, bf16[3,64,256]{2,1,0:T(8,128)(2,1)S(1)}, u32[]{:S(2)}, u32[]{:S(2)}) %collective-permute-start.24) | collective-permute-done | bytes 98336 | tf_op jit(solution)/shard_map/ppermute | solution.py:24
  61.8 0.3 fusion.11
  62.3 0.4 collective-permute-start.33
  62.7 4.4 %collective-permute-start.31 = (bf16[3,64,256]{2,1,0:T(8,128)(2,1)S(1)}, bf16[3,64,256]{2,1,0:T(8,128)(2,1)S(1)}, u32[]{:S(2)}, u32[]{:S(2)}) collective-permute-start(bf16[3,64,256]{2,1,0:T(8,128)(2,1)S(1)} %get-tuple-element.80.refs_0_), channel_id=1, source_target_pairs={{0,4},{1,5},{2,6},{3,7},{4,0},{5,1},{6,2},{7,3},{8,12},{9,13},{10,... | collective-permute-start | bytes 294920 | tf_op jit(solution)/shard_map/ppermute | solution.py:24
  67.1 0.7 collective-permute-done.36.refs_8_
  68.0 1.3 %collective-permute-start.34 = (bf16[3,64,256]{2,1,0:T(8,128)(2,1)S(1)}, bf16[3,64,256]{2,1,0:T(8,128)(2,1)S(1)}, u32[]{:S(2)}, u32[]{:S(2)}) collective-permute-start(bf16[3,64,256]{2,1,0:T(8,128)(2,1)S(1)} %collective-permute-done.33.refs_4_), channel_id=1, source_target_pairs={{0,2},{1,3},{2,0},{3,1},{4,6},{5,7},{6,4},{7,5},{8,10},{9,11},{10,... | collective-permute-start | bytes 294920 | tf_op jit(solution)/shard_map/ppermute | solution.py:24
  69.3 1.0 %collective-permute-done.31.refs_2_ = bf16[3,64,256]{2,1,0:T(8,128)(2,1)S(1)} collective-permute-done((bf16[3,64,256]{2,1,0:T(8,128)(2,1)S(1)}, bf16[3,64,256]{2,1,0:T(8,128)(2,1)S(1)}, u32[]{:S(2)}, u32[]{:S(2)}) %collective-permute-start.31) | collective-permute-done | bytes 98336 | tf_op jit(solution)/shard_map/ppermute | solution.py:24
  70.3 2.5 %collective-permute-done.30.refs_1_ = bf16[3,64,256]{2,1,0:T(8,128)(2,1)S(1)} collective-permute-done((bf16[3,64,256]{2,1,0:T(8,128)(2,1)S(1)}, bf16[3,64,256]{2,1,0:T(8,128)(2,1)S(1)}, u32[]{:S(2)}, u32[]{:S(2)}) %collective-permute-start.30) | collective-permute-done | bytes 98336 | tf_op jit(solution)/shard_map/ppermute | solution.py:24
  73.0 1.9 %collective-permute-done.34.refs_5_ = bf16[3,64,256]{2,1,0:T(8,128)(2,1)S(1)} collective-permute-done((bf16[3,64,256]{2,1,0:T(8,128)(2,1)S(1)}, bf16[3,64,256]{2,1,0:T(8,128)(2,1)S(1)}, u32[]{:S(2)}, u32[]{:S(2)}) %collective-permute-start.34) | collective-permute-done | bytes 98336 | tf_op jit(solution)/shard_map/ppermute | solution.py:24
  74.8 0.6 collective-permute-start.43
  75.4 1.5 %collective-permute-start.41 = (bf16[3,64,256]{2,1,0:T(8,128)(2,1)S(1)}, bf16[3,64,256]{2,1,0:T(8,128)(2,1)S(1)}, u32[]{:S(2)}, u32[]{:S(2)}) collective-permute-start(bf16[3,64,256]{2,1,0:T(8,128)(2,1)S(1)} %collective-permute-done.40.refs_12_), channel_id=1, source_target_pairs={{0,2},{1,3},{2,0},{3,1},{4,6},{5,7},{6,4},{7,5},{8,10},{9,11},{10,... | collective-permute-start | bytes 294920 | tf_op jit(solution)/shard_map/ppermute | solution.py:24
  77.0 0.4 collective-permute-done.35.refs_6_
  77.4 1.6 %collective-permute-start.39 = (bf16[3,64,256]{2,1,0:T(8,128)(2,1)S(1)}, bf16[3,64,256]{2,1,0:T(8,128)(2,1)S(1)}, u32[]{:S(2)}, u32[]{:S(2)}) collective-permute-start(bf16[3,64,256]{2,1,0:T(8,128)(2,1)S(1)} %collective-permute-done.36.refs_8_), channel_id=1, source_target_pairs={{0,4},{1,5},{2,6},{3,7},{4,0},{5,1},{6,2},{7,3},{8,12},{9,13},{10,... | collective-permute-start | bytes 294920 | tf_op jit(solution)/shard_map/ppermute | solution.py:24
  79.0 0.6 collective-permute-start.38
  79.6 0.4 collective-permute-done.41.refs_13_
  80.0 1.4 %collective-permute-start.42 = (bf16[3,64,256]{2,1,0:T(8,128)(2,1)S(1)}, bf16[3,64,256]{2,1,0:T(8,128)(2,1)S(1)}, u32[]{:S(2)}, u32[]{:S(2)}) collective-permute-start(bf16[3,64,256]{2,1,0:T(8,128)(2,1)S(1)} %collective-permute-done.37.refs_9_), channel_id=1, source_target_pairs={{0,4},{1,5},{2,6},{3,7},{4,0},{5,1},{6,2},{7,3},{8,12},{9,13},{10,... | collective-permute-start | bytes 294920 | tf_op jit(solution)/shard_map/ppermute | solution.py:24
  81.7 1.0 %collective-permute-done.39.refs_10_ = bf16[3,64,256]{2,1,0:T(8,128)(2,1)S(1)} collective-permute-done((bf16[3,64,256]{2,1,0:T(8,128)(2,1)S(1)}, bf16[3,64,256]{2,1,0:T(8,128)(2,1)S(1)}, u32[]{:S(2)}, u32[]{:S(2)}) %collective-permute-start.39) | collective-permute-done | bytes 98336 | tf_op jit(solution)/shard_map/ppermute | solution.py:24
  82.6 1.0 %collective-permute-done.38.refs_7_ = bf16[3,64,256]{2,1,0:T(8,128)(2,1)S(1)} collective-permute-done((bf16[3,64,256]{2,1,0:T(8,128)(2,1)S(1)}, bf16[3,64,256]{2,1,0:T(8,128)(2,1)S(1)}, u32[]{:S(2)}, u32[]{:S(2)}) %collective-permute-start.38) | collective-permute-done | bytes 98336 | tf_op jit(solution)/shard_map/ppermute | solution.py:24
  83.6 2.5 %collective-permute-done.44.refs_15_ = bf16[3,64,256]{2,1,0:T(8,128)(2,1)S(1)} collective-permute-done((bf16[3,64,256]{2,1,0:T(8,128)(2,1)S(1)}, bf16[3,64,256]{2,1,0:T(8,128)(2,1)S(1)}, u32[]{:S(2)}, u32[]{:S(2)}) %collective-permute-start.44) | collective-permute-done | bytes 98336 | tf_op jit(solution)/shard_map/ppermute | solution.py:24
  86.1 1.9 %expert_outputs.1 = (bf16[256,1024]{1,0:T(8,128)(2,1)S(1)}, bf16[256,1024]{1,0:T(8,128)(2,1)S(1)}, s32[1]{0:T(128)}) custom-call(s32[32]{0:T(128)S(1)} %copy-done.4, bf16[3,64,256]{2,1,0:T(8,128)(2,1)S(1)} %get-tuple-element.80.refs_0_, bf16[3,64,256]{2,1,0:T(8,128)(2,1)S(1)} %collective-permute-done.30.refs_1_, ...), custom_call_target="tpu_custom_call" | custom-call | flops 805306368 | bytes 3670016 | tf_op jit(solution)/shard_map/expert_outputs/pallas_call | solution.py:170
  88.1 0.8 slice_bitcast_fusion
  89.6 0.4 collective-permute-done.45
  89.9 0.8 select_bitcast_fusion
  (58 shorter events, 1.9 us)
Async XLA Ops:
  0.6 2.8 %collective-permute-start.3 = (bf16[256,1024]{1,0:T(8,128)(2,1)}, bf16[256,1024]{1,0:T(8,128)(2,1)S(1)}, u32[]{:S(2)}, u32[]{:S(2)}) collective-permute-start(bf16[256,1024]{1,0:T(8,128)(2,1)} %bitcast.95), channel_id=1, source_target_pairs={{0,1},{1,0},{2,3},{3,2},{4,5},{5,4},{6,7},{7,6},{8,9},{9,8},{10,11... | collective-permute-start | bytes 1572872 | tf_op jit(solution)/shard_map/ppermute | solution.py:24
  1.1 2.5 %collective-permute-start.4 = (bf16[256,1024]{1,0:T(8,128)(2,1)}, bf16[256,1024]{1,0:T(8,128)(2,1)S(1)}, u32[]{:S(2)}, u32[]{:S(2)}) collective-permute-start(bf16[256,1024]{1,0:T(8,128)(2,1)} %bitcast.98), channel_id=1, source_target_pairs={{0,1},{1,0},{2,3},{3,2},{4,5},{5,4},{6,7},{7,6},{8,9},{9,8},{10,11... | collective-permute-start | bytes 1572872 | tf_op jit(solution)/shard_map/ppermute | solution.py:24
  1.2 3.5 %collective-permute-start.1 = (bf16[256,1024]{1,0:T(8,128)(2,1)}, bf16[256,1024]{1,0:T(8,128)(2,1)S(1)}, u32[]{:S(2)}, u32[]{:S(2)}) collective-permute-start(bf16[256,1024]{1,0:T(8,128)(2,1)} %bitcast.101), channel_id=1, source_target_pairs={{0,1},{1,0},{2,3},{3,2},{4,5},{5,4},{6,7},{7,6},{8,9},{9,8},{10,11... | collective-permute-start | bytes 1572872 | tf_op jit(solution)/shard_map/ppermute | solution.py:24
  1.7 1.1 %copy-start.5 = (f32[2,3,32,256]{3,2,1,0:T(8,128)S(1)}, f32[2,3,32,256]{3,2,1,0:T(8,128)}, u32[]{:S(2)}) copy-start(f32[2,3,32,256]{3,2,1,0:T(8,128)} %param.11) | copy-start | bytes 589828
  1.7 2.0 %copy-start.1 = (bf16[1,256,1024]{2,1,0:T(8,128)(2,1)S(1)}, bf16[1,256,1024]{2,1,0:T(8,128)(2,1)}, u32[]{:S(2)}) copy-start(bf16[1,256,1024]{2,1,0:T(8,128)(2,1)} %param.13) | copy-start | bytes 1572868
  2.8 1.1 %copy-start = (bf16[1,256,1024]{2,1,0:T(8,128)(2,1)S(1)}, bf16[1,256,1024]{2,1,0:T(8,128)(2,1)}, u32[]{:S(2)}) copy-start(bf16[1,256,1024]{2,1,0:T(8,128)(2,1)} %param.12) | copy-start | bytes 1572868
  2.9 1.9 %collective-permute-start = (f32[3,3,32,256]{3,2,1,0:T(8,128)S(1)}, f32[3,3,32,256]{3,2,1,0:T(8,128)S(1)}, u32[]{:S(2)}, u32[]{:S(2)}) collective-permute-start(f32[3,3,32,256]{3,2,1,0:T(8,128)S(1)} %pad_maximum_fusion.1), channel_id=1, source_target_pairs={{0,1},{1,0},{2,3},{3,2},{4,5},{5,4},{6,7},{7,6},{8,9},{9,8},{10,11... | collective-permute-start | bytes 884744 | tf_op jit(solution)/shard_map/ppermute | solution.py:24
  3.0 1.7 %collective-permute-start.2 = (s32[1]{0:T(128)}, s32[1]{0:T(128)}, u32[]{:S(2)}, u32[]{:S(2)}) collective-permute-start(s32[1]{0:T(128)} %param.17), channel_id=1, source_target_pairs={{0,1},{1,0},{2,3},{3,2},{4,5},{5,4},{6,7},{7,6},{8,9},{9,8},{10,11... | collective-permute-start | bytes 20 | tf_op jit(solution)/shard_map/ppermute | solution.py:24
  4.8 27.2 %copy-start.3 = (s32[32]{0:T(128)S(1)}, s32[32]{0:T(128)}, u32[]{:S(2)}) copy-start(s32[32]{0:T(128)} %slots.2) | copy-start | bytes 388
  4.8 9.3 %collective-permute-start.11 = (bf16[3,64,256]{2,1,0:T(8,128)(2,1)S(1)}, bf16[3,64,256]{2,1,0:T(8,128)(2,1)S(1)}, u32[]{:S(2)}, u32[]{:S(2)}) collective-permute-start(bf16[3,64,256]{2,1,0:T(8,128)(2,1)S(1)} %fusion.8.refs_0_), channel_id=1, source_target_pairs={{0,16},{1,17},{2,18},{3,19},{4,20},{5,21},{6,22},{7,23},{8,24},{9,... | collective-permute-start | bytes 294920 | tf_op jit(solution)/shard_map/ppermute | solution.py:24
  8.8 6.0 %collective-permute-start.8 = (bf16[3,64,256]{2,1,0:T(8,128)(2,1)S(1)}, bf16[3,64,256]{2,1,0:T(8,128)(2,1)S(1)}, u32[]{:S(2)}, u32[]{:S(2)}) collective-permute-start(bf16[3,64,256]{2,1,0:T(8,128)(2,1)S(1)} %fusion.8.refs_0_), channel_id=1, source_target_pairs={{0,8},{1,9},{2,10},{3,11},{4,12},{5,13},{6,14},{7,15},{8,0},{9,1},... | collective-permute-start | bytes 294920 | tf_op jit(solution)/shard_map/ppermute | solution.py:24
  10.3 5.9 %collective-permute-start.5 = (bf16[3,64,256]{2,1,0:T(8,128)(2,1)S(1)}, bf16[3,64,256]{2,1,0:T(8,128)(2,1)S(1)}, u32[]{:S(2)}, u32[]{:S(2)}) collective-permute-start(bf16[3,64,256]{2,1,0:T(8,128)(2,1)S(1)} %fusion.8.refs_0_), channel_id=1, source_target_pairs={{0,2},{1,3},{2,0},{3,1},{4,6},{5,7},{6,4},{7,5},{8,10},{9,11},{10,... | collective-permute-start | bytes 294920 | tf_op jit(solution)/shard_map/ppermute | solution.py:24
  11.8 6.0 %collective-permute-start.6 = (bf16[3,64,256]{2,1,0:T(8,128)(2,1)S(1)}, bf16[3,64,256]{2,1,0:T(8,128)(2,1)S(1)}, u32[]{:S(2)}, u32[]{:S(2)}) collective-permute-start(bf16[3,64,256]{2,1,0:T(8,128)(2,1)S(1)} %fusion.8.refs_0_), channel_id=1, source_target_pairs={{0,4},{1,5},{2,6},{3,7},{4,0},{5,1},{6,2},{7,3},{8,12},{9,13},{10,... | collective-permute-start | bytes 294920 | tf_op jit(solution)/shard_map/ppermute | solution.py:24
  14.1 4.6 %collective-permute-start.15 = (bf16[3,64,256]{2,1,0:T(8,128)(2,1)S(1)}, bf16[3,64,256]{2,1,0:T(8,128)(2,1)S(1)}, u32[]{:S(2)}, u32[]{:S(2)}) collective-permute-start(bf16[3,64,256]{2,1,0:T(8,128)(2,1)S(1)} %collective-permute-done.11.refs_8_), channel_id=1, source_target_pairs={{0,8},{1,9},{2,10},{3,11},{4,12},{5,13},{6,14},{7,15},{8,0},{9,1},... | collective-permute-start | bytes 294920 | tf_op jit(solution)/shard_map/ppermute | solution.py:24
  14.8 4.6 %collective-permute-start.9 = (bf16[3,64,256]{2,1,0:T(8,128)(2,1)S(1)}, bf16[3,64,256]{2,1,0:T(8,128)(2,1)S(1)}, u32[]{:S(2)}, u32[]{:S(2)}) collective-permute-start(bf16[3,64,256]{2,1,0:T(8,128)(2,1)S(1)} %collective-permute-done.8.refs_4_), channel_id=1, source_target_pairs={{0,2},{1,3},{2,0},{3,1},{4,6},{5,7},{6,4},{7,5},{8,10},{9,11},{10,... | collective-permute-start | bytes 294920 | tf_op jit(solution)/shard_map/ppermute | solution.py:24
  16.3 7.4 %collective-permute-start.10 = (bf16[3,64,256]{2,1,0:T(8,128)(2,1)S(1)}, bf16[3,64,256]{2,1,0:T(8,128)(2,1)S(1)}, u32[]{:S(2)}, u32[]{:S(2)}) collective-permute-start(bf16[3,64,256]{2,1,0:T(8,128)(2,1)S(1)} %collective-permute-done.8.refs_4_), channel_id=1, source_target_pairs={{0,4},{1,5},{2,6},{3,7},{4,0},{5,1},{6,2},{7,3},{8,12},{9,13},{10,... | collective-permute-start | bytes 294920 | tf_op jit(solution)/shard_map/ppermute | solution.py:24
  17.8 7.5 %collective-permute-start.12 = (bf16[3,64,256]{2,1,0:T(8,128)(2,1)S(1)}, bf16[3,64,256]{2,1,0:T(8,128)(2,1)S(1)}, u32[]{:S(2)}, u32[]{:S(2)}) collective-permute-start(bf16[3,64,256]{2,1,0:T(8,128)(2,1)S(1)} %collective-permute-done.11.refs_8_), channel_id=1, source_target_pairs={{0,2},{1,3},{2,0},{3,1},{4,6},{5,7},{6,4},{7,5},{8,10},{9,11},{10,... | collective-permute-start | bytes 294920 | tf_op jit(solution)/shard_map/ppermute | solution.py:24
  19.4 6.4 %collective-permute-start.16 = (bf16[3,64,256]{2,1,0:T(8,128)(2,1)S(1)}, bf16[3,64,256]{2,1,0:T(8,128)(2,1)S(1)}, u32[]{:S(2)}, u32[]{:S(2)}) collective-permute-start(bf16[3,64,256]{2,1,0:T(8,128)(2,1)S(1)} %collective-permute-done.15.refs_12_), channel_id=1, source_target_pairs={{0,2},{1,3},{2,0},{3,1},{4,6},{5,7},{6,4},{7,5},{8,10},{9,11},{10,... | collective-permute-start | bytes 294920 | tf_op jit(solution)/shard_map/ppermute | solution.py:24
  21.6 5.0 %collective-permute-start.18 = (bf16[3,64,256]{2,1,0:T(8,128)(2,1)S(1)}, bf16[3,64,256]{2,1,0:T(8,128)(2,1)S(1)}, u32[]{:S(2)}, u32[]{:S(2)}) collective-permute-start(bf16[3,64,256]{2,1,0:T(8,128)(2,1)S(1)} %collective-permute-done.15.refs_12_), channel_id=1, source_target_pairs={{0,4},{1,5},{2,6},{3,7},{4,0},{5,1},{6,2},{7,3},{8,12},{9,13},{10,... | collective-permute-start | bytes 294920 | tf_op jit(solution)/shard_map/ppermute | solution.py:24
  23.3 5.8 %collective-permute-start.7 = (bf16[3,64,256]{2,1,0:T(8,128)(2,1)S(1)}, bf16[3,64,256]{2,1,0:T(8,128)(2,1)S(1)}, u32[]{:S(2)}, u32[]{:S(2)}) collective-permute-start(bf16[3,64,256]{2,1,0:T(8,128)(2,1)S(1)} %collective-permute-done.5.refs_1_), channel_id=1, source_target_pairs={{0,4},{1,5},{2,6},{3,7},{4,0},{5,1},{6,2},{7,3},{8,12},{9,13},{10,... | collective-permute-start | bytes 294920 | tf_op jit(solution)/shard_map/ppermute | solution.py:24
  23.7 6.0 %collective-permute-start.14 = (bf16[3,64,256]{2,1,0:T(8,128)(2,1)S(1)}, bf16[3,64,256]{2,1,0:T(8,128)(2,1)S(1)}, u32[]{:S(2)}, u32[]{:S(2)}) collective-permute-start(bf16[3,64,256]{2,1,0:T(8,128)(2,1)S(1)} %collective-permute-done.11.refs_8_), channel_id=1, source_target_pairs={{0,4},{1,5},{2,6},{3,7},{4,0},{5,1},{6,2},{7,3},{8,12},{9,13},{10,... | collective-permute-start | bytes 294920 | tf_op jit(solution)/shard_map/ppermute | solution.py:24
  25.3 4.6 %collective-permute-start.13 = (bf16[3,64,256]{2,1,0:T(8,128)(2,1)S(1)}, bf16[3,64,256]{2,1,0:T(8,128)(2,1)S(1)}, u32[]{:S(2)}, u32[]{:S(2)}) collective-permute-start(bf16[3,64,256]{2,1,0:T(8,128)(2,1)S(1)} %collective-permute-done.10.refs_6_), channel_id=1, source_target_pairs={{0,2},{1,3},{2,0},{3,1},{4,6},{5,7},{6,4},{7,5},{8,10},{9,11},{10,... | collective-permute-start | bytes 294920 | tf_op jit(solution)/shard_map/ppermute | solution.py:24
  26.6 4.6 %collective-permute-start.19 = (bf16[3,64,256]{2,1,0:T(8,128)(2,1)S(1)}, bf16[3,64,256]{2,1,0:T(8,128)(2,1)S(1)}, u32[]{:S(2)}, u32[]{:S(2)}) collective-permute-start(bf16[3,64,256]{2,1,0:T(8,128)(2,1)S(1)} %collective-permute-done.18.refs_14_), channel_id=1, source_target_pairs={{0,2},{1,3},{2,0},{3,1},{4,6},{5,7},{6,4},{7,5},{8,10},{9,11},{10,... | collective-permute-start | bytes 294920 | tf_op jit(solution)/shard_map/ppermute | solution.py:24
  27.3 4.6 %collective-permute-start.17 = (bf16[3,64,256]{2,1,0:T(8,128)(2,1)S(1)}, bf16[3,64,256]{2,1,0:T(8,128)(2,1)S(1)}, u32[]{:S(2)}, u32[]{:S(2)}) collective-permute-start(bf16[3,64,256]{2,1,0:T(8,128)(2,1)S(1)} %collective-permute-done.12.refs_9_), channel_id=1, source_target_pairs={{0,4},{1,5},{2,6},{3,7},{4,0},{5,1},{6,2},{7,3},{8,12},{9,13},{10,... | collective-permute-start | bytes 294920 | tf_op jit(solution)/shard_map/ppermute | solution.py:24
  35.3 7.2 %collective-permute-start.20 = (bf16[2,3,64,256]{3,2,1,0:T(8,128)(2,1)S(1)}, bf16[2,3,64,256]{3,2,1,0:T(8,128)(2,1)S(1)}, u32[]{:S(2)}, u32[]{:S(2)}) collective-permute-start(bf16[2,3,64,256]{3,2,1,0:T(8,128)(2,1)S(1)} %get-tuple-element.58), channel_id=1, source_target_pairs={{0,2},{1,3},{2,0},{3,1},{4,6},{5,7},{6,4},{7,5},{8,10},{9,11},{10,... | collective-permute-start | bytes 589832 | tf_op jit(solution)/shard_map/ppermute | solution.py:24
  36.7 13.5 %collective-permute-start.21 = (bf16[2,3,64,256]{3,2,1,0:T(8,128)(2,1)S(1)}, bf16[2,3,64,256]{3,2,1,0:T(8,128)(2,1)S(1)}, u32[]{:S(2)}, u32[]{:S(2)}) collective-permute-start(bf16[2,3,64,256]{3,2,1,0:T(8,128)(2,1)S(1)} %get-tuple-element.59), channel_id=1, source_target_pairs={{0,4},{1,5},{2,6},{3,7},{4,0},{5,1},{6,2},{7,3},{8,12},{9,13},{10,... | collective-permute-start | bytes 589832 | tf_op jit(solution)/shard_map/ppermute | solution.py:24
  38.3 11.8 %collective-permute-start.22 = (bf16[2,3,64,256]{3,2,1,0:T(8,128)(2,1)S(1)}, bf16[2,3,64,256]{3,2,1,0:T(8,128)(2,1)S(1)}, u32[]{:S(2)}, u32[]{:S(2)}) collective-permute-start(bf16[2,3,64,256]{3,2,1,0:T(8,128)(2,1)S(1)} %get-tuple-element.60), channel_id=1, source_target_pairs={{0,6},{1,7},{2,4},{3,5},{4,2},{5,3},{6,0},{7,1},{8,14},{9,15},{10,... | collective-permute-start | bytes 589832 | tf_op jit(solution)/shard_map/ppermute | solution.py:24
  42.4 11.2 %collective-permute-start.27 = (bf16[2,3,64,256]{3,2,1,0:T(8,128)(2,1)S(1)}, bf16[2,3,64,256]{3,2,1,0:T(8,128)(2,1)S(1)}, u32[]{:S(2)}, u32[]{:S(2)}) collective-permute-start(bf16[2,3,64,256]{3,2,1,0:T(8,128)(2,1)S(1)} %get-tuple-element.68), channel_id=1, source_target_pairs={{0,6},{1,7},{2,4},{3,5},{4,2},{5,3},{6,0},{7,1},{8,14},{9,15},{10,... | collective-permute-start | bytes 589832 | tf_op jit(solution)/shard_map/ppermute | solution.py:24
  45.5 8.1 %collective-permute-start.25 = (bf16[2,3,64,256]{3,2,1,0:T(8,128)(2,1)S(1)}, bf16[2,3,64,256]{3,2,1,0:T(8,128)(2,1)S(1)}, u32[]{:S(2)}, u32[]{:S(2)}) collective-permute-start(bf16[2,3,64,256]{3,2,1,0:T(8,128)(2,1)S(1)} %get-tuple-element.64), channel_id=1, source_target_pairs={{0,2},{1,3},{2,0},{3,1},{4,6},{5,7},{6,4},{7,5},{8,10},{9,11},{10,... | collective-permute-start | bytes 589832 | tf_op jit(solution)/shard_map/ppermute | solution.py:24
  45.5 8.1 %collective-permute-start.26 = (bf16[2,3,64,256]{3,2,1,0:T(8,128)(2,1)S(1)}, bf16[2,3,64,256]{3,2,1,0:T(8,128)(2,1)S(1)}, u32[]{:S(2)}, u32[]{:S(2)}) collective-permute-start(bf16[2,3,64,256]{3,2,1,0:T(8,128)(2,1)S(1)} %get-tuple-element.66), channel_id=1, source_target_pairs={{0,4},{1,5},{2,6},{3,7},{4,0},{5,1},{6,2},{7,3},{8,12},{9,13},{10,... | collective-permute-start | bytes 589832 | tf_op jit(solution)/shard_map/ppermute | solution.py:24
  50.2 7.2 %collective-permute-start.23 = (bf16[3,64,256]{2,1,0:T(8,128)(2,1)S(1)}, bf16[3,64,256]{2,1,0:T(8,128)(2,1)S(1)}, u32[]{:S(2)}, u32[]{:S(2)}) collective-permute-start(bf16[3,64,256]{2,1,0:T(8,128)(2,1)S(1)} %get-tuple-element.88), channel_id=1, source_target_pairs={{0,24},{1,25},{2,26},{3,27},{4,28},{5,29},{6,30},{7,31},{8,16},{9,... | collective-permute-start | bytes 294920 | tf_op jit(solution)/shard_map/ppermute | solution.py:24
  53.6 8.2 %collective-permute-start.24 = (bf16[3,64,256]{2,1,0:T(8,128)(2,1)S(1)}, bf16[3,64,256]{2,1,0:T(8,128)(2,1)S(1)}, u32[]{:S(2)}, u32[]{:S(2)}) collective-permute-start(bf16[3,64,256]{2,1,0:T(8,128)(2,1)S(1)} %get-tuple-element.89), channel_id=1, source_target_pairs={{0,16},{1,17},{2,18},{3,19},{4,20},{5,21},{6,22},{7,23},{8,24},{9,... | collective-permute-start | bytes 294920 | tf_op jit(solution)/shard_map/ppermute | solution.py:24
  53.7 8.1 %collective-permute-start.28 = (bf16[3,64,256]{2,1,0:T(8,128)(2,1)S(1)}, bf16[3,64,256]{2,1,0:T(8,128)(2,1)S(1)}, u32[]{:S(2)}, u32[]{:S(2)}) collective-permute-start(bf16[3,64,256]{2,1,0:T(8,128)(2,1)S(1)} %fusion.5), channel_id=1, source_target_pairs={{0,8},{1,9},{2,10},{3,11},{4,12},{5,13},{6,14},{7,15},{8,0},{9,1},... | collective-permute-start | bytes 294920 | tf_op jit(solution)/shard_map/ppermute | solution.py:24
  62.1 5.7 %collective-permute-start.36 = (bf16[3,64,256]{2,1,0:T(8,128)(2,1)S(1)}, bf16[3,64,256]{2,1,0:T(8,128)(2,1)S(1)}, u32[]{:S(2)}, u32[]{:S(2)}) collective-permute-start(bf16[3,64,256]{2,1,0:T(8,128)(2,1)S(1)} %get-tuple-element.80.refs_0_), channel_id=1, source_target_pairs={{0,16},{1,17},{2,18},{3,19},{4,20},{5,21},{6,22},{7,23},{8,24},{9,... | collective-permute-start | bytes 294920 | tf_op jit(solution)/shard_map/ppermute | solution.py:24
  62.3 5.7 %collective-permute-start.33 = (bf16[3,64,256]{2,1,0:T(8,128)(2,1)S(1)}, bf16[3,64,256]{2,1,0:T(8,128)(2,1)S(1)}, u32[]{:S(2)}, u32[]{:S(2)}) collective-permute-start(bf16[3,64,256]{2,1,0:T(8,128)(2,1)S(1)} %get-tuple-element.80.refs_0_), channel_id=1, source_target_pairs={{0,8},{1,9},{2,10},{3,11},{4,12},{5,13},{6,14},{7,15},{8,0},{9,1},... | collective-permute-start | bytes 294920 | tf_op jit(solution)/shard_map/ppermute | solution.py:24
  62.7 7.6 %collective-permute-start.31 = (bf16[3,64,256]{2,1,0:T(8,128)(2,1)S(1)}, bf16[3,64,256]{2,1,0:T(8,128)(2,1)S(1)}, u32[]{:S(2)}, u32[]{:S(2)}) collective-permute-start(bf16[3,64,256]{2,1,0:T(8,128)(2,1)S(1)} %get-tuple-element.80.refs_0_), channel_id=1, source_target_pairs={{0,4},{1,5},{2,6},{3,7},{4,0},{5,1},{6,2},{7,3},{8,12},{9,13},{10,... | collective-permute-start | bytes 294920 | tf_op jit(solution)/shard_map/ppermute | solution.py:24
  67.1 5.7 %collective-permute-start.30 = (bf16[3,64,256]{2,1,0:T(8,128)(2,1)S(1)}, bf16[3,64,256]{2,1,0:T(8,128)(2,1)S(1)}, u32[]{:S(2)}, u32[]{:S(2)}) collective-permute-start(bf16[3,64,256]{2,1,0:T(8,128)(2,1)S(1)} %get-tuple-element.80.refs_0_), channel_id=1, source_target_pairs={{0,2},{1,3},{2,0},{3,1},{4,6},{5,7},{6,4},{7,5},{8,10},{9,11},{10,... | collective-permute-start | bytes 294920 | tf_op jit(solution)/shard_map/ppermute | solution.py:24
  67.8 5.2 %collective-permute-start.40 = (bf16[3,64,256]{2,1,0:T(8,128)(2,1)S(1)}, bf16[3,64,256]{2,1,0:T(8,128)(2,1)S(1)}, u32[]{:S(2)}, u32[]{:S(2)}) collective-permute-start(bf16[3,64,256]{2,1,0:T(8,128)(2,1)S(1)} %collective-permute-done.36.refs_8_), channel_id=1, source_target_pairs={{0,8},{1,9},{2,10},{3,11},{4,12},{5,13},{6,14},{7,15},{8,0},{9,1},... | collective-permute-start | bytes 294920 | tf_op jit(solution)/shard_map/ppermute | solution.py:24
  68.0 6.8 %collective-permute-start.34 = (bf16[3,64,256]{2,1,0:T(8,128)(2,1)S(1)}, bf16[3,64,256]{2,1,0:T(8,128)(2,1)S(1)}, u32[]{:S(2)}, u32[]{:S(2)}) collective-permute-start(bf16[3,64,256]{2,1,0:T(8,128)(2,1)S(1)} %collective-permute-done.33.refs_4_), channel_id=1, source_target_pairs={{0,2},{1,3},{2,0},{3,1},{4,6},{5,7},{6,4},{7,5},{8,10},{9,11},{10,... | collective-permute-start | bytes 294920 | tf_op jit(solution)/shard_map/ppermute | solution.py:24
  72.8 4.6 %collective-permute-start.35 = (bf16[3,64,256]{2,1,0:T(8,128)(2,1)S(1)}, bf16[3,64,256]{2,1,0:T(8,128)(2,1)S(1)}, u32[]{:S(2)}, u32[]{:S(2)}) collective-permute-start(bf16[3,64,256]{2,1,0:T(8,128)(2,1)S(1)} %collective-permute-done.33.refs_4_), channel_id=1, source_target_pairs={{0,4},{1,5},{2,6},{3,7},{4,0},{5,1},{6,2},{7,3},{8,12},{9,13},{10,... | collective-permute-start | bytes 294920 | tf_op jit(solution)/shard_map/ppermute | solution.py:24
  72.8 6.2 %collective-permute-start.37 = (bf16[3,64,256]{2,1,0:T(8,128)(2,1)S(1)}, bf16[3,64,256]{2,1,0:T(8,128)(2,1)S(1)}, u32[]{:S(2)}, u32[]{:S(2)}) collective-permute-start(bf16[3,64,256]{2,1,0:T(8,128)(2,1)S(1)} %collective-permute-done.36.refs_8_), channel_id=1, source_target_pairs={{0,2},{1,3},{2,0},{3,1},{4,6},{5,7},{6,4},{7,5},{8,10},{9,11},{10,... | collective-permute-start | bytes 294920 | tf_op jit(solution)/shard_map/ppermute | solution.py:24
  74.8 6.6 %collective-permute-start.43 = (bf16[3,64,256]{2,1,0:T(8,128)(2,1)S(1)}, bf16[3,64,256]{2,1,0:T(8,128)(2,1)S(1)}, u32[]{:S(2)}, u32[]{:S(2)}) collective-permute-start(bf16[3,64,256]{2,1,0:T(8,128)(2,1)S(1)} %collective-permute-done.40.refs_12_), channel_id=1, source_target_pairs={{0,4},{1,5},{2,6},{3,7},{4,0},{5,1},{6,2},{7,3},{8,12},{9,13},{10,... | collective-permute-start | bytes 294920 | tf_op jit(solution)/shard_map/ppermute | solution.py:24
  75.4 4.6 %collective-permute-start.41 = (bf16[3,64,256]{2,1,0:T(8,128)(2,1)S(1)}, bf16[3,64,256]{2,1,0:T(8,128)(2,1)S(1)}, u32[]{:S(2)}, u32[]{:S(2)}) collective-permute-start(bf16[3,64,256]{2,1,0:T(8,128)(2,1)S(1)} %collective-permute-done.40.refs_12_), channel_id=1, source_target_pairs={{0,2},{1,3},{2,0},{3,1},{4,6},{5,7},{6,4},{7,5},{8,10},{9,11},{10,... | collective-permute-start | bytes 294920 | tf_op jit(solution)/shard_map/ppermute | solution.py:24
  76.9 9.2 %copy-start.2 = (bf16[1,256,1024]{2,1,0:T(8,128)(2,1)S(1)}, bf16[1,256,1024]{2,1,0:T(8,128)(2,1)}, u32[]{:S(2)}) copy-start(bf16[1,256,1024]{2,1,0:T(8,128)(2,1)} %param.14) | copy-start | bytes 1572868
  76.9 4.7 %collective-permute-start.32 = (bf16[3,64,256]{2,1,0:T(8,128)(2,1)S(1)}, bf16[3,64,256]{2,1,0:T(8,128)(2,1)S(1)}, u32[]{:S(2)}, u32[]{:S(2)}) collective-permute-start(bf16[3,64,256]{2,1,0:T(8,128)(2,1)S(1)} %collective-permute-done.30.refs_1_), channel_id=1, source_target_pairs={{0,4},{1,5},{2,6},{3,7},{4,0},{5,1},{6,2},{7,3},{8,12},{9,13},{10,... | collective-permute-start | bytes 294920 | tf_op jit(solution)/shard_map/ppermute | solution.py:24
  77.4 5.2 %collective-permute-start.39 = (bf16[3,64,256]{2,1,0:T(8,128)(2,1)S(1)}, bf16[3,64,256]{2,1,0:T(8,128)(2,1)S(1)}, u32[]{:S(2)}, u32[]{:S(2)}) collective-permute-start(bf16[3,64,256]{2,1,0:T(8,128)(2,1)S(1)} %collective-permute-done.36.refs_8_), channel_id=1, source_target_pairs={{0,4},{1,5},{2,6},{3,7},{4,0},{5,1},{6,2},{7,3},{8,12},{9,13},{10,... | collective-permute-start | bytes 294920 | tf_op jit(solution)/shard_map/ppermute | solution.py:24
  79.0 4.6 %collective-permute-start.38 = (bf16[3,64,256]{2,1,0:T(8,128)(2,1)S(1)}, bf16[3,64,256]{2,1,0:T(8,128)(2,1)S(1)}, u32[]{:S(2)}, u32[]{:S(2)}) collective-permute-start(bf16[3,64,256]{2,1,0:T(8,128)(2,1)S(1)} %collective-permute-done.35.refs_6_), channel_id=1, source_target_pairs={{0,2},{1,3},{2,0},{3,1},{4,6},{5,7},{6,4},{7,5},{8,10},{9,11},{10,... | collective-permute-start | bytes 294920 | tf_op jit(solution)/shard_map/ppermute | solution.py:24
  80.0 6.1 %collective-permute-start.42 = (bf16[3,64,256]{2,1,0:T(8,128)(2,1)S(1)}, bf16[3,64,256]{2,1,0:T(8,128)(2,1)S(1)}, u32[]{:S(2)}, u32[]{:S(2)}) collective-permute-start(bf16[3,64,256]{2,1,0:T(8,128)(2,1)S(1)} %collective-permute-done.37.refs_9_), channel_id=1, source_target_pairs={{0,4},{1,5},{2,6},{3,7},{4,0},{5,1},{6,2},{7,3},{8,12},{9,13},{10,... | collective-permute-start | bytes 294920 | tf_op jit(solution)/shard_map/ppermute | solution.py:24
  81.5 4.6 %collective-permute-start.44 = (bf16[3,64,256]{2,1,0:T(8,128)(2,1)S(1)}, bf16[3,64,256]{2,1,0:T(8,128)(2,1)S(1)}, u32[]{:S(2)}, u32[]{:S(2)}) collective-permute-start(bf16[3,64,256]{2,1,0:T(8,128)(2,1)S(1)} %collective-permute-done.43.refs_14_), channel_id=1, source_target_pairs={{0,2},{1,3},{2,0},{3,1},{4,6},{5,7},{6,4},{7,5},{8,10},{9,11},{10,... | collective-permute-start | bytes 294920 | tf_op jit(solution)/shard_map/ppermute | solution.py:24
  81.6 4.5 %copy-start.4 = (s32[32]{0:T(128)S(1)}, s32[32]{0:T(128)}, u32[]{:S(2)}) copy-start(s32[32]{0:T(128)} %slots.3) | copy-start | bytes 388
  81.6 6.4 %collective-permute-start.29 = (f32[3,3,32,256]{3,2,1,0:T(8,128)S(1)}, f32[3,3,32,256]{3,2,1,0:T(8,128)S(1)}, u32[]{:S(2)}, u32[]{:S(2)}) collective-permute-start(f32[3,3,32,256]{3,2,1,0:T(8,128)S(1)} %get-tuple-element.87), channel_id=1, source_target_pairs={{0,1},{1,0},{2,3},{3,2},{4,5},{5,4},{6,7},{7,6},{8,9},{9,8},{10,11... | collective-permute-start | bytes 884744 | tf_op jit(solution)/shard_map/ppermute | solution.py:24
  88.0 2.0 %collective-permute-start.45 = (bf16[256,1024]{1,0:T(8,128)(2,1)S(1)}, bf16[256,1024]{1,0:T(8,128)(2,1)S(1)}, u32[]{:S(2)}, u32[]{:S(2)}) collective-permute-start(bf16[256,1024]{1,0:T(8,128)(2,1)S(1)} %get-tuple-element.79), channel_id=1, source_target_pairs={{0,1},{1,0},{2,3},{3,2},{4,5},{5,4},{6,7},{7,6},{8,9},{9,8},{10,11... | collective-permute-start | bytes 1572872 | tf_op jit(solution)/shard_map/ppermute | solution.py:24

commit v6 on v5

--- a/solution.py
+++ b/solution.py
@@ -56,17 +56,33 @@
 
 def places(outs):
     found = []
-    for zj in range(2 * len(outs) // 5):
-        here = outs[5 * (zj // 2) : 5 * (zj // 2) + 5]
-        found += [(here[zj % 2], ())] + [(pair, (zj % 2,)) for pair in here[2:]]
+    for zj in range(len(outs) // 3):
+        own, later, pair = outs[3 * zj : 3 * zj + 3]
+        by_x, by_y = ((pair, (1,)), (later, ())) if zj % 2 else ((later, ()), (pair, (1,)))
+        found += [(own, ()), by_x, by_y, (pair, (0,))]
     return found
+
+
+def gradient_rows(first_row, products, outs):
+    outs = places(outs)
+    rows = outs[0][0].shape[1]
+    width = len(outs) * rows
+    tall = min(width, 256)
+    for at in range(0, width, tall):
+        for kind, (left, right) in enumerate(products):
+            product = jnp.dot(
+                left[first_row + at : first_row + at + tall], right[...], preferred_element_type=jnp.float32
+            ).astype(jnp.bfloat16)
+            for low in range(0, tall, rows):
+                out, before = outs[(at + low) // rows]
+                out[before + (kind,)] = product[low : low + rows]
 
 
 def backward_kernel(count, slots, own_live, other_live, *refs):
     pieces = refs[:count]
     own_x, other_x, own_c, other_c, x_turned, c_turned = refs[count : count + 6]
-    weights, gate_grad, up_grad, hidden_all = refs[-4:]
-    outs = places(refs[count + 6 : -4])
+    outs = refs[count + 6 : -4]
+    gate_grad, up_grad, hidden_all, weights = refs[-4:]
     me_index = lax.axis_index("dev")
     core = me_index & CORE
     place_pieces(me_index // 2, pieces, weights)
@@ -86,18 +102,8 @@
         hidden_all[span] = jnp.where(keep, gate_act * up_pre, 0.0).astype(jnp.bfloat16)
         up_grad[span] = jnp.where(keep, grad_up, 0.0).astype(jnp.bfloat16)
         gate_grad[span] = jnp.where(keep, grad_gate, 0.0).astype(jnp.bfloat16)
-    rows = pieces[0].shape[1]
-    width = count * rows
-    tall = min(width, 256)
-    for at in range(0, width, tall):
-        for kind, (left, right) in enumerate(
-            ((x_turned, gate_grad), (x_turned, up_grad), (c_turned, hidden_all))
-        ):
-            product = jnp.dot(left[at : at + tall], right[...], preferred_element_type=jnp.float32)
-            product = product.astype(jnp.bfloat16)
-            for low in range(0, tall, rows):
-                out, before = outs[(at + low) // rows]
-                out[before + (kind,)] = product[low : low + rows]
+    products = ((x_turned, gate_grad), (x_turned, up_grad), (c_turned, hidden_all))
+    gradient_rows(0, products, outs)
 
 
 def forward_kernel(count, slots, *refs):
@@ -143,14 +149,14 @@
     two = jax.ShapeDtypeStruct((2, kinds, rows, units), jnp.bfloat16)
     return pl.pallas_call(
         functools.partial(backward_kernel, count),
-        out_shape=[one, one, two, two, two] * (count // 8),
+        out_shape=[one, one, two] * (count // 4),
         in_specs=[SMEM] * 3 + [VMEM] * (count + 6),
-        out_specs=[VMEM] * (5 * count // 8),
+        out_specs=[VMEM] * (3 * count // 4),
         scratch_shapes=[
-            pltpu.VMEM((kinds, width, units), jnp.bfloat16),
             pltpu.VMEM((2 * tokens, units), jnp.bfloat16),
             pltpu.VMEM((2 * tokens, units), jnp.bfloat16),
             pltpu.VMEM((2 * tokens, units), jnp.bfloat16),
+            pltpu.VMEM((kinds, width, units), jnp.bfloat16),
         ],
         compiler_params=params(),
         cost_estimate=pl.CostEstimate(
@@ -221,19 +227,27 @@
 
 
 def reduce_chips(pieces):
-    total, arrived = None, ()
-    for pair in reversed(range(len(pieces) // 5)):
-        low, high, by_x, by_y, across = pieces[5 * pair : 5 * pair + 5]
-        across = hop(after(across, *arrived), X_STEP | Y_STEP)
-        by_x = hop(after(by_x, *arrived), X_STEP)
-        by_y = hop(after(by_y, *arrived), Y_STEP)
-        arrived = (by_x,)
-        for zj, own in ((2 * pair + 1, high), (2 * pair, low)):
-            column = add_all(own, by_x[zj % 2], by_y[zj % 2], across[zj % 2])
+    depth = lax.axis_size("dev") // Z_UNIT
+    column = [[pieces[3 * zj]] for zj in range(depth)]
+    arrived, crossed, risen = (), (), ()
+    for upper in reversed(range(1, depth, 2)):
+        up_y, pair_x = pieces[3 * upper + 1 : 3 * upper + 3]
+        below_x, pair_y = pieces[3 * upper - 2 : 3 * upper]
+        got_x = hop(pair_x, X_STEP)
+        got_y = hop(after(pair_y, *arrived), Y_STEP)
+        up_y = add_all(up_y, got_x[0]).astype(jnp.bfloat16)
+        column[upper] += [got_x[1], hop(after(up_y, *crossed), Y_STEP)]
+        below_x = add_all(below_x, got_y[0]).astype(jnp.bfloat16)
+        column[upper - 1] += [got_y[1], hop(after(below_x, *risen), X_STEP)]
+        arrived, crossed, risen = (got_x,), (column[upper][-1],), ()
+        for zj in (upper, upper - 1):
+            top = 1 << zj.bit_length() - 1 if zj else 0
+            low = zj - top
             if zj:
-                column = hop(column.astype(jnp.bfloat16), zj * Z_UNIT).astype(jnp.float32)
-            total = column if total is None else total + column
-    return total
+                part = add_all(*column[zj]).astype(jnp.bfloat16)
+                column[top if low else 0].append(hop(part, (low or top) * Z_UNIT))
+                risen = risen or (column[top if low else 0][-1],)
+    return add_all(*column[0])
 
 
 def block_a_core(master, first, second, old_rows, old_cotangent, new_rows, old_slots, new_slots, live):

time: 91 us -> 90.5 us (level)
  waiting for transfers between devices: 32.4 us -> 29.2 us
  starting transfers between devices: 46.6 us -> 49.4 us
    ppermute x46 -> x48, waiting for transfers between devices: 32.4 us -> 29.2 us  [hop(): lax.ppermute(block, 'dev', [(low, low ^ mask) for low in range(count)])]
    ppermute x46 -> x48, starting transfers between devices: 46.6 us -> 49.4 us  [hop(): lax.ppermute(block, 'dev', [(low, low ^ mask) for low in range(count)])]
  transfers between devices with their start and end apart: 46 -> 48, of which waited for: 25 -> 28; matrix products, arithmetic and copies ran while one was open for 3% -> 3% of each run, Pallas kernels for 3% -> 3%
where the time goes in v6:
time: 90.5 us; the launch traced here: 90.3 us
  starting transfers between devices  49.4 us (55%)
  waiting for transfers between devices  29.2 us (32%)
  Pallas kernels  5.75 us (6%)
  local copies, waits for them, and re-layouts  2.31 us (3%)
  between operations  2.18 us (2%)
  other arithmetic  1.47 us (2%)
    ppermute x48, starting transfers between devices, hop(): lax.ppermute(block, 'dev', [(low, low ^ mask) for low in range(count)])  49.4 us
    ppermute x48, waiting for transfers between devices, hop(): lax.ppermute(block, 'dev', [(low, low ^ mask) for low in range(count)])  29.2 us
    pallas_call x1, Pallas kernels, backward(): pl.pallas_call(functools.partial(backward_kernel, count), out_shape=[one,...  3.3 us
    pallas_call x1, Pallas kernels, forward(): pl.pallas_call(functools.partial(forward_kernel, count), out_shape=[one,...  1.85 us
  transfers between devices with their start and end apart: 48, of which 28 were waited for; matrix products, arithmetic and copies ran while one was open for 3% of the time, Pallas kernels for 3%

profile of v6, /device:TPU:0, one launch (start us, length us, event | category | flops | bytes accessed | tf_op | source)
XLA Modules:
  0.0 90.3 jit_solution(16805126077958624537)
XLA Ops:
  0.6 0.5 collective-permute-start.3
  1.2 0.4 collective-permute-start.1
  1.7 1.1 %dynamic-slice_bitcast_fusion.1 = (f32[3,32,256]{2,1,0:T(8,128)S(1)}, f32[1,3,32,256]{3,2,1,0:T(8,128)S(1)}, f32[1,3,32,256]{3,2,1,0:T(8,128)S(1)}, f32[3,32,256]{2,1,0:T(8,128)S(1)}) fusion(f32[2,3,32,256]{3,2,1,0:T(8,128)} %param.11, s32[]{:T(128)S(6)} %select_n.51, s32[]{:T(128)S(6)} %select_n.52, f32[2,3,32,256]{3,2,1,0:T(8,128)} %param.10), kind=kLoop, calls=%fused_computation.48 | loop fusion | bytes 786440 | tf_op jit(solution)/shard_map/jit(dynamic_index_in_dim)/squeeze | solution.py:258
  3.0 0.4 collective-permute-start.2
  3.9 0.6 transpose_rows.1
  4.8 4.0 %collective-permute-start.11 = (bf16[3,64,256]{2,1,0:T(8,128)(2,1)S(1)}, bf16[3,64,256]{2,1,0:T(8,128)(2,1)S(1)}, u32[]{:S(2)}, u32[]{:S(2)}) collective-permute-start(bf16[3,64,256]{2,1,0:T(8,128)(2,1)S(1)} %fusion.17.refs_0_), channel_id=1, source_target_pairs={{0,16},{1,17},{2,18},{3,19},{4,20},{5,21},{6,22},{7,23},{8,24},{9,... | collective-permute-start | bytes 294920 | tf_op jit(solution)/shard_map/ppermute | solution.py:24
  8.8 1.6 %collective-permute-start.8 = (bf16[3,64,256]{2,1,0:T(8,128)(2,1)S(1)}, bf16[3,64,256]{2,1,0:T(8,128)(2,1)S(1)}, u32[]{:S(2)}, u32[]{:S(2)}) collective-permute-start(bf16[3,64,256]{2,1,0:T(8,128)(2,1)S(1)} %fusion.17.refs_0_), channel_id=1, source_target_pairs={{0,8},{1,9},{2,10},{3,11},{4,12},{5,13},{6,14},{7,15},{8,0},{9,1},... | collective-permute-start | bytes 294920 | tf_op jit(solution)/shard_map/ppermute | solution.py:24
  10.3 1.5 %collective-permute-start.5 = (bf16[3,64,256]{2,1,0:T(8,128)(2,1)S(1)}, bf16[3,64,256]{2,1,0:T(8,128)(2,1)S(1)}, u32[]{:S(2)}, u32[]{:S(2)}) collective-permute-start(bf16[3,64,256]{2,1,0:T(8,128)(2,1)S(1)} %fusion.17.refs_0_), channel_id=1, source_target_pairs={{0,2},{1,3},{2,0},{3,1},{4,6},{5,7},{6,4},{7,5},{8,10},{9,11},{10,... | collective-permute-start | bytes 294920 | tf_op jit(solution)/shard_map/ppermute | solution.py:24
  11.8 1.5 %collective-permute-start.6 = (bf16[3,64,256]{2,1,0:T(8,128)(2,1)S(1)}, bf16[3,64,256]{2,1,0:T(8,128)(2,1)S(1)}, u32[]{:S(2)}, u32[]{:S(2)}) collective-permute-start(bf16[3,64,256]{2,1,0:T(8,128)(2,1)S(1)} %fusion.17.refs_0_), channel_id=1, source_target_pairs={{0,4},{1,5},{2,6},{3,7},{4,0},{5,1},{6,2},{7,3},{8,12},{9,13},{10,... | collective-permute-start | bytes 294920 | tf_op jit(solution)/shard_map/ppermute | solution.py:24
  13.3 0.8 collective-permute-done.11.refs_8_
  14.1 0.6 collective-permute-start.15
  14.8 1.5 %collective-permute-start.9 = (bf16[3,64,256]{2,1,0:T(8,128)(2,1)S(1)}, bf16[3,64,256]{2,1,0:T(8,128)(2,1)S(1)}, u32[]{:S(2)}, u32[]{:S(2)}) collective-permute-start(bf16[3,64,256]{2,1,0:T(8,128)(2,1)S(1)} %collective-permute-done.8.refs_4_), channel_id=1, source_target_pairs={{0,2},{1,3},{2,0},{3,1},{4,6},{5,7},{6,4},{7,5},{8,10},{9,11},{10,... | collective-permute-start | bytes 294920 | tf_op jit(solution)/shard_map/ppermute | solution.py:24
  16.3 1.5 %collective-permute-start.10 = (bf16[3,64,256]{2,1,0:T(8,128)(2,1)S(1)}, bf16[3,64,256]{2,1,0:T(8,128)(2,1)S(1)}, u32[]{:S(2)}, u32[]{:S(2)}) collective-permute-start(bf16[3,64,256]{2,1,0:T(8,128)(2,1)S(1)} %collective-permute-done.8.refs_4_), channel_id=1, source_target_pairs={{0,4},{1,5},{2,6},{3,7},{4,0},{5,1},{6,2},{7,3},{8,12},{9,13},{10,... | collective-permute-start | bytes 294920 | tf_op jit(solution)/shard_map/ppermute | solution.py:24
  17.8 0.5 collective-permute-start.12
  18.3 0.4 collective-permute-done.15.refs_12_
  18.7 0.6 collective-permute-done.9.refs_5_
  19.4 2.3 %collective-permute-start.16 = (bf16[3,64,256]{2,1,0:T(8,128)(2,1)S(1)}, bf16[3,64,256]{2,1,0:T(8,128)(2,1)S(1)}, u32[]{:S(2)}, u32[]{:S(2)}) collective-permute-start(bf16[3,64,256]{2,1,0:T(8,128)(2,1)S(1)} %collective-permute-done.15.refs_12_), channel_id=1, source_target_pairs={{0,2},{1,3},{2,0},{3,1},{4,6},{5,7},{6,4},{7,5},{8,10},{9,11},{10,... | collective-permute-start | bytes 294920 | tf_op jit(solution)/shard_map/ppermute | solution.py:24
  21.6 1.6 %collective-permute-start.18 = (bf16[3,64,256]{2,1,0:T(8,128)(2,1)S(1)}, bf16[3,64,256]{2,1,0:T(8,128)(2,1)S(1)}, u32[]{:S(2)}, u32[]{:S(2)}) collective-permute-start(bf16[3,64,256]{2,1,0:T(8,128)(2,1)S(1)} %collective-permute-done.15.refs_12_), channel_id=1, source_target_pairs={{0,4},{1,5},{2,6},{3,7},{4,0},{5,1},{6,2},{7,3},{8,12},{9,13},{10,... | collective-permute-start | bytes 294920 | tf_op jit(solution)/shard_map/ppermute | solution.py:24
  23.3 0.4 collective-permute-start.7
  23.7 1.6 %collective-permute-start.14 = (bf16[3,64,256]{2,1,0:T(8,128)(2,1)S(1)}, bf16[3,64,256]{2,1,0:T(8,128)(2,1)S(1)}, u32[]{:S(2)}, u32[]{:S(2)}) collective-permute-start(bf16[3,64,256]{2,1,0:T(8,128)(2,1)S(1)} %collective-permute-done.11.refs_8_), channel_id=1, source_target_pairs={{0,4},{1,5},{2,6},{3,7},{4,0},{5,1},{6,2},{7,3},{8,12},{9,13},{10,... | collective-permute-start | bytes 294920 | tf_op jit(solution)/shard_map/ppermute | solution.py:24
  25.3 0.5 collective-permute-start.13
  25.8 0.8 collective-permute-done.18.refs_14_
  26.6 0.7 collective-permute-start.19
  27.3 1.0 %collective-permute-start.17 = (bf16[3,64,256]{2,1,0:T(8,128)(2,1)S(1)}, bf16[3,64,256]{2,1,0:T(8,128)(2,1)S(1)}, u32[]{:S(2)}, u32[]{:S(2)}) collective-permute-start(bf16[3,64,256]{2,1,0:T(8,128)(2,1)S(1)} %collective-permute-done.12.refs_9_), channel_id=1, source_target_pairs={{0,4},{1,5},{2,6},{3,7},{4,0},{5,1},{6,2},{7,3},{8,12},{9,13},{10,... | collective-permute-start | bytes 294920 | tf_op jit(solution)/shard_map/ppermute | solution.py:24
  29.0 0.6 collective-permute-done.14.refs_10_
  29.6 0.3 collective-permute-done.13.refs_7_
  29.9 1.3 %collective-permute-done.19.refs_15_ = bf16[3,64,256]{2,1,0:T(8,128)(2,1)S(1)} collective-permute-done((bf16[3,64,256]{2,1,0:T(8,128)(2,1)S(1)}, bf16[3,64,256]{2,1,0:T(8,128)(2,1)S(1)}, u32[]{:S(2)}, u32[]{:S(2)}) %collective-permute-start.19) | collective-permute-done | bytes 98336 | tf_op jit(solution)/shard_map/ppermute | solution.py:24
  31.3 0.7 collective-permute-done.17.refs_11_
  32.0 3.3 %slot_gradients.1 = (bf16[3,64,256]{2,1,0:T(8,128)(2,1)S(1)}, bf16[3,64,256]{2,1,0:T(8,128)(2,1)S(1)}, bf16[2,3,64,256]{3,2,1,0:T(8,128)(2,1)S(1)}, bf16[3,64,25...) custom-call(s32[32]{0:T(128)S(1)} %copy-done.3, ...), custom_call_target="tpu_custom_call" | custom-call | flops 1610612736 | bytes 7340032 | tf_op jit(solution)/shard_map/slot_gradients/pallas_call | solution.py:150
  35.3 1.1 %collective-permute-start.20 = (bf16[2,3,64,256]{3,2,1,0:T(8,128)(2,1)S(1)}, bf16[2,3,64,256]{3,2,1,0:T(8,128)(2,1)S(1)}, u32[]{:S(2)}, u32[]{:S(2)}) collective-permute-start(bf16[2,3,64,256]{3,2,1,0:T(8,128)(2,1)S(1)} %get-tuple-element.60), channel_id=1, source_target_pairs={{0,4},{1,5},{2,6},{3,7},{4,0},{5,1},{6,2},{7,3},{8,12},{9,13},{10,... | collective-permute-start | bytes 589832 | tf_op jit(solution)/shard_map/ppermute | solution.py:24
  36.4 2.0 %collective-permute-start.22 = (bf16[2,3,64,256]{3,2,1,0:T(8,128)(2,1)S(1)}, bf16[2,3,64,256]{3,2,1,0:T(8,128)(2,1)S(1)}, u32[]{:S(2)}, u32[]{:S(2)}) collective-permute-start(bf16[2,3,64,256]{3,2,1,0:T(8,128)(2,1)S(1)} %get-tuple-element.63), channel_id=1, source_target_pairs={{0,2},{1,3},{2,0},{3,1},{4,6},{5,7},{6,4},{7,5},{8,10},{9,11},{10,... | collective-permute-start | bytes 589832 | tf_op jit(solution)/shard_map/ppermute | solution.py:24
  38.4 3.6 %collective-permute-done.20 = bf16[2,3,64,256]{3,2,1,0:T(8,128)(2,1)S(1)} collective-permute-done((bf16[2,3,64,256]{3,2,1,0:T(8,128)(2,1)S(1)}, bf16[2,3,64,256]{3,2,1,0:T(8,128)(2,1)S(1)}, u32[]{:S(2)}, u32[]{:S(2)}) %collective-permute-start.20) | collective-permute-done | bytes 196640 | tf_op jit(solution)/shard_map/ppermute | solution.py:24
  42.0 1.5 %collective-permute-start.21 = (bf16[3,64,256]{2,1,0:T(8,128)(2,1)S(1)}, bf16[3,64,256]{2,1,0:T(8,128)(2,1)S(1)}, u32[]{:S(2)}, u32[]{:S(2)}) collective-permute-start(bf16[3,64,256]{2,1,0:T(8,128)(2,1)S(1)} %fusion.13), channel_id=1, source_target_pairs={{0,2},{1,3},{2,0},{3,1},{4,6},{5,7},{6,4},{7,5},{8,10},{9,11},{10,... | collective-permute-start | bytes 294920 | tf_op jit(solution)/shard_map/ppermute | solution.py:24
  43.5 2.5 %collective-permute-start.23 = (bf16[3,64,256]{2,1,0:T(8,128)(2,1)S(1)}, bf16[3,64,256]{2,1,0:T(8,128)(2,1)S(1)}, u32[]{:S(2)}, u32[]{:S(2)}) collective-permute-start(bf16[3,64,256]{2,1,0:T(8,128)(2,1)S(1)} %fusion.10), channel_id=1, source_target_pairs={{0,4},{1,5},{2,6},{3,7},{4,0},{5,1},{6,2},{7,3},{8,12},{9,13},{10,... | collective-permute-start | bytes 294920 | tf_op jit(solution)/shard_map/ppermute | solution.py:24
  46.2 2.5 %collective-permute-done.23 = bf16[3,64,256]{2,1,0:T(8,128)(2,1)S(1)} collective-permute-done((bf16[3,64,256]{2,1,0:T(8,128)(2,1)S(1)}, bf16[3,64,256]{2,1,0:T(8,128)(2,1)S(1)}, u32[]{:S(2)}, u32[]{:S(2)}) %collective-permute-start.23) | collective-permute-done | bytes 98336 | tf_op jit(solution)/shard_map/ppermute | solution.py:24
  48.7 0.8 collective-permute-start.24
  49.6 1.9 %collective-permute-start.29 = (bf16[3,64,256]{2,1,0:T(8,128)(2,1)S(1)}, bf16[3,64,256]{2,1,0:T(8,128)(2,1)S(1)}, u32[]{:S(2)}, u32[]{:S(2)}) collective-permute-start(bf16[3,64,256]{2,1,0:T(8,128)(2,1)S(1)} %fusion.4), channel_id=1, source_target_pairs={{0,4},{1,5},{2,6},{3,7},{4,0},{5,1},{6,2},{7,3},{8,12},{9,13},{10,... | collective-permute-start | bytes 294920 | tf_op jit(solution)/shard_map/ppermute | solution.py:24
  51.4 0.3 collective-permute-done.26
  51.8 2.6 %collective-permute-done.24 = bf16[3,64,256]{2,1,0:T(8,128)(2,1)S(1)} collective-permute-done((bf16[3,64,256]{2,1,0:T(8,128)(2,1)S(1)}, bf16[3,64,256]{2,1,0:T(8,128)(2,1)S(1)}, u32[]{:S(2)}, u32[]{:S(2)}) %collective-permute-start.24) | collective-permute-done | bytes 98336 | tf_op jit(solution)/shard_map/ppermute | solution.py:24
  54.5 2.4 %collective-permute-start.25 = (bf16[3,64,256]{2,1,0:T(8,128)(2,1)S(1)}, bf16[3,64,256]{2,1,0:T(8,128)(2,1)S(1)}, u32[]{:S(2)}, u32[]{:S(2)}) collective-permute-start(bf16[3,64,256]{2,1,0:T(8,128)(2,1)S(1)} %fusion.16), channel_id=1, source_target_pairs={{0,16},{1,17},{2,18},{3,19},{4,20},{5,21},{6,22},{7,23},{8,24},{9,... | collective-permute-start | bytes 294920 | tf_op jit(solution)/shard_map/ppermute | solution.py:24
  57.1 1.1 %collective-permute-start.30 = (bf16[3,64,256]{2,1,0:T(8,128)(2,1)S(1)}, bf16[3,64,256]{2,1,0:T(8,128)(2,1)S(1)}, u32[]{:S(2)}, u32[]{:S(2)}) collective-permute-start(bf16[3,64,256]{2,1,0:T(8,128)(2,1)S(1)} %fusion.6), channel_id=1, source_target_pairs={{0,8},{1,9},{2,10},{3,11},{4,12},{5,13},{6,14},{7,15},{8,0},{9,1},... | collective-permute-start | bytes 294920 | tf_op jit(solution)/shard_map/ppermute | solution.py:24
  58.2 4.5 %collective-permute-done.25 = bf16[3,64,256]{2,1,0:T(8,128)(2,1)S(1)} collective-permute-done((bf16[3,64,256]{2,1,0:T(8,128)(2,1)S(1)}, bf16[3,64,256]{2,1,0:T(8,128)(2,1)S(1)}, u32[]{:S(2)}, u32[]{:S(2)}) %collective-permute-start.25) | collective-permute-done | bytes 98336 | tf_op jit(solution)/shard_map/ppermute | solution.py:24
  62.7 0.7 collective-permute-done.30
  63.8 1.0 %collective-permute-start.35 = (bf16[3,64,256]{2,1,0:T(8,128)(2,1)S(1)}, bf16[3,64,256]{2,1,0:T(8,128)(2,1)S(1)}, u32[]{:S(2)}, u32[]{:S(2)}) collective-permute-start(bf16[3,64,256]{2,1,0:T(8,128)(2,1)S(1)} %get-tuple-element.84.refs_0_), channel_id=1, source_target_pairs={{0,8},{1,9},{2,10},{3,11},{4,12},{5,13},{6,14},{7,15},{8,0},{9,1},... | collective-permute-start | bytes 294920 | tf_op jit(solution)/shard_map/ppermute | solution.py:24
  64.8 2.2 %collective-permute-start.33 = (bf16[3,64,256]{2,1,0:T(8,128)(2,1)S(1)}, bf16[3,64,256]{2,1,0:T(8,128)(2,1)S(1)}, u32[]{:S(2)}, u32[]{:S(2)}) collective-permute-start(bf16[3,64,256]{2,1,0:T(8,128)(2,1)S(1)} %get-tuple-element.84.refs_0_), channel_id=1, source_target_pairs={{0,4},{1,5},{2,6},{3,7},{4,0},{5,1},{6,2},{7,3},{8,12},{9,13},{10,... | collective-permute-start | bytes 294920 | tf_op jit(solution)/shard_map/ppermute | solution.py:24
  67.0 2.4 %collective-permute-done.38.refs_8_ = bf16[3,64,256]{2,1,0:T(8,128)(2,1)S(1)} collective-permute-done((bf16[3,64,256]{2,1,0:T(8,128)(2,1)S(1)}, bf16[3,64,256]{2,1,0:T(8,128)(2,1)S(1)}, u32[]{:S(2)}, u32[]{:S(2)}) %collective-permute-start.38) | collective-permute-done | bytes 98336 | tf_op jit(solution)/shard_map/ppermute | solution.py:24
  69.5 0.9 collective-permute-start.36
  70.7 1.1 %collective-permute-done.32.refs_1_ = bf16[3,64,256]{2,1,0:T(8,128)(2,1)S(1)} collective-permute-done((bf16[3,64,256]{2,1,0:T(8,128)(2,1)S(1)}, bf16[3,64,256]{2,1,0:T(8,128)(2,1)S(1)}, u32[]{:S(2)}, u32[]{:S(2)}) %collective-permute-start.32) | collective-permute-done | bytes 98336 | tf_op jit(solution)/shard_map/ppermute | solution.py:24
  71.8 0.6 collective-permute-start.37
  72.4 0.8 collective-permute-start.39
  73.2 0.8 collective-permute-done.42.refs_12_
  74.1 2.3 %collective-permute-start.45 = (bf16[3,64,256]{2,1,0:T(8,128)(2,1)S(1)}, bf16[3,64,256]{2,1,0:T(8,128)(2,1)S(1)}, u32[]{:S(2)}, u32[]{:S(2)}) collective-permute-start(bf16[3,64,256]{2,1,0:T(8,128)(2,1)S(1)} %collective-permute-done.42.refs_12_), channel_id=1, source_target_pairs={{0,4},{1,5},{2,6},{3,7},{4,0},{5,1},{6,2},{7,3},{8,12},{9,13},{10,... | collective-permute-start | bytes 294920 | tf_op jit(solution)/shard_map/ppermute | solution.py:24
  76.4 1.1 %collective-permute-start.43 = (bf16[3,64,256]{2,1,0:T(8,128)(2,1)S(1)}, bf16[3,64,256]{2,1,0:T(8,128)(2,1)S(1)}, u32[]{:S(2)}, u32[]{:S(2)}) collective-permute-start(bf16[3,64,256]{2,1,0:T(8,128)(2,1)S(1)} %collective-permute-done.42.refs_12_), channel_id=1, source_target_pairs={{0,2},{1,3},{2,0},{3,1},{4,6},{5,7},{6,4},{7,5},{8,10},{9,11},{10,... | collective-permute-start | bytes 294920 | tf_op jit(solution)/shard_map/ppermute | solution.py:24
  77.6 2.0 %collective-permute-start.41 = (bf16[3,64,256]{2,1,0:T(8,128)(2,1)S(1)}, bf16[3,64,256]{2,1,0:T(8,128)(2,1)S(1)}, u32[]{:S(2)}, u32[]{:S(2)}) collective-permute-start(bf16[3,64,256]{2,1,0:T(8,128)(2,1)S(1)} %collective-permute-done.38.refs_8_), channel_id=1, source_target_pairs={{0,4},{1,5},{2,6},{3,7},{4,0},{5,1},{6,2},{7,3},{8,12},{9,13},{10,... | collective-permute-start | bytes 294920 | tf_op jit(solution)/shard_map/ppermute | solution.py:24
  79.6 0.9 %collective-permute-start.40 = (bf16[3,64,256]{2,1,0:T(8,128)(2,1)S(1)}, bf16[3,64,256]{2,1,0:T(8,128)(2,1)S(1)}, u32[]{:S(2)}, u32[]{:S(2)}) collective-permute-start(bf16[3,64,256]{2,1,0:T(8,128)(2,1)S(1)} %collective-permute-done.37.refs_6_), channel_id=1, source_target_pairs={{0,2},{1,3},{2,0},{3,1},{4,6},{5,7},{6,4},{7,5},{8,10},{9,11},{10,... | collective-permute-start | bytes 294920 | tf_op jit(solution)/shard_map/ppermute | solution.py:24
  80.6 0.4 collective-permute-done.43.refs_13_
  81.0 1.1 %collective-permute-start.46 = (bf16[3,64,256]{2,1,0:T(8,128)(2,1)S(1)}, bf16[3,64,256]{2,1,0:T(8,128)(2,1)S(1)}, u32[]{:S(2)}, u32[]{:S(2)}) collective-permute-start(bf16[3,64,256]{2,1,0:T(8,128)(2,1)S(1)} %collective-permute-done.45.refs_14_), channel_id=1, source_target_pairs={{0,2},{1,3},{2,0},{3,1},{4,6},{5,7},{6,4},{7,5},{8,10},{9,11},{10,... | collective-permute-start | bytes 294920 | tf_op jit(solution)/shard_map/ppermute | solution.py:24
  82.3 1.0 %collective-permute-done.41.refs_10_ = bf16[3,64,256]{2,1,0:T(8,128)(2,1)S(1)} collective-permute-done((bf16[3,64,256]{2,1,0:T(8,128)(2,1)S(1)}, bf16[3,64,256]{2,1,0:T(8,128)(2,1)S(1)}, u32[]{:S(2)}, u32[]{:S(2)}) %collective-permute-start.41) | collective-permute-done | bytes 98336 | tf_op jit(solution)/shard_map/ppermute | solution.py:24
  83.3 1.0 %collective-permute-done.40.refs_7_ = bf16[3,64,256]{2,1,0:T(8,128)(2,1)S(1)} collective-permute-done((bf16[3,64,256]{2,1,0:T(8,128)(2,1)S(1)}, bf16[3,64,256]{2,1,0:T(8,128)(2,1)S(1)}, u32[]{:S(2)}, u32[]{:S(2)}) %collective-permute-start.40) | collective-permute-done | bytes 98336 | tf_op jit(solution)/shard_map/ppermute | solution.py:24
  84.3 1.4 %collective-permute-done.46.refs_15_ = bf16[3,64,256]{2,1,0:T(8,128)(2,1)S(1)} collective-permute-done((bf16[3,64,256]{2,1,0:T(8,128)(2,1)S(1)}, bf16[3,64,256]{2,1,0:T(8,128)(2,1)S(1)}, u32[]{:S(2)}, u32[]{:S(2)}) %collective-permute-start.46) | collective-permute-done | bytes 98336 | tf_op jit(solution)/shard_map/ppermute | solution.py:24
  85.6 1.9 %expert_outputs.1 = (bf16[256,1024]{1,0:T(8,128)(2,1)S(1)}, bf16[256,1024]{1,0:T(8,128)(2,1)S(1)}, s32[1]{0:T(128)}) custom-call(s32[32]{0:T(128)S(1)} %copy-done.4, bf16[3,64,256]{2,1,0:T(8,128)(2,1)S(1)} %get-tuple-element.84.refs_0_, bf16[3,64,256]{2,1,0:T(8,128)(2,1)S(1)} %collective-permute-done.32.refs_1_, ...), custom_call_target="tpu_custom_call" | custom-call | flops 805306368 | bytes 3670016 | tf_op jit(solution)/shard_map/expert_outputs/pallas_call | solution.py:176
  87.6 0.8 slice_bitcast_fusion
  89.1 0.4 collective-permute-done.47
  89.5 0.8 select_bitcast_fusion
  (66 shorter events, 2.9 us)
Async XLA Ops:
  0.6 2.8 %collective-permute-start.3 = (bf16[256,1024]{1,0:T(8,128)(2,1)}, bf16[256,1024]{1,0:T(8,128)(2,1)S(1)}, u32[]{:S(2)}, u32[]{:S(2)}) collective-permute-start(bf16[256,1024]{1,0:T(8,128)(2,1)} %bitcast.76), channel_id=1, source_target_pairs={{0,1},{1,0},{2,3},{3,2},{4,5},{5,4},{6,7},{7,6},{8,9},{9,8},{10,11... | collective-permute-start | bytes 1572872 | tf_op jit(solution)/shard_map/ppermute | solution.py:24
  1.1 2.5 %collective-permute-start.4 = (bf16[256,1024]{1,0:T(8,128)(2,1)}, bf16[256,1024]{1,0:T(8,128)(2,1)S(1)}, u32[]{:S(2)}, u32[]{:S(2)}) collective-permute-start(bf16[256,1024]{1,0:T(8,128)(2,1)} %bitcast.79), channel_id=1, source_target_pairs={{0,1},{1,0},{2,3},{3,2},{4,5},{5,4},{6,7},{7,6},{8,9},{9,8},{10,11... | collective-permute-start | bytes 1572872 | tf_op jit(solution)/shard_map/ppermute | solution.py:24
  1.2 3.5 %collective-permute-start.1 = (bf16[256,1024]{1,0:T(8,128)(2,1)}, bf16[256,1024]{1,0:T(8,128)(2,1)S(1)}, u32[]{:S(2)}, u32[]{:S(2)}) collective-permute-start(bf16[256,1024]{1,0:T(8,128)(2,1)} %bitcast.82), channel_id=1, source_target_pairs={{0,1},{1,0},{2,3},{3,2},{4,5},{5,4},{6,7},{7,6},{8,9},{9,8},{10,11... | collective-permute-start | bytes 1572872 | tf_op jit(solution)/shard_map/ppermute | solution.py:24
  1.7 1.1 %copy-start.5 = (f32[2,3,32,256]{3,2,1,0:T(8,128)S(1)}, f32[2,3,32,256]{3,2,1,0:T(8,128)}, u32[]{:S(2)}) copy-start(f32[2,3,32,256]{3,2,1,0:T(8,128)} %param.9) | copy-start | bytes 589828
  1.7 2.0 %copy-start.1 = (bf16[1,256,1024]{2,1,0:T(8,128)(2,1)S(1)}, bf16[1,256,1024]{2,1,0:T(8,128)(2,1)}, u32[]{:S(2)}) copy-start(bf16[1,256,1024]{2,1,0:T(8,128)(2,1)} %param.13) | copy-start | bytes 1572868
  2.8 1.1 %copy-start = (bf16[1,256,1024]{2,1,0:T(8,128)(2,1)S(1)}, bf16[1,256,1024]{2,1,0:T(8,128)(2,1)}, u32[]{:S(2)}) copy-start(bf16[1,256,1024]{2,1,0:T(8,128)(2,1)} %param.12) | copy-start | bytes 1572868
  2.9 1.9 %collective-permute-start = (f32[3,3,32,256]{3,2,1,0:T(8,128)S(1)}, f32[3,3,32,256]{3,2,1,0:T(8,128)S(1)}, u32[]{:S(2)}, u32[]{:S(2)}) collective-permute-start(f32[3,3,32,256]{3,2,1,0:T(8,128)S(1)} %pad_maximum_fusion.1), channel_id=1, source_target_pairs={{0,1},{1,0},{2,3},{3,2},{4,5},{5,4},{6,7},{7,6},{8,9},{9,8},{10,11... | collective-permute-start | bytes 884744 | tf_op jit(solution)/shard_map/ppermute | solution.py:24
  3.0 1.7 %collective-permute-start.2 = (s32[1]{0:T(128)}, s32[1]{0:T(128)}, u32[]{:S(2)}, u32[]{:S(2)}) collective-permute-start(s32[1]{0:T(128)} %param.17), channel_id=1, source_target_pairs={{0,1},{1,0},{2,3},{3,2},{4,5},{5,4},{6,7},{7,6},{8,9},{9,8},{10,11... | collective-permute-start | bytes 20 | tf_op jit(solution)/shard_map/ppermute | solution.py:24
  4.8 27.2 %copy-start.3 = (s32[32]{0:T(128)S(1)}, s32[32]{0:T(128)}, u32[]{:S(2)}) copy-start(s32[32]{0:T(128)} %slots.2) | copy-start | bytes 388
  4.8 9.3 %collective-permute-start.11 = (bf16[3,64,256]{2,1,0:T(8,128)(2,1)S(1)}, bf16[3,64,256]{2,1,0:T(8,128)(2,1)S(1)}, u32[]{:S(2)}, u32[]{:S(2)}) collective-permute-start(bf16[3,64,256]{2,1,0:T(8,128)(2,1)S(1)} %fusion.17.refs_0_), channel_id=1, source_target_pairs={{0,16},{1,17},{2,18},{3,19},{4,20},{5,21},{6,22},{7,23},{8,24},{9,... | collective-permute-start | bytes 294920 | tf_op jit(solution)/shard_map/ppermute | solution.py:24
  8.8 6.0 %collective-permute-start.8 = (bf16[3,64,256]{2,1,0:T(8,128)(2,1)S(1)}, bf16[3,64,256]{2,1,0:T(8,128)(2,1)S(1)}, u32[]{:S(2)}, u32[]{:S(2)}) collective-permute-start(bf16[3,64,256]{2,1,0:T(8,128)(2,1)S(1)} %fusion.17.refs_0_), channel_id=1, source_target_pairs={{0,8},{1,9},{2,10},{3,11},{4,12},{5,13},{6,14},{7,15},{8,0},{9,1},... | collective-permute-start | bytes 294920 | tf_op jit(solution)/shard_map/ppermute | solution.py:24
  10.3 5.9 %collective-permute-start.5 = (bf16[3,64,256]{2,1,0:T(8,128)(2,1)S(1)}, bf16[3,64,256]{2,1,0:T(8,128)(2,1)S(1)}, u32[]{:S(2)}, u32[]{:S(2)}) collective-permute-start(bf16[3,64,256]{2,1,0:T(8,128)(2,1)S(1)} %fusion.17.refs_0_), channel_id=1, source_target_pairs={{0,2},{1,3},{2,0},{3,1},{4,6},{5,7},{6,4},{7,5},{8,10},{9,11},{10,... | collective-permute-start | bytes 294920 | tf_op jit(solution)/shard_map/ppermute | solution.py:24
  11.8 6.0 %collective-permute-start.6 = (bf16[3,64,256]{2,1,0:T(8,128)(2,1)S(1)}, bf16[3,64,256]{2,1,0:T(8,128)(2,1)S(1)}, u32[]{:S(2)}, u32[]{:S(2)}) collective-permute-start(bf16[3,64,256]{2,1,0:T(8,128)(2,1)S(1)} %fusion.17.refs_0_), channel_id=1, source_target_pairs={{0,4},{1,5},{2,6},{3,7},{4,0},{5,1},{6,2},{7,3},{8,12},{9,13},{10,... | collective-permute-start | bytes 294920 | tf_op jit(solution)/shard_map/ppermute | solution.py:24
  14.1 4.6 %collective-permute-start.15 = (bf16[3,64,256]{2,1,0:T(8,128)(2,1)S(1)}, bf16[3,64,256]{2,1,0:T(8,128)(2,1)S(1)}, u32[]{:S(2)}, u32[]{:S(2)}) collective-permute-start(bf16[3,64,256]{2,1,0:T(8,128)(2,1)S(1)} %collective-permute-done.11.refs_8_), channel_id=1, source_target_pairs={{0,8},{1,9},{2,10},{3,11},{4,12},{5,13},{6,14},{7,15},{8,0},{9,1},... | collective-permute-start | bytes 294920 | tf_op jit(solution)/shard_map/ppermute | solution.py:24
  14.8 4.6 %collective-permute-start.9 = (bf16[3,64,256]{2,1,0:T(8,128)(2,1)S(1)}, bf16[3,64,256]{2,1,0:T(8,128)(2,1)S(1)}, u32[]{:S(2)}, u32[]{:S(2)}) collective-permute-start(bf16[3,64,256]{2,1,0:T(8,128)(2,1)S(1)} %collective-permute-done.8.refs_4_), channel_id=1, source_target_pairs={{0,2},{1,3},{2,0},{3,1},{4,6},{5,7},{6,4},{7,5},{8,10},{9,11},{10,... | collective-permute-start | bytes 294920 | tf_op jit(solution)/shard_map/ppermute | solution.py:24
  16.3 7.4 %collective-permute-start.10 = (bf16[3,64,256]{2,1,0:T(8,128)(2,1)S(1)}, bf16[3,64,256]{2,1,0:T(8,128)(2,1)S(1)}, u32[]{:S(2)}, u32[]{:S(2)}) collective-permute-start(bf16[3,64,256]{2,1,0:T(8,128)(2,1)S(1)} %collective-permute-done.8.refs_4_), channel_id=1, source_target_pairs={{0,4},{1,5},{2,6},{3,7},{4,0},{5,1},{6,2},{7,3},{8,12},{9,13},{10,... | collective-permute-start | bytes 294920 | tf_op jit(solution)/shard_map/ppermute | solution.py:24
  17.8 7.5 %collective-permute-start.12 = (bf16[3,64,256]{2,1,0:T(8,128)(2,1)S(1)}, bf16[3,64,256]{2,1,0:T(8,128)(2,1)S(1)}, u32[]{:S(2)}, u32[]{:S(2)}) collective-permute-start(bf16[3,64,256]{2,1,0:T(8,128)(2,1)S(1)} %collective-permute-done.11.refs_8_), channel_id=1, source_target_pairs={{0,2},{1,3},{2,0},{3,1},{4,6},{5,7},{6,4},{7,5},{8,10},{9,11},{10,... | collective-permute-start | bytes 294920 | tf_op jit(solution)/shard_map/ppermute | solution.py:24
  19.4 6.4 %collective-permute-start.16 = (bf16[3,64,256]{2,1,0:T(8,128)(2,1)S(1)}, bf16[3,64,256]{2,1,0:T(8,128)(2,1)S(1)}, u32[]{:S(2)}, u32[]{:S(2)}) collective-permute-start(bf16[3,64,256]{2,1,0:T(8,128)(2,1)S(1)} %collective-permute-done.15.refs_12_), channel_id=1, source_target_pairs={{0,2},{1,3},{2,0},{3,1},{4,6},{5,7},{6,4},{7,5},{8,10},{9,11},{10,... | collective-permute-start | bytes 294920 | tf_op jit(solution)/shard_map/ppermute | solution.py:24
  21.6 5.0 %collective-permute-start.18 = (bf16[3,64,256]{2,1,0:T(8,128)(2,1)S(1)}, bf16[3,64,256]{2,1,0:T(8,128)(2,1)S(1)}, u32[]{:S(2)}, u32[]{:S(2)}) collective-permute-start(bf16[3,64,256]{2,1,0:T(8,128)(2,1)S(1)} %collective-permute-done.15.refs_12_), channel_id=1, source_target_pairs={{0,4},{1,5},{2,6},{3,7},{4,0},{5,1},{6,2},{7,3},{8,12},{9,13},{10,... | collective-permute-start | bytes 294920 | tf_op jit(solution)/shard_map/ppermute | solution.py:24
  23.3 5.8 %collective-permute-start.7 = (bf16[3,64,256]{2,1,0:T(8,128)(2,1)S(1)}, bf16[3,64,256]{2,1,0:T(8,128)(2,1)S(1)}, u32[]{:S(2)}, u32[]{:S(2)}) collective-permute-start(bf16[3,64,256]{2,1,0:T(8,128)(2,1)S(1)} %collective-permute-done.5.refs_1_), channel_id=1, source_target_pairs={{0,4},{1,5},{2,6},{3,7},{4,0},{5,1},{6,2},{7,3},{8,12},{9,13},{10,... | collective-permute-start | bytes 294920 | tf_op jit(solution)/shard_map/ppermute | solution.py:24
  23.7 6.0 %collective-permute-start.14 = (bf16[3,64,256]{2,1,0:T(8,128)(2,1)S(1)}, bf16[3,64,256]{2,1,0:T(8,128)(2,1)S(1)}, u32[]{:S(2)}, u32[]{:S(2)}) collective-permute-start(bf16[3,64,256]{2,1,0:T(8,128)(2,1)S(1)} %collective-permute-done.11.refs_8_), channel_id=1, source_target_pairs={{0,4},{1,5},{2,6},{3,7},{4,0},{5,1},{6,2},{7,3},{8,12},{9,13},{10,... | collective-permute-start | bytes 294920 | tf_op jit(solution)/shard_map/ppermute | solution.py:24
  25.3 4.6 %collective-permute-start.13 = (bf16[3,64,256]{2,1,0:T(8,128)(2,1)S(1)}, bf16[3,64,256]{2,1,0:T(8,128)(2,1)S(1)}, u32[]{:S(2)}, u32[]{:S(2)}) collective-permute-start(bf16[3,64,256]{2,1,0:T(8,128)(2,1)S(1)} %collective-permute-done.10.refs_6_), channel_id=1, source_target_pairs={{0,2},{1,3},{2,0},{3,1},{4,6},{5,7},{6,4},{7,5},{8,10},{9,11},{10,... | collective-permute-start | bytes 294920 | tf_op jit(solution)/shard_map/ppermute | solution.py:24
  26.6 4.6 %collective-permute-start.19 = (bf16[3,64,256]{2,1,0:T(8,128)(2,1)S(1)}, bf16[3,64,256]{2,1,0:T(8,128)(2,1)S(1)}, u32[]{:S(2)}, u32[]{:S(2)}) collective-permute-start(bf16[3,64,256]{2,1,0:T(8,128)(2,1)S(1)} %collective-permute-done.18.refs_14_), channel_id=1, source_target_pairs={{0,2},{1,3},{2,0},{3,1},{4,6},{5,7},{6,4},{7,5},{8,10},{9,11},{10,... | collective-permute-start | bytes 294920 | tf_op jit(solution)/shard_map/ppermute | solution.py:24
  27.3 4.6 %collective-permute-start.17 = (bf16[3,64,256]{2,1,0:T(8,128)(2,1)S(1)}, bf16[3,64,256]{2,1,0:T(8,128)(2,1)S(1)}, u32[]{:S(2)}, u32[]{:S(2)}) collective-permute-start(bf16[3,64,256]{2,1,0:T(8,128)(2,1)S(1)} %collective-permute-done.12.refs_9_), channel_id=1, source_target_pairs={{0,4},{1,5},{2,6},{3,7},{4,0},{5,1},{6,2},{7,3},{8,12},{9,13},{10,... | collective-permute-start | bytes 294920 | tf_op jit(solution)/shard_map/ppermute | solution.py:24
  35.3 6.7 %collective-permute-start.20 = (bf16[2,3,64,256]{3,2,1,0:T(8,128)(2,1)S(1)}, bf16[2,3,64,256]{3,2,1,0:T(8,128)(2,1)S(1)}, u32[]{:S(2)}, u32[]{:S(2)}) collective-permute-start(bf16[2,3,64,256]{3,2,1,0:T(8,128)(2,1)S(1)} %get-tuple-element.60), channel_id=1, source_target_pairs={{0,4},{1,5},{2,6},{3,7},{4,0},{5,1},{6,2},{7,3},{8,12},{9,13},{10,... | collective-permute-start | bytes 589832 | tf_op jit(solution)/shard_map/ppermute | solution.py:24
  36.4 7.1 %collective-permute-start.22 = (bf16[2,3,64,256]{3,2,1,0:T(8,128)(2,1)S(1)}, bf16[2,3,64,256]{3,2,1,0:T(8,128)(2,1)S(1)}, u32[]{:S(2)}, u32[]{:S(2)}) collective-permute-start(bf16[2,3,64,256]{3,2,1,0:T(8,128)(2,1)S(1)} %get-tuple-element.63), channel_id=1, source_target_pairs={{0,2},{1,3},{2,0},{3,1},{4,6},{5,7},{6,4},{7,5},{8,10},{9,11},{10,... | collective-permute-start | bytes 589832 | tf_op jit(solution)/shard_map/ppermute | solution.py:24
  38.3 7.8 %collective-permute-start.28 = (bf16[2,3,64,256]{3,2,1,0:T(8,128)(2,1)S(1)}, bf16[2,3,64,256]{3,2,1,0:T(8,128)(2,1)S(1)}, u32[]{:S(2)}, u32[]{:S(2)}) collective-permute-start(bf16[2,3,64,256]{3,2,1,0:T(8,128)(2,1)S(1)} %get-tuple-element.70), channel_id=1, source_target_pairs={{0,2},{1,3},{2,0},{3,1},{4,6},{5,7},{6,4},{7,5},{8,10},{9,11},{10,... | collective-permute-start | bytes 589832 | tf_op jit(solution)/shard_map/ppermute | solution.py:24
  42.0 9.8 %collective-permute-start.21 = (bf16[3,64,256]{2,1,0:T(8,128)(2,1)S(1)}, bf16[3,64,256]{2,1,0:T(8,128)(2,1)S(1)}, u32[]{:S(2)}, u32[]{:S(2)}) collective-permute-start(bf16[3,64,256]{2,1,0:T(8,128)(2,1)S(1)} %fusion.13), channel_id=1, source_target_pairs={{0,2},{1,3},{2,0},{3,1},{4,6},{5,7},{6,4},{7,5},{8,10},{9,11},{10,... | collective-permute-start | bytes 294920 | tf_op jit(solution)/shard_map/ppermute | solution.py:24
  43.5 5.1 %collective-permute-start.23 = (bf16[3,64,256]{2,1,0:T(8,128)(2,1)S(1)}, bf16[3,64,256]{2,1,0:T(8,128)(2,1)S(1)}, u32[]{:S(2)}, u32[]{:S(2)}) collective-permute-start(bf16[3,64,256]{2,1,0:T(8,128)(2,1)S(1)} %fusion.10), channel_id=1, source_target_pairs={{0,4},{1,5},{2,6},{3,7},{4,0},{5,1},{6,2},{7,3},{8,12},{9,13},{10,... | collective-permute-start | bytes 294920 | tf_op jit(solution)/shard_map/ppermute | solution.py:24
  46.1 5.7 %collective-permute-start.26 = (bf16[2,3,64,256]{3,2,1,0:T(8,128)(2,1)S(1)}, bf16[2,3,64,256]{3,2,1,0:T(8,128)(2,1)S(1)}, u32[]{:S(2)}, u32[]{:S(2)}) collective-permute-start(bf16[2,3,64,256]{3,2,1,0:T(8,128)(2,1)S(1)} %get-tuple-element.66), channel_id=1, source_target_pairs={{0,4},{1,5},{2,6},{3,7},{4,0},{5,1},{6,2},{7,3},{8,12},{9,13},{10,... | collective-permute-start | bytes 589832 | tf_op jit(solution)/shard_map/ppermute | solution.py:24
  48.7 5.7 %collective-permute-start.24 = (bf16[3,64,256]{2,1,0:T(8,128)(2,1)S(1)}, bf16[3,64,256]{2,1,0:T(8,128)(2,1)S(1)}, u32[]{:S(2)}, u32[]{:S(2)}) collective-permute-start(bf16[3,64,256]{2,1,0:T(8,128)(2,1)S(1)} %fusion.12), channel_id=1, source_target_pairs={{0,8},{1,9},{2,10},{3,11},{4,12},{5,13},{6,14},{7,15},{8,0},{9,1},... | collective-permute-start | bytes 294920 | tf_op jit(solution)/shard_map/ppermute | solution.py:24
  49.6 7.5 %collective-permute-start.29 = (bf16[3,64,256]{2,1,0:T(8,128)(2,1)S(1)}, bf16[3,64,256]{2,1,0:T(8,128)(2,1)S(1)}, u32[]{:S(2)}, u32[]{:S(2)}) collective-permute-start(bf16[3,64,256]{2,1,0:T(8,128)(2,1)S(1)} %fusion.4), channel_id=1, source_target_pairs={{0,4},{1,5},{2,6},{3,7},{4,0},{5,1},{6,2},{7,3},{8,12},{9,13},{10,... | collective-permute-start | bytes 294920 | tf_op jit(solution)/shard_map/ppermute | solution.py:24
  54.5 8.2 %collective-permute-start.25 = (bf16[3,64,256]{2,1,0:T(8,128)(2,1)S(1)}, bf16[3,64,256]{2,1,0:T(8,128)(2,1)S(1)}, u32[]{:S(2)}, u32[]{:S(2)}) collective-permute-start(bf16[3,64,256]{2,1,0:T(8,128)(2,1)S(1)} %fusion.16), channel_id=1, source_target_pairs={{0,16},{1,17},{2,18},{3,19},{4,20},{5,21},{6,22},{7,23},{8,24},{9,... | collective-permute-start | bytes 294920 | tf_op jit(solution)/shard_map/ppermute | solution.py:24
  56.9 5.8 %collective-permute-start.27 = (bf16[3,64,256]{2,1,0:T(8,128)(2,1)S(1)}, bf16[3,64,256]{2,1,0:T(8,128)(2,1)S(1)}, u32[]{:S(2)}, u32[]{:S(2)}) collective-permute-start(bf16[3,64,256]{2,1,0:T(8,128)(2,1)S(1)} %fusion.7), channel_id=1, source_target_pairs={{0,2},{1,3},{2,0},{3,1},{4,6},{5,7},{6,4},{7,5},{8,10},{9,11},{10,... | collective-permute-start | bytes 294920 | tf_op jit(solution)/shard_map/ppermute | solution.py:24
  57.1 6.3 %collective-permute-start.30 = (bf16[3,64,256]{2,1,0:T(8,128)(2,1)S(1)}, bf16[3,64,256]{2,1,0:T(8,128)(2,1)S(1)}, u32[]{:S(2)}, u32[]{:S(2)}) collective-permute-start(bf16[3,64,256]{2,1,0:T(8,128)(2,1)S(1)} %fusion.6), channel_id=1, source_target_pairs={{0,8},{1,9},{2,10},{3,11},{4,12},{5,13},{6,14},{7,15},{8,0},{9,1},... | collective-permute-start | bytes 294920 | tf_op jit(solution)/shard_map/ppermute | solution.py:24
  63.7 5.7 %collective-permute-start.38 = (bf16[3,64,256]{2,1,0:T(8,128)(2,1)S(1)}, bf16[3,64,256]{2,1,0:T(8,128)(2,1)S(1)}, u32[]{:S(2)}, u32[]{:S(2)}) collective-permute-start(bf16[3,64,256]{2,1,0:T(8,128)(2,1)S(1)} %get-tuple-element.84.refs_0_), channel_id=1, source_target_pairs={{0,16},{1,17},{2,18},{3,19},{4,20},{5,21},{6,22},{7,23},{8,24},{9,... | collective-permute-start | bytes 294920 | tf_op jit(solution)/shard_map/ppermute | solution.py:24
  63.8 5.7 %collective-permute-start.35 = (bf16[3,64,256]{2,1,0:T(8,128)(2,1)S(1)}, bf16[3,64,256]{2,1,0:T(8,128)(2,1)S(1)}, u32[]{:S(2)}, u32[]{:S(2)}) collective-permute-start(bf16[3,64,256]{2,1,0:T(8,128)(2,1)S(1)} %get-tuple-element.84.refs_0_), channel_id=1, source_target_pairs={{0,8},{1,9},{2,10},{3,11},{4,12},{5,13},{6,14},{7,15},{8,0},{9,1},... | collective-permute-start | bytes 294920 | tf_op jit(solution)/shard_map/ppermute | solution.py:24
  64.8 5.8 %collective-permute-start.33 = (bf16[3,64,256]{2,1,0:T(8,128)(2,1)S(1)}, bf16[3,64,256]{2,1,0:T(8,128)(2,1)S(1)}, u32[]{:S(2)}, u32[]{:S(2)}) collective-permute-start(bf16[3,64,256]{2,1,0:T(8,128)(2,1)S(1)} %get-tuple-element.84.refs_0_), channel_id=1, source_target_pairs={{0,4},{1,5},{2,6},{3,7},{4,0},{5,1},{6,2},{7,3},{8,12},{9,13},{10,... | collective-permute-start | bytes 294920 | tf_op jit(solution)/shard_map/ppermute | solution.py:24
  67.0 4.7 %collective-permute-start.32 = (bf16[3,64,256]{2,1,0:T(8,128)(2,1)S(1)}, bf16[3,64,256]{2,1,0:T(8,128)(2,1)S(1)}, u32[]{:S(2)}, u32[]{:S(2)}) collective-permute-start(bf16[3,64,256]{2,1,0:T(8,128)(2,1)S(1)} %get-tuple-element.84.refs_0_), channel_id=1, source_target_pairs={{0,2},{1,3},{2,0},{3,1},{4,6},{5,7},{6,4},{7,5},{8,10},{9,11},{10,... | collective-permute-start | bytes 294920 | tf_op jit(solution)/shard_map/ppermute | solution.py:24
  69.4 4.6 %collective-permute-start.42 = (bf16[3,64,256]{2,1,0:T(8,128)(2,1)S(1)}, bf16[3,64,256]{2,1,0:T(8,128)(2,1)S(1)}, u32[]{:S(2)}, u32[]{:S(2)}) collective-permute-start(bf16[3,64,256]{2,1,0:T(8,128)(2,1)S(1)} %collective-permute-done.38.refs_8_), channel_id=1, source_target_pairs={{0,8},{1,9},{2,10},{3,11},{4,12},{5,13},{6,14},{7,15},{8,0},{9,1},... | collective-permute-start | bytes 294920 | tf_op jit(solution)/shard_map/ppermute | solution.py:24
  69.5 4.6 %collective-permute-start.36 = (bf16[3,64,256]{2,1,0:T(8,128)(2,1)S(1)}, bf16[3,64,256]{2,1,0:T(8,128)(2,1)S(1)}, u32[]{:S(2)}, u32[]{:S(2)}) collective-permute-start(bf16[3,64,256]{2,1,0:T(8,128)(2,1)S(1)} %collective-permute-done.35.refs_4_), channel_id=1, source_target_pairs={{0,2},{1,3},{2,0},{3,1},{4,6},{5,7},{6,4},{7,5},{8,10},{9,11},{10,... | collective-permute-start | bytes 294920 | tf_op jit(solution)/shard_map/ppermute | solution.py:24
  71.8 5.9 %collective-permute-start.37 = (bf16[3,64,256]{2,1,0:T(8,128)(2,1)S(1)}, bf16[3,64,256]{2,1,0:T(8,128)(2,1)S(1)}, u32[]{:S(2)}, u32[]{:S(2)}) collective-permute-start(bf16[3,64,256]{2,1,0:T(8,128)(2,1)S(1)} %collective-permute-done.35.refs_4_), channel_id=1, source_target_pairs={{0,4},{1,5},{2,6},{3,7},{4,0},{5,1},{6,2},{7,3},{8,12},{9,13},{10,... | collective-permute-start | bytes 294920 | tf_op jit(solution)/shard_map/ppermute | solution.py:24
  72.4 7.2 %collective-permute-start.39 = (bf16[3,64,256]{2,1,0:T(8,128)(2,1)S(1)}, bf16[3,64,256]{2,1,0:T(8,128)(2,1)S(1)}, u32[]{:S(2)}, u32[]{:S(2)}) collective-permute-start(bf16[3,64,256]{2,1,0:T(8,128)(2,1)S(1)} %collective-permute-done.38.refs_8_), channel_id=1, source_target_pairs={{0,2},{1,3},{2,0},{3,1},{4,6},{5,7},{6,4},{7,5},{8,10},{9,11},{10,... | collective-permute-start | bytes 294920 | tf_op jit(solution)/shard_map/ppermute | solution.py:24
  74.1 6.9 %collective-permute-start.45 = (bf16[3,64,256]{2,1,0:T(8,128)(2,1)S(1)}, bf16[3,64,256]{2,1,0:T(8,128)(2,1)S(1)}, u32[]{:S(2)}, u32[]{:S(2)}) collective-permute-start(bf16[3,64,256]{2,1,0:T(8,128)(2,1)S(1)} %collective-permute-done.42.refs_12_), channel_id=1, source_target_pairs={{0,4},{1,5},{2,6},{3,7},{4,0},{5,1},{6,2},{7,3},{8,12},{9,13},{10,... | collective-permute-start | bytes 294920 | tf_op jit(solution)/shard_map/ppermute | solution.py:24
  76.4 4.6 %collective-permute-start.43 = (bf16[3,64,256]{2,1,0:T(8,128)(2,1)S(1)}, bf16[3,64,256]{2,1,0:T(8,128)(2,1)S(1)}, u32[]{:S(2)}, u32[]{:S(2)}) collective-permute-start(bf16[3,64,256]{2,1,0:T(8,128)(2,1)S(1)} %collective-permute-done.42.refs_12_), channel_id=1, source_target_pairs={{0,2},{1,3},{2,0},{3,1},{4,6},{5,7},{6,4},{7,5},{8,10},{9,11},{10,... | collective-permute-start | bytes 294920 | tf_op jit(solution)/shard_map/ppermute | solution.py:24
  77.5 8.1 %copy-start.2 = (bf16[1,256,1024]{2,1,0:T(8,128)(2,1)S(1)}, bf16[1,256,1024]{2,1,0:T(8,128)(2,1)}, u32[]{:S(2)}) copy-start(bf16[1,256,1024]{2,1,0:T(8,128)(2,1)} %param.14) | copy-start | bytes 1572868
  77.5 4.7 %collective-permute-start.34 = (bf16[3,64,256]{2,1,0:T(8,128)(2,1)S(1)}, bf16[3,64,256]{2,1,0:T(8,128)(2,1)S(1)}, u32[]{:S(2)}, u32[]{:S(2)}) collective-permute-start(bf16[3,64,256]{2,1,0:T(8,128)(2,1)S(1)} %collective-permute-done.32.refs_1_), channel_id=1, source_target_pairs={{0,4},{1,5},{2,6},{3,7},{4,0},{5,1},{6,2},{7,3},{8,12},{9,13},{10,... | collective-permute-start | bytes 294920 | tf_op jit(solution)/shard_map/ppermute | solution.py:24
  77.6 5.6 %collective-permute-start.41 = (bf16[3,64,256]{2,1,0:T(8,128)(2,1)S(1)}, bf16[3,64,256]{2,1,0:T(8,128)(2,1)S(1)}, u32[]{:S(2)}, u32[]{:S(2)}) collective-permute-start(bf16[3,64,256]{2,1,0:T(8,128)(2,1)S(1)} %collective-permute-done.38.refs_8_), channel_id=1, source_target_pairs={{0,4},{1,5},{2,6},{3,7},{4,0},{5,1},{6,2},{7,3},{8,12},{9,13},{10,... | collective-permute-start | bytes 294920 | tf_op jit(solution)/shard_map/ppermute | solution.py:24
  79.6 4.6 %collective-permute-start.40 = (bf16[3,64,256]{2,1,0:T(8,128)(2,1)S(1)}, bf16[3,64,256]{2,1,0:T(8,128)(2,1)S(1)}, u32[]{:S(2)}, u32[]{:S(2)}) collective-permute-start(bf16[3,64,256]{2,1,0:T(8,128)(2,1)S(1)} %collective-permute-done.37.refs_6_), channel_id=1, source_target_pairs={{0,2},{1,3},{2,0},{3,1},{4,6},{5,7},{6,4},{7,5},{8,10},{9,11},{10,... | collective-permute-start | bytes 294920 | tf_op jit(solution)/shard_map/ppermute | solution.py:24
  81.0 4.6 %collective-permute-start.44 = (bf16[3,64,256]{2,1,0:T(8,128)(2,1)S(1)}, bf16[3,64,256]{2,1,0:T(8,128)(2,1)S(1)}, u32[]{:S(2)}, u32[]{:S(2)}) collective-permute-start(bf16[3,64,256]{2,1,0:T(8,128)(2,1)S(1)} %collective-permute-done.39.refs_9_), channel_id=1, source_target_pairs={{0,4},{1,5},{2,6},{3,7},{4,0},{5,1},{6,2},{7,3},{8,12},{9,13},{10,... | collective-permute-start | bytes 294920 | tf_op jit(solution)/shard_map/ppermute | solution.py:24
  81.0 4.6 %collective-permute-start.46 = (bf16[3,64,256]{2,1,0:T(8,128)(2,1)S(1)}, bf16[3,64,256]{2,1,0:T(8,128)(2,1)S(1)}, u32[]{:S(2)}, u32[]{:S(2)}) collective-permute-start(bf16[3,64,256]{2,1,0:T(8,128)(2,1)S(1)} %collective-permute-done.45.refs_14_), channel_id=1, source_target_pairs={{0,2},{1,3},{2,0},{3,1},{4,6},{5,7},{6,4},{7,5},{8,10},{9,11},{10,... | collective-permute-start | bytes 294920 | tf_op jit(solution)/shard_map/ppermute | solution.py:24
  82.2 3.5 %copy-start.4 = (s32[32]{0:T(128)S(1)}, s32[32]{0:T(128)}, u32[]{:S(2)}) copy-start(s32[32]{0:T(128)} %slots.3) | copy-start | bytes 388
  82.2 5.3 %collective-permute-start.31 = (f32[3,3,32,256]{3,2,1,0:T(8,128)S(1)}, f32[3,3,32,256]{3,2,1,0:T(8,128)S(1)}, u32[]{:S(2)}, u32[]{:S(2)}) collective-permute-start(f32[3,3,32,256]{3,2,1,0:T(8,128)S(1)} %get-tuple-element.92), channel_id=1, source_target_pairs={{0,1},{1,0},{2,3},{3,2},{4,5},{5,4},{6,7},{7,6},{8,9},{9,8},{10,11... | collective-permute-start | bytes 884744 | tf_op jit(solution)/shard_map/ppermute | solution.py:24
  87.5 2.0 %collective-permute-start.47 = (bf16[256,1024]{1,0:T(8,128)(2,1)S(1)}, bf16[256,1024]{1,0:T(8,128)(2,1)S(1)}, u32[]{:S(2)}, u32[]{:S(2)}) collective-permute-start(bf16[256,1024]{1,0:T(8,128)(2,1)S(1)} %get-tuple-element.83), channel_id=1, source_target_pairs={{0,1},{1,0},{2,3},{3,2},{4,5},{5,4},{6,7},{7,6},{8,9},{9,8},{10,11... | collective-permute-start | bytes 1572872 | tf_op jit(solution)/shard_map/ppermute | solution.py:24

commit v7 on v6

--- a/solution.py
+++ b/solution.py
@@ -56,11 +56,9 @@
 
 def places(outs):
     found = []
-    for zj in range(len(outs) // 3):
-        own, later, pair = outs[3 * zj : 3 * zj + 3]
-        by_x, by_y = ((pair, (1,)), (later, ())) if zj % 2 else ((later, ()), (pair, (1,)))
-        found += [(own, ()), by_x, by_y, (pair, (0,))]
-    return found
+    for zj in range(2):
+        found += [(outs[zj], ())] + [(pair, (zj,)) for pair in outs[2:5]]
+    return found + [(out, ()) for out in outs[5:]]
 
 
 def gradient_rows(first_row, products, outs):
@@ -149,9 +147,9 @@
     two = jax.ShapeDtypeStruct((2, kinds, rows, units), jnp.bfloat16)
     return pl.pallas_call(
         functools.partial(backward_kernel, count),
-        out_shape=[one, one, two] * (count // 4),
+        out_shape=[one] * 2 + [two] * 3 + [one] * (count - 8),
         in_specs=[SMEM] * 3 + [VMEM] * (count + 6),
-        out_specs=[VMEM] * (3 * count // 4),
+        out_specs=[VMEM] * (count - 3),
         scratch_shapes=[
             pltpu.VMEM((2 * tokens, units), jnp.bfloat16),
             pltpu.VMEM((2 * tokens, units), jnp.bfloat16),
@@ -228,26 +226,27 @@
 
 def reduce_chips(pieces):
     depth = lax.axis_size("dev") // Z_UNIT
-    column = [[pieces[3 * zj]] for zj in range(depth)]
-    arrived, crossed, risen = (), (), ()
-    for upper in reversed(range(1, depth, 2)):
-        up_y, pair_x = pieces[3 * upper + 1 : 3 * upper + 3]
-        below_x, pair_y = pieces[3 * upper - 2 : 3 * upper]
-        got_x = hop(pair_x, X_STEP)
-        got_y = hop(after(pair_y, *arrived), Y_STEP)
-        up_y = add_all(up_y, got_x[0]).astype(jnp.bfloat16)
-        column[upper] += [got_x[1], hop(after(up_y, *crossed), Y_STEP)]
-        below_x = add_all(below_x, got_y[0]).astype(jnp.bfloat16)
-        column[upper - 1] += [got_y[1], hop(after(below_x, *risen), X_STEP)]
-        arrived, crossed, risen = (got_x,), (column[upper][-1],), ()
-        for zj in (upper, upper - 1):
-            top = 1 << zj.bit_length() - 1 if zj else 0
-            low = zj - top
-            if zj:
-                part = add_all(*column[zj]).astype(jnp.bfloat16)
-                column[top if low else 0].append(hop(part, (low or top) * Z_UNIT))
-                risen = risen or (column[top if low else 0][-1],)
-    return add_all(*column[0])
+    own_here, own_next, near_x, near_y, near_across = pieces[:5]
+    total, early, late = None, (), ()
+    for upper in reversed(range(3, depth, 2)):
+        own_up, up_x, up_y, up_across = pieces[4 * upper - 3 : 4 * upper + 1]
+        own_low, low_x, low_y, low_across = pieces[4 * upper - 7 : 4 * upper - 3]
+        from_x = hop(after(up_across, *late), X_STEP)
+        from_y = hop(after(low_across, *late), Y_STEP)
+        up_x = hop(after(up_x, *late), X_STEP)
+        up_y = hop(add_all(up_y, from_x).astype(jnp.bfloat16), Y_STEP)
+        low_x = hop(add_all(low_x, from_y).astype(jnp.bfloat16), X_STEP)
+        low_y = hop(after(low_y, from_x), Y_STEP)
+        up = hop(add_all(own_up, up_x, up_y).astype(jnp.bfloat16), upper * Z_UNIT)
+        low = hop(add_all(own_low, low_x, low_y).astype(jnp.bfloat16), (upper - 1) * Z_UNIT)
+        total = add_all(up, low) if total is None else add_all(total, up, low)
+        early, late = (from_y,), (up_y, up_x)
+    near_across = hop(after(near_across, *early), X_STEP | Y_STEP)
+    near_x = hop(after(near_x, *late), X_STEP)
+    near_y = hop(after(near_y, *late), Y_STEP)
+    column = add_all(own_next, near_x[1], near_y[1], near_across[1]).astype(jnp.bfloat16)
+    here = add_all(own_here, near_x[0], near_y[0], near_across[0], hop(column, Z_UNIT))
+    return here if total is None else here + total
 
 
 def block_a_core(master, first, second, old_rows, old_cotangent, new_rows, old_slots, new_slots, live):

time: 90.5 us -> 92.6 us (1.023)
  starting transfers between devices: 49.4 us -> 51 us
    ppermute x48 -> x49, starting transfers between devices: 49.4 us -> 51 us  [hop(): lax.ppermute(block, 'dev', [(low, low ^ mask) for low in range(count)])]
    ppermute x48 -> x49, waiting for transfers between devices: 29.2 us -> 29.9 us  [hop(): lax.ppermute(block, 'dev', [(low, low ^ mask) for low in range(count)])]
  transfers between devices with their start and end apart: 48 -> 49, of which waited for: 28 -> 24; matrix products, arithmetic and copies ran while one was open for 3% -> 3% of each run, Pallas kernels for 3% -> 3%
where the time goes in v7:
time: 92.6 us; the launch traced here: 92.5 us
  starting transfers between devices  51 us (55%)
  waiting for transfers between devices  29.9 us (32%)
  Pallas kernels  5.61 us (6%)
  local copies, waits for them, and re-layouts  2.31 us (2%)
  between operations  2.19 us (2%)
  other arithmetic  1.52 us (2%)
    ppermute x49, starting transfers between devices, hop(): lax.ppermute(block, 'dev', [(low, low ^ mask) for low in range(count)])  51 us
    ppermute x49, waiting for transfers between devices, hop(): lax.ppermute(block, 'dev', [(low, low ^ mask) for low in range(count)])  29.9 us
    pallas_call x1, Pallas kernels, backward(): pl.pallas_call(functools.partial(backward_kernel, count), out_shape=[one]...  3.17 us
    pallas_call x1, Pallas kernels, forward(): pl.pallas_call(functools.partial(forward_kernel, count), out_shape=[one,...  1.85 us
  transfers between devices with their start and end apart: 49, of which 24 were waited for; matrix products, arithmetic and copies ran while one was open for 3% of the time, Pallas kernels for 3%

profile of v7, /device:TPU:0, one launch (start us, length us, event | category | flops | bytes accessed | tf_op | source)
XLA Modules:
  0.0 92.5 jit_solution(1410833857535319870)
XLA Ops:
  0.6 0.5 collective-permute-start.3
  1.2 0.4 collective-permute-start.1
  1.7 1.1 %dynamic-slice_bitcast_fusion.2 = (f32[3,32,256]{2,1,0:T(8,128)S(1)}, f32[1,3,32,256]{3,2,1,0:T(8,128)S(1)}, f32[1,3,32,256]{3,2,1,0:T(8,128)S(1)}, f32[3,32,256]{2,1,0:T(8,128)S(1)}) fusion(f32[2,3,32,256]{3,2,1,0:T(8,128)} %param.10, s32[]{:T(128)S(6)} %select_n.51, s32[]{:T(128)S(6)} %select_n.52, f32[2,3,32,256]{3,2,1,0:T(8,128)} %param.9), kind=kLoop, calls=%fused_computation.40 | loop fusion | bytes 786440 | tf_op jit(solution)/shard_map/jit(dynamic_index_in_dim)/squeeze | solution.py:257
  3.0 0.4 collective-permute-start.2
  3.9 0.6 transpose_rows.1
  4.5 0.4 collective-permute-done.2.other_live
  4.9 4.0 %collective-permute-start.11 = (bf16[3,64,256]{2,1,0:T(8,128)(2,1)S(1)}, bf16[3,64,256]{2,1,0:T(8,128)(2,1)S(1)}, u32[]{:S(2)}, u32[]{:S(2)}) collective-permute-start(bf16[3,64,256]{2,1,0:T(8,128)(2,1)S(1)} %fusion.7.refs_0_), channel_id=1, source_target_pairs={{0,16},{1,17},{2,18},{3,19},{4,20},{5,21},{6,22},{7,23},{8,24},{9,... | collective-permute-start | bytes 294920 | tf_op jit(solution)/shard_map/ppermute | solution.py:24
  8.9 1.6 %collective-permute-start.8 = (bf16[3,64,256]{2,1,0:T(8,128)(2,1)S(1)}, bf16[3,64,256]{2,1,0:T(8,128)(2,1)S(1)}, u32[]{:S(2)}, u32[]{:S(2)}) collective-permute-start(bf16[3,64,256]{2,1,0:T(8,128)(2,1)S(1)} %fusion.7.refs_0_), channel_id=1, source_target_pairs={{0,8},{1,9},{2,10},{3,11},{4,12},{5,13},{6,14},{7,15},{8,0},{9,1},... | collective-permute-start | bytes 294920 | tf_op jit(solution)/shard_map/ppermute | solution.py:24
  10.5 1.5 %collective-permute-start.5 = (bf16[3,64,256]{2,1,0:T(8,128)(2,1)S(1)}, bf16[3,64,256]{2,1,0:T(8,128)(2,1)S(1)}, u32[]{:S(2)}, u32[]{:S(2)}) collective-permute-start(bf16[3,64,256]{2,1,0:T(8,128)(2,1)S(1)} %fusion.7.refs_0_), channel_id=1, source_target_pairs={{0,2},{1,3},{2,0},{3,1},{4,6},{5,7},{6,4},{7,5},{8,10},{9,11},{10,... | collective-permute-start | bytes 294920 | tf_op jit(solution)/shard_map/ppermute | solution.py:24
  12.0 1.5 %collective-permute-start.6 = (bf16[3,64,256]{2,1,0:T(8,128)(2,1)S(1)}, bf16[3,64,256]{2,1,0:T(8,128)(2,1)S(1)}, u32[]{:S(2)}, u32[]{:S(2)}) collective-permute-start(bf16[3,64,256]{2,1,0:T(8,128)(2,1)S(1)} %fusion.7.refs_0_), channel_id=1, source_target_pairs={{0,4},{1,5},{2,6},{3,7},{4,0},{5,1},{6,2},{7,3},{8,12},{9,13},{10,... | collective-permute-start | bytes 294920 | tf_op jit(solution)/shard_map/ppermute | solution.py:24
  13.5 0.8 collective-permute-done.11.refs_8_
  14.3 0.6 collective-permute-start.15
  14.9 1.5 %collective-permute-start.9 = (bf16[3,64,256]{2,1,0:T(8,128)(2,1)S(1)}, bf16[3,64,256]{2,1,0:T(8,128)(2,1)S(1)}, u32[]{:S(2)}, u32[]{:S(2)}) collective-permute-start(bf16[3,64,256]{2,1,0:T(8,128)(2,1)S(1)} %collective-permute-done.8.refs_4_), channel_id=1, source_target_pairs={{0,2},{1,3},{2,0},{3,1},{4,6},{5,7},{6,4},{7,5},{8,10},{9,11},{10,... | collective-permute-start | bytes 294920 | tf_op jit(solution)/shard_map/ppermute | solution.py:24
  16.4 1.5 %collective-permute-start.10 = (bf16[3,64,256]{2,1,0:T(8,128)(2,1)S(1)}, bf16[3,64,256]{2,1,0:T(8,128)(2,1)S(1)}, u32[]{:S(2)}, u32[]{:S(2)}) collective-permute-start(bf16[3,64,256]{2,1,0:T(8,128)(2,1)S(1)} %collective-permute-done.8.refs_4_), channel_id=1, source_target_pairs={{0,4},{1,5},{2,6},{3,7},{4,0},{5,1},{6,2},{7,3},{8,12},{9,13},{10,... | collective-permute-start | bytes 294920 | tf_op jit(solution)/shard_map/ppermute | solution.py:24
  17.9 0.5 collective-permute-start.12
  18.4 0.4 collective-permute-done.15.refs_12_
  18.9 0.6 collective-permute-done.9.refs_5_
  19.5 2.3 %collective-permute-start.16 = (bf16[3,64,256]{2,1,0:T(8,128)(2,1)S(1)}, bf16[3,64,256]{2,1,0:T(8,128)(2,1)S(1)}, u32[]{:S(2)}, u32[]{:S(2)}) collective-permute-start(bf16[3,64,256]{2,1,0:T(8,128)(2,1)S(1)} %collective-permute-done.15.refs_12_), channel_id=1, source_target_pairs={{0,2},{1,3},{2,0},{3,1},{4,6},{5,7},{6,4},{7,5},{8,10},{9,11},{10,... | collective-permute-start | bytes 294920 | tf_op jit(solution)/shard_map/ppermute | solution.py:24
  21.8 1.6 %collective-permute-start.18 = (bf16[3,64,256]{2,1,0:T(8,128)(2,1)S(1)}, bf16[3,64,256]{2,1,0:T(8,128)(2,1)S(1)}, u32[]{:S(2)}, u32[]{:S(2)}) collective-permute-start(bf16[3,64,256]{2,1,0:T(8,128)(2,1)S(1)} %collective-permute-done.15.refs_12_), channel_id=1, source_target_pairs={{0,4},{1,5},{2,6},{3,7},{4,0},{5,1},{6,2},{7,3},{8,12},{9,13},{10,... | collective-permute-start | bytes 294920 | tf_op jit(solution)/shard_map/ppermute | solution.py:24
  23.4 0.4 collective-permute-start.7
  23.8 1.6 %collective-permute-start.14 = (bf16[3,64,256]{2,1,0:T(8,128)(2,1)S(1)}, bf16[3,64,256]{2,1,0:T(8,128)(2,1)S(1)}, u32[]{:S(2)}, u32[]{:S(2)}) collective-permute-start(bf16[3,64,256]{2,1,0:T(8,128)(2,1)S(1)} %collective-permute-done.11.refs_8_), channel_id=1, source_target_pairs={{0,4},{1,5},{2,6},{3,7},{4,0},{5,1},{6,2},{7,3},{8,12},{9,13},{10,... | collective-permute-start | bytes 294920 | tf_op jit(solution)/shard_map/ppermute | solution.py:24
  25.4 0.5 collective-permute-start.13
  25.9 0.8 collective-permute-done.18.refs_14_
  26.8 0.7 collective-permute-start.19
  27.5 1.0 %collective-permute-start.17 = (bf16[3,64,256]{2,1,0:T(8,128)(2,1)S(1)}, bf16[3,64,256]{2,1,0:T(8,128)(2,1)S(1)}, u32[]{:S(2)}, u32[]{:S(2)}) collective-permute-start(bf16[3,64,256]{2,1,0:T(8,128)(2,1)S(1)} %collective-permute-done.12.refs_9_), channel_id=1, source_target_pairs={{0,4},{1,5},{2,6},{3,7},{4,0},{5,1},{6,2},{7,3},{8,12},{9,13},{10,... | collective-permute-start | bytes 294920 | tf_op jit(solution)/shard_map/ppermute | solution.py:24
  29.2 0.6 collective-permute-done.14.refs_10_
  30.1 1.3 %collective-permute-done.19.refs_15_ = bf16[3,64,256]{2,1,0:T(8,128)(2,1)S(1)} collective-permute-done((bf16[3,64,256]{2,1,0:T(8,128)(2,1)S(1)}, bf16[3,64,256]{2,1,0:T(8,128)(2,1)S(1)}, u32[]{:S(2)}, u32[]{:S(2)}) %collective-permute-start.19) | collective-permute-done | bytes 98336 | tf_op jit(solution)/shard_map/ppermute | solution.py:24
  31.4 0.7 collective-permute-done.17.refs_11_
  32.1 3.2 %slot_gradients.1 = (bf16[3,64,256]{2,1,0:T(8,128)(2,1)S(1)}, bf16[3,64,256]{2,1,0:T(8,128)(2,1)S(1)}, bf16[2,3,64,256]{3,2,1,0:T(8,128)(2,1)S(1)}, bf16[2,3,64,...) custom-call(s32[32]{0:T(128)S(1)} %copy-done.3, ...), custom_call_target="tpu_custom_call" | custom-call | flops 1610612736 | bytes 7340032 | tf_op jit(solution)/shard_map/slot_gradients/pallas_call | solution.py:148
  35.3 1.4 %collective-permute-start.20 = (bf16[3,64,256]{2,1,0:T(8,128)(2,1)S(1)}, bf16[3,64,256]{2,1,0:T(8,128)(2,1)S(1)}, u32[]{:S(2)}, u32[]{:S(2)}) collective-permute-start(bf16[3,64,256]{2,1,0:T(8,128)(2,1)S(1)} %get-tuple-element.63), channel_id=1, source_target_pairs={{0,2},{1,3},{2,0},{3,1},{4,6},{5,7},{6,4},{7,5},{8,10},{9,11},{10,... | collective-permute-start | bytes 294920 | tf_op jit(solution)/shard_map/ppermute | solution.py:24
  36.7 0.7 collective-permute-start.22
  37.4 1.0 %collective-permute-start.25 = (bf16[3,64,256]{2,1,0:T(8,128)(2,1)S(1)}, bf16[3,64,256]{2,1,0:T(8,128)(2,1)S(1)}, u32[]{:S(2)}, u32[]{:S(2)}) collective-permute-start(bf16[3,64,256]{2,1,0:T(8,128)(2,1)S(1)} %get-tuple-element.69), channel_id=1, source_target_pairs={{0,4},{1,5},{2,6},{3,7},{4,0},{5,1},{6,2},{7,3},{8,12},{9,13},{10,... | collective-permute-start | bytes 294920 | tf_op jit(solution)/shard_map/ppermute | solution.py:24
  38.4 2.1 %collective-permute-done.20 = bf16[3,64,256]{2,1,0:T(8,128)(2,1)S(1)} collective-permute-done((bf16[3,64,256]{2,1,0:T(8,128)(2,1)S(1)}, bf16[3,64,256]{2,1,0:T(8,128)(2,1)S(1)}, u32[]{:S(2)}, u32[]{:S(2)}) %collective-permute-start.20) | collective-permute-done | bytes 98336 | tf_op jit(solution)/shard_map/ppermute | solution.py:24
  40.5 0.7 collective-permute-start.30
  41.2 1.4 %collective-permute-start.21 = (bf16[3,64,256]{2,1,0:T(8,128)(2,1)S(1)}, bf16[3,64,256]{2,1,0:T(8,128)(2,1)S(1)}, u32[]{:S(2)}, u32[]{:S(2)}) collective-permute-start(bf16[3,64,256]{2,1,0:T(8,128)(2,1)S(1)} %add_convert_fusion.3), channel_id=1, source_target_pairs={{0,4},{1,5},{2,6},{3,7},{4,0},{5,1},{6,2},{7,3},{8,12},{9,13},{10,... | collective-permute-start | bytes 294920 | tf_op jit(solution)/shard_map/ppermute | solution.py:24
  42.6 1.5 %collective-permute-start.29 = (bf16[3,64,256]{2,1,0:T(8,128)(2,1)S(1)}, bf16[3,64,256]{2,1,0:T(8,128)(2,1)S(1)}, u32[]{:S(2)}, u32[]{:S(2)}) collective-permute-start(bf16[3,64,256]{2,1,0:T(8,128)(2,1)S(1)} %add_convert_fusion.1), channel_id=1, source_target_pairs={{0,2},{1,3},{2,0},{3,1},{4,6},{5,7},{6,4},{7,5},{8,10},{9,11},{10,... | collective-permute-start | bytes 294920 | tf_op jit(solution)/shard_map/ppermute | solution.py:24
  44.1 2.6 %collective-permute-start.26 = (bf16[2,3,64,256]{3,2,1,0:T(8,128)(2,1)S(1)}, bf16[2,3,64,256]{3,2,1,0:T(8,128)(2,1)S(1)}, u32[]{:S(2)}, u32[]{:S(2)}) collective-permute-start(bf16[2,3,64,256]{3,2,1,0:T(8,128)(2,1)S(1)} %get-tuple-element.70), channel_id=1, source_target_pairs={{0,6},{1,7},{2,4},{3,5},{4,2},{5,3},{6,0},{7,1},{8,14},{9,15},{10,... | collective-permute-start | bytes 589832 | tf_op jit(solution)/shard_map/ppermute | solution.py:24
  46.8 5.3 %collective-permute-start.28 = (bf16[3,64,256]{2,1,0:T(8,128)(2,1)S(1)}, bf16[3,64,256]{2,1,0:T(8,128)(2,1)S(1)}, u32[]{:S(2)}, u32[]{:S(2)}) collective-permute-start(bf16[3,64,256]{2,1,0:T(8,128)(2,1)S(1)} %add_convert_fusion.2), channel_id=1, source_target_pairs={{0,24},{1,25},{2,26},{3,27},{4,28},{5,29},{6,30},{7,31},{8,16},{9,... | collective-permute-start | bytes 294920 | tf_op jit(solution)/shard_map/ppermute | solution.py:24
  52.1 1.8 %collective-permute-start.23 = (bf16[2,3,64,256]{3,2,1,0:T(8,128)(2,1)S(1)}, bf16[2,3,64,256]{3,2,1,0:T(8,128)(2,1)S(1)}, u32[]{:S(2)}, u32[]{:S(2)}) collective-permute-start(bf16[2,3,64,256]{3,2,1,0:T(8,128)(2,1)S(1)} %get-tuple-element.65), channel_id=1, source_target_pairs={{0,2},{1,3},{2,0},{3,1},{4,6},{5,7},{6,4},{7,5},{8,10},{9,11},{10,... | collective-permute-start | bytes 589832 | tf_op jit(solution)/shard_map/ppermute | solution.py:24
  53.9 0.7 collective-permute-start.24
  55.0 2.8 %collective-permute-done.23 = bf16[2,3,64,256]{3,2,1,0:T(8,128)(2,1)S(1)} collective-permute-done((bf16[2,3,64,256]{3,2,1,0:T(8,128)(2,1)S(1)}, bf16[2,3,64,256]{3,2,1,0:T(8,128)(2,1)S(1)}, u32[]{:S(2)}, u32[]{:S(2)}) %collective-permute-start.23) | collective-permute-done | bytes 196640 | tf_op jit(solution)/shard_map/ppermute | solution.py:24
  57.8 2.2 %collective-permute-done.24 = bf16[2,3,64,256]{3,2,1,0:T(8,128)(2,1)S(1)} collective-permute-done((bf16[2,3,64,256]{3,2,1,0:T(8,128)(2,1)S(1)}, bf16[2,3,64,256]{3,2,1,0:T(8,128)(2,1)S(1)}, u32[]{:S(2)}, u32[]{:S(2)}) %collective-permute-start.24) | collective-permute-done | bytes 196640 | tf_op jit(solution)/shard_map/ppermute | solution.py:24
  60.2 1.2 %collective-permute-done.31 = bf16[3,64,256]{2,1,0:T(8,128)(2,1)S(1)} collective-permute-done((bf16[3,64,256]{2,1,0:T(8,128)(2,1)S(1)}, bf16[3,64,256]{2,1,0:T(8,128)(2,1)S(1)}, u32[]{:S(2)}, u32[]{:S(2)}) %collective-permute-start.31) | collective-permute-done | bytes 98336 | tf_op jit(solution)/shard_map/ppermute | solution.py:24
  61.4 3.3 %collective-permute-done.27 = bf16[3,64,256]{2,1,0:T(8,128)(2,1)S(1)} collective-permute-done((bf16[3,64,256]{2,1,0:T(8,128)(2,1)S(1)}, bf16[3,64,256]{2,1,0:T(8,128)(2,1)S(1)}, u32[]{:S(2)}, u32[]{:S(2)}) %collective-permute-start.27) | collective-permute-done | bytes 98336 | tf_op jit(solution)/shard_map/ppermute | solution.py:24
  65.1 0.9 collective-permute-start.36
  66.0 1.2 %collective-permute-start.34 = (bf16[3,64,256]{2,1,0:T(8,128)(2,1)S(1)}, bf16[3,64,256]{2,1,0:T(8,128)(2,1)S(1)}, u32[]{:S(2)}, u32[]{:S(2)}) collective-permute-start(bf16[3,64,256]{2,1,0:T(8,128)(2,1)S(1)} %get-tuple-element.88.refs_0_), channel_id=1, source_target_pairs={{0,4},{1,5},{2,6},{3,7},{4,0},{5,1},{6,2},{7,3},{8,12},{9,13},{10,... | collective-permute-start | bytes 294920 | tf_op jit(solution)/shard_map/ppermute | solution.py:24
  67.2 4.4 %collective-permute-done.39.refs_8_ = bf16[3,64,256]{2,1,0:T(8,128)(2,1)S(1)} collective-permute-done((bf16[3,64,256]{2,1,0:T(8,128)(2,1)S(1)}, bf16[3,64,256]{2,1,0:T(8,128)(2,1)S(1)}, u32[]{:S(2)}, u32[]{:S(2)}) %collective-permute-start.39) | collective-permute-done | bytes 98336 | tf_op jit(solution)/shard_map/ppermute | solution.py:24
  71.8 0.7 collective-permute-done.33.refs_1_
  72.5 0.4 collective-permute-start.38
  72.9 2.0 %collective-permute-start.40 = (bf16[3,64,256]{2,1,0:T(8,128)(2,1)S(1)}, bf16[3,64,256]{2,1,0:T(8,128)(2,1)S(1)}, u32[]{:S(2)}, u32[]{:S(2)}) collective-permute-start(bf16[3,64,256]{2,1,0:T(8,128)(2,1)S(1)} %collective-permute-done.39.refs_8_), channel_id=1, source_target_pairs={{0,2},{1,3},{2,0},{3,1},{4,6},{5,7},{6,4},{7,5},{8,10},{9,11},{10,... | collective-permute-start | bytes 294920 | tf_op jit(solution)/shard_map/ppermute | solution.py:24
  74.9 1.3 %collective-permute-done.43.refs_12_ = bf16[3,64,256]{2,1,0:T(8,128)(2,1)S(1)} collective-permute-done((bf16[3,64,256]{2,1,0:T(8,128)(2,1)S(1)}, bf16[3,64,256]{2,1,0:T(8,128)(2,1)S(1)}, u32[]{:S(2)}, u32[]{:S(2)}) %collective-permute-start.43) | collective-permute-done | bytes 98336 | tf_op jit(solution)/shard_map/ppermute | solution.py:24
  76.5 0.9 collective-permute-start.46
  77.4 1.0 %collective-permute-start.44 = (bf16[3,64,256]{2,1,0:T(8,128)(2,1)S(1)}, bf16[3,64,256]{2,1,0:T(8,128)(2,1)S(1)}, u32[]{:S(2)}, u32[]{:S(2)}) collective-permute-start(bf16[3,64,256]{2,1,0:T(8,128)(2,1)S(1)} %collective-permute-done.43.refs_12_), channel_id=1, source_target_pairs={{0,2},{1,3},{2,0},{3,1},{4,6},{5,7},{6,4},{7,5},{8,10},{9,11},{10,... | collective-permute-start | bytes 294920 | tf_op jit(solution)/shard_map/ppermute | solution.py:24
  78.7 1.8 %collective-permute-start.42 = (bf16[3,64,256]{2,1,0:T(8,128)(2,1)S(1)}, bf16[3,64,256]{2,1,0:T(8,128)(2,1)S(1)}, u32[]{:S(2)}, u32[]{:S(2)}) collective-permute-start(bf16[3,64,256]{2,1,0:T(8,128)(2,1)S(1)} %collective-permute-done.39.refs_8_), channel_id=1, source_target_pairs={{0,4},{1,5},{2,6},{3,7},{4,0},{5,1},{6,2},{7,3},{8,12},{9,13},{10,... | collective-permute-start | bytes 294920 | tf_op jit(solution)/shard_map/ppermute | solution.py:24
  80.5 1.1 %collective-permute-start.41 = (bf16[3,64,256]{2,1,0:T(8,128)(2,1)S(1)}, bf16[3,64,256]{2,1,0:T(8,128)(2,1)S(1)}, u32[]{:S(2)}, u32[]{:S(2)}) collective-permute-start(bf16[3,64,256]{2,1,0:T(8,128)(2,1)S(1)} %collective-permute-done.38.refs_6_), channel_id=1, source_target_pairs={{0,2},{1,3},{2,0},{3,1},{4,6},{5,7},{6,4},{7,5},{8,10},{9,11},{10,... | collective-permute-start | bytes 294920 | tf_op jit(solution)/shard_map/ppermute | solution.py:24
  81.6 0.4 collective-permute-done.44.refs_13_
  82.0 1.1 %collective-permute-start.45 = (bf16[3,64,256]{2,1,0:T(8,128)(2,1)S(1)}, bf16[3,64,256]{2,1,0:T(8,128)(2,1)S(1)}, u32[]{:S(2)}, u32[]{:S(2)}) collective-permute-start(bf16[3,64,256]{2,1,0:T(8,128)(2,1)S(1)} %collective-permute-done.40.refs_9_), channel_id=1, source_target_pairs={{0,4},{1,5},{2,6},{3,7},{4,0},{5,1},{6,2},{7,3},{8,12},{9,13},{10,... | collective-permute-start | bytes 294920 | tf_op jit(solution)/shard_map/ppermute | solution.py:24
  83.3 0.8 collective-permute-done.42.refs_10_
  84.1 1.0 %collective-permute-done.41.refs_7_ = bf16[3,64,256]{2,1,0:T(8,128)(2,1)S(1)} collective-permute-done((bf16[3,64,256]{2,1,0:T(8,128)(2,1)S(1)}, bf16[3,64,256]{2,1,0:T(8,128)(2,1)S(1)}, u32[]{:S(2)}, u32[]{:S(2)}) %collective-permute-start.41) | collective-permute-done | bytes 98336 | tf_op jit(solution)/shard_map/ppermute | solution.py:24
  85.1 2.7 %collective-permute-done.47.refs_15_ = bf16[3,64,256]{2,1,0:T(8,128)(2,1)S(1)} collective-permute-done((bf16[3,64,256]{2,1,0:T(8,128)(2,1)S(1)}, bf16[3,64,256]{2,1,0:T(8,128)(2,1)S(1)}, u32[]{:S(2)}, u32[]{:S(2)}) %collective-permute-start.47) | collective-permute-done | bytes 98336 | tf_op jit(solution)/shard_map/ppermute | solution.py:24
  87.8 1.9 %expert_outputs.1 = (bf16[256,1024]{1,0:T(8,128)(2,1)S(1)}, bf16[256,1024]{1,0:T(8,128)(2,1)S(1)}, s32[1]{0:T(128)}) custom-call(s32[32]{0:T(128)S(1)} %copy-done.4, bf16[3,64,256]{2,1,0:T(8,128)(2,1)S(1)} %get-tuple-element.88.refs_0_, bf16[3,64,256]{2,1,0:T(8,128)(2,1)S(1)} %collective-permute-done.33.refs_1_, ...), custom_call_target="tpu_custom_call" | custom-call | flops 805306368 | bytes 3670016 | tf_op jit(solution)/shard_map/expert_outputs/pallas_call | solution.py:174
  89.8 0.8 slice_bitcast_fusion
  91.3 0.4 collective-permute-done.48
  91.6 0.8 select_bitcast_fusion
  (67 shorter events, 3.0 us)
Async XLA Ops:
  0.6 2.8 %collective-permute-start.3 = (bf16[256,1024]{1,0:T(8,128)(2,1)}, bf16[256,1024]{1,0:T(8,128)(2,1)S(1)}, u32[]{:S(2)}, u32[]{:S(2)}) collective-permute-start(bf16[256,1024]{1,0:T(8,128)(2,1)} %bitcast.65), channel_id=1, source_target_pairs={{0,1},{1,0},{2,3},{3,2},{4,5},{5,4},{6,7},{7,6},{8,9},{9,8},{10,11... | collective-permute-start | bytes 1572872 | tf_op jit(solution)/shard_map/ppermute | solution.py:24
  1.1 2.5 %collective-permute-start.4 = (bf16[256,1024]{1,0:T(8,128)(2,1)}, bf16[256,1024]{1,0:T(8,128)(2,1)S(1)}, u32[]{:S(2)}, u32[]{:S(2)}) collective-permute-start(bf16[256,1024]{1,0:T(8,128)(2,1)} %bitcast.68), channel_id=1, source_target_pairs={{0,1},{1,0},{2,3},{3,2},{4,5},{5,4},{6,7},{7,6},{8,9},{9,8},{10,11... | collective-permute-start | bytes 1572872 | tf_op jit(solution)/shard_map/ppermute | solution.py:24
  1.2 3.6 %collective-permute-start.1 = (bf16[256,1024]{1,0:T(8,128)(2,1)}, bf16[256,1024]{1,0:T(8,128)(2,1)S(1)}, u32[]{:S(2)}, u32[]{:S(2)}) collective-permute-start(bf16[256,1024]{1,0:T(8,128)(2,1)} %bitcast.71), channel_id=1, source_target_pairs={{0,1},{1,0},{2,3},{3,2},{4,5},{5,4},{6,7},{7,6},{8,9},{9,8},{10,11... | collective-permute-start | bytes 1572872 | tf_op jit(solution)/shard_map/ppermute | solution.py:24
  1.7 1.1 %copy-start.5 = (f32[2,3,32,256]{3,2,1,0:T(8,128)S(1)}, f32[2,3,32,256]{3,2,1,0:T(8,128)}, u32[]{:S(2)}) copy-start(f32[2,3,32,256]{3,2,1,0:T(8,128)} %param.11) | copy-start | bytes 589828
  1.7 2.0 %copy-start.1 = (bf16[1,256,1024]{2,1,0:T(8,128)(2,1)S(1)}, bf16[1,256,1024]{2,1,0:T(8,128)(2,1)}, u32[]{:S(2)}) copy-start(bf16[1,256,1024]{2,1,0:T(8,128)(2,1)} %param.13) | copy-start | bytes 1572868
  2.8 1.1 %copy-start = (bf16[1,256,1024]{2,1,0:T(8,128)(2,1)S(1)}, bf16[1,256,1024]{2,1,0:T(8,128)(2,1)}, u32[]{:S(2)}) copy-start(bf16[1,256,1024]{2,1,0:T(8,128)(2,1)} %param.12) | copy-start | bytes 1572868
  2.9 2.0 %collective-permute-start = (f32[3,3,32,256]{3,2,1,0:T(8,128)S(1)}, f32[3,3,32,256]{3,2,1,0:T(8,128)S(1)}, u32[]{:S(2)}, u32[]{:S(2)}) collective-permute-start(f32[3,3,32,256]{3,2,1,0:T(8,128)S(1)} %pad_maximum_fusion.1), channel_id=1, source_target_pairs={{0,1},{1,0},{2,3},{3,2},{4,5},{5,4},{6,7},{7,6},{8,9},{9,8},{10,11... | collective-permute-start | bytes 884744 | tf_op jit(solution)/shard_map/ppermute | solution.py:24
  3.0 1.8 %collective-permute-start.2 = (s32[1]{0:T(128)}, s32[1]{0:T(128)}, u32[]{:S(2)}, u32[]{:S(2)}) collective-permute-start(s32[1]{0:T(128)} %param.17), channel_id=1, source_target_pairs={{0,1},{1,0},{2,3},{3,2},{4,5},{5,4},{6,7},{7,6},{8,9},{9,8},{10,11... | collective-permute-start | bytes 20 | tf_op jit(solution)/shard_map/ppermute | solution.py:24
  4.9 27.2 %copy-start.3 = (s32[32]{0:T(128)S(1)}, s32[32]{0:T(128)}, u32[]{:S(2)}) copy-start(s32[32]{0:T(128)} %slots.2) | copy-start | bytes 388
  4.9 9.3 %collective-permute-start.11 = (bf16[3,64,256]{2,1,0:T(8,128)(2,1)S(1)}, bf16[3,64,256]{2,1,0:T(8,128)(2,1)S(1)}, u32[]{:S(2)}, u32[]{:S(2)}) collective-permute-start(bf16[3,64,256]{2,1,0:T(8,128)(2,1)S(1)} %fusion.7.refs_0_), channel_id=1, source_target_pairs={{0,16},{1,17},{2,18},{3,19},{4,20},{5,21},{6,22},{7,23},{8,24},{9,... | collective-permute-start | bytes 294920 | tf_op jit(solution)/shard_map/ppermute | solution.py:24
  8.9 6.0 %collective-permute-start.8 = (bf16[3,64,256]{2,1,0:T(8,128)(2,1)S(1)}, bf16[3,64,256]{2,1,0:T(8,128)(2,1)S(1)}, u32[]{:S(2)}, u32[]{:S(2)}) collective-permute-start(bf16[3,64,256]{2,1,0:T(8,128)(2,1)S(1)} %fusion.7.refs_0_), channel_id=1, source_target_pairs={{0,8},{1,9},{2,10},{3,11},{4,12},{5,13},{6,14},{7,15},{8,0},{9,1},... | collective-permute-start | bytes 294920 | tf_op jit(solution)/shard_map/ppermute | solution.py:24
  10.5 5.9 %collective-permute-start.5 = (bf16[3,64,256]{2,1,0:T(8,128)(2,1)S(1)}, bf16[3,64,256]{2,1,0:T(8,128)(2,1)S(1)}, u32[]{:S(2)}, u32[]{:S(2)}) collective-permute-start(bf16[3,64,256]{2,1,0:T(8,128)(2,1)S(1)} %fusion.7.refs_0_), channel_id=1, source_target_pairs={{0,2},{1,3},{2,0},{3,1},{4,6},{5,7},{6,4},{7,5},{8,10},{9,11},{10,... | collective-permute-start | bytes 294920 | tf_op jit(solution)/shard_map/ppermute | solution.py:24
  12.0 5.9 %collective-permute-start.6 = (bf16[3,64,256]{2,1,0:T(8,128)(2,1)S(1)}, bf16[3,64,256]{2,1,0:T(8,128)(2,1)S(1)}, u32[]{:S(2)}, u32[]{:S(2)}) collective-permute-start(bf16[3,64,256]{2,1,0:T(8,128)(2,1)S(1)} %fusion.7.refs_0_), channel_id=1, source_target_pairs={{0,4},{1,5},{2,6},{3,7},{4,0},{5,1},{6,2},{7,3},{8,12},{9,13},{10,... | collective-permute-start | bytes 294920 | tf_op jit(solution)/shard_map/ppermute | solution.py:24
  14.3 4.6 %collective-permute-start.15 = (bf16[3,64,256]{2,1,0:T(8,128)(2,1)S(1)}, bf16[3,64,256]{2,1,0:T(8,128)(2,1)S(1)}, u32[]{:S(2)}, u32[]{:S(2)}) collective-permute-start(bf16[3,64,256]{2,1,0:T(8,128)(2,1)S(1)} %collective-permute-done.11.refs_8_), channel_id=1, source_target_pairs={{0,8},{1,9},{2,10},{3,11},{4,12},{5,13},{6,14},{7,15},{8,0},{9,1},... | collective-permute-start | bytes 294920 | tf_op jit(solution)/shard_map/ppermute | solution.py:24
  14.9 4.6 %collective-permute-start.9 = (bf16[3,64,256]{2,1,0:T(8,128)(2,1)S(1)}, bf16[3,64,256]{2,1,0:T(8,128)(2,1)S(1)}, u32[]{:S(2)}, u32[]{:S(2)}) collective-permute-start(bf16[3,64,256]{2,1,0:T(8,128)(2,1)S(1)} %collective-permute-done.8.refs_4_), channel_id=1, source_target_pairs={{0,2},{1,3},{2,0},{3,1},{4,6},{5,7},{6,4},{7,5},{8,10},{9,11},{10,... | collective-permute-start | bytes 294920 | tf_op jit(solution)/shard_map/ppermute | solution.py:24
  16.4 7.4 %collective-permute-start.10 = (bf16[3,64,256]{2,1,0:T(8,128)(2,1)S(1)}, bf16[3,64,256]{2,1,0:T(8,128)(2,1)S(1)}, u32[]{:S(2)}, u32[]{:S(2)}) collective-permute-start(bf16[3,64,256]{2,1,0:T(8,128)(2,1)S(1)} %collective-permute-done.8.refs_4_), channel_id=1, source_target_pairs={{0,4},{1,5},{2,6},{3,7},{4,0},{5,1},{6,2},{7,3},{8,12},{9,13},{10,... | collective-permute-start | bytes 294920 | tf_op jit(solution)/shard_map/ppermute | solution.py:24
  17.9 7.5 %collective-permute-start.12 = (bf16[3,64,256]{2,1,0:T(8,128)(2,1)S(1)}, bf16[3,64,256]{2,1,0:T(8,128)(2,1)S(1)}, u32[]{:S(2)}, u32[]{:S(2)}) collective-permute-start(bf16[3,64,256]{2,1,0:T(8,128)(2,1)S(1)} %collective-permute-done.11.refs_8_), channel_id=1, source_target_pairs={{0,2},{1,3},{2,0},{3,1},{4,6},{5,7},{6,4},{7,5},{8,10},{9,11},{10,... | collective-permute-start | bytes 294920 | tf_op jit(solution)/shard_map/ppermute | solution.py:24
  19.5 6.4 %collective-permute-start.16 = (bf16[3,64,256]{2,1,0:T(8,128)(2,1)S(1)}, bf16[3,64,256]{2,1,0:T(8,128)(2,1)S(1)}, u32[]{:S(2)}, u32[]{:S(2)}) collective-permute-start(bf16[3,64,256]{2,1,0:T(8,128)(2,1)S(1)} %collective-permute-done.15.refs_12_), channel_id=1, source_target_pairs={{0,2},{1,3},{2,0},{3,1},{4,6},{5,7},{6,4},{7,5},{8,10},{9,11},{10,... | collective-permute-start | bytes 294920 | tf_op jit(solution)/shard_map/ppermute | solution.py:24
  21.8 5.0 %collective-permute-start.18 = (bf16[3,64,256]{2,1,0:T(8,128)(2,1)S(1)}, bf16[3,64,256]{2,1,0:T(8,128)(2,1)S(1)}, u32[]{:S(2)}, u32[]{:S(2)}) collective-permute-start(bf16[3,64,256]{2,1,0:T(8,128)(2,1)S(1)} %collective-permute-done.15.refs_12_), channel_id=1, source_target_pairs={{0,4},{1,5},{2,6},{3,7},{4,0},{5,1},{6,2},{7,3},{8,12},{9,13},{10,... | collective-permute-start | bytes 294920 | tf_op jit(solution)/shard_map/ppermute | solution.py:24
  23.4 5.8 %collective-permute-start.7 = (bf16[3,64,256]{2,1,0:T(8,128)(2,1)S(1)}, bf16[3,64,256]{2,1,0:T(8,128)(2,1)S(1)}, u32[]{:S(2)}, u32[]{:S(2)}) collective-permute-start(bf16[3,64,256]{2,1,0:T(8,128)(2,1)S(1)} %collective-permute-done.5.refs_1_), channel_id=1, source_target_pairs={{0,4},{1,5},{2,6},{3,7},{4,0},{5,1},{6,2},{7,3},{8,12},{9,13},{10,... | collective-permute-start | bytes 294920 | tf_op jit(solution)/shard_map/ppermute | solution.py:24
  23.8 6.0 %collective-permute-start.14 = (bf16[3,64,256]{2,1,0:T(8,128)(2,1)S(1)}, bf16[3,64,256]{2,1,0:T(8,128)(2,1)S(1)}, u32[]{:S(2)}, u32[]{:S(2)}) collective-permute-start(bf16[3,64,256]{2,1,0:T(8,128)(2,1)S(1)} %collective-permute-done.11.refs_8_), channel_id=1, source_target_pairs={{0,4},{1,5},{2,6},{3,7},{4,0},{5,1},{6,2},{7,3},{8,12},{9,13},{10,... | collective-permute-start | bytes 294920 | tf_op jit(solution)/shard_map/ppermute | solution.py:24
  25.4 4.6 %collective-permute-start.13 = (bf16[3,64,256]{2,1,0:T(8,128)(2,1)S(1)}, bf16[3,64,256]{2,1,0:T(8,128)(2,1)S(1)}, u32[]{:S(2)}, u32[]{:S(2)}) collective-permute-start(bf16[3,64,256]{2,1,0:T(8,128)(2,1)S(1)} %collective-permute-done.10.refs_6_), channel_id=1, source_target_pairs={{0,2},{1,3},{2,0},{3,1},{4,6},{5,7},{6,4},{7,5},{8,10},{9,11},{10,... | collective-permute-start | bytes 294920 | tf_op jit(solution)/shard_map/ppermute | solution.py:24
  26.8 4.6 %collective-permute-start.19 = (bf16[3,64,256]{2,1,0:T(8,128)(2,1)S(1)}, bf16[3,64,256]{2,1,0:T(8,128)(2,1)S(1)}, u32[]{:S(2)}, u32[]{:S(2)}) collective-permute-start(bf16[3,64,256]{2,1,0:T(8,128)(2,1)S(1)} %collective-permute-done.18.refs_14_), channel_id=1, source_target_pairs={{0,2},{1,3},{2,0},{3,1},{4,6},{5,7},{6,4},{7,5},{8,10},{9,11},{10,... | collective-permute-start | bytes 294920 | tf_op jit(solution)/shard_map/ppermute | solution.py:24
  27.5 4.6 %collective-permute-start.17 = (bf16[3,64,256]{2,1,0:T(8,128)(2,1)S(1)}, bf16[3,64,256]{2,1,0:T(8,128)(2,1)S(1)}, u32[]{:S(2)}, u32[]{:S(2)}) collective-permute-start(bf16[3,64,256]{2,1,0:T(8,128)(2,1)S(1)} %collective-permute-done.12.refs_9_), channel_id=1, source_target_pairs={{0,4},{1,5},{2,6},{3,7},{4,0},{5,1},{6,2},{7,3},{8,12},{9,13},{10,... | collective-permute-start | bytes 294920 | tf_op jit(solution)/shard_map/ppermute | solution.py:24
  35.3 5.2 %collective-permute-start.20 = (bf16[3,64,256]{2,1,0:T(8,128)(2,1)S(1)}, bf16[3,64,256]{2,1,0:T(8,128)(2,1)S(1)}, u32[]{:S(2)}, u32[]{:S(2)}) collective-permute-start(bf16[3,64,256]{2,1,0:T(8,128)(2,1)S(1)} %get-tuple-element.63), channel_id=1, source_target_pairs={{0,2},{1,3},{2,0},{3,1},{4,6},{5,7},{6,4},{7,5},{8,10},{9,11},{10,... | collective-permute-start | bytes 294920 | tf_op jit(solution)/shard_map/ppermute | solution.py:24
  36.7 10.0 %collective-permute-start.22 = (bf16[3,64,256]{2,1,0:T(8,128)(2,1)S(1)}, bf16[3,64,256]{2,1,0:T(8,128)(2,1)S(1)}, u32[]{:S(2)}, u32[]{:S(2)}) collective-permute-start(bf16[3,64,256]{2,1,0:T(8,128)(2,1)S(1)} %get-tuple-element.64), channel_id=1, source_target_pairs={{0,2},{1,3},{2,0},{3,1},{4,6},{5,7},{6,4},{7,5},{8,10},{9,11},{10,... | collective-permute-start | bytes 294920 | tf_op jit(solution)/shard_map/ppermute | solution.py:24
  37.4 5.2 %collective-permute-start.25 = (bf16[3,64,256]{2,1,0:T(8,128)(2,1)S(1)}, bf16[3,64,256]{2,1,0:T(8,128)(2,1)S(1)}, u32[]{:S(2)}, u32[]{:S(2)}) collective-permute-start(bf16[3,64,256]{2,1,0:T(8,128)(2,1)S(1)} %get-tuple-element.69), channel_id=1, source_target_pairs={{0,4},{1,5},{2,6},{3,7},{4,0},{5,1},{6,2},{7,3},{8,12},{9,13},{10,... | collective-permute-start | bytes 294920 | tf_op jit(solution)/shard_map/ppermute | solution.py:24
  40.5 13.5 %collective-permute-start.30 = (bf16[3,64,256]{2,1,0:T(8,128)(2,1)S(1)}, bf16[3,64,256]{2,1,0:T(8,128)(2,1)S(1)}, u32[]{:S(2)}, u32[]{:S(2)}) collective-permute-start(bf16[3,64,256]{2,1,0:T(8,128)(2,1)S(1)} %get-tuple-element.76), channel_id=1, source_target_pairs={{0,4},{1,5},{2,6},{3,7},{4,0},{5,1},{6,2},{7,3},{8,12},{9,13},{10,... | collective-permute-start | bytes 294920 | tf_op jit(solution)/shard_map/ppermute | solution.py:24
  41.2 5.5 %collective-permute-start.21 = (bf16[3,64,256]{2,1,0:T(8,128)(2,1)S(1)}, bf16[3,64,256]{2,1,0:T(8,128)(2,1)S(1)}, u32[]{:S(2)}, u32[]{:S(2)}) collective-permute-start(bf16[3,64,256]{2,1,0:T(8,128)(2,1)S(1)} %add_convert_fusion.3), channel_id=1, source_target_pairs={{0,4},{1,5},{2,6},{3,7},{4,0},{5,1},{6,2},{7,3},{8,12},{9,13},{10,... | collective-permute-start | bytes 294920 | tf_op jit(solution)/shard_map/ppermute | solution.py:24
  42.6 12.0 %collective-permute-start.29 = (bf16[3,64,256]{2,1,0:T(8,128)(2,1)S(1)}, bf16[3,64,256]{2,1,0:T(8,128)(2,1)S(1)}, u32[]{:S(2)}, u32[]{:S(2)}) collective-permute-start(bf16[3,64,256]{2,1,0:T(8,128)(2,1)S(1)} %add_convert_fusion.1), channel_id=1, source_target_pairs={{0,2},{1,3},{2,0},{3,1},{4,6},{5,7},{6,4},{7,5},{8,10},{9,11},{10,... | collective-permute-start | bytes 294920 | tf_op jit(solution)/shard_map/ppermute | solution.py:24
  44.1 10.9 %collective-permute-start.26 = (bf16[2,3,64,256]{3,2,1,0:T(8,128)(2,1)S(1)}, bf16[2,3,64,256]{3,2,1,0:T(8,128)(2,1)S(1)}, u32[]{:S(2)}, u32[]{:S(2)}) collective-permute-start(bf16[2,3,64,256]{3,2,1,0:T(8,128)(2,1)S(1)} %get-tuple-element.70), channel_id=1, source_target_pairs={{0,6},{1,7},{2,4},{3,5},{4,2},{5,3},{6,0},{7,1},{8,14},{9,15},{10,... | collective-permute-start | bytes 589832 | tf_op jit(solution)/shard_map/ppermute | solution.py:24
  46.8 13.4 %collective-permute-start.28 = (bf16[3,64,256]{2,1,0:T(8,128)(2,1)S(1)}, bf16[3,64,256]{2,1,0:T(8,128)(2,1)S(1)}, u32[]{:S(2)}, u32[]{:S(2)}) collective-permute-start(bf16[3,64,256]{2,1,0:T(8,128)(2,1)S(1)} %add_convert_fusion.2), channel_id=1, source_target_pairs={{0,24},{1,25},{2,26},{3,27},{4,28},{5,29},{6,30},{7,31},{8,16},{9,... | collective-permute-start | bytes 294920 | tf_op jit(solution)/shard_map/ppermute | solution.py:24
  52.1 5.7 %collective-permute-start.23 = (bf16[2,3,64,256]{3,2,1,0:T(8,128)(2,1)S(1)}, bf16[2,3,64,256]{3,2,1,0:T(8,128)(2,1)S(1)}, u32[]{:S(2)}, u32[]{:S(2)}) collective-permute-start(bf16[2,3,64,256]{3,2,1,0:T(8,128)(2,1)S(1)} %get-tuple-element.65), channel_id=1, source_target_pairs={{0,2},{1,3},{2,0},{3,1},{4,6},{5,7},{6,4},{7,5},{8,10},{9,11},{10,... | collective-permute-start | bytes 589832 | tf_op jit(solution)/shard_map/ppermute | solution.py:24
  53.9 6.1 %collective-permute-start.24 = (bf16[2,3,64,256]{3,2,1,0:T(8,128)(2,1)S(1)}, bf16[2,3,64,256]{3,2,1,0:T(8,128)(2,1)S(1)}, u32[]{:S(2)}, u32[]{:S(2)}) collective-permute-start(bf16[2,3,64,256]{3,2,1,0:T(8,128)(2,1)S(1)} %get-tuple-element.67), channel_id=1, source_target_pairs={{0,4},{1,5},{2,6},{3,7},{4,0},{5,1},{6,2},{7,3},{8,12},{9,13},{10,... | collective-permute-start | bytes 589832 | tf_op jit(solution)/shard_map/ppermute | solution.py:24
  54.6 6.8 %collective-permute-start.31 = (bf16[3,64,256]{2,1,0:T(8,128)(2,1)S(1)}, bf16[3,64,256]{2,1,0:T(8,128)(2,1)S(1)}, u32[]{:S(2)}, u32[]{:S(2)}) collective-permute-start(bf16[3,64,256]{2,1,0:T(8,128)(2,1)S(1)} %add_convert_fusion), channel_id=1, source_target_pairs={{0,16},{1,17},{2,18},{3,19},{4,20},{5,21},{6,22},{7,23},{8,24},{9,... | collective-permute-start | bytes 294920 | tf_op jit(solution)/shard_map/ppermute | solution.py:24
  60.1 4.7 %collective-permute-start.27 = (bf16[3,64,256]{2,1,0:T(8,128)(2,1)S(1)}, bf16[3,64,256]{2,1,0:T(8,128)(2,1)S(1)}, u32[]{:S(2)}, u32[]{:S(2)}) collective-permute-start(bf16[3,64,256]{2,1,0:T(8,128)(2,1)S(1)} %fusion.4), channel_id=1, source_target_pairs={{0,8},{1,9},{2,10},{3,11},{4,12},{5,13},{6,14},{7,15},{8,0},{9,1},... | collective-permute-start | bytes 294920 | tf_op jit(solution)/shard_map/ppermute | solution.py:24
  65.0 6.6 %collective-permute-start.39 = (bf16[3,64,256]{2,1,0:T(8,128)(2,1)S(1)}, bf16[3,64,256]{2,1,0:T(8,128)(2,1)S(1)}, u32[]{:S(2)}, u32[]{:S(2)}) collective-permute-start(bf16[3,64,256]{2,1,0:T(8,128)(2,1)S(1)} %get-tuple-element.88.refs_0_), channel_id=1, source_target_pairs={{0,16},{1,17},{2,18},{3,19},{4,20},{5,21},{6,22},{7,23},{8,24},{9,... | collective-permute-start | bytes 294920 | tf_op jit(solution)/shard_map/ppermute | solution.py:24
  65.1 6.6 %collective-permute-start.36 = (bf16[3,64,256]{2,1,0:T(8,128)(2,1)S(1)}, bf16[3,64,256]{2,1,0:T(8,128)(2,1)S(1)}, u32[]{:S(2)}, u32[]{:S(2)}) collective-permute-start(bf16[3,64,256]{2,1,0:T(8,128)(2,1)S(1)} %get-tuple-element.88.refs_0_), channel_id=1, source_target_pairs={{0,8},{1,9},{2,10},{3,11},{4,12},{5,13},{6,14},{7,15},{8,0},{9,1},... | collective-permute-start | bytes 294920 | tf_op jit(solution)/shard_map/ppermute | solution.py:24
  66.0 5.7 %collective-permute-start.34 = (bf16[3,64,256]{2,1,0:T(8,128)(2,1)S(1)}, bf16[3,64,256]{2,1,0:T(8,128)(2,1)S(1)}, u32[]{:S(2)}, u32[]{:S(2)}) collective-permute-start(bf16[3,64,256]{2,1,0:T(8,128)(2,1)S(1)} %get-tuple-element.88.refs_0_), channel_id=1, source_target_pairs={{0,4},{1,5},{2,6},{3,7},{4,0},{5,1},{6,2},{7,3},{8,12},{9,13},{10,... | collective-permute-start | bytes 294920 | tf_op jit(solution)/shard_map/ppermute | solution.py:24
  67.2 5.2 %collective-permute-start.33 = (bf16[3,64,256]{2,1,0:T(8,128)(2,1)S(1)}, bf16[3,64,256]{2,1,0:T(8,128)(2,1)S(1)}, u32[]{:S(2)}, u32[]{:S(2)}) collective-permute-start(bf16[3,64,256]{2,1,0:T(8,128)(2,1)S(1)} %get-tuple-element.88.refs_0_), channel_id=1, source_target_pairs={{0,2},{1,3},{2,0},{3,1},{4,6},{5,7},{6,4},{7,5},{8,10},{9,11},{10,... | collective-permute-start | bytes 294920 | tf_op jit(solution)/shard_map/ppermute | solution.py:24
  71.7 4.6 %collective-permute-start.43 = (bf16[3,64,256]{2,1,0:T(8,128)(2,1)S(1)}, bf16[3,64,256]{2,1,0:T(8,128)(2,1)S(1)}, u32[]{:S(2)}, u32[]{:S(2)}) collective-permute-start(bf16[3,64,256]{2,1,0:T(8,128)(2,1)S(1)} %collective-permute-done.39.refs_8_), channel_id=1, source_target_pairs={{0,8},{1,9},{2,10},{3,11},{4,12},{5,13},{6,14},{7,15},{8,0},{9,1},... | collective-permute-start | bytes 294920 | tf_op jit(solution)/shard_map/ppermute | solution.py:24
  71.7 4.8 %collective-permute-start.37 = (bf16[3,64,256]{2,1,0:T(8,128)(2,1)S(1)}, bf16[3,64,256]{2,1,0:T(8,128)(2,1)S(1)}, u32[]{:S(2)}, u32[]{:S(2)}) collective-permute-start(bf16[3,64,256]{2,1,0:T(8,128)(2,1)S(1)} %collective-permute-done.36.refs_4_), channel_id=1, source_target_pairs={{0,2},{1,3},{2,0},{3,1},{4,6},{5,7},{6,4},{7,5},{8,10},{9,11},{10,... | collective-permute-start | bytes 294920 | tf_op jit(solution)/shard_map/ppermute | solution.py:24
  72.5 6.2 %collective-permute-start.38 = (bf16[3,64,256]{2,1,0:T(8,128)(2,1)S(1)}, bf16[3,64,256]{2,1,0:T(8,128)(2,1)S(1)}, u32[]{:S(2)}, u32[]{:S(2)}) collective-permute-start(bf16[3,64,256]{2,1,0:T(8,128)(2,1)S(1)} %collective-permute-done.36.refs_4_), channel_id=1, source_target_pairs={{0,4},{1,5},{2,6},{3,7},{4,0},{5,1},{6,2},{7,3},{8,12},{9,13},{10,... | collective-permute-start | bytes 294920 | tf_op jit(solution)/shard_map/ppermute | solution.py:24
  72.9 7.6 %collective-permute-start.40 = (bf16[3,64,256]{2,1,0:T(8,128)(2,1)S(1)}, bf16[3,64,256]{2,1,0:T(8,128)(2,1)S(1)}, u32[]{:S(2)}, u32[]{:S(2)}) collective-permute-start(bf16[3,64,256]{2,1,0:T(8,128)(2,1)S(1)} %collective-permute-done.39.refs_8_), channel_id=1, source_target_pairs={{0,2},{1,3},{2,0},{3,1},{4,6},{5,7},{6,4},{7,5},{8,10},{9,11},{10,... | collective-permute-start | bytes 294920 | tf_op jit(solution)/shard_map/ppermute | solution.py:24
  76.5 6.6 %collective-permute-start.46 = (bf16[3,64,256]{2,1,0:T(8,128)(2,1)S(1)}, bf16[3,64,256]{2,1,0:T(8,128)(2,1)S(1)}, u32[]{:S(2)}, u32[]{:S(2)}) collective-permute-start(bf16[3,64,256]{2,1,0:T(8,128)(2,1)S(1)} %collective-permute-done.43.refs_12_), channel_id=1, source_target_pairs={{0,4},{1,5},{2,6},{3,7},{4,0},{5,1},{6,2},{7,3},{8,12},{9,13},{10,... | collective-permute-start | bytes 294920 | tf_op jit(solution)/shard_map/ppermute | solution.py:24
  77.4 4.6 %collective-permute-start.44 = (bf16[3,64,256]{2,1,0:T(8,128)(2,1)S(1)}, bf16[3,64,256]{2,1,0:T(8,128)(2,1)S(1)}, u32[]{:S(2)}, u32[]{:S(2)}) collective-permute-start(bf16[3,64,256]{2,1,0:T(8,128)(2,1)S(1)} %collective-permute-done.43.refs_12_), channel_id=1, source_target_pairs={{0,2},{1,3},{2,0},{3,1},{4,6},{5,7},{6,4},{7,5},{8,10},{9,11},{10,... | collective-permute-start | bytes 294920 | tf_op jit(solution)/shard_map/ppermute | solution.py:24
  78.4 9.4 %copy-start.2 = (bf16[1,256,1024]{2,1,0:T(8,128)(2,1)S(1)}, bf16[1,256,1024]{2,1,0:T(8,128)(2,1)}, u32[]{:S(2)}) copy-start(bf16[1,256,1024]{2,1,0:T(8,128)(2,1)} %param.14) | copy-start | bytes 1572868
  78.4 4.8 %collective-permute-start.35 = (bf16[3,64,256]{2,1,0:T(8,128)(2,1)S(1)}, bf16[3,64,256]{2,1,0:T(8,128)(2,1)S(1)}, u32[]{:S(2)}, u32[]{:S(2)}) collective-permute-start(bf16[3,64,256]{2,1,0:T(8,128)(2,1)S(1)} %collective-permute-done.33.refs_1_), channel_id=1, source_target_pairs={{0,4},{1,5},{2,6},{3,7},{4,0},{5,1},{6,2},{7,3},{8,12},{9,13},{10,... | collective-permute-start | bytes 294920 | tf_op jit(solution)/shard_map/ppermute | solution.py:24
  78.7 5.5 %collective-permute-start.42 = (bf16[3,64,256]{2,1,0:T(8,128)(2,1)S(1)}, bf16[3,64,256]{2,1,0:T(8,128)(2,1)S(1)}, u32[]{:S(2)}, u32[]{:S(2)}) collective-permute-start(bf16[3,64,256]{2,1,0:T(8,128)(2,1)S(1)} %collective-permute-done.39.refs_8_), channel_id=1, source_target_pairs={{0,4},{1,5},{2,6},{3,7},{4,0},{5,1},{6,2},{7,3},{8,12},{9,13},{10,... | collective-permute-start | bytes 294920 | tf_op jit(solution)/shard_map/ppermute | solution.py:24
  80.5 4.6 %collective-permute-start.41 = (bf16[3,64,256]{2,1,0:T(8,128)(2,1)S(1)}, bf16[3,64,256]{2,1,0:T(8,128)(2,1)S(1)}, u32[]{:S(2)}, u32[]{:S(2)}) collective-permute-start(bf16[3,64,256]{2,1,0:T(8,128)(2,1)S(1)} %collective-permute-done.38.refs_6_), channel_id=1, source_target_pairs={{0,2},{1,3},{2,0},{3,1},{4,6},{5,7},{6,4},{7,5},{8,10},{9,11},{10,... | collective-permute-start | bytes 294920 | tf_op jit(solution)/shard_map/ppermute | solution.py:24
  82.0 5.8 %collective-permute-start.45 = (bf16[3,64,256]{2,1,0:T(8,128)(2,1)S(1)}, bf16[3,64,256]{2,1,0:T(8,128)(2,1)S(1)}, u32[]{:S(2)}, u32[]{:S(2)}) collective-permute-start(bf16[3,64,256]{2,1,0:T(8,128)(2,1)S(1)} %collective-permute-done.40.refs_9_), channel_id=1, source_target_pairs={{0,4},{1,5},{2,6},{3,7},{4,0},{5,1},{6,2},{7,3},{8,12},{9,13},{10,... | collective-permute-start | bytes 294920 | tf_op jit(solution)/shard_map/ppermute | solution.py:24
  83.1 4.6 %collective-permute-start.47 = (bf16[3,64,256]{2,1,0:T(8,128)(2,1)S(1)}, bf16[3,64,256]{2,1,0:T(8,128)(2,1)S(1)}, u32[]{:S(2)}, u32[]{:S(2)}) collective-permute-start(bf16[3,64,256]{2,1,0:T(8,128)(2,1)S(1)} %collective-permute-done.46.refs_14_), channel_id=1, source_target_pairs={{0,2},{1,3},{2,0},{3,1},{4,6},{5,7},{6,4},{7,5},{8,10},{9,11},{10,... | collective-permute-start | bytes 294920 | tf_op jit(solution)/shard_map/ppermute | solution.py:24
  83.2 4.6 %copy-start.4 = (s32[32]{0:T(128)S(1)}, s32[32]{0:T(128)}, u32[]{:S(2)}) copy-start(s32[32]{0:T(128)} %slots.3) | copy-start | bytes 388
  83.2 6.5 %collective-permute-start.32 = (f32[3,3,32,256]{3,2,1,0:T(8,128)S(1)}, f32[3,3,32,256]{3,2,1,0:T(8,128)S(1)}, u32[]{:S(2)}, u32[]{:S(2)}) collective-permute-start(f32[3,3,32,256]{3,2,1,0:T(8,128)S(1)} %get-tuple-element.95), channel_id=1, source_target_pairs={{0,1},{1,0},{2,3},{3,2},{4,5},{5,4},{6,7},{7,6},{8,9},{9,8},{10,11... | collective-permute-start | bytes 884744 | tf_op jit(solution)/shard_map/ppermute | solution.py:24
  89.6 2.0 %collective-permute-start.48 = (bf16[256,1024]{1,0:T(8,128)(2,1)S(1)}, bf16[256,1024]{1,0:T(8,128)(2,1)S(1)}, u32[]{:S(2)}, u32[]{:S(2)}) collective-permute-start(bf16[256,1024]{1,0:T(8,128)(2,1)S(1)} %get-tuple-element.87), channel_id=1, source_target_pairs={{0,1},{1,0},{2,3},{3,2},{4,5},{5,4},{6,7},{7,6},{8,9},{9,8},{10,11... | collective-permute-start | bytes 1572872 | tf_op jit(solution)/shard_map/ppermute | solution.py:24

commit v8 on v6

--- a/solution.py
+++ b/solution.py
@@ -55,17 +55,13 @@
 
 
 def places(outs):
-    found = []
-    for zj in range(len(outs) // 3):
-        own, later, pair = outs[3 * zj : 3 * zj + 3]
-        by_x, by_y = ((pair, (1,)), (later, ())) if zj % 2 else ((later, ()), (pair, (1,)))
-        found += [(own, ()), by_x, by_y, (pair, (0,))]
-    return found
+    plane = lax.axis_index("dev") // 2 % 4
+    return [(outs[j // 8], (lax.bitwise_xor(plane, j % 4), j // 4 % 2)) for j in range(8 * len(outs))]
 
 
 def gradient_rows(first_row, products, outs):
     outs = places(outs)
-    rows = outs[0][0].shape[1]
+    rows = outs[0][0].shape[-2]
     width = len(outs) * rows
     tall = min(width, 256)
     for at in range(0, width, tall):
@@ -145,13 +141,11 @@
     count = len(pieces)
     kinds, rows, units = pieces[0].shape
     tokens, width = own_x.shape
-    one = jax.ShapeDtypeStruct((kinds, rows, units), jnp.bfloat16)
-    two = jax.ShapeDtypeStruct((2, kinds, rows, units), jnp.bfloat16)
     return pl.pallas_call(
         functools.partial(backward_kernel, count),
-        out_shape=[one, one, two] * (count // 4),
+        out_shape=[jax.ShapeDtypeStruct((4, 2, kinds, rows, units), jnp.bfloat16)] * (count // 8),
         in_specs=[SMEM] * 3 + [VMEM] * (count + 6),
-        out_specs=[VMEM] * (3 * count // 4),
+        out_specs=[VMEM] * (count // 8),
         scratch_shapes=[
             pltpu.VMEM((2 * tokens, units), jnp.bfloat16),
             pltpu.VMEM((2 * tokens, units), jnp.bfloat16),
@@ -195,27 +189,19 @@
 
 def gather_chips(piece):
     depth = lax.axis_size("dev") // Z_UNIT
-    column = [piece] + [None] * (depth - 1)
-    for top in reversed([1 << bit for bit in range(depth.bit_length() - 1)]):
-        column[top] = hop(piece, top * Z_UNIT)
-    along_x, along_y, across = [None] * depth, [None] * depth, [None] * depth
-    along_x[0] = hop(piece, X_STEP)
-    along_y[0] = hop(piece, Y_STEP)
-    along_x[1] = hop(column[1], X_STEP)
-    for zj in range(2, depth):
-        top = 1 << zj.bit_length() - 1
-        if zj != top:
-            column[zj] = hop(column[top], (zj - top) * Z_UNIT)
-    along_y[1] = hop(after(column[1], along_x[0]), Y_STEP)
-    for zj in range(2, depth, 2):
-        along_x[zj] = hop(after(column[zj], along_x[zj - 2], along_y[zj - 2]), X_STEP)
-        across[zj - 2] = hop(after(along_x[zj - 2], along_y[zj - 2]), Y_STEP)
-        along_x[zj + 1] = hop(after(column[zj + 1], along_x[zj - 1]), X_STEP)
-        along_y[zj + 1] = hop(after(column[zj + 1], along_x[zj - 1]), Y_STEP)
-        along_y[zj] = hop(after(column[zj], along_y[zj - 1]), Y_STEP)
-        across[zj - 1] = hop(after(along_y[zj - 1], along_x[zj]), X_STEP)
-    across[-2] = hop(after(along_x[-2], along_x[-1]), Y_STEP)
-    across[-1] = hop(along_y[-1], X_STEP)
+    column = [piece] + [hop(piece, zj * Z_UNIT) for zj in range(1, depth)]
+    along_x, along_y, across = [], [], []
+    for zj, here in enumerate(column):
+        if zj > 1:
+            here = after(here, column[zj - 1], along_x[zj - 2], along_y[zj - 2])
+        along_x.append(hop(here, X_STEP))
+        along_y.append(hop(here, Y_STEP))
+        if zj > 1 and zj == depth - 1:
+            across.append(hop(here, X_STEP | Y_STEP))
+        elif zj % 2:
+            across.append(hop(after(along_y[zj], along_x[zj]), X_STEP))
+        else:
+            across.append(hop(after(along_x[zj], along_y[zj]), Y_STEP))
     return [part for group in zip(column, along_x, along_y, across) for part in group]
 
 
@@ -227,27 +213,22 @@
 
 
 def reduce_chips(pieces):
-    depth = lax.axis_size("dev") // Z_UNIT
-    column = [[pieces[3 * zj]] for zj in range(depth)]
-    arrived, crossed, risen = (), (), ()
-    for upper in reversed(range(1, depth, 2)):
-        up_y, pair_x = pieces[3 * upper + 1 : 3 * upper + 3]
-        below_x, pair_y = pieces[3 * upper - 2 : 3 * upper]
-        got_x = hop(pair_x, X_STEP)
-        got_y = hop(after(pair_y, *arrived), Y_STEP)
-        up_y = add_all(up_y, got_x[0]).astype(jnp.bfloat16)
-        column[upper] += [got_x[1], hop(after(up_y, *crossed), Y_STEP)]
-        below_x = add_all(below_x, got_y[0]).astype(jnp.bfloat16)
-        column[upper - 1] += [got_y[1], hop(after(below_x, *risen), X_STEP)]
-        arrived, crossed, risen = (got_x,), (column[upper][-1],), ()
-        for zj in (upper, upper - 1):
-            top = 1 << zj.bit_length() - 1 if zj else 0
-            low = zj - top
+    devices = lax.axis_size("dev")
+    planes = [
+        [base + core + 2 * chip for chip in range(4)] for base in range(0, devices, Z_UNIT) for core in range(2)
+    ]
+    total, sent = None, ()
+    for pair in reversed(range(len(pieces))):
+        got = lax.all_to_all(after(pieces[pair], *sent), "dev", 0, 0, axis_index_groups=planes)
+        sent = ()
+        for zj in (2 * pair + 1, 2 * pair):
+            column = add_all(*[got[chip, zj % 2] for chip in range(4)])
             if zj:
-                part = add_all(*column[zj]).astype(jnp.bfloat16)
-                column[top if low else 0].append(hop(part, (low or top) * Z_UNIT))
-                risen = risen or (column[top if low else 0][-1],)
-    return add_all(*column[0])
+                column = column.astype(jnp.bfloat16)
+                sent += (column,)
+                column = hop(column, zj * Z_UNIT).astype(jnp.float32)
+            total = column if total is None else total + column
+    return total
 
 
 def block_a_core(master, first, second, old_rows, old_cotangent, new_rows, old_slots, new_slots, live):

time: 90.5 us -> 101 us (1.12)
  blocking collectives: 0 us -> 11.7 us
  waiting for transfers between devices: 29.2 us -> 24.2 us
  starting transfers between devices: 49.4 us -> 51.8 us
    all_to_all x0 -> x1, blocking collectives: none -> 11.7 us  [reduce_chips(): lax.all_to_all(after(pieces[pair], *sent), 'dev', 0, 0, axis_index_groups...]
    ppermute x48 -> x40, waiting for transfers between devices: 29.2 us -> 20.3 us  [hop(): lax.ppermute(block, 'dev', [(low, low ^ mask) for low in range(count)])]
    all_to_all x0 -> x1, waiting for transfers between devices: none -> 3.92 us  [reduce_chips(): lax.all_to_all(after(pieces[pair], *sent), 'dev', 0, 0, axis_index_groups...]
    all_to_all x0 -> x1, starting transfers between devices: none -> 3.5 us  [reduce_chips(): lax.all_to_all(after(pieces[pair], *sent), 'dev', 0, 0, axis_index_groups...]
    ppermute x48 -> x40, starting transfers between devices: 49.4 us -> 48.3 us  [hop(): lax.ppermute(block, 'dev', [(low, low ^ mask) for low in range(count)])]
  transfers between devices with their start and end apart: 48 -> 41, of which waited for: 28 -> 14; matrix products, arithmetic and copies ran while one was open for 3% -> 3% of each run, Pallas kernels for 3% -> 2%
where the time goes in v8:
time: 101 us; the launch traced here: 100 us
  starting transfers between devices  51.8 us (51%)
  waiting for transfers between devices  24.2 us (24%)
  blocking collectives  11.7 us (12%)
  Pallas kernels  6.37 us (6%)
  other arithmetic  2.19 us (2%)
  between operations  2.15 us (2%)
  local copies, waits for them, and re-layouts  2.07 us (2%)
    ppermute x40, starting transfers between devices, hop(): lax.ppermute(block, 'dev', [(low, low ^ mask) for low in range(count)])  48.3 us
    ppermute x40, waiting for transfers between devices, hop(): lax.ppermute(block, 'dev', [(low, low ^ mask) for low in range(count)])  20.3 us
    all_to_all x1, blocking collectives, reduce_chips(): lax.all_to_all(after(pieces[pair], *sent), 'dev', 0, 0, axis_index_groups...  11.7 us
    pallas_call x1, Pallas kernels, backward(): pl.pallas_call(functools.partial(backward_kernel, count), out_shape=[jax....  3.93 us
    all_to_all x1, waiting for transfers between devices, reduce_chips(): lax.all_to_all(after(pieces[pair], *sent), 'dev', 0, 0, axis_index_groups...  3.92 us
    all_to_all x1, starting transfers between devices, reduce_chips(): lax.all_to_all(after(pieces[pair], *sent), 'dev', 0, 0, axis_index_groups...  3.5 us
  transfers between devices with their start and end apart: 41, of which 14 were waited for; matrix products, arithmetic and copies ran while one was open for 3% of the time, Pallas kernels for 2%

profile of v8, /device:TPU:0, one launch (start us, length us, event | category | flops | bytes accessed | tf_op | source)
XLA Modules:
  0.0 100.4 jit_solution(15691128390008200753)
XLA Ops:
  0.6 0.5 collective-permute-start.3
  1.1 0.1 collective-permute-start.4
  1.2 0.4 collective-permute-start.1
  1.7 1.1 %dynamic-slice_bitcast_fusion.2 = (f32[3,32,256]{2,1,0:T(8,128)S(1)}, f32[1,3,32,256]{3,2,1,0:T(8,128)S(1)}, f32[1,3,32,256]{3,2,1,0:T(8,128)S(1)}, f32[3,32,256]{2,1,0:T(8,128)S(1)}) fusion(f32[2,3,32,256]{3,2,1,0:T(8,128)} %param.10, s32[]{:T(128)S(6)} %select_n.51, s32[]{:T(128)S(6)} %select_n.52, f32[2,3,32,256]{3,2,1,0:T(8,128)} %param.9), kind=kLoop, calls=%fused_computation.28 | loop fusion | bytes 786440 | tf_op jit(solution)/shard_map/jit(dynamic_index_in_dim)/squeeze | solution.py:239
  2.9 0.7 pad_maximum_fusion.1
  3.6 0.1 collective-permute-start
  3.7 0.4 collective-permute-start.2
  4.1 0.6 transpose_rows.1
  4.7 0.7 collective-permute-done.2.other_live
  5.5 2.8 %collective-permute-start.8 = (bf16[3,64,256]{2,1,0:T(8,128)(2,1)S(1)}, bf16[3,64,256]{2,1,0:T(8,128)(2,1)S(1)}, u32[]{:S(2)}, u32[]{:S(2)}) collective-permute-start(bf16[3,64,256]{2,1,0:T(8,128)(2,1)S(1)} %fusion.4.refs_0_), channel_id=1, source_target_pairs={{0,8},{1,9},{2,10},{3,11},{4,12},{5,13},{6,14},{7,15},{8,0},{9,1},... | collective-permute-start | bytes 294920 | tf_op jit(solution)/shard_map/ppermute | solution.py:24
  8.3 2.6 %collective-permute-start.12 = (bf16[3,64,256]{2,1,0:T(8,128)(2,1)S(1)}, bf16[3,64,256]{2,1,0:T(8,128)(2,1)S(1)}, u32[]{:S(2)}, u32[]{:S(2)}) collective-permute-start(bf16[3,64,256]{2,1,0:T(8,128)(2,1)S(1)} %fusion.4.refs_0_), channel_id=1, source_target_pairs={{0,16},{1,17},{2,18},{3,19},{4,20},{5,21},{6,22},{7,23},{8,24},{9,... | collective-permute-start | bytes 294920 | tf_op jit(solution)/shard_map/ppermute | solution.py:24
  10.9 1.5 %collective-permute-start.6 = (bf16[3,64,256]{2,1,0:T(8,128)(2,1)S(1)}, bf16[3,64,256]{2,1,0:T(8,128)(2,1)S(1)}, u32[]{:S(2)}, u32[]{:S(2)}) collective-permute-start(bf16[3,64,256]{2,1,0:T(8,128)(2,1)S(1)} %fusion.4.refs_0_), channel_id=1, source_target_pairs={{0,4},{1,5},{2,6},{3,7},{4,0},{5,1},{6,2},{7,3},{8,12},{9,13},{10,... | collective-permute-start | bytes 294920 | tf_op jit(solution)/shard_map/ppermute | solution.py:24
  12.4 1.5 %collective-permute-start.5 = (bf16[3,64,256]{2,1,0:T(8,128)(2,1)S(1)}, bf16[3,64,256]{2,1,0:T(8,128)(2,1)S(1)}, u32[]{:S(2)}, u32[]{:S(2)}) collective-permute-start(bf16[3,64,256]{2,1,0:T(8,128)(2,1)S(1)} %fusion.4.refs_0_), channel_id=1, source_target_pairs={{0,2},{1,3},{2,0},{3,1},{4,6},{5,7},{6,4},{7,5},{8,10},{9,11},{10,... | collective-permute-start | bytes 294920 | tf_op jit(solution)/shard_map/ppermute | solution.py:24
  13.9 0.2 collective-permute-start.16
  14.1 0.5 collective-permute-start.10
  14.6 1.4 %collective-permute-done.12.refs_8_ = bf16[3,64,256]{2,1,0:T(8,128)(2,1)S(1)} collective-permute-done((bf16[3,64,256]{2,1,0:T(8,128)(2,1)S(1)}, bf16[3,64,256]{2,1,0:T(8,128)(2,1)S(1)}, u32[]{:S(2)}, u32[]{:S(2)}) %collective-permute-start.12) | collective-permute-done | bytes 98336 | tf_op jit(solution)/shard_map/ppermute | solution.py:24
  16.0 1.5 %collective-permute-start.9 = (bf16[3,64,256]{2,1,0:T(8,128)(2,1)S(1)}, bf16[3,64,256]{2,1,0:T(8,128)(2,1)S(1)}, u32[]{:S(2)}, u32[]{:S(2)}) collective-permute-start(bf16[3,64,256]{2,1,0:T(8,128)(2,1)S(1)} %collective-permute-done.8.refs_4_), channel_id=1, source_target_pairs={{0,2},{1,3},{2,0},{3,1},{4,6},{5,7},{6,4},{7,5},{8,10},{9,11},{10,... | collective-permute-start | bytes 294920 | tf_op jit(solution)/shard_map/ppermute | solution.py:24
  17.5 0.5 collective-permute-done.5.refs_1_
  18.0 3.7 %collective-permute-start.14 = (bf16[3,64,256]{2,1,0:T(8,128)(2,1)S(1)}, bf16[3,64,256]{2,1,0:T(8,128)(2,1)S(1)}, u32[]{:S(2)}, u32[]{:S(2)}) collective-permute-start(bf16[3,64,256]{2,1,0:T(8,128)(2,1)S(1)} %collective-permute-done.12.refs_8_), channel_id=1, source_target_pairs={{0,4},{1,5},{2,6},{3,7},{4,0},{5,1},{6,2},{7,3},{8,12},{9,13},{10,... | collective-permute-start | bytes 294920 | tf_op jit(solution)/shard_map/ppermute | solution.py:24
  21.7 0.1 collective-permute-start.13
  21.8 0.1 collective-permute-start.7
  21.9 4.5 %collective-permute-start.19 = (bf16[3,64,256]{2,1,0:T(8,128)(2,1)S(1)}, bf16[3,64,256]{2,1,0:T(8,128)(2,1)S(1)}, u32[]{:S(2)}, u32[]{:S(2)}) collective-permute-start(bf16[3,64,256]{2,1,0:T(8,128)(2,1)S(1)} %collective-permute-done.16.refs_12_), channel_id=1, source_target_pairs={{0,6},{1,7},{2,4},{3,5},{4,2},{5,3},{6,0},{7,1},{8,14},{9,15},{10,... | collective-permute-start | bytes 294920 | tf_op jit(solution)/shard_map/ppermute | solution.py:24
  26.4 0.6 collective-permute-start.17
  27.0 1.5 %collective-permute-start.11 = (bf16[3,64,256]{2,1,0:T(8,128)(2,1)S(1)}, bf16[3,64,256]{2,1,0:T(8,128)(2,1)S(1)}, u32[]{:S(2)}, u32[]{:S(2)}) collective-permute-start(bf16[3,64,256]{2,1,0:T(8,128)(2,1)S(1)} %collective-permute-done.10.refs_6_), channel_id=1, source_target_pairs={{0,2},{1,3},{2,0},{3,1},{4,6},{5,7},{6,4},{7,5},{8,10},{9,11},{10,... | collective-permute-start | bytes 294920 | tf_op jit(solution)/shard_map/ppermute | solution.py:24
  28.5 2.0 %collective-permute-start.15 = (bf16[3,64,256]{2,1,0:T(8,128)(2,1)S(1)}, bf16[3,64,256]{2,1,0:T(8,128)(2,1)S(1)}, u32[]{:S(2)}, u32[]{:S(2)}) collective-permute-start(bf16[3,64,256]{2,1,0:T(8,128)(2,1)S(1)} %collective-permute-done.13.refs_9_), channel_id=1, source_target_pairs={{0,4},{1,5},{2,6},{3,7},{4,0},{5,1},{6,2},{7,3},{8,12},{9,13},{10,... | collective-permute-start | bytes 294920 | tf_op jit(solution)/shard_map/ppermute | solution.py:24
  31.1 1.0 collective-permute-done.11.refs_7_
  32.1 1.0 collective-permute-done.15.refs_11_
  33.1 3.9 %slot_gradients.1 = (bf16[4,2,3,64,256]{4,3,2,1,0:T(8,128)(2,1)}, bf16[4,2,3,64,256]{4,3,2,1,0:T(8,128)(2,1)S(1)}) custom-call(s32[32]{0:T(128)S(1)} %copy-done.3, s32[1]{0:T(128)S(6)} %copy.13.own_live, s32[1]{0:T(128)} %collective-permute-done.2.other_live, bf16[3,64,256]{2,1,0:T(8,128)(2,1)S(1)} %fusion.4.refs_0_, ...), custom_call_target="tpu_custom_call" | custom-call | flops 1610612736 | bytes 7340032 | tf_op jit(solution)/shard_map/slot_gradients/pallas_call | solution.py:144
  37.0 11.7 %all_to_all.10 = bf16[4,2,3,64,256]{4,3,2,1,0:T(8,128)(2,1)S(1)} all-to-all(bf16[4,2,3,64,256]{4,3,2,1,0:T(8,128)(2,1)S(1)} %get-tuple-element.41), channel_id=1, replica_groups={{0,2,4,6},{1,3,5,7},{8,10,12,14},{9,11,13,15},{16,18,20,22},{17,19,21,2..., dimensions={0} | all-to-all | bytes 1572864 | tf_op jit(solution)/shard_map/all_to_all | solution.py:222
  48.7 0.1 fusion.6
  48.8 3.5 %all-to-all-start.1 = ((bf16[4,2,3,64,256]{4,3,2,1,0:T(8,128)(2,1)}), bf16[4,2,3,64,256]{4,3,2,1,0:T(8,128)(2,1)S(1)}, u32[]{:S(2)}, u32[]{:S(2)}) async-start(bf16[4,2,3,64,256]{4,3,2,1,0:T(8,128)(2,1)} %get-tuple-element.42), calls=%async_computation.1 | async-start | bytes 1572864 | tf_op jit(solution)/shard_map/all_to_all | solution.py:222
  52.3 1.5 %collective-permute-start.21 = (bf16[3,64,256]{2,1,0:T(8,128)(2,1)S(1)}, bf16[3,64,256]{2,1,0:T(8,128)(2,1)S(1)}, u32[]{:S(2)}, u32[]{:S(2)}) collective-permute-start(bf16[3,64,256]{2,1,0:T(8,128)(2,1)S(1)} %get-tuple-element.55), channel_id=1, source_target_pairs={{0,16},{1,17},{2,18},{3,19},{4,20},{5,21},{6,22},{7,23},{8,24},{9,... | collective-permute-start | bytes 294920 | tf_op jit(solution)/shard_map/ppermute | solution.py:24
  53.8 2.5 %collective-permute-start.20 = (bf16[3,64,256]{2,1,0:T(8,128)(2,1)S(1)}, bf16[3,64,256]{2,1,0:T(8,128)(2,1)S(1)}, u32[]{:S(2)}, u32[]{:S(2)}) collective-permute-start(bf16[3,64,256]{2,1,0:T(8,128)(2,1)S(1)} %get-tuple-element.56), channel_id=1, source_target_pairs={{0,24},{1,25},{2,26},{3,27},{4,28},{5,29},{6,30},{7,31},{8,16},{9,... | collective-permute-start | bytes 294920 | tf_op jit(solution)/shard_map/ppermute | solution.py:24
  56.4 3.9 %all-to-all-done.1 = bf16[4,2,3,64,256]{4,3,2,1,0:T(8,128)(2,1)S(1)} async-done(((bf16[4,2,3,64,256]{4,3,2,1,0:T(8,128)(2,1)}), bf16[4,2,3,64,256]{4,3,2,1,0:T(8,128)(2,1)S(1)}, u32[]{:S(2)}, u32[]{:S(2)}) %all-to-all-start.1) | async-done | bytes 786464 | tf_op jit(solution)/shard_map/all_to_all | solution.py:222
  60.3 0.1 fusion.7
  60.3 1.7 %collective-permute-start.22 = (bf16[3,64,256]{2,1,0:T(8,128)(2,1)S(1)}, bf16[3,64,256]{2,1,0:T(8,128)(2,1)S(1)}, u32[]{:S(2)}, u32[]{:S(2)}) collective-permute-start(bf16[3,64,256]{2,1,0:T(8,128)(2,1)S(1)} %fusion.7), channel_id=1, source_target_pairs={{0,8},{1,9},{2,10},{3,11},{4,12},{5,13},{6,14},{7,15},{8,0},{9,1},... | collective-permute-start | bytes 294920 | tf_op jit(solution)/shard_map/ppermute | solution.py:24
  62.1 4.0 %collective-permute-done.22 = bf16[3,64,256]{2,1,0:T(8,128)(2,1)S(1)} collective-permute-done((bf16[3,64,256]{2,1,0:T(8,128)(2,1)S(1)}, bf16[3,64,256]{2,1,0:T(8,128)(2,1)S(1)}, u32[]{:S(2)}, u32[]{:S(2)}) %collective-permute-start.22) | collective-permute-done | bytes 98336 | tf_op jit(solution)/shard_map/ppermute | solution.py:24
  66.1 0.3 fusion.10
  66.4 5.3 %collective-permute-start.35 = (bf16[3,64,256]{2,1,0:T(8,128)(2,1)S(1)}, bf16[3,64,256]{2,1,0:T(8,128)(2,1)S(1)}, u32[]{:S(2)}, u32[]{:S(2)}) collective-permute-start(bf16[3,64,256]{2,1,0:T(8,128)(2,1)S(1)} %get-tuple-element.52.refs_0_), channel_id=1, source_target_pairs={{0,24},{1,25},{2,26},{3,27},{4,28},{5,29},{6,30},{7,31},{8,16},{9,... | collective-permute-start | bytes 294920 | tf_op jit(solution)/shard_map/ppermute | solution.py:24
  71.7 0.6 collective-permute-start.27
  72.3 1.6 %collective-permute-start.25 = (bf16[3,64,256]{2,1,0:T(8,128)(2,1)S(1)}, bf16[3,64,256]{2,1,0:T(8,128)(2,1)S(1)}, u32[]{:S(2)}, u32[]{:S(2)}) collective-permute-start(bf16[3,64,256]{2,1,0:T(8,128)(2,1)S(1)} %get-tuple-element.52.refs_0_), channel_id=1, source_target_pairs={{0,4},{1,5},{2,6},{3,7},{4,0},{5,1},{6,2},{7,3},{8,12},{9,13},{10,... | collective-permute-start | bytes 294920 | tf_op jit(solution)/shard_map/ppermute | solution.py:24
  73.9 0.1 fusion.8
  74.0 3.4 %collective-permute-done.31.refs_8_ = bf16[3,64,256]{2,1,0:T(8,128)(2,1)S(1)} collective-permute-done((bf16[3,64,256]{2,1,0:T(8,128)(2,1)S(1)}, bf16[3,64,256]{2,1,0:T(8,128)(2,1)S(1)}, u32[]{:S(2)}, u32[]{:S(2)}) %collective-permute-start.31) | collective-permute-done | bytes 98336 | tf_op jit(solution)/shard_map/ppermute | solution.py:24
  77.3 0.0 collective-permute-done.27.refs_4_
  77.4 1.4 %collective-permute-done.24.refs_1_ = bf16[3,64,256]{2,1,0:T(8,128)(2,1)S(1)} collective-permute-done((bf16[3,64,256]{2,1,0:T(8,128)(2,1)S(1)}, bf16[3,64,256]{2,1,0:T(8,128)(2,1)S(1)}, u32[]{:S(2)}, u32[]{:S(2)}) %collective-permute-start.24) | collective-permute-done | bytes 98336 | tf_op jit(solution)/shard_map/ppermute | solution.py:24
  78.8 0.2 collective-permute-start.33
  79.0 1.2 %collective-permute-start.32 = (bf16[3,64,256]{2,1,0:T(8,128)(2,1)S(1)}, bf16[3,64,256]{2,1,0:T(8,128)(2,1)S(1)}, u32[]{:S(2)}, u32[]{:S(2)}) collective-permute-start(bf16[3,64,256]{2,1,0:T(8,128)(2,1)S(1)} %collective-permute-done.31.refs_8_), channel_id=1, source_target_pairs={{0,2},{1,3},{2,0},{3,1},{4,6},{5,7},{6,4},{7,5},{8,10},{9,11},{10,... | collective-permute-start | bytes 294920 | tf_op jit(solution)/shard_map/ppermute | solution.py:24
  80.2 0.6 collective-permute-start.26
  80.8 1.4 %collective-permute-start.29 = (bf16[3,64,256]{2,1,0:T(8,128)(2,1)S(1)}, bf16[3,64,256]{2,1,0:T(8,128)(2,1)S(1)}, u32[]{:S(2)}, u32[]{:S(2)}) collective-permute-start(bf16[3,64,256]{2,1,0:T(8,128)(2,1)S(1)} %collective-permute-done.27.refs_4_), channel_id=1, source_target_pairs={{0,4},{1,5},{2,6},{3,7},{4,0},{5,1},{6,2},{7,3},{8,12},{9,13},{10,... | collective-permute-start | bytes 294920 | tf_op jit(solution)/shard_map/ppermute | solution.py:24
  82.2 0.8 collective-permute-start.28
  83.1 3.3 %collective-permute-done.29.refs_6_ = bf16[3,64,256]{2,1,0:T(8,128)(2,1)S(1)} collective-permute-done((bf16[3,64,256]{2,1,0:T(8,128)(2,1)S(1)}, bf16[3,64,256]{2,1,0:T(8,128)(2,1)S(1)}, u32[]{:S(2)}, u32[]{:S(2)}) %collective-permute-start.29) | collective-permute-done | bytes 98336 | tf_op jit(solution)/shard_map/ppermute | solution.py:24
  86.4 0.5 collective-permute-done.28.refs_5_
  86.9 2.1 %collective-permute-start.38 = (bf16[3,64,256]{2,1,0:T(8,128)(2,1)S(1)}, bf16[3,64,256]{2,1,0:T(8,128)(2,1)S(1)}, u32[]{:S(2)}, u32[]{:S(2)}) collective-permute-start(bf16[3,64,256]{2,1,0:T(8,128)(2,1)S(1)} %collective-permute-done.35.refs_12_), channel_id=1, source_target_pairs={{0,6},{1,7},{2,4},{3,5},{4,2},{5,3},{6,0},{7,1},{8,14},{9,15},{10,... | collective-permute-start | bytes 294920 | tf_op jit(solution)/shard_map/ppermute | solution.py:24
  88.9 0.2 collective-permute-start.37
  89.1 1.2 %collective-permute-start.36 = (bf16[3,64,256]{2,1,0:T(8,128)(2,1)S(1)}, bf16[3,64,256]{2,1,0:T(8,128)(2,1)S(1)}, u32[]{:S(2)}, u32[]{:S(2)}) collective-permute-start(bf16[3,64,256]{2,1,0:T(8,128)(2,1)S(1)} %collective-permute-done.35.refs_12_), channel_id=1, source_target_pairs={{0,2},{1,3},{2,0},{3,1},{4,6},{5,7},{6,4},{7,5},{8,10},{9,11},{10,... | collective-permute-start | bytes 294920 | tf_op jit(solution)/shard_map/ppermute | solution.py:24
  90.4 0.8 collective-permute-start.30
  91.1 1.8 %collective-permute-start.34 = (bf16[3,64,256]{2,1,0:T(8,128)(2,1)S(1)}, bf16[3,64,256]{2,1,0:T(8,128)(2,1)S(1)}, u32[]{:S(2)}, u32[]{:S(2)}) collective-permute-start(bf16[3,64,256]{2,1,0:T(8,128)(2,1)S(1)} %collective-permute-done.32.refs_9_), channel_id=1, source_target_pairs={{0,4},{1,5},{2,6},{3,7},{4,0},{5,1},{6,2},{7,3},{8,12},{9,13},{10,... | collective-permute-start | bytes 294920 | tf_op jit(solution)/shard_map/ppermute | solution.py:24
  93.0 1.9 %collective-permute-done.30.refs_7_ = bf16[3,64,256]{2,1,0:T(8,128)(2,1)S(1)} collective-permute-done((bf16[3,64,256]{2,1,0:T(8,128)(2,1)S(1)}, bf16[3,64,256]{2,1,0:T(8,128)(2,1)S(1)}, u32[]{:S(2)}, u32[]{:S(2)}) %collective-permute-start.30) | collective-permute-done | bytes 98336 | tf_op jit(solution)/shard_map/ppermute | solution.py:24
  95.0 0.8 collective-permute-done.34.refs_11_
  95.8 1.8 %expert_outputs.1 = (bf16[256,1024]{1,0:T(8,128)(2,1)S(1)}, bf16[256,1024]{1,0:T(8,128)(2,1)S(1)}, s32[1]{0:T(128)}) custom-call(s32[32]{0:T(128)S(1)} %copy-done.4, bf16[3,64,256]{2,1,0:T(8,128)(2,1)S(1)} %get-tuple-element.52.refs_0_, bf16[3,64,256]{2,1,0:T(8,128)(2,1)S(1)} %collective-permute-done.24.refs_1_, ...), custom_call_target="tpu_custom_call" | custom-call | flops 805306368 | bytes 3670016 | tf_op jit(solution)/shard_map/expert_outputs/pallas_call | solution.py:170
  97.6 0.1 collective-permute-start.39
  97.8 0.8 slice_bitcast_fusion
  99.2 0.4 collective-permute-done.39
  99.6 0.8 select_bitcast_fusion
  (49 shorter events, 0.3 us)
Async XLA Ops:
  0.6 3.5 %collective-permute-start.3 = (bf16[256,1024]{1,0:T(8,128)(2,1)}, bf16[256,1024]{1,0:T(8,128)(2,1)S(1)}, u32[]{:S(2)}, u32[]{:S(2)}) collective-permute-start(bf16[256,1024]{1,0:T(8,128)(2,1)} %bitcast.41), channel_id=1, source_target_pairs={{0,1},{1,0},{2,3},{3,2},{4,5},{5,4},{6,7},{7,6},{8,9},{9,8},{10,11... | collective-permute-start | bytes 1572872 | tf_op jit(solution)/shard_map/ppermute | solution.py:24
  1.1 3.0 %collective-permute-start.4 = (bf16[256,1024]{1,0:T(8,128)(2,1)}, bf16[256,1024]{1,0:T(8,128)(2,1)S(1)}, u32[]{:S(2)}, u32[]{:S(2)}) collective-permute-start(bf16[256,1024]{1,0:T(8,128)(2,1)} %bitcast.44), channel_id=1, source_target_pairs={{0,1},{1,0},{2,3},{3,2},{4,5},{5,4},{6,7},{7,6},{8,9},{9,8},{10,11... | collective-permute-start | bytes 1572872 | tf_op jit(solution)/shard_map/ppermute | solution.py:24
  1.2 4.2 %collective-permute-start.1 = (bf16[256,1024]{1,0:T(8,128)(2,1)}, bf16[256,1024]{1,0:T(8,128)(2,1)S(1)}, u32[]{:S(2)}, u32[]{:S(2)}) collective-permute-start(bf16[256,1024]{1,0:T(8,128)(2,1)} %bitcast.47), channel_id=1, source_target_pairs={{0,1},{1,0},{2,3},{3,2},{4,5},{5,4},{6,7},{7,6},{8,9},{9,8},{10,11... | collective-permute-start | bytes 1572872 | tf_op jit(solution)/shard_map/ppermute | solution.py:24
  1.7 1.1 %copy-start.5 = (f32[2,3,32,256]{3,2,1,0:T(8,128)S(1)}, f32[2,3,32,256]{3,2,1,0:T(8,128)}, u32[]{:S(2)}) copy-start(f32[2,3,32,256]{3,2,1,0:T(8,128)} %param.11) | copy-start | bytes 589828
  1.7 2.4 %copy-start.1 = (bf16[1,256,1024]{2,1,0:T(8,128)(2,1)S(1)}, bf16[1,256,1024]{2,1,0:T(8,128)(2,1)}, u32[]{:S(2)}) copy-start(bf16[1,256,1024]{2,1,0:T(8,128)(2,1)} %param.13) | copy-start | bytes 1572868
  2.8 1.3 %copy-start = (bf16[1,256,1024]{2,1,0:T(8,128)(2,1)S(1)}, bf16[1,256,1024]{2,1,0:T(8,128)(2,1)}, u32[]{:S(2)}) copy-start(bf16[1,256,1024]{2,1,0:T(8,128)(2,1)} %param.12) | copy-start | bytes 1572868
  3.6 1.8 %collective-permute-start = (f32[3,3,32,256]{3,2,1,0:T(8,128)}, f32[3,3,32,256]{3,2,1,0:T(8,128)S(1)}, u32[]{:S(2)}, u32[]{:S(2)}) collective-permute-start(f32[3,3,32,256]{3,2,1,0:T(8,128)} %pad_maximum_fusion.1), channel_id=1, source_target_pairs={{0,1},{1,0},{2,3},{3,2},{4,5},{5,4},{6,7},{7,6},{8,9},{9,8},{10,11... | collective-permute-start | bytes 884744 | tf_op jit(solution)/shard_map/ppermute | solution.py:24
  3.7 1.7 %collective-permute-start.2 = (s32[1]{0:T(128)}, s32[1]{0:T(128)}, u32[]{:S(2)}, u32[]{:S(2)}) collective-permute-start(s32[1]{0:T(128)} %param.17), channel_id=1, source_target_pairs={{0,1},{1,0},{2,3},{3,2},{4,5},{5,4},{6,7},{7,6},{8,9},{9,8},{10,11... | collective-permute-start | bytes 20 | tf_op jit(solution)/shard_map/ppermute | solution.py:24
  5.4 27.6 %copy-start.3 = (s32[32]{0:T(128)S(1)}, s32[32]{0:T(128)}, u32[]{:S(2)}) copy-start(s32[32]{0:T(128)} %slots.2) | copy-start | bytes 388
  5.5 8.6 %collective-permute-start.8 = (bf16[3,64,256]{2,1,0:T(8,128)(2,1)S(1)}, bf16[3,64,256]{2,1,0:T(8,128)(2,1)S(1)}, u32[]{:S(2)}, u32[]{:S(2)}) collective-permute-start(bf16[3,64,256]{2,1,0:T(8,128)(2,1)S(1)} %fusion.4.refs_0_), channel_id=1, source_target_pairs={{0,8},{1,9},{2,10},{3,11},{4,12},{5,13},{6,14},{7,15},{8,0},{9,1},... | collective-permute-start | bytes 294920 | tf_op jit(solution)/shard_map/ppermute | solution.py:24
  8.3 7.8 %collective-permute-start.12 = (bf16[3,64,256]{2,1,0:T(8,128)(2,1)S(1)}, bf16[3,64,256]{2,1,0:T(8,128)(2,1)S(1)}, u32[]{:S(2)}, u32[]{:S(2)}) collective-permute-start(bf16[3,64,256]{2,1,0:T(8,128)(2,1)S(1)} %fusion.4.refs_0_), channel_id=1, source_target_pairs={{0,16},{1,17},{2,18},{3,19},{4,20},{5,21},{6,22},{7,23},{8,24},{9,... | collective-permute-start | bytes 294920 | tf_op jit(solution)/shard_map/ppermute | solution.py:24
  10.9 6.7 %collective-permute-start.6 = (bf16[3,64,256]{2,1,0:T(8,128)(2,1)S(1)}, bf16[3,64,256]{2,1,0:T(8,128)(2,1)S(1)}, u32[]{:S(2)}, u32[]{:S(2)}) collective-permute-start(bf16[3,64,256]{2,1,0:T(8,128)(2,1)S(1)} %fusion.4.refs_0_), channel_id=1, source_target_pairs={{0,4},{1,5},{2,6},{3,7},{4,0},{5,1},{6,2},{7,3},{8,12},{9,13},{10,... | collective-permute-start | bytes 294920 | tf_op jit(solution)/shard_map/ppermute | solution.py:24
  12.4 5.6 %collective-permute-start.5 = (bf16[3,64,256]{2,1,0:T(8,128)(2,1)S(1)}, bf16[3,64,256]{2,1,0:T(8,128)(2,1)S(1)}, u32[]{:S(2)}, u32[]{:S(2)}) collective-permute-start(bf16[3,64,256]{2,1,0:T(8,128)(2,1)S(1)} %fusion.4.refs_0_), channel_id=1, source_target_pairs={{0,2},{1,3},{2,0},{3,1},{4,6},{5,7},{6,4},{7,5},{8,10},{9,11},{10,... | collective-permute-start | bytes 294920 | tf_op jit(solution)/shard_map/ppermute | solution.py:24
  13.9 7.9 %collective-permute-start.16 = (bf16[3,64,256]{2,1,0:T(8,128)(2,1)S(1)}, bf16[3,64,256]{2,1,0:T(8,128)(2,1)S(1)}, u32[]{:S(2)}, u32[]{:S(2)}) collective-permute-start(bf16[3,64,256]{2,1,0:T(8,128)(2,1)S(1)} %fusion.4.refs_0_), channel_id=1, source_target_pairs={{0,24},{1,25},{2,26},{3,27},{4,28},{5,29},{6,30},{7,31},{8,16},{9,... | collective-permute-start | bytes 294920 | tf_op jit(solution)/shard_map/ppermute | solution.py:24
  14.1 7.8 %collective-permute-start.10 = (bf16[3,64,256]{2,1,0:T(8,128)(2,1)S(1)}, bf16[3,64,256]{2,1,0:T(8,128)(2,1)S(1)}, u32[]{:S(2)}, u32[]{:S(2)}) collective-permute-start(bf16[3,64,256]{2,1,0:T(8,128)(2,1)S(1)} %collective-permute-done.8.refs_4_), channel_id=1, source_target_pairs={{0,4},{1,5},{2,6},{3,7},{4,0},{5,1},{6,2},{7,3},{8,12},{9,13},{10,... | collective-permute-start | bytes 294920 | tf_op jit(solution)/shard_map/ppermute | solution.py:24
  16.0 5.8 %collective-permute-start.9 = (bf16[3,64,256]{2,1,0:T(8,128)(2,1)S(1)}, bf16[3,64,256]{2,1,0:T(8,128)(2,1)S(1)}, u32[]{:S(2)}, u32[]{:S(2)}) collective-permute-start(bf16[3,64,256]{2,1,0:T(8,128)(2,1)S(1)} %collective-permute-done.8.refs_4_), channel_id=1, source_target_pairs={{0,2},{1,3},{2,0},{3,1},{4,6},{5,7},{6,4},{7,5},{8,10},{9,11},{10,... | collective-permute-start | bytes 294920 | tf_op jit(solution)/shard_map/ppermute | solution.py:24
  18.0 8.4 %collective-permute-start.14 = (bf16[3,64,256]{2,1,0:T(8,128)(2,1)S(1)}, bf16[3,64,256]{2,1,0:T(8,128)(2,1)S(1)}, u32[]{:S(2)}, u32[]{:S(2)}) collective-permute-start(bf16[3,64,256]{2,1,0:T(8,128)(2,1)S(1)} %collective-permute-done.12.refs_8_), channel_id=1, source_target_pairs={{0,4},{1,5},{2,6},{3,7},{4,0},{5,1},{6,2},{7,3},{8,12},{9,13},{10,... | collective-permute-start | bytes 294920 | tf_op jit(solution)/shard_map/ppermute | solution.py:24
  21.7 5.3 %collective-permute-start.13 = (bf16[3,64,256]{2,1,0:T(8,128)(2,1)S(1)}, bf16[3,64,256]{2,1,0:T(8,128)(2,1)S(1)}, u32[]{:S(2)}, u32[]{:S(2)}) collective-permute-start(bf16[3,64,256]{2,1,0:T(8,128)(2,1)S(1)} %collective-permute-done.12.refs_8_), channel_id=1, source_target_pairs={{0,2},{1,3},{2,0},{3,1},{4,6},{5,7},{6,4},{7,5},{8,10},{9,11},{10,... | collective-permute-start | bytes 294920 | tf_op jit(solution)/shard_map/ppermute | solution.py:24
  21.8 6.7 %collective-permute-start.7 = (bf16[3,64,256]{2,1,0:T(8,128)(2,1)S(1)}, bf16[3,64,256]{2,1,0:T(8,128)(2,1)S(1)}, u32[]{:S(2)}, u32[]{:S(2)}) collective-permute-start(bf16[3,64,256]{2,1,0:T(8,128)(2,1)S(1)} %collective-permute-done.5.refs_1_), channel_id=1, source_target_pairs={{0,4},{1,5},{2,6},{3,7},{4,0},{5,1},{6,2},{7,3},{8,12},{9,13},{10,... | collective-permute-start | bytes 294920 | tf_op jit(solution)/shard_map/ppermute | solution.py:24
  21.9 10.2 %collective-permute-start.19 = (bf16[3,64,256]{2,1,0:T(8,128)(2,1)S(1)}, bf16[3,64,256]{2,1,0:T(8,128)(2,1)S(1)}, u32[]{:S(2)}, u32[]{:S(2)}) collective-permute-start(bf16[3,64,256]{2,1,0:T(8,128)(2,1)S(1)} %collective-permute-done.16.refs_12_), channel_id=1, source_target_pairs={{0,6},{1,7},{2,4},{3,5},{4,2},{5,3},{6,0},{7,1},{8,14},{9,15},{10,... | collective-permute-start | bytes 294920 | tf_op jit(solution)/shard_map/ppermute | solution.py:24
  26.4 5.7 %collective-permute-start.18 = (bf16[3,64,256]{2,1,0:T(8,128)(2,1)S(1)}, bf16[3,64,256]{2,1,0:T(8,128)(2,1)S(1)}, u32[]{:S(2)}, u32[]{:S(2)}) collective-permute-start(bf16[3,64,256]{2,1,0:T(8,128)(2,1)S(1)} %collective-permute-done.16.refs_12_), channel_id=1, source_target_pairs={{0,4},{1,5},{2,6},{3,7},{4,0},{5,1},{6,2},{7,3},{8,12},{9,13},{10,... | collective-permute-start | bytes 294920 | tf_op jit(solution)/shard_map/ppermute | solution.py:24
  26.4 5.7 %collective-permute-start.17 = (bf16[3,64,256]{2,1,0:T(8,128)(2,1)S(1)}, bf16[3,64,256]{2,1,0:T(8,128)(2,1)S(1)}, u32[]{:S(2)}, u32[]{:S(2)}) collective-permute-start(bf16[3,64,256]{2,1,0:T(8,128)(2,1)S(1)} %collective-permute-done.16.refs_12_), channel_id=1, source_target_pairs={{0,2},{1,3},{2,0},{3,1},{4,6},{5,7},{6,4},{7,5},{8,10},{9,11},{10,... | collective-permute-start | bytes 294920 | tf_op jit(solution)/shard_map/ppermute | solution.py:24
  27.0 5.1 %collective-permute-start.11 = (bf16[3,64,256]{2,1,0:T(8,128)(2,1)S(1)}, bf16[3,64,256]{2,1,0:T(8,128)(2,1)S(1)}, u32[]{:S(2)}, u32[]{:S(2)}) collective-permute-start(bf16[3,64,256]{2,1,0:T(8,128)(2,1)S(1)} %collective-permute-done.10.refs_6_), channel_id=1, source_target_pairs={{0,2},{1,3},{2,0},{3,1},{4,6},{5,7},{6,4},{7,5},{8,10},{9,11},{10,... | collective-permute-start | bytes 294920 | tf_op jit(solution)/shard_map/ppermute | solution.py:24
  28.5 4.6 %collective-permute-start.15 = (bf16[3,64,256]{2,1,0:T(8,128)(2,1)S(1)}, bf16[3,64,256]{2,1,0:T(8,128)(2,1)S(1)}, u32[]{:S(2)}, u32[]{:S(2)}) collective-permute-start(bf16[3,64,256]{2,1,0:T(8,128)(2,1)S(1)} %collective-permute-done.13.refs_9_), channel_id=1, source_target_pairs={{0,4},{1,5},{2,6},{3,7},{4,0},{5,1},{6,2},{7,3},{8,12},{9,13},{10,... | collective-permute-start | bytes 294920 | tf_op jit(solution)/shard_map/ppermute | solution.py:24
  48.8 11.5 %all-to-all-start.1 = ((bf16[4,2,3,64,256]{4,3,2,1,0:T(8,128)(2,1)}), bf16[4,2,3,64,256]{4,3,2,1,0:T(8,128)(2,1)S(1)}, u32[]{:S(2)}, u32[]{:S(2)}) async-start(bf16[4,2,3,64,256]{4,3,2,1,0:T(8,128)(2,1)} %get-tuple-element.42), calls=%async_computation.1 | async-start | bytes 1572864 | tf_op jit(solution)/shard_map/all_to_all | solution.py:222
  52.3 9.8 %collective-permute-start.21 = (bf16[3,64,256]{2,1,0:T(8,128)(2,1)S(1)}, bf16[3,64,256]{2,1,0:T(8,128)(2,1)S(1)}, u32[]{:S(2)}, u32[]{:S(2)}) collective-permute-start(bf16[3,64,256]{2,1,0:T(8,128)(2,1)S(1)} %get-tuple-element.55), channel_id=1, source_target_pairs={{0,16},{1,17},{2,18},{3,19},{4,20},{5,21},{6,22},{7,23},{8,24},{9,... | collective-permute-start | bytes 294920 | tf_op jit(solution)/shard_map/ppermute | solution.py:24
  53.8 8.3 %collective-permute-start.20 = (bf16[3,64,256]{2,1,0:T(8,128)(2,1)S(1)}, bf16[3,64,256]{2,1,0:T(8,128)(2,1)S(1)}, u32[]{:S(2)}, u32[]{:S(2)}) collective-permute-start(bf16[3,64,256]{2,1,0:T(8,128)(2,1)S(1)} %get-tuple-element.56), channel_id=1, source_target_pairs={{0,24},{1,25},{2,26},{3,27},{4,28},{5,29},{6,30},{7,31},{8,16},{9,... | collective-permute-start | bytes 294920 | tf_op jit(solution)/shard_map/ppermute | solution.py:24
  60.3 5.8 %collective-permute-start.22 = (bf16[3,64,256]{2,1,0:T(8,128)(2,1)S(1)}, bf16[3,64,256]{2,1,0:T(8,128)(2,1)S(1)}, u32[]{:S(2)}, u32[]{:S(2)}) collective-permute-start(bf16[3,64,256]{2,1,0:T(8,128)(2,1)S(1)} %fusion.7), channel_id=1, source_target_pairs={{0,8},{1,9},{2,10},{3,11},{4,12},{5,13},{6,14},{7,15},{8,0},{9,1},... | collective-permute-start | bytes 294920 | tf_op jit(solution)/shard_map/ppermute | solution.py:24
  66.4 15.8 %collective-permute-start.35 = (bf16[3,64,256]{2,1,0:T(8,128)(2,1)S(1)}, bf16[3,64,256]{2,1,0:T(8,128)(2,1)S(1)}, u32[]{:S(2)}, u32[]{:S(2)}) collective-permute-start(bf16[3,64,256]{2,1,0:T(8,128)(2,1)S(1)} %get-tuple-element.52.refs_0_), channel_id=1, source_target_pairs={{0,24},{1,25},{2,26},{3,27},{4,28},{5,29},{6,30},{7,31},{8,16},{9,... | collective-permute-start | bytes 294920 | tf_op jit(solution)/shard_map/ppermute | solution.py:24
  71.7 5.6 %collective-permute-start.31 = (bf16[3,64,256]{2,1,0:T(8,128)(2,1)S(1)}, bf16[3,64,256]{2,1,0:T(8,128)(2,1)S(1)}, u32[]{:S(2)}, u32[]{:S(2)}) collective-permute-start(bf16[3,64,256]{2,1,0:T(8,128)(2,1)S(1)} %get-tuple-element.52.refs_0_), channel_id=1, source_target_pairs={{0,16},{1,17},{2,18},{3,19},{4,20},{5,21},{6,22},{7,23},{8,24},{9,... | collective-permute-start | bytes 294920 | tf_op jit(solution)/shard_map/ppermute | solution.py:24
  71.7 5.7 %collective-permute-start.27 = (bf16[3,64,256]{2,1,0:T(8,128)(2,1)S(1)}, bf16[3,64,256]{2,1,0:T(8,128)(2,1)S(1)}, u32[]{:S(2)}, u32[]{:S(2)}) collective-permute-start(bf16[3,64,256]{2,1,0:T(8,128)(2,1)S(1)} %get-tuple-element.52.refs_0_), channel_id=1, source_target_pairs={{0,8},{1,9},{2,10},{3,11},{4,12},{5,13},{6,14},{7,15},{8,0},{9,1},... | collective-permute-start | bytes 294920 | tf_op jit(solution)/shard_map/ppermute | solution.py:24
  72.3 5.0 %collective-permute-start.25 = (bf16[3,64,256]{2,1,0:T(8,128)(2,1)S(1)}, bf16[3,64,256]{2,1,0:T(8,128)(2,1)S(1)}, u32[]{:S(2)}, u32[]{:S(2)}) collective-permute-start(bf16[3,64,256]{2,1,0:T(8,128)(2,1)S(1)} %get-tuple-element.52.refs_0_), channel_id=1, source_target_pairs={{0,4},{1,5},{2,6},{3,7},{4,0},{5,1},{6,2},{7,3},{8,12},{9,13},{10,... | collective-permute-start | bytes 294920 | tf_op jit(solution)/shard_map/ppermute | solution.py:24
  73.9 4.9 %collective-permute-start.24 = (bf16[3,64,256]{2,1,0:T(8,128)(2,1)S(1)}, bf16[3,64,256]{2,1,0:T(8,128)(2,1)S(1)}, u32[]{:S(2)}, u32[]{:S(2)}) collective-permute-start(bf16[3,64,256]{2,1,0:T(8,128)(2,1)S(1)} %get-tuple-element.52.refs_0_), channel_id=1, source_target_pairs={{0,2},{1,3},{2,0},{3,1},{4,6},{5,7},{6,4},{7,5},{8,10},{9,11},{10,... | collective-permute-start | bytes 294920 | tf_op jit(solution)/shard_map/ppermute | solution.py:24
  78.8 10.3 %collective-permute-start.33 = (bf16[3,64,256]{2,1,0:T(8,128)(2,1)S(1)}, bf16[3,64,256]{2,1,0:T(8,128)(2,1)S(1)}, u32[]{:S(2)}, u32[]{:S(2)}) collective-permute-start(bf16[3,64,256]{2,1,0:T(8,128)(2,1)S(1)} %collective-permute-done.31.refs_8_), channel_id=1, source_target_pairs={{0,4},{1,5},{2,6},{3,7},{4,0},{5,1},{6,2},{7,3},{8,12},{9,13},{10,... | collective-permute-start | bytes 294920 | tf_op jit(solution)/shard_map/ppermute | solution.py:24
  79.0 11.4 %collective-permute-start.32 = (bf16[3,64,256]{2,1,0:T(8,128)(2,1)S(1)}, bf16[3,64,256]{2,1,0:T(8,128)(2,1)S(1)}, u32[]{:S(2)}, u32[]{:S(2)}) collective-permute-start(bf16[3,64,256]{2,1,0:T(8,128)(2,1)S(1)} %collective-permute-done.31.refs_8_), channel_id=1, source_target_pairs={{0,2},{1,3},{2,0},{3,1},{4,6},{5,7},{6,4},{7,5},{8,10},{9,11},{10,... | collective-permute-start | bytes 294920 | tf_op jit(solution)/shard_map/ppermute | solution.py:24
  80.2 10.9 %collective-permute-start.26 = (bf16[3,64,256]{2,1,0:T(8,128)(2,1)S(1)}, bf16[3,64,256]{2,1,0:T(8,128)(2,1)S(1)}, u32[]{:S(2)}, u32[]{:S(2)}) collective-permute-start(bf16[3,64,256]{2,1,0:T(8,128)(2,1)S(1)} %collective-permute-done.24.refs_1_), channel_id=1, source_target_pairs={{0,4},{1,5},{2,6},{3,7},{4,0},{5,1},{6,2},{7,3},{8,12},{9,13},{10,... | collective-permute-start | bytes 294920 | tf_op jit(solution)/shard_map/ppermute | solution.py:24
  80.8 5.6 %collective-permute-start.29 = (bf16[3,64,256]{2,1,0:T(8,128)(2,1)S(1)}, bf16[3,64,256]{2,1,0:T(8,128)(2,1)S(1)}, u32[]{:S(2)}, u32[]{:S(2)}) collective-permute-start(bf16[3,64,256]{2,1,0:T(8,128)(2,1)S(1)} %collective-permute-done.27.refs_4_), channel_id=1, source_target_pairs={{0,4},{1,5},{2,6},{3,7},{4,0},{5,1},{6,2},{7,3},{8,12},{9,13},{10,... | collective-permute-start | bytes 294920 | tf_op jit(solution)/shard_map/ppermute | solution.py:24
  82.2 4.6 %collective-permute-start.28 = (bf16[3,64,256]{2,1,0:T(8,128)(2,1)S(1)}, bf16[3,64,256]{2,1,0:T(8,128)(2,1)S(1)}, u32[]{:S(2)}, u32[]{:S(2)}) collective-permute-start(bf16[3,64,256]{2,1,0:T(8,128)(2,1)S(1)} %collective-permute-done.27.refs_4_), channel_id=1, source_target_pairs={{0,2},{1,3},{2,0},{3,1},{4,6},{5,7},{6,4},{7,5},{8,10},{9,11},{10,... | collective-permute-start | bytes 294920 | tf_op jit(solution)/shard_map/ppermute | solution.py:24
  83.1 12.7 %copy-start.2 = (bf16[1,256,1024]{2,1,0:T(8,128)(2,1)S(1)}, bf16[1,256,1024]{2,1,0:T(8,128)(2,1)}, u32[]{:S(2)}) copy-start(bf16[1,256,1024]{2,1,0:T(8,128)(2,1)} %param.14) | copy-start | bytes 1572868
  86.9 8.1 %collective-permute-start.38 = (bf16[3,64,256]{2,1,0:T(8,128)(2,1)S(1)}, bf16[3,64,256]{2,1,0:T(8,128)(2,1)S(1)}, u32[]{:S(2)}, u32[]{:S(2)}) collective-permute-start(bf16[3,64,256]{2,1,0:T(8,128)(2,1)S(1)} %collective-permute-done.35.refs_12_), channel_id=1, source_target_pairs={{0,6},{1,7},{2,4},{3,5},{4,2},{5,3},{6,0},{7,1},{8,14},{9,15},{10,... | collective-permute-start | bytes 294920 | tf_op jit(solution)/shard_map/ppermute | solution.py:24
  88.9 6.1 %collective-permute-start.37 = (bf16[3,64,256]{2,1,0:T(8,128)(2,1)S(1)}, bf16[3,64,256]{2,1,0:T(8,128)(2,1)S(1)}, u32[]{:S(2)}, u32[]{:S(2)}) collective-permute-start(bf16[3,64,256]{2,1,0:T(8,128)(2,1)S(1)} %collective-permute-done.35.refs_12_), channel_id=1, source_target_pairs={{0,4},{1,5},{2,6},{3,7},{4,0},{5,1},{6,2},{7,3},{8,12},{9,13},{10,... | collective-permute-start | bytes 294920 | tf_op jit(solution)/shard_map/ppermute | solution.py:24
  89.1 5.9 %collective-permute-start.36 = (bf16[3,64,256]{2,1,0:T(8,128)(2,1)S(1)}, bf16[3,64,256]{2,1,0:T(8,128)(2,1)S(1)}, u32[]{:S(2)}, u32[]{:S(2)}) collective-permute-start(bf16[3,64,256]{2,1,0:T(8,128)(2,1)S(1)} %collective-permute-done.35.refs_12_), channel_id=1, source_target_pairs={{0,2},{1,3},{2,0},{3,1},{4,6},{5,7},{6,4},{7,5},{8,10},{9,11},{10,... | collective-permute-start | bytes 294920 | tf_op jit(solution)/shard_map/ppermute | solution.py:24
  90.4 4.6 %collective-permute-start.30 = (bf16[3,64,256]{2,1,0:T(8,128)(2,1)S(1)}, bf16[3,64,256]{2,1,0:T(8,128)(2,1)S(1)}, u32[]{:S(2)}, u32[]{:S(2)}) collective-permute-start(bf16[3,64,256]{2,1,0:T(8,128)(2,1)S(1)} %collective-permute-done.29.refs_6_), channel_id=1, source_target_pairs={{0,2},{1,3},{2,0},{3,1},{4,6},{5,7},{6,4},{7,5},{8,10},{9,11},{10,... | collective-permute-start | bytes 294920 | tf_op jit(solution)/shard_map/ppermute | solution.py:24
  91.1 4.6 %collective-permute-start.34 = (bf16[3,64,256]{2,1,0:T(8,128)(2,1)S(1)}, bf16[3,64,256]{2,1,0:T(8,128)(2,1)S(1)}, u32[]{:S(2)}, u32[]{:S(2)}) collective-permute-start(bf16[3,64,256]{2,1,0:T(8,128)(2,1)S(1)} %collective-permute-done.32.refs_9_), channel_id=1, source_target_pairs={{0,4},{1,5},{2,6},{3,7},{4,0},{5,1},{6,2},{7,3},{8,12},{9,13},{10,... | collective-permute-start | bytes 294920 | tf_op jit(solution)/shard_map/ppermute | solution.py:24
  93.0 2.8 %copy-start.4 = (s32[32]{0:T(128)S(1)}, s32[32]{0:T(128)}, u32[]{:S(2)}) copy-start(s32[32]{0:T(128)} %slots.3) | copy-start | bytes 388
  95.0 2.7 %collective-permute-start.23 = (f32[3,3,32,256]{3,2,1,0:T(8,128)S(1)}, f32[3,3,32,256]{3,2,1,0:T(8,128)S(1)}, u32[]{:S(2)}, u32[]{:S(2)}) collective-permute-start(f32[3,3,32,256]{3,2,1,0:T(8,128)S(1)} %get-tuple-element.61), channel_id=1, source_target_pairs={{0,1},{1,0},{2,3},{3,2},{4,5},{5,4},{6,7},{7,6},{8,9},{9,8},{10,11... | collective-permute-start | bytes 884744 | tf_op jit(solution)/shard_map/ppermute | solution.py:24
  97.6 2.0 %collective-permute-start.39 = (bf16[256,1024]{1,0:T(8,128)(2,1)S(1)}, bf16[256,1024]{1,0:T(8,128)(2,1)S(1)}, u32[]{:S(2)}, u32[]{:S(2)}) collective-permute-start(bf16[256,1024]{1,0:T(8,128)(2,1)S(1)} %get-tuple-element.51), channel_id=1, source_target_pairs={{0,1},{1,0},{2,3},{3,2},{4,5},{5,4},{6,7},{7,6},{8,9},{9,8},{10,11... | collective-permute-start | bytes 1572872 | tf_op jit(solution)/shard_map/ppermute | solution.py:24

commit v9 on v6

--- a/solution.py
+++ b/solution.py
@@ -39,19 +39,21 @@
         weights[:, pl.ds(start, rows), :] = piece[...]
 
 
-def transpose_kernel(own_x, other_x, own_c, other_c, x_turned, c_turned):
+def transpose_kernel(own_x, other_x, own_c, other_c, x_turned, c_turned, x_rows, c_rows):
     chip = lax.axis_index("dev") // 2
     tokens, width = own_x.shape
     rows = 2 * width // lax.axis_size("dev")
     lanes = max(128, rows)
-    for out, pair in ((x_turned, (own_x, other_x)), (c_turned, (own_c, other_c))):
+    for out, straight, pair in ((x_turned, x_rows, (own_x, other_x)), (c_turned, c_rows, (own_c, other_c))):
         for part, ref in enumerate(pair):
+            span = slice(part * tokens, (part + 1) * tokens)
+            straight[span] = ref[...]
             for at in range(0, width, lanes):
                 turned = ref[:, at : at + lanes].T
                 for low in range(0, lanes, rows):
                     j = lax.bitwise_xor(chip, (at + low) // rows)
                     start = pl.multiple_of(j * rows, rows)
-                    out[pl.ds(start, rows), part * tokens : (part + 1) * tokens] = turned[low : low + rows]
+                    out[pl.ds(start, rows), span] = turned[low : low + rows]
 
 
 def places(outs):
@@ -80,28 +82,27 @@
 
 def backward_kernel(count, slots, own_live, other_live, *refs):
     pieces = refs[:count]
-    own_x, other_x, own_c, other_c, x_turned, c_turned = refs[count : count + 6]
-    outs = refs[count + 6 : -4]
+    x_turned, c_turned, x_rows, c_rows = refs[count : count + 4]
+    outs = refs[count + 4 : -4]
     gate_grad, up_grad, hidden_all, weights = refs[-4:]
     me_index = lax.axis_index("dev")
     core = me_index & CORE
     place_pieces(me_index // 2, pieces, weights)
-    tokens = own_x.shape[0]
-    sides = ((own_x, own_c, me_index, own_live), (other_x, other_c, me_index ^ CORE, other_live))
-    for part, (x_ref, c_ref, slot, live) in enumerate(sides):
-        span = slice(part * tokens, (part + 1) * tokens)
-        gate_pre = jnp.dot(x_ref[...], weights[0], preferred_element_type=jnp.float32)
-        up_pre = jnp.dot(x_ref[...], weights[1], preferred_element_type=jnp.float32)
-        grad_hidden = jnp.dot(c_ref[...], weights[2], preferred_element_type=jnp.float32)
-        gate_sig = jax.nn.sigmoid(gate_pre)
-        gate_act = gate_pre * gate_sig
-        alive = jnp.where(slots[slot] == core, live[0], 0)
-        keep = lax.broadcasted_iota(jnp.int32, gate_pre.shape, 0) < alive
-        grad_up = grad_hidden * gate_act
-        grad_gate = grad_hidden * up_pre * gate_sig * (1.0 + gate_pre * (1.0 - gate_sig))
-        hidden_all[span] = jnp.where(keep, gate_act * up_pre, 0.0).astype(jnp.bfloat16)
-        up_grad[span] = jnp.where(keep, grad_up, 0.0).astype(jnp.bfloat16)
-        gate_grad[span] = jnp.where(keep, grad_gate, 0.0).astype(jnp.bfloat16)
+    tokens = x_rows.shape[0] // 2
+    gate_pre = jnp.dot(x_rows[...], weights[0], preferred_element_type=jnp.float32)
+    up_pre = jnp.dot(x_rows[...], weights[1], preferred_element_type=jnp.float32)
+    grad_hidden = jnp.dot(c_rows[...], weights[2], preferred_element_type=jnp.float32)
+    gate_sig = jax.nn.sigmoid(gate_pre)
+    gate_act = gate_pre * gate_sig
+    own_alive = jnp.where(slots[me_index] == core, own_live[0], 0)
+    other_alive = jnp.where(slots[me_index ^ CORE] == core, other_live[0], 0)
+    row = lax.broadcasted_iota(jnp.int32, gate_pre.shape, 0)
+    keep = (row < own_alive) | ((row >= tokens) & (row < tokens + other_alive))
+    grad_up = grad_hidden * gate_act
+    grad_gate = grad_hidden * up_pre * gate_sig * (1.0 + gate_pre * (1.0 - gate_sig))
+    hidden_all[...] = jnp.where(keep, gate_act * up_pre, 0.0).astype(jnp.bfloat16)
+    up_grad[...] = jnp.where(keep, grad_up, 0.0).astype(jnp.bfloat16)
+    gate_grad[...] = jnp.where(keep, grad_gate, 0.0).astype(jnp.bfloat16)
     products = ((x_turned, gate_grad), (x_turned, up_grad), (c_turned, hidden_all))
     gradient_rows(0, products, outs)
 
@@ -132,25 +133,26 @@
     tokens, width = own_x.shape
     return pl.pallas_call(
         transpose_kernel,
-        out_shape=[jax.ShapeDtypeStruct((width, 2 * tokens), own_x.dtype)] * 2,
+        out_shape=[jax.ShapeDtypeStruct((width, 2 * tokens), own_x.dtype)] * 2
+        + [jax.ShapeDtypeStruct((2 * tokens, width), own_x.dtype)] * 2,
         in_specs=[VMEM] * 4,
-        out_specs=[VMEM] * 2,
+        out_specs=[VMEM] * 4,
         compiler_params=params(),
         cost_estimate=pl.CostEstimate(flops=0, bytes_accessed=16 * tokens * width, transcendentals=0),
         name="transpose_rows",
     )(own_x, other_x, own_c, other_c)
 
 
-def backward(slots, own_live, other_live, pieces, own_x, other_x, own_c, other_c, x_turned, c_turned):
+def backward(slots, own_live, other_live, pieces, x_turned, c_turned, x_rows, c_rows):
     count = len(pieces)
     kinds, rows, units = pieces[0].shape
-    tokens, width = own_x.shape
+    tokens, width = x_rows.shape[0] // 2, x_rows.shape[1]
     one = jax.ShapeDtypeStruct((kinds, rows, units), jnp.bfloat16)
     two = jax.ShapeDtypeStruct((2, kinds, rows, units), jnp.bfloat16)
     return pl.pallas_call(
         functools.partial(backward_kernel, count),
         out_shape=[one, one, two] * (count // 4),
-        in_specs=[SMEM] * 3 + [VMEM] * (count + 6),
+        in_specs=[SMEM] * 3 + [VMEM] * (count + 4),
         out_specs=[VMEM] * (3 * count // 4),
         scratch_shapes=[
             pltpu.VMEM((2 * tokens, units), jnp.bfloat16),
@@ -165,7 +167,7 @@
             transcendentals=2 * tokens * units,
         ),
         name="slot_gradients",
-    )(slots, own_live, other_live, *pieces, own_x, other_x, own_c, other_c, x_turned, c_turned)
+    )(slots, own_live, other_live, *pieces, x_turned, c_turned, x_rows, c_rows)
 
 
 def forward(slots, pieces, own_y, other_y):
@@ -209,12 +211,13 @@
     along_y[1] = hop(after(column[1], along_x[0]), Y_STEP)
     for zj in range(2, depth, 2):
         along_x[zj] = hop(after(column[zj], along_x[zj - 2], along_y[zj - 2]), X_STEP)
-        across[zj - 2] = hop(after(along_x[zj - 2], along_y[zj - 2]), Y_STEP)
         along_x[zj + 1] = hop(after(column[zj + 1], along_x[zj - 1]), X_STEP)
         along_y[zj + 1] = hop(after(column[zj + 1], along_x[zj - 1]), Y_STEP)
         along_y[zj] = hop(after(column[zj], along_y[zj - 1]), Y_STEP)
         across[zj - 1] = hop(after(along_y[zj - 1], along_x[zj]), X_STEP)
-    across[-2] = hop(after(along_x[-2], along_x[-1]), Y_STEP)
+    for zj in range(0, depth, 4):
+        two = hop(after(jnp.stack([along_x[zj], along_x[zj + 2]]), along_x[-1], along_y[zj + 1]), Y_STEP)
+        across[zj], across[zj + 2] = two[0], two[1]
     across[-1] = hop(along_y[-1], X_STEP)
     return [part for group in zip(column, along_x, along_y, across) for part in group]
 
@@ -265,29 +268,19 @@
             core == 0, jnp.concatenate([own, other], axis=-2), jnp.concatenate([other, own], axis=-2)
         )
 
-    other_x = hop(old_rows, CORE)
-    other_c = hop(old_cotangent, CORE)
-    theirs = hop(jnp.stack([partners(master), partners(first), partners(second)]), CORE)
-    other_y = hop(new_rows, CORE)
-    other_live = hop(live, CORE)
-    x_turned, c_turned = transposed(old_rows, other_x, old_cotangent, other_c)
-    theirs, other_y, other_live, x_turned, c_turned = lax.optimization_barrier(
-        (theirs, other_y, other_live, x_turned, c_turned)
-    )
+    leaving = jnp.stack([partners(master), partners(first), partners(second)])
+    theirs = hop(leaving, CORE)
+    other_x = hop(after(old_rows, leaving), CORE)
+    other_c = hop(after(old_cotangent, leaving), CORE)
+    other_y = hop(after(new_rows, leaving), CORE)
+    other_live = hop(after(live, leaving), CORE)
+    theirs, other_x, other_c, other_y, other_live = lax.optimization_barrier(
+        (theirs, other_x, other_c, other_y, other_live)
+    )
+    laid = transposed(old_rows, other_x, old_cotangent, other_c)
     master_two = both_rows(mine(master), theirs[0])
     pieces = gather_chips(master_two.astype(jnp.bfloat16))
-    grads = backward(
-        old_slots,
-        live,
-        other_live,
-        pieces,
-        old_rows,
-        other_x,
-        old_cotangent,
-        other_c,
-        x_turned,
-        c_turned,
-    )
+    grads = backward(old_slots, live, other_live, pieces, *laid)
     theirs = after(theirs, grads[0])
     first_two = both_rows(mine(first), theirs[1])
     second_two = both_rows(mine(second), theirs[2])
@@ -298,7 +291,7 @@
     updated = jnp.stack(updated)
     own_part = lax.dynamic_slice_in_dim(updated, core * local_rows, local_rows, 2)
     other_part = lax.dynamic_slice_in_dim(updated, (1 - core) * local_rows, local_rows, 2)
-    from_other = hop(other_part, CORE)
+    from_other = hop(after(other_part, new_pieces[-1]), CORE)
     state = jnp.where(
         core == 0, jnp.stack([own_part, from_other], axis=1), jnp.stack([from_other, own_part], axis=1)
     )
@@ -387,7 +380,7 @@
     blocks, kinds, local_rows, units = master.shape
     devices = lax.axis_size("dev")
     whole_tiles = local_rows % 16 == 0 and units % 128 == 0 and old_rows.shape[1] % 128 == 0
-    form = block_a_core if blocks == 2 and devices % (2 * Z_UNIT) == 0 and whole_tiles else any_shape
+    form = block_a_core if blocks == 2 and devices % (4 * Z_UNIT) == 0 and whole_tiles else any_shape
     return form(
         master,
         first_moment,

time: 90.5 us -> 102 us (1.13)
  waiting for transfers between devices: 29.2 us -> 34.1 us
  local copies, waits for them, and re-layouts: 2.31 us -> 6.16 us
  starting transfers between devices: 49.4 us -> 50.8 us
    ppermute x48 -> x46, waiting for transfers between devices: 29.2 us -> 34.1 us  [hop(): lax.ppermute(block, 'dev', [(low, low ^ mask) for low in range(count)])]
    ppermute x48 -> x46, starting transfers between devices: 49.4 us -> 50.8 us  [hop(): lax.ppermute(block, 'dev', [(low, low ^ mask) for low in range(count)])]
    unnamed x12, local copies, waits for them, and re-layouts: 0.27 us -> 1.33 us
  transfers between devices with their start and end apart: 48 -> 46, of which waited for: 28 -> 26; matrix products, arithmetic and copies ran while one was open for 3% -> 2% of each run, Pallas kernels for 3% -> 2%
where the time goes in v9:
time: 102 us
  starting transfers between devices  50.8 us (50%)
  waiting for transfers between devices  34.1 us (33%)
  Pallas kernels  6.27 us (6%)
  local copies, waits for them, and re-layouts  6.16 us (6%)
  other arithmetic  2.24 us (2%)
  between operations  2.17 us (2%)
    ppermute x46, starting transfers between devices, hop(): lax.ppermute(block, 'dev', [(low, low ^ mask) for low in range(count)])  50.8 us
    ppermute x46, waiting for transfers between devices, hop(): lax.ppermute(block, 'dev', [(low, low ^ mask) for low in range(count)])  34.1 us
    pallas_call x1, Pallas kernels, backward(): pl.pallas_call(functools.partial(backward_kernel, count), out_shape=[one,...  3.77 us
  transfers between devices with their start and end apart: 46, of which 26 were waited for; matrix products, arithmetic and copies ran while one was open for 2% of the time, Pallas kernels for 2%

profile of v9, /device:TPU:0, one launch (start us, length us, event | category | flops | bytes accessed | tf_op | source)
XLA Modules:
  0.0 101.7 jit_solution(8753664147594492675)
XLA Ops:
  0.7 1.0 %constant_dynamic-slice_fusion.3 = (f32[1,3,32,256]{3,2,1,0:T(8,128)S(1)}, f32[3,32,256]{2,1,0:T(8,128)S(1)}) fusion(f32[2,3,32,256]{3,2,1,0:T(8,128)} %param.9, s32[]{:T(128)S(6)} %select_n.52, s32[]{:T(128)S(6)} %select_n.51), kind=kLoop, calls=%fused_computation.62 | loop fusion | bytes 393224 | tf_op jit(solution)/shard_map/jit(dynamic_index_in_dim)/dynamic_slice | solution.py:264
  1.7 1.1 %dynamic-slice_bitcast_fusion.1 = (f32[3,32,256]{2,1,0:T(8,128)S(1)}, f32[1,3,32,256]{3,2,1,0:T(8,128)S(1)}, f32[1,3,32,256]{3,2,1,0:T(8,128)S(1)}, f32[3,32,256]{2,1,0:T(8,128)S(1)}) fusion(f32[2,3,32,256]{3,2,1,0:T(8,128)S(1)} %copy-done.5, s32[]{:T(128)S(6)} %select_n.51, s32[]{:T(128)S(6)} %select_n.52, f32[2,3,32,256]{3,2,1,0:T(8,128)} %param.10), kind=kLoop, calls=%fused_computation.54 | loop fusion | bytes 786440 | tf_op jit(solution)/shard_map/jit(dynamic_index_in_dim)/squeeze | solution.py:261
  2.8 0.7 pad_maximum_fusion.1
  5.0 2.4 %collective-permute-done.4.other_live = s32[1]{0:T(128)} collective-permute-done((s32[1]{0:T(128)}, s32[1]{0:T(128)}, u32[]{:S(2)}, u32[]{:S(2)}) %collective-permute-start.4) | collective-permute-done | bytes 36 | tf_op jit(solution)/shard_map/ppermute | solution.py:24
  7.4 0.9 slice_bitcast_fusion.17
  8.4 3.0 %collective-permute-start.10 = (bf16[3,64,256]{2,1,0:T(8,128)(2,1)S(1)}, bf16[3,64,256]{2,1,0:T(8,128)(2,1)S(1)}, u32[]{:S(2)}, u32[]{:S(2)}) collective-permute-start(bf16[3,64,256]{2,1,0:T(8,128)(2,1)S(1)} %fusion.17.refs_0_), channel_id=1, source_target_pairs={{0,8},{1,9},{2,10},{3,11},{4,12},{5,13},{6,14},{7,15},{8,0},{9,1},... | collective-permute-start | bytes 294920 | tf_op jit(solution)/shard_map/ppermute | solution.py:24
  11.4 2.6 %collective-permute-start.7 = (bf16[3,64,256]{2,1,0:T(8,128)(2,1)S(1)}, bf16[3,64,256]{2,1,0:T(8,128)(2,1)S(1)}, u32[]{:S(2)}, u32[]{:S(2)}) collective-permute-start(bf16[3,64,256]{2,1,0:T(8,128)(2,1)S(1)} %fusion.17.refs_0_), channel_id=1, source_target_pairs={{0,16},{1,17},{2,18},{3,19},{4,20},{5,21},{6,22},{7,23},{8,24},{9,... | collective-permute-start | bytes 294920 | tf_op jit(solution)/shard_map/ppermute | solution.py:24
  14.0 1.5 %collective-permute-start.6 = (bf16[3,64,256]{2,1,0:T(8,128)(2,1)S(1)}, bf16[3,64,256]{2,1,0:T(8,128)(2,1)S(1)}, u32[]{:S(2)}, u32[]{:S(2)}) collective-permute-start(bf16[3,64,256]{2,1,0:T(8,128)(2,1)S(1)} %fusion.17.refs_0_), channel_id=1, source_target_pairs={{0,4},{1,5},{2,6},{3,7},{4,0},{5,1},{6,2},{7,3},{8,12},{9,13},{10,... | collective-permute-start | bytes 294920 | tf_op jit(solution)/shard_map/ppermute | solution.py:24
  15.5 1.5 %collective-permute-start.5 = (bf16[3,64,256]{2,1,0:T(8,128)(2,1)S(1)}, bf16[3,64,256]{2,1,0:T(8,128)(2,1)S(1)}, u32[]{:S(2)}, u32[]{:S(2)}) collective-permute-start(bf16[3,64,256]{2,1,0:T(8,128)(2,1)S(1)} %fusion.17.refs_0_), channel_id=1, source_target_pairs={{0,2},{1,3},{2,0},{3,1},{4,6},{5,7},{6,4},{7,5},{8,10},{9,11},{10,... | collective-permute-start | bytes 294920 | tf_op jit(solution)/shard_map/ppermute | solution.py:24
  17.0 0.5 collective-permute-start.11
  17.5 1.5 %collective-permute-done.7.refs_8_ = bf16[3,64,256]{2,1,0:T(8,128)(2,1)S(1)} collective-permute-done((bf16[3,64,256]{2,1,0:T(8,128)(2,1)S(1)}, bf16[3,64,256]{2,1,0:T(8,128)(2,1)S(1)}, u32[]{:S(2)}, u32[]{:S(2)}) %collective-permute-start.7) | collective-permute-done | bytes 98336 | tf_op jit(solution)/shard_map/ppermute | solution.py:24
  19.4 1.3 %collective-permute-done.5.refs_1_ = bf16[3,64,256]{2,1,0:T(8,128)(2,1)S(1)} collective-permute-done((bf16[3,64,256]{2,1,0:T(8,128)(2,1)S(1)}, bf16[3,64,256]{2,1,0:T(8,128)(2,1)S(1)}, u32[]{:S(2)}, u32[]{:S(2)}) %collective-permute-start.5) | collective-permute-done | bytes 98336 | tf_op jit(solution)/shard_map/ppermute | solution.py:24
  20.7 1.3 %collective-permute-start.8 = (bf16[3,64,256]{2,1,0:T(8,128)(2,1)S(1)}, bf16[3,64,256]{2,1,0:T(8,128)(2,1)S(1)}, u32[]{:S(2)}, u32[]{:S(2)}) collective-permute-start(bf16[3,64,256]{2,1,0:T(8,128)(2,1)S(1)} %collective-permute-done.7.refs_8_), channel_id=1, source_target_pairs={{0,2},{1,3},{2,0},{3,1},{4,6},{5,7},{6,4},{7,5},{8,10},{9,11},{10,... | collective-permute-start | bytes 294920 | tf_op jit(solution)/shard_map/ppermute | solution.py:24
  22.5 1.1 %collective-permute-done.9.refs_12_ = bf16[3,64,256]{2,1,0:T(8,128)(2,1)S(1)} collective-permute-done((bf16[3,64,256]{2,1,0:T(8,128)(2,1)S(1)}, bf16[3,64,256]{2,1,0:T(8,128)(2,1)S(1)}, u32[]{:S(2)}, u32[]{:S(2)}) %collective-permute-start.9) | collective-permute-done | bytes 98336 | tf_op jit(solution)/shard_map/ppermute | solution.py:24
  23.6 1.5 %collective-permute-start.12 = (bf16[3,64,256]{2,1,0:T(8,128)(2,1)S(1)}, bf16[3,64,256]{2,1,0:T(8,128)(2,1)S(1)}, u32[]{:S(2)}, u32[]{:S(2)}) collective-permute-start(bf16[3,64,256]{2,1,0:T(8,128)(2,1)S(1)} %collective-permute-done.9.refs_12_), channel_id=1, source_target_pairs={{0,2},{1,3},{2,0},{3,1},{4,6},{5,7},{6,4},{7,5},{8,10},{9,11},{10,... | collective-permute-start | bytes 294920 | tf_op jit(solution)/shard_map/ppermute | solution.py:24
  25.5 1.1 %collective-permute-done.13.refs_6_ = bf16[3,64,256]{2,1,0:T(8,128)(2,1)S(1)} collective-permute-done((bf16[3,64,256]{2,1,0:T(8,128)(2,1)S(1)}, bf16[3,64,256]{2,1,0:T(8,128)(2,1)S(1)}, u32[]{:S(2)}, u32[]{:S(2)}) %collective-permute-start.13) | collective-permute-done | bytes 98336 | tf_op jit(solution)/shard_map/ppermute | solution.py:24
  26.6 1.6 %collective-permute-done.12.refs_13_ = bf16[3,64,256]{2,1,0:T(8,128)(2,1)S(1)} collective-permute-done((bf16[3,64,256]{2,1,0:T(8,128)(2,1)S(1)}, bf16[3,64,256]{2,1,0:T(8,128)(2,1)S(1)}, u32[]{:S(2)}, u32[]{:S(2)}) %collective-permute-start.12) | collective-permute-done | bytes 98336 | tf_op jit(solution)/shard_map/ppermute | solution.py:24
  28.2 1.5 %collective-permute-start.14 = (bf16[2,3,64,256]{3,2,1,0:T(8,128)(2,1)S(1)}, bf16[2,3,64,256]{3,2,1,0:T(8,128)(2,1)S(1)}, u32[]{:S(2)}, u32[]{:S(2)}) collective-permute-start(bf16[2,3,64,256]{3,2,1,0:T(8,128)(2,1)S(1)} %pad_maximum_fusion.2), channel_id=1, source_target_pairs={{0,4},{1,5},{2,6},{3,7},{4,0},{5,1},{6,2},{7,3},{8,12},{9,13},{10,... | collective-permute-start | bytes 589832 | tf_op jit(solution)/shard_map/ppermute | solution.py:24
  30.9 0.7 transpose_rows.1
  31.6 1.6 %collective-permute-start.15 = (bf16[3,64,256]{2,1,0:T(8,128)(2,1)S(1)}, bf16[3,64,256]{2,1,0:T(8,128)(2,1)S(1)}, u32[]{:S(2)}, u32[]{:S(2)}) collective-permute-start(bf16[3,64,256]{2,1,0:T(8,128)(2,1)S(1)} %collective-permute-done.13.refs_6_), channel_id=1, source_target_pairs={{0,2},{1,3},{2,0},{3,1},{4,6},{5,7},{6,4},{7,5},{8,10},{9,11},{10,... | collective-permute-start | bytes 294920 | tf_op jit(solution)/shard_map/ppermute | solution.py:24
  33.1 1.5 %collective-permute-start.16 = (bf16[3,64,256]{2,1,0:T(8,128)(2,1)S(1)}, bf16[3,64,256]{2,1,0:T(8,128)(2,1)S(1)}, u32[]{:S(2)}, u32[]{:S(2)}) collective-permute-start(bf16[3,64,256]{2,1,0:T(8,128)(2,1)S(1)} %collective-permute-done.7.refs_8_), channel_id=1, source_target_pairs={{0,4},{1,5},{2,6},{3,7},{4,0},{5,1},{6,2},{7,3},{8,12},{9,13},{10,... | collective-permute-start | bytes 294920 | tf_op jit(solution)/shard_map/ppermute | solution.py:24
  34.7 1.2 %collective-permute-done.17.refs_14_ = bf16[3,64,256]{2,1,0:T(8,128)(2,1)S(1)} collective-permute-done((bf16[3,64,256]{2,1,0:T(8,128)(2,1)S(1)}, bf16[3,64,256]{2,1,0:T(8,128)(2,1)S(1)}, u32[]{:S(2)}, u32[]{:S(2)}) %collective-permute-start.17) | collective-permute-done | bytes 98336 | tf_op jit(solution)/shard_map/ppermute | solution.py:24
  35.8 0.9 collective-permute-start.18
  36.7 1.0 %collective-permute-done.16.refs_10_ = bf16[3,64,256]{2,1,0:T(8,128)(2,1)S(1)} collective-permute-done((bf16[3,64,256]{2,1,0:T(8,128)(2,1)S(1)}, bf16[3,64,256]{2,1,0:T(8,128)(2,1)S(1)}, u32[]{:S(2)}, u32[]{:S(2)}) %collective-permute-start.16) | collective-permute-done | bytes 98336 | tf_op jit(solution)/shard_map/ppermute | solution.py:24
  37.8 2.7 %collective-permute-done.18.refs_15_ = bf16[3,64,256]{2,1,0:T(8,128)(2,1)S(1)} collective-permute-done((bf16[3,64,256]{2,1,0:T(8,128)(2,1)S(1)}, bf16[3,64,256]{2,1,0:T(8,128)(2,1)S(1)}, u32[]{:S(2)}, u32[]{:S(2)}) %collective-permute-start.18) | collective-permute-done | bytes 98336 | tf_op jit(solution)/shard_map/ppermute | solution.py:24
  40.4 0.7 copy-done.3
  41.1 3.8 %slot_gradients.1 = (bf16[3,64,256]{2,1,0:T(8,128)(2,1)S(1)}, bf16[3,64,256]{2,1,0:T(8,128)(2,1)S(1)}, bf16[2,3,64,256]{3,2,1,0:T(8,128)(2,1)S(1)}, bf16[3,64,25...) custom-call(s32[32]{0:T(128)S(1)} %copy-done.3, ...), custom_call_target="tpu_custom_call" | custom-call | flops 1610612736 | bytes 7340032 | tf_op jit(solution)/shard_map/slot_gradients/pallas_call | solution.py:152
  44.9 1.8 %collective-permute-start.19 = (bf16[2,3,64,256]{3,2,1,0:T(8,128)(2,1)S(1)}, bf16[2,3,64,256]{3,2,1,0:T(8,128)(2,1)S(1)}, u32[]{:S(2)}, u32[]{:S(2)}) collective-permute-start(bf16[2,3,64,256]{3,2,1,0:T(8,128)(2,1)S(1)} %get-tuple-element.70), channel_id=1, source_target_pairs={{0,4},{1,5},{2,6},{3,7},{4,0},{5,1},{6,2},{7,3},{8,12},{9,13},{10,... | collective-permute-start | bytes 589832 | tf_op jit(solution)/shard_map/ppermute | solution.py:24
  46.6 0.9 collective-permute-start.21
  47.5 1.2 %collective-permute-start.27 = (bf16[2,3,64,256]{3,2,1,0:T(8,128)(2,1)S(1)}, bf16[2,3,64,256]{3,2,1,0:T(8,128)(2,1)S(1)}, u32[]{:S(2)}, u32[]{:S(2)}) collective-permute-start(bf16[2,3,64,256]{3,2,1,0:T(8,128)(2,1)S(1)} %get-tuple-element.80), channel_id=1, source_target_pairs={{0,2},{1,3},{2,0},{3,1},{4,6},{5,7},{6,4},{7,5},{8,10},{9,11},{10,... | collective-permute-start | bytes 589832 | tf_op jit(solution)/shard_map/ppermute | solution.py:24
  48.7 4.0 %collective-permute-done.19 = bf16[2,3,64,256]{3,2,1,0:T(8,128)(2,1)S(1)} collective-permute-done((bf16[2,3,64,256]{3,2,1,0:T(8,128)(2,1)S(1)}, bf16[2,3,64,256]{3,2,1,0:T(8,128)(2,1)S(1)}, u32[]{:S(2)}, u32[]{:S(2)}) %collective-permute-start.19) | collective-permute-done | bytes 196640 | tf_op jit(solution)/shard_map/ppermute | solution.py:24
  52.7 0.9 collective-permute-start.20
  53.6 1.7 %collective-permute-start.22 = (bf16[3,64,256]{2,1,0:T(8,128)(2,1)S(1)}, bf16[3,64,256]{2,1,0:T(8,128)(2,1)S(1)}, u32[]{:S(2)}, u32[]{:S(2)}) collective-permute-start(bf16[3,64,256]{2,1,0:T(8,128)(2,1)S(1)} %fusion.10), channel_id=1, source_target_pairs={{0,4},{1,5},{2,6},{3,7},{4,0},{5,1},{6,2},{7,3},{8,12},{9,13},{10,... | collective-permute-start | bytes 294920 | tf_op jit(solution)/shard_map/ppermute | solution.py:24
  55.8 2.6 %collective-permute-done.22 = bf16[3,64,256]{2,1,0:T(8,128)(2,1)S(1)} collective-permute-done((bf16[3,64,256]{2,1,0:T(8,128)(2,1)S(1)}, bf16[3,64,256]{2,1,0:T(8,128)(2,1)S(1)}, u32[]{:S(2)}, u32[]{:S(2)}) %collective-permute-start.22) | collective-permute-done | bytes 98336 | tf_op jit(solution)/shard_map/ppermute | solution.py:24
  58.4 0.8 collective-permute-start.23
  59.2 2.0 %collective-permute-start.28 = (bf16[3,64,256]{2,1,0:T(8,128)(2,1)S(1)}, bf16[3,64,256]{2,1,0:T(8,128)(2,1)S(1)}, u32[]{:S(2)}, u32[]{:S(2)}) collective-permute-start(bf16[3,64,256]{2,1,0:T(8,128)(2,1)S(1)} %fusion.4), channel_id=1, source_target_pairs={{0,4},{1,5},{2,6},{3,7},{4,0},{5,1},{6,2},{7,3},{8,12},{9,13},{10,... | collective-permute-start | bytes 294920 | tf_op jit(solution)/shard_map/ppermute | solution.py:24
  61.2 1.8 %collective-permute-done.23 = bf16[3,64,256]{2,1,0:T(8,128)(2,1)S(1)} collective-permute-done((bf16[3,64,256]{2,1,0:T(8,128)(2,1)S(1)}, bf16[3,64,256]{2,1,0:T(8,128)(2,1)S(1)}, u32[]{:S(2)}, u32[]{:S(2)}) %collective-permute-start.23) | collective-permute-done | bytes 98336 | tf_op jit(solution)/shard_map/ppermute | solution.py:24
  63.1 1.5 %collective-permute-start.24 = (bf16[3,64,256]{2,1,0:T(8,128)(2,1)S(1)}, bf16[3,64,256]{2,1,0:T(8,128)(2,1)S(1)}, u32[]{:S(2)}, u32[]{:S(2)}) collective-permute-start(bf16[3,64,256]{2,1,0:T(8,128)(2,1)S(1)} %fusion.16), channel_id=1, source_target_pairs={{0,16},{1,17},{2,18},{3,19},{4,20},{5,21},{6,22},{7,23},{8,24},{9,... | collective-permute-start | bytes 294920 | tf_op jit(solution)/shard_map/ppermute | solution.py:24
  64.6 0.7 collective-permute-start.26
  65.3 1.9 %collective-permute-start.29 = (bf16[3,64,256]{2,1,0:T(8,128)(2,1)S(1)}, bf16[3,64,256]{2,1,0:T(8,128)(2,1)S(1)}, u32[]{:S(2)}, u32[]{:S(2)}) collective-permute-start(bf16[3,64,256]{2,1,0:T(8,128)(2,1)S(1)} %fusion.6), channel_id=1, source_target_pairs={{0,8},{1,9},{2,10},{3,11},{4,12},{5,13},{6,14},{7,15},{8,0},{9,1},... | collective-permute-start | bytes 294920 | tf_op jit(solution)/shard_map/ppermute | solution.py:24
  67.2 1.0 slice_bitcast_fusion.15
  68.2 1.6 %collective-permute-done.24 = bf16[3,64,256]{2,1,0:T(8,128)(2,1)S(1)} collective-permute-done((bf16[3,64,256]{2,1,0:T(8,128)(2,1)S(1)}, bf16[3,64,256]{2,1,0:T(8,128)(2,1)S(1)}, u32[]{:S(2)}, u32[]{:S(2)}) %collective-permute-start.24) | collective-permute-done | bytes 98336 | tf_op jit(solution)/shard_map/ppermute | solution.py:24
  70.1 1.7 %collective-permute-done.29 = bf16[3,64,256]{2,1,0:T(8,128)(2,1)S(1)} collective-permute-done((bf16[3,64,256]{2,1,0:T(8,128)(2,1)S(1)}, bf16[3,64,256]{2,1,0:T(8,128)(2,1)S(1)}, u32[]{:S(2)}, u32[]{:S(2)}) %collective-permute-start.29) | collective-permute-done | bytes 98336 | tf_op jit(solution)/shard_map/ppermute | solution.py:24
  72.5 1.0 %collective-permute-start.30 = (bf16[3,64,256]{2,1,0:T(8,128)(2,1)S(1)}, bf16[3,64,256]{2,1,0:T(8,128)(2,1)S(1)}, u32[]{:S(2)}, u32[]{:S(2)}) collective-permute-start(bf16[3,64,256]{2,1,0:T(8,128)(2,1)S(1)} %get-tuple-element.94.refs_0_), channel_id=1, source_target_pairs={{0,16},{1,17},{2,18},{3,19},{4,20},{5,21},{6,22},{7,23},{8,24},{9,... | collective-permute-start | bytes 294920 | tf_op jit(solution)/shard_map/ppermute | solution.py:24
  73.5 3.0 %collective-permute-start.38 = (bf16[3,64,256]{2,1,0:T(8,128)(2,1)S(1)}, bf16[3,64,256]{2,1,0:T(8,128)(2,1)S(1)}, u32[]{:S(2)}, u32[]{:S(2)}) collective-permute-start(bf16[3,64,256]{2,1,0:T(8,128)(2,1)S(1)} %get-tuple-element.94.refs_0_), channel_id=1, source_target_pairs={{0,4},{1,5},{2,6},{3,7},{4,0},{5,1},{6,2},{7,3},{8,12},{9,13},{10,... | collective-permute-start | bytes 294920 | tf_op jit(solution)/shard_map/ppermute | solution.py:24
  76.9 1.6 %collective-permute-start.33 = (bf16[3,64,256]{2,1,0:T(8,128)(2,1)S(1)}, bf16[3,64,256]{2,1,0:T(8,128)(2,1)S(1)}, u32[]{:S(2)}, u32[]{:S(2)}) collective-permute-start(bf16[3,64,256]{2,1,0:T(8,128)(2,1)S(1)} %collective-permute-done.32.refs_4_), channel_id=1, source_target_pairs={{0,2},{1,3},{2,0},{3,1},{4,6},{5,7},{6,4},{7,5},{8,10},{9,11},{10,... | collective-permute-start | bytes 294920 | tf_op jit(solution)/shard_map/ppermute | solution.py:24
  78.5 1.1 %collective-permute-start.31 = (bf16[3,64,256]{2,1,0:T(8,128)(2,1)S(1)}, bf16[3,64,256]{2,1,0:T(8,128)(2,1)S(1)}, u32[]{:S(2)}, u32[]{:S(2)}) collective-permute-start(bf16[3,64,256]{2,1,0:T(8,128)(2,1)S(1)} %collective-permute-done.30.refs_8_), channel_id=1, source_target_pairs={{0,8},{1,9},{2,10},{3,11},{4,12},{5,13},{6,14},{7,15},{8,0},{9,1},... | collective-permute-start | bytes 294920 | tf_op jit(solution)/shard_map/ppermute | solution.py:24
  80.1 2.0 %collective-permute-done.37.refs_1_ = bf16[3,64,256]{2,1,0:T(8,128)(2,1)S(1)} collective-permute-done((bf16[3,64,256]{2,1,0:T(8,128)(2,1)S(1)}, bf16[3,64,256]{2,1,0:T(8,128)(2,1)S(1)}, u32[]{:S(2)}, u32[]{:S(2)}) %collective-permute-start.37) | collective-permute-done | bytes 98336 | tf_op jit(solution)/shard_map/ppermute | solution.py:24
  82.5 0.6 collective-permute-start.41
  83.2 1.3 %collective-permute-start.40 = (bf16[3,64,256]{2,1,0:T(8,128)(2,1)S(1)}, bf16[3,64,256]{2,1,0:T(8,128)(2,1)S(1)}, u32[]{:S(2)}, u32[]{:S(2)}) collective-permute-start(bf16[3,64,256]{2,1,0:T(8,128)(2,1)S(1)} %collective-permute-done.31.refs_12_), channel_id=1, source_target_pairs={{0,2},{1,3},{2,0},{3,1},{4,6},{5,7},{6,4},{7,5},{8,10},{9,11},{10,... | collective-permute-start | bytes 294920 | tf_op jit(solution)/shard_map/ppermute | solution.py:24
  84.5 1.7 %collective-permute-start.34 = (bf16[3,64,256]{2,1,0:T(8,128)(2,1)S(1)}, bf16[3,64,256]{2,1,0:T(8,128)(2,1)S(1)}, u32[]{:S(2)}, u32[]{:S(2)}) collective-permute-start(bf16[3,64,256]{2,1,0:T(8,128)(2,1)S(1)} %collective-permute-done.31.refs_12_), channel_id=1, source_target_pairs={{0,4},{1,5},{2,6},{3,7},{4,0},{5,1},{6,2},{7,3},{8,12},{9,13},{10,... | collective-permute-start | bytes 294920 | tf_op jit(solution)/shard_map/ppermute | solution.py:24
  86.2 0.6 collective-permute-done.39.refs_9_
  87.1 0.7 collective-permute-done.40.refs_13_
  87.8 1.7 %collective-permute-start.42 = (bf16[2,3,64,256]{3,2,1,0:T(8,128)(2,1)S(1)}, bf16[2,3,64,256]{3,2,1,0:T(8,128)(2,1)S(1)}, u32[]{:S(2)}, u32[]{:S(2)}) collective-permute-start(bf16[2,3,64,256]{3,2,1,0:T(8,128)(2,1)S(1)} %pad_maximum_fusion.3), channel_id=1, source_target_pairs={{0,4},{1,5},{2,6},{3,7},{4,0},{5,1},{6,2},{7,3},{8,12},{9,13},{10,... | collective-permute-start | bytes 589832 | tf_op jit(solution)/shard_map/ppermute | solution.py:24
  89.6 1.4 %collective-permute-start.35 = (bf16[3,64,256]{2,1,0:T(8,128)(2,1)S(1)}, bf16[3,64,256]{2,1,0:T(8,128)(2,1)S(1)}, u32[]{:S(2)}, u32[]{:S(2)}) collective-permute-start(bf16[3,64,256]{2,1,0:T(8,128)(2,1)S(1)} %collective-permute-done.34.refs_14_), channel_id=1, source_target_pairs={{0,2},{1,3},{2,0},{3,1},{4,6},{5,7},{6,4},{7,5},{8,10},{9,11},{10,... | collective-permute-start | bytes 294920 | tf_op jit(solution)/shard_map/ppermute | solution.py:24
  91.0 0.8 collective-permute-start.43
  91.8 1.2 %collective-permute-start.44 = (bf16[3,64,256]{2,1,0:T(8,128)(2,1)S(1)}, bf16[3,64,256]{2,1,0:T(8,128)(2,1)S(1)}, u32[]{:S(2)}, u32[]{:S(2)}) collective-permute-start(bf16[3,64,256]{2,1,0:T(8,128)(2,1)S(1)} %collective-permute-done.30.refs_8_), channel_id=1, source_target_pairs={{0,4},{1,5},{2,6},{3,7},{4,0},{5,1},{6,2},{7,3},{8,12},{9,13},{10,... | collective-permute-start | bytes 294920 | tf_op jit(solution)/shard_map/ppermute | solution.py:24
  93.0 1.3 %collective-permute-done.35.refs_15_ = bf16[3,64,256]{2,1,0:T(8,128)(2,1)S(1)} collective-permute-done((bf16[3,64,256]{2,1,0:T(8,128)(2,1)S(1)}, bf16[3,64,256]{2,1,0:T(8,128)(2,1)S(1)}, u32[]{:S(2)}, u32[]{:S(2)}) %collective-permute-start.35) | collective-permute-done | bytes 98336 | tf_op jit(solution)/shard_map/ppermute | solution.py:24
  94.3 1.4 %collective-permute-done.43.refs_7_ = bf16[3,64,256]{2,1,0:T(8,128)(2,1)S(1)} collective-permute-done((bf16[3,64,256]{2,1,0:T(8,128)(2,1)S(1)}, bf16[3,64,256]{2,1,0:T(8,128)(2,1)S(1)}, u32[]{:S(2)}, u32[]{:S(2)}) %collective-permute-start.43) | collective-permute-done | bytes 98336 | tf_op jit(solution)/shard_map/ppermute | solution.py:24
  95.7 0.7 collective-permute-done.44.refs_10_
  96.4 0.7 copy-done.4
  97.0 1.8 %expert_outputs.1 = (bf16[256,1024]{1,0:T(8,128)(2,1)S(1)}, bf16[256,1024]{1,0:T(8,128)(2,1)S(1)}, s32[1]{0:T(128)}) custom-call(s32[32]{0:T(128)S(1)} %copy-done.4, bf16[3,64,256]{2,1,0:T(8,128)(2,1)S(1)} %get-tuple-element.94.refs_0_, bf16[3,64,256]{2,1,0:T(8,128)(2,1)S(1)} %collective-permute-done.37.refs_1_, ...), custom_call_target="tpu_custom_call" | custom-call | flops 805306368 | bytes 3670016 | tf_op jit(solution)/shard_map/expert_outputs/pallas_call | solution.py:178
  99.7 0.8 slice_bitcast_fusion
  100.9 0.8 select_bitcast_fusion
  (66 shorter events, 7.3 us)
Async XLA Ops:
  0.6 1.1 %copy-start.5 = (f32[2,3,32,256]{3,2,1,0:T(8,128)S(1)}, f32[2,3,32,256]{3,2,1,0:T(8,128)}, u32[]{:S(2)}) copy-start(f32[2,3,32,256]{3,2,1,0:T(8,128)} %param.11) | copy-start | bytes 589828
  0.6 3.4 %copy-start.2 = (bf16[1,256,1024]{2,1,0:T(8,128)(2,1)S(1)}, bf16[1,256,1024]{2,1,0:T(8,128)(2,1)}, u32[]{:S(2)}) copy-start(bf16[1,256,1024]{2,1,0:T(8,128)(2,1)} %param.14) | copy-start | bytes 1572868
  1.7 1.8 %copy-start = (bf16[1,256,1024]{2,1,0:T(8,128)(2,1)S(1)}, bf16[1,256,1024]{2,1,0:T(8,128)(2,1)}, u32[]{:S(2)}) copy-start(bf16[1,256,1024]{2,1,0:T(8,128)(2,1)} %param.12) | copy-start | bytes 1572868
  1.7 2.3 %copy-start.1 = (bf16[1,256,1024]{2,1,0:T(8,128)(2,1)S(1)}, bf16[1,256,1024]{2,1,0:T(8,128)(2,1)}, u32[]{:S(2)}) copy-start(bf16[1,256,1024]{2,1,0:T(8,128)(2,1)} %param.13) | copy-start | bytes 1572868
  3.5 3.9 %collective-permute-start.1 = (bf16[256,1024]{1,0:T(8,128)(2,1)S(1)}, bf16[256,1024]{1,0:T(8,128)(2,1)S(1)}, u32[]{:S(2)}, u32[]{:S(2)}) collective-permute-start(bf16[256,1024]{1,0:T(8,128)(2,1)S(1)} %bitcast.88), channel_id=1, source_target_pairs={{0,1},{1,0},{2,3},{3,2},{4,5},{5,4},{6,7},{7,6},{8,9},{9,8},{10,11... | collective-permute-start | bytes 1572872 | tf_op jit(solution)/shard_map/ppermute | solution.py:24
  4.0 3.4 %collective-permute-start.2 = (bf16[256,1024]{1,0:T(8,128)(2,1)S(1)}, bf16[256,1024]{1,0:T(8,128)(2,1)S(1)}, u32[]{:S(2)}, u32[]{:S(2)}) collective-permute-start(bf16[256,1024]{1,0:T(8,128)(2,1)S(1)} %bitcast.90), channel_id=1, source_target_pairs={{0,1},{1,0},{2,3},{3,2},{4,5},{5,4},{6,7},{7,6},{8,9},{9,8},{10,11... | collective-permute-start | bytes 1572872 | tf_op jit(solution)/shard_map/ppermute | solution.py:24
  4.1 3.4 %collective-permute-start.3 = (bf16[256,1024]{1,0:T(8,128)(2,1)S(1)}, bf16[256,1024]{1,0:T(8,128)(2,1)S(1)}, u32[]{:S(2)}, u32[]{:S(2)}) collective-permute-start(bf16[256,1024]{1,0:T(8,128)(2,1)S(1)} %bitcast.96), channel_id=1, source_target_pairs={{0,1},{1,0},{2,3},{3,2},{4,5},{5,4},{6,7},{7,6},{8,9},{9,8},{10,11... | collective-permute-start | bytes 1572872 | tf_op jit(solution)/shard_map/ppermute | solution.py:24
  4.5 2.9 %collective-permute-start = (f32[3,3,32,256]{3,2,1,0:T(8,128)}, f32[3,3,32,256]{3,2,1,0:T(8,128)}, u32[]{:S(2)}, u32[]{:S(2)}) collective-permute-start(f32[3,3,32,256]{3,2,1,0:T(8,128)} %pad_maximum_fusion.1), channel_id=1, source_target_pairs={{0,1},{1,0},{2,3},{3,2},{4,5},{5,4},{6,7},{7,6},{8,9},{9,8},{10,11... | collective-permute-start | bytes 884744 | tf_op jit(solution)/shard_map/ppermute | solution.py:24
  4.6 2.8 %collective-permute-start.4 = (s32[1]{0:T(128)}, s32[1]{0:T(128)}, u32[]{:S(2)}, u32[]{:S(2)}) collective-permute-start(s32[1]{0:T(128)} %param.17), channel_id=1, source_target_pairs={{0,1},{1,0},{2,3},{3,2},{4,5},{5,4},{6,7},{7,6},{8,9},{9,8},{10,11... | collective-permute-start | bytes 20 | tf_op jit(solution)/shard_map/ppermute | solution.py:24
  8.4 8.6 %collective-permute-start.10 = (bf16[3,64,256]{2,1,0:T(8,128)(2,1)S(1)}, bf16[3,64,256]{2,1,0:T(8,128)(2,1)S(1)}, u32[]{:S(2)}, u32[]{:S(2)}) collective-permute-start(bf16[3,64,256]{2,1,0:T(8,128)(2,1)S(1)} %fusion.17.refs_0_), channel_id=1, source_target_pairs={{0,8},{1,9},{2,10},{3,11},{4,12},{5,13},{6,14},{7,15},{8,0},{9,1},... | collective-permute-start | bytes 294920 | tf_op jit(solution)/shard_map/ppermute | solution.py:24
  11.4 7.6 %collective-permute-start.7 = (bf16[3,64,256]{2,1,0:T(8,128)(2,1)S(1)}, bf16[3,64,256]{2,1,0:T(8,128)(2,1)S(1)}, u32[]{:S(2)}, u32[]{:S(2)}) collective-permute-start(bf16[3,64,256]{2,1,0:T(8,128)(2,1)S(1)} %fusion.17.refs_0_), channel_id=1, source_target_pairs={{0,16},{1,17},{2,18},{3,19},{4,20},{5,21},{6,22},{7,23},{8,24},{9,... | collective-permute-start | bytes 294920 | tf_op jit(solution)/shard_map/ppermute | solution.py:24
  14.0 5.5 %collective-permute-start.6 = (bf16[3,64,256]{2,1,0:T(8,128)(2,1)S(1)}, bf16[3,64,256]{2,1,0:T(8,128)(2,1)S(1)}, u32[]{:S(2)}, u32[]{:S(2)}) collective-permute-start(bf16[3,64,256]{2,1,0:T(8,128)(2,1)S(1)} %fusion.17.refs_0_), channel_id=1, source_target_pairs={{0,4},{1,5},{2,6},{3,7},{4,0},{5,1},{6,2},{7,3},{8,12},{9,13},{10,... | collective-permute-start | bytes 294920 | tf_op jit(solution)/shard_map/ppermute | solution.py:24
  15.5 5.2 %collective-permute-start.5 = (bf16[3,64,256]{2,1,0:T(8,128)(2,1)S(1)}, bf16[3,64,256]{2,1,0:T(8,128)(2,1)S(1)}, u32[]{:S(2)}, u32[]{:S(2)}) collective-permute-start(bf16[3,64,256]{2,1,0:T(8,128)(2,1)S(1)} %fusion.17.refs_0_), channel_id=1, source_target_pairs={{0,2},{1,3},{2,0},{3,1},{4,6},{5,7},{6,4},{7,5},{8,10},{9,11},{10,... | collective-permute-start | bytes 294920 | tf_op jit(solution)/shard_map/ppermute | solution.py:24
  17.0 5.6 %collective-permute-start.11 = (bf16[3,64,256]{2,1,0:T(8,128)(2,1)S(1)}, bf16[3,64,256]{2,1,0:T(8,128)(2,1)S(1)}, u32[]{:S(2)}, u32[]{:S(2)}) collective-permute-start(bf16[3,64,256]{2,1,0:T(8,128)(2,1)S(1)} %collective-permute-done.10.refs_4_), channel_id=1, source_target_pairs={{0,2},{1,3},{2,0},{3,1},{4,6},{5,7},{6,4},{7,5},{8,10},{9,11},{10,... | collective-permute-start | bytes 294920 | tf_op jit(solution)/shard_map/ppermute | solution.py:24
  19.0 4.6 %collective-permute-start.9 = (bf16[3,64,256]{2,1,0:T(8,128)(2,1)S(1)}, bf16[3,64,256]{2,1,0:T(8,128)(2,1)S(1)}, u32[]{:S(2)}, u32[]{:S(2)}) collective-permute-start(bf16[3,64,256]{2,1,0:T(8,128)(2,1)S(1)} %collective-permute-done.7.refs_8_), channel_id=1, source_target_pairs={{0,8},{1,9},{2,10},{3,11},{4,12},{5,13},{6,14},{7,15},{8,0},{9,1},... | collective-permute-start | bytes 294920 | tf_op jit(solution)/shard_map/ppermute | solution.py:24
  20.7 4.8 %collective-permute-start.8 = (bf16[3,64,256]{2,1,0:T(8,128)(2,1)S(1)}, bf16[3,64,256]{2,1,0:T(8,128)(2,1)S(1)}, u32[]{:S(2)}, u32[]{:S(2)}) collective-permute-start(bf16[3,64,256]{2,1,0:T(8,128)(2,1)S(1)} %collective-permute-done.7.refs_8_), channel_id=1, source_target_pairs={{0,2},{1,3},{2,0},{3,1},{4,6},{5,7},{6,4},{7,5},{8,10},{9,11},{10,... | collective-permute-start | bytes 294920 | tf_op jit(solution)/shard_map/ppermute | solution.py:24
  22.0 4.6 %collective-permute-start.13 = (bf16[3,64,256]{2,1,0:T(8,128)(2,1)S(1)}, bf16[3,64,256]{2,1,0:T(8,128)(2,1)S(1)}, u32[]{:S(2)}, u32[]{:S(2)}) collective-permute-start(bf16[3,64,256]{2,1,0:T(8,128)(2,1)S(1)} %collective-permute-done.10.refs_4_), channel_id=1, source_target_pairs={{0,4},{1,5},{2,6},{3,7},{4,0},{5,1},{6,2},{7,3},{8,12},{9,13},{10,... | collective-permute-start | bytes 294920 | tf_op jit(solution)/shard_map/ppermute | solution.py:24
  23.6 4.6 %collective-permute-start.12 = (bf16[3,64,256]{2,1,0:T(8,128)(2,1)S(1)}, bf16[3,64,256]{2,1,0:T(8,128)(2,1)S(1)}, u32[]{:S(2)}, u32[]{:S(2)}) collective-permute-start(bf16[3,64,256]{2,1,0:T(8,128)(2,1)S(1)} %collective-permute-done.9.refs_12_), channel_id=1, source_target_pairs={{0,2},{1,3},{2,0},{3,1},{4,6},{5,7},{6,4},{7,5},{8,10},{9,11},{10,... | collective-permute-start | bytes 294920 | tf_op jit(solution)/shard_map/ppermute | solution.py:24
  28.2 8.5 %collective-permute-start.14 = (bf16[2,3,64,256]{3,2,1,0:T(8,128)(2,1)S(1)}, bf16[2,3,64,256]{3,2,1,0:T(8,128)(2,1)S(1)}, u32[]{:S(2)}, u32[]{:S(2)}) collective-permute-start(bf16[2,3,64,256]{3,2,1,0:T(8,128)(2,1)S(1)} %pad_maximum_fusion.2), channel_id=1, source_target_pairs={{0,4},{1,5},{2,6},{3,7},{4,0},{5,1},{6,2},{7,3},{8,12},{9,13},{10,... | collective-permute-start | bytes 589832 | tf_op jit(solution)/shard_map/ppermute | solution.py:24
  29.7 6.1 %collective-permute-start.17 = (bf16[3,64,256]{2,1,0:T(8,128)(2,1)S(1)}, bf16[3,64,256]{2,1,0:T(8,128)(2,1)S(1)}, u32[]{:S(2)}, u32[]{:S(2)}) collective-permute-start(bf16[3,64,256]{2,1,0:T(8,128)(2,1)S(1)} %collective-permute-done.9.refs_12_), channel_id=1, source_target_pairs={{0,4},{1,5},{2,6},{3,7},{4,0},{5,1},{6,2},{7,3},{8,12},{9,13},{10,... | collective-permute-start | bytes 294920 | tf_op jit(solution)/shard_map/ppermute | solution.py:24
  31.6 5.1 %collective-permute-start.15 = (bf16[3,64,256]{2,1,0:T(8,128)(2,1)S(1)}, bf16[3,64,256]{2,1,0:T(8,128)(2,1)S(1)}, u32[]{:S(2)}, u32[]{:S(2)}) collective-permute-start(bf16[3,64,256]{2,1,0:T(8,128)(2,1)S(1)} %collective-permute-done.13.refs_6_), channel_id=1, source_target_pairs={{0,2},{1,3},{2,0},{3,1},{4,6},{5,7},{6,4},{7,5},{8,10},{9,11},{10,... | collective-permute-start | bytes 294920 | tf_op jit(solution)/shard_map/ppermute | solution.py:24
  33.1 4.6 %collective-permute-start.16 = (bf16[3,64,256]{2,1,0:T(8,128)(2,1)S(1)}, bf16[3,64,256]{2,1,0:T(8,128)(2,1)S(1)}, u32[]{:S(2)}, u32[]{:S(2)}) collective-permute-start(bf16[3,64,256]{2,1,0:T(8,128)(2,1)S(1)} %collective-permute-done.7.refs_8_), channel_id=1, source_target_pairs={{0,4},{1,5},{2,6},{3,7},{4,0},{5,1},{6,2},{7,3},{8,12},{9,13},{10,... | collective-permute-start | bytes 294920 | tf_op jit(solution)/shard_map/ppermute | solution.py:24
  35.8 4.6 %collective-permute-start.18 = (bf16[3,64,256]{2,1,0:T(8,128)(2,1)S(1)}, bf16[3,64,256]{2,1,0:T(8,128)(2,1)S(1)}, u32[]{:S(2)}, u32[]{:S(2)}) collective-permute-start(bf16[3,64,256]{2,1,0:T(8,128)(2,1)S(1)} %collective-permute-done.17.refs_14_), channel_id=1, source_target_pairs={{0,2},{1,3},{2,0},{3,1},{4,6},{5,7},{6,4},{7,5},{8,10},{9,11},{10,... | collective-permute-start | bytes 294920 | tf_op jit(solution)/shard_map/ppermute | solution.py:24
  40.4 0.7 copy-start.3
  44.9 7.8 %collective-permute-start.19 = (bf16[2,3,64,256]{3,2,1,0:T(8,128)(2,1)S(1)}, bf16[2,3,64,256]{3,2,1,0:T(8,128)(2,1)S(1)}, u32[]{:S(2)}, u32[]{:S(2)}) collective-permute-start(bf16[2,3,64,256]{3,2,1,0:T(8,128)(2,1)S(1)} %get-tuple-element.70), channel_id=1, source_target_pairs={{0,4},{1,5},{2,6},{3,7},{4,0},{5,1},{6,2},{7,3},{8,12},{9,13},{10,... | collective-permute-start | bytes 589832 | tf_op jit(solution)/shard_map/ppermute | solution.py:24
  46.6 7.0 %collective-permute-start.21 = (bf16[2,3,64,256]{3,2,1,0:T(8,128)(2,1)S(1)}, bf16[2,3,64,256]{3,2,1,0:T(8,128)(2,1)S(1)}, u32[]{:S(2)}, u32[]{:S(2)}) collective-permute-start(bf16[2,3,64,256]{3,2,1,0:T(8,128)(2,1)S(1)} %get-tuple-element.73), channel_id=1, source_target_pairs={{0,2},{1,3},{2,0},{3,1},{4,6},{5,7},{6,4},{7,5},{8,10},{9,11},{10,... | collective-permute-start | bytes 589832 | tf_op jit(solution)/shard_map/ppermute | solution.py:24
  47.5 8.2 %collective-permute-start.27 = (bf16[2,3,64,256]{3,2,1,0:T(8,128)(2,1)S(1)}, bf16[2,3,64,256]{3,2,1,0:T(8,128)(2,1)S(1)}, u32[]{:S(2)}, u32[]{:S(2)}) collective-permute-start(bf16[2,3,64,256]{3,2,1,0:T(8,128)(2,1)S(1)} %get-tuple-element.80), channel_id=1, source_target_pairs={{0,2},{1,3},{2,0},{3,1},{4,6},{5,7},{6,4},{7,5},{8,10},{9,11},{10,... | collective-permute-start | bytes 589832 | tf_op jit(solution)/shard_map/ppermute | solution.py:24
  52.7 8.5 %collective-permute-start.20 = (bf16[3,64,256]{2,1,0:T(8,128)(2,1)S(1)}, bf16[3,64,256]{2,1,0:T(8,128)(2,1)S(1)}, u32[]{:S(2)}, u32[]{:S(2)}) collective-permute-start(bf16[3,64,256]{2,1,0:T(8,128)(2,1)S(1)} %fusion.13), channel_id=1, source_target_pairs={{0,2},{1,3},{2,0},{3,1},{4,6},{5,7},{6,4},{7,5},{8,10},{9,11},{10,... | collective-permute-start | bytes 294920 | tf_op jit(solution)/shard_map/ppermute | solution.py:24
  53.6 4.7 %collective-permute-start.22 = (bf16[3,64,256]{2,1,0:T(8,128)(2,1)S(1)}, bf16[3,64,256]{2,1,0:T(8,128)(2,1)S(1)}, u32[]{:S(2)}, u32[]{:S(2)}) collective-permute-start(bf16[3,64,256]{2,1,0:T(8,128)(2,1)S(1)} %fusion.10), channel_id=1, source_target_pairs={{0,4},{1,5},{2,6},{3,7},{4,0},{5,1},{6,2},{7,3},{8,12},{9,13},{10,... | collective-permute-start | bytes 294920 | tf_op jit(solution)/shard_map/ppermute | solution.py:24
  55.3 5.9 %collective-permute-start.25 = (bf16[2,3,64,256]{3,2,1,0:T(8,128)(2,1)S(1)}, bf16[2,3,64,256]{3,2,1,0:T(8,128)(2,1)S(1)}, u32[]{:S(2)}, u32[]{:S(2)}) collective-permute-start(bf16[2,3,64,256]{3,2,1,0:T(8,128)(2,1)S(1)} %get-tuple-element.76), channel_id=1, source_target_pairs={{0,4},{1,5},{2,6},{3,7},{4,0},{5,1},{6,2},{7,3},{8,12},{9,13},{10,... | collective-permute-start | bytes 589832 | tf_op jit(solution)/shard_map/ppermute | solution.py:24
  58.4 4.7 %collective-permute-start.23 = (bf16[3,64,256]{2,1,0:T(8,128)(2,1)S(1)}, bf16[3,64,256]{2,1,0:T(8,128)(2,1)S(1)}, u32[]{:S(2)}, u32[]{:S(2)}) collective-permute-start(bf16[3,64,256]{2,1,0:T(8,128)(2,1)S(1)} %fusion.12), channel_id=1, source_target_pairs={{0,8},{1,9},{2,10},{3,11},{4,12},{5,13},{6,14},{7,15},{8,0},{9,1},... | collective-permute-start | bytes 294920 | tf_op jit(solution)/shard_map/ppermute | solution.py:24
  59.2 6.1 %collective-permute-start.28 = (bf16[3,64,256]{2,1,0:T(8,128)(2,1)S(1)}, bf16[3,64,256]{2,1,0:T(8,128)(2,1)S(1)}, u32[]{:S(2)}, u32[]{:S(2)}) collective-permute-start(bf16[3,64,256]{2,1,0:T(8,128)(2,1)S(1)} %fusion.4), channel_id=1, source_target_pairs={{0,4},{1,5},{2,6},{3,7},{4,0},{5,1},{6,2},{7,3},{8,12},{9,13},{10,... | collective-permute-start | bytes 294920 | tf_op jit(solution)/shard_map/ppermute | solution.py:24
  63.1 6.7 %collective-permute-start.24 = (bf16[3,64,256]{2,1,0:T(8,128)(2,1)S(1)}, bf16[3,64,256]{2,1,0:T(8,128)(2,1)S(1)}, u32[]{:S(2)}, u32[]{:S(2)}) collective-permute-start(bf16[3,64,256]{2,1,0:T(8,128)(2,1)S(1)} %fusion.16), channel_id=1, source_target_pairs={{0,16},{1,17},{2,18},{3,19},{4,20},{5,21},{6,22},{7,23},{8,24},{9,... | collective-permute-start | bytes 294920 | tf_op jit(solution)/shard_map/ppermute | solution.py:24
  64.6 5.5 %collective-permute-start.26 = (bf16[3,64,256]{2,1,0:T(8,128)(2,1)S(1)}, bf16[3,64,256]{2,1,0:T(8,128)(2,1)S(1)}, u32[]{:S(2)}, u32[]{:S(2)}) collective-permute-start(bf16[3,64,256]{2,1,0:T(8,128)(2,1)S(1)} %fusion.7), channel_id=1, source_target_pairs={{0,2},{1,3},{2,0},{3,1},{4,6},{5,7},{6,4},{7,5},{8,10},{9,11},{10,... | collective-permute-start | bytes 294920 | tf_op jit(solution)/shard_map/ppermute | solution.py:24
  65.3 6.4 %collective-permute-start.29 = (bf16[3,64,256]{2,1,0:T(8,128)(2,1)S(1)}, bf16[3,64,256]{2,1,0:T(8,128)(2,1)S(1)}, u32[]{:S(2)}, u32[]{:S(2)}) collective-permute-start(bf16[3,64,256]{2,1,0:T(8,128)(2,1)S(1)} %fusion.6), channel_id=1, source_target_pairs={{0,8},{1,9},{2,10},{3,11},{4,12},{5,13},{6,14},{7,15},{8,0},{9,1},... | collective-permute-start | bytes 294920 | tf_op jit(solution)/shard_map/ppermute | solution.py:24
  72.0 4.8 %collective-permute-start.32 = (bf16[3,64,256]{2,1,0:T(8,128)(2,1)S(1)}, bf16[3,64,256]{2,1,0:T(8,128)(2,1)S(1)}, u32[]{:S(2)}, u32[]{:S(2)}) collective-permute-start(bf16[3,64,256]{2,1,0:T(8,128)(2,1)S(1)} %get-tuple-element.94.refs_0_), channel_id=1, source_target_pairs={{0,8},{1,9},{2,10},{3,11},{4,12},{5,13},{6,14},{7,15},{8,0},{9,1},... | collective-permute-start | bytes 294920 | tf_op jit(solution)/shard_map/ppermute | solution.py:24
  72.5 6.0 %collective-permute-start.30 = (bf16[3,64,256]{2,1,0:T(8,128)(2,1)S(1)}, bf16[3,64,256]{2,1,0:T(8,128)(2,1)S(1)}, u32[]{:S(2)}, u32[]{:S(2)}) collective-permute-start(bf16[3,64,256]{2,1,0:T(8,128)(2,1)S(1)} %get-tuple-element.94.refs_0_), channel_id=1, source_target_pairs={{0,16},{1,17},{2,18},{3,19},{4,20},{5,21},{6,22},{7,23},{8,24},{9,... | collective-permute-start | bytes 294920 | tf_op jit(solution)/shard_map/ppermute | solution.py:24
  73.5 6.6 %collective-permute-start.38 = (bf16[3,64,256]{2,1,0:T(8,128)(2,1)S(1)}, bf16[3,64,256]{2,1,0:T(8,128)(2,1)S(1)}, u32[]{:S(2)}, u32[]{:S(2)}) collective-permute-start(bf16[3,64,256]{2,1,0:T(8,128)(2,1)S(1)} %get-tuple-element.94.refs_0_), channel_id=1, source_target_pairs={{0,4},{1,5},{2,6},{3,7},{4,0},{5,1},{6,2},{7,3},{8,12},{9,13},{10,... | collective-permute-start | bytes 294920 | tf_op jit(solution)/shard_map/ppermute | solution.py:24
  76.5 5.7 %collective-permute-start.37 = (bf16[3,64,256]{2,1,0:T(8,128)(2,1)S(1)}, bf16[3,64,256]{2,1,0:T(8,128)(2,1)S(1)}, u32[]{:S(2)}, u32[]{:S(2)}) collective-permute-start(bf16[3,64,256]{2,1,0:T(8,128)(2,1)S(1)} %get-tuple-element.94.refs_0_), channel_id=1, source_target_pairs={{0,2},{1,3},{2,0},{3,1},{4,6},{5,7},{6,4},{7,5},{8,10},{9,11},{10,... | collective-permute-start | bytes 294920 | tf_op jit(solution)/shard_map/ppermute | solution.py:24
  76.9 6.3 %collective-permute-start.33 = (bf16[3,64,256]{2,1,0:T(8,128)(2,1)S(1)}, bf16[3,64,256]{2,1,0:T(8,128)(2,1)S(1)}, u32[]{:S(2)}, u32[]{:S(2)}) collective-permute-start(bf16[3,64,256]{2,1,0:T(8,128)(2,1)S(1)} %collective-permute-done.32.refs_4_), channel_id=1, source_target_pairs={{0,2},{1,3},{2,0},{3,1},{4,6},{5,7},{6,4},{7,5},{8,10},{9,11},{10,... | collective-permute-start | bytes 294920 | tf_op jit(solution)/shard_map/ppermute | solution.py:24
  78.5 4.7 %collective-permute-start.31 = (bf16[3,64,256]{2,1,0:T(8,128)(2,1)S(1)}, bf16[3,64,256]{2,1,0:T(8,128)(2,1)S(1)}, u32[]{:S(2)}, u32[]{:S(2)}) collective-permute-start(bf16[3,64,256]{2,1,0:T(8,128)(2,1)S(1)} %collective-permute-done.30.refs_8_), channel_id=1, source_target_pairs={{0,8},{1,9},{2,10},{3,11},{4,12},{5,13},{6,14},{7,15},{8,0},{9,1},... | collective-permute-start | bytes 294920 | tf_op jit(solution)/shard_map/ppermute | solution.py:24
  82.1 4.6 %collective-permute-start.39 = (bf16[3,64,256]{2,1,0:T(8,128)(2,1)S(1)}, bf16[3,64,256]{2,1,0:T(8,128)(2,1)S(1)}, u32[]{:S(2)}, u32[]{:S(2)}) collective-permute-start(bf16[3,64,256]{2,1,0:T(8,128)(2,1)S(1)} %collective-permute-done.30.refs_8_), channel_id=1, source_target_pairs={{0,2},{1,3},{2,0},{3,1},{4,6},{5,7},{6,4},{7,5},{8,10},{9,11},{10,... | collective-permute-start | bytes 294920 | tf_op jit(solution)/shard_map/ppermute | solution.py:24
  82.5 4.6 %collective-permute-start.41 = (bf16[3,64,256]{2,1,0:T(8,128)(2,1)S(1)}, bf16[3,64,256]{2,1,0:T(8,128)(2,1)S(1)}, u32[]{:S(2)}, u32[]{:S(2)}) collective-permute-start(bf16[3,64,256]{2,1,0:T(8,128)(2,1)S(1)} %collective-permute-done.32.refs_4_), channel_id=1, source_target_pairs={{0,4},{1,5},{2,6},{3,7},{4,0},{5,1},{6,2},{7,3},{8,12},{9,13},{10,... | collective-permute-start | bytes 294920 | tf_op jit(solution)/shard_map/ppermute | solution.py:24
  83.2 4.6 %collective-permute-start.40 = (bf16[3,64,256]{2,1,0:T(8,128)(2,1)S(1)}, bf16[3,64,256]{2,1,0:T(8,128)(2,1)S(1)}, u32[]{:S(2)}, u32[]{:S(2)}) collective-permute-start(bf16[3,64,256]{2,1,0:T(8,128)(2,1)S(1)} %collective-permute-done.31.refs_12_), channel_id=1, source_target_pairs={{0,2},{1,3},{2,0},{3,1},{4,6},{5,7},{6,4},{7,5},{8,10},{9,11},{10,... | collective-permute-start | bytes 294920 | tf_op jit(solution)/shard_map/ppermute | solution.py:24
  84.5 5.1 %collective-permute-start.34 = (bf16[3,64,256]{2,1,0:T(8,128)(2,1)S(1)}, bf16[3,64,256]{2,1,0:T(8,128)(2,1)S(1)}, u32[]{:S(2)}, u32[]{:S(2)}) collective-permute-start(bf16[3,64,256]{2,1,0:T(8,128)(2,1)S(1)} %collective-permute-done.31.refs_12_), channel_id=1, source_target_pairs={{0,4},{1,5},{2,6},{3,7},{4,0},{5,1},{6,2},{7,3},{8,12},{9,13},{10,... | collective-permute-start | bytes 294920 | tf_op jit(solution)/shard_map/ppermute | solution.py:24
  87.8 6.4 %collective-permute-start.42 = (bf16[2,3,64,256]{3,2,1,0:T(8,128)(2,1)S(1)}, bf16[2,3,64,256]{3,2,1,0:T(8,128)(2,1)S(1)}, u32[]{:S(2)}, u32[]{:S(2)}) collective-permute-start(bf16[2,3,64,256]{3,2,1,0:T(8,128)(2,1)S(1)} %pad_maximum_fusion.3), channel_id=1, source_target_pairs={{0,4},{1,5},{2,6},{3,7},{4,0},{5,1},{6,2},{7,3},{8,12},{9,13},{10,... | collective-permute-start | bytes 589832 | tf_op jit(solution)/shard_map/ppermute | solution.py:24
  89.6 4.7 %collective-permute-start.35 = (bf16[3,64,256]{2,1,0:T(8,128)(2,1)S(1)}, bf16[3,64,256]{2,1,0:T(8,128)(2,1)S(1)}, u32[]{:S(2)}, u32[]{:S(2)}) collective-permute-start(bf16[3,64,256]{2,1,0:T(8,128)(2,1)S(1)} %collective-permute-done.34.refs_14_), channel_id=1, source_target_pairs={{0,2},{1,3},{2,0},{3,1},{4,6},{5,7},{6,4},{7,5},{8,10},{9,11},{10,... | collective-permute-start | bytes 294920 | tf_op jit(solution)/shard_map/ppermute | solution.py:24
  91.0 4.7 %collective-permute-start.43 = (bf16[3,64,256]{2,1,0:T(8,128)(2,1)S(1)}, bf16[3,64,256]{2,1,0:T(8,128)(2,1)S(1)}, u32[]{:S(2)}, u32[]{:S(2)}) collective-permute-start(bf16[3,64,256]{2,1,0:T(8,128)(2,1)S(1)} %collective-permute-done.41.refs_6_), channel_id=1, source_target_pairs={{0,2},{1,3},{2,0},{3,1},{4,6},{5,7},{6,4},{7,5},{8,10},{9,11},{10,... | collective-permute-start | bytes 294920 | tf_op jit(solution)/shard_map/ppermute | solution.py:24
  91.8 4.6 %collective-permute-start.44 = (bf16[3,64,256]{2,1,0:T(8,128)(2,1)S(1)}, bf16[3,64,256]{2,1,0:T(8,128)(2,1)S(1)}, u32[]{:S(2)}, u32[]{:S(2)}) collective-permute-start(bf16[3,64,256]{2,1,0:T(8,128)(2,1)S(1)} %collective-permute-done.30.refs_8_), channel_id=1, source_target_pairs={{0,4},{1,5},{2,6},{3,7},{4,0},{5,1},{6,2},{7,3},{8,12},{9,13},{10,... | collective-permute-start | bytes 294920 | tf_op jit(solution)/shard_map/ppermute | solution.py:24
  94.2 5.4 %collective-permute-start.36 = (f32[3,3,32,256]{3,2,1,0:T(8,128)S(1)}, f32[3,3,32,256]{3,2,1,0:T(8,128)S(1)}, u32[]{:S(2)}, u32[]{:S(2)}) collective-permute-start(f32[3,3,32,256]{3,2,1,0:T(8,128)S(1)} %get-tuple-element.84), channel_id=1, source_target_pairs={{0,1},{1,0},{2,3},{3,2},{4,5},{5,4},{6,7},{7,6},{8,9},{9,8},{10,11... | collective-permute-start | bytes 884744 | tf_op jit(solution)/shard_map/ppermute | solution.py:24
  96.4 0.7 copy-start.4
  98.9 2.0 %collective-permute-start.45 = (bf16[256,1024]{1,0:T(8,128)(2,1)S(1)}, bf16[256,1024]{1,0:T(8,128)(2,1)S(1)}, u32[]{:S(2)}, u32[]{:S(2)}) collective-permute-start(bf16[256,1024]{1,0:T(8,128)(2,1)S(1)} %get-tuple-element.93), channel_id=1, source_target_pairs={{0,1},{1,0},{2,3},{3,2},{4,5},{5,4},{6,7},{7,6},{8,9},{9,8},{10,11... | collective-permute-start | bytes 1572872 | tf_op jit(solution)/shard_map/ppermute | solution.py:24

commit v10 on v7

--- a/solution.py
+++ b/solution.py
@@ -227,26 +227,35 @@
 def reduce_chips(pieces):
     depth = lax.axis_size("dev") // Z_UNIT
     own_here, own_next, near_x, near_y, near_across = pieces[:5]
-    total, early, late = None, (), ()
+    column = [[own_here], [own_next]] + [[pieces[4 * zj - 3]] for zj in range(2, depth)]
+    early, late, sums = (), (), [None] * depth
+
+    def rise(zj):
+        top = 1 << zj.bit_length() - 1
+        sums[zj] = hop(add_all(*column[zj]).astype(jnp.bfloat16), (zj - top or top) * Z_UNIT)
+        column[0 if zj == top else top].append(sums[zj])
+
     for upper in reversed(range(3, depth, 2)):
-        own_up, up_x, up_y, up_across = pieces[4 * upper - 3 : 4 * upper + 1]
-        own_low, low_x, low_y, low_across = pieces[4 * upper - 7 : 4 * upper - 3]
+        up_x, up_y, up_across = pieces[4 * upper - 2 : 4 * upper + 1]
+        low_x, low_y, low_across = pieces[4 * upper - 6 : 4 * upper - 3]
         from_x = hop(after(up_across, *late), X_STEP)
         from_y = hop(after(low_across, *late), Y_STEP)
         up_x = hop(after(up_x, *late), X_STEP)
         up_y = hop(add_all(up_y, from_x).astype(jnp.bfloat16), Y_STEP)
         low_x = hop(add_all(low_x, from_y).astype(jnp.bfloat16), X_STEP)
         low_y = hop(after(low_y, from_x), Y_STEP)
-        up = hop(add_all(own_up, up_x, up_y).astype(jnp.bfloat16), upper * Z_UNIT)
-        low = hop(add_all(own_low, low_x, low_y).astype(jnp.bfloat16), (upper - 1) * Z_UNIT)
-        total = add_all(up, low) if total is None else add_all(total, up, low)
+        column[upper] += [up_x, up_y]
+        column[upper - 1] += [low_x, low_y]
+        rise(upper)
+        rise(upper - 1)
         early, late = (from_y,), (up_y, up_x)
     near_across = hop(after(near_across, *early), X_STEP | Y_STEP)
     near_x = hop(after(near_x, *late), X_STEP)
     near_y = hop(after(near_y, *late), Y_STEP)
-    column = add_all(own_next, near_x[1], near_y[1], near_across[1]).astype(jnp.bfloat16)
-    here = add_all(own_here, near_x[0], near_y[0], near_across[0], hop(column, Z_UNIT))
-    return here if total is None else here + total
+    for zj in range(2):
+        column[zj] += [near_x[zj], near_y[zj], near_across[zj]]
+    rise(1)
+    return add_all(*column[0])
 
 
 def block_a_core(master, first, second, old_rows, old_cotangent, new_rows, old_slots, new_slots, live):

time: 92.6 us -> 92.3 us (level)
  waiting for transfers between devices: 29.9 us -> 27.1 us
  starting transfers between devices: 51 us -> 53.4 us
    ppermute x49, waiting for transfers between devices: 29.9 us -> 27.1 us  [hop(): lax.ppermute(block, 'dev', [(low, low ^ mask) for low in range(count)])]
    ppermute x49, starting transfers between devices: 51 us -> 53.4 us  [hop(): lax.ppermute(block, 'dev', [(low, low ^ mask) for low in range(count)])]
  transfers between devices with their start and end apart: 49 -> 49, of which waited for: 24 -> 27; matrix products, arithmetic and copies ran while one was open for 3% -> 3% of each run, Pallas kernels for 3% -> 3%
where the time goes in v10:
time: 92.3 us; the launch traced here: 92.1 us
  starting transfers between devices  53.4 us (58%)
  waiting for transfers between devices  27.1 us (29%)
  Pallas kernels  5.61 us (6%)
  local copies, waits for them, and re-layouts  2.31 us (3%)
  between operations  2.17 us (2%)
  other arithmetic  1.52 us (2%)
    ppermute x49, starting transfers between devices, hop(): lax.ppermute(block, 'dev', [(low, low ^ mask) for low in range(count)])  53.4 us
    ppermute x49, waiting for transfers between devices, hop(): lax.ppermute(block, 'dev', [(low, low ^ mask) for low in range(count)])  27.1 us
    pallas_call x1, Pallas kernels, backward(): pl.pallas_call(functools.partial(backward_kernel, count), out_shape=[one]...  3.17 us
    pallas_call x1, Pallas kernels, forward(): pl.pallas_call(functools.partial(forward_kernel, count), out_shape=[one,...  1.85 us
  transfers between devices with their start and end apart: 49, of which 27 were waited for; matrix products, arithmetic and copies ran while one was open for 3% of the time, Pallas kernels for 3%

profile of v10, /device:TPU:0, one launch (start us, length us, event | category | flops | bytes accessed | tf_op | source)
XLA Modules:
  0.0 92.1 jit_solution(14642312324676591737)
XLA Ops:
  0.6 0.5 collective-permute-start.3
  1.7 1.1 %dynamic-slice_bitcast_fusion.2 = (f32[3,32,256]{2,1,0:T(8,128)S(1)}, f32[1,3,32,256]{3,2,1,0:T(8,128)S(1)}, f32[1,3,32,256]{3,2,1,0:T(8,128)S(1)}, f32[3,32,256]{2,1,0:T(8,128)S(1)}) fusion(f32[2,3,32,256]{3,2,1,0:T(8,128)} %param.10, s32[]{:T(128)S(6)} %select_n.51, s32[]{:T(128)S(6)} %select_n.52, f32[2,3,32,256]{3,2,1,0:T(8,128)} %param.9), kind=kLoop, calls=%fused_computation.39 | loop fusion | bytes 786440 | tf_op jit(solution)/shard_map/jit(dynamic_index_in_dim)/squeeze | solution.py:266
  3.0 0.4 collective-permute-start.2
  3.9 0.6 transpose_rows.1
  4.9 4.0 %collective-permute-start.11 = (bf16[3,64,256]{2,1,0:T(8,128)(2,1)S(1)}, bf16[3,64,256]{2,1,0:T(8,128)(2,1)S(1)}, u32[]{:S(2)}, u32[]{:S(2)}) collective-permute-start(bf16[3,64,256]{2,1,0:T(8,128)(2,1)S(1)} %fusion.6.refs_0_), channel_id=1, source_target_pairs={{0,16},{1,17},{2,18},{3,19},{4,20},{5,21},{6,22},{7,23},{8,24},{9,... | collective-permute-start | bytes 294920 | tf_op jit(solution)/shard_map/ppermute | solution.py:24
  8.9 1.6 %collective-permute-start.8 = (bf16[3,64,256]{2,1,0:T(8,128)(2,1)S(1)}, bf16[3,64,256]{2,1,0:T(8,128)(2,1)S(1)}, u32[]{:S(2)}, u32[]{:S(2)}) collective-permute-start(bf16[3,64,256]{2,1,0:T(8,128)(2,1)S(1)} %fusion.6.refs_0_), channel_id=1, source_target_pairs={{0,8},{1,9},{2,10},{3,11},{4,12},{5,13},{6,14},{7,15},{8,0},{9,1},... | collective-permute-start | bytes 294920 | tf_op jit(solution)/shard_map/ppermute | solution.py:24
  10.5 1.5 %collective-permute-start.5 = (bf16[3,64,256]{2,1,0:T(8,128)(2,1)S(1)}, bf16[3,64,256]{2,1,0:T(8,128)(2,1)S(1)}, u32[]{:S(2)}, u32[]{:S(2)}) collective-permute-start(bf16[3,64,256]{2,1,0:T(8,128)(2,1)S(1)} %fusion.6.refs_0_), channel_id=1, source_target_pairs={{0,2},{1,3},{2,0},{3,1},{4,6},{5,7},{6,4},{7,5},{8,10},{9,11},{10,... | collective-permute-start | bytes 294920 | tf_op jit(solution)/shard_map/ppermute | solution.py:24
  12.0 1.5 %collective-permute-start.6 = (bf16[3,64,256]{2,1,0:T(8,128)(2,1)S(1)}, bf16[3,64,256]{2,1,0:T(8,128)(2,1)S(1)}, u32[]{:S(2)}, u32[]{:S(2)}) collective-permute-start(bf16[3,64,256]{2,1,0:T(8,128)(2,1)S(1)} %fusion.6.refs_0_), channel_id=1, source_target_pairs={{0,4},{1,5},{2,6},{3,7},{4,0},{5,1},{6,2},{7,3},{8,12},{9,13},{10,... | collective-permute-start | bytes 294920 | tf_op jit(solution)/shard_map/ppermute | solution.py:24
  13.5 0.8 collective-permute-done.11.refs_8_
  14.3 0.6 collective-permute-start.15
  14.9 1.5 %collective-permute-start.9 = (bf16[3,64,256]{2,1,0:T(8,128)(2,1)S(1)}, bf16[3,64,256]{2,1,0:T(8,128)(2,1)S(1)}, u32[]{:S(2)}, u32[]{:S(2)}) collective-permute-start(bf16[3,64,256]{2,1,0:T(8,128)(2,1)S(1)} %collective-permute-done.8.refs_4_), channel_id=1, source_target_pairs={{0,2},{1,3},{2,0},{3,1},{4,6},{5,7},{6,4},{7,5},{8,10},{9,11},{10,... | collective-permute-start | bytes 294920 | tf_op jit(solution)/shard_map/ppermute | solution.py:24
  16.4 1.5 %collective-permute-start.10 = (bf16[3,64,256]{2,1,0:T(8,128)(2,1)S(1)}, bf16[3,64,256]{2,1,0:T(8,128)(2,1)S(1)}, u32[]{:S(2)}, u32[]{:S(2)}) collective-permute-start(bf16[3,64,256]{2,1,0:T(8,128)(2,1)S(1)} %collective-permute-done.8.refs_4_), channel_id=1, source_target_pairs={{0,4},{1,5},{2,6},{3,7},{4,0},{5,1},{6,2},{7,3},{8,12},{9,13},{10,... | collective-permute-start | bytes 294920 | tf_op jit(solution)/shard_map/ppermute | solution.py:24
  17.9 0.5 collective-permute-start.12
  18.4 0.4 collective-permute-done.15.refs_12_
  18.9 0.6 collective-permute-done.9.refs_5_
  19.5 2.3 %collective-permute-start.16 = (bf16[3,64,256]{2,1,0:T(8,128)(2,1)S(1)}, bf16[3,64,256]{2,1,0:T(8,128)(2,1)S(1)}, u32[]{:S(2)}, u32[]{:S(2)}) collective-permute-start(bf16[3,64,256]{2,1,0:T(8,128)(2,1)S(1)} %collective-permute-done.15.refs_12_), channel_id=1, source_target_pairs={{0,2},{1,3},{2,0},{3,1},{4,6},{5,7},{6,4},{7,5},{8,10},{9,11},{10,... | collective-permute-start | bytes 294920 | tf_op jit(solution)/shard_map/ppermute | solution.py:24
  21.8 1.6 %collective-permute-start.18 = (bf16[3,64,256]{2,1,0:T(8,128)(2,1)S(1)}, bf16[3,64,256]{2,1,0:T(8,128)(2,1)S(1)}, u32[]{:S(2)}, u32[]{:S(2)}) collective-permute-start(bf16[3,64,256]{2,1,0:T(8,128)(2,1)S(1)} %collective-permute-done.15.refs_12_), channel_id=1, source_target_pairs={{0,4},{1,5},{2,6},{3,7},{4,0},{5,1},{6,2},{7,3},{8,12},{9,13},{10,... | collective-permute-start | bytes 294920 | tf_op jit(solution)/shard_map/ppermute | solution.py:24
  23.8 1.6 %collective-permute-start.14 = (bf16[3,64,256]{2,1,0:T(8,128)(2,1)S(1)}, bf16[3,64,256]{2,1,0:T(8,128)(2,1)S(1)}, u32[]{:S(2)}, u32[]{:S(2)}) collective-permute-start(bf16[3,64,256]{2,1,0:T(8,128)(2,1)S(1)} %collective-permute-done.11.refs_8_), channel_id=1, source_target_pairs={{0,4},{1,5},{2,6},{3,7},{4,0},{5,1},{6,2},{7,3},{8,12},{9,13},{10,... | collective-permute-start | bytes 294920 | tf_op jit(solution)/shard_map/ppermute | solution.py:24
  25.4 0.5 collective-permute-start.13
  25.9 0.8 collective-permute-done.18.refs_14_
  26.8 0.7 collective-permute-start.19
  27.5 1.0 %collective-permute-start.17 = (bf16[3,64,256]{2,1,0:T(8,128)(2,1)S(1)}, bf16[3,64,256]{2,1,0:T(8,128)(2,1)S(1)}, u32[]{:S(2)}, u32[]{:S(2)}) collective-permute-start(bf16[3,64,256]{2,1,0:T(8,128)(2,1)S(1)} %collective-permute-done.12.refs_9_), channel_id=1, source_target_pairs={{0,4},{1,5},{2,6},{3,7},{4,0},{5,1},{6,2},{7,3},{8,12},{9,13},{10,... | collective-permute-start | bytes 294920 | tf_op jit(solution)/shard_map/ppermute | solution.py:24
  29.2 0.6 collective-permute-done.14.refs_10_
  30.1 1.3 %collective-permute-done.19.refs_15_ = bf16[3,64,256]{2,1,0:T(8,128)(2,1)S(1)} collective-permute-done((bf16[3,64,256]{2,1,0:T(8,128)(2,1)S(1)}, bf16[3,64,256]{2,1,0:T(8,128)(2,1)S(1)}, u32[]{:S(2)}, u32[]{:S(2)}) %collective-permute-start.19) | collective-permute-done | bytes 98336 | tf_op jit(solution)/shard_map/ppermute | solution.py:24
  31.4 0.7 collective-permute-done.17.refs_11_
  32.1 3.2 %slot_gradients.1 = (bf16[3,64,256]{2,1,0:T(8,128)(2,1)S(1)}, bf16[3,64,256]{2,1,0:T(8,128)(2,1)S(1)}, bf16[2,3,64,256]{3,2,1,0:T(8,128)(2,1)S(1)}, bf16[2,3,64,...) custom-call(s32[32]{0:T(128)S(1)} %copy-done.3, ...), custom_call_target="tpu_custom_call" | custom-call | flops 1610612736 | bytes 7340032 | tf_op jit(solution)/shard_map/slot_gradients/pallas_call | solution.py:148
  35.3 1.4 %collective-permute-start.22 = (bf16[3,64,256]{2,1,0:T(8,128)(2,1)S(1)}, bf16[3,64,256]{2,1,0:T(8,128)(2,1)S(1)}, u32[]{:S(2)}, u32[]{:S(2)}) collective-permute-start(bf16[3,64,256]{2,1,0:T(8,128)(2,1)S(1)} %get-tuple-element.65), channel_id=1, source_target_pairs={{0,2},{1,3},{2,0},{3,1},{4,6},{5,7},{6,4},{7,5},{8,10},{9,11},{10,... | collective-permute-start | bytes 294920 | tf_op jit(solution)/shard_map/ppermute | solution.py:24
  36.7 1.7 %collective-permute-start.20 = (bf16[3,64,256]{2,1,0:T(8,128)(2,1)S(1)}, bf16[3,64,256]{2,1,0:T(8,128)(2,1)S(1)}, u32[]{:S(2)}, u32[]{:S(2)}) collective-permute-start(bf16[3,64,256]{2,1,0:T(8,128)(2,1)S(1)} %get-tuple-element.63), channel_id=1, source_target_pairs={{0,4},{1,5},{2,6},{3,7},{4,0},{5,1},{6,2},{7,3},{8,12},{9,13},{10,... | collective-permute-start | bytes 294920 | tf_op jit(solution)/shard_map/ppermute | solution.py:24
  38.4 2.5 %collective-permute-done.22 = bf16[3,64,256]{2,1,0:T(8,128)(2,1)S(1)} collective-permute-done((bf16[3,64,256]{2,1,0:T(8,128)(2,1)S(1)}, bf16[3,64,256]{2,1,0:T(8,128)(2,1)S(1)}, u32[]{:S(2)}, u32[]{:S(2)}) %collective-permute-start.22) | collective-permute-done | bytes 98336 | tf_op jit(solution)/shard_map/ppermute | solution.py:24
  40.9 0.9 collective-permute-start.25
  41.8 0.5 collective-permute-done.20
  42.3 1.0 %collective-permute-start.21 = (bf16[3,64,256]{2,1,0:T(8,128)(2,1)S(1)}, bf16[3,64,256]{2,1,0:T(8,128)(2,1)S(1)}, u32[]{:S(2)}, u32[]{:S(2)}) collective-permute-start(bf16[3,64,256]{2,1,0:T(8,128)(2,1)S(1)} %add_convert_fusion.3), channel_id=1, source_target_pairs={{0,2},{1,3},{2,0},{3,1},{4,6},{5,7},{6,4},{7,5},{8,10},{9,11},{10,... | collective-permute-start | bytes 294920 | tf_op jit(solution)/shard_map/ppermute | solution.py:24
  43.3 1.0 %collective-permute-start.23 = (bf16[3,64,256]{2,1,0:T(8,128)(2,1)S(1)}, bf16[3,64,256]{2,1,0:T(8,128)(2,1)S(1)}, u32[]{:S(2)}, u32[]{:S(2)}) collective-permute-start(bf16[3,64,256]{2,1,0:T(8,128)(2,1)S(1)} %get-tuple-element.66), channel_id=1, source_target_pairs={{0,4},{1,5},{2,6},{3,7},{4,0},{5,1},{6,2},{7,3},{8,12},{9,13},{10,... | collective-permute-start | bytes 294920 | tf_op jit(solution)/shard_map/ppermute | solution.py:24
  44.3 3.4 %collective-permute-done.25 = bf16[3,64,256]{2,1,0:T(8,128)(2,1)S(1)} collective-permute-done((bf16[3,64,256]{2,1,0:T(8,128)(2,1)S(1)}, bf16[3,64,256]{2,1,0:T(8,128)(2,1)S(1)}, u32[]{:S(2)}, u32[]{:S(2)}) %collective-permute-start.25) | collective-permute-done | bytes 98336 | tf_op jit(solution)/shard_map/ppermute | solution.py:24
  47.7 1.0 %collective-permute-start.26 = (bf16[3,64,256]{2,1,0:T(8,128)(2,1)S(1)}, bf16[3,64,256]{2,1,0:T(8,128)(2,1)S(1)}, u32[]{:S(2)}, u32[]{:S(2)}) collective-permute-start(bf16[3,64,256]{2,1,0:T(8,128)(2,1)S(1)} %add_convert_fusion.1), channel_id=1, source_target_pairs={{0,8},{1,9},{2,10},{3,11},{4,12},{5,13},{6,14},{7,15},{8,0},{9,1},... | collective-permute-start | bytes 294920 | tf_op jit(solution)/shard_map/ppermute | solution.py:24
  48.7 1.8 %collective-permute-start.30 = (bf16[2,3,64,256]{3,2,1,0:T(8,128)(2,1)S(1)}, bf16[2,3,64,256]{3,2,1,0:T(8,128)(2,1)S(1)}, u32[]{:S(2)}, u32[]{:S(2)}) collective-permute-start(bf16[2,3,64,256]{3,2,1,0:T(8,128)(2,1)S(1)} %get-tuple-element.75), channel_id=1, source_target_pairs={{0,6},{1,7},{2,4},{3,5},{4,2},{5,3},{6,0},{7,1},{8,14},{9,15},{10,... | collective-permute-start | bytes 589832 | tf_op jit(solution)/shard_map/ppermute | solution.py:24
  50.6 1.0 %collective-permute-start.28 = (bf16[2,3,64,256]{3,2,1,0:T(8,128)(2,1)S(1)}, bf16[2,3,64,256]{3,2,1,0:T(8,128)(2,1)S(1)}, u32[]{:S(2)}, u32[]{:S(2)}) collective-permute-start(bf16[2,3,64,256]{3,2,1,0:T(8,128)(2,1)S(1)} %get-tuple-element.71), channel_id=1, source_target_pairs={{0,2},{1,3},{2,0},{3,1},{4,6},{5,7},{6,4},{7,5},{8,10},{9,11},{10,... | collective-permute-start | bytes 589832 | tf_op jit(solution)/shard_map/ppermute | solution.py:24
  51.5 0.7 collective-permute-start.29
  52.5 3.0 %collective-permute-start.27 = (bf16[3,64,256]{2,1,0:T(8,128)(2,1)S(1)}, bf16[3,64,256]{2,1,0:T(8,128)(2,1)S(1)}, u32[]{:S(2)}, u32[]{:S(2)}) collective-permute-start(bf16[3,64,256]{2,1,0:T(8,128)(2,1)S(1)} %add_convert_fusion), channel_id=1, source_target_pairs={{0,16},{1,17},{2,18},{3,19},{4,20},{5,21},{6,22},{7,23},{8,24},{9,... | collective-permute-start | bytes 294920 | tf_op jit(solution)/shard_map/ppermute | solution.py:24
  55.5 1.8 %collective-permute-done.28 = bf16[2,3,64,256]{3,2,1,0:T(8,128)(2,1)S(1)} collective-permute-done((bf16[2,3,64,256]{3,2,1,0:T(8,128)(2,1)S(1)}, bf16[2,3,64,256]{3,2,1,0:T(8,128)(2,1)S(1)}, u32[]{:S(2)}, u32[]{:S(2)}) %collective-permute-start.28) | collective-permute-done | bytes 196640 | tf_op jit(solution)/shard_map/ppermute | solution.py:24
  57.5 1.2 %collective-permute-start.31 = (bf16[3,64,256]{2,1,0:T(8,128)(2,1)S(1)}, bf16[3,64,256]{2,1,0:T(8,128)(2,1)S(1)}, u32[]{:S(2)}, u32[]{:S(2)}) collective-permute-start(bf16[3,64,256]{2,1,0:T(8,128)(2,1)S(1)} %fusion.4), channel_id=1, source_target_pairs={{0,8},{1,9},{2,10},{3,11},{4,12},{5,13},{6,14},{7,15},{8,0},{9,1},... | collective-permute-start | bytes 294920 | tf_op jit(solution)/shard_map/ppermute | solution.py:24
  58.6 2.3 %collective-permute-done.27 = bf16[3,64,256]{2,1,0:T(8,128)(2,1)S(1)} collective-permute-done((bf16[3,64,256]{2,1,0:T(8,128)(2,1)S(1)}, bf16[3,64,256]{2,1,0:T(8,128)(2,1)S(1)}, u32[]{:S(2)}, u32[]{:S(2)}) %collective-permute-start.27) | collective-permute-done | bytes 98336 | tf_op jit(solution)/shard_map/ppermute | solution.py:24
  60.9 2.2 %collective-permute-done.31 = bf16[3,64,256]{2,1,0:T(8,128)(2,1)S(1)} collective-permute-done((bf16[3,64,256]{2,1,0:T(8,128)(2,1)S(1)}, bf16[3,64,256]{2,1,0:T(8,128)(2,1)S(1)}, u32[]{:S(2)}, u32[]{:S(2)}) %collective-permute-start.31) | collective-permute-done | bytes 98336 | tf_op jit(solution)/shard_map/ppermute | solution.py:24
  63.4 2.4 %collective-permute-start.39 = (bf16[3,64,256]{2,1,0:T(8,128)(2,1)S(1)}, bf16[3,64,256]{2,1,0:T(8,128)(2,1)S(1)}, u32[]{:S(2)}, u32[]{:S(2)}) collective-permute-start(bf16[3,64,256]{2,1,0:T(8,128)(2,1)S(1)} %get-tuple-element.88.refs_0_), channel_id=1, source_target_pairs={{0,16},{1,17},{2,18},{3,19},{4,20},{5,21},{6,22},{7,23},{8,24},{9,... | collective-permute-start | bytes 294920 | tf_op jit(solution)/shard_map/ppermute | solution.py:24
  65.7 0.8 collective-permute-start.36
  66.5 1.7 %collective-permute-start.34 = (bf16[3,64,256]{2,1,0:T(8,128)(2,1)S(1)}, bf16[3,64,256]{2,1,0:T(8,128)(2,1)S(1)}, u32[]{:S(2)}, u32[]{:S(2)}) collective-permute-start(bf16[3,64,256]{2,1,0:T(8,128)(2,1)S(1)} %get-tuple-element.88.refs_0_), channel_id=1, source_target_pairs={{0,4},{1,5},{2,6},{3,7},{4,0},{5,1},{6,2},{7,3},{8,12},{9,13},{10,... | collective-permute-start | bytes 294920 | tf_op jit(solution)/shard_map/ppermute | solution.py:24
  68.2 0.8 collective-permute-start.33
  69.1 0.6 collective-permute-done.39.refs_8_
  70.0 0.7 collective-permute-done.36.refs_4_
  70.7 1.3 %collective-permute-start.37 = (bf16[3,64,256]{2,1,0:T(8,128)(2,1)S(1)}, bf16[3,64,256]{2,1,0:T(8,128)(2,1)S(1)}, u32[]{:S(2)}, u32[]{:S(2)}) collective-permute-start(bf16[3,64,256]{2,1,0:T(8,128)(2,1)S(1)} %collective-permute-done.36.refs_4_), channel_id=1, source_target_pairs={{0,2},{1,3},{2,0},{3,1},{4,6},{5,7},{6,4},{7,5},{8,10},{9,11},{10,... | collective-permute-start | bytes 294920 | tf_op jit(solution)/shard_map/ppermute | solution.py:24
  72.2 1.6 %collective-permute-done.33.refs_1_ = bf16[3,64,256]{2,1,0:T(8,128)(2,1)S(1)} collective-permute-done((bf16[3,64,256]{2,1,0:T(8,128)(2,1)S(1)}, bf16[3,64,256]{2,1,0:T(8,128)(2,1)S(1)}, u32[]{:S(2)}, u32[]{:S(2)}) %collective-permute-start.33) | collective-permute-done | bytes 98336 | tf_op jit(solution)/shard_map/ppermute | solution.py:24
  73.9 1.2 %collective-permute-start.40 = (bf16[3,64,256]{2,1,0:T(8,128)(2,1)S(1)}, bf16[3,64,256]{2,1,0:T(8,128)(2,1)S(1)}, u32[]{:S(2)}, u32[]{:S(2)}) collective-permute-start(bf16[3,64,256]{2,1,0:T(8,128)(2,1)S(1)} %collective-permute-done.39.refs_8_), channel_id=1, source_target_pairs={{0,2},{1,3},{2,0},{3,1},{4,6},{5,7},{6,4},{7,5},{8,10},{9,11},{10,... | collective-permute-start | bytes 294920 | tf_op jit(solution)/shard_map/ppermute | solution.py:24
  75.0 1.1 %collective-permute-done.37.refs_5_ = bf16[3,64,256]{2,1,0:T(8,128)(2,1)S(1)} collective-permute-done((bf16[3,64,256]{2,1,0:T(8,128)(2,1)S(1)}, bf16[3,64,256]{2,1,0:T(8,128)(2,1)S(1)}, u32[]{:S(2)}, u32[]{:S(2)}) %collective-permute-start.37) | collective-permute-done | bytes 98336 | tf_op jit(solution)/shard_map/ppermute | solution.py:24
  76.2 0.8 collective-permute-start.46
  77.0 0.9 collective-permute-start.44
  78.0 1.8 %collective-permute-start.35 = (bf16[3,64,256]{2,1,0:T(8,128)(2,1)S(1)}, bf16[3,64,256]{2,1,0:T(8,128)(2,1)S(1)}, u32[]{:S(2)}, u32[]{:S(2)}) collective-permute-start(bf16[3,64,256]{2,1,0:T(8,128)(2,1)S(1)} %collective-permute-done.33.refs_1_), channel_id=1, source_target_pairs={{0,4},{1,5},{2,6},{3,7},{4,0},{5,1},{6,2},{7,3},{8,12},{9,13},{10,... | collective-permute-start | bytes 294920 | tf_op jit(solution)/shard_map/ppermute | solution.py:24
  80.1 1.1 %collective-permute-start.41 = (bf16[3,64,256]{2,1,0:T(8,128)(2,1)S(1)}, bf16[3,64,256]{2,1,0:T(8,128)(2,1)S(1)}, u32[]{:S(2)}, u32[]{:S(2)}) collective-permute-start(bf16[3,64,256]{2,1,0:T(8,128)(2,1)S(1)} %collective-permute-done.38.refs_6_), channel_id=1, source_target_pairs={{0,2},{1,3},{2,0},{3,1},{4,6},{5,7},{6,4},{7,5},{8,10},{9,11},{10,... | collective-permute-start | bytes 294920 | tf_op jit(solution)/shard_map/ppermute | solution.py:24
  81.2 0.4 collective-permute-done.44.refs_13_
  81.6 1.2 %collective-permute-start.45 = (bf16[3,64,256]{2,1,0:T(8,128)(2,1)S(1)}, bf16[3,64,256]{2,1,0:T(8,128)(2,1)S(1)}, u32[]{:S(2)}, u32[]{:S(2)}) collective-permute-start(bf16[3,64,256]{2,1,0:T(8,128)(2,1)S(1)} %collective-permute-done.40.refs_9_), channel_id=1, source_target_pairs={{0,4},{1,5},{2,6},{3,7},{4,0},{5,1},{6,2},{7,3},{8,12},{9,13},{10,... | collective-permute-start | bytes 294920 | tf_op jit(solution)/shard_map/ppermute | solution.py:24
  82.8 1.4 %collective-permute-start.47 = (bf16[3,64,256]{2,1,0:T(8,128)(2,1)S(1)}, bf16[3,64,256]{2,1,0:T(8,128)(2,1)S(1)}, u32[]{:S(2)}, u32[]{:S(2)}) collective-permute-start(bf16[3,64,256]{2,1,0:T(8,128)(2,1)S(1)} %collective-permute-done.46.refs_14_), channel_id=1, source_target_pairs={{0,2},{1,3},{2,0},{3,1},{4,6},{5,7},{6,4},{7,5},{8,10},{9,11},{10,... | collective-permute-start | bytes 294920 | tf_op jit(solution)/shard_map/ppermute | solution.py:24
  84.7 2.8 %collective-permute-done.47.refs_15_ = bf16[3,64,256]{2,1,0:T(8,128)(2,1)S(1)} collective-permute-done((bf16[3,64,256]{2,1,0:T(8,128)(2,1)S(1)}, bf16[3,64,256]{2,1,0:T(8,128)(2,1)S(1)}, u32[]{:S(2)}, u32[]{:S(2)}) %collective-permute-start.47) | collective-permute-done | bytes 98336 | tf_op jit(solution)/shard_map/ppermute | solution.py:24
  87.5 1.9 %expert_outputs.1 = (bf16[256,1024]{1,0:T(8,128)(2,1)S(1)}, bf16[256,1024]{1,0:T(8,128)(2,1)S(1)}, s32[1]{0:T(128)}) custom-call(s32[32]{0:T(128)S(1)} %copy-done.4, bf16[3,64,256]{2,1,0:T(8,128)(2,1)S(1)} %get-tuple-element.88.refs_0_, bf16[3,64,256]{2,1,0:T(8,128)(2,1)S(1)} %collective-permute-done.33.refs_1_, ...), custom_call_target="tpu_custom_call" | custom-call | flops 805306368 | bytes 3670016 | tf_op jit(solution)/shard_map/expert_outputs/pallas_call | solution.py:174
  89.5 0.8 slice_bitcast_fusion
  91.3 0.8 select_bitcast_fusion
  (67 shorter events, 4.9 us)
Async XLA Ops:
  0.6 2.8 %collective-permute-start.3 = (bf16[256,1024]{1,0:T(8,128)(2,1)}, bf16[256,1024]{1,0:T(8,128)(2,1)S(1)}, u32[]{:S(2)}, u32[]{:S(2)}) collective-permute-start(bf16[256,1024]{1,0:T(8,128)(2,1)} %bitcast.65), channel_id=1, source_target_pairs={{0,1},{1,0},{2,3},{3,2},{4,5},{5,4},{6,7},{7,6},{8,9},{9,8},{10,11... | collective-permute-start | bytes 1572872 | tf_op jit(solution)/shard_map/ppermute | solution.py:24
  1.1 2.5 %collective-permute-start.4 = (bf16[256,1024]{1,0:T(8,128)(2,1)}, bf16[256,1024]{1,0:T(8,128)(2,1)S(1)}, u32[]{:S(2)}, u32[]{:S(2)}) collective-permute-start(bf16[256,1024]{1,0:T(8,128)(2,1)} %bitcast.68), channel_id=1, source_target_pairs={{0,1},{1,0},{2,3},{3,2},{4,5},{5,4},{6,7},{7,6},{8,9},{9,8},{10,11... | collective-permute-start | bytes 1572872 | tf_op jit(solution)/shard_map/ppermute | solution.py:24
  1.2 3.6 %collective-permute-start.1 = (bf16[256,1024]{1,0:T(8,128)(2,1)}, bf16[256,1024]{1,0:T(8,128)(2,1)S(1)}, u32[]{:S(2)}, u32[]{:S(2)}) collective-permute-start(bf16[256,1024]{1,0:T(8,128)(2,1)} %bitcast.71), channel_id=1, source_target_pairs={{0,1},{1,0},{2,3},{3,2},{4,5},{5,4},{6,7},{7,6},{8,9},{9,8},{10,11... | collective-permute-start | bytes 1572872 | tf_op jit(solution)/shard_map/ppermute | solution.py:24
  1.7 1.1 %copy-start.5 = (f32[2,3,32,256]{3,2,1,0:T(8,128)S(1)}, f32[2,3,32,256]{3,2,1,0:T(8,128)}, u32[]{:S(2)}) copy-start(f32[2,3,32,256]{3,2,1,0:T(8,128)} %param.11) | copy-start | bytes 589828
  1.7 2.0 %copy-start.1 = (bf16[1,256,1024]{2,1,0:T(8,128)(2,1)S(1)}, bf16[1,256,1024]{2,1,0:T(8,128)(2,1)}, u32[]{:S(2)}) copy-start(bf16[1,256,1024]{2,1,0:T(8,128)(2,1)} %param.13) | copy-start | bytes 1572868
  2.8 1.1 %copy-start = (bf16[1,256,1024]{2,1,0:T(8,128)(2,1)S(1)}, bf16[1,256,1024]{2,1,0:T(8,128)(2,1)}, u32[]{:S(2)}) copy-start(bf16[1,256,1024]{2,1,0:T(8,128)(2,1)} %param.12) | copy-start | bytes 1572868
  2.9 2.0 %collective-permute-start = (f32[3,3,32,256]{3,2,1,0:T(8,128)S(1)}, f32[3,3,32,256]{3,2,1,0:T(8,128)S(1)}, u32[]{:S(2)}, u32[]{:S(2)}) collective-permute-start(f32[3,3,32,256]{3,2,1,0:T(8,128)S(1)} %pad_maximum_fusion.1), channel_id=1, source_target_pairs={{0,1},{1,0},{2,3},{3,2},{4,5},{5,4},{6,7},{7,6},{8,9},{9,8},{10,11... | collective-permute-start | bytes 884744 | tf_op jit(solution)/shard_map/ppermute | solution.py:24
  3.0 1.8 %collective-permute-start.2 = (s32[1]{0:T(128)}, s32[1]{0:T(128)}, u32[]{:S(2)}, u32[]{:S(2)}) collective-permute-start(s32[1]{0:T(128)} %param.17), channel_id=1, source_target_pairs={{0,1},{1,0},{2,3},{3,2},{4,5},{5,4},{6,7},{7,6},{8,9},{9,8},{10,11... | collective-permute-start | bytes 20 | tf_op jit(solution)/shard_map/ppermute | solution.py:24
  4.9 27.2 %copy-start.3 = (s32[32]{0:T(128)S(1)}, s32[32]{0:T(128)}, u32[]{:S(2)}) copy-start(s32[32]{0:T(128)} %slots.2) | copy-start | bytes 388
  4.9 9.3 %collective-permute-start.11 = (bf16[3,64,256]{2,1,0:T(8,128)(2,1)S(1)}, bf16[3,64,256]{2,1,0:T(8,128)(2,1)S(1)}, u32[]{:S(2)}, u32[]{:S(2)}) collective-permute-start(bf16[3,64,256]{2,1,0:T(8,128)(2,1)S(1)} %fusion.6.refs_0_), channel_id=1, source_target_pairs={{0,16},{1,17},{2,18},{3,19},{4,20},{5,21},{6,22},{7,23},{8,24},{9,... | collective-permute-start | bytes 294920 | tf_op jit(solution)/shard_map/ppermute | solution.py:24
  8.9 6.0 %collective-permute-start.8 = (bf16[3,64,256]{2,1,0:T(8,128)(2,1)S(1)}, bf16[3,64,256]{2,1,0:T(8,128)(2,1)S(1)}, u32[]{:S(2)}, u32[]{:S(2)}) collective-permute-start(bf16[3,64,256]{2,1,0:T(8,128)(2,1)S(1)} %fusion.6.refs_0_), channel_id=1, source_target_pairs={{0,8},{1,9},{2,10},{3,11},{4,12},{5,13},{6,14},{7,15},{8,0},{9,1},... | collective-permute-start | bytes 294920 | tf_op jit(solution)/shard_map/ppermute | solution.py:24
  10.5 5.9 %collective-permute-start.5 = (bf16[3,64,256]{2,1,0:T(8,128)(2,1)S(1)}, bf16[3,64,256]{2,1,0:T(8,128)(2,1)S(1)}, u32[]{:S(2)}, u32[]{:S(2)}) collective-permute-start(bf16[3,64,256]{2,1,0:T(8,128)(2,1)S(1)} %fusion.6.refs_0_), channel_id=1, source_target_pairs={{0,2},{1,3},{2,0},{3,1},{4,6},{5,7},{6,4},{7,5},{8,10},{9,11},{10,... | collective-permute-start | bytes 294920 | tf_op jit(solution)/shard_map/ppermute | solution.py:24
  12.0 5.9 %collective-permute-start.6 = (bf16[3,64,256]{2,1,0:T(8,128)(2,1)S(1)}, bf16[3,64,256]{2,1,0:T(8,128)(2,1)S(1)}, u32[]{:S(2)}, u32[]{:S(2)}) collective-permute-start(bf16[3,64,256]{2,1,0:T(8,128)(2,1)S(1)} %fusion.6.refs_0_), channel_id=1, source_target_pairs={{0,4},{1,5},{2,6},{3,7},{4,0},{5,1},{6,2},{7,3},{8,12},{9,13},{10,... | collective-permute-start | bytes 294920 | tf_op jit(solution)/shard_map/ppermute | solution.py:24
  14.3 4.6 %collective-permute-start.15 = (bf16[3,64,256]{2,1,0:T(8,128)(2,1)S(1)}, bf16[3,64,256]{2,1,0:T(8,128)(2,1)S(1)}, u32[]{:S(2)}, u32[]{:S(2)}) collective-permute-start(bf16[3,64,256]{2,1,0:T(8,128)(2,1)S(1)} %collective-permute-done.11.refs_8_), channel_id=1, source_target_pairs={{0,8},{1,9},{2,10},{3,11},{4,12},{5,13},{6,14},{7,15},{8,0},{9,1},... | collective-permute-start | bytes 294920 | tf_op jit(solution)/shard_map/ppermute | solution.py:24
  14.9 4.6 %collective-permute-start.9 = (bf16[3,64,256]{2,1,0:T(8,128)(2,1)S(1)}, bf16[3,64,256]{2,1,0:T(8,128)(2,1)S(1)}, u32[]{:S(2)}, u32[]{:S(2)}) collective-permute-start(bf16[3,64,256]{2,1,0:T(8,128)(2,1)S(1)} %collective-permute-done.8.refs_4_), channel_id=1, source_target_pairs={{0,2},{1,3},{2,0},{3,1},{4,6},{5,7},{6,4},{7,5},{8,10},{9,11},{10,... | collective-permute-start | bytes 294920 | tf_op jit(solution)/shard_map/ppermute | solution.py:24
  16.4 7.4 %collective-permute-start.10 = (bf16[3,64,256]{2,1,0:T(8,128)(2,1)S(1)}, bf16[3,64,256]{2,1,0:T(8,128)(2,1)S(1)}, u32[]{:S(2)}, u32[]{:S(2)}) collective-permute-start(bf16[3,64,256]{2,1,0:T(8,128)(2,1)S(1)} %collective-permute-done.8.refs_4_), channel_id=1, source_target_pairs={{0,4},{1,5},{2,6},{3,7},{4,0},{5,1},{6,2},{7,3},{8,12},{9,13},{10,... | collective-permute-start | bytes 294920 | tf_op jit(solution)/shard_map/ppermute | solution.py:24
  17.9 7.5 %collective-permute-start.12 = (bf16[3,64,256]{2,1,0:T(8,128)(2,1)S(1)}, bf16[3,64,256]{2,1,0:T(8,128)(2,1)S(1)}, u32[]{:S(2)}, u32[]{:S(2)}) collective-permute-start(bf16[3,64,256]{2,1,0:T(8,128)(2,1)S(1)} %collective-permute-done.11.refs_8_), channel_id=1, source_target_pairs={{0,2},{1,3},{2,0},{3,1},{4,6},{5,7},{6,4},{7,5},{8,10},{9,11},{10,... | collective-permute-start | bytes 294920 | tf_op jit(solution)/shard_map/ppermute | solution.py:24
  19.5 6.4 %collective-permute-start.16 = (bf16[3,64,256]{2,1,0:T(8,128)(2,1)S(1)}, bf16[3,64,256]{2,1,0:T(8,128)(2,1)S(1)}, u32[]{:S(2)}, u32[]{:S(2)}) collective-permute-start(bf16[3,64,256]{2,1,0:T(8,128)(2,1)S(1)} %collective-permute-done.15.refs_12_), channel_id=1, source_target_pairs={{0,2},{1,3},{2,0},{3,1},{4,6},{5,7},{6,4},{7,5},{8,10},{9,11},{10,... | collective-permute-start | bytes 294920 | tf_op jit(solution)/shard_map/ppermute | solution.py:24
  21.8 5.0 %collective-permute-start.18 = (bf16[3,64,256]{2,1,0:T(8,128)(2,1)S(1)}, bf16[3,64,256]{2,1,0:T(8,128)(2,1)S(1)}, u32[]{:S(2)}, u32[]{:S(2)}) collective-permute-start(bf16[3,64,256]{2,1,0:T(8,128)(2,1)S(1)} %collective-permute-done.15.refs_12_), channel_id=1, source_target_pairs={{0,4},{1,5},{2,6},{3,7},{4,0},{5,1},{6,2},{7,3},{8,12},{9,13},{10,... | collective-permute-start | bytes 294920 | tf_op jit(solution)/shard_map/ppermute | solution.py:24
  23.4 5.8 %collective-permute-start.7 = (bf16[3,64,256]{2,1,0:T(8,128)(2,1)S(1)}, bf16[3,64,256]{2,1,0:T(8,128)(2,1)S(1)}, u32[]{:S(2)}, u32[]{:S(2)}) collective-permute-start(bf16[3,64,256]{2,1,0:T(8,128)(2,1)S(1)} %collective-permute-done.5.refs_1_), channel_id=1, source_target_pairs={{0,4},{1,5},{2,6},{3,7},{4,0},{5,1},{6,2},{7,3},{8,12},{9,13},{10,... | collective-permute-start | bytes 294920 | tf_op jit(solution)/shard_map/ppermute | solution.py:24
  23.8 6.0 %collective-permute-start.14 = (bf16[3,64,256]{2,1,0:T(8,128)(2,1)S(1)}, bf16[3,64,256]{2,1,0:T(8,128)(2,1)S(1)}, u32[]{:S(2)}, u32[]{:S(2)}) collective-permute-start(bf16[3,64,256]{2,1,0:T(8,128)(2,1)S(1)} %collective-permute-done.11.refs_8_), channel_id=1, source_target_pairs={{0,4},{1,5},{2,6},{3,7},{4,0},{5,1},{6,2},{7,3},{8,12},{9,13},{10,... | collective-permute-start | bytes 294920 | tf_op jit(solution)/shard_map/ppermute | solution.py:24
  25.4 4.6 %collective-permute-start.13 = (bf16[3,64,256]{2,1,0:T(8,128)(2,1)S(1)}, bf16[3,64,256]{2,1,0:T(8,128)(2,1)S(1)}, u32[]{:S(2)}, u32[]{:S(2)}) collective-permute-start(bf16[3,64,256]{2,1,0:T(8,128)(2,1)S(1)} %collective-permute-done.10.refs_6_), channel_id=1, source_target_pairs={{0,2},{1,3},{2,0},{3,1},{4,6},{5,7},{6,4},{7,5},{8,10},{9,11},{10,... | collective-permute-start | bytes 294920 | tf_op jit(solution)/shard_map/ppermute | solution.py:24
  26.8 4.6 %collective-permute-start.19 = (bf16[3,64,256]{2,1,0:T(8,128)(2,1)S(1)}, bf16[3,64,256]{2,1,0:T(8,128)(2,1)S(1)}, u32[]{:S(2)}, u32[]{:S(2)}) collective-permute-start(bf16[3,64,256]{2,1,0:T(8,128)(2,1)S(1)} %collective-permute-done.18.refs_14_), channel_id=1, source_target_pairs={{0,2},{1,3},{2,0},{3,1},{4,6},{5,7},{6,4},{7,5},{8,10},{9,11},{10,... | collective-permute-start | bytes 294920 | tf_op jit(solution)/shard_map/ppermute | solution.py:24
  27.5 4.6 %collective-permute-start.17 = (bf16[3,64,256]{2,1,0:T(8,128)(2,1)S(1)}, bf16[3,64,256]{2,1,0:T(8,128)(2,1)S(1)}, u32[]{:S(2)}, u32[]{:S(2)}) collective-permute-start(bf16[3,64,256]{2,1,0:T(8,128)(2,1)S(1)} %collective-permute-done.12.refs_9_), channel_id=1, source_target_pairs={{0,4},{1,5},{2,6},{3,7},{4,0},{5,1},{6,2},{7,3},{8,12},{9,13},{10,... | collective-permute-start | bytes 294920 | tf_op jit(solution)/shard_map/ppermute | solution.py:24
  35.3 5.6 %collective-permute-start.22 = (bf16[3,64,256]{2,1,0:T(8,128)(2,1)S(1)}, bf16[3,64,256]{2,1,0:T(8,128)(2,1)S(1)}, u32[]{:S(2)}, u32[]{:S(2)}) collective-permute-start(bf16[3,64,256]{2,1,0:T(8,128)(2,1)S(1)} %get-tuple-element.65), channel_id=1, source_target_pairs={{0,2},{1,3},{2,0},{3,1},{4,6},{5,7},{6,4},{7,5},{8,10},{9,11},{10,... | collective-permute-start | bytes 294920 | tf_op jit(solution)/shard_map/ppermute | solution.py:24
  36.7 5.6 %collective-permute-start.20 = (bf16[3,64,256]{2,1,0:T(8,128)(2,1)S(1)}, bf16[3,64,256]{2,1,0:T(8,128)(2,1)S(1)}, u32[]{:S(2)}, u32[]{:S(2)}) collective-permute-start(bf16[3,64,256]{2,1,0:T(8,128)(2,1)S(1)} %get-tuple-element.63), channel_id=1, source_target_pairs={{0,4},{1,5},{2,6},{3,7},{4,0},{5,1},{6,2},{7,3},{8,12},{9,13},{10,... | collective-permute-start | bytes 294920 | tf_op jit(solution)/shard_map/ppermute | solution.py:24
  38.3 6.0 %collective-permute-start.24 = (bf16[3,64,256]{2,1,0:T(8,128)(2,1)S(1)}, bf16[3,64,256]{2,1,0:T(8,128)(2,1)S(1)}, u32[]{:S(2)}, u32[]{:S(2)}) collective-permute-start(bf16[3,64,256]{2,1,0:T(8,128)(2,1)S(1)} %get-tuple-element.68), channel_id=1, source_target_pairs={{0,2},{1,3},{2,0},{3,1},{4,6},{5,7},{6,4},{7,5},{8,10},{9,11},{10,... | collective-permute-start | bytes 294920 | tf_op jit(solution)/shard_map/ppermute | solution.py:24
  40.9 6.8 %collective-permute-start.25 = (bf16[3,64,256]{2,1,0:T(8,128)(2,1)S(1)}, bf16[3,64,256]{2,1,0:T(8,128)(2,1)S(1)}, u32[]{:S(2)}, u32[]{:S(2)}) collective-permute-start(bf16[3,64,256]{2,1,0:T(8,128)(2,1)S(1)} %add_convert_fusion.2), channel_id=1, source_target_pairs={{0,4},{1,5},{2,6},{3,7},{4,0},{5,1},{6,2},{7,3},{8,12},{9,13},{10,... | collective-permute-start | bytes 294920 | tf_op jit(solution)/shard_map/ppermute | solution.py:24
  42.3 9.2 %collective-permute-start.21 = (bf16[3,64,256]{2,1,0:T(8,128)(2,1)S(1)}, bf16[3,64,256]{2,1,0:T(8,128)(2,1)S(1)}, u32[]{:S(2)}, u32[]{:S(2)}) collective-permute-start(bf16[3,64,256]{2,1,0:T(8,128)(2,1)S(1)} %add_convert_fusion.3), channel_id=1, source_target_pairs={{0,2},{1,3},{2,0},{3,1},{4,6},{5,7},{6,4},{7,5},{8,10},{9,11},{10,... | collective-permute-start | bytes 294920 | tf_op jit(solution)/shard_map/ppermute | solution.py:24
  43.3 8.9 %collective-permute-start.23 = (bf16[3,64,256]{2,1,0:T(8,128)(2,1)S(1)}, bf16[3,64,256]{2,1,0:T(8,128)(2,1)S(1)}, u32[]{:S(2)}, u32[]{:S(2)}) collective-permute-start(bf16[3,64,256]{2,1,0:T(8,128)(2,1)S(1)} %get-tuple-element.66), channel_id=1, source_target_pairs={{0,4},{1,5},{2,6},{3,7},{4,0},{5,1},{6,2},{7,3},{8,12},{9,13},{10,... | collective-permute-start | bytes 294920 | tf_op jit(solution)/shard_map/ppermute | solution.py:24
  47.7 4.7 %collective-permute-start.26 = (bf16[3,64,256]{2,1,0:T(8,128)(2,1)S(1)}, bf16[3,64,256]{2,1,0:T(8,128)(2,1)S(1)}, u32[]{:S(2)}, u32[]{:S(2)}) collective-permute-start(bf16[3,64,256]{2,1,0:T(8,128)(2,1)S(1)} %add_convert_fusion.1), channel_id=1, source_target_pairs={{0,8},{1,9},{2,10},{3,11},{4,12},{5,13},{6,14},{7,15},{8,0},{9,1},... | collective-permute-start | bytes 294920 | tf_op jit(solution)/shard_map/ppermute | solution.py:24
  48.7 6.8 %collective-permute-start.30 = (bf16[2,3,64,256]{3,2,1,0:T(8,128)(2,1)S(1)}, bf16[2,3,64,256]{3,2,1,0:T(8,128)(2,1)S(1)}, u32[]{:S(2)}, u32[]{:S(2)}) collective-permute-start(bf16[2,3,64,256]{3,2,1,0:T(8,128)(2,1)S(1)} %get-tuple-element.75), channel_id=1, source_target_pairs={{0,6},{1,7},{2,4},{3,5},{4,2},{5,3},{6,0},{7,1},{8,14},{9,15},{10,... | collective-permute-start | bytes 589832 | tf_op jit(solution)/shard_map/ppermute | solution.py:24
  50.6 6.7 %collective-permute-start.28 = (bf16[2,3,64,256]{3,2,1,0:T(8,128)(2,1)S(1)}, bf16[2,3,64,256]{3,2,1,0:T(8,128)(2,1)S(1)}, u32[]{:S(2)}, u32[]{:S(2)}) collective-permute-start(bf16[2,3,64,256]{3,2,1,0:T(8,128)(2,1)S(1)} %get-tuple-element.71), channel_id=1, source_target_pairs={{0,2},{1,3},{2,0},{3,1},{4,6},{5,7},{6,4},{7,5},{8,10},{9,11},{10,... | collective-permute-start | bytes 589832 | tf_op jit(solution)/shard_map/ppermute | solution.py:24
  51.5 5.9 %collective-permute-start.29 = (bf16[2,3,64,256]{3,2,1,0:T(8,128)(2,1)S(1)}, bf16[2,3,64,256]{3,2,1,0:T(8,128)(2,1)S(1)}, u32[]{:S(2)}, u32[]{:S(2)}) collective-permute-start(bf16[2,3,64,256]{3,2,1,0:T(8,128)(2,1)S(1)} %get-tuple-element.73), channel_id=1, source_target_pairs={{0,4},{1,5},{2,6},{3,7},{4,0},{5,1},{6,2},{7,3},{8,12},{9,13},{10,... | collective-permute-start | bytes 589832 | tf_op jit(solution)/shard_map/ppermute | solution.py:24
  52.5 8.5 %collective-permute-start.27 = (bf16[3,64,256]{2,1,0:T(8,128)(2,1)S(1)}, bf16[3,64,256]{2,1,0:T(8,128)(2,1)S(1)}, u32[]{:S(2)}, u32[]{:S(2)}) collective-permute-start(bf16[3,64,256]{2,1,0:T(8,128)(2,1)S(1)} %add_convert_fusion), channel_id=1, source_target_pairs={{0,16},{1,17},{2,18},{3,19},{4,20},{5,21},{6,22},{7,23},{8,24},{9,... | collective-permute-start | bytes 294920 | tf_op jit(solution)/shard_map/ppermute | solution.py:24
  57.5 5.6 %collective-permute-start.31 = (bf16[3,64,256]{2,1,0:T(8,128)(2,1)S(1)}, bf16[3,64,256]{2,1,0:T(8,128)(2,1)S(1)}, u32[]{:S(2)}, u32[]{:S(2)}) collective-permute-start(bf16[3,64,256]{2,1,0:T(8,128)(2,1)S(1)} %fusion.4), channel_id=1, source_target_pairs={{0,8},{1,9},{2,10},{3,11},{4,12},{5,13},{6,14},{7,15},{8,0},{9,1},... | collective-permute-start | bytes 294920 | tf_op jit(solution)/shard_map/ppermute | solution.py:24
  63.4 6.3 %collective-permute-start.39 = (bf16[3,64,256]{2,1,0:T(8,128)(2,1)S(1)}, bf16[3,64,256]{2,1,0:T(8,128)(2,1)S(1)}, u32[]{:S(2)}, u32[]{:S(2)}) collective-permute-start(bf16[3,64,256]{2,1,0:T(8,128)(2,1)S(1)} %get-tuple-element.88.refs_0_), channel_id=1, source_target_pairs={{0,16},{1,17},{2,18},{3,19},{4,20},{5,21},{6,22},{7,23},{8,24},{9,... | collective-permute-start | bytes 294920 | tf_op jit(solution)/shard_map/ppermute | solution.py:24
  65.7 5.0 %collective-permute-start.36 = (bf16[3,64,256]{2,1,0:T(8,128)(2,1)S(1)}, bf16[3,64,256]{2,1,0:T(8,128)(2,1)S(1)}, u32[]{:S(2)}, u32[]{:S(2)}) collective-permute-start(bf16[3,64,256]{2,1,0:T(8,128)(2,1)S(1)} %get-tuple-element.88.refs_0_), channel_id=1, source_target_pairs={{0,8},{1,9},{2,10},{3,11},{4,12},{5,13},{6,14},{7,15},{8,0},{9,1},... | collective-permute-start | bytes 294920 | tf_op jit(solution)/shard_map/ppermute | solution.py:24
  66.5 5.6 %collective-permute-start.34 = (bf16[3,64,256]{2,1,0:T(8,128)(2,1)S(1)}, bf16[3,64,256]{2,1,0:T(8,128)(2,1)S(1)}, u32[]{:S(2)}, u32[]{:S(2)}) collective-permute-start(bf16[3,64,256]{2,1,0:T(8,128)(2,1)S(1)} %get-tuple-element.88.refs_0_), channel_id=1, source_target_pairs={{0,4},{1,5},{2,6},{3,7},{4,0},{5,1},{6,2},{7,3},{8,12},{9,13},{10,... | collective-permute-start | bytes 294920 | tf_op jit(solution)/shard_map/ppermute | solution.py:24
  68.2 5.5 %collective-permute-start.33 = (bf16[3,64,256]{2,1,0:T(8,128)(2,1)S(1)}, bf16[3,64,256]{2,1,0:T(8,128)(2,1)S(1)}, u32[]{:S(2)}, u32[]{:S(2)}) collective-permute-start(bf16[3,64,256]{2,1,0:T(8,128)(2,1)S(1)} %get-tuple-element.88.refs_0_), channel_id=1, source_target_pairs={{0,2},{1,3},{2,0},{3,1},{4,6},{5,7},{6,4},{7,5},{8,10},{9,11},{10,... | collective-permute-start | bytes 294920 | tf_op jit(solution)/shard_map/ppermute | solution.py:24
  69.7 5.3 %collective-permute-start.43 = (bf16[3,64,256]{2,1,0:T(8,128)(2,1)S(1)}, bf16[3,64,256]{2,1,0:T(8,128)(2,1)S(1)}, u32[]{:S(2)}, u32[]{:S(2)}) collective-permute-start(bf16[3,64,256]{2,1,0:T(8,128)(2,1)S(1)} %collective-permute-done.39.refs_8_), channel_id=1, source_target_pairs={{0,8},{1,9},{2,10},{3,11},{4,12},{5,13},{6,14},{7,15},{8,0},{9,1},... | collective-permute-start | bytes 294920 | tf_op jit(solution)/shard_map/ppermute | solution.py:24
  70.7 5.5 %collective-permute-start.37 = (bf16[3,64,256]{2,1,0:T(8,128)(2,1)S(1)}, bf16[3,64,256]{2,1,0:T(8,128)(2,1)S(1)}, u32[]{:S(2)}, u32[]{:S(2)}) collective-permute-start(bf16[3,64,256]{2,1,0:T(8,128)(2,1)S(1)} %collective-permute-done.36.refs_4_), channel_id=1, source_target_pairs={{0,2},{1,3},{2,0},{3,1},{4,6},{5,7},{6,4},{7,5},{8,10},{9,11},{10,... | collective-permute-start | bytes 294920 | tf_op jit(solution)/shard_map/ppermute | solution.py:24
  73.8 6.0 %collective-permute-start.38 = (bf16[3,64,256]{2,1,0:T(8,128)(2,1)S(1)}, bf16[3,64,256]{2,1,0:T(8,128)(2,1)S(1)}, u32[]{:S(2)}, u32[]{:S(2)}) collective-permute-start(bf16[3,64,256]{2,1,0:T(8,128)(2,1)S(1)} %collective-permute-done.36.refs_4_), channel_id=1, source_target_pairs={{0,4},{1,5},{2,6},{3,7},{4,0},{5,1},{6,2},{7,3},{8,12},{9,13},{10,... | collective-permute-start | bytes 294920 | tf_op jit(solution)/shard_map/ppermute | solution.py:24
  73.9 6.2 %collective-permute-start.40 = (bf16[3,64,256]{2,1,0:T(8,128)(2,1)S(1)}, bf16[3,64,256]{2,1,0:T(8,128)(2,1)S(1)}, u32[]{:S(2)}, u32[]{:S(2)}) collective-permute-start(bf16[3,64,256]{2,1,0:T(8,128)(2,1)S(1)} %collective-permute-done.39.refs_8_), channel_id=1, source_target_pairs={{0,2},{1,3},{2,0},{3,1},{4,6},{5,7},{6,4},{7,5},{8,10},{9,11},{10,... | collective-permute-start | bytes 294920 | tf_op jit(solution)/shard_map/ppermute | solution.py:24
  76.2 6.6 %collective-permute-start.46 = (bf16[3,64,256]{2,1,0:T(8,128)(2,1)S(1)}, bf16[3,64,256]{2,1,0:T(8,128)(2,1)S(1)}, u32[]{:S(2)}, u32[]{:S(2)}) collective-permute-start(bf16[3,64,256]{2,1,0:T(8,128)(2,1)S(1)} %collective-permute-done.43.refs_12_), channel_id=1, source_target_pairs={{0,4},{1,5},{2,6},{3,7},{4,0},{5,1},{6,2},{7,3},{8,12},{9,13},{10,... | collective-permute-start | bytes 294920 | tf_op jit(solution)/shard_map/ppermute | solution.py:24
  77.0 4.6 %collective-permute-start.44 = (bf16[3,64,256]{2,1,0:T(8,128)(2,1)S(1)}, bf16[3,64,256]{2,1,0:T(8,128)(2,1)S(1)}, u32[]{:S(2)}, u32[]{:S(2)}) collective-permute-start(bf16[3,64,256]{2,1,0:T(8,128)(2,1)S(1)} %collective-permute-done.43.refs_12_), channel_id=1, source_target_pairs={{0,2},{1,3},{2,0},{3,1},{4,6},{5,7},{6,4},{7,5},{8,10},{9,11},{10,... | collective-permute-start | bytes 294920 | tf_op jit(solution)/shard_map/ppermute | solution.py:24
  78.0 9.5 %copy-start.2 = (bf16[1,256,1024]{2,1,0:T(8,128)(2,1)S(1)}, bf16[1,256,1024]{2,1,0:T(8,128)(2,1)}, u32[]{:S(2)}) copy-start(bf16[1,256,1024]{2,1,0:T(8,128)(2,1)} %param.14) | copy-start | bytes 1572868
  78.0 6.4 %collective-permute-start.35 = (bf16[3,64,256]{2,1,0:T(8,128)(2,1)S(1)}, bf16[3,64,256]{2,1,0:T(8,128)(2,1)S(1)}, u32[]{:S(2)}, u32[]{:S(2)}) collective-permute-start(bf16[3,64,256]{2,1,0:T(8,128)(2,1)S(1)} %collective-permute-done.33.refs_1_), channel_id=1, source_target_pairs={{0,4},{1,5},{2,6},{3,7},{4,0},{5,1},{6,2},{7,3},{8,12},{9,13},{10,... | collective-permute-start | bytes 294920 | tf_op jit(solution)/shard_map/ppermute | solution.py:24
  79.8 4.6 %collective-permute-start.42 = (bf16[3,64,256]{2,1,0:T(8,128)(2,1)S(1)}, bf16[3,64,256]{2,1,0:T(8,128)(2,1)S(1)}, u32[]{:S(2)}, u32[]{:S(2)}) collective-permute-start(bf16[3,64,256]{2,1,0:T(8,128)(2,1)S(1)} %collective-permute-done.39.refs_8_), channel_id=1, source_target_pairs={{0,4},{1,5},{2,6},{3,7},{4,0},{5,1},{6,2},{7,3},{8,12},{9,13},{10,... | collective-permute-start | bytes 294920 | tf_op jit(solution)/shard_map/ppermute | solution.py:24
  80.1 4.6 %collective-permute-start.41 = (bf16[3,64,256]{2,1,0:T(8,128)(2,1)S(1)}, bf16[3,64,256]{2,1,0:T(8,128)(2,1)S(1)}, u32[]{:S(2)}, u32[]{:S(2)}) collective-permute-start(bf16[3,64,256]{2,1,0:T(8,128)(2,1)S(1)} %collective-permute-done.38.refs_6_), channel_id=1, source_target_pairs={{0,2},{1,3},{2,0},{3,1},{4,6},{5,7},{6,4},{7,5},{8,10},{9,11},{10,... | collective-permute-start | bytes 294920 | tf_op jit(solution)/shard_map/ppermute | solution.py:24
  81.6 5.8 %collective-permute-start.45 = (bf16[3,64,256]{2,1,0:T(8,128)(2,1)S(1)}, bf16[3,64,256]{2,1,0:T(8,128)(2,1)S(1)}, u32[]{:S(2)}, u32[]{:S(2)}) collective-permute-start(bf16[3,64,256]{2,1,0:T(8,128)(2,1)S(1)} %collective-permute-done.40.refs_9_), channel_id=1, source_target_pairs={{0,4},{1,5},{2,6},{3,7},{4,0},{5,1},{6,2},{7,3},{8,12},{9,13},{10,... | collective-permute-start | bytes 294920 | tf_op jit(solution)/shard_map/ppermute | solution.py:24
  82.8 4.6 %collective-permute-start.47 = (bf16[3,64,256]{2,1,0:T(8,128)(2,1)S(1)}, bf16[3,64,256]{2,1,0:T(8,128)(2,1)S(1)}, u32[]{:S(2)}, u32[]{:S(2)}) collective-permute-start(bf16[3,64,256]{2,1,0:T(8,128)(2,1)S(1)} %collective-permute-done.46.refs_14_), channel_id=1, source_target_pairs={{0,2},{1,3},{2,0},{3,1},{4,6},{5,7},{6,4},{7,5},{8,10},{9,11},{10,... | collective-permute-start | bytes 294920 | tf_op jit(solution)/shard_map/ppermute | solution.py:24
  84.3 3.1 %copy-start.4 = (s32[32]{0:T(128)S(1)}, s32[32]{0:T(128)}, u32[]{:S(2)}) copy-start(s32[32]{0:T(128)} %slots.3) | copy-start | bytes 388
  84.3 5.1 %collective-permute-start.32 = (f32[3,3,32,256]{3,2,1,0:T(8,128)S(1)}, f32[3,3,32,256]{3,2,1,0:T(8,128)S(1)}, u32[]{:S(2)}, u32[]{:S(2)}) collective-permute-start(f32[3,3,32,256]{3,2,1,0:T(8,128)S(1)} %get-tuple-element.95), channel_id=1, source_target_pairs={{0,1},{1,0},{2,3},{3,2},{4,5},{5,4},{6,7},{7,6},{8,9},{9,8},{10,11... | collective-permute-start | bytes 884744 | tf_op jit(solution)/shard_map/ppermute | solution.py:24
  89.3 2.0 %collective-permute-start.48 = (bf16[256,1024]{1,0:T(8,128)(2,1)S(1)}, bf16[256,1024]{1,0:T(8,128)(2,1)S(1)}, u32[]{:S(2)}, u32[]{:S(2)}) collective-permute-start(bf16[256,1024]{1,0:T(8,128)(2,1)S(1)} %get-tuple-element.87), channel_id=1, source_target_pairs={{0,1},{1,0},{2,3},{3,2},{4,5},{5,4},{6,7},{7,6},{8,9},{9,8},{10,11... | collective-permute-start | bytes 1572872 | tf_op jit(solution)/shard_map/ppermute | solution.py:24

commit v11 on v6

--- a/solution.py
+++ b/solution.py
@@ -106,18 +106,25 @@
     gradient_rows(0, products, outs)
 
 
-def forward_kernel(count, slots, *refs):
+def expert_rows(y_ref, weights, out_ref):
+    gate_pre = jnp.dot(y_ref[...], weights[0], preferred_element_type=jnp.float32)
+    up_pre = jnp.dot(y_ref[...], weights[1], preferred_element_type=jnp.float32)
+    act = (gate_pre * jax.nn.sigmoid(gate_pre) * up_pre).astype(jnp.bfloat16)
+    result = lax.dot_general(act, weights[2], (((1,), (1,)), ((), ())), preferred_element_type=jnp.float32)
+    out_ref[...] = result.astype(jnp.bfloat16)
+
+
+def other_kernel(count, *refs):
     pieces = refs[:count]
-    own_y, other_y, own_out, other_out, matches, weights = refs[count:]
+    other_y, other_out, weights = refs[count:]
+    place_pieces(lax.axis_index("dev") // 2, pieces, weights)
+    expert_rows(other_y, weights, other_out)
+
+
+def own_kernel(slots, weights, own_y, own_out, matches):
     me_index = lax.axis_index("dev")
-    place_pieces(me_index // 2, pieces, weights)
     matches[0] = jnp.where(slots[me_index] == (me_index & CORE), 1, 0)
-    for y_ref, out_ref in ((other_y, other_out), (own_y, own_out)):
-        gate_pre = jnp.dot(y_ref[...], weights[0], preferred_element_type=jnp.float32)
-        up_pre = jnp.dot(y_ref[...], weights[1], preferred_element_type=jnp.float32)
-        act = (gate_pre * jax.nn.sigmoid(gate_pre) * up_pre).astype(jnp.bfloat16)
-        result = lax.dot_general(act, weights[2], (((1,), (1,)), ((), ())), preferred_element_type=jnp.float32)
-        out_ref[...] = result.astype(jnp.bfloat16)
+    expert_rows(own_y, weights, own_out)
 
 
 VMEM = pl.BlockSpec(memory_space=pltpu.VMEM)
@@ -173,20 +180,30 @@
     kinds, rows, units = pieces[0].shape
     tokens, width = own_y.shape
     one = jax.ShapeDtypeStruct((tokens, width), jnp.bfloat16)
-    return pl.pallas_call(
-        functools.partial(forward_kernel, count),
-        out_shape=[one, one, jax.ShapeDtypeStruct((1,), jnp.int32)],
-        in_specs=[SMEM] + [VMEM] * (count + 2),
-        out_specs=[VMEM, VMEM, SMEM],
-        scratch_shapes=[pltpu.VMEM((kinds, width, units), jnp.bfloat16)],
+    cost = pl.CostEstimate(
+        flops=6 * tokens * width * units,
+        bytes_accessed=4 * tokens * width + 6 * width * units,
+        transcendentals=tokens * units,
+    )
+    other_out, weights = pl.pallas_call(
+        functools.partial(other_kernel, count),
+        out_shape=[one, jax.ShapeDtypeStruct((kinds, width, units), jnp.bfloat16)],
+        in_specs=[VMEM] * (count + 1),
+        out_specs=[VMEM] * 2,
         compiler_params=params(),
-        cost_estimate=pl.CostEstimate(
-            flops=12 * tokens * width * units,
-            bytes_accessed=8 * tokens * width + 6 * width * units,
-            transcendentals=2 * tokens * units,
-        ),
-        name="expert_outputs",
-    )(slots, *pieces, own_y, other_y)
+        cost_estimate=cost,
+        name="other_outputs",
+    )(*pieces, other_y)
+    own_out, matches = pl.pallas_call(
+        own_kernel,
+        out_shape=[one, jax.ShapeDtypeStruct((1,), jnp.int32)],
+        in_specs=[SMEM, VMEM, VMEM],
+        out_specs=[VMEM, SMEM],
+        compiler_params=params(),
+        cost_estimate=cost,
+        name="own_outputs",
+    )(slots, weights, own_y)
+    return own_out, other_out, matches
 
 
 def after(value, *others):
@@ -270,10 +287,10 @@
     theirs = hop(jnp.stack([partners(master), partners(first), partners(second)]), CORE)
     other_y = hop(new_rows, CORE)
     other_live = hop(live, CORE)
+    theirs, other_x, other_c, other_y, other_live = lax.optimization_barrier(
+        (theirs, other_x, other_c, other_y, other_live)
+    )
     x_turned, c_turned = transposed(old_rows, other_x, old_cotangent, other_c)
-    theirs, other_y, other_live, x_turned, c_turned = lax.optimization_barrier(
-        (theirs, other_y, other_live, x_turned, c_turned)
-    )
     master_two = both_rows(mine(master), theirs[0])
     pieces = gather_chips(master_two.astype(jnp.bfloat16))
     grads = backward(
@@ -298,11 +315,11 @@
     updated = jnp.stack(updated)
     own_part = lax.dynamic_slice_in_dim(updated, core * local_rows, local_rows, 2)
     other_part = lax.dynamic_slice_in_dim(updated, (1 - core) * local_rows, local_rows, 2)
-    from_other = hop(other_part, CORE)
+    own_out, other_out, matches = forward(new_slots, new_pieces, new_rows, other_y)
+    from_other = hop(after(other_part, other_out), CORE)
     state = jnp.where(
         core == 0, jnp.stack([own_part, from_other], axis=1), jnp.stack([from_other, own_part], axis=1)
     )
-    own_out, other_out, matches = forward(new_slots, new_pieces, new_rows, other_y)
     new_outputs = jnp.where(matches[0] == 1, own_out, hop(other_out, CORE))
     return (state[0], state[1], state[2], new_outputs[None])
 

time: 90.5 us -> 91.8 us (1.014)
    dynamic_slice x1, local copies, waits for them, and re-layouts: 0.02 us -> 0.96 us  [partners(): return lax.dynamic_index_in_dim(state, 1 - core, 0, keepdims=False)]
    pallas_call x1 -> x2, Pallas kernels: 1.85 us -> 2.32 us  [the longest x1 1.54 us: forward(): pl.pallas_call(own_kernel, out_shape=[one, jax.ShapeDtypeStruct((1,), jnp...]
  transfers between devices with their start and end apart: 48 -> 48, of which waited for: 28 -> 25; matrix products, arithmetic and copies ran while one was open for 3% -> 4% of each run, Pallas kernels for 3% -> 2%
where the time goes in v11:
time: 91.8 us; the launch traced here: 91.5 us
  starting transfers between devices  49.9 us (54%)
  waiting for transfers between devices  28.8 us (31%)
  Pallas kernels  6.22 us (7%)
  local copies, waits for them, and re-layouts  2.93 us (3%)
  between operations  2.21 us (2%)
  other arithmetic  1.5 us (2%)
    ppermute x48, starting transfers between devices, hop(): lax.ppermute(block, 'dev', [(low, low ^ mask) for low in range(count)])  49.9 us
    ppermute x48, waiting for transfers between devices, hop(): lax.ppermute(block, 'dev', [(low, low ^ mask) for low in range(count)])  28.8 us
    pallas_call x1, Pallas kernels, backward(): pl.pallas_call(functools.partial(backward_kernel, count), out_shape=[one,...  3.3 us
  transfers between devices with their start and end apart: 48, of which 25 were waited for; matrix products, arithmetic and copies ran while one was open for 4% of the time, Pallas kernels for 2%

profile of v11, /device:TPU:0, one launch (start us, length us, event | category | flops | bytes accessed | tf_op | source)
XLA Modules:
  0.0 91.5 jit_solution(13747789379661384205)
XLA Ops:
  0.7 0.5 collective-permute-start.1
  1.2 0.4 collective-permute-start.3
  1.7 1.1 %dynamic-slice_bitcast_fusion.1 = (f32[3,32,256]{2,1,0:T(8,128)S(1)}, f32[1,3,32,256]{3,2,1,0:T(8,128)S(1)}, f32[1,3,32,256]{3,2,1,0:T(8,128)S(1)}, f32[3,32,256]{2,1,0:T(8,128)S(1)}) fusion(f32[2,3,32,256]{3,2,1,0:T(8,128)} %param.11, s32[]{:T(128)S(6)} %select_n.51, s32[]{:T(128)S(6)} %select_n.52, f32[2,3,32,256]{3,2,1,0:T(8,128)} %param.10), kind=kLoop, calls=%fused_computation.48 | loop fusion | bytes 786440 | tf_op jit(solution)/shard_map/jit(dynamic_index_in_dim)/squeeze | solution.py:275
  2.7 1.0 %constant_dynamic-slice_fusion.3 = (f32[1,3,32,256]{3,2,1,0:T(8,128)S(1)}, f32[3,32,256]{2,1,0:T(8,128)S(1)}) fusion(f32[2,3,32,256]{3,2,1,0:T(8,128)} %param.9, s32[]{:T(128)S(6)} %select_n.52, s32[]{:T(128)S(6)} %select_n.51), kind=kLoop, calls=%fused_computation.56 | loop fusion | bytes 393224 | tf_op jit(solution)/shard_map/jit(dynamic_index_in_dim)/dynamic_slice | solution.py:278
  3.9 0.4 collective-permute-start.4
  4.3 1.1 %collective-permute-done.4.other_live = s32[1]{0:T(128)} collective-permute-done((s32[1]{0:T(128)}, s32[1]{0:T(128)}, u32[]{:S(2)}, u32[]{:S(2)}) %collective-permute-start.4) | collective-permute-done | bytes 36 | tf_op jit(solution)/shard_map/ppermute | solution.py:24
  5.5 3.8 %collective-permute-start.11 = (bf16[3,64,256]{2,1,0:T(8,128)(2,1)S(1)}, bf16[3,64,256]{2,1,0:T(8,128)(2,1)S(1)}, u32[]{:S(2)}, u32[]{:S(2)}) collective-permute-start(bf16[3,64,256]{2,1,0:T(8,128)(2,1)S(1)} %fusion.17.refs_0_), channel_id=1, source_target_pairs={{0,16},{1,17},{2,18},{3,19},{4,20},{5,21},{6,22},{7,23},{8,24},{9,... | collective-permute-start | bytes 294920 | tf_op jit(solution)/shard_map/ppermute | solution.py:24
  9.4 1.6 %collective-permute-start.8 = (bf16[3,64,256]{2,1,0:T(8,128)(2,1)S(1)}, bf16[3,64,256]{2,1,0:T(8,128)(2,1)S(1)}, u32[]{:S(2)}, u32[]{:S(2)}) collective-permute-start(bf16[3,64,256]{2,1,0:T(8,128)(2,1)S(1)} %fusion.17.refs_0_), channel_id=1, source_target_pairs={{0,8},{1,9},{2,10},{3,11},{4,12},{5,13},{6,14},{7,15},{8,0},{9,1},... | collective-permute-start | bytes 294920 | tf_op jit(solution)/shard_map/ppermute | solution.py:24
  11.0 1.5 %collective-permute-start.5 = (bf16[3,64,256]{2,1,0:T(8,128)(2,1)S(1)}, bf16[3,64,256]{2,1,0:T(8,128)(2,1)S(1)}, u32[]{:S(2)}, u32[]{:S(2)}) collective-permute-start(bf16[3,64,256]{2,1,0:T(8,128)(2,1)S(1)} %fusion.17.refs_0_), channel_id=1, source_target_pairs={{0,2},{1,3},{2,0},{3,1},{4,6},{5,7},{6,4},{7,5},{8,10},{9,11},{10,... | collective-permute-start | bytes 294920 | tf_op jit(solution)/shard_map/ppermute | solution.py:24
  12.5 1.5 %collective-permute-start.6 = (bf16[3,64,256]{2,1,0:T(8,128)(2,1)S(1)}, bf16[3,64,256]{2,1,0:T(8,128)(2,1)S(1)}, u32[]{:S(2)}, u32[]{:S(2)}) collective-permute-start(bf16[3,64,256]{2,1,0:T(8,128)(2,1)S(1)} %fusion.17.refs_0_), channel_id=1, source_target_pairs={{0,4},{1,5},{2,6},{3,7},{4,0},{5,1},{6,2},{7,3},{8,12},{9,13},{10,... | collective-permute-start | bytes 294920 | tf_op jit(solution)/shard_map/ppermute | solution.py:24
  14.0 0.9 collective-permute-done.11.refs_8_
  14.9 0.6 collective-permute-start.15
  15.5 1.5 %collective-permute-start.9 = (bf16[3,64,256]{2,1,0:T(8,128)(2,1)S(1)}, bf16[3,64,256]{2,1,0:T(8,128)(2,1)S(1)}, u32[]{:S(2)}, u32[]{:S(2)}) collective-permute-start(bf16[3,64,256]{2,1,0:T(8,128)(2,1)S(1)} %collective-permute-done.8.refs_4_), channel_id=1, source_target_pairs={{0,2},{1,3},{2,0},{3,1},{4,6},{5,7},{6,4},{7,5},{8,10},{9,11},{10,... | collective-permute-start | bytes 294920 | tf_op jit(solution)/shard_map/ppermute | solution.py:24
  17.0 1.5 %collective-permute-start.10 = (bf16[3,64,256]{2,1,0:T(8,128)(2,1)S(1)}, bf16[3,64,256]{2,1,0:T(8,128)(2,1)S(1)}, u32[]{:S(2)}, u32[]{:S(2)}) collective-permute-start(bf16[3,64,256]{2,1,0:T(8,128)(2,1)S(1)} %collective-permute-done.8.refs_4_), channel_id=1, source_target_pairs={{0,4},{1,5},{2,6},{3,7},{4,0},{5,1},{6,2},{7,3},{8,12},{9,13},{10,... | collective-permute-start | bytes 294920 | tf_op jit(solution)/shard_map/ppermute | solution.py:24
  18.5 0.5 collective-permute-start.12
  19.1 0.4 collective-permute-done.15.refs_12_
  19.5 0.6 collective-permute-done.9.refs_5_
  20.1 2.3 %collective-permute-start.16 = (bf16[3,64,256]{2,1,0:T(8,128)(2,1)S(1)}, bf16[3,64,256]{2,1,0:T(8,128)(2,1)S(1)}, u32[]{:S(2)}, u32[]{:S(2)}) collective-permute-start(bf16[3,64,256]{2,1,0:T(8,128)(2,1)S(1)} %collective-permute-done.15.refs_12_), channel_id=1, source_target_pairs={{0,2},{1,3},{2,0},{3,1},{4,6},{5,7},{6,4},{7,5},{8,10},{9,11},{10,... | collective-permute-start | bytes 294920 | tf_op jit(solution)/shard_map/ppermute | solution.py:24
  22.4 1.6 %collective-permute-start.18 = (bf16[3,64,256]{2,1,0:T(8,128)(2,1)S(1)}, bf16[3,64,256]{2,1,0:T(8,128)(2,1)S(1)}, u32[]{:S(2)}, u32[]{:S(2)}) collective-permute-start(bf16[3,64,256]{2,1,0:T(8,128)(2,1)S(1)} %collective-permute-done.15.refs_12_), channel_id=1, source_target_pairs={{0,4},{1,5},{2,6},{3,7},{4,0},{5,1},{6,2},{7,3},{8,12},{9,13},{10,... | collective-permute-start | bytes 294920 | tf_op jit(solution)/shard_map/ppermute | solution.py:24
  24.0 0.4 collective-permute-start.7
  24.4 1.6 %collective-permute-start.14 = (bf16[3,64,256]{2,1,0:T(8,128)(2,1)S(1)}, bf16[3,64,256]{2,1,0:T(8,128)(2,1)S(1)}, u32[]{:S(2)}, u32[]{:S(2)}) collective-permute-start(bf16[3,64,256]{2,1,0:T(8,128)(2,1)S(1)} %collective-permute-done.11.refs_8_), channel_id=1, source_target_pairs={{0,4},{1,5},{2,6},{3,7},{4,0},{5,1},{6,2},{7,3},{8,12},{9,13},{10,... | collective-permute-start | bytes 294920 | tf_op jit(solution)/shard_map/ppermute | solution.py:24
  26.1 0.5 collective-permute-start.13
  26.5 0.9 collective-permute-done.18.refs_14_
  27.4 0.7 collective-permute-start.19
  28.1 1.0 %collective-permute-start.17 = (bf16[3,64,256]{2,1,0:T(8,128)(2,1)S(1)}, bf16[3,64,256]{2,1,0:T(8,128)(2,1)S(1)}, u32[]{:S(2)}, u32[]{:S(2)}) collective-permute-start(bf16[3,64,256]{2,1,0:T(8,128)(2,1)S(1)} %collective-permute-done.12.refs_9_), channel_id=1, source_target_pairs={{0,4},{1,5},{2,6},{3,7},{4,0},{5,1},{6,2},{7,3},{8,12},{9,13},{10,... | collective-permute-start | bytes 294920 | tf_op jit(solution)/shard_map/ppermute | solution.py:24
  29.8 0.6 transpose_rows.1
  30.7 1.3 %collective-permute-done.19.refs_15_ = bf16[3,64,256]{2,1,0:T(8,128)(2,1)S(1)} collective-permute-done((bf16[3,64,256]{2,1,0:T(8,128)(2,1)S(1)}, bf16[3,64,256]{2,1,0:T(8,128)(2,1)S(1)}, u32[]{:S(2)}, u32[]{:S(2)}) %collective-permute-start.19) | collective-permute-done | bytes 98336 | tf_op jit(solution)/shard_map/ppermute | solution.py:24
  32.0 0.7 collective-permute-done.17.refs_11_
  32.7 3.3 %slot_gradients.1 = (bf16[3,64,256]{2,1,0:T(8,128)(2,1)S(1)}, bf16[3,64,256]{2,1,0:T(8,128)(2,1)S(1)}, bf16[2,3,64,256]{3,2,1,0:T(8,128)(2,1)S(1)}, bf16[3,64,25...) custom-call(s32[32]{0:T(128)S(1)} %copy-done.4, ...), custom_call_target="tpu_custom_call" | custom-call | flops 1610612736 | bytes 7340032 | tf_op jit(solution)/shard_map/slot_gradients/pallas_call | solution.py:157
  36.0 1.1 %collective-permute-start.20 = (bf16[2,3,64,256]{3,2,1,0:T(8,128)(2,1)S(1)}, bf16[2,3,64,256]{3,2,1,0:T(8,128)(2,1)S(1)}, u32[]{:S(2)}, u32[]{:S(2)}) collective-permute-start(bf16[2,3,64,256]{3,2,1,0:T(8,128)(2,1)S(1)} %get-tuple-element.62), channel_id=1, source_target_pairs={{0,4},{1,5},{2,6},{3,7},{4,0},{5,1},{6,2},{7,3},{8,12},{9,13},{10,... | collective-permute-start | bytes 589832 | tf_op jit(solution)/shard_map/ppermute | solution.py:24
  37.1 2.0 %collective-permute-start.22 = (bf16[2,3,64,256]{3,2,1,0:T(8,128)(2,1)S(1)}, bf16[2,3,64,256]{3,2,1,0:T(8,128)(2,1)S(1)}, u32[]{:S(2)}, u32[]{:S(2)}) collective-permute-start(bf16[2,3,64,256]{3,2,1,0:T(8,128)(2,1)S(1)} %get-tuple-element.65), channel_id=1, source_target_pairs={{0,2},{1,3},{2,0},{3,1},{4,6},{5,7},{6,4},{7,5},{8,10},{9,11},{10,... | collective-permute-start | bytes 589832 | tf_op jit(solution)/shard_map/ppermute | solution.py:24
  39.1 3.6 %collective-permute-done.20 = bf16[2,3,64,256]{3,2,1,0:T(8,128)(2,1)S(1)} collective-permute-done((bf16[2,3,64,256]{3,2,1,0:T(8,128)(2,1)S(1)}, bf16[2,3,64,256]{3,2,1,0:T(8,128)(2,1)S(1)}, u32[]{:S(2)}, u32[]{:S(2)}) %collective-permute-start.20) | collective-permute-done | bytes 196640 | tf_op jit(solution)/shard_map/ppermute | solution.py:24
  42.7 1.5 %collective-permute-start.21 = (bf16[3,64,256]{2,1,0:T(8,128)(2,1)S(1)}, bf16[3,64,256]{2,1,0:T(8,128)(2,1)S(1)}, u32[]{:S(2)}, u32[]{:S(2)}) collective-permute-start(bf16[3,64,256]{2,1,0:T(8,128)(2,1)S(1)} %fusion.13), channel_id=1, source_target_pairs={{0,2},{1,3},{2,0},{3,1},{4,6},{5,7},{6,4},{7,5},{8,10},{9,11},{10,... | collective-permute-start | bytes 294920 | tf_op jit(solution)/shard_map/ppermute | solution.py:24
  44.3 2.5 %collective-permute-start.23 = (bf16[3,64,256]{2,1,0:T(8,128)(2,1)S(1)}, bf16[3,64,256]{2,1,0:T(8,128)(2,1)S(1)}, u32[]{:S(2)}, u32[]{:S(2)}) collective-permute-start(bf16[3,64,256]{2,1,0:T(8,128)(2,1)S(1)} %fusion.10), channel_id=1, source_target_pairs={{0,4},{1,5},{2,6},{3,7},{4,0},{5,1},{6,2},{7,3},{8,12},{9,13},{10,... | collective-permute-start | bytes 294920 | tf_op jit(solution)/shard_map/ppermute | solution.py:24
  46.9 2.5 %collective-permute-done.23 = bf16[3,64,256]{2,1,0:T(8,128)(2,1)S(1)} collective-permute-done((bf16[3,64,256]{2,1,0:T(8,128)(2,1)S(1)}, bf16[3,64,256]{2,1,0:T(8,128)(2,1)S(1)}, u32[]{:S(2)}, u32[]{:S(2)}) %collective-permute-start.23) | collective-permute-done | bytes 98336 | tf_op jit(solution)/shard_map/ppermute | solution.py:24
  49.5 0.8 collective-permute-start.24
  50.3 2.0 %collective-permute-start.29 = (bf16[3,64,256]{2,1,0:T(8,128)(2,1)S(1)}, bf16[3,64,256]{2,1,0:T(8,128)(2,1)S(1)}, u32[]{:S(2)}, u32[]{:S(2)}) collective-permute-start(bf16[3,64,256]{2,1,0:T(8,128)(2,1)S(1)} %fusion.4), channel_id=1, source_target_pairs={{0,4},{1,5},{2,6},{3,7},{4,0},{5,1},{6,2},{7,3},{8,12},{9,13},{10,... | collective-permute-start | bytes 294920 | tf_op jit(solution)/shard_map/ppermute | solution.py:24
  52.5 2.6 %collective-permute-done.24 = bf16[3,64,256]{2,1,0:T(8,128)(2,1)S(1)} collective-permute-done((bf16[3,64,256]{2,1,0:T(8,128)(2,1)S(1)}, bf16[3,64,256]{2,1,0:T(8,128)(2,1)S(1)}, u32[]{:S(2)}, u32[]{:S(2)}) %collective-permute-start.24) | collective-permute-done | bytes 98336 | tf_op jit(solution)/shard_map/ppermute | solution.py:24
  55.2 2.4 %collective-permute-start.25 = (bf16[3,64,256]{2,1,0:T(8,128)(2,1)S(1)}, bf16[3,64,256]{2,1,0:T(8,128)(2,1)S(1)}, u32[]{:S(2)}, u32[]{:S(2)}) collective-permute-start(bf16[3,64,256]{2,1,0:T(8,128)(2,1)S(1)} %fusion.16), channel_id=1, source_target_pairs={{0,16},{1,17},{2,18},{3,19},{4,20},{5,21},{6,22},{7,23},{8,24},{9,... | collective-permute-start | bytes 294920 | tf_op jit(solution)/shard_map/ppermute | solution.py:24
  57.9 1.1 %collective-permute-start.30 = (bf16[3,64,256]{2,1,0:T(8,128)(2,1)S(1)}, bf16[3,64,256]{2,1,0:T(8,128)(2,1)S(1)}, u32[]{:S(2)}, u32[]{:S(2)}) collective-permute-start(bf16[3,64,256]{2,1,0:T(8,128)(2,1)S(1)} %fusion.6), channel_id=1, source_target_pairs={{0,8},{1,9},{2,10},{3,11},{4,12},{5,13},{6,14},{7,15},{8,0},{9,1},... | collective-permute-start | bytes 294920 | tf_op jit(solution)/shard_map/ppermute | solution.py:24
  58.9 4.5 %collective-permute-done.25 = bf16[3,64,256]{2,1,0:T(8,128)(2,1)S(1)} collective-permute-done((bf16[3,64,256]{2,1,0:T(8,128)(2,1)S(1)}, bf16[3,64,256]{2,1,0:T(8,128)(2,1)S(1)}, u32[]{:S(2)}, u32[]{:S(2)}) %collective-permute-start.25) | collective-permute-done | bytes 98336 | tf_op jit(solution)/shard_map/ppermute | solution.py:24
  63.4 0.7 collective-permute-done.30
  64.6 1.0 %collective-permute-start.34 = (bf16[3,64,256]{2,1,0:T(8,128)(2,1)S(1)}, bf16[3,64,256]{2,1,0:T(8,128)(2,1)S(1)}, u32[]{:S(2)}, u32[]{:S(2)}) collective-permute-start(bf16[3,64,256]{2,1,0:T(8,128)(2,1)S(1)} %get-tuple-element.88.refs_0_), channel_id=1, source_target_pairs={{0,8},{1,9},{2,10},{3,11},{4,12},{5,13},{6,14},{7,15},{8,0},{9,1},... | collective-permute-start | bytes 294920 | tf_op jit(solution)/shard_map/ppermute | solution.py:24
  65.6 2.1 %collective-permute-start.32 = (bf16[3,64,256]{2,1,0:T(8,128)(2,1)S(1)}, bf16[3,64,256]{2,1,0:T(8,128)(2,1)S(1)}, u32[]{:S(2)}, u32[]{:S(2)}) collective-permute-start(bf16[3,64,256]{2,1,0:T(8,128)(2,1)S(1)} %get-tuple-element.88.refs_0_), channel_id=1, source_target_pairs={{0,4},{1,5},{2,6},{3,7},{4,0},{5,1},{6,2},{7,3},{8,12},{9,13},{10,... | collective-permute-start | bytes 294920 | tf_op jit(solution)/shard_map/ppermute | solution.py:24
  67.7 2.4 %collective-permute-done.37.refs_8_ = bf16[3,64,256]{2,1,0:T(8,128)(2,1)S(1)} collective-permute-done((bf16[3,64,256]{2,1,0:T(8,128)(2,1)S(1)}, bf16[3,64,256]{2,1,0:T(8,128)(2,1)S(1)}, u32[]{:S(2)}, u32[]{:S(2)}) %collective-permute-start.37) | collective-permute-done | bytes 98336 | tf_op jit(solution)/shard_map/ppermute | solution.py:24
  70.3 1.0 %collective-permute-start.35 = (bf16[3,64,256]{2,1,0:T(8,128)(2,1)S(1)}, bf16[3,64,256]{2,1,0:T(8,128)(2,1)S(1)}, u32[]{:S(2)}, u32[]{:S(2)}) collective-permute-start(bf16[3,64,256]{2,1,0:T(8,128)(2,1)S(1)} %collective-permute-done.34.refs_4_), channel_id=1, source_target_pairs={{0,2},{1,3},{2,0},{3,1},{4,6},{5,7},{6,4},{7,5},{8,10},{9,11},{10,... | collective-permute-start | bytes 294920 | tf_op jit(solution)/shard_map/ppermute | solution.py:24
  71.4 1.0 %collective-permute-done.31.refs_1_ = bf16[3,64,256]{2,1,0:T(8,128)(2,1)S(1)} collective-permute-done((bf16[3,64,256]{2,1,0:T(8,128)(2,1)S(1)}, bf16[3,64,256]{2,1,0:T(8,128)(2,1)S(1)}, u32[]{:S(2)}, u32[]{:S(2)}) %collective-permute-start.31) | collective-permute-done | bytes 98336 | tf_op jit(solution)/shard_map/ppermute | solution.py:24
  72.3 0.7 collective-permute-start.36
  73.1 1.0 %collective-permute-start.38 = (bf16[3,64,256]{2,1,0:T(8,128)(2,1)S(1)}, bf16[3,64,256]{2,1,0:T(8,128)(2,1)S(1)}, u32[]{:S(2)}, u32[]{:S(2)}) collective-permute-start(bf16[3,64,256]{2,1,0:T(8,128)(2,1)S(1)} %collective-permute-done.37.refs_8_), channel_id=1, source_target_pairs={{0,2},{1,3},{2,0},{3,1},{4,6},{5,7},{6,4},{7,5},{8,10},{9,11},{10,... | collective-permute-start | bytes 294920 | tf_op jit(solution)/shard_map/ppermute | solution.py:24
  74.1 0.7 collective-permute-done.41.refs_12_
  74.9 2.1 %collective-permute-start.44 = (bf16[3,64,256]{2,1,0:T(8,128)(2,1)S(1)}, bf16[3,64,256]{2,1,0:T(8,128)(2,1)S(1)}, u32[]{:S(2)}, u32[]{:S(2)}) collective-permute-start(bf16[3,64,256]{2,1,0:T(8,128)(2,1)S(1)} %collective-permute-done.41.refs_12_), channel_id=1, source_target_pairs={{0,4},{1,5},{2,6},{3,7},{4,0},{5,1},{6,2},{7,3},{8,12},{9,13},{10,... | collective-permute-start | bytes 294920 | tf_op jit(solution)/shard_map/ppermute | solution.py:24
  77.0 1.0 %collective-permute-start.42 = (bf16[3,64,256]{2,1,0:T(8,128)(2,1)S(1)}, bf16[3,64,256]{2,1,0:T(8,128)(2,1)S(1)}, u32[]{:S(2)}, u32[]{:S(2)}) collective-permute-start(bf16[3,64,256]{2,1,0:T(8,128)(2,1)S(1)} %collective-permute-done.41.refs_12_), channel_id=1, source_target_pairs={{0,2},{1,3},{2,0},{3,1},{4,6},{5,7},{6,4},{7,5},{8,10},{9,11},{10,... | collective-permute-start | bytes 294920 | tf_op jit(solution)/shard_map/ppermute | solution.py:24
  78.1 2.0 %collective-permute-start.40 = (bf16[3,64,256]{2,1,0:T(8,128)(2,1)S(1)}, bf16[3,64,256]{2,1,0:T(8,128)(2,1)S(1)}, u32[]{:S(2)}, u32[]{:S(2)}) collective-permute-start(bf16[3,64,256]{2,1,0:T(8,128)(2,1)S(1)} %collective-permute-done.37.refs_8_), channel_id=1, source_target_pairs={{0,4},{1,5},{2,6},{3,7},{4,0},{5,1},{6,2},{7,3},{8,12},{9,13},{10,... | collective-permute-start | bytes 294920 | tf_op jit(solution)/shard_map/ppermute | solution.py:24
  80.2 1.0 %collective-permute-start.39 = (bf16[3,64,256]{2,1,0:T(8,128)(2,1)S(1)}, bf16[3,64,256]{2,1,0:T(8,128)(2,1)S(1)}, u32[]{:S(2)}, u32[]{:S(2)}) collective-permute-start(bf16[3,64,256]{2,1,0:T(8,128)(2,1)S(1)} %collective-permute-done.36.refs_6_), channel_id=1, source_target_pairs={{0,2},{1,3},{2,0},{3,1},{4,6},{5,7},{6,4},{7,5},{8,10},{9,11},{10,... | collective-permute-start | bytes 294920 | tf_op jit(solution)/shard_map/ppermute | solution.py:24
  81.2 0.4 collective-permute-done.42.refs_13_
  81.6 1.0 %collective-permute-start.45 = (bf16[3,64,256]{2,1,0:T(8,128)(2,1)S(1)}, bf16[3,64,256]{2,1,0:T(8,128)(2,1)S(1)}, u32[]{:S(2)}, u32[]{:S(2)}) collective-permute-start(bf16[3,64,256]{2,1,0:T(8,128)(2,1)S(1)} %collective-permute-done.44.refs_14_), channel_id=1, source_target_pairs={{0,2},{1,3},{2,0},{3,1},{4,6},{5,7},{6,4},{7,5},{8,10},{9,11},{10,... | collective-permute-start | bytes 294920 | tf_op jit(solution)/shard_map/ppermute | solution.py:24
  82.7 1.1 %collective-permute-done.40.refs_10_ = bf16[3,64,256]{2,1,0:T(8,128)(2,1)S(1)} collective-permute-done((bf16[3,64,256]{2,1,0:T(8,128)(2,1)S(1)}, bf16[3,64,256]{2,1,0:T(8,128)(2,1)S(1)}, u32[]{:S(2)}, u32[]{:S(2)}) %collective-permute-start.40) | collective-permute-done | bytes 98336 | tf_op jit(solution)/shard_map/ppermute | solution.py:24
  83.8 1.0 %collective-permute-done.39.refs_7_ = bf16[3,64,256]{2,1,0:T(8,128)(2,1)S(1)} collective-permute-done((bf16[3,64,256]{2,1,0:T(8,128)(2,1)S(1)}, bf16[3,64,256]{2,1,0:T(8,128)(2,1)S(1)}, u32[]{:S(2)}, u32[]{:S(2)}) %collective-permute-start.39) | collective-permute-done | bytes 98336 | tf_op jit(solution)/shard_map/ppermute | solution.py:24
  84.8 1.5 %collective-permute-done.45.refs_15_ = bf16[3,64,256]{2,1,0:T(8,128)(2,1)S(1)} collective-permute-done((bf16[3,64,256]{2,1,0:T(8,128)(2,1)S(1)}, bf16[3,64,256]{2,1,0:T(8,128)(2,1)S(1)}, u32[]{:S(2)}, u32[]{:S(2)}) %collective-permute-start.45) | collective-permute-done | bytes 98336 | tf_op jit(solution)/shard_map/ppermute | solution.py:24
  86.2 0.8 other_outputs.1
  87.1 0.5 collective-permute-start.47
  87.6 1.5 %own_outputs.1 = (bf16[256,1024]{1,0:T(8,128)(2,1)S(1)}, s32[1]{0:T(128)}) custom-call(s32[32]{0:T(128)S(1)} %copy-done.3, bf16[3,1024,256]{2,1,0:T(8,128)(2,1)S(1)} %get-tuple-element.85.weights, bf16[256,1024]{1,0:T(8,128)(2,1)S(1)} %bitcast.77), custom_call_target="tpu_custom_call" | custom-call | flops 402653184 | bytes 2621440 | tf_op jit(solution)/shard_map/own_outputs/pallas_call | solution.py:197
  89.9 0.8 slice_bitcast_fusion
  90.7 0.9 select_bitcast_fusion
  (65 shorter events, 2.5 us)
Async XLA Ops:
  0.6 29.1 %copy-start.1 = (bf16[1,256,1024]{2,1,0:T(8,128)(2,1)S(1)}, bf16[1,256,1024]{2,1,0:T(8,128)(2,1)}, u32[]{:S(2)}) copy-start(bf16[1,256,1024]{2,1,0:T(8,128)(2,1)} %param.12) | copy-start | bytes 1572868
  0.6 29.1 %copy-start.2 = (bf16[1,256,1024]{2,1,0:T(8,128)(2,1)S(1)}, bf16[1,256,1024]{2,1,0:T(8,128)(2,1)}, u32[]{:S(2)}) copy-start(bf16[1,256,1024]{2,1,0:T(8,128)(2,1)} %param.13) | copy-start | bytes 1572868
  0.7 4.8 %collective-permute-start.1 = (bf16[256,1024]{1,0:T(8,128)(2,1)}, bf16[256,1024]{1,0:T(8,128)(2,1)S(1)}, u32[]{:S(2)}, u32[]{:S(2)}) collective-permute-start(bf16[256,1024]{1,0:T(8,128)(2,1)} %bitcast.78), channel_id=1, source_target_pairs={{0,1},{1,0},{2,3},{3,2},{4,5},{5,4},{6,7},{7,6},{8,9},{9,8},{10,11... | collective-permute-start | bytes 1572872 | tf_op jit(solution)/shard_map/ppermute | solution.py:24
  1.2 4.3 %collective-permute-start.2 = (bf16[256,1024]{1,0:T(8,128)(2,1)}, bf16[256,1024]{1,0:T(8,128)(2,1)S(1)}, u32[]{:S(2)}, u32[]{:S(2)}) collective-permute-start(bf16[256,1024]{1,0:T(8,128)(2,1)} %bitcast.81), channel_id=1, source_target_pairs={{0,1},{1,0},{2,3},{3,2},{4,5},{5,4},{6,7},{7,6},{8,9},{9,8},{10,11... | collective-permute-start | bytes 1572872 | tf_op jit(solution)/shard_map/ppermute | solution.py:24
  1.2 4.2 %collective-permute-start.3 = (bf16[256,1024]{1,0:T(8,128)(2,1)}, bf16[256,1024]{1,0:T(8,128)(2,1)S(1)}, u32[]{:S(2)}, u32[]{:S(2)}) collective-permute-start(bf16[256,1024]{1,0:T(8,128)(2,1)} %bitcast.76), channel_id=1, source_target_pairs={{0,1},{1,0},{2,3},{3,2},{4,5},{5,4},{6,7},{7,6},{8,9},{9,8},{10,11... | collective-permute-start | bytes 1572872 | tf_op jit(solution)/shard_map/ppermute | solution.py:24
  3.7 29.0 %copy-start.4 = (s32[32]{0:T(128)S(1)}, s32[32]{0:T(128)}, u32[]{:S(2)}) copy-start(s32[32]{0:T(128)} %slots.2) | copy-start | bytes 388
  3.8 1.7 %collective-permute-start = (f32[3,3,32,256]{3,2,1,0:T(8,128)S(1)}, f32[3,3,32,256]{3,2,1,0:T(8,128)S(1)}, u32[]{:S(2)}, u32[]{:S(2)}) collective-permute-start(f32[3,3,32,256]{3,2,1,0:T(8,128)S(1)} %pad_maximum_fusion.1), channel_id=1, source_target_pairs={{0,1},{1,0},{2,3},{3,2},{4,5},{5,4},{6,7},{7,6},{8,9},{9,8},{10,11... | collective-permute-start | bytes 884744 | tf_op jit(solution)/shard_map/ppermute | solution.py:24
  3.9 1.6 %collective-permute-start.4 = (s32[1]{0:T(128)}, s32[1]{0:T(128)}, u32[]{:S(2)}, u32[]{:S(2)}) collective-permute-start(s32[1]{0:T(128)} %param.17), channel_id=1, source_target_pairs={{0,1},{1,0},{2,3},{3,2},{4,5},{5,4},{6,7},{7,6},{8,9},{9,8},{10,11... | collective-permute-start | bytes 20 | tf_op jit(solution)/shard_map/ppermute | solution.py:24
  5.5 9.3 %collective-permute-start.11 = (bf16[3,64,256]{2,1,0:T(8,128)(2,1)S(1)}, bf16[3,64,256]{2,1,0:T(8,128)(2,1)S(1)}, u32[]{:S(2)}, u32[]{:S(2)}) collective-permute-start(bf16[3,64,256]{2,1,0:T(8,128)(2,1)S(1)} %fusion.17.refs_0_), channel_id=1, source_target_pairs={{0,16},{1,17},{2,18},{3,19},{4,20},{5,21},{6,22},{7,23},{8,24},{9,... | collective-permute-start | bytes 294920 | tf_op jit(solution)/shard_map/ppermute | solution.py:24
  9.4 6.1 %collective-permute-start.8 = (bf16[3,64,256]{2,1,0:T(8,128)(2,1)S(1)}, bf16[3,64,256]{2,1,0:T(8,128)(2,1)S(1)}, u32[]{:S(2)}, u32[]{:S(2)}) collective-permute-start(bf16[3,64,256]{2,1,0:T(8,128)(2,1)S(1)} %fusion.17.refs_0_), channel_id=1, source_target_pairs={{0,8},{1,9},{2,10},{3,11},{4,12},{5,13},{6,14},{7,15},{8,0},{9,1},... | collective-permute-start | bytes 294920 | tf_op jit(solution)/shard_map/ppermute | solution.py:24
  11.0 6.0 %collective-permute-start.5 = (bf16[3,64,256]{2,1,0:T(8,128)(2,1)S(1)}, bf16[3,64,256]{2,1,0:T(8,128)(2,1)S(1)}, u32[]{:S(2)}, u32[]{:S(2)}) collective-permute-start(bf16[3,64,256]{2,1,0:T(8,128)(2,1)S(1)} %fusion.17.refs_0_), channel_id=1, source_target_pairs={{0,2},{1,3},{2,0},{3,1},{4,6},{5,7},{6,4},{7,5},{8,10},{9,11},{10,... | collective-permute-start | bytes 294920 | tf_op jit(solution)/shard_map/ppermute | solution.py:24
  12.5 6.1 %collective-permute-start.6 = (bf16[3,64,256]{2,1,0:T(8,128)(2,1)S(1)}, bf16[3,64,256]{2,1,0:T(8,128)(2,1)S(1)}, u32[]{:S(2)}, u32[]{:S(2)}) collective-permute-start(bf16[3,64,256]{2,1,0:T(8,128)(2,1)S(1)} %fusion.17.refs_0_), channel_id=1, source_target_pairs={{0,4},{1,5},{2,6},{3,7},{4,0},{5,1},{6,2},{7,3},{8,12},{9,13},{10,... | collective-permute-start | bytes 294920 | tf_op jit(solution)/shard_map/ppermute | solution.py:24
  14.9 4.6 %collective-permute-start.15 = (bf16[3,64,256]{2,1,0:T(8,128)(2,1)S(1)}, bf16[3,64,256]{2,1,0:T(8,128)(2,1)S(1)}, u32[]{:S(2)}, u32[]{:S(2)}) collective-permute-start(bf16[3,64,256]{2,1,0:T(8,128)(2,1)S(1)} %collective-permute-done.11.refs_8_), channel_id=1, source_target_pairs={{0,8},{1,9},{2,10},{3,11},{4,12},{5,13},{6,14},{7,15},{8,0},{9,1},... | collective-permute-start | bytes 294920 | tf_op jit(solution)/shard_map/ppermute | solution.py:24
  15.5 4.6 %collective-permute-start.9 = (bf16[3,64,256]{2,1,0:T(8,128)(2,1)S(1)}, bf16[3,64,256]{2,1,0:T(8,128)(2,1)S(1)}, u32[]{:S(2)}, u32[]{:S(2)}) collective-permute-start(bf16[3,64,256]{2,1,0:T(8,128)(2,1)S(1)} %collective-permute-done.8.refs_4_), channel_id=1, source_target_pairs={{0,2},{1,3},{2,0},{3,1},{4,6},{5,7},{6,4},{7,5},{8,10},{9,11},{10,... | collective-permute-start | bytes 294920 | tf_op jit(solution)/shard_map/ppermute | solution.py:24
  17.0 7.4 %collective-permute-start.10 = (bf16[3,64,256]{2,1,0:T(8,128)(2,1)S(1)}, bf16[3,64,256]{2,1,0:T(8,128)(2,1)S(1)}, u32[]{:S(2)}, u32[]{:S(2)}) collective-permute-start(bf16[3,64,256]{2,1,0:T(8,128)(2,1)S(1)} %collective-permute-done.8.refs_4_), channel_id=1, source_target_pairs={{0,4},{1,5},{2,6},{3,7},{4,0},{5,1},{6,2},{7,3},{8,12},{9,13},{10,... | collective-permute-start | bytes 294920 | tf_op jit(solution)/shard_map/ppermute | solution.py:24
  18.5 7.5 %collective-permute-start.12 = (bf16[3,64,256]{2,1,0:T(8,128)(2,1)S(1)}, bf16[3,64,256]{2,1,0:T(8,128)(2,1)S(1)}, u32[]{:S(2)}, u32[]{:S(2)}) collective-permute-start(bf16[3,64,256]{2,1,0:T(8,128)(2,1)S(1)} %collective-permute-done.11.refs_8_), channel_id=1, source_target_pairs={{0,2},{1,3},{2,0},{3,1},{4,6},{5,7},{6,4},{7,5},{8,10},{9,11},{10,... | collective-permute-start | bytes 294920 | tf_op jit(solution)/shard_map/ppermute | solution.py:24
  20.1 6.4 %collective-permute-start.16 = (bf16[3,64,256]{2,1,0:T(8,128)(2,1)S(1)}, bf16[3,64,256]{2,1,0:T(8,128)(2,1)S(1)}, u32[]{:S(2)}, u32[]{:S(2)}) collective-permute-start(bf16[3,64,256]{2,1,0:T(8,128)(2,1)S(1)} %collective-permute-done.15.refs_12_), channel_id=1, source_target_pairs={{0,2},{1,3},{2,0},{3,1},{4,6},{5,7},{6,4},{7,5},{8,10},{9,11},{10,... | collective-permute-start | bytes 294920 | tf_op jit(solution)/shard_map/ppermute | solution.py:24
  22.4 5.0 %collective-permute-start.18 = (bf16[3,64,256]{2,1,0:T(8,128)(2,1)S(1)}, bf16[3,64,256]{2,1,0:T(8,128)(2,1)S(1)}, u32[]{:S(2)}, u32[]{:S(2)}) collective-permute-start(bf16[3,64,256]{2,1,0:T(8,128)(2,1)S(1)} %collective-permute-done.15.refs_12_), channel_id=1, source_target_pairs={{0,4},{1,5},{2,6},{3,7},{4,0},{5,1},{6,2},{7,3},{8,12},{9,13},{10,... | collective-permute-start | bytes 294920 | tf_op jit(solution)/shard_map/ppermute | solution.py:24
  24.0 6.4 %collective-permute-start.7 = (bf16[3,64,256]{2,1,0:T(8,128)(2,1)S(1)}, bf16[3,64,256]{2,1,0:T(8,128)(2,1)S(1)}, u32[]{:S(2)}, u32[]{:S(2)}) collective-permute-start(bf16[3,64,256]{2,1,0:T(8,128)(2,1)S(1)} %collective-permute-done.5.refs_1_), channel_id=1, source_target_pairs={{0,4},{1,5},{2,6},{3,7},{4,0},{5,1},{6,2},{7,3},{8,12},{9,13},{10,... | collective-permute-start | bytes 294920 | tf_op jit(solution)/shard_map/ppermute | solution.py:24
  24.4 6.0 %collective-permute-start.14 = (bf16[3,64,256]{2,1,0:T(8,128)(2,1)S(1)}, bf16[3,64,256]{2,1,0:T(8,128)(2,1)S(1)}, u32[]{:S(2)}, u32[]{:S(2)}) collective-permute-start(bf16[3,64,256]{2,1,0:T(8,128)(2,1)S(1)} %collective-permute-done.11.refs_8_), channel_id=1, source_target_pairs={{0,4},{1,5},{2,6},{3,7},{4,0},{5,1},{6,2},{7,3},{8,12},{9,13},{10,... | collective-permute-start | bytes 294920 | tf_op jit(solution)/shard_map/ppermute | solution.py:24
  26.1 4.6 %collective-permute-start.13 = (bf16[3,64,256]{2,1,0:T(8,128)(2,1)S(1)}, bf16[3,64,256]{2,1,0:T(8,128)(2,1)S(1)}, u32[]{:S(2)}, u32[]{:S(2)}) collective-permute-start(bf16[3,64,256]{2,1,0:T(8,128)(2,1)S(1)} %collective-permute-done.10.refs_6_), channel_id=1, source_target_pairs={{0,2},{1,3},{2,0},{3,1},{4,6},{5,7},{6,4},{7,5},{8,10},{9,11},{10,... | collective-permute-start | bytes 294920 | tf_op jit(solution)/shard_map/ppermute | solution.py:24
  27.4 4.6 %collective-permute-start.19 = (bf16[3,64,256]{2,1,0:T(8,128)(2,1)S(1)}, bf16[3,64,256]{2,1,0:T(8,128)(2,1)S(1)}, u32[]{:S(2)}, u32[]{:S(2)}) collective-permute-start(bf16[3,64,256]{2,1,0:T(8,128)(2,1)S(1)} %collective-permute-done.18.refs_14_), channel_id=1, source_target_pairs={{0,2},{1,3},{2,0},{3,1},{4,6},{5,7},{6,4},{7,5},{8,10},{9,11},{10,... | collective-permute-start | bytes 294920 | tf_op jit(solution)/shard_map/ppermute | solution.py:24
  28.1 4.6 %collective-permute-start.17 = (bf16[3,64,256]{2,1,0:T(8,128)(2,1)S(1)}, bf16[3,64,256]{2,1,0:T(8,128)(2,1)S(1)}, u32[]{:S(2)}, u32[]{:S(2)}) collective-permute-start(bf16[3,64,256]{2,1,0:T(8,128)(2,1)S(1)} %collective-permute-done.12.refs_9_), channel_id=1, source_target_pairs={{0,4},{1,5},{2,6},{3,7},{4,0},{5,1},{6,2},{7,3},{8,12},{9,13},{10,... | collective-permute-start | bytes 294920 | tf_op jit(solution)/shard_map/ppermute | solution.py:24
  36.0 6.7 %collective-permute-start.20 = (bf16[2,3,64,256]{3,2,1,0:T(8,128)(2,1)S(1)}, bf16[2,3,64,256]{3,2,1,0:T(8,128)(2,1)S(1)}, u32[]{:S(2)}, u32[]{:S(2)}) collective-permute-start(bf16[2,3,64,256]{3,2,1,0:T(8,128)(2,1)S(1)} %get-tuple-element.62), channel_id=1, source_target_pairs={{0,4},{1,5},{2,6},{3,7},{4,0},{5,1},{6,2},{7,3},{8,12},{9,13},{10,... | collective-permute-start | bytes 589832 | tf_op jit(solution)/shard_map/ppermute | solution.py:24
  37.1 7.1 %collective-permute-start.22 = (bf16[2,3,64,256]{3,2,1,0:T(8,128)(2,1)S(1)}, bf16[2,3,64,256]{3,2,1,0:T(8,128)(2,1)S(1)}, u32[]{:S(2)}, u32[]{:S(2)}) collective-permute-start(bf16[2,3,64,256]{3,2,1,0:T(8,128)(2,1)S(1)} %get-tuple-element.65), channel_id=1, source_target_pairs={{0,2},{1,3},{2,0},{3,1},{4,6},{5,7},{6,4},{7,5},{8,10},{9,11},{10,... | collective-permute-start | bytes 589832 | tf_op jit(solution)/shard_map/ppermute | solution.py:24
  39.1 7.8 %collective-permute-start.28 = (bf16[2,3,64,256]{3,2,1,0:T(8,128)(2,1)S(1)}, bf16[2,3,64,256]{3,2,1,0:T(8,128)(2,1)S(1)}, u32[]{:S(2)}, u32[]{:S(2)}) collective-permute-start(bf16[2,3,64,256]{3,2,1,0:T(8,128)(2,1)S(1)} %get-tuple-element.72), channel_id=1, source_target_pairs={{0,2},{1,3},{2,0},{3,1},{4,6},{5,7},{6,4},{7,5},{8,10},{9,11},{10,... | collective-permute-start | bytes 589832 | tf_op jit(solution)/shard_map/ppermute | solution.py:24
  42.7 9.8 %collective-permute-start.21 = (bf16[3,64,256]{2,1,0:T(8,128)(2,1)S(1)}, bf16[3,64,256]{2,1,0:T(8,128)(2,1)S(1)}, u32[]{:S(2)}, u32[]{:S(2)}) collective-permute-start(bf16[3,64,256]{2,1,0:T(8,128)(2,1)S(1)} %fusion.13), channel_id=1, source_target_pairs={{0,2},{1,3},{2,0},{3,1},{4,6},{5,7},{6,4},{7,5},{8,10},{9,11},{10,... | collective-permute-start | bytes 294920 | tf_op jit(solution)/shard_map/ppermute | solution.py:24
  44.3 5.1 %collective-permute-start.23 = (bf16[3,64,256]{2,1,0:T(8,128)(2,1)S(1)}, bf16[3,64,256]{2,1,0:T(8,128)(2,1)S(1)}, u32[]{:S(2)}, u32[]{:S(2)}) collective-permute-start(bf16[3,64,256]{2,1,0:T(8,128)(2,1)S(1)} %fusion.10), channel_id=1, source_target_pairs={{0,4},{1,5},{2,6},{3,7},{4,0},{5,1},{6,2},{7,3},{8,12},{9,13},{10,... | collective-permute-start | bytes 294920 | tf_op jit(solution)/shard_map/ppermute | solution.py:24
  46.8 5.7 %collective-permute-start.26 = (bf16[2,3,64,256]{3,2,1,0:T(8,128)(2,1)S(1)}, bf16[2,3,64,256]{3,2,1,0:T(8,128)(2,1)S(1)}, u32[]{:S(2)}, u32[]{:S(2)}) collective-permute-start(bf16[2,3,64,256]{3,2,1,0:T(8,128)(2,1)S(1)} %get-tuple-element.68), channel_id=1, source_target_pairs={{0,4},{1,5},{2,6},{3,7},{4,0},{5,1},{6,2},{7,3},{8,12},{9,13},{10,... | collective-permute-start | bytes 589832 | tf_op jit(solution)/shard_map/ppermute | solution.py:24
  49.5 5.7 %collective-permute-start.24 = (bf16[3,64,256]{2,1,0:T(8,128)(2,1)S(1)}, bf16[3,64,256]{2,1,0:T(8,128)(2,1)S(1)}, u32[]{:S(2)}, u32[]{:S(2)}) collective-permute-start(bf16[3,64,256]{2,1,0:T(8,128)(2,1)S(1)} %fusion.12), channel_id=1, source_target_pairs={{0,8},{1,9},{2,10},{3,11},{4,12},{5,13},{6,14},{7,15},{8,0},{9,1},... | collective-permute-start | bytes 294920 | tf_op jit(solution)/shard_map/ppermute | solution.py:24
  50.3 7.5 %collective-permute-start.29 = (bf16[3,64,256]{2,1,0:T(8,128)(2,1)S(1)}, bf16[3,64,256]{2,1,0:T(8,128)(2,1)S(1)}, u32[]{:S(2)}, u32[]{:S(2)}) collective-permute-start(bf16[3,64,256]{2,1,0:T(8,128)(2,1)S(1)} %fusion.4), channel_id=1, source_target_pairs={{0,4},{1,5},{2,6},{3,7},{4,0},{5,1},{6,2},{7,3},{8,12},{9,13},{10,... | collective-permute-start | bytes 294920 | tf_op jit(solution)/shard_map/ppermute | solution.py:24
  55.2 8.2 %collective-permute-start.25 = (bf16[3,64,256]{2,1,0:T(8,128)(2,1)S(1)}, bf16[3,64,256]{2,1,0:T(8,128)(2,1)S(1)}, u32[]{:S(2)}, u32[]{:S(2)}) collective-permute-start(bf16[3,64,256]{2,1,0:T(8,128)(2,1)S(1)} %fusion.16), channel_id=1, source_target_pairs={{0,16},{1,17},{2,18},{3,19},{4,20},{5,21},{6,22},{7,23},{8,24},{9,... | collective-permute-start | bytes 294920 | tf_op jit(solution)/shard_map/ppermute | solution.py:24
  57.6 5.8 %collective-permute-start.27 = (bf16[3,64,256]{2,1,0:T(8,128)(2,1)S(1)}, bf16[3,64,256]{2,1,0:T(8,128)(2,1)S(1)}, u32[]{:S(2)}, u32[]{:S(2)}) collective-permute-start(bf16[3,64,256]{2,1,0:T(8,128)(2,1)S(1)} %fusion.7), channel_id=1, source_target_pairs={{0,2},{1,3},{2,0},{3,1},{4,6},{5,7},{6,4},{7,5},{8,10},{9,11},{10,... | collective-permute-start | bytes 294920 | tf_op jit(solution)/shard_map/ppermute | solution.py:24
  57.9 6.3 %collective-permute-start.30 = (bf16[3,64,256]{2,1,0:T(8,128)(2,1)S(1)}, bf16[3,64,256]{2,1,0:T(8,128)(2,1)S(1)}, u32[]{:S(2)}, u32[]{:S(2)}) collective-permute-start(bf16[3,64,256]{2,1,0:T(8,128)(2,1)S(1)} %fusion.6), channel_id=1, source_target_pairs={{0,8},{1,9},{2,10},{3,11},{4,12},{5,13},{6,14},{7,15},{8,0},{9,1},... | collective-permute-start | bytes 294920 | tf_op jit(solution)/shard_map/ppermute | solution.py:24
  64.4 5.7 %collective-permute-start.37 = (bf16[3,64,256]{2,1,0:T(8,128)(2,1)S(1)}, bf16[3,64,256]{2,1,0:T(8,128)(2,1)S(1)}, u32[]{:S(2)}, u32[]{:S(2)}) collective-permute-start(bf16[3,64,256]{2,1,0:T(8,128)(2,1)S(1)} %get-tuple-element.88.refs_0_), channel_id=1, source_target_pairs={{0,16},{1,17},{2,18},{3,19},{4,20},{5,21},{6,22},{7,23},{8,24},{9,... | collective-permute-start | bytes 294920 | tf_op jit(solution)/shard_map/ppermute | solution.py:24
  64.6 5.7 %collective-permute-start.34 = (bf16[3,64,256]{2,1,0:T(8,128)(2,1)S(1)}, bf16[3,64,256]{2,1,0:T(8,128)(2,1)S(1)}, u32[]{:S(2)}, u32[]{:S(2)}) collective-permute-start(bf16[3,64,256]{2,1,0:T(8,128)(2,1)S(1)} %get-tuple-element.88.refs_0_), channel_id=1, source_target_pairs={{0,8},{1,9},{2,10},{3,11},{4,12},{5,13},{6,14},{7,15},{8,0},{9,1},... | collective-permute-start | bytes 294920 | tf_op jit(solution)/shard_map/ppermute | solution.py:24
  65.6 5.8 %collective-permute-start.32 = (bf16[3,64,256]{2,1,0:T(8,128)(2,1)S(1)}, bf16[3,64,256]{2,1,0:T(8,128)(2,1)S(1)}, u32[]{:S(2)}, u32[]{:S(2)}) collective-permute-start(bf16[3,64,256]{2,1,0:T(8,128)(2,1)S(1)} %get-tuple-element.88.refs_0_), channel_id=1, source_target_pairs={{0,4},{1,5},{2,6},{3,7},{4,0},{5,1},{6,2},{7,3},{8,12},{9,13},{10,... | collective-permute-start | bytes 294920 | tf_op jit(solution)/shard_map/ppermute | solution.py:24
  67.7 4.6 %collective-permute-start.31 = (bf16[3,64,256]{2,1,0:T(8,128)(2,1)S(1)}, bf16[3,64,256]{2,1,0:T(8,128)(2,1)S(1)}, u32[]{:S(2)}, u32[]{:S(2)}) collective-permute-start(bf16[3,64,256]{2,1,0:T(8,128)(2,1)S(1)} %get-tuple-element.88.refs_0_), channel_id=1, source_target_pairs={{0,2},{1,3},{2,0},{3,1},{4,6},{5,7},{6,4},{7,5},{8,10},{9,11},{10,... | collective-permute-start | bytes 294920 | tf_op jit(solution)/shard_map/ppermute | solution.py:24
  70.2 4.6 %collective-permute-start.41 = (bf16[3,64,256]{2,1,0:T(8,128)(2,1)S(1)}, bf16[3,64,256]{2,1,0:T(8,128)(2,1)S(1)}, u32[]{:S(2)}, u32[]{:S(2)}) collective-permute-start(bf16[3,64,256]{2,1,0:T(8,128)(2,1)S(1)} %collective-permute-done.37.refs_8_), channel_id=1, source_target_pairs={{0,8},{1,9},{2,10},{3,11},{4,12},{5,13},{6,14},{7,15},{8,0},{9,1},... | collective-permute-start | bytes 294920 | tf_op jit(solution)/shard_map/ppermute | solution.py:24
  70.3 4.6 %collective-permute-start.35 = (bf16[3,64,256]{2,1,0:T(8,128)(2,1)S(1)}, bf16[3,64,256]{2,1,0:T(8,128)(2,1)S(1)}, u32[]{:S(2)}, u32[]{:S(2)}) collective-permute-start(bf16[3,64,256]{2,1,0:T(8,128)(2,1)S(1)} %collective-permute-done.34.refs_4_), channel_id=1, source_target_pairs={{0,2},{1,3},{2,0},{3,1},{4,6},{5,7},{6,4},{7,5},{8,10},{9,11},{10,... | collective-permute-start | bytes 294920 | tf_op jit(solution)/shard_map/ppermute | solution.py:24
  72.3 5.8 %collective-permute-start.36 = (bf16[3,64,256]{2,1,0:T(8,128)(2,1)S(1)}, bf16[3,64,256]{2,1,0:T(8,128)(2,1)S(1)}, u32[]{:S(2)}, u32[]{:S(2)}) collective-permute-start(bf16[3,64,256]{2,1,0:T(8,128)(2,1)S(1)} %collective-permute-done.34.refs_4_), channel_id=1, source_target_pairs={{0,4},{1,5},{2,6},{3,7},{4,0},{5,1},{6,2},{7,3},{8,12},{9,13},{10,... | collective-permute-start | bytes 294920 | tf_op jit(solution)/shard_map/ppermute | solution.py:24
  73.1 7.1 %collective-permute-start.38 = (bf16[3,64,256]{2,1,0:T(8,128)(2,1)S(1)}, bf16[3,64,256]{2,1,0:T(8,128)(2,1)S(1)}, u32[]{:S(2)}, u32[]{:S(2)}) collective-permute-start(bf16[3,64,256]{2,1,0:T(8,128)(2,1)S(1)} %collective-permute-done.37.refs_8_), channel_id=1, source_target_pairs={{0,2},{1,3},{2,0},{3,1},{4,6},{5,7},{6,4},{7,5},{8,10},{9,11},{10,... | collective-permute-start | bytes 294920 | tf_op jit(solution)/shard_map/ppermute | solution.py:24
  74.9 6.7 %collective-permute-start.44 = (bf16[3,64,256]{2,1,0:T(8,128)(2,1)S(1)}, bf16[3,64,256]{2,1,0:T(8,128)(2,1)S(1)}, u32[]{:S(2)}, u32[]{:S(2)}) collective-permute-start(bf16[3,64,256]{2,1,0:T(8,128)(2,1)S(1)} %collective-permute-done.41.refs_12_), channel_id=1, source_target_pairs={{0,4},{1,5},{2,6},{3,7},{4,0},{5,1},{6,2},{7,3},{8,12},{9,13},{10,... | collective-permute-start | bytes 294920 | tf_op jit(solution)/shard_map/ppermute | solution.py:24
  77.0 4.6 %collective-permute-start.42 = (bf16[3,64,256]{2,1,0:T(8,128)(2,1)S(1)}, bf16[3,64,256]{2,1,0:T(8,128)(2,1)S(1)}, u32[]{:S(2)}, u32[]{:S(2)}) collective-permute-start(bf16[3,64,256]{2,1,0:T(8,128)(2,1)S(1)} %collective-permute-done.41.refs_12_), channel_id=1, source_target_pairs={{0,2},{1,3},{2,0},{3,1},{4,6},{5,7},{6,4},{7,5},{8,10},{9,11},{10,... | collective-permute-start | bytes 294920 | tf_op jit(solution)/shard_map/ppermute | solution.py:24
  78.0 9.6 %copy-start = (bf16[1,256,1024]{2,1,0:T(8,128)(2,1)S(1)}, bf16[1,256,1024]{2,1,0:T(8,128)(2,1)}, u32[]{:S(2)}) copy-start(bf16[1,256,1024]{2,1,0:T(8,128)(2,1)} %param.14) | copy-start | bytes 1572868
  78.0 9.6 %copy-start.3 = (s32[32]{0:T(128)S(1)}, s32[32]{0:T(128)}, u32[]{:S(2)}) copy-start(s32[32]{0:T(128)} %slots.3) | copy-start | bytes 388
  78.1 4.7 %collective-permute-start.33 = (bf16[3,64,256]{2,1,0:T(8,128)(2,1)S(1)}, bf16[3,64,256]{2,1,0:T(8,128)(2,1)S(1)}, u32[]{:S(2)}, u32[]{:S(2)}) collective-permute-start(bf16[3,64,256]{2,1,0:T(8,128)(2,1)S(1)} %collective-permute-done.31.refs_1_), channel_id=1, source_target_pairs={{0,4},{1,5},{2,6},{3,7},{4,0},{5,1},{6,2},{7,3},{8,12},{9,13},{10,... | collective-permute-start | bytes 294920 | tf_op jit(solution)/shard_map/ppermute | solution.py:24
  78.1 5.6 %collective-permute-start.40 = (bf16[3,64,256]{2,1,0:T(8,128)(2,1)S(1)}, bf16[3,64,256]{2,1,0:T(8,128)(2,1)S(1)}, u32[]{:S(2)}, u32[]{:S(2)}) collective-permute-start(bf16[3,64,256]{2,1,0:T(8,128)(2,1)S(1)} %collective-permute-done.37.refs_8_), channel_id=1, source_target_pairs={{0,4},{1,5},{2,6},{3,7},{4,0},{5,1},{6,2},{7,3},{8,12},{9,13},{10,... | collective-permute-start | bytes 294920 | tf_op jit(solution)/shard_map/ppermute | solution.py:24
  80.2 4.6 %collective-permute-start.39 = (bf16[3,64,256]{2,1,0:T(8,128)(2,1)S(1)}, bf16[3,64,256]{2,1,0:T(8,128)(2,1)S(1)}, u32[]{:S(2)}, u32[]{:S(2)}) collective-permute-start(bf16[3,64,256]{2,1,0:T(8,128)(2,1)S(1)} %collective-permute-done.36.refs_6_), channel_id=1, source_target_pairs={{0,2},{1,3},{2,0},{3,1},{4,6},{5,7},{6,4},{7,5},{8,10},{9,11},{10,... | collective-permute-start | bytes 294920 | tf_op jit(solution)/shard_map/ppermute | solution.py:24
  81.6 4.6 %collective-permute-start.43 = (bf16[3,64,256]{2,1,0:T(8,128)(2,1)S(1)}, bf16[3,64,256]{2,1,0:T(8,128)(2,1)S(1)}, u32[]{:S(2)}, u32[]{:S(2)}) collective-permute-start(bf16[3,64,256]{2,1,0:T(8,128)(2,1)S(1)} %collective-permute-done.38.refs_9_), channel_id=1, source_target_pairs={{0,4},{1,5},{2,6},{3,7},{4,0},{5,1},{6,2},{7,3},{8,12},{9,13},{10,... | collective-permute-start | bytes 294920 | tf_op jit(solution)/shard_map/ppermute | solution.py:24
  81.6 4.6 %collective-permute-start.45 = (bf16[3,64,256]{2,1,0:T(8,128)(2,1)S(1)}, bf16[3,64,256]{2,1,0:T(8,128)(2,1)S(1)}, u32[]{:S(2)}, u32[]{:S(2)}) collective-permute-start(bf16[3,64,256]{2,1,0:T(8,128)(2,1)S(1)} %collective-permute-done.44.refs_14_), channel_id=1, source_target_pairs={{0,2},{1,3},{2,0},{3,1},{4,6},{5,7},{6,4},{7,5},{8,10},{9,11},{10,... | collective-permute-start | bytes 294920 | tf_op jit(solution)/shard_map/ppermute | solution.py:24
  87.0 2.8 %collective-permute-start.46 = (f32[3,3,32,256]{3,2,1,0:T(8,128)S(1)}, f32[3,3,32,256]{3,2,1,0:T(8,128)S(1)}, u32[]{:S(2)}, u32[]{:S(2)}) collective-permute-start(f32[3,3,32,256]{3,2,1,0:T(8,128)S(1)} %get-tuple-element.84), channel_id=1, source_target_pairs={{0,1},{1,0},{2,3},{3,2},{4,5},{5,4},{6,7},{7,6},{8,9},{9,8},{10,11... | collective-permute-start | bytes 884744 | tf_op jit(solution)/shard_map/ppermute | solution.py:24
  87.1 3.6 %collective-permute-start.47 = (bf16[256,1024]{1,0:T(8,128)(2,1)S(1)}, bf16[256,1024]{1,0:T(8,128)(2,1)S(1)}, u32[]{:S(2)}, u32[]{:S(2)}) collective-permute-start(bf16[256,1024]{1,0:T(8,128)(2,1)S(1)} %get-tuple-element.83), channel_id=1, source_target_pairs={{0,1},{1,0},{2,3},{3,2},{4,5},{5,4},{6,7},{7,6},{8,9},{9,8},{10,11... | collective-permute-start | bytes 1572872 | tf_op jit(solution)/shard_map/ppermute | solution.py:24

commit v12 on v11

--- a/solution.py
+++ b/solution.py
@@ -39,8 +39,10 @@
         weights[:, pl.ds(start, rows), :] = piece[...]
 
 
-def transpose_kernel(own_x, other_x, own_c, other_c, x_turned, c_turned):
-    chip = lax.axis_index("dev") // 2
+def transpose_kernel(slots, own_x, other_x, own_c, other_c, x_turned, c_turned, matches):
+    me_index = lax.axis_index("dev")
+    matches[0] = jnp.where(slots[me_index] == (me_index & CORE), 1, 0)
+    chip = me_index // 2
     tokens, width = own_x.shape
     rows = 2 * width // lax.axis_size("dev")
     lanes = max(128, rows)
@@ -116,14 +118,12 @@
 
 def other_kernel(count, *refs):
     pieces = refs[:count]
-    other_y, other_out, weights = refs[count:]
+    other_y, own_y, other_out, weights = refs[count:]
     place_pieces(lax.axis_index("dev") // 2, pieces, weights)
     expert_rows(other_y, weights, other_out)
 
 
-def own_kernel(slots, weights, own_y, own_out, matches):
-    me_index = lax.axis_index("dev")
-    matches[0] = jnp.where(slots[me_index] == (me_index & CORE), 1, 0)
+def own_kernel(weights, own_y, own_out):
     expert_rows(own_y, weights, own_out)
 
 
@@ -135,17 +135,18 @@
     return pltpu.CompilerParams(vmem_limit_bytes=VMEM_LIMIT)
 
 
-def transposed(own_x, other_x, own_c, other_c):
+def transposed(slots, own_x, other_x, own_c, other_c):
     tokens, width = own_x.shape
     return pl.pallas_call(
         transpose_kernel,
-        out_shape=[jax.ShapeDtypeStruct((width, 2 * tokens), own_x.dtype)] * 2,
-        in_specs=[VMEM] * 4,
-        out_specs=[VMEM] * 2,
+        out_shape=[jax.ShapeDtypeStruct((width, 2 * tokens), own_x.dtype)] * 2
+        + [jax.ShapeDtypeStruct((1,), jnp.int32)],
+        in_specs=[SMEM] + [VMEM] * 4,
+        out_specs=[VMEM, VMEM, SMEM],
         compiler_params=params(),
         cost_estimate=pl.CostEstimate(flops=0, bytes_accessed=16 * tokens * width, transcendentals=0),
         name="transpose_rows",
-    )(own_x, other_x, own_c, other_c)
+    )(slots, own_x, other_x, own_c, other_c)
 
 
 def backward(slots, own_live, other_live, pieces, own_x, other_x, own_c, other_c, x_turned, c_turned):
@@ -175,7 +176,7 @@
     )(slots, own_live, other_live, *pieces, own_x, other_x, own_c, other_c, x_turned, c_turned)
 
 
-def forward(slots, pieces, own_y, other_y):
+def forward(pieces, own_y, other_y):
     count = len(pieces)
     kinds, rows, units = pieces[0].shape
     tokens, width = own_y.shape
@@ -188,22 +189,22 @@
     other_out, weights = pl.pallas_call(
         functools.partial(other_kernel, count),
         out_shape=[one, jax.ShapeDtypeStruct((kinds, width, units), jnp.bfloat16)],
-        in_specs=[VMEM] * (count + 1),
+        in_specs=[VMEM] * (count + 2),
         out_specs=[VMEM] * 2,
         compiler_params=params(),
         cost_estimate=cost,
         name="other_outputs",
-    )(*pieces, other_y)
-    own_out, matches = pl.pallas_call(
+    )(*pieces, other_y, own_y)
+    own_out = pl.pallas_call(
         own_kernel,
-        out_shape=[one, jax.ShapeDtypeStruct((1,), jnp.int32)],
-        in_specs=[SMEM, VMEM, VMEM],
-        out_specs=[VMEM, SMEM],
+        out_shape=one,
+        in_specs=[VMEM, VMEM],
+        out_specs=VMEM,
         compiler_params=params(),
         cost_estimate=cost,
         name="own_outputs",
-    )(slots, weights, own_y)
-    return own_out, other_out, matches
+    )(weights, own_y)
+    return own_out, other_out
 
 
 def after(value, *others):
@@ -245,26 +246,25 @@
 
 def reduce_chips(pieces):
     depth = lax.axis_size("dev") // Z_UNIT
-    column = [[pieces[3 * zj]] for zj in range(depth)]
-    arrived, crossed, risen = (), (), ()
+    total, waiting, arrived, crossed = [], [], (), ()
     for upper in reversed(range(1, depth, 2)):
-        up_y, pair_x = pieces[3 * upper + 1 : 3 * upper + 3]
-        below_x, pair_y = pieces[3 * upper - 2 : 3 * upper]
+        own_up, up_y, pair_x = pieces[3 * upper : 3 * upper + 3]
+        own_low, low_x, pair_y = pieces[3 * upper - 3 : 3 * upper]
         got_x = hop(pair_x, X_STEP)
         got_y = hop(after(pair_y, *arrived), Y_STEP)
-        up_y = add_all(up_y, got_x[0]).astype(jnp.bfloat16)
-        column[upper] += [got_x[1], hop(after(up_y, *crossed), Y_STEP)]
-        below_x = add_all(below_x, got_y[0]).astype(jnp.bfloat16)
-        column[upper - 1] += [got_y[1], hop(after(below_x, *risen), X_STEP)]
-        arrived, crossed, risen = (got_x,), (column[upper][-1],), ()
-        for zj in (upper, upper - 1):
-            top = 1 << zj.bit_length() - 1 if zj else 0
-            low = zj - top
-            if zj:
-                part = add_all(*column[zj]).astype(jnp.bfloat16)
-                column[top if low else 0].append(hop(part, (low or top) * Z_UNIT))
-                risen = risen or (column[top if low else 0][-1],)
-    return add_all(*column[0])
+        up_y = hop(after(add_all(up_y, got_x[0]).astype(jnp.bfloat16), *crossed), Y_STEP)
+        low_x = hop(after(add_all(low_x, got_y[0]).astype(jnp.bfloat16), *crossed), X_STEP)
+        arrived, crossed = (got_x,), (low_x,)
+        low = [own_low, got_y[1], low_x]
+        up = add_all(own_up, got_x[1], up_y).astype(jnp.bfloat16)
+        if upper > 1:
+            total.append(hop(add_all(*low).astype(jnp.bfloat16), (upper - 1) * Z_UNIT))
+            waiting.append((up, upper * Z_UNIT))
+        else:
+            total += low
+            total += [hop(after(part, got_y), mask) for part, mask in waiting]
+            total.append(hop(up, Z_UNIT))
+    return add_all(*total)
 
 
 def block_a_core(master, first, second, old_rows, old_cotangent, new_rows, old_slots, new_slots, live):
@@ -287,10 +287,10 @@
     theirs = hop(jnp.stack([partners(master), partners(first), partners(second)]), CORE)
     other_y = hop(new_rows, CORE)
     other_live = hop(live, CORE)
-    theirs, other_x, other_c, other_y, other_live = lax.optimization_barrier(
-        (theirs, other_x, other_c, other_y, other_live)
-    )
-    x_turned, c_turned = transposed(old_rows, other_x, old_cotangent, other_c)
+    x_turned, c_turned, matches = transposed(new_slots, old_rows, other_x, old_cotangent, other_c)
+    theirs, other_y, other_live, x_turned, c_turned = lax.optimization_barrier(
+        (theirs, other_y, other_live, x_turned, c_turned)
+    )
     master_two = both_rows(mine(master), theirs[0])
     pieces = gather_chips(master_two.astype(jnp.bfloat16))
     grads = backward(
@@ -315,7 +315,7 @@
     updated = jnp.stack(updated)
     own_part = lax.dynamic_slice_in_dim(updated, core * local_rows, local_rows, 2)
     other_part = lax.dynamic_slice_in_dim(updated, (1 - core) * local_rows, local_rows, 2)
-    own_out, other_out, matches = forward(new_slots, new_pieces, new_rows, other_y)
+    own_out, other_out = forward(new_pieces, new_rows, other_y)
     from_other = hop(after(other_part, other_out), CORE)
     state = jnp.where(
         core == 0, jnp.stack([own_part, from_other], axis=1), jnp.stack([from_other, own_part], axis=1)

time: 91.8 us -> 91.2 us (level)
  waiting for transfers between devices: 28.8 us -> 25.9 us
  starting transfers between devices: 49.9 us -> 52.1 us
    ppermute x48, waiting for transfers between devices: 28.8 us -> 25.9 us  [hop(): lax.ppermute(block, 'dev', [(low, low ^ mask) for low in range(count)])]
    ppermute x48, starting transfers between devices: 49.9 us -> 52.1 us  [hop(): lax.ppermute(block, 'dev', [(low, low ^ mask) for low in range(count)])]
    pallas_call x1, Pallas kernels: 0.59 us -> 1.57 us  [transposed(): pl.pallas_call(transpose_kernel, out_shape=[jax.ShapeDtypeStruct((width,...]
  transfers between devices with their start and end apart: 48 -> 48, of which waited for: 25 -> 23; matrix products, arithmetic and copies ran while one was open for 4% -> 4% of each run, Pallas kernels for 2% -> 2%
where the time goes in v12:
time: 91.2 us; the launch traced here: 91 us
  starting transfers between devices  52.1 us (57%)
  waiting for transfers between devices  25.9 us (28%)
  Pallas kernels  6.3 us (7%)
  local copies, waits for them, and re-layouts  2.93 us (3%)
  between operations  2.22 us (2%)
  other arithmetic  1.57 us (2%)
    ppermute x48, starting transfers between devices, hop(): lax.ppermute(block, 'dev', [(low, low ^ mask) for low in range(count)])  52.1 us
    ppermute x48, waiting for transfers between devices, hop(): lax.ppermute(block, 'dev', [(low, low ^ mask) for low in range(count)])  25.9 us
    pallas_call x1, Pallas kernels, backward(): pl.pallas_call(functools.partial(backward_kernel, count), out_shape=[one,...  3.3 us
  transfers between devices with their start and end apart: 48, of which 23 were waited for; matrix products, arithmetic and copies ran while one was open for 4% of the time, Pallas kernels for 2%

profile of v12, /device:TPU:0, one launch (start us, length us, event | category | flops | bytes accessed | tf_op | source)
XLA Modules:
  0.0 91.0 jit_solution(11097875145656250243)
XLA Ops:
  0.7 0.5 collective-permute-start.3
  1.3 0.4 collective-permute-start.1
  1.7 1.1 %dynamic-slice_bitcast_fusion.2 = (f32[3,32,256]{2,1,0:T(8,128)S(1)}, f32[1,3,32,256]{3,2,1,0:T(8,128)S(1)}, f32[1,3,32,256]{3,2,1,0:T(8,128)S(1)}, f32[3,32,256]{2,1,0:T(8,128)S(1)}) fusion(f32[2,3,32,256]{3,2,1,0:T(8,128)} %param.10, s32[]{:T(128)S(6)} %select_n.51, s32[]{:T(128)S(6)} %select_n.52, f32[2,3,32,256]{3,2,1,0:T(8,128)} %param.9), kind=kLoop, calls=%fused_computation.50 | loop fusion | bytes 786440 | tf_op jit(solution)/shard_map/jit(dynamic_index_in_dim)/squeeze | solution.py:275
  2.8 1.0 %constant_dynamic-slice_fusion.1 = (f32[1,3,32,256]{3,2,1,0:T(8,128)S(1)}, f32[3,32,256]{2,1,0:T(8,128)S(1)}) fusion(f32[2,3,32,256]{3,2,1,0:T(8,128)} %param.11, s32[]{:T(128)S(6)} %select_n.52, s32[]{:T(128)S(6)} %select_n.51), kind=kLoop, calls=%fused_computation.54 | loop fusion | bytes 393224 | tf_op jit(solution)/shard_map/jit(dynamic_index_in_dim)/dynamic_slice | solution.py:278
  3.9 0.4 collective-permute-start.2
  4.4 1.6 %transpose_rows.1 = (bf16[1024,512]{1,0:T(8,128)(2,1)S(1)}, bf16[1024,512]{1,0:T(8,128)(2,1)S(1)}, s32[1]{0:T(128)}) custom-call(s32[32]{0:T(128)S(1)} %copy-done.3, bf16[256,1024]{1,0:T(8,128)(2,1)S(1)} %bitcast.77, bf16[256,1024]{1,0:T(8,128)(2,1)S(1)} %collective-permute-done.3.other_x.refs_17_, bf16[256,1024]{1,0:T(8,128)(2,1)S(1)} %bitcast.80, ...), custom_call_target="tpu_custom_call" | custom-call | bytes 4194304 | tf_op jit(solution)/shard_map/transpose_rows/pallas_call | solution.py:140
  6.0 3.7 %collective-permute-start.11 = (bf16[3,64,256]{2,1,0:T(8,128)(2,1)S(1)}, bf16[3,64,256]{2,1,0:T(8,128)(2,1)S(1)}, u32[]{:S(2)}, u32[]{:S(2)}) collective-permute-start(bf16[3,64,256]{2,1,0:T(8,128)(2,1)S(1)} %fusion.17.refs_0_), channel_id=1, source_target_pairs={{0,16},{1,17},{2,18},{3,19},{4,20},{5,21},{6,22},{7,23},{8,24},{9,... | collective-permute-start | bytes 294920 | tf_op jit(solution)/shard_map/ppermute | solution.py:24
  9.7 1.6 %collective-permute-start.8 = (bf16[3,64,256]{2,1,0:T(8,128)(2,1)S(1)}, bf16[3,64,256]{2,1,0:T(8,128)(2,1)S(1)}, u32[]{:S(2)}, u32[]{:S(2)}) collective-permute-start(bf16[3,64,256]{2,1,0:T(8,128)(2,1)S(1)} %fusion.17.refs_0_), channel_id=1, source_target_pairs={{0,8},{1,9},{2,10},{3,11},{4,12},{5,13},{6,14},{7,15},{8,0},{9,1},... | collective-permute-start | bytes 294920 | tf_op jit(solution)/shard_map/ppermute | solution.py:24
  11.3 1.5 %collective-permute-start.5 = (bf16[3,64,256]{2,1,0:T(8,128)(2,1)S(1)}, bf16[3,64,256]{2,1,0:T(8,128)(2,1)S(1)}, u32[]{:S(2)}, u32[]{:S(2)}) collective-permute-start(bf16[3,64,256]{2,1,0:T(8,128)(2,1)S(1)} %fusion.17.refs_0_), channel_id=1, source_target_pairs={{0,2},{1,3},{2,0},{3,1},{4,6},{5,7},{6,4},{7,5},{8,10},{9,11},{10,... | collective-permute-start | bytes 294920 | tf_op jit(solution)/shard_map/ppermute | solution.py:24
  12.8 1.5 %collective-permute-start.6 = (bf16[3,64,256]{2,1,0:T(8,128)(2,1)S(1)}, bf16[3,64,256]{2,1,0:T(8,128)(2,1)S(1)}, u32[]{:S(2)}, u32[]{:S(2)}) collective-permute-start(bf16[3,64,256]{2,1,0:T(8,128)(2,1)S(1)} %fusion.17.refs_0_), channel_id=1, source_target_pairs={{0,4},{1,5},{2,6},{3,7},{4,0},{5,1},{6,2},{7,3},{8,12},{9,13},{10,... | collective-permute-start | bytes 294920 | tf_op jit(solution)/shard_map/ppermute | solution.py:24
  14.3 1.0 %collective-permute-done.11.refs_8_ = bf16[3,64,256]{2,1,0:T(8,128)(2,1)S(1)} collective-permute-done((bf16[3,64,256]{2,1,0:T(8,128)(2,1)S(1)}, bf16[3,64,256]{2,1,0:T(8,128)(2,1)S(1)}, u32[]{:S(2)}, u32[]{:S(2)}) %collective-permute-start.11) | collective-permute-done | bytes 98336 | tf_op jit(solution)/shard_map/ppermute | solution.py:24
  15.4 0.6 collective-permute-start.15
  16.0 1.5 %collective-permute-start.9 = (bf16[3,64,256]{2,1,0:T(8,128)(2,1)S(1)}, bf16[3,64,256]{2,1,0:T(8,128)(2,1)S(1)}, u32[]{:S(2)}, u32[]{:S(2)}) collective-permute-start(bf16[3,64,256]{2,1,0:T(8,128)(2,1)S(1)} %collective-permute-done.8.refs_4_), channel_id=1, source_target_pairs={{0,2},{1,3},{2,0},{3,1},{4,6},{5,7},{6,4},{7,5},{8,10},{9,11},{10,... | collective-permute-start | bytes 294920 | tf_op jit(solution)/shard_map/ppermute | solution.py:24
  17.5 1.5 %collective-permute-start.10 = (bf16[3,64,256]{2,1,0:T(8,128)(2,1)S(1)}, bf16[3,64,256]{2,1,0:T(8,128)(2,1)S(1)}, u32[]{:S(2)}, u32[]{:S(2)}) collective-permute-start(bf16[3,64,256]{2,1,0:T(8,128)(2,1)S(1)} %collective-permute-done.8.refs_4_), channel_id=1, source_target_pairs={{0,4},{1,5},{2,6},{3,7},{4,0},{5,1},{6,2},{7,3},{8,12},{9,13},{10,... | collective-permute-start | bytes 294920 | tf_op jit(solution)/shard_map/ppermute | solution.py:24
  19.0 0.5 collective-permute-start.12
  19.6 0.4 collective-permute-done.15.refs_12_
  20.0 0.6 collective-permute-done.9.refs_5_
  20.6 2.2 %collective-permute-start.16 = (bf16[3,64,256]{2,1,0:T(8,128)(2,1)S(1)}, bf16[3,64,256]{2,1,0:T(8,128)(2,1)S(1)}, u32[]{:S(2)}, u32[]{:S(2)}) collective-permute-start(bf16[3,64,256]{2,1,0:T(8,128)(2,1)S(1)} %collective-permute-done.15.refs_12_), channel_id=1, source_target_pairs={{0,2},{1,3},{2,0},{3,1},{4,6},{5,7},{6,4},{7,5},{8,10},{9,11},{10,... | collective-permute-start | bytes 294920 | tf_op jit(solution)/shard_map/ppermute | solution.py:24
  22.9 1.7 %collective-permute-start.18 = (bf16[3,64,256]{2,1,0:T(8,128)(2,1)S(1)}, bf16[3,64,256]{2,1,0:T(8,128)(2,1)S(1)}, u32[]{:S(2)}, u32[]{:S(2)}) collective-permute-start(bf16[3,64,256]{2,1,0:T(8,128)(2,1)S(1)} %collective-permute-done.15.refs_12_), channel_id=1, source_target_pairs={{0,4},{1,5},{2,6},{3,7},{4,0},{5,1},{6,2},{7,3},{8,12},{9,13},{10,... | collective-permute-start | bytes 294920 | tf_op jit(solution)/shard_map/ppermute | solution.py:24
  24.9 1.7 %collective-permute-start.14 = (bf16[3,64,256]{2,1,0:T(8,128)(2,1)S(1)}, bf16[3,64,256]{2,1,0:T(8,128)(2,1)S(1)}, u32[]{:S(2)}, u32[]{:S(2)}) collective-permute-start(bf16[3,64,256]{2,1,0:T(8,128)(2,1)S(1)} %collective-permute-done.11.refs_8_), channel_id=1, source_target_pairs={{0,4},{1,5},{2,6},{3,7},{4,0},{5,1},{6,2},{7,3},{8,12},{9,13},{10,... | collective-permute-start | bytes 294920 | tf_op jit(solution)/shard_map/ppermute | solution.py:24
  26.6 0.4 collective-permute-start.13
  27.0 0.9 collective-permute-done.18.refs_14_
  27.9 0.7 collective-permute-start.19
  28.6 1.0 %collective-permute-start.17 = (bf16[3,64,256]{2,1,0:T(8,128)(2,1)S(1)}, bf16[3,64,256]{2,1,0:T(8,128)(2,1)S(1)}, u32[]{:S(2)}, u32[]{:S(2)}) collective-permute-start(bf16[3,64,256]{2,1,0:T(8,128)(2,1)S(1)} %collective-permute-done.12.refs_9_), channel_id=1, source_target_pairs={{0,4},{1,5},{2,6},{3,7},{4,0},{5,1},{6,2},{7,3},{8,12},{9,13},{10,... | collective-permute-start | bytes 294920 | tf_op jit(solution)/shard_map/ppermute | solution.py:24
  30.3 0.6 collective-permute-done.14.refs_10_
  31.2 1.3 %collective-permute-done.19.refs_15_ = bf16[3,64,256]{2,1,0:T(8,128)(2,1)S(1)} collective-permute-done((bf16[3,64,256]{2,1,0:T(8,128)(2,1)S(1)}, bf16[3,64,256]{2,1,0:T(8,128)(2,1)S(1)}, u32[]{:S(2)}, u32[]{:S(2)}) %collective-permute-start.19) | collective-permute-done | bytes 98336 | tf_op jit(solution)/shard_map/ppermute | solution.py:24
  32.5 0.7 collective-permute-done.17.refs_11_
  33.2 3.3 %slot_gradients.1 = (bf16[3,64,256]{2,1,0:T(8,128)(2,1)S(1)}, bf16[3,64,256]{2,1,0:T(8,128)(2,1)S(1)}, bf16[2,3,64,256]{3,2,1,0:T(8,128)(2,1)S(1)}, bf16[3,64,25...) custom-call(s32[32]{0:T(128)S(1)} %copy-done.4, ...), custom_call_target="tpu_custom_call" | custom-call | flops 1610612736 | bytes 7340032 | tf_op jit(solution)/shard_map/slot_gradients/pallas_call | solution.py:158
  36.5 1.1 %collective-permute-start.20 = (bf16[2,3,64,256]{3,2,1,0:T(8,128)(2,1)S(1)}, bf16[2,3,64,256]{3,2,1,0:T(8,128)(2,1)S(1)}, u32[]{:S(2)}, u32[]{:S(2)}) collective-permute-start(bf16[2,3,64,256]{3,2,1,0:T(8,128)(2,1)S(1)} %get-tuple-element.62), channel_id=1, source_target_pairs={{0,4},{1,5},{2,6},{3,7},{4,0},{5,1},{6,2},{7,3},{8,12},{9,13},{10,... | collective-permute-start | bytes 589832 | tf_op jit(solution)/shard_map/ppermute | solution.py:24
  37.6 2.0 %collective-permute-start.23 = (bf16[2,3,64,256]{3,2,1,0:T(8,128)(2,1)S(1)}, bf16[2,3,64,256]{3,2,1,0:T(8,128)(2,1)S(1)}, u32[]{:S(2)}, u32[]{:S(2)}) collective-permute-start(bf16[2,3,64,256]{3,2,1,0:T(8,128)(2,1)S(1)} %get-tuple-element.65), channel_id=1, source_target_pairs={{0,2},{1,3},{2,0},{3,1},{4,6},{5,7},{6,4},{7,5},{8,10},{9,11},{10,... | collective-permute-start | bytes 589832 | tf_op jit(solution)/shard_map/ppermute | solution.py:24
  39.6 3.6 %collective-permute-done.20 = bf16[2,3,64,256]{3,2,1,0:T(8,128)(2,1)S(1)} collective-permute-done((bf16[2,3,64,256]{3,2,1,0:T(8,128)(2,1)S(1)}, bf16[2,3,64,256]{3,2,1,0:T(8,128)(2,1)S(1)}, u32[]{:S(2)}, u32[]{:S(2)}) %collective-permute-start.20) | collective-permute-done | bytes 196640 | tf_op jit(solution)/shard_map/ppermute | solution.py:24
  43.2 1.5 %collective-permute-start.21 = (bf16[3,64,256]{2,1,0:T(8,128)(2,1)S(1)}, bf16[3,64,256]{2,1,0:T(8,128)(2,1)S(1)}, u32[]{:S(2)}, u32[]{:S(2)}) collective-permute-start(bf16[3,64,256]{2,1,0:T(8,128)(2,1)S(1)} %fusion.14), channel_id=1, source_target_pairs={{0,2},{1,3},{2,0},{3,1},{4,6},{5,7},{6,4},{7,5},{8,10},{9,11},{10,... | collective-permute-start | bytes 294920 | tf_op jit(solution)/shard_map/ppermute | solution.py:24
  44.8 2.5 %collective-permute-start.26 = (bf16[3,64,256]{2,1,0:T(8,128)(2,1)S(1)}, bf16[3,64,256]{2,1,0:T(8,128)(2,1)S(1)}, u32[]{:S(2)}, u32[]{:S(2)}) collective-permute-start(bf16[3,64,256]{2,1,0:T(8,128)(2,1)S(1)} %fusion.7), channel_id=1, source_target_pairs={{0,4},{1,5},{2,6},{3,7},{4,0},{5,1},{6,2},{7,3},{8,12},{9,13},{10,... | collective-permute-start | bytes 294920 | tf_op jit(solution)/shard_map/ppermute | solution.py:24
  47.4 0.5 collective-permute-done.21
  48.0 3.5 %collective-permute-start.22 = (bf16[3,64,256]{2,1,0:T(8,128)(2,1)S(1)}, bf16[3,64,256]{2,1,0:T(8,128)(2,1)S(1)}, u32[]{:S(2)}, u32[]{:S(2)}) collective-permute-start(bf16[3,64,256]{2,1,0:T(8,128)(2,1)S(1)} %fusion.16), channel_id=1, source_target_pairs={{0,16},{1,17},{2,18},{3,19},{4,20},{5,21},{6,22},{7,23},{8,24},{9,... | collective-permute-start | bytes 294920 | tf_op jit(solution)/shard_map/ppermute | solution.py:24
  51.5 2.4 %collective-permute-start.29 = (bf16[3,64,256]{2,1,0:T(8,128)(2,1)S(1)}, bf16[3,64,256]{2,1,0:T(8,128)(2,1)S(1)}, u32[]{:S(2)}, u32[]{:S(2)}) collective-permute-start(bf16[3,64,256]{2,1,0:T(8,128)(2,1)S(1)} %fusion.4), channel_id=1, source_target_pairs={{0,4},{1,5},{2,6},{3,7},{4,0},{5,1},{6,2},{7,3},{8,12},{9,13},{10,... | collective-permute-start | bytes 294920 | tf_op jit(solution)/shard_map/ppermute | solution.py:24
  54.0 2.2 %collective-permute-start.27 = (bf16[3,64,256]{2,1,0:T(8,128)(2,1)S(1)}, bf16[3,64,256]{2,1,0:T(8,128)(2,1)S(1)}, u32[]{:S(2)}, u32[]{:S(2)}) collective-permute-start(bf16[3,64,256]{2,1,0:T(8,128)(2,1)S(1)} %fusion.9), channel_id=1, source_target_pairs={{0,24},{1,25},{2,26},{3,27},{4,28},{5,29},{6,30},{7,31},{8,16},{9,... | collective-permute-start | bytes 294920 | tf_op jit(solution)/shard_map/ppermute | solution.py:24
  56.6 0.6 collective-permute-start.30
  57.2 4.0 %collective-permute-done.27 = bf16[3,64,256]{2,1,0:T(8,128)(2,1)S(1)} collective-permute-done((bf16[3,64,256]{2,1,0:T(8,128)(2,1)S(1)}, bf16[3,64,256]{2,1,0:T(8,128)(2,1)S(1)}, u32[]{:S(2)}, u32[]{:S(2)}) %collective-permute-start.27) | collective-permute-done | bytes 98336 | tf_op jit(solution)/shard_map/ppermute | solution.py:24
  61.4 1.1 %collective-permute-done.30 = bf16[3,64,256]{2,1,0:T(8,128)(2,1)S(1)} collective-permute-done((bf16[3,64,256]{2,1,0:T(8,128)(2,1)S(1)}, bf16[3,64,256]{2,1,0:T(8,128)(2,1)S(1)}, u32[]{:S(2)}, u32[]{:S(2)}) %collective-permute-start.30) | collective-permute-done | bytes 98336 | tf_op jit(solution)/shard_map/ppermute | solution.py:24
  62.7 1.3 %collective-permute-start.37 = (bf16[3,64,256]{2,1,0:T(8,128)(2,1)S(1)}, bf16[3,64,256]{2,1,0:T(8,128)(2,1)S(1)}, u32[]{:S(2)}, u32[]{:S(2)}) collective-permute-start(bf16[3,64,256]{2,1,0:T(8,128)(2,1)S(1)} %get-tuple-element.88.refs_0_), channel_id=1, source_target_pairs={{0,16},{1,17},{2,18},{3,19},{4,20},{5,21},{6,22},{7,23},{8,24},{9,... | collective-permute-start | bytes 294920 | tf_op jit(solution)/shard_map/ppermute | solution.py:24
  64.1 2.5 %collective-permute-start.34 = (bf16[3,64,256]{2,1,0:T(8,128)(2,1)S(1)}, bf16[3,64,256]{2,1,0:T(8,128)(2,1)S(1)}, u32[]{:S(2)}, u32[]{:S(2)}) collective-permute-start(bf16[3,64,256]{2,1,0:T(8,128)(2,1)S(1)} %get-tuple-element.88.refs_0_), channel_id=1, source_target_pairs={{0,8},{1,9},{2,10},{3,11},{4,12},{5,13},{6,14},{7,15},{8,0},{9,1},... | collective-permute-start | bytes 294920 | tf_op jit(solution)/shard_map/ppermute | solution.py:24
  66.6 1.1 %collective-permute-start.31 = (bf16[3,64,256]{2,1,0:T(8,128)(2,1)S(1)}, bf16[3,64,256]{2,1,0:T(8,128)(2,1)S(1)}, u32[]{:S(2)}, u32[]{:S(2)}) collective-permute-start(bf16[3,64,256]{2,1,0:T(8,128)(2,1)S(1)} %get-tuple-element.88.refs_0_), channel_id=1, source_target_pairs={{0,2},{1,3},{2,0},{3,1},{4,6},{5,7},{6,4},{7,5},{8,10},{9,11},{10,... | collective-permute-start | bytes 294920 | tf_op jit(solution)/shard_map/ppermute | solution.py:24
  67.6 1.8 %collective-permute-done.37.refs_8_ = bf16[3,64,256]{2,1,0:T(8,128)(2,1)S(1)} collective-permute-done((bf16[3,64,256]{2,1,0:T(8,128)(2,1)S(1)}, bf16[3,64,256]{2,1,0:T(8,128)(2,1)S(1)}, u32[]{:S(2)}, u32[]{:S(2)}) %collective-permute-start.37) | collective-permute-done | bytes 98336 | tf_op jit(solution)/shard_map/ppermute | solution.py:24
  69.5 0.4 collective-permute-done.34.refs_4_
  69.8 0.5 collective-permute-start.35
  70.4 1.8 %collective-permute-done.32.refs_2_ = bf16[3,64,256]{2,1,0:T(8,128)(2,1)S(1)} collective-permute-done((bf16[3,64,256]{2,1,0:T(8,128)(2,1)S(1)}, bf16[3,64,256]{2,1,0:T(8,128)(2,1)S(1)}, u32[]{:S(2)}, u32[]{:S(2)}) %collective-permute-start.32) | collective-permute-done | bytes 98336 | tf_op jit(solution)/shard_map/ppermute | solution.py:24
  72.2 1.2 %collective-permute-start.36 = (bf16[3,64,256]{2,1,0:T(8,128)(2,1)S(1)}, bf16[3,64,256]{2,1,0:T(8,128)(2,1)S(1)}, u32[]{:S(2)}, u32[]{:S(2)}) collective-permute-start(bf16[3,64,256]{2,1,0:T(8,128)(2,1)S(1)} %collective-permute-done.34.refs_4_), channel_id=1, source_target_pairs={{0,4},{1,5},{2,6},{3,7},{4,0},{5,1},{6,2},{7,3},{8,12},{9,13},{10,... | collective-permute-start | bytes 294920 | tf_op jit(solution)/shard_map/ppermute | solution.py:24
  73.4 0.7 collective-permute-done.41.refs_12_
  74.1 1.2 %collective-permute-done.35.refs_5_ = bf16[3,64,256]{2,1,0:T(8,128)(2,1)S(1)} collective-permute-done((bf16[3,64,256]{2,1,0:T(8,128)(2,1)S(1)}, bf16[3,64,256]{2,1,0:T(8,128)(2,1)S(1)}, u32[]{:S(2)}, u32[]{:S(2)}) %collective-permute-start.35) | collective-permute-done | bytes 98336 | tf_op jit(solution)/shard_map/ppermute | solution.py:24
  75.4 1.6 %collective-permute-start.42 = (bf16[3,64,256]{2,1,0:T(8,128)(2,1)S(1)}, bf16[3,64,256]{2,1,0:T(8,128)(2,1)S(1)}, u32[]{:S(2)}, u32[]{:S(2)}) collective-permute-start(bf16[3,64,256]{2,1,0:T(8,128)(2,1)S(1)} %collective-permute-done.41.refs_12_), channel_id=1, source_target_pairs={{0,2},{1,3},{2,0},{3,1},{4,6},{5,7},{6,4},{7,5},{8,10},{9,11},{10,... | collective-permute-start | bytes 294920 | tf_op jit(solution)/shard_map/ppermute | solution.py:24
  77.0 0.7 collective-permute-start.33
  77.7 1.4 %collective-permute-start.40 = (bf16[3,64,256]{2,1,0:T(8,128)(2,1)S(1)}, bf16[3,64,256]{2,1,0:T(8,128)(2,1)S(1)}, u32[]{:S(2)}, u32[]{:S(2)}) collective-permute-start(bf16[3,64,256]{2,1,0:T(8,128)(2,1)S(1)} %collective-permute-done.37.refs_8_), channel_id=1, source_target_pairs={{0,4},{1,5},{2,6},{3,7},{4,0},{5,1},{6,2},{7,3},{8,12},{9,13},{10,... | collective-permute-start | bytes 294920 | tf_op jit(solution)/shard_map/ppermute | solution.py:24
  79.1 0.5 collective-permute-start.39
  79.6 0.4 collective-permute-done.42.refs_13_
  80.0 1.9 %collective-permute-start.43 = (bf16[3,64,256]{2,1,0:T(8,128)(2,1)S(1)}, bf16[3,64,256]{2,1,0:T(8,128)(2,1)S(1)}, u32[]{:S(2)}, u32[]{:S(2)}) collective-permute-start(bf16[3,64,256]{2,1,0:T(8,128)(2,1)S(1)} %collective-permute-done.38.refs_9_), channel_id=1, source_target_pairs={{0,4},{1,5},{2,6},{3,7},{4,0},{5,1},{6,2},{7,3},{8,12},{9,13},{10,... | collective-permute-start | bytes 294920 | tf_op jit(solution)/shard_map/ppermute | solution.py:24
  82.3 0.4 collective-permute-done.40.refs_10_
  82.7 1.0 %collective-permute-done.39.refs_7_ = bf16[3,64,256]{2,1,0:T(8,128)(2,1)S(1)} collective-permute-done((bf16[3,64,256]{2,1,0:T(8,128)(2,1)S(1)}, bf16[3,64,256]{2,1,0:T(8,128)(2,1)S(1)}, u32[]{:S(2)}, u32[]{:S(2)}) %collective-permute-start.39) | collective-permute-done | bytes 98336 | tf_op jit(solution)/shard_map/ppermute | solution.py:24
  83.7 2.9 %collective-permute-done.45.refs_15_ = bf16[3,64,256]{2,1,0:T(8,128)(2,1)S(1)} collective-permute-done((bf16[3,64,256]{2,1,0:T(8,128)(2,1)S(1)}, bf16[3,64,256]{2,1,0:T(8,128)(2,1)S(1)}, u32[]{:S(2)}, u32[]{:S(2)}) %collective-permute-start.45) | collective-permute-done | bytes 98336 | tf_op jit(solution)/shard_map/ppermute | solution.py:24
  86.6 0.8 other_outputs.1
  87.4 0.5 collective-permute-start.47
  88.6 0.7 own_outputs.1
  89.3 0.8 slice_bitcast_fusion
  90.1 0.8 select_bitcast_fusion
  (66 shorter events, 2.8 us)
Async XLA Ops:
  0.6 3.7 %copy-start.1 = (bf16[1,256,1024]{2,1,0:T(8,128)(2,1)S(1)}, bf16[1,256,1024]{2,1,0:T(8,128)(2,1)}, u32[]{:S(2)}) copy-start(bf16[1,256,1024]{2,1,0:T(8,128)(2,1)} %param.12) | copy-start | bytes 1572868
  0.6 3.7 %copy-start.2 = (bf16[1,256,1024]{2,1,0:T(8,128)(2,1)S(1)}, bf16[1,256,1024]{2,1,0:T(8,128)(2,1)}, u32[]{:S(2)}) copy-start(bf16[1,256,1024]{2,1,0:T(8,128)(2,1)} %param.13) | copy-start | bytes 1572868
  0.7 3.7 %copy-start.3 = (s32[32]{0:T(128)S(1)}, s32[32]{0:T(128)}, u32[]{:S(2)}) copy-start(s32[32]{0:T(128)} %slots.2) | copy-start | bytes 388
  0.7 3.7 %collective-permute-start.3 = (bf16[256,1024]{1,0:T(8,128)(2,1)}, bf16[256,1024]{1,0:T(8,128)(2,1)S(1)}, u32[]{:S(2)}, u32[]{:S(2)}) collective-permute-start(bf16[256,1024]{1,0:T(8,128)(2,1)} %bitcast.76), channel_id=1, source_target_pairs={{0,1},{1,0},{2,3},{3,2},{4,5},{5,4},{6,7},{7,6},{8,9},{9,8},{10,11... | collective-permute-start | bytes 1572872 | tf_op jit(solution)/shard_map/ppermute | solution.py:24
  1.2 3.2 %collective-permute-start.4 = (bf16[256,1024]{1,0:T(8,128)(2,1)}, bf16[256,1024]{1,0:T(8,128)(2,1)S(1)}, u32[]{:S(2)}, u32[]{:S(2)}) collective-permute-start(bf16[256,1024]{1,0:T(8,128)(2,1)} %bitcast.79), channel_id=1, source_target_pairs={{0,1},{1,0},{2,3},{3,2},{4,5},{5,4},{6,7},{7,6},{8,9},{9,8},{10,11... | collective-permute-start | bytes 1572872 | tf_op jit(solution)/shard_map/ppermute | solution.py:24
  1.3 4.7 %collective-permute-start.1 = (bf16[256,1024]{1,0:T(8,128)(2,1)}, bf16[256,1024]{1,0:T(8,128)(2,1)S(1)}, u32[]{:S(2)}, u32[]{:S(2)}) collective-permute-start(bf16[256,1024]{1,0:T(8,128)(2,1)} %bitcast.73), channel_id=1, source_target_pairs={{0,1},{1,0},{2,3},{3,2},{4,5},{5,4},{6,7},{7,6},{8,9},{9,8},{10,11... | collective-permute-start | bytes 1572872 | tf_op jit(solution)/shard_map/ppermute | solution.py:24
  3.7 29.5 %copy-start.4 = (s32[32]{0:T(128)S(1)}, s32[32]{0:T(128)}, u32[]{:S(2)}) copy-start(s32[32]{0:T(128)} %slots.3) | copy-start | bytes 388
  3.8 2.2 %collective-permute-start = (f32[3,3,32,256]{3,2,1,0:T(8,128)S(1)}, f32[3,3,32,256]{3,2,1,0:T(8,128)S(1)}, u32[]{:S(2)}, u32[]{:S(2)}) collective-permute-start(f32[3,3,32,256]{3,2,1,0:T(8,128)S(1)} %pad_maximum_fusion.1), channel_id=1, source_target_pairs={{0,1},{1,0},{2,3},{3,2},{4,5},{5,4},{6,7},{7,6},{8,9},{9,8},{10,11... | collective-permute-start | bytes 884744 | tf_op jit(solution)/shard_map/ppermute | solution.py:24
  3.9 2.0 %collective-permute-start.2 = (s32[1]{0:T(128)}, s32[1]{0:T(128)}, u32[]{:S(2)}, u32[]{:S(2)}) collective-permute-start(s32[1]{0:T(128)} %param.17), channel_id=1, source_target_pairs={{0,1},{1,0},{2,3},{3,2},{4,5},{5,4},{6,7},{7,6},{8,9},{9,8},{10,11... | collective-permute-start | bytes 20 | tf_op jit(solution)/shard_map/ppermute | solution.py:24
  6.0 9.3 %collective-permute-start.11 = (bf16[3,64,256]{2,1,0:T(8,128)(2,1)S(1)}, bf16[3,64,256]{2,1,0:T(8,128)(2,1)S(1)}, u32[]{:S(2)}, u32[]{:S(2)}) collective-permute-start(bf16[3,64,256]{2,1,0:T(8,128)(2,1)S(1)} %fusion.17.refs_0_), channel_id=1, source_target_pairs={{0,16},{1,17},{2,18},{3,19},{4,20},{5,21},{6,22},{7,23},{8,24},{9,... | collective-permute-start | bytes 294920 | tf_op jit(solution)/shard_map/ppermute | solution.py:24
  9.7 6.3 %collective-permute-start.8 = (bf16[3,64,256]{2,1,0:T(8,128)(2,1)S(1)}, bf16[3,64,256]{2,1,0:T(8,128)(2,1)S(1)}, u32[]{:S(2)}, u32[]{:S(2)}) collective-permute-start(bf16[3,64,256]{2,1,0:T(8,128)(2,1)S(1)} %fusion.17.refs_0_), channel_id=1, source_target_pairs={{0,8},{1,9},{2,10},{3,11},{4,12},{5,13},{6,14},{7,15},{8,0},{9,1},... | collective-permute-start | bytes 294920 | tf_op jit(solution)/shard_map/ppermute | solution.py:24
  11.3 6.2 %collective-permute-start.5 = (bf16[3,64,256]{2,1,0:T(8,128)(2,1)S(1)}, bf16[3,64,256]{2,1,0:T(8,128)(2,1)S(1)}, u32[]{:S(2)}, u32[]{:S(2)}) collective-permute-start(bf16[3,64,256]{2,1,0:T(8,128)(2,1)S(1)} %fusion.17.refs_0_), channel_id=1, source_target_pairs={{0,2},{1,3},{2,0},{3,1},{4,6},{5,7},{6,4},{7,5},{8,10},{9,11},{10,... | collective-permute-start | bytes 294920 | tf_op jit(solution)/shard_map/ppermute | solution.py:24
  12.8 6.2 %collective-permute-start.6 = (bf16[3,64,256]{2,1,0:T(8,128)(2,1)S(1)}, bf16[3,64,256]{2,1,0:T(8,128)(2,1)S(1)}, u32[]{:S(2)}, u32[]{:S(2)}) collective-permute-start(bf16[3,64,256]{2,1,0:T(8,128)(2,1)S(1)} %fusion.17.refs_0_), channel_id=1, source_target_pairs={{0,4},{1,5},{2,6},{3,7},{4,0},{5,1},{6,2},{7,3},{8,12},{9,13},{10,... | collective-permute-start | bytes 294920 | tf_op jit(solution)/shard_map/ppermute | solution.py:24
  15.4 4.6 %collective-permute-start.15 = (bf16[3,64,256]{2,1,0:T(8,128)(2,1)S(1)}, bf16[3,64,256]{2,1,0:T(8,128)(2,1)S(1)}, u32[]{:S(2)}, u32[]{:S(2)}) collective-permute-start(bf16[3,64,256]{2,1,0:T(8,128)(2,1)S(1)} %collective-permute-done.11.refs_8_), channel_id=1, source_target_pairs={{0,8},{1,9},{2,10},{3,11},{4,12},{5,13},{6,14},{7,15},{8,0},{9,1},... | collective-permute-start | bytes 294920 | tf_op jit(solution)/shard_map/ppermute | solution.py:24
  16.0 4.6 %collective-permute-start.9 = (bf16[3,64,256]{2,1,0:T(8,128)(2,1)S(1)}, bf16[3,64,256]{2,1,0:T(8,128)(2,1)S(1)}, u32[]{:S(2)}, u32[]{:S(2)}) collective-permute-start(bf16[3,64,256]{2,1,0:T(8,128)(2,1)S(1)} %collective-permute-done.8.refs_4_), channel_id=1, source_target_pairs={{0,2},{1,3},{2,0},{3,1},{4,6},{5,7},{6,4},{7,5},{8,10},{9,11},{10,... | collective-permute-start | bytes 294920 | tf_op jit(solution)/shard_map/ppermute | solution.py:24
  17.5 7.4 %collective-permute-start.10 = (bf16[3,64,256]{2,1,0:T(8,128)(2,1)S(1)}, bf16[3,64,256]{2,1,0:T(8,128)(2,1)S(1)}, u32[]{:S(2)}, u32[]{:S(2)}) collective-permute-start(bf16[3,64,256]{2,1,0:T(8,128)(2,1)S(1)} %collective-permute-done.8.refs_4_), channel_id=1, source_target_pairs={{0,4},{1,5},{2,6},{3,7},{4,0},{5,1},{6,2},{7,3},{8,12},{9,13},{10,... | collective-permute-start | bytes 294920 | tf_op jit(solution)/shard_map/ppermute | solution.py:24
  19.0 7.6 %collective-permute-start.12 = (bf16[3,64,256]{2,1,0:T(8,128)(2,1)S(1)}, bf16[3,64,256]{2,1,0:T(8,128)(2,1)S(1)}, u32[]{:S(2)}, u32[]{:S(2)}) collective-permute-start(bf16[3,64,256]{2,1,0:T(8,128)(2,1)S(1)} %collective-permute-done.11.refs_8_), channel_id=1, source_target_pairs={{0,2},{1,3},{2,0},{3,1},{4,6},{5,7},{6,4},{7,5},{8,10},{9,11},{10,... | collective-permute-start | bytes 294920 | tf_op jit(solution)/shard_map/ppermute | solution.py:24
  20.6 6.4 %collective-permute-start.16 = (bf16[3,64,256]{2,1,0:T(8,128)(2,1)S(1)}, bf16[3,64,256]{2,1,0:T(8,128)(2,1)S(1)}, u32[]{:S(2)}, u32[]{:S(2)}) collective-permute-start(bf16[3,64,256]{2,1,0:T(8,128)(2,1)S(1)} %collective-permute-done.15.refs_12_), channel_id=1, source_target_pairs={{0,2},{1,3},{2,0},{3,1},{4,6},{5,7},{6,4},{7,5},{8,10},{9,11},{10,... | collective-permute-start | bytes 294920 | tf_op jit(solution)/shard_map/ppermute | solution.py:24
  22.9 5.0 %collective-permute-start.18 = (bf16[3,64,256]{2,1,0:T(8,128)(2,1)S(1)}, bf16[3,64,256]{2,1,0:T(8,128)(2,1)S(1)}, u32[]{:S(2)}, u32[]{:S(2)}) collective-permute-start(bf16[3,64,256]{2,1,0:T(8,128)(2,1)S(1)} %collective-permute-done.15.refs_12_), channel_id=1, source_target_pairs={{0,4},{1,5},{2,6},{3,7},{4,0},{5,1},{6,2},{7,3},{8,12},{9,13},{10,... | collective-permute-start | bytes 294920 | tf_op jit(solution)/shard_map/ppermute | solution.py:24
  24.5 5.7 %collective-permute-start.7 = (bf16[3,64,256]{2,1,0:T(8,128)(2,1)S(1)}, bf16[3,64,256]{2,1,0:T(8,128)(2,1)S(1)}, u32[]{:S(2)}, u32[]{:S(2)}) collective-permute-start(bf16[3,64,256]{2,1,0:T(8,128)(2,1)S(1)} %collective-permute-done.5.refs_1_), channel_id=1, source_target_pairs={{0,4},{1,5},{2,6},{3,7},{4,0},{5,1},{6,2},{7,3},{8,12},{9,13},{10,... | collective-permute-start | bytes 294920 | tf_op jit(solution)/shard_map/ppermute | solution.py:24
  24.9 6.0 %collective-permute-start.14 = (bf16[3,64,256]{2,1,0:T(8,128)(2,1)S(1)}, bf16[3,64,256]{2,1,0:T(8,128)(2,1)S(1)}, u32[]{:S(2)}, u32[]{:S(2)}) collective-permute-start(bf16[3,64,256]{2,1,0:T(8,128)(2,1)S(1)} %collective-permute-done.11.refs_8_), channel_id=1, source_target_pairs={{0,4},{1,5},{2,6},{3,7},{4,0},{5,1},{6,2},{7,3},{8,12},{9,13},{10,... | collective-permute-start | bytes 294920 | tf_op jit(solution)/shard_map/ppermute | solution.py:24
  26.6 4.6 %collective-permute-start.13 = (bf16[3,64,256]{2,1,0:T(8,128)(2,1)S(1)}, bf16[3,64,256]{2,1,0:T(8,128)(2,1)S(1)}, u32[]{:S(2)}, u32[]{:S(2)}) collective-permute-start(bf16[3,64,256]{2,1,0:T(8,128)(2,1)S(1)} %collective-permute-done.10.refs_6_), channel_id=1, source_target_pairs={{0,2},{1,3},{2,0},{3,1},{4,6},{5,7},{6,4},{7,5},{8,10},{9,11},{10,... | collective-permute-start | bytes 294920 | tf_op jit(solution)/shard_map/ppermute | solution.py:24
  27.9 4.6 %collective-permute-start.19 = (bf16[3,64,256]{2,1,0:T(8,128)(2,1)S(1)}, bf16[3,64,256]{2,1,0:T(8,128)(2,1)S(1)}, u32[]{:S(2)}, u32[]{:S(2)}) collective-permute-start(bf16[3,64,256]{2,1,0:T(8,128)(2,1)S(1)} %collective-permute-done.18.refs_14_), channel_id=1, source_target_pairs={{0,2},{1,3},{2,0},{3,1},{4,6},{5,7},{6,4},{7,5},{8,10},{9,11},{10,... | collective-permute-start | bytes 294920 | tf_op jit(solution)/shard_map/ppermute | solution.py:24
  28.6 4.6 %collective-permute-start.17 = (bf16[3,64,256]{2,1,0:T(8,128)(2,1)S(1)}, bf16[3,64,256]{2,1,0:T(8,128)(2,1)S(1)}, u32[]{:S(2)}, u32[]{:S(2)}) collective-permute-start(bf16[3,64,256]{2,1,0:T(8,128)(2,1)S(1)} %collective-permute-done.12.refs_9_), channel_id=1, source_target_pairs={{0,4},{1,5},{2,6},{3,7},{4,0},{5,1},{6,2},{7,3},{8,12},{9,13},{10,... | collective-permute-start | bytes 294920 | tf_op jit(solution)/shard_map/ppermute | solution.py:24
  36.5 6.7 %collective-permute-start.20 = (bf16[2,3,64,256]{3,2,1,0:T(8,128)(2,1)S(1)}, bf16[2,3,64,256]{3,2,1,0:T(8,128)(2,1)S(1)}, u32[]{:S(2)}, u32[]{:S(2)}) collective-permute-start(bf16[2,3,64,256]{3,2,1,0:T(8,128)(2,1)S(1)} %get-tuple-element.62), channel_id=1, source_target_pairs={{0,4},{1,5},{2,6},{3,7},{4,0},{5,1},{6,2},{7,3},{8,12},{9,13},{10,... | collective-permute-start | bytes 589832 | tf_op jit(solution)/shard_map/ppermute | solution.py:24
  37.6 7.2 %collective-permute-start.23 = (bf16[2,3,64,256]{3,2,1,0:T(8,128)(2,1)S(1)}, bf16[2,3,64,256]{3,2,1,0:T(8,128)(2,1)S(1)}, u32[]{:S(2)}, u32[]{:S(2)}) collective-permute-start(bf16[2,3,64,256]{3,2,1,0:T(8,128)(2,1)S(1)} %get-tuple-element.65), channel_id=1, source_target_pairs={{0,2},{1,3},{2,0},{3,1},{4,6},{5,7},{6,4},{7,5},{8,10},{9,11},{10,... | collective-permute-start | bytes 589832 | tf_op jit(solution)/shard_map/ppermute | solution.py:24
  39.6 7.8 %collective-permute-start.28 = (bf16[2,3,64,256]{3,2,1,0:T(8,128)(2,1)S(1)}, bf16[2,3,64,256]{3,2,1,0:T(8,128)(2,1)S(1)}, u32[]{:S(2)}, u32[]{:S(2)}) collective-permute-start(bf16[2,3,64,256]{3,2,1,0:T(8,128)(2,1)S(1)} %get-tuple-element.73), channel_id=1, source_target_pairs={{0,2},{1,3},{2,0},{3,1},{4,6},{5,7},{6,4},{7,5},{8,10},{9,11},{10,... | collective-permute-start | bytes 589832 | tf_op jit(solution)/shard_map/ppermute | solution.py:24
  43.2 4.7 %collective-permute-start.21 = (bf16[3,64,256]{2,1,0:T(8,128)(2,1)S(1)}, bf16[3,64,256]{2,1,0:T(8,128)(2,1)S(1)}, u32[]{:S(2)}, u32[]{:S(2)}) collective-permute-start(bf16[3,64,256]{2,1,0:T(8,128)(2,1)S(1)} %fusion.14), channel_id=1, source_target_pairs={{0,2},{1,3},{2,0},{3,1},{4,6},{5,7},{6,4},{7,5},{8,10},{9,11},{10,... | collective-permute-start | bytes 294920 | tf_op jit(solution)/shard_map/ppermute | solution.py:24
  44.8 9.1 %collective-permute-start.26 = (bf16[3,64,256]{2,1,0:T(8,128)(2,1)S(1)}, bf16[3,64,256]{2,1,0:T(8,128)(2,1)S(1)}, u32[]{:S(2)}, u32[]{:S(2)}) collective-permute-start(bf16[3,64,256]{2,1,0:T(8,128)(2,1)S(1)} %fusion.7), channel_id=1, source_target_pairs={{0,4},{1,5},{2,6},{3,7},{4,0},{5,1},{6,2},{7,3},{8,12},{9,13},{10,... | collective-permute-start | bytes 294920 | tf_op jit(solution)/shard_map/ppermute | solution.py:24
  47.3 6.6 %collective-permute-start.24 = (bf16[2,3,64,256]{3,2,1,0:T(8,128)(2,1)S(1)}, bf16[2,3,64,256]{3,2,1,0:T(8,128)(2,1)S(1)}, u32[]{:S(2)}, u32[]{:S(2)}) collective-permute-start(bf16[2,3,64,256]{3,2,1,0:T(8,128)(2,1)S(1)} %get-tuple-element.66), channel_id=1, source_target_pairs={{0,4},{1,5},{2,6},{3,7},{4,0},{5,1},{6,2},{7,3},{8,12},{9,13},{10,... | collective-permute-start | bytes 589832 | tf_op jit(solution)/shard_map/ppermute | solution.py:24
  48.0 9.2 %collective-permute-start.22 = (bf16[3,64,256]{2,1,0:T(8,128)(2,1)S(1)}, bf16[3,64,256]{2,1,0:T(8,128)(2,1)S(1)}, u32[]{:S(2)}, u32[]{:S(2)}) collective-permute-start(bf16[3,64,256]{2,1,0:T(8,128)(2,1)S(1)} %fusion.16), channel_id=1, source_target_pairs={{0,16},{1,17},{2,18},{3,19},{4,20},{5,21},{6,22},{7,23},{8,24},{9,... | collective-permute-start | bytes 294920 | tf_op jit(solution)/shard_map/ppermute | solution.py:24
  51.5 5.0 %collective-permute-start.29 = (bf16[3,64,256]{2,1,0:T(8,128)(2,1)S(1)}, bf16[3,64,256]{2,1,0:T(8,128)(2,1)S(1)}, u32[]{:S(2)}, u32[]{:S(2)}) collective-permute-start(bf16[3,64,256]{2,1,0:T(8,128)(2,1)S(1)} %fusion.4), channel_id=1, source_target_pairs={{0,4},{1,5},{2,6},{3,7},{4,0},{5,1},{6,2},{7,3},{8,12},{9,13},{10,... | collective-permute-start | bytes 294920 | tf_op jit(solution)/shard_map/ppermute | solution.py:24
  54.0 7.2 %collective-permute-start.27 = (bf16[3,64,256]{2,1,0:T(8,128)(2,1)S(1)}, bf16[3,64,256]{2,1,0:T(8,128)(2,1)S(1)}, u32[]{:S(2)}, u32[]{:S(2)}) collective-permute-start(bf16[3,64,256]{2,1,0:T(8,128)(2,1)S(1)} %fusion.9), channel_id=1, source_target_pairs={{0,24},{1,25},{2,26},{3,27},{4,28},{5,29},{6,30},{7,31},{8,16},{9,... | collective-permute-start | bytes 294920 | tf_op jit(solution)/shard_map/ppermute | solution.py:24
  56.2 5.2 %collective-permute-start.25 = (bf16[3,64,256]{2,1,0:T(8,128)(2,1)S(1)}, bf16[3,64,256]{2,1,0:T(8,128)(2,1)S(1)}, u32[]{:S(2)}, u32[]{:S(2)}) collective-permute-start(bf16[3,64,256]{2,1,0:T(8,128)(2,1)S(1)} %fusion.10), channel_id=1, source_target_pairs={{0,2},{1,3},{2,0},{3,1},{4,6},{5,7},{6,4},{7,5},{8,10},{9,11},{10,... | collective-permute-start | bytes 294920 | tf_op jit(solution)/shard_map/ppermute | solution.py:24
  56.6 5.9 %collective-permute-start.30 = (bf16[3,64,256]{2,1,0:T(8,128)(2,1)S(1)}, bf16[3,64,256]{2,1,0:T(8,128)(2,1)S(1)}, u32[]{:S(2)}, u32[]{:S(2)}) collective-permute-start(bf16[3,64,256]{2,1,0:T(8,128)(2,1)S(1)} %fusion.6), channel_id=1, source_target_pairs={{0,8},{1,9},{2,10},{3,11},{4,12},{5,13},{6,14},{7,15},{8,0},{9,1},... | collective-permute-start | bytes 294920 | tf_op jit(solution)/shard_map/ppermute | solution.py:24
  62.7 6.7 %collective-permute-start.37 = (bf16[3,64,256]{2,1,0:T(8,128)(2,1)S(1)}, bf16[3,64,256]{2,1,0:T(8,128)(2,1)S(1)}, u32[]{:S(2)}, u32[]{:S(2)}) collective-permute-start(bf16[3,64,256]{2,1,0:T(8,128)(2,1)S(1)} %get-tuple-element.88.refs_0_), channel_id=1, source_target_pairs={{0,16},{1,17},{2,18},{3,19},{4,20},{5,21},{6,22},{7,23},{8,24},{9,... | collective-permute-start | bytes 294920 | tf_op jit(solution)/shard_map/ppermute | solution.py:24
  64.1 5.8 %collective-permute-start.34 = (bf16[3,64,256]{2,1,0:T(8,128)(2,1)S(1)}, bf16[3,64,256]{2,1,0:T(8,128)(2,1)S(1)}, u32[]{:S(2)}, u32[]{:S(2)}) collective-permute-start(bf16[3,64,256]{2,1,0:T(8,128)(2,1)S(1)} %get-tuple-element.88.refs_0_), channel_id=1, source_target_pairs={{0,8},{1,9},{2,10},{3,11},{4,12},{5,13},{6,14},{7,15},{8,0},{9,1},... | collective-permute-start | bytes 294920 | tf_op jit(solution)/shard_map/ppermute | solution.py:24
  66.6 5.7 %collective-permute-start.32 = (bf16[3,64,256]{2,1,0:T(8,128)(2,1)S(1)}, bf16[3,64,256]{2,1,0:T(8,128)(2,1)S(1)}, u32[]{:S(2)}, u32[]{:S(2)}) collective-permute-start(bf16[3,64,256]{2,1,0:T(8,128)(2,1)S(1)} %get-tuple-element.88.refs_0_), channel_id=1, source_target_pairs={{0,4},{1,5},{2,6},{3,7},{4,0},{5,1},{6,2},{7,3},{8,12},{9,13},{10,... | collective-permute-start | bytes 294920 | tf_op jit(solution)/shard_map/ppermute | solution.py:24
  66.6 5.7 %collective-permute-start.31 = (bf16[3,64,256]{2,1,0:T(8,128)(2,1)S(1)}, bf16[3,64,256]{2,1,0:T(8,128)(2,1)S(1)}, u32[]{:S(2)}, u32[]{:S(2)}) collective-permute-start(bf16[3,64,256]{2,1,0:T(8,128)(2,1)S(1)} %get-tuple-element.88.refs_0_), channel_id=1, source_target_pairs={{0,2},{1,3},{2,0},{3,1},{4,6},{5,7},{6,4},{7,5},{8,10},{9,11},{10,... | collective-permute-start | bytes 294920 | tf_op jit(solution)/shard_map/ppermute | solution.py:24
  69.5 4.6 %collective-permute-start.41 = (bf16[3,64,256]{2,1,0:T(8,128)(2,1)S(1)}, bf16[3,64,256]{2,1,0:T(8,128)(2,1)S(1)}, u32[]{:S(2)}, u32[]{:S(2)}) collective-permute-start(bf16[3,64,256]{2,1,0:T(8,128)(2,1)S(1)} %collective-permute-done.37.refs_8_), channel_id=1, source_target_pairs={{0,8},{1,9},{2,10},{3,11},{4,12},{5,13},{6,14},{7,15},{8,0},{9,1},... | collective-permute-start | bytes 294920 | tf_op jit(solution)/shard_map/ppermute | solution.py:24
  69.8 5.5 %collective-permute-start.35 = (bf16[3,64,256]{2,1,0:T(8,128)(2,1)S(1)}, bf16[3,64,256]{2,1,0:T(8,128)(2,1)S(1)}, u32[]{:S(2)}, u32[]{:S(2)}) collective-permute-start(bf16[3,64,256]{2,1,0:T(8,128)(2,1)S(1)} %collective-permute-done.34.refs_4_), channel_id=1, source_target_pairs={{0,2},{1,3},{2,0},{3,1},{4,6},{5,7},{6,4},{7,5},{8,10},{9,11},{10,... | collective-permute-start | bytes 294920 | tf_op jit(solution)/shard_map/ppermute | solution.py:24
  70.4 16.2 %copy-start = (bf16[1,256,1024]{2,1,0:T(8,128)(2,1)S(1)}, bf16[1,256,1024]{2,1,0:T(8,128)(2,1)}, u32[]{:S(2)}) copy-start(bf16[1,256,1024]{2,1,0:T(8,128)(2,1)} %param.14) | copy-start | bytes 1572868
  72.2 5.5 %collective-permute-start.36 = (bf16[3,64,256]{2,1,0:T(8,128)(2,1)S(1)}, bf16[3,64,256]{2,1,0:T(8,128)(2,1)S(1)}, u32[]{:S(2)}, u32[]{:S(2)}) collective-permute-start(bf16[3,64,256]{2,1,0:T(8,128)(2,1)S(1)} %collective-permute-done.34.refs_4_), channel_id=1, source_target_pairs={{0,4},{1,5},{2,6},{3,7},{4,0},{5,1},{6,2},{7,3},{8,12},{9,13},{10,... | collective-permute-start | bytes 294920 | tf_op jit(solution)/shard_map/ppermute | solution.py:24
  73.4 5.6 %collective-permute-start.38 = (bf16[3,64,256]{2,1,0:T(8,128)(2,1)S(1)}, bf16[3,64,256]{2,1,0:T(8,128)(2,1)S(1)}, u32[]{:S(2)}, u32[]{:S(2)}) collective-permute-start(bf16[3,64,256]{2,1,0:T(8,128)(2,1)S(1)} %collective-permute-done.37.refs_8_), channel_id=1, source_target_pairs={{0,2},{1,3},{2,0},{3,1},{4,6},{5,7},{6,4},{7,5},{8,10},{9,11},{10,... | collective-permute-start | bytes 294920 | tf_op jit(solution)/shard_map/ppermute | solution.py:24
  75.3 6.6 %collective-permute-start.44 = (bf16[3,64,256]{2,1,0:T(8,128)(2,1)S(1)}, bf16[3,64,256]{2,1,0:T(8,128)(2,1)S(1)}, u32[]{:S(2)}, u32[]{:S(2)}) collective-permute-start(bf16[3,64,256]{2,1,0:T(8,128)(2,1)S(1)} %collective-permute-done.41.refs_12_), channel_id=1, source_target_pairs={{0,4},{1,5},{2,6},{3,7},{4,0},{5,1},{6,2},{7,3},{8,12},{9,13},{10,... | collective-permute-start | bytes 294920 | tf_op jit(solution)/shard_map/ppermute | solution.py:24
  75.4 4.6 %collective-permute-start.42 = (bf16[3,64,256]{2,1,0:T(8,128)(2,1)S(1)}, bf16[3,64,256]{2,1,0:T(8,128)(2,1)S(1)}, u32[]{:S(2)}, u32[]{:S(2)}) collective-permute-start(bf16[3,64,256]{2,1,0:T(8,128)(2,1)S(1)} %collective-permute-done.41.refs_12_), channel_id=1, source_target_pairs={{0,2},{1,3},{2,0},{3,1},{4,6},{5,7},{6,4},{7,5},{8,10},{9,11},{10,... | collective-permute-start | bytes 294920 | tf_op jit(solution)/shard_map/ppermute | solution.py:24
  77.0 5.3 %collective-permute-start.33 = (bf16[3,64,256]{2,1,0:T(8,128)(2,1)S(1)}, bf16[3,64,256]{2,1,0:T(8,128)(2,1)S(1)}, u32[]{:S(2)}, u32[]{:S(2)}) collective-permute-start(bf16[3,64,256]{2,1,0:T(8,128)(2,1)S(1)} %collective-permute-done.31.refs_1_), channel_id=1, source_target_pairs={{0,4},{1,5},{2,6},{3,7},{4,0},{5,1},{6,2},{7,3},{8,12},{9,13},{10,... | collective-permute-start | bytes 294920 | tf_op jit(solution)/shard_map/ppermute | solution.py:24
  77.7 5.0 %collective-permute-start.40 = (bf16[3,64,256]{2,1,0:T(8,128)(2,1)S(1)}, bf16[3,64,256]{2,1,0:T(8,128)(2,1)S(1)}, u32[]{:S(2)}, u32[]{:S(2)}) collective-permute-start(bf16[3,64,256]{2,1,0:T(8,128)(2,1)S(1)} %collective-permute-done.37.refs_8_), channel_id=1, source_target_pairs={{0,4},{1,5},{2,6},{3,7},{4,0},{5,1},{6,2},{7,3},{8,12},{9,13},{10,... | collective-permute-start | bytes 294920 | tf_op jit(solution)/shard_map/ppermute | solution.py:24
  79.1 4.6 %collective-permute-start.39 = (bf16[3,64,256]{2,1,0:T(8,128)(2,1)S(1)}, bf16[3,64,256]{2,1,0:T(8,128)(2,1)S(1)}, u32[]{:S(2)}, u32[]{:S(2)}) collective-permute-start(bf16[3,64,256]{2,1,0:T(8,128)(2,1)S(1)} %collective-permute-done.36.refs_6_), channel_id=1, source_target_pairs={{0,2},{1,3},{2,0},{3,1},{4,6},{5,7},{6,4},{7,5},{8,10},{9,11},{10,... | collective-permute-start | bytes 294920 | tf_op jit(solution)/shard_map/ppermute | solution.py:24
  80.0 6.6 %collective-permute-start.43 = (bf16[3,64,256]{2,1,0:T(8,128)(2,1)S(1)}, bf16[3,64,256]{2,1,0:T(8,128)(2,1)S(1)}, u32[]{:S(2)}, u32[]{:S(2)}) collective-permute-start(bf16[3,64,256]{2,1,0:T(8,128)(2,1)S(1)} %collective-permute-done.38.refs_9_), channel_id=1, source_target_pairs={{0,4},{1,5},{2,6},{3,7},{4,0},{5,1},{6,2},{7,3},{8,12},{9,13},{10,... | collective-permute-start | bytes 294920 | tf_op jit(solution)/shard_map/ppermute | solution.py:24
  81.9 4.6 %collective-permute-start.45 = (bf16[3,64,256]{2,1,0:T(8,128)(2,1)S(1)}, bf16[3,64,256]{2,1,0:T(8,128)(2,1)S(1)}, u32[]{:S(2)}, u32[]{:S(2)}) collective-permute-start(bf16[3,64,256]{2,1,0:T(8,128)(2,1)S(1)} %collective-permute-done.44.refs_14_), channel_id=1, source_target_pairs={{0,2},{1,3},{2,0},{3,1},{4,6},{5,7},{6,4},{7,5},{8,10},{9,11},{10,... | collective-permute-start | bytes 294920 | tf_op jit(solution)/shard_map/ppermute | solution.py:24
  87.4 1.9 %collective-permute-start.46 = (f32[3,3,32,256]{3,2,1,0:T(8,128)S(1)}, f32[3,3,32,256]{3,2,1,0:T(8,128)S(1)}, u32[]{:S(2)}, u32[]{:S(2)}) collective-permute-start(f32[3,3,32,256]{3,2,1,0:T(8,128)S(1)} %get-tuple-element.85), channel_id=1, source_target_pairs={{0,1},{1,0},{2,3},{3,2},{4,5},{5,4},{6,7},{7,6},{8,9},{9,8},{10,11... | collective-permute-start | bytes 884744 | tf_op jit(solution)/shard_map/ppermute | solution.py:24
  87.4 2.7 %collective-permute-start.47 = (bf16[256,1024]{1,0:T(8,128)(2,1)S(1)}, bf16[256,1024]{1,0:T(8,128)(2,1)S(1)}, u32[]{:S(2)}, u32[]{:S(2)}) collective-permute-start(bf16[256,1024]{1,0:T(8,128)(2,1)S(1)} %get-tuple-element.84), channel_id=1, source_target_pairs={{0,1},{1,0},{2,3},{3,2},{4,5},{5,4},{6,7},{7,6},{8,9},{9,8},{10,11... | collective-permute-start | bytes 1572872 | tf_op jit(solution)/shard_map/ppermute | solution.py:24

commit v13 on v12

--- a/solution.py
+++ b/solution.py
@@ -39,10 +39,8 @@
         weights[:, pl.ds(start, rows), :] = piece[...]
 
 
-def transpose_kernel(slots, own_x, other_x, own_c, other_c, x_turned, c_turned, matches):
-    me_index = lax.axis_index("dev")
-    matches[0] = jnp.where(slots[me_index] == (me_index & CORE), 1, 0)
-    chip = me_index // 2
+def transpose_kernel(own_x, other_x, own_c, other_c, x_turned, c_turned):
+    chip = lax.axis_index("dev") // 2
     tokens, width = own_x.shape
     rows = 2 * width // lax.axis_size("dev")
     lanes = max(128, rows)
@@ -80,14 +78,20 @@
                 out[before + (kind,)] = product[low : low + rows]
 
 
-def backward_kernel(count, slots, own_live, other_live, *refs):
+def slot_block(slots, slot):
+    lane = lax.broadcasted_iota(jnp.int32, slots.shape, 1)
+    return jnp.sum(jnp.where(lane == slot, slots[...], 0), axis=1, keepdims=True)
+
+
+def backward_kernel(count, slots, new_slots, own_live, other_live, *refs):
     pieces = refs[:count]
     own_x, other_x, own_c, other_c, x_turned, c_turned = refs[count : count + 6]
-    outs = refs[count + 6 : -4]
+    outs, matches = refs[count + 6 : -5], refs[-5]
     gate_grad, up_grad, hidden_all, weights = refs[-4:]
     me_index = lax.axis_index("dev")
     core = me_index & CORE
     place_pieces(me_index // 2, pieces, weights)
+    matches[...] = jnp.where(slot_block(new_slots, me_index) == core, 1, 0)
     tokens = own_x.shape[0]
     sides = ((own_x, own_c, me_index, own_live), (other_x, other_c, me_index ^ CORE, other_live))
     for part, (x_ref, c_ref, slot, live) in enumerate(sides):
@@ -97,7 +101,7 @@
         grad_hidden = jnp.dot(c_ref[...], weights[2], preferred_element_type=jnp.float32)
         gate_sig = jax.nn.sigmoid(gate_pre)
         gate_act = gate_pre * gate_sig
-        alive = jnp.where(slots[slot] == core, live[0], 0)
+        alive = jnp.where(slot_block(slots, slot) == core, live[...], 0)
         keep = lax.broadcasted_iota(jnp.int32, gate_pre.shape, 0) < alive
         grad_up = grad_hidden * gate_act
         grad_gate = grad_hidden * up_pre * gate_sig * (1.0 + gate_pre * (1.0 - gate_sig))
@@ -128,28 +132,26 @@
 
 
 VMEM = pl.BlockSpec(memory_space=pltpu.VMEM)
-SMEM = pl.BlockSpec(memory_space=pltpu.SMEM)
 
 
 def params():
     return pltpu.CompilerParams(vmem_limit_bytes=VMEM_LIMIT)
 
 
-def transposed(slots, own_x, other_x, own_c, other_c):
+def transposed(own_x, other_x, own_c, other_c):
     tokens, width = own_x.shape
     return pl.pallas_call(
         transpose_kernel,
-        out_shape=[jax.ShapeDtypeStruct((width, 2 * tokens), own_x.dtype)] * 2
-        + [jax.ShapeDtypeStruct((1,), jnp.int32)],
-        in_specs=[SMEM] + [VMEM] * 4,
-        out_specs=[VMEM, VMEM, SMEM],
+        out_shape=[jax.ShapeDtypeStruct((width, 2 * tokens), own_x.dtype)] * 2,
+        in_specs=[VMEM] * 4,
+        out_specs=[VMEM] * 2,
         compiler_params=params(),
         cost_estimate=pl.CostEstimate(flops=0, bytes_accessed=16 * tokens * width, transcendentals=0),
         name="transpose_rows",
-    )(slots, own_x, other_x, own_c, other_c)
-
-
-def backward(slots, own_live, other_live, pieces, own_x, other_x, own_c, other_c, x_turned, c_turned):
+    )(own_x, other_x, own_c, other_c)
+
+
+def backward(slots, new_slots, own_live, other_live, pieces, own_x, other_x, own_c, other_c, x_turned, c_turned):
     count = len(pieces)
     kinds, rows, units = pieces[0].shape
     tokens, width = own_x.shape
@@ -157,9 +159,9 @@
     two = jax.ShapeDtypeStruct((2, kinds, rows, units), jnp.bfloat16)
     return pl.pallas_call(
         functools.partial(backward_kernel, count),
-        out_shape=[one, one, two] * (count // 4),
-        in_specs=[SMEM] * 3 + [VMEM] * (count + 6),
-        out_specs=[VMEM] * (3 * count // 4),
+        out_shape=[one, one, two] * (count // 4) + [jax.ShapeDtypeStruct((1, 1), jnp.int32)],
+        in_specs=[VMEM] * (count + 10),
+        out_specs=[VMEM] * (3 * count // 4 + 1),
         scratch_shapes=[
             pltpu.VMEM((2 * tokens, units), jnp.bfloat16),
             pltpu.VMEM((2 * tokens, units), jnp.bfloat16),
@@ -173,7 +175,7 @@
             transcendentals=2 * tokens * units,
         ),
         name="slot_gradients",
-    )(slots, own_live, other_live, *pieces, own_x, other_x, own_c, other_c, x_turned, c_turned)
+    )(slots, new_slots, own_live, other_live, *pieces, own_x, other_x, own_c, other_c, x_turned, c_turned)
 
 
 def forward(pieces, own_y, other_y):
@@ -271,12 +273,6 @@
     local_rows = master.shape[2]
     core = lax.axis_index("dev") & CORE
 
-    def mine(state):
-        return lax.dynamic_index_in_dim(state, core, 0, keepdims=False)
-
-    def partners(state):
-        return lax.dynamic_index_in_dim(state, 1 - core, 0, keepdims=False)
-
     def both_rows(own, other):
         return jnp.where(
             core == 0, jnp.concatenate([own, other], axis=-2), jnp.concatenate([other, own], axis=-2)
@@ -284,19 +280,22 @@
 
     other_x = hop(old_rows, CORE)
     other_c = hop(old_cotangent, CORE)
-    theirs = hop(jnp.stack([partners(master), partners(first), partners(second)]), CORE)
+    state = jnp.stack([master, first, second], axis=1)
+    mine = lax.dynamic_index_in_dim(state, core, 0, keepdims=False)
+    theirs = hop(lax.dynamic_index_in_dim(state, 1 - core, 0, keepdims=False), CORE)
     other_y = hop(new_rows, CORE)
     other_live = hop(live, CORE)
-    x_turned, c_turned, matches = transposed(new_slots, old_rows, other_x, old_cotangent, other_c)
+    x_turned, c_turned = transposed(old_rows, other_x, old_cotangent, other_c)
     theirs, other_y, other_live, x_turned, c_turned = lax.optimization_barrier(
         (theirs, other_y, other_live, x_turned, c_turned)
     )
-    master_two = both_rows(mine(master), theirs[0])
+    master_two = both_rows(mine[0], theirs[0])
     pieces = gather_chips(master_two.astype(jnp.bfloat16))
-    grads = backward(
-        old_slots,
-        live,
-        other_live,
+    *grads, matches = backward(
+        old_slots[None],
+        new_slots[None],
+        live[None],
+        other_live[None],
         pieces,
         old_rows,
         other_x,
@@ -306,8 +305,8 @@
         c_turned,
     )
     theirs = after(theirs, grads[0])
-    first_two = both_rows(mine(first), theirs[1])
-    second_two = both_rows(mine(second), theirs[2])
+    first_two = both_rows(mine[1], theirs[1])
+    second_two = both_rows(mine[2], theirs[2])
     grad = reduce_chips(grads)
     updated = adam_update(master_two, first_two, second_two, grad)
 
@@ -320,7 +319,7 @@
     state = jnp.where(
         core == 0, jnp.stack([own_part, from_other], axis=1), jnp.stack([from_other, own_part], axis=1)
     )
-    new_outputs = jnp.where(matches[0] == 1, own_out, hop(other_out, CORE))
+    new_outputs = jnp.where(matches == 1, own_out, hop(other_out, CORE))
     return (state[0], state[1], state[2], new_outputs[None])
 
 

time: 91.2 us -> 91.4 us (level)
  Pallas kernels: 6.3 us -> 5.15 us
  other arithmetic: 1.57 us -> 2.67 us
    squeeze x3 -> x4, local copies, waits for them, and re-layouts: 1.08 us -> 2.62 us  [the longest x2 0.97 us: block_a_core(): first_two = both_rows(mine[1], theirs[1])]
    another operation x1, other arithmetic: 0.02 us -> 1.15 us  [block_a_core(): state = jnp.stack([master, first, second], axis=1)]
    pallas_call x1, Pallas kernels: 1.57 us -> 0.59 us  [transposed(): pl.pallas_call(transpose_kernel, out_shape=[jax.ShapeDtypeStruct((width,...]
    dynamic_slice x1 -> x0, local copies, waits for them, and re-layouts: 0.96 us -> none  [partners(): return lax.dynamic_index_in_dim(state, 1 - core, 0, keepdims=False)]
  transfers between devices with their start and end apart: 48 -> 48, of which waited for: 23 -> 24; matrix products, arithmetic and copies ran while one was open for 4% -> 5% of each run, Pallas kernels for 2% -> 1%
where the time goes in v13:
time: 91.4 us; the launch traced here: 91.1 us
  starting transfers between devices  52.1 us (57%)
  waiting for transfers between devices  25.5 us (28%)
  Pallas kernels  5.15 us (6%)
  local copies, waits for them, and re-layouts  3.51 us (4%)
  other arithmetic  2.67 us (3%)
  between operations  2.18 us (2%)
    ppermute x48, starting transfers between devices, hop(): lax.ppermute(block, 'dev', [(low, low ^ mask) for low in range(count)])  52.1 us
    ppermute x48, waiting for transfers between devices, hop(): lax.ppermute(block, 'dev', [(low, low ^ mask) for low in range(count)])  25.5 us
    pallas_call x1, Pallas kernels, backward(): pl.pallas_call(functools.partial(backward_kernel, count), out_shape=[one,...  3.12 us
  transfers between devices with their start and end apart: 48, of which 24 were waited for; matrix products, arithmetic and copies ran while one was open for 5% of the time, Pallas kernels for 1%

profile of v13, /device:TPU:0, one launch (start us, length us, event | category | flops | bytes accessed | tf_op | source)
XLA Modules:
  0.0 91.1 jit_solution(12088745725006805374)
XLA Ops:
  0.7 0.5 collective-permute-start.3
  1.2 0.4 collective-permute-start.1
  1.7 1.2 %pad_maximum_fusion = f32[2,3,3,32,256]{4,3,2,1,0:T(8,128)S(1)} fusion(f32[2,1,3,32,256]{4,3,2,1,0:T(8,128)} %bitcast.96, f32[2,1,3,32,256]{4,3,2,1,0:T(8,128)} %bitcast.97, f32[2,1,3,32,256]{4,3,2,1,0:T(8,128)} %bitcast.98), kind=kLoop, calls=%fused_computation | loop fusion | flops 294912 | bytes 1179648 | tf_op jit(solution)/shard_map/stack | solution.py:283
  2.8 0.8 dynamic-slice_bitcast_fusion.1
  3.7 0.4 collective-permute-start.2
  4.2 0.6 transpose_rows.1
  4.8 0.7 collective-permute-done.2
  5.5 0.9 slice_bitcast_fusion.13
  6.4 3.8 %collective-permute-start.11 = (bf16[3,64,256]{2,1,0:T(8,128)(2,1)S(1)}, bf16[3,64,256]{2,1,0:T(8,128)(2,1)S(1)}, u32[]{:S(2)}, u32[]{:S(2)}) collective-permute-start(bf16[3,64,256]{2,1,0:T(8,128)(2,1)S(1)} %fusion.17.refs_0_), channel_id=1, source_target_pairs={{0,16},{1,17},{2,18},{3,19},{4,20},{5,21},{6,22},{7,23},{8,24},{9,... | collective-permute-start | bytes 294920 | tf_op jit(solution)/shard_map/ppermute | solution.py:24
  10.2 1.6 %collective-permute-start.8 = (bf16[3,64,256]{2,1,0:T(8,128)(2,1)S(1)}, bf16[3,64,256]{2,1,0:T(8,128)(2,1)S(1)}, u32[]{:S(2)}, u32[]{:S(2)}) collective-permute-start(bf16[3,64,256]{2,1,0:T(8,128)(2,1)S(1)} %fusion.17.refs_0_), channel_id=1, source_target_pairs={{0,8},{1,9},{2,10},{3,11},{4,12},{5,13},{6,14},{7,15},{8,0},{9,1},... | collective-permute-start | bytes 294920 | tf_op jit(solution)/shard_map/ppermute | solution.py:24
  11.8 1.5 %collective-permute-start.5 = (bf16[3,64,256]{2,1,0:T(8,128)(2,1)S(1)}, bf16[3,64,256]{2,1,0:T(8,128)(2,1)S(1)}, u32[]{:S(2)}, u32[]{:S(2)}) collective-permute-start(bf16[3,64,256]{2,1,0:T(8,128)(2,1)S(1)} %fusion.17.refs_0_), channel_id=1, source_target_pairs={{0,2},{1,3},{2,0},{3,1},{4,6},{5,7},{6,4},{7,5},{8,10},{9,11},{10,... | collective-permute-start | bytes 294920 | tf_op jit(solution)/shard_map/ppermute | solution.py:24
  13.3 1.5 %collective-permute-start.6 = (bf16[3,64,256]{2,1,0:T(8,128)(2,1)S(1)}, bf16[3,64,256]{2,1,0:T(8,128)(2,1)S(1)}, u32[]{:S(2)}, u32[]{:S(2)}) collective-permute-start(bf16[3,64,256]{2,1,0:T(8,128)(2,1)S(1)} %fusion.17.refs_0_), channel_id=1, source_target_pairs={{0,4},{1,5},{2,6},{3,7},{4,0},{5,1},{6,2},{7,3},{8,12},{9,13},{10,... | collective-permute-start | bytes 294920 | tf_op jit(solution)/shard_map/ppermute | solution.py:24
  14.8 0.9 %collective-permute-done.11.refs_8_ = bf16[3,64,256]{2,1,0:T(8,128)(2,1)S(1)} collective-permute-done((bf16[3,64,256]{2,1,0:T(8,128)(2,1)S(1)}, bf16[3,64,256]{2,1,0:T(8,128)(2,1)S(1)}, u32[]{:S(2)}, u32[]{:S(2)}) %collective-permute-start.11) | collective-permute-done | bytes 98336 | tf_op jit(solution)/shard_map/ppermute | solution.py:24
  15.8 0.6 collective-permute-start.15
  16.4 1.5 %collective-permute-start.9 = (bf16[3,64,256]{2,1,0:T(8,128)(2,1)S(1)}, bf16[3,64,256]{2,1,0:T(8,128)(2,1)S(1)}, u32[]{:S(2)}, u32[]{:S(2)}) collective-permute-start(bf16[3,64,256]{2,1,0:T(8,128)(2,1)S(1)} %collective-permute-done.8.refs_4_), channel_id=1, source_target_pairs={{0,2},{1,3},{2,0},{3,1},{4,6},{5,7},{6,4},{7,5},{8,10},{9,11},{10,... | collective-permute-start | bytes 294920 | tf_op jit(solution)/shard_map/ppermute | solution.py:24
  17.9 1.5 %collective-permute-start.10 = (bf16[3,64,256]{2,1,0:T(8,128)(2,1)S(1)}, bf16[3,64,256]{2,1,0:T(8,128)(2,1)S(1)}, u32[]{:S(2)}, u32[]{:S(2)}) collective-permute-start(bf16[3,64,256]{2,1,0:T(8,128)(2,1)S(1)} %collective-permute-done.8.refs_4_), channel_id=1, source_target_pairs={{0,4},{1,5},{2,6},{3,7},{4,0},{5,1},{6,2},{7,3},{8,12},{9,13},{10,... | collective-permute-start | bytes 294920 | tf_op jit(solution)/shard_map/ppermute | solution.py:24
  19.4 0.5 collective-permute-start.12
  20.4 0.6 collective-permute-done.9.refs_5_
  21.0 2.3 %collective-permute-start.16 = (bf16[3,64,256]{2,1,0:T(8,128)(2,1)S(1)}, bf16[3,64,256]{2,1,0:T(8,128)(2,1)S(1)}, u32[]{:S(2)}, u32[]{:S(2)}) collective-permute-start(bf16[3,64,256]{2,1,0:T(8,128)(2,1)S(1)} %collective-permute-done.15.refs_12_), channel_id=1, source_target_pairs={{0,2},{1,3},{2,0},{3,1},{4,6},{5,7},{6,4},{7,5},{8,10},{9,11},{10,... | collective-permute-start | bytes 294920 | tf_op jit(solution)/shard_map/ppermute | solution.py:24
  23.3 1.6 %collective-permute-start.18 = (bf16[3,64,256]{2,1,0:T(8,128)(2,1)S(1)}, bf16[3,64,256]{2,1,0:T(8,128)(2,1)S(1)}, u32[]{:S(2)}, u32[]{:S(2)}) collective-permute-start(bf16[3,64,256]{2,1,0:T(8,128)(2,1)S(1)} %collective-permute-done.15.refs_12_), channel_id=1, source_target_pairs={{0,4},{1,5},{2,6},{3,7},{4,0},{5,1},{6,2},{7,3},{8,12},{9,13},{10,... | collective-permute-start | bytes 294920 | tf_op jit(solution)/shard_map/ppermute | solution.py:24
  25.3 1.6 %collective-permute-start.14 = (bf16[3,64,256]{2,1,0:T(8,128)(2,1)S(1)}, bf16[3,64,256]{2,1,0:T(8,128)(2,1)S(1)}, u32[]{:S(2)}, u32[]{:S(2)}) collective-permute-start(bf16[3,64,256]{2,1,0:T(8,128)(2,1)S(1)} %collective-permute-done.11.refs_8_), channel_id=1, source_target_pairs={{0,4},{1,5},{2,6},{3,7},{4,0},{5,1},{6,2},{7,3},{8,12},{9,13},{10,... | collective-permute-start | bytes 294920 | tf_op jit(solution)/shard_map/ppermute | solution.py:24
  27.0 0.5 collective-permute-start.13
  27.4 0.9 collective-permute-done.18.refs_14_
  28.3 0.7 collective-permute-start.19
  29.0 1.0 %collective-permute-start.17 = (bf16[3,64,256]{2,1,0:T(8,128)(2,1)S(1)}, bf16[3,64,256]{2,1,0:T(8,128)(2,1)S(1)}, u32[]{:S(2)}, u32[]{:S(2)}) collective-permute-start(bf16[3,64,256]{2,1,0:T(8,128)(2,1)S(1)} %collective-permute-done.12.refs_9_), channel_id=1, source_target_pairs={{0,4},{1,5},{2,6},{3,7},{4,0},{5,1},{6,2},{7,3},{8,12},{9,13},{10,... | collective-permute-start | bytes 294920 | tf_op jit(solution)/shard_map/ppermute | solution.py:24
  30.7 0.6 collective-permute-done.14.refs_10_
  31.6 1.3 %collective-permute-done.19.refs_15_ = bf16[3,64,256]{2,1,0:T(8,128)(2,1)S(1)} collective-permute-done((bf16[3,64,256]{2,1,0:T(8,128)(2,1)S(1)}, bf16[3,64,256]{2,1,0:T(8,128)(2,1)S(1)}, u32[]{:S(2)}, u32[]{:S(2)}) %collective-permute-start.19) | collective-permute-done | bytes 98336 | tf_op jit(solution)/shard_map/ppermute | solution.py:24
  32.9 0.7 collective-permute-done.17.refs_11_
  33.6 3.1 %slot_gradients.1 = (bf16[3,64,256]{2,1,0:T(8,128)(2,1)S(1)}, bf16[3,64,256]{2,1,0:T(8,128)(2,1)S(1)}, bf16[2,3,64,256]{3,2,1,0:T(8,128)(2,1)S(1)}, bf16[3,64,25...) custom-call(s32[1,32]{1,0:T(1,128)S(1)} %bitcast.92, ...), custom_call_target="tpu_custom_call" | custom-call | flops 1610612736 | bytes 7340032 | tf_op jit(solution)/shard_map/slot_gradients/pallas_call | solution.py:160
  36.7 1.0 %collective-permute-start.20 = (bf16[2,3,64,256]{3,2,1,0:T(8,128)(2,1)S(1)}, bf16[2,3,64,256]{3,2,1,0:T(8,128)(2,1)S(1)}, u32[]{:S(2)}, u32[]{:S(2)}) collective-permute-start(bf16[2,3,64,256]{3,2,1,0:T(8,128)(2,1)S(1)} %get-tuple-element.62), channel_id=1, source_target_pairs={{0,4},{1,5},{2,6},{3,7},{4,0},{5,1},{6,2},{7,3},{8,12},{9,13},{10,... | collective-permute-start | bytes 589832 | tf_op jit(solution)/shard_map/ppermute | solution.py:24
  37.8 2.0 %collective-permute-start.23 = (bf16[2,3,64,256]{3,2,1,0:T(8,128)(2,1)S(1)}, bf16[2,3,64,256]{3,2,1,0:T(8,128)(2,1)S(1)}, u32[]{:S(2)}, u32[]{:S(2)}) collective-permute-start(bf16[2,3,64,256]{3,2,1,0:T(8,128)(2,1)S(1)} %get-tuple-element.65), channel_id=1, source_target_pairs={{0,2},{1,3},{2,0},{3,1},{4,6},{5,7},{6,4},{7,5},{8,10},{9,11},{10,... | collective-permute-start | bytes 589832 | tf_op jit(solution)/shard_map/ppermute | solution.py:24
  39.8 3.6 %collective-permute-done.20 = bf16[2,3,64,256]{3,2,1,0:T(8,128)(2,1)S(1)} collective-permute-done((bf16[2,3,64,256]{3,2,1,0:T(8,128)(2,1)S(1)}, bf16[2,3,64,256]{3,2,1,0:T(8,128)(2,1)S(1)}, u32[]{:S(2)}, u32[]{:S(2)}) %collective-permute-start.20) | collective-permute-done | bytes 196640 | tf_op jit(solution)/shard_map/ppermute | solution.py:24
  43.4 1.5 %collective-permute-start.21 = (bf16[3,64,256]{2,1,0:T(8,128)(2,1)S(1)}, bf16[3,64,256]{2,1,0:T(8,128)(2,1)S(1)}, u32[]{:S(2)}, u32[]{:S(2)}) collective-permute-start(bf16[3,64,256]{2,1,0:T(8,128)(2,1)S(1)} %fusion.14), channel_id=1, source_target_pairs={{0,2},{1,3},{2,0},{3,1},{4,6},{5,7},{6,4},{7,5},{8,10},{9,11},{10,... | collective-permute-start | bytes 294920 | tf_op jit(solution)/shard_map/ppermute | solution.py:24
  44.9 2.5 %collective-permute-start.26 = (bf16[3,64,256]{2,1,0:T(8,128)(2,1)S(1)}, bf16[3,64,256]{2,1,0:T(8,128)(2,1)S(1)}, u32[]{:S(2)}, u32[]{:S(2)}) collective-permute-start(bf16[3,64,256]{2,1,0:T(8,128)(2,1)S(1)} %fusion.7), channel_id=1, source_target_pairs={{0,4},{1,5},{2,6},{3,7},{4,0},{5,1},{6,2},{7,3},{8,12},{9,13},{10,... | collective-permute-start | bytes 294920 | tf_op jit(solution)/shard_map/ppermute | solution.py:24
  47.6 0.5 collective-permute-done.21
  48.1 3.5 %collective-permute-start.22 = (bf16[3,64,256]{2,1,0:T(8,128)(2,1)S(1)}, bf16[3,64,256]{2,1,0:T(8,128)(2,1)S(1)}, u32[]{:S(2)}, u32[]{:S(2)}) collective-permute-start(bf16[3,64,256]{2,1,0:T(8,128)(2,1)S(1)} %fusion.16), channel_id=1, source_target_pairs={{0,16},{1,17},{2,18},{3,19},{4,20},{5,21},{6,22},{7,23},{8,24},{9,... | collective-permute-start | bytes 294920 | tf_op jit(solution)/shard_map/ppermute | solution.py:24
  51.6 2.5 %collective-permute-start.29 = (bf16[3,64,256]{2,1,0:T(8,128)(2,1)S(1)}, bf16[3,64,256]{2,1,0:T(8,128)(2,1)S(1)}, u32[]{:S(2)}, u32[]{:S(2)}) collective-permute-start(bf16[3,64,256]{2,1,0:T(8,128)(2,1)S(1)} %fusion.4), channel_id=1, source_target_pairs={{0,4},{1,5},{2,6},{3,7},{4,0},{5,1},{6,2},{7,3},{8,12},{9,13},{10,... | collective-permute-start | bytes 294920 | tf_op jit(solution)/shard_map/ppermute | solution.py:24
  54.2 2.3 %collective-permute-start.27 = (bf16[3,64,256]{2,1,0:T(8,128)(2,1)S(1)}, bf16[3,64,256]{2,1,0:T(8,128)(2,1)S(1)}, u32[]{:S(2)}, u32[]{:S(2)}) collective-permute-start(bf16[3,64,256]{2,1,0:T(8,128)(2,1)S(1)} %fusion.9), channel_id=1, source_target_pairs={{0,24},{1,25},{2,26},{3,27},{4,28},{5,29},{6,30},{7,31},{8,16},{9,... | collective-permute-start | bytes 294920 | tf_op jit(solution)/shard_map/ppermute | solution.py:24
  56.7 0.6 collective-permute-start.30
  57.3 1.0 %slice_bitcast_fusion.12 = (f32[3,32,256]{2,1,0:T(8,128)S(1)}, f32[3,32,256]{2,1,0:T(8,128)S(1)}) fusion(f32[3,3,32,256]{3,2,1,0:T(8,128)} %collective-permute-done), kind=kLoop, calls=%fused_computation.52 | loop fusion | bytes 393216 | tf_op jit(solution)/shard_map/squeeze | solution.py:308
  58.3 2.9 %collective-permute-done.27 = bf16[3,64,256]{2,1,0:T(8,128)(2,1)S(1)} collective-permute-done((bf16[3,64,256]{2,1,0:T(8,128)(2,1)S(1)}, bf16[3,64,256]{2,1,0:T(8,128)(2,1)S(1)}, u32[]{:S(2)}, u32[]{:S(2)}) %collective-permute-start.27) | collective-permute-done | bytes 98336 | tf_op jit(solution)/shard_map/ppermute | solution.py:24
  61.6 1.0 %collective-permute-done.30 = bf16[3,64,256]{2,1,0:T(8,128)(2,1)S(1)} collective-permute-done((bf16[3,64,256]{2,1,0:T(8,128)(2,1)S(1)}, bf16[3,64,256]{2,1,0:T(8,128)(2,1)S(1)}, u32[]{:S(2)}, u32[]{:S(2)}) %collective-permute-start.30) | collective-permute-done | bytes 98336 | tf_op jit(solution)/shard_map/ppermute | solution.py:24
  62.9 1.4 %collective-permute-start.37 = (bf16[3,64,256]{2,1,0:T(8,128)(2,1)S(1)}, bf16[3,64,256]{2,1,0:T(8,128)(2,1)S(1)}, u32[]{:S(2)}, u32[]{:S(2)}) collective-permute-start(bf16[3,64,256]{2,1,0:T(8,128)(2,1)S(1)} %get-tuple-element.88.refs_0_), channel_id=1, source_target_pairs={{0,16},{1,17},{2,18},{3,19},{4,20},{5,21},{6,22},{7,23},{8,24},{9,... | collective-permute-start | bytes 294920 | tf_op jit(solution)/shard_map/ppermute | solution.py:24
  64.3 2.5 %collective-permute-start.34 = (bf16[3,64,256]{2,1,0:T(8,128)(2,1)S(1)}, bf16[3,64,256]{2,1,0:T(8,128)(2,1)S(1)}, u32[]{:S(2)}, u32[]{:S(2)}) collective-permute-start(bf16[3,64,256]{2,1,0:T(8,128)(2,1)S(1)} %get-tuple-element.88.refs_0_), channel_id=1, source_target_pairs={{0,8},{1,9},{2,10},{3,11},{4,12},{5,13},{6,14},{7,15},{8,0},{9,1},... | collective-permute-start | bytes 294920 | tf_op jit(solution)/shard_map/ppermute | solution.py:24
  66.7 1.1 %collective-permute-start.31 = (bf16[3,64,256]{2,1,0:T(8,128)(2,1)S(1)}, bf16[3,64,256]{2,1,0:T(8,128)(2,1)S(1)}, u32[]{:S(2)}, u32[]{:S(2)}) collective-permute-start(bf16[3,64,256]{2,1,0:T(8,128)(2,1)S(1)} %get-tuple-element.88.refs_0_), channel_id=1, source_target_pairs={{0,2},{1,3},{2,0},{3,1},{4,6},{5,7},{6,4},{7,5},{8,10},{9,11},{10,... | collective-permute-start | bytes 294920 | tf_op jit(solution)/shard_map/ppermute | solution.py:24
  67.8 1.8 %collective-permute-done.37.refs_8_ = bf16[3,64,256]{2,1,0:T(8,128)(2,1)S(1)} collective-permute-done((bf16[3,64,256]{2,1,0:T(8,128)(2,1)S(1)}, bf16[3,64,256]{2,1,0:T(8,128)(2,1)S(1)}, u32[]{:S(2)}, u32[]{:S(2)}) %collective-permute-start.37) | collective-permute-done | bytes 98336 | tf_op jit(solution)/shard_map/ppermute | solution.py:24
  69.9 0.6 collective-permute-start.35
  70.6 1.8 %collective-permute-done.32.refs_2_ = bf16[3,64,256]{2,1,0:T(8,128)(2,1)S(1)} collective-permute-done((bf16[3,64,256]{2,1,0:T(8,128)(2,1)S(1)}, bf16[3,64,256]{2,1,0:T(8,128)(2,1)S(1)}, u32[]{:S(2)}, u32[]{:S(2)}) %collective-permute-start.32) | collective-permute-done | bytes 98336 | tf_op jit(solution)/shard_map/ppermute | solution.py:24
  72.4 1.1 %collective-permute-start.36 = (bf16[3,64,256]{2,1,0:T(8,128)(2,1)S(1)}, bf16[3,64,256]{2,1,0:T(8,128)(2,1)S(1)}, u32[]{:S(2)}, u32[]{:S(2)}) collective-permute-start(bf16[3,64,256]{2,1,0:T(8,128)(2,1)S(1)} %collective-permute-done.34.refs_4_), channel_id=1, source_target_pairs={{0,4},{1,5},{2,6},{3,7},{4,0},{5,1},{6,2},{7,3},{8,12},{9,13},{10,... | collective-permute-start | bytes 294920 | tf_op jit(solution)/shard_map/ppermute | solution.py:24
  73.6 0.6 collective-permute-done.41.refs_12_
  74.2 1.2 %collective-permute-done.35.refs_5_ = bf16[3,64,256]{2,1,0:T(8,128)(2,1)S(1)} collective-permute-done((bf16[3,64,256]{2,1,0:T(8,128)(2,1)S(1)}, bf16[3,64,256]{2,1,0:T(8,128)(2,1)S(1)}, u32[]{:S(2)}, u32[]{:S(2)}) %collective-permute-start.35) | collective-permute-done | bytes 98336 | tf_op jit(solution)/shard_map/ppermute | solution.py:24
  75.6 1.4 %collective-permute-start.42 = (bf16[3,64,256]{2,1,0:T(8,128)(2,1)S(1)}, bf16[3,64,256]{2,1,0:T(8,128)(2,1)S(1)}, u32[]{:S(2)}, u32[]{:S(2)}) collective-permute-start(bf16[3,64,256]{2,1,0:T(8,128)(2,1)S(1)} %collective-permute-done.41.refs_12_), channel_id=1, source_target_pairs={{0,2},{1,3},{2,0},{3,1},{4,6},{5,7},{6,4},{7,5},{8,10},{9,11},{10,... | collective-permute-start | bytes 294920 | tf_op jit(solution)/shard_map/ppermute | solution.py:24
  77.1 0.7 collective-permute-start.33
  77.9 1.4 %collective-permute-start.40 = (bf16[3,64,256]{2,1,0:T(8,128)(2,1)S(1)}, bf16[3,64,256]{2,1,0:T(8,128)(2,1)S(1)}, u32[]{:S(2)}, u32[]{:S(2)}) collective-permute-start(bf16[3,64,256]{2,1,0:T(8,128)(2,1)S(1)} %collective-permute-done.37.refs_8_), channel_id=1, source_target_pairs={{0,4},{1,5},{2,6},{3,7},{4,0},{5,1},{6,2},{7,3},{8,12},{9,13},{10,... | collective-permute-start | bytes 294920 | tf_op jit(solution)/shard_map/ppermute | solution.py:24
  79.2 0.6 collective-permute-start.39
  79.8 0.4 collective-permute-done.42.refs_13_
  80.3 1.8 %collective-permute-start.43 = (bf16[3,64,256]{2,1,0:T(8,128)(2,1)S(1)}, bf16[3,64,256]{2,1,0:T(8,128)(2,1)S(1)}, u32[]{:S(2)}, u32[]{:S(2)}) collective-permute-start(bf16[3,64,256]{2,1,0:T(8,128)(2,1)S(1)} %collective-permute-done.38.refs_9_), channel_id=1, source_target_pairs={{0,4},{1,5},{2,6},{3,7},{4,0},{5,1},{6,2},{7,3},{8,12},{9,13},{10,... | collective-permute-start | bytes 294920 | tf_op jit(solution)/shard_map/ppermute | solution.py:24
  82.9 1.0 %collective-permute-done.39.refs_7_ = bf16[3,64,256]{2,1,0:T(8,128)(2,1)S(1)} collective-permute-done((bf16[3,64,256]{2,1,0:T(8,128)(2,1)S(1)}, bf16[3,64,256]{2,1,0:T(8,128)(2,1)S(1)}, u32[]{:S(2)}, u32[]{:S(2)}) %collective-permute-start.39) | collective-permute-done | bytes 98336 | tf_op jit(solution)/shard_map/ppermute | solution.py:24
  83.8 2.9 %collective-permute-done.45.refs_15_ = bf16[3,64,256]{2,1,0:T(8,128)(2,1)S(1)} collective-permute-done((bf16[3,64,256]{2,1,0:T(8,128)(2,1)S(1)}, bf16[3,64,256]{2,1,0:T(8,128)(2,1)S(1)}, u32[]{:S(2)}, u32[]{:S(2)}) %collective-permute-start.45) | collective-permute-done | bytes 98336 | tf_op jit(solution)/shard_map/ppermute | solution.py:24
  86.7 0.8 other_outputs.1
  87.6 0.5 collective-permute-start.47
  88.7 0.7 own_outputs.1
  89.5 0.8 slice_bitcast_fusion
  90.3 0.8 select_bitcast_fusion
  (66 shorter events, 4.2 us)
Async XLA Ops:
  0.6 3.5 %copy-start.1 = (bf16[1,256,1024]{2,1,0:T(8,128)(2,1)S(1)}, bf16[1,256,1024]{2,1,0:T(8,128)(2,1)}, u32[]{:S(2)}) copy-start(bf16[1,256,1024]{2,1,0:T(8,128)(2,1)} %param.12) | copy-start | bytes 1572868
  0.6 3.5 %copy-start.2 = (bf16[1,256,1024]{2,1,0:T(8,128)(2,1)S(1)}, bf16[1,256,1024]{2,1,0:T(8,128)(2,1)}, u32[]{:S(2)}) copy-start(bf16[1,256,1024]{2,1,0:T(8,128)(2,1)} %param.13) | copy-start | bytes 1572868
  0.7 3.5 %collective-permute-start.3 = (bf16[256,1024]{1,0:T(8,128)(2,1)}, bf16[256,1024]{1,0:T(8,128)(2,1)S(1)}, u32[]{:S(2)}, u32[]{:S(2)}) collective-permute-start(bf16[256,1024]{1,0:T(8,128)(2,1)} %bitcast.86), channel_id=1, source_target_pairs={{0,1},{1,0},{2,3},{3,2},{4,5},{5,4},{6,7},{7,6},{8,9},{9,8},{10,11... | collective-permute-start | bytes 1572872 | tf_op jit(solution)/shard_map/ppermute | solution.py:24
  1.2 3.0 %collective-permute-start.4 = (bf16[256,1024]{1,0:T(8,128)(2,1)}, bf16[256,1024]{1,0:T(8,128)(2,1)S(1)}, u32[]{:S(2)}, u32[]{:S(2)}) collective-permute-start(bf16[256,1024]{1,0:T(8,128)(2,1)} %bitcast.89), channel_id=1, source_target_pairs={{0,1},{1,0},{2,3},{3,2},{4,5},{5,4},{6,7},{7,6},{8,9},{9,8},{10,11... | collective-permute-start | bytes 1572872 | tf_op jit(solution)/shard_map/ppermute | solution.py:24
  1.2 4.3 %collective-permute-start.1 = (bf16[256,1024]{1,0:T(8,128)(2,1)}, bf16[256,1024]{1,0:T(8,128)(2,1)S(1)}, u32[]{:S(2)}, u32[]{:S(2)}) collective-permute-start(bf16[256,1024]{1,0:T(8,128)(2,1)} %bitcast.83), channel_id=1, source_target_pairs={{0,1},{1,0},{2,3},{3,2},{4,5},{5,4},{6,7},{7,6},{8,9},{9,8},{10,11... | collective-permute-start | bytes 1572872 | tf_op jit(solution)/shard_map/ppermute | solution.py:24
  3.6 1.9 %collective-permute-start = (f32[3,3,32,256]{3,2,1,0:T(8,128)}, f32[3,3,32,256]{3,2,1,0:T(8,128)}, u32[]{:S(2)}, u32[]{:S(2)}) collective-permute-start(f32[3,3,32,256]{3,2,1,0:T(8,128)} %dynamic-slice_bitcast_fusion.1), channel_id=1, source_target_pairs={{0,1},{1,0},{2,3},{3,2},{4,5},{5,4},{6,7},{7,6},{8,9},{9,8},{10,11... | collective-permute-start | bytes 884744 | tf_op jit(solution)/shard_map/ppermute | solution.py:24
  3.7 1.8 %collective-permute-start.2 = (s32[1]{0:T(128)}, s32[1]{0:T(128)}, u32[]{:S(2)}, u32[]{:S(2)}) collective-permute-start(s32[1]{0:T(128)} %param.17), channel_id=1, source_target_pairs={{0,1},{1,0},{2,3},{3,2},{4,5},{5,4},{6,7},{7,6},{8,9},{9,8},{10,11... | collective-permute-start | bytes 20 | tf_op jit(solution)/shard_map/ppermute | solution.py:24
  4.1 29.5 %copy-start.3 = (s32[32]{0:T(128)S(1)}, s32[32]{0:T(128)}, u32[]{:S(2)}) copy-start(s32[32]{0:T(128)} %param.15) | copy-start | bytes 388
  4.1 29.5 %copy-start.4 = (s32[32]{0:T(128)S(1)}, s32[32]{0:T(128)}, u32[]{:S(2)}) copy-start(s32[32]{0:T(128)} %param.16) | copy-start | bytes 388
  6.4 9.3 %collective-permute-start.11 = (bf16[3,64,256]{2,1,0:T(8,128)(2,1)S(1)}, bf16[3,64,256]{2,1,0:T(8,128)(2,1)S(1)}, u32[]{:S(2)}, u32[]{:S(2)}) collective-permute-start(bf16[3,64,256]{2,1,0:T(8,128)(2,1)S(1)} %fusion.17.refs_0_), channel_id=1, source_target_pairs={{0,16},{1,17},{2,18},{3,19},{4,20},{5,21},{6,22},{7,23},{8,24},{9,... | collective-permute-start | bytes 294920 | tf_op jit(solution)/shard_map/ppermute | solution.py:24
  10.2 6.2 %collective-permute-start.8 = (bf16[3,64,256]{2,1,0:T(8,128)(2,1)S(1)}, bf16[3,64,256]{2,1,0:T(8,128)(2,1)S(1)}, u32[]{:S(2)}, u32[]{:S(2)}) collective-permute-start(bf16[3,64,256]{2,1,0:T(8,128)(2,1)S(1)} %fusion.17.refs_0_), channel_id=1, source_target_pairs={{0,8},{1,9},{2,10},{3,11},{4,12},{5,13},{6,14},{7,15},{8,0},{9,1},... | collective-permute-start | bytes 294920 | tf_op jit(solution)/shard_map/ppermute | solution.py:24
  11.8 6.1 %collective-permute-start.5 = (bf16[3,64,256]{2,1,0:T(8,128)(2,1)S(1)}, bf16[3,64,256]{2,1,0:T(8,128)(2,1)S(1)}, u32[]{:S(2)}, u32[]{:S(2)}) collective-permute-start(bf16[3,64,256]{2,1,0:T(8,128)(2,1)S(1)} %fusion.17.refs_0_), channel_id=1, source_target_pairs={{0,2},{1,3},{2,0},{3,1},{4,6},{5,7},{6,4},{7,5},{8,10},{9,11},{10,... | collective-permute-start | bytes 294920 | tf_op jit(solution)/shard_map/ppermute | solution.py:24
  13.3 6.1 %collective-permute-start.6 = (bf16[3,64,256]{2,1,0:T(8,128)(2,1)S(1)}, bf16[3,64,256]{2,1,0:T(8,128)(2,1)S(1)}, u32[]{:S(2)}, u32[]{:S(2)}) collective-permute-start(bf16[3,64,256]{2,1,0:T(8,128)(2,1)S(1)} %fusion.17.refs_0_), channel_id=1, source_target_pairs={{0,4},{1,5},{2,6},{3,7},{4,0},{5,1},{6,2},{7,3},{8,12},{9,13},{10,... | collective-permute-start | bytes 294920 | tf_op jit(solution)/shard_map/ppermute | solution.py:24
  15.8 4.6 %collective-permute-start.15 = (bf16[3,64,256]{2,1,0:T(8,128)(2,1)S(1)}, bf16[3,64,256]{2,1,0:T(8,128)(2,1)S(1)}, u32[]{:S(2)}, u32[]{:S(2)}) collective-permute-start(bf16[3,64,256]{2,1,0:T(8,128)(2,1)S(1)} %collective-permute-done.11.refs_8_), channel_id=1, source_target_pairs={{0,8},{1,9},{2,10},{3,11},{4,12},{5,13},{6,14},{7,15},{8,0},{9,1},... | collective-permute-start | bytes 294920 | tf_op jit(solution)/shard_map/ppermute | solution.py:24
  16.4 4.6 %collective-permute-start.9 = (bf16[3,64,256]{2,1,0:T(8,128)(2,1)S(1)}, bf16[3,64,256]{2,1,0:T(8,128)(2,1)S(1)}, u32[]{:S(2)}, u32[]{:S(2)}) collective-permute-start(bf16[3,64,256]{2,1,0:T(8,128)(2,1)S(1)} %collective-permute-done.8.refs_4_), channel_id=1, source_target_pairs={{0,2},{1,3},{2,0},{3,1},{4,6},{5,7},{6,4},{7,5},{8,10},{9,11},{10,... | collective-permute-start | bytes 294920 | tf_op jit(solution)/shard_map/ppermute | solution.py:24
  17.9 7.4 %collective-permute-start.10 = (bf16[3,64,256]{2,1,0:T(8,128)(2,1)S(1)}, bf16[3,64,256]{2,1,0:T(8,128)(2,1)S(1)}, u32[]{:S(2)}, u32[]{:S(2)}) collective-permute-start(bf16[3,64,256]{2,1,0:T(8,128)(2,1)S(1)} %collective-permute-done.8.refs_4_), channel_id=1, source_target_pairs={{0,4},{1,5},{2,6},{3,7},{4,0},{5,1},{6,2},{7,3},{8,12},{9,13},{10,... | collective-permute-start | bytes 294920 | tf_op jit(solution)/shard_map/ppermute | solution.py:24
  19.4 7.5 %collective-permute-start.12 = (bf16[3,64,256]{2,1,0:T(8,128)(2,1)S(1)}, bf16[3,64,256]{2,1,0:T(8,128)(2,1)S(1)}, u32[]{:S(2)}, u32[]{:S(2)}) collective-permute-start(bf16[3,64,256]{2,1,0:T(8,128)(2,1)S(1)} %collective-permute-done.11.refs_8_), channel_id=1, source_target_pairs={{0,2},{1,3},{2,0},{3,1},{4,6},{5,7},{6,4},{7,5},{8,10},{9,11},{10,... | collective-permute-start | bytes 294920 | tf_op jit(solution)/shard_map/ppermute | solution.py:24
  21.0 6.4 %collective-permute-start.16 = (bf16[3,64,256]{2,1,0:T(8,128)(2,1)S(1)}, bf16[3,64,256]{2,1,0:T(8,128)(2,1)S(1)}, u32[]{:S(2)}, u32[]{:S(2)}) collective-permute-start(bf16[3,64,256]{2,1,0:T(8,128)(2,1)S(1)} %collective-permute-done.15.refs_12_), channel_id=1, source_target_pairs={{0,2},{1,3},{2,0},{3,1},{4,6},{5,7},{6,4},{7,5},{8,10},{9,11},{10,... | collective-permute-start | bytes 294920 | tf_op jit(solution)/shard_map/ppermute | solution.py:24
  23.3 5.0 %collective-permute-start.18 = (bf16[3,64,256]{2,1,0:T(8,128)(2,1)S(1)}, bf16[3,64,256]{2,1,0:T(8,128)(2,1)S(1)}, u32[]{:S(2)}, u32[]{:S(2)}) collective-permute-start(bf16[3,64,256]{2,1,0:T(8,128)(2,1)S(1)} %collective-permute-done.15.refs_12_), channel_id=1, source_target_pairs={{0,4},{1,5},{2,6},{3,7},{4,0},{5,1},{6,2},{7,3},{8,12},{9,13},{10,... | collective-permute-start | bytes 294920 | tf_op jit(solution)/shard_map/ppermute | solution.py:24
  24.9 5.7 %collective-permute-start.7 = (bf16[3,64,256]{2,1,0:T(8,128)(2,1)S(1)}, bf16[3,64,256]{2,1,0:T(8,128)(2,1)S(1)}, u32[]{:S(2)}, u32[]{:S(2)}) collective-permute-start(bf16[3,64,256]{2,1,0:T(8,128)(2,1)S(1)} %collective-permute-done.5.refs_1_), channel_id=1, source_target_pairs={{0,4},{1,5},{2,6},{3,7},{4,0},{5,1},{6,2},{7,3},{8,12},{9,13},{10,... | collective-permute-start | bytes 294920 | tf_op jit(solution)/shard_map/ppermute | solution.py:24
  25.3 6.0 %collective-permute-start.14 = (bf16[3,64,256]{2,1,0:T(8,128)(2,1)S(1)}, bf16[3,64,256]{2,1,0:T(8,128)(2,1)S(1)}, u32[]{:S(2)}, u32[]{:S(2)}) collective-permute-start(bf16[3,64,256]{2,1,0:T(8,128)(2,1)S(1)} %collective-permute-done.11.refs_8_), channel_id=1, source_target_pairs={{0,4},{1,5},{2,6},{3,7},{4,0},{5,1},{6,2},{7,3},{8,12},{9,13},{10,... | collective-permute-start | bytes 294920 | tf_op jit(solution)/shard_map/ppermute | solution.py:24
  27.0 4.6 %collective-permute-start.13 = (bf16[3,64,256]{2,1,0:T(8,128)(2,1)S(1)}, bf16[3,64,256]{2,1,0:T(8,128)(2,1)S(1)}, u32[]{:S(2)}, u32[]{:S(2)}) collective-permute-start(bf16[3,64,256]{2,1,0:T(8,128)(2,1)S(1)} %collective-permute-done.10.refs_6_), channel_id=1, source_target_pairs={{0,2},{1,3},{2,0},{3,1},{4,6},{5,7},{6,4},{7,5},{8,10},{9,11},{10,... | collective-permute-start | bytes 294920 | tf_op jit(solution)/shard_map/ppermute | solution.py:24
  28.3 4.6 %collective-permute-start.19 = (bf16[3,64,256]{2,1,0:T(8,128)(2,1)S(1)}, bf16[3,64,256]{2,1,0:T(8,128)(2,1)S(1)}, u32[]{:S(2)}, u32[]{:S(2)}) collective-permute-start(bf16[3,64,256]{2,1,0:T(8,128)(2,1)S(1)} %collective-permute-done.18.refs_14_), channel_id=1, source_target_pairs={{0,2},{1,3},{2,0},{3,1},{4,6},{5,7},{6,4},{7,5},{8,10},{9,11},{10,... | collective-permute-start | bytes 294920 | tf_op jit(solution)/shard_map/ppermute | solution.py:24
  29.0 4.6 %collective-permute-start.17 = (bf16[3,64,256]{2,1,0:T(8,128)(2,1)S(1)}, bf16[3,64,256]{2,1,0:T(8,128)(2,1)S(1)}, u32[]{:S(2)}, u32[]{:S(2)}) collective-permute-start(bf16[3,64,256]{2,1,0:T(8,128)(2,1)S(1)} %collective-permute-done.12.refs_9_), channel_id=1, source_target_pairs={{0,4},{1,5},{2,6},{3,7},{4,0},{5,1},{6,2},{7,3},{8,12},{9,13},{10,... | collective-permute-start | bytes 294920 | tf_op jit(solution)/shard_map/ppermute | solution.py:24
  36.7 6.6 %collective-permute-start.20 = (bf16[2,3,64,256]{3,2,1,0:T(8,128)(2,1)S(1)}, bf16[2,3,64,256]{3,2,1,0:T(8,128)(2,1)S(1)}, u32[]{:S(2)}, u32[]{:S(2)}) collective-permute-start(bf16[2,3,64,256]{3,2,1,0:T(8,128)(2,1)S(1)} %get-tuple-element.62), channel_id=1, source_target_pairs={{0,4},{1,5},{2,6},{3,7},{4,0},{5,1},{6,2},{7,3},{8,12},{9,13},{10,... | collective-permute-start | bytes 589832 | tf_op jit(solution)/shard_map/ppermute | solution.py:24
  37.8 7.1 %collective-permute-start.23 = (bf16[2,3,64,256]{3,2,1,0:T(8,128)(2,1)S(1)}, bf16[2,3,64,256]{3,2,1,0:T(8,128)(2,1)S(1)}, u32[]{:S(2)}, u32[]{:S(2)}) collective-permute-start(bf16[2,3,64,256]{3,2,1,0:T(8,128)(2,1)S(1)} %get-tuple-element.65), channel_id=1, source_target_pairs={{0,2},{1,3},{2,0},{3,1},{4,6},{5,7},{6,4},{7,5},{8,10},{9,11},{10,... | collective-permute-start | bytes 589832 | tf_op jit(solution)/shard_map/ppermute | solution.py:24
  39.7 7.8 %collective-permute-start.28 = (bf16[2,3,64,256]{3,2,1,0:T(8,128)(2,1)S(1)}, bf16[2,3,64,256]{3,2,1,0:T(8,128)(2,1)S(1)}, u32[]{:S(2)}, u32[]{:S(2)}) collective-permute-start(bf16[2,3,64,256]{3,2,1,0:T(8,128)(2,1)S(1)} %get-tuple-element.73), channel_id=1, source_target_pairs={{0,2},{1,3},{2,0},{3,1},{4,6},{5,7},{6,4},{7,5},{8,10},{9,11},{10,... | collective-permute-start | bytes 589832 | tf_op jit(solution)/shard_map/ppermute | solution.py:24
  43.4 4.7 %collective-permute-start.21 = (bf16[3,64,256]{2,1,0:T(8,128)(2,1)S(1)}, bf16[3,64,256]{2,1,0:T(8,128)(2,1)S(1)}, u32[]{:S(2)}, u32[]{:S(2)}) collective-permute-start(bf16[3,64,256]{2,1,0:T(8,128)(2,1)S(1)} %fusion.14), channel_id=1, source_target_pairs={{0,2},{1,3},{2,0},{3,1},{4,6},{5,7},{6,4},{7,5},{8,10},{9,11},{10,... | collective-permute-start | bytes 294920 | tf_op jit(solution)/shard_map/ppermute | solution.py:24
  44.9 9.2 %collective-permute-start.26 = (bf16[3,64,256]{2,1,0:T(8,128)(2,1)S(1)}, bf16[3,64,256]{2,1,0:T(8,128)(2,1)S(1)}, u32[]{:S(2)}, u32[]{:S(2)}) collective-permute-start(bf16[3,64,256]{2,1,0:T(8,128)(2,1)S(1)} %fusion.7), channel_id=1, source_target_pairs={{0,4},{1,5},{2,6},{3,7},{4,0},{5,1},{6,2},{7,3},{8,12},{9,13},{10,... | collective-permute-start | bytes 294920 | tf_op jit(solution)/shard_map/ppermute | solution.py:24
  47.5 6.7 %collective-permute-start.24 = (bf16[2,3,64,256]{3,2,1,0:T(8,128)(2,1)S(1)}, bf16[2,3,64,256]{3,2,1,0:T(8,128)(2,1)S(1)}, u32[]{:S(2)}, u32[]{:S(2)}) collective-permute-start(bf16[2,3,64,256]{3,2,1,0:T(8,128)(2,1)S(1)} %get-tuple-element.66), channel_id=1, source_target_pairs={{0,4},{1,5},{2,6},{3,7},{4,0},{5,1},{6,2},{7,3},{8,12},{9,13},{10,... | collective-permute-start | bytes 589832 | tf_op jit(solution)/shard_map/ppermute | solution.py:24
  48.1 10.2 %collective-permute-start.22 = (bf16[3,64,256]{2,1,0:T(8,128)(2,1)S(1)}, bf16[3,64,256]{2,1,0:T(8,128)(2,1)S(1)}, u32[]{:S(2)}, u32[]{:S(2)}) collective-permute-start(bf16[3,64,256]{2,1,0:T(8,128)(2,1)S(1)} %fusion.16), channel_id=1, source_target_pairs={{0,16},{1,17},{2,18},{3,19},{4,20},{5,21},{6,22},{7,23},{8,24},{9,... | collective-permute-start | bytes 294920 | tf_op jit(solution)/shard_map/ppermute | solution.py:24
  51.6 5.1 %collective-permute-start.29 = (bf16[3,64,256]{2,1,0:T(8,128)(2,1)S(1)}, bf16[3,64,256]{2,1,0:T(8,128)(2,1)S(1)}, u32[]{:S(2)}, u32[]{:S(2)}) collective-permute-start(bf16[3,64,256]{2,1,0:T(8,128)(2,1)S(1)} %fusion.4), channel_id=1, source_target_pairs={{0,4},{1,5},{2,6},{3,7},{4,0},{5,1},{6,2},{7,3},{8,12},{9,13},{10,... | collective-permute-start | bytes 294920 | tf_op jit(solution)/shard_map/ppermute | solution.py:24
  54.2 7.1 %collective-permute-start.27 = (bf16[3,64,256]{2,1,0:T(8,128)(2,1)S(1)}, bf16[3,64,256]{2,1,0:T(8,128)(2,1)S(1)}, u32[]{:S(2)}, u32[]{:S(2)}) collective-permute-start(bf16[3,64,256]{2,1,0:T(8,128)(2,1)S(1)} %fusion.9), channel_id=1, source_target_pairs={{0,24},{1,25},{2,26},{3,27},{4,28},{5,29},{6,30},{7,31},{8,16},{9,... | collective-permute-start | bytes 294920 | tf_op jit(solution)/shard_map/ppermute | solution.py:24
  56.4 5.1 %collective-permute-start.25 = (bf16[3,64,256]{2,1,0:T(8,128)(2,1)S(1)}, bf16[3,64,256]{2,1,0:T(8,128)(2,1)S(1)}, u32[]{:S(2)}, u32[]{:S(2)}) collective-permute-start(bf16[3,64,256]{2,1,0:T(8,128)(2,1)S(1)} %fusion.10), channel_id=1, source_target_pairs={{0,2},{1,3},{2,0},{3,1},{4,6},{5,7},{6,4},{7,5},{8,10},{9,11},{10,... | collective-permute-start | bytes 294920 | tf_op jit(solution)/shard_map/ppermute | solution.py:24
  56.7 5.9 %collective-permute-start.30 = (bf16[3,64,256]{2,1,0:T(8,128)(2,1)S(1)}, bf16[3,64,256]{2,1,0:T(8,128)(2,1)S(1)}, u32[]{:S(2)}, u32[]{:S(2)}) collective-permute-start(bf16[3,64,256]{2,1,0:T(8,128)(2,1)S(1)} %fusion.6), channel_id=1, source_target_pairs={{0,8},{1,9},{2,10},{3,11},{4,12},{5,13},{6,14},{7,15},{8,0},{9,1},... | collective-permute-start | bytes 294920 | tf_op jit(solution)/shard_map/ppermute | solution.py:24
  62.9 6.7 %collective-permute-start.37 = (bf16[3,64,256]{2,1,0:T(8,128)(2,1)S(1)}, bf16[3,64,256]{2,1,0:T(8,128)(2,1)S(1)}, u32[]{:S(2)}, u32[]{:S(2)}) collective-permute-start(bf16[3,64,256]{2,1,0:T(8,128)(2,1)S(1)} %get-tuple-element.88.refs_0_), channel_id=1, source_target_pairs={{0,16},{1,17},{2,18},{3,19},{4,20},{5,21},{6,22},{7,23},{8,24},{9,... | collective-permute-start | bytes 294920 | tf_op jit(solution)/shard_map/ppermute | solution.py:24
  64.3 5.7 %collective-permute-start.34 = (bf16[3,64,256]{2,1,0:T(8,128)(2,1)S(1)}, bf16[3,64,256]{2,1,0:T(8,128)(2,1)S(1)}, u32[]{:S(2)}, u32[]{:S(2)}) collective-permute-start(bf16[3,64,256]{2,1,0:T(8,128)(2,1)S(1)} %get-tuple-element.88.refs_0_), channel_id=1, source_target_pairs={{0,8},{1,9},{2,10},{3,11},{4,12},{5,13},{6,14},{7,15},{8,0},{9,1},... | collective-permute-start | bytes 294920 | tf_op jit(solution)/shard_map/ppermute | solution.py:24
  66.7 5.7 %collective-permute-start.32 = (bf16[3,64,256]{2,1,0:T(8,128)(2,1)S(1)}, bf16[3,64,256]{2,1,0:T(8,128)(2,1)S(1)}, u32[]{:S(2)}, u32[]{:S(2)}) collective-permute-start(bf16[3,64,256]{2,1,0:T(8,128)(2,1)S(1)} %get-tuple-element.88.refs_0_), channel_id=1, source_target_pairs={{0,4},{1,5},{2,6},{3,7},{4,0},{5,1},{6,2},{7,3},{8,12},{9,13},{10,... | collective-permute-start | bytes 294920 | tf_op jit(solution)/shard_map/ppermute | solution.py:24
  66.7 5.7 %collective-permute-start.31 = (bf16[3,64,256]{2,1,0:T(8,128)(2,1)S(1)}, bf16[3,64,256]{2,1,0:T(8,128)(2,1)S(1)}, u32[]{:S(2)}, u32[]{:S(2)}) collective-permute-start(bf16[3,64,256]{2,1,0:T(8,128)(2,1)S(1)} %get-tuple-element.88.refs_0_), channel_id=1, source_target_pairs={{0,2},{1,3},{2,0},{3,1},{4,6},{5,7},{6,4},{7,5},{8,10},{9,11},{10,... | collective-permute-start | bytes 294920 | tf_op jit(solution)/shard_map/ppermute | solution.py:24
  69.6 4.6 %collective-permute-start.41 = (bf16[3,64,256]{2,1,0:T(8,128)(2,1)S(1)}, bf16[3,64,256]{2,1,0:T(8,128)(2,1)S(1)}, u32[]{:S(2)}, u32[]{:S(2)}) collective-permute-start(bf16[3,64,256]{2,1,0:T(8,128)(2,1)S(1)} %collective-permute-done.37.refs_8_), channel_id=1, source_target_pairs={{0,8},{1,9},{2,10},{3,11},{4,12},{5,13},{6,14},{7,15},{8,0},{9,1},... | collective-permute-start | bytes 294920 | tf_op jit(solution)/shard_map/ppermute | solution.py:24
  69.9 5.5 %collective-permute-start.35 = (bf16[3,64,256]{2,1,0:T(8,128)(2,1)S(1)}, bf16[3,64,256]{2,1,0:T(8,128)(2,1)S(1)}, u32[]{:S(2)}, u32[]{:S(2)}) collective-permute-start(bf16[3,64,256]{2,1,0:T(8,128)(2,1)S(1)} %collective-permute-done.34.refs_4_), channel_id=1, source_target_pairs={{0,2},{1,3},{2,0},{3,1},{4,6},{5,7},{6,4},{7,5},{8,10},{9,11},{10,... | collective-permute-start | bytes 294920 | tf_op jit(solution)/shard_map/ppermute | solution.py:24
  70.5 16.2 %copy-start = (bf16[1,256,1024]{2,1,0:T(8,128)(2,1)S(1)}, bf16[1,256,1024]{2,1,0:T(8,128)(2,1)}, u32[]{:S(2)}) copy-start(bf16[1,256,1024]{2,1,0:T(8,128)(2,1)} %param.14) | copy-start | bytes 1572868
  72.4 5.5 %collective-permute-start.36 = (bf16[3,64,256]{2,1,0:T(8,128)(2,1)S(1)}, bf16[3,64,256]{2,1,0:T(8,128)(2,1)S(1)}, u32[]{:S(2)}, u32[]{:S(2)}) collective-permute-start(bf16[3,64,256]{2,1,0:T(8,128)(2,1)S(1)} %collective-permute-done.34.refs_4_), channel_id=1, source_target_pairs={{0,4},{1,5},{2,6},{3,7},{4,0},{5,1},{6,2},{7,3},{8,12},{9,13},{10,... | collective-permute-start | bytes 294920 | tf_op jit(solution)/shard_map/ppermute | solution.py:24
  73.5 5.7 %collective-permute-start.38 = (bf16[3,64,256]{2,1,0:T(8,128)(2,1)S(1)}, bf16[3,64,256]{2,1,0:T(8,128)(2,1)S(1)}, u32[]{:S(2)}, u32[]{:S(2)}) collective-permute-start(bf16[3,64,256]{2,1,0:T(8,128)(2,1)S(1)} %collective-permute-done.37.refs_8_), channel_id=1, source_target_pairs={{0,2},{1,3},{2,0},{3,1},{4,6},{5,7},{6,4},{7,5},{8,10},{9,11},{10,... | collective-permute-start | bytes 294920 | tf_op jit(solution)/shard_map/ppermute | solution.py:24
  75.4 6.6 %collective-permute-start.44 = (bf16[3,64,256]{2,1,0:T(8,128)(2,1)S(1)}, bf16[3,64,256]{2,1,0:T(8,128)(2,1)S(1)}, u32[]{:S(2)}, u32[]{:S(2)}) collective-permute-start(bf16[3,64,256]{2,1,0:T(8,128)(2,1)S(1)} %collective-permute-done.41.refs_12_), channel_id=1, source_target_pairs={{0,4},{1,5},{2,6},{3,7},{4,0},{5,1},{6,2},{7,3},{8,12},{9,13},{10,... | collective-permute-start | bytes 294920 | tf_op jit(solution)/shard_map/ppermute | solution.py:24
  75.6 4.6 %collective-permute-start.42 = (bf16[3,64,256]{2,1,0:T(8,128)(2,1)S(1)}, bf16[3,64,256]{2,1,0:T(8,128)(2,1)S(1)}, u32[]{:S(2)}, u32[]{:S(2)}) collective-permute-start(bf16[3,64,256]{2,1,0:T(8,128)(2,1)S(1)} %collective-permute-done.41.refs_12_), channel_id=1, source_target_pairs={{0,2},{1,3},{2,0},{3,1},{4,6},{5,7},{6,4},{7,5},{8,10},{9,11},{10,... | collective-permute-start | bytes 294920 | tf_op jit(solution)/shard_map/ppermute | solution.py:24
  77.1 5.3 %collective-permute-start.33 = (bf16[3,64,256]{2,1,0:T(8,128)(2,1)S(1)}, bf16[3,64,256]{2,1,0:T(8,128)(2,1)S(1)}, u32[]{:S(2)}, u32[]{:S(2)}) collective-permute-start(bf16[3,64,256]{2,1,0:T(8,128)(2,1)S(1)} %collective-permute-done.31.refs_1_), channel_id=1, source_target_pairs={{0,4},{1,5},{2,6},{3,7},{4,0},{5,1},{6,2},{7,3},{8,12},{9,13},{10,... | collective-permute-start | bytes 294920 | tf_op jit(solution)/shard_map/ppermute | solution.py:24
  77.9 5.0 %collective-permute-start.40 = (bf16[3,64,256]{2,1,0:T(8,128)(2,1)S(1)}, bf16[3,64,256]{2,1,0:T(8,128)(2,1)S(1)}, u32[]{:S(2)}, u32[]{:S(2)}) collective-permute-start(bf16[3,64,256]{2,1,0:T(8,128)(2,1)S(1)} %collective-permute-done.37.refs_8_), channel_id=1, source_target_pairs={{0,4},{1,5},{2,6},{3,7},{4,0},{5,1},{6,2},{7,3},{8,12},{9,13},{10,... | collective-permute-start | bytes 294920 | tf_op jit(solution)/shard_map/ppermute | solution.py:24
  79.2 4.6 %collective-permute-start.39 = (bf16[3,64,256]{2,1,0:T(8,128)(2,1)S(1)}, bf16[3,64,256]{2,1,0:T(8,128)(2,1)S(1)}, u32[]{:S(2)}, u32[]{:S(2)}) collective-permute-start(bf16[3,64,256]{2,1,0:T(8,128)(2,1)S(1)} %collective-permute-done.36.refs_6_), channel_id=1, source_target_pairs={{0,2},{1,3},{2,0},{3,1},{4,6},{5,7},{6,4},{7,5},{8,10},{9,11},{10,... | collective-permute-start | bytes 294920 | tf_op jit(solution)/shard_map/ppermute | solution.py:24
  80.3 6.4 %collective-permute-start.43 = (bf16[3,64,256]{2,1,0:T(8,128)(2,1)S(1)}, bf16[3,64,256]{2,1,0:T(8,128)(2,1)S(1)}, u32[]{:S(2)}, u32[]{:S(2)}) collective-permute-start(bf16[3,64,256]{2,1,0:T(8,128)(2,1)S(1)} %collective-permute-done.38.refs_9_), channel_id=1, source_target_pairs={{0,4},{1,5},{2,6},{3,7},{4,0},{5,1},{6,2},{7,3},{8,12},{9,13},{10,... | collective-permute-start | bytes 294920 | tf_op jit(solution)/shard_map/ppermute | solution.py:24
  82.1 4.6 %collective-permute-start.45 = (bf16[3,64,256]{2,1,0:T(8,128)(2,1)S(1)}, bf16[3,64,256]{2,1,0:T(8,128)(2,1)S(1)}, u32[]{:S(2)}, u32[]{:S(2)}) collective-permute-start(bf16[3,64,256]{2,1,0:T(8,128)(2,1)S(1)} %collective-permute-done.44.refs_14_), channel_id=1, source_target_pairs={{0,2},{1,3},{2,0},{3,1},{4,6},{5,7},{6,4},{7,5},{8,10},{9,11},{10,... | collective-permute-start | bytes 294920 | tf_op jit(solution)/shard_map/ppermute | solution.py:24
  87.5 1.9 %collective-permute-start.46 = (f32[3,3,32,256]{3,2,1,0:T(8,128)S(1)}, f32[3,3,32,256]{3,2,1,0:T(8,128)S(1)}, u32[]{:S(2)}, u32[]{:S(2)}) collective-permute-start(f32[3,3,32,256]{3,2,1,0:T(8,128)S(1)} %get-tuple-element.85), channel_id=1, source_target_pairs={{0,1},{1,0},{2,3},{3,2},{4,5},{5,4},{6,7},{7,6},{8,9},{9,8},{10,11... | collective-permute-start | bytes 884744 | tf_op jit(solution)/shard_map/ppermute | solution.py:24
  87.6 2.7 %collective-permute-start.47 = (bf16[256,1024]{1,0:T(8,128)(2,1)S(1)}, bf16[256,1024]{1,0:T(8,128)(2,1)S(1)}, u32[]{:S(2)}, u32[]{:S(2)}) collective-permute-start(bf16[256,1024]{1,0:T(8,128)(2,1)S(1)} %get-tuple-element.84), channel_id=1, source_target_pairs={{0,1},{1,0},{2,3},{3,2},{4,5},{5,4},{6,7},{7,6},{8,9},{9,8},{10,11... | collective-permute-start | bytes 1572872 | tf_op jit(solution)/shard_map/ppermute | solution.py:24

commit v14 on v13

--- a/solution.py
+++ b/solution.py
@@ -273,6 +273,12 @@
     local_rows = master.shape[2]
     core = lax.axis_index("dev") & CORE
 
+    def mine(state):
+        return lax.dynamic_index_in_dim(state, core, 0, keepdims=False)
+
+    def partners(state):
+        return lax.dynamic_index_in_dim(state, 1 - core, 0, keepdims=False)
+
     def both_rows(own, other):
         return jnp.where(
             core == 0, jnp.concatenate([own, other], axis=-2), jnp.concatenate([other, own], axis=-2)
@@ -280,16 +286,14 @@
 
     other_x = hop(old_rows, CORE)
     other_c = hop(old_cotangent, CORE)
-    state = jnp.stack([master, first, second], axis=1)
-    mine = lax.dynamic_index_in_dim(state, core, 0, keepdims=False)
-    theirs = hop(lax.dynamic_index_in_dim(state, 1 - core, 0, keepdims=False), CORE)
+    theirs = hop(jnp.stack([partners(master), partners(first), partners(second)]), CORE)
     other_y = hop(new_rows, CORE)
     other_live = hop(live, CORE)
     x_turned, c_turned = transposed(old_rows, other_x, old_cotangent, other_c)
     theirs, other_y, other_live, x_turned, c_turned = lax.optimization_barrier(
         (theirs, other_y, other_live, x_turned, c_turned)
     )
-    master_two = both_rows(mine[0], theirs[0])
+    master_two = both_rows(mine(master), theirs[0])
     pieces = gather_chips(master_two.astype(jnp.bfloat16))
     *grads, matches = backward(
         old_slots[None],
@@ -305,8 +309,8 @@
         c_turned,
     )
     theirs = after(theirs, grads[0])
-    first_two = both_rows(mine[1], theirs[1])
-    second_two = both_rows(mine[2], theirs[2])
+    first_two = both_rows(mine(first), theirs[1])
+    second_two = both_rows(mine(second), theirs[2])
     grad = reduce_chips(grads)
     updated = adam_update(master_two, first_two, second_two, grad)
 

time: 91.4 us -> 90.5 us (level)
  other arithmetic: 2.67 us -> 1.56 us
    squeeze x4 -> x3, local copies, waits for them, and re-layouts: 2.62 us -> 1.08 us  [the longest x1 1.06 us: mine(): return lax.dynamic_index_in_dim(state, core, 0, keepdims=False)]
    another operation x1, other arithmetic: 1.15 us -> 0.02 us  [block_a_core(): jnp.stack([partners(master), partners(first), partners(second)])]
    dynamic_slice x0 -> x1, local copies, waits for them, and re-layouts: none -> 0.96 us  [partners(): return lax.dynamic_index_in_dim(state, 1 - core, 0, keepdims=False)]
  transfers between devices with their start and end apart: 48 -> 48, of which waited for: 24 -> 24; matrix products, arithmetic and copies ran while one was open for 5% -> 4% of each run, Pallas kernels for 1% -> 1%
where the time goes in v14:
time: 90.5 us; the launch traced here: 90.3 us
  starting transfers between devices  52.1 us (58%)
  waiting for transfers between devices  26.3 us (29%)
  Pallas kernels  5.21 us (6%)
  local copies, waits for them, and re-layouts  2.93 us (3%)
  between operations  2.18 us (2%)
  other arithmetic  1.56 us (2%)
    ppermute x48, starting transfers between devices, hop(): lax.ppermute(block, 'dev', [(low, low ^ mask) for low in range(count)])  52.1 us
    ppermute x48, waiting for transfers between devices, hop(): lax.ppermute(block, 'dev', [(low, low ^ mask) for low in range(count)])  26.3 us
    pallas_call x1, Pallas kernels, backward(): pl.pallas_call(functools.partial(backward_kernel, count), out_shape=[one,...  3.18 us
  transfers between devices with their start and end apart: 48, of which 24 were waited for; matrix products, arithmetic and copies ran while one was open for 4% of the time, Pallas kernels for 1%

profile of v14, /device:TPU:0, one launch (start us, length us, event | category | flops | bytes accessed | tf_op | source)
XLA Modules:
  0.0 90.3 jit_solution(13044352585435268755)
XLA Ops:
  0.7 0.5 collective-permute-start.3
  1.2 0.4 collective-permute-start.1
  1.7 1.1 %dynamic-slice_bitcast_fusion.2 = (f32[3,32,256]{2,1,0:T(8,128)S(1)}, f32[1,3,32,256]{3,2,1,0:T(8,128)S(1)}, f32[1,3,32,256]{3,2,1,0:T(8,128)S(1)}, f32[3,32,256]{2,1,0:T(8,128)S(1)}) fusion(f32[2,3,32,256]{3,2,1,0:T(8,128)} %param.10, s32[]{:T(128)S(6)} %select_n.47, s32[]{:T(128)S(6)} %select_n.48, f32[2,3,32,256]{3,2,1,0:T(8,128)} %param.9), kind=kLoop, calls=%fused_computation.50 | loop fusion | bytes 786440 | tf_op jit(solution)/shard_map/jit(dynamic_index_in_dim)/squeeze | solution.py:277
  2.7 1.0 %constant_dynamic-slice_fusion.1 = (f32[1,3,32,256]{3,2,1,0:T(8,128)S(1)}, f32[3,32,256]{2,1,0:T(8,128)S(1)}) fusion(f32[2,3,32,256]{3,2,1,0:T(8,128)} %param.11, s32[]{:T(128)S(6)} %select_n.48, s32[]{:T(128)S(6)} %select_n.47), kind=kLoop, calls=%fused_computation.54 | loop fusion | bytes 393224 | tf_op jit(solution)/shard_map/jit(dynamic_index_in_dim)/dynamic_slice | solution.py:280
  3.9 0.4 collective-permute-start.2
  4.4 0.6 transpose_rows.1
  5.0 0.5 collective-permute-done.2
  5.5 3.8 %collective-permute-start.11 = (bf16[3,64,256]{2,1,0:T(8,128)(2,1)S(1)}, bf16[3,64,256]{2,1,0:T(8,128)(2,1)S(1)}, u32[]{:S(2)}, u32[]{:S(2)}) collective-permute-start(bf16[3,64,256]{2,1,0:T(8,128)(2,1)S(1)} %fusion.17.refs_0_), channel_id=1, source_target_pairs={{0,16},{1,17},{2,18},{3,19},{4,20},{5,21},{6,22},{7,23},{8,24},{9,... | collective-permute-start | bytes 294920 | tf_op jit(solution)/shard_map/ppermute | solution.py:24
  9.4 1.6 %collective-permute-start.8 = (bf16[3,64,256]{2,1,0:T(8,128)(2,1)S(1)}, bf16[3,64,256]{2,1,0:T(8,128)(2,1)S(1)}, u32[]{:S(2)}, u32[]{:S(2)}) collective-permute-start(bf16[3,64,256]{2,1,0:T(8,128)(2,1)S(1)} %fusion.17.refs_0_), channel_id=1, source_target_pairs={{0,8},{1,9},{2,10},{3,11},{4,12},{5,13},{6,14},{7,15},{8,0},{9,1},... | collective-permute-start | bytes 294920 | tf_op jit(solution)/shard_map/ppermute | solution.py:24
  11.0 1.5 %collective-permute-start.5 = (bf16[3,64,256]{2,1,0:T(8,128)(2,1)S(1)}, bf16[3,64,256]{2,1,0:T(8,128)(2,1)S(1)}, u32[]{:S(2)}, u32[]{:S(2)}) collective-permute-start(bf16[3,64,256]{2,1,0:T(8,128)(2,1)S(1)} %fusion.17.refs_0_), channel_id=1, source_target_pairs={{0,2},{1,3},{2,0},{3,1},{4,6},{5,7},{6,4},{7,5},{8,10},{9,11},{10,... | collective-permute-start | bytes 294920 | tf_op jit(solution)/shard_map/ppermute | solution.py:24
  12.4 1.5 %collective-permute-start.6 = (bf16[3,64,256]{2,1,0:T(8,128)(2,1)S(1)}, bf16[3,64,256]{2,1,0:T(8,128)(2,1)S(1)}, u32[]{:S(2)}, u32[]{:S(2)}) collective-permute-start(bf16[3,64,256]{2,1,0:T(8,128)(2,1)S(1)} %fusion.17.refs_0_), channel_id=1, source_target_pairs={{0,4},{1,5},{2,6},{3,7},{4,0},{5,1},{6,2},{7,3},{8,12},{9,13},{10,... | collective-permute-start | bytes 294920 | tf_op jit(solution)/shard_map/ppermute | solution.py:24
  14.0 0.9 collective-permute-done.11.refs_8_
  14.9 0.6 collective-permute-start.15
  15.5 1.5 %collective-permute-start.9 = (bf16[3,64,256]{2,1,0:T(8,128)(2,1)S(1)}, bf16[3,64,256]{2,1,0:T(8,128)(2,1)S(1)}, u32[]{:S(2)}, u32[]{:S(2)}) collective-permute-start(bf16[3,64,256]{2,1,0:T(8,128)(2,1)S(1)} %collective-permute-done.8.refs_4_), channel_id=1, source_target_pairs={{0,2},{1,3},{2,0},{3,1},{4,6},{5,7},{6,4},{7,5},{8,10},{9,11},{10,... | collective-permute-start | bytes 294920 | tf_op jit(solution)/shard_map/ppermute | solution.py:24
  17.0 1.5 %collective-permute-start.10 = (bf16[3,64,256]{2,1,0:T(8,128)(2,1)S(1)}, bf16[3,64,256]{2,1,0:T(8,128)(2,1)S(1)}, u32[]{:S(2)}, u32[]{:S(2)}) collective-permute-start(bf16[3,64,256]{2,1,0:T(8,128)(2,1)S(1)} %collective-permute-done.8.refs_4_), channel_id=1, source_target_pairs={{0,4},{1,5},{2,6},{3,7},{4,0},{5,1},{6,2},{7,3},{8,12},{9,13},{10,... | collective-permute-start | bytes 294920 | tf_op jit(solution)/shard_map/ppermute | solution.py:24
  18.5 0.5 collective-permute-start.12
  19.1 0.4 collective-permute-done.15.refs_12_
  19.5 0.6 collective-permute-done.9.refs_5_
  20.1 2.3 %collective-permute-start.16 = (bf16[3,64,256]{2,1,0:T(8,128)(2,1)S(1)}, bf16[3,64,256]{2,1,0:T(8,128)(2,1)S(1)}, u32[]{:S(2)}, u32[]{:S(2)}) collective-permute-start(bf16[3,64,256]{2,1,0:T(8,128)(2,1)S(1)} %collective-permute-done.15.refs_12_), channel_id=1, source_target_pairs={{0,2},{1,3},{2,0},{3,1},{4,6},{5,7},{6,4},{7,5},{8,10},{9,11},{10,... | collective-permute-start | bytes 294920 | tf_op jit(solution)/shard_map/ppermute | solution.py:24
  22.4 1.6 %collective-permute-start.18 = (bf16[3,64,256]{2,1,0:T(8,128)(2,1)S(1)}, bf16[3,64,256]{2,1,0:T(8,128)(2,1)S(1)}, u32[]{:S(2)}, u32[]{:S(2)}) collective-permute-start(bf16[3,64,256]{2,1,0:T(8,128)(2,1)S(1)} %collective-permute-done.15.refs_12_), channel_id=1, source_target_pairs={{0,4},{1,5},{2,6},{3,7},{4,0},{5,1},{6,2},{7,3},{8,12},{9,13},{10,... | collective-permute-start | bytes 294920 | tf_op jit(solution)/shard_map/ppermute | solution.py:24
  24.4 1.6 %collective-permute-start.14 = (bf16[3,64,256]{2,1,0:T(8,128)(2,1)S(1)}, bf16[3,64,256]{2,1,0:T(8,128)(2,1)S(1)}, u32[]{:S(2)}, u32[]{:S(2)}) collective-permute-start(bf16[3,64,256]{2,1,0:T(8,128)(2,1)S(1)} %collective-permute-done.11.refs_8_), channel_id=1, source_target_pairs={{0,4},{1,5},{2,6},{3,7},{4,0},{5,1},{6,2},{7,3},{8,12},{9,13},{10,... | collective-permute-start | bytes 294920 | tf_op jit(solution)/shard_map/ppermute | solution.py:24
  26.1 0.5 collective-permute-start.13
  26.5 0.9 collective-permute-done.18.refs_14_
  27.4 0.7 collective-permute-start.19
  28.1 1.0 %collective-permute-start.17 = (bf16[3,64,256]{2,1,0:T(8,128)(2,1)S(1)}, bf16[3,64,256]{2,1,0:T(8,128)(2,1)S(1)}, u32[]{:S(2)}, u32[]{:S(2)}) collective-permute-start(bf16[3,64,256]{2,1,0:T(8,128)(2,1)S(1)} %collective-permute-done.12.refs_9_), channel_id=1, source_target_pairs={{0,4},{1,5},{2,6},{3,7},{4,0},{5,1},{6,2},{7,3},{8,12},{9,13},{10,... | collective-permute-start | bytes 294920 | tf_op jit(solution)/shard_map/ppermute | solution.py:24
  29.8 0.6 collective-permute-done.14.refs_10_
  30.7 1.3 %collective-permute-done.19.refs_15_ = bf16[3,64,256]{2,1,0:T(8,128)(2,1)S(1)} collective-permute-done((bf16[3,64,256]{2,1,0:T(8,128)(2,1)S(1)}, bf16[3,64,256]{2,1,0:T(8,128)(2,1)S(1)}, u32[]{:S(2)}, u32[]{:S(2)}) %collective-permute-start.19) | collective-permute-done | bytes 98336 | tf_op jit(solution)/shard_map/ppermute | solution.py:24
  32.0 0.7 collective-permute-done.17.refs_11_
  32.7 3.2 %slot_gradients.1 = (bf16[3,64,256]{2,1,0:T(8,128)(2,1)S(1)}, bf16[3,64,256]{2,1,0:T(8,128)(2,1)S(1)}, bf16[2,3,64,256]{3,2,1,0:T(8,128)(2,1)S(1)}, bf16[3,64,25...) custom-call(s32[1,32]{1,0:T(1,128)S(1)} %bitcast.87, ...), custom_call_target="tpu_custom_call" | custom-call | flops 1610612736 | bytes 7340032 | tf_op jit(solution)/shard_map/slot_gradients/pallas_call | solution.py:160
  35.9 1.0 %collective-permute-start.20 = (bf16[2,3,64,256]{3,2,1,0:T(8,128)(2,1)S(1)}, bf16[2,3,64,256]{3,2,1,0:T(8,128)(2,1)S(1)}, u32[]{:S(2)}, u32[]{:S(2)}) collective-permute-start(bf16[2,3,64,256]{3,2,1,0:T(8,128)(2,1)S(1)} %get-tuple-element.62), channel_id=1, source_target_pairs={{0,4},{1,5},{2,6},{3,7},{4,0},{5,1},{6,2},{7,3},{8,12},{9,13},{10,... | collective-permute-start | bytes 589832 | tf_op jit(solution)/shard_map/ppermute | solution.py:24
  36.9 2.0 %collective-permute-start.23 = (bf16[2,3,64,256]{3,2,1,0:T(8,128)(2,1)S(1)}, bf16[2,3,64,256]{3,2,1,0:T(8,128)(2,1)S(1)}, u32[]{:S(2)}, u32[]{:S(2)}) collective-permute-start(bf16[2,3,64,256]{3,2,1,0:T(8,128)(2,1)S(1)} %get-tuple-element.65), channel_id=1, source_target_pairs={{0,2},{1,3},{2,0},{3,1},{4,6},{5,7},{6,4},{7,5},{8,10},{9,11},{10,... | collective-permute-start | bytes 589832 | tf_op jit(solution)/shard_map/ppermute | solution.py:24
  38.9 3.6 %collective-permute-done.20 = bf16[2,3,64,256]{3,2,1,0:T(8,128)(2,1)S(1)} collective-permute-done((bf16[2,3,64,256]{3,2,1,0:T(8,128)(2,1)S(1)}, bf16[2,3,64,256]{3,2,1,0:T(8,128)(2,1)S(1)}, u32[]{:S(2)}, u32[]{:S(2)}) %collective-permute-start.20) | collective-permute-done | bytes 196640 | tf_op jit(solution)/shard_map/ppermute | solution.py:24
  42.5 1.5 %collective-permute-start.21 = (bf16[3,64,256]{2,1,0:T(8,128)(2,1)S(1)}, bf16[3,64,256]{2,1,0:T(8,128)(2,1)S(1)}, u32[]{:S(2)}, u32[]{:S(2)}) collective-permute-start(bf16[3,64,256]{2,1,0:T(8,128)(2,1)S(1)} %fusion.14), channel_id=1, source_target_pairs={{0,2},{1,3},{2,0},{3,1},{4,6},{5,7},{6,4},{7,5},{8,10},{9,11},{10,... | collective-permute-start | bytes 294920 | tf_op jit(solution)/shard_map/ppermute | solution.py:24
  44.1 2.5 %collective-permute-start.26 = (bf16[3,64,256]{2,1,0:T(8,128)(2,1)S(1)}, bf16[3,64,256]{2,1,0:T(8,128)(2,1)S(1)}, u32[]{:S(2)}, u32[]{:S(2)}) collective-permute-start(bf16[3,64,256]{2,1,0:T(8,128)(2,1)S(1)} %fusion.7), channel_id=1, source_target_pairs={{0,4},{1,5},{2,6},{3,7},{4,0},{5,1},{6,2},{7,3},{8,12},{9,13},{10,... | collective-permute-start | bytes 294920 | tf_op jit(solution)/shard_map/ppermute | solution.py:24
  46.7 0.5 collective-permute-done.21
  47.3 3.5 %collective-permute-start.22 = (bf16[3,64,256]{2,1,0:T(8,128)(2,1)S(1)}, bf16[3,64,256]{2,1,0:T(8,128)(2,1)S(1)}, u32[]{:S(2)}, u32[]{:S(2)}) collective-permute-start(bf16[3,64,256]{2,1,0:T(8,128)(2,1)S(1)} %fusion.16), channel_id=1, source_target_pairs={{0,16},{1,17},{2,18},{3,19},{4,20},{5,21},{6,22},{7,23},{8,24},{9,... | collective-permute-start | bytes 294920 | tf_op jit(solution)/shard_map/ppermute | solution.py:24
  50.8 2.5 %collective-permute-start.29 = (bf16[3,64,256]{2,1,0:T(8,128)(2,1)S(1)}, bf16[3,64,256]{2,1,0:T(8,128)(2,1)S(1)}, u32[]{:S(2)}, u32[]{:S(2)}) collective-permute-start(bf16[3,64,256]{2,1,0:T(8,128)(2,1)S(1)} %fusion.4), channel_id=1, source_target_pairs={{0,4},{1,5},{2,6},{3,7},{4,0},{5,1},{6,2},{7,3},{8,12},{9,13},{10,... | collective-permute-start | bytes 294920 | tf_op jit(solution)/shard_map/ppermute | solution.py:24
  53.3 2.2 %collective-permute-start.27 = (bf16[3,64,256]{2,1,0:T(8,128)(2,1)S(1)}, bf16[3,64,256]{2,1,0:T(8,128)(2,1)S(1)}, u32[]{:S(2)}, u32[]{:S(2)}) collective-permute-start(bf16[3,64,256]{2,1,0:T(8,128)(2,1)S(1)} %fusion.9), channel_id=1, source_target_pairs={{0,24},{1,25},{2,26},{3,27},{4,28},{5,29},{6,30},{7,31},{8,16},{9,... | collective-permute-start | bytes 294920 | tf_op jit(solution)/shard_map/ppermute | solution.py:24
  55.8 0.6 collective-permute-start.30
  56.5 3.9 %collective-permute-done.27 = bf16[3,64,256]{2,1,0:T(8,128)(2,1)S(1)} collective-permute-done((bf16[3,64,256]{2,1,0:T(8,128)(2,1)S(1)}, bf16[3,64,256]{2,1,0:T(8,128)(2,1)S(1)}, u32[]{:S(2)}, u32[]{:S(2)}) %collective-permute-start.27) | collective-permute-done | bytes 98336 | tf_op jit(solution)/shard_map/ppermute | solution.py:24
  60.7 1.0 %collective-permute-done.30 = bf16[3,64,256]{2,1,0:T(8,128)(2,1)S(1)} collective-permute-done((bf16[3,64,256]{2,1,0:T(8,128)(2,1)S(1)}, bf16[3,64,256]{2,1,0:T(8,128)(2,1)S(1)}, u32[]{:S(2)}, u32[]{:S(2)}) %collective-permute-start.30) | collective-permute-done | bytes 98336 | tf_op jit(solution)/shard_map/ppermute | solution.py:24
  62.0 1.4 %collective-permute-start.37 = (bf16[3,64,256]{2,1,0:T(8,128)(2,1)S(1)}, bf16[3,64,256]{2,1,0:T(8,128)(2,1)S(1)}, u32[]{:S(2)}, u32[]{:S(2)}) collective-permute-start(bf16[3,64,256]{2,1,0:T(8,128)(2,1)S(1)} %get-tuple-element.88.refs_0_), channel_id=1, source_target_pairs={{0,16},{1,17},{2,18},{3,19},{4,20},{5,21},{6,22},{7,23},{8,24},{9,... | collective-permute-start | bytes 294920 | tf_op jit(solution)/shard_map/ppermute | solution.py:24
  63.4 2.5 %collective-permute-start.34 = (bf16[3,64,256]{2,1,0:T(8,128)(2,1)S(1)}, bf16[3,64,256]{2,1,0:T(8,128)(2,1)S(1)}, u32[]{:S(2)}, u32[]{:S(2)}) collective-permute-start(bf16[3,64,256]{2,1,0:T(8,128)(2,1)S(1)} %get-tuple-element.88.refs_0_), channel_id=1, source_target_pairs={{0,8},{1,9},{2,10},{3,11},{4,12},{5,13},{6,14},{7,15},{8,0},{9,1},... | collective-permute-start | bytes 294920 | tf_op jit(solution)/shard_map/ppermute | solution.py:24
  65.9 1.1 %collective-permute-start.31 = (bf16[3,64,256]{2,1,0:T(8,128)(2,1)S(1)}, bf16[3,64,256]{2,1,0:T(8,128)(2,1)S(1)}, u32[]{:S(2)}, u32[]{:S(2)}) collective-permute-start(bf16[3,64,256]{2,1,0:T(8,128)(2,1)S(1)} %get-tuple-element.88.refs_0_), channel_id=1, source_target_pairs={{0,2},{1,3},{2,0},{3,1},{4,6},{5,7},{6,4},{7,5},{8,10},{9,11},{10,... | collective-permute-start | bytes 294920 | tf_op jit(solution)/shard_map/ppermute | solution.py:24
  66.9 1.8 %collective-permute-done.37.refs_8_ = bf16[3,64,256]{2,1,0:T(8,128)(2,1)S(1)} collective-permute-done((bf16[3,64,256]{2,1,0:T(8,128)(2,1)S(1)}, bf16[3,64,256]{2,1,0:T(8,128)(2,1)S(1)}, u32[]{:S(2)}, u32[]{:S(2)}) %collective-permute-start.37) | collective-permute-done | bytes 98336 | tf_op jit(solution)/shard_map/ppermute | solution.py:24
  69.1 0.5 collective-permute-start.35
  69.7 1.8 %collective-permute-done.32.refs_2_ = bf16[3,64,256]{2,1,0:T(8,128)(2,1)S(1)} collective-permute-done((bf16[3,64,256]{2,1,0:T(8,128)(2,1)S(1)}, bf16[3,64,256]{2,1,0:T(8,128)(2,1)S(1)}, u32[]{:S(2)}, u32[]{:S(2)}) %collective-permute-start.32) | collective-permute-done | bytes 98336 | tf_op jit(solution)/shard_map/ppermute | solution.py:24
  71.5 1.1 %collective-permute-start.36 = (bf16[3,64,256]{2,1,0:T(8,128)(2,1)S(1)}, bf16[3,64,256]{2,1,0:T(8,128)(2,1)S(1)}, u32[]{:S(2)}, u32[]{:S(2)}) collective-permute-start(bf16[3,64,256]{2,1,0:T(8,128)(2,1)S(1)} %collective-permute-done.34.refs_4_), channel_id=1, source_target_pairs={{0,4},{1,5},{2,6},{3,7},{4,0},{5,1},{6,2},{7,3},{8,12},{9,13},{10,... | collective-permute-start | bytes 294920 | tf_op jit(solution)/shard_map/ppermute | solution.py:24
  72.7 0.6 collective-permute-done.41.refs_12_
  73.4 1.2 %collective-permute-done.35.refs_5_ = bf16[3,64,256]{2,1,0:T(8,128)(2,1)S(1)} collective-permute-done((bf16[3,64,256]{2,1,0:T(8,128)(2,1)S(1)}, bf16[3,64,256]{2,1,0:T(8,128)(2,1)S(1)}, u32[]{:S(2)}, u32[]{:S(2)}) %collective-permute-start.35) | collective-permute-done | bytes 98336 | tf_op jit(solution)/shard_map/ppermute | solution.py:24
  74.7 1.5 %collective-permute-start.42 = (bf16[3,64,256]{2,1,0:T(8,128)(2,1)S(1)}, bf16[3,64,256]{2,1,0:T(8,128)(2,1)S(1)}, u32[]{:S(2)}, u32[]{:S(2)}) collective-permute-start(bf16[3,64,256]{2,1,0:T(8,128)(2,1)S(1)} %collective-permute-done.41.refs_12_), channel_id=1, source_target_pairs={{0,2},{1,3},{2,0},{3,1},{4,6},{5,7},{6,4},{7,5},{8,10},{9,11},{10,... | collective-permute-start | bytes 294920 | tf_op jit(solution)/shard_map/ppermute | solution.py:24
  76.3 0.7 collective-permute-start.33
  77.0 1.4 %collective-permute-start.40 = (bf16[3,64,256]{2,1,0:T(8,128)(2,1)S(1)}, bf16[3,64,256]{2,1,0:T(8,128)(2,1)S(1)}, u32[]{:S(2)}, u32[]{:S(2)}) collective-permute-start(bf16[3,64,256]{2,1,0:T(8,128)(2,1)S(1)} %collective-permute-done.37.refs_8_), channel_id=1, source_target_pairs={{0,4},{1,5},{2,6},{3,7},{4,0},{5,1},{6,2},{7,3},{8,12},{9,13},{10,... | collective-permute-start | bytes 294920 | tf_op jit(solution)/shard_map/ppermute | solution.py:24
  78.4 0.5 collective-permute-start.39
  78.9 0.4 collective-permute-done.42.refs_13_
  79.3 1.9 %collective-permute-start.43 = (bf16[3,64,256]{2,1,0:T(8,128)(2,1)S(1)}, bf16[3,64,256]{2,1,0:T(8,128)(2,1)S(1)}, u32[]{:S(2)}, u32[]{:S(2)}) collective-permute-start(bf16[3,64,256]{2,1,0:T(8,128)(2,1)S(1)} %collective-permute-done.38.refs_9_), channel_id=1, source_target_pairs={{0,4},{1,5},{2,6},{3,7},{4,0},{5,1},{6,2},{7,3},{8,12},{9,13},{10,... | collective-permute-start | bytes 294920 | tf_op jit(solution)/shard_map/ppermute | solution.py:24
  81.6 0.4 collective-permute-done.40.refs_10_
  82.0 1.0 %collective-permute-done.39.refs_7_ = bf16[3,64,256]{2,1,0:T(8,128)(2,1)S(1)} collective-permute-done((bf16[3,64,256]{2,1,0:T(8,128)(2,1)S(1)}, bf16[3,64,256]{2,1,0:T(8,128)(2,1)S(1)}, u32[]{:S(2)}, u32[]{:S(2)}) %collective-permute-start.39) | collective-permute-done | bytes 98336 | tf_op jit(solution)/shard_map/ppermute | solution.py:24
  83.0 2.9 %collective-permute-done.45.refs_15_ = bf16[3,64,256]{2,1,0:T(8,128)(2,1)S(1)} collective-permute-done((bf16[3,64,256]{2,1,0:T(8,128)(2,1)S(1)}, bf16[3,64,256]{2,1,0:T(8,128)(2,1)S(1)}, u32[]{:S(2)}, u32[]{:S(2)}) %collective-permute-start.45) | collective-permute-done | bytes 98336 | tf_op jit(solution)/shard_map/ppermute | solution.py:24
  85.9 0.8 other_outputs.1
  86.7 0.5 collective-permute-start.47
  87.9 0.7 own_outputs.1
  88.6 0.8 slice_bitcast_fusion
  89.4 0.8 select_bitcast_fusion
  (66 shorter events, 3.3 us)
Async XLA Ops:
  0.6 3.7 %copy-start.1 = (bf16[1,256,1024]{2,1,0:T(8,128)(2,1)S(1)}, bf16[1,256,1024]{2,1,0:T(8,128)(2,1)}, u32[]{:S(2)}) copy-start(bf16[1,256,1024]{2,1,0:T(8,128)(2,1)} %param.12) | copy-start | bytes 1572868
  0.6 3.7 %copy-start.2 = (bf16[1,256,1024]{2,1,0:T(8,128)(2,1)S(1)}, bf16[1,256,1024]{2,1,0:T(8,128)(2,1)}, u32[]{:S(2)}) copy-start(bf16[1,256,1024]{2,1,0:T(8,128)(2,1)} %param.13) | copy-start | bytes 1572868
  0.7 3.7 %collective-permute-start.3 = (bf16[256,1024]{1,0:T(8,128)(2,1)}, bf16[256,1024]{1,0:T(8,128)(2,1)S(1)}, u32[]{:S(2)}, u32[]{:S(2)}) collective-permute-start(bf16[256,1024]{1,0:T(8,128)(2,1)} %bitcast.81), channel_id=1, source_target_pairs={{0,1},{1,0},{2,3},{3,2},{4,5},{5,4},{6,7},{7,6},{8,9},{9,8},{10,11... | collective-permute-start | bytes 1572872 | tf_op jit(solution)/shard_map/ppermute | solution.py:24
  1.2 3.2 %collective-permute-start.4 = (bf16[256,1024]{1,0:T(8,128)(2,1)}, bf16[256,1024]{1,0:T(8,128)(2,1)S(1)}, u32[]{:S(2)}, u32[]{:S(2)}) collective-permute-start(bf16[256,1024]{1,0:T(8,128)(2,1)} %bitcast.84), channel_id=1, source_target_pairs={{0,1},{1,0},{2,3},{3,2},{4,5},{5,4},{6,7},{7,6},{8,9},{9,8},{10,11... | collective-permute-start | bytes 1572872 | tf_op jit(solution)/shard_map/ppermute | solution.py:24
  1.2 4.2 %collective-permute-start.1 = (bf16[256,1024]{1,0:T(8,128)(2,1)}, bf16[256,1024]{1,0:T(8,128)(2,1)S(1)}, u32[]{:S(2)}, u32[]{:S(2)}) collective-permute-start(bf16[256,1024]{1,0:T(8,128)(2,1)} %bitcast.78), channel_id=1, source_target_pairs={{0,1},{1,0},{2,3},{3,2},{4,5},{5,4},{6,7},{7,6},{8,9},{9,8},{10,11... | collective-permute-start | bytes 1572872 | tf_op jit(solution)/shard_map/ppermute | solution.py:24
  3.7 29.0 %copy-start.3 = (s32[32]{0:T(128)S(1)}, s32[32]{0:T(128)}, u32[]{:S(2)}) copy-start(s32[32]{0:T(128)} %param.15) | copy-start | bytes 388
  3.7 29.0 %copy-start.4 = (s32[32]{0:T(128)S(1)}, s32[32]{0:T(128)}, u32[]{:S(2)}) copy-start(s32[32]{0:T(128)} %param.16) | copy-start | bytes 388
  3.8 1.7 %collective-permute-start = (f32[3,3,32,256]{3,2,1,0:T(8,128)S(1)}, f32[3,3,32,256]{3,2,1,0:T(8,128)S(1)}, u32[]{:S(2)}, u32[]{:S(2)}) collective-permute-start(f32[3,3,32,256]{3,2,1,0:T(8,128)S(1)} %pad_maximum_fusion.1), channel_id=1, source_target_pairs={{0,1},{1,0},{2,3},{3,2},{4,5},{5,4},{6,7},{7,6},{8,9},{9,8},{10,11... | collective-permute-start | bytes 884744 | tf_op jit(solution)/shard_map/ppermute | solution.py:24
  3.9 1.6 %collective-permute-start.2 = (s32[1]{0:T(128)}, s32[1]{0:T(128)}, u32[]{:S(2)}, u32[]{:S(2)}) collective-permute-start(s32[1]{0:T(128)} %param.17), channel_id=1, source_target_pairs={{0,1},{1,0},{2,3},{3,2},{4,5},{5,4},{6,7},{7,6},{8,9},{9,8},{10,11... | collective-permute-start | bytes 20 | tf_op jit(solution)/shard_map/ppermute | solution.py:24
  5.5 9.3 %collective-permute-start.11 = (bf16[3,64,256]{2,1,0:T(8,128)(2,1)S(1)}, bf16[3,64,256]{2,1,0:T(8,128)(2,1)S(1)}, u32[]{:S(2)}, u32[]{:S(2)}) collective-permute-start(bf16[3,64,256]{2,1,0:T(8,128)(2,1)S(1)} %fusion.17.refs_0_), channel_id=1, source_target_pairs={{0,16},{1,17},{2,18},{3,19},{4,20},{5,21},{6,22},{7,23},{8,24},{9,... | collective-permute-start | bytes 294920 | tf_op jit(solution)/shard_map/ppermute | solution.py:24
  9.4 6.1 %collective-permute-start.8 = (bf16[3,64,256]{2,1,0:T(8,128)(2,1)S(1)}, bf16[3,64,256]{2,1,0:T(8,128)(2,1)S(1)}, u32[]{:S(2)}, u32[]{:S(2)}) collective-permute-start(bf16[3,64,256]{2,1,0:T(8,128)(2,1)S(1)} %fusion.17.refs_0_), channel_id=1, source_target_pairs={{0,8},{1,9},{2,10},{3,11},{4,12},{5,13},{6,14},{7,15},{8,0},{9,1},... | collective-permute-start | bytes 294920 | tf_op jit(solution)/shard_map/ppermute | solution.py:24
  11.0 6.0 %collective-permute-start.5 = (bf16[3,64,256]{2,1,0:T(8,128)(2,1)S(1)}, bf16[3,64,256]{2,1,0:T(8,128)(2,1)S(1)}, u32[]{:S(2)}, u32[]{:S(2)}) collective-permute-start(bf16[3,64,256]{2,1,0:T(8,128)(2,1)S(1)} %fusion.17.refs_0_), channel_id=1, source_target_pairs={{0,2},{1,3},{2,0},{3,1},{4,6},{5,7},{6,4},{7,5},{8,10},{9,11},{10,... | collective-permute-start | bytes 294920 | tf_op jit(solution)/shard_map/ppermute | solution.py:24
  12.4 6.1 %collective-permute-start.6 = (bf16[3,64,256]{2,1,0:T(8,128)(2,1)S(1)}, bf16[3,64,256]{2,1,0:T(8,128)(2,1)S(1)}, u32[]{:S(2)}, u32[]{:S(2)}) collective-permute-start(bf16[3,64,256]{2,1,0:T(8,128)(2,1)S(1)} %fusion.17.refs_0_), channel_id=1, source_target_pairs={{0,4},{1,5},{2,6},{3,7},{4,0},{5,1},{6,2},{7,3},{8,12},{9,13},{10,... | collective-permute-start | bytes 294920 | tf_op jit(solution)/shard_map/ppermute | solution.py:24
  14.9 4.6 %collective-permute-start.15 = (bf16[3,64,256]{2,1,0:T(8,128)(2,1)S(1)}, bf16[3,64,256]{2,1,0:T(8,128)(2,1)S(1)}, u32[]{:S(2)}, u32[]{:S(2)}) collective-permute-start(bf16[3,64,256]{2,1,0:T(8,128)(2,1)S(1)} %collective-permute-done.11.refs_8_), channel_id=1, source_target_pairs={{0,8},{1,9},{2,10},{3,11},{4,12},{5,13},{6,14},{7,15},{8,0},{9,1},... | collective-permute-start | bytes 294920 | tf_op jit(solution)/shard_map/ppermute | solution.py:24
  15.5 4.6 %collective-permute-start.9 = (bf16[3,64,256]{2,1,0:T(8,128)(2,1)S(1)}, bf16[3,64,256]{2,1,0:T(8,128)(2,1)S(1)}, u32[]{:S(2)}, u32[]{:S(2)}) collective-permute-start(bf16[3,64,256]{2,1,0:T(8,128)(2,1)S(1)} %collective-permute-done.8.refs_4_), channel_id=1, source_target_pairs={{0,2},{1,3},{2,0},{3,1},{4,6},{5,7},{6,4},{7,5},{8,10},{9,11},{10,... | collective-permute-start | bytes 294920 | tf_op jit(solution)/shard_map/ppermute | solution.py:24
  17.0 7.4 %collective-permute-start.10 = (bf16[3,64,256]{2,1,0:T(8,128)(2,1)S(1)}, bf16[3,64,256]{2,1,0:T(8,128)(2,1)S(1)}, u32[]{:S(2)}, u32[]{:S(2)}) collective-permute-start(bf16[3,64,256]{2,1,0:T(8,128)(2,1)S(1)} %collective-permute-done.8.refs_4_), channel_id=1, source_target_pairs={{0,4},{1,5},{2,6},{3,7},{4,0},{5,1},{6,2},{7,3},{8,12},{9,13},{10,... | collective-permute-start | bytes 294920 | tf_op jit(solution)/shard_map/ppermute | solution.py:24
  18.5 7.5 %collective-permute-start.12 = (bf16[3,64,256]{2,1,0:T(8,128)(2,1)S(1)}, bf16[3,64,256]{2,1,0:T(8,128)(2,1)S(1)}, u32[]{:S(2)}, u32[]{:S(2)}) collective-permute-start(bf16[3,64,256]{2,1,0:T(8,128)(2,1)S(1)} %collective-permute-done.11.refs_8_), channel_id=1, source_target_pairs={{0,2},{1,3},{2,0},{3,1},{4,6},{5,7},{6,4},{7,5},{8,10},{9,11},{10,... | collective-permute-start | bytes 294920 | tf_op jit(solution)/shard_map/ppermute | solution.py:24
  20.1 6.4 %collective-permute-start.16 = (bf16[3,64,256]{2,1,0:T(8,128)(2,1)S(1)}, bf16[3,64,256]{2,1,0:T(8,128)(2,1)S(1)}, u32[]{:S(2)}, u32[]{:S(2)}) collective-permute-start(bf16[3,64,256]{2,1,0:T(8,128)(2,1)S(1)} %collective-permute-done.15.refs_12_), channel_id=1, source_target_pairs={{0,2},{1,3},{2,0},{3,1},{4,6},{5,7},{6,4},{7,5},{8,10},{9,11},{10,... | collective-permute-start | bytes 294920 | tf_op jit(solution)/shard_map/ppermute | solution.py:24
  22.4 5.0 %collective-permute-start.18 = (bf16[3,64,256]{2,1,0:T(8,128)(2,1)S(1)}, bf16[3,64,256]{2,1,0:T(8,128)(2,1)S(1)}, u32[]{:S(2)}, u32[]{:S(2)}) collective-permute-start(bf16[3,64,256]{2,1,0:T(8,128)(2,1)S(1)} %collective-permute-done.15.refs_12_), channel_id=1, source_target_pairs={{0,4},{1,5},{2,6},{3,7},{4,0},{5,1},{6,2},{7,3},{8,12},{9,13},{10,... | collective-permute-start | bytes 294920 | tf_op jit(solution)/shard_map/ppermute | solution.py:24
  24.0 5.7 %collective-permute-start.7 = (bf16[3,64,256]{2,1,0:T(8,128)(2,1)S(1)}, bf16[3,64,256]{2,1,0:T(8,128)(2,1)S(1)}, u32[]{:S(2)}, u32[]{:S(2)}) collective-permute-start(bf16[3,64,256]{2,1,0:T(8,128)(2,1)S(1)} %collective-permute-done.5.refs_1_), channel_id=1, source_target_pairs={{0,4},{1,5},{2,6},{3,7},{4,0},{5,1},{6,2},{7,3},{8,12},{9,13},{10,... | collective-permute-start | bytes 294920 | tf_op jit(solution)/shard_map/ppermute | solution.py:24
  24.4 6.0 %collective-permute-start.14 = (bf16[3,64,256]{2,1,0:T(8,128)(2,1)S(1)}, bf16[3,64,256]{2,1,0:T(8,128)(2,1)S(1)}, u32[]{:S(2)}, u32[]{:S(2)}) collective-permute-start(bf16[3,64,256]{2,1,0:T(8,128)(2,1)S(1)} %collective-permute-done.11.refs_8_), channel_id=1, source_target_pairs={{0,4},{1,5},{2,6},{3,7},{4,0},{5,1},{6,2},{7,3},{8,12},{9,13},{10,... | collective-permute-start | bytes 294920 | tf_op jit(solution)/shard_map/ppermute | solution.py:24
  26.1 4.6 %collective-permute-start.13 = (bf16[3,64,256]{2,1,0:T(8,128)(2,1)S(1)}, bf16[3,64,256]{2,1,0:T(8,128)(2,1)S(1)}, u32[]{:S(2)}, u32[]{:S(2)}) collective-permute-start(bf16[3,64,256]{2,1,0:T(8,128)(2,1)S(1)} %collective-permute-done.10.refs_6_), channel_id=1, source_target_pairs={{0,2},{1,3},{2,0},{3,1},{4,6},{5,7},{6,4},{7,5},{8,10},{9,11},{10,... | collective-permute-start | bytes 294920 | tf_op jit(solution)/shard_map/ppermute | solution.py:24
  27.4 4.6 %collective-permute-start.19 = (bf16[3,64,256]{2,1,0:T(8,128)(2,1)S(1)}, bf16[3,64,256]{2,1,0:T(8,128)(2,1)S(1)}, u32[]{:S(2)}, u32[]{:S(2)}) collective-permute-start(bf16[3,64,256]{2,1,0:T(8,128)(2,1)S(1)} %collective-permute-done.18.refs_14_), channel_id=1, source_target_pairs={{0,2},{1,3},{2,0},{3,1},{4,6},{5,7},{6,4},{7,5},{8,10},{9,11},{10,... | collective-permute-start | bytes 294920 | tf_op jit(solution)/shard_map/ppermute | solution.py:24
  28.1 4.6 %collective-permute-start.17 = (bf16[3,64,256]{2,1,0:T(8,128)(2,1)S(1)}, bf16[3,64,256]{2,1,0:T(8,128)(2,1)S(1)}, u32[]{:S(2)}, u32[]{:S(2)}) collective-permute-start(bf16[3,64,256]{2,1,0:T(8,128)(2,1)S(1)} %collective-permute-done.12.refs_9_), channel_id=1, source_target_pairs={{0,4},{1,5},{2,6},{3,7},{4,0},{5,1},{6,2},{7,3},{8,12},{9,13},{10,... | collective-permute-start | bytes 294920 | tf_op jit(solution)/shard_map/ppermute | solution.py:24
  35.9 6.6 %collective-permute-start.20 = (bf16[2,3,64,256]{3,2,1,0:T(8,128)(2,1)S(1)}, bf16[2,3,64,256]{3,2,1,0:T(8,128)(2,1)S(1)}, u32[]{:S(2)}, u32[]{:S(2)}) collective-permute-start(bf16[2,3,64,256]{3,2,1,0:T(8,128)(2,1)S(1)} %get-tuple-element.62), channel_id=1, source_target_pairs={{0,4},{1,5},{2,6},{3,7},{4,0},{5,1},{6,2},{7,3},{8,12},{9,13},{10,... | collective-permute-start | bytes 589832 | tf_op jit(solution)/shard_map/ppermute | solution.py:24
  36.9 7.1 %collective-permute-start.23 = (bf16[2,3,64,256]{3,2,1,0:T(8,128)(2,1)S(1)}, bf16[2,3,64,256]{3,2,1,0:T(8,128)(2,1)S(1)}, u32[]{:S(2)}, u32[]{:S(2)}) collective-permute-start(bf16[2,3,64,256]{3,2,1,0:T(8,128)(2,1)S(1)} %get-tuple-element.65), channel_id=1, source_target_pairs={{0,2},{1,3},{2,0},{3,1},{4,6},{5,7},{6,4},{7,5},{8,10},{9,11},{10,... | collective-permute-start | bytes 589832 | tf_op jit(solution)/shard_map/ppermute | solution.py:24
  38.9 7.8 %collective-permute-start.28 = (bf16[2,3,64,256]{3,2,1,0:T(8,128)(2,1)S(1)}, bf16[2,3,64,256]{3,2,1,0:T(8,128)(2,1)S(1)}, u32[]{:S(2)}, u32[]{:S(2)}) collective-permute-start(bf16[2,3,64,256]{3,2,1,0:T(8,128)(2,1)S(1)} %get-tuple-element.73), channel_id=1, source_target_pairs={{0,2},{1,3},{2,0},{3,1},{4,6},{5,7},{6,4},{7,5},{8,10},{9,11},{10,... | collective-permute-start | bytes 589832 | tf_op jit(solution)/shard_map/ppermute | solution.py:24
  42.5 4.7 %collective-permute-start.21 = (bf16[3,64,256]{2,1,0:T(8,128)(2,1)S(1)}, bf16[3,64,256]{2,1,0:T(8,128)(2,1)S(1)}, u32[]{:S(2)}, u32[]{:S(2)}) collective-permute-start(bf16[3,64,256]{2,1,0:T(8,128)(2,1)S(1)} %fusion.14), channel_id=1, source_target_pairs={{0,2},{1,3},{2,0},{3,1},{4,6},{5,7},{6,4},{7,5},{8,10},{9,11},{10,... | collective-permute-start | bytes 294920 | tf_op jit(solution)/shard_map/ppermute | solution.py:24
  44.1 9.1 %collective-permute-start.26 = (bf16[3,64,256]{2,1,0:T(8,128)(2,1)S(1)}, bf16[3,64,256]{2,1,0:T(8,128)(2,1)S(1)}, u32[]{:S(2)}, u32[]{:S(2)}) collective-permute-start(bf16[3,64,256]{2,1,0:T(8,128)(2,1)S(1)} %fusion.7), channel_id=1, source_target_pairs={{0,4},{1,5},{2,6},{3,7},{4,0},{5,1},{6,2},{7,3},{8,12},{9,13},{10,... | collective-permute-start | bytes 294920 | tf_op jit(solution)/shard_map/ppermute | solution.py:24
  46.6 6.6 %collective-permute-start.24 = (bf16[2,3,64,256]{3,2,1,0:T(8,128)(2,1)S(1)}, bf16[2,3,64,256]{3,2,1,0:T(8,128)(2,1)S(1)}, u32[]{:S(2)}, u32[]{:S(2)}) collective-permute-start(bf16[2,3,64,256]{3,2,1,0:T(8,128)(2,1)S(1)} %get-tuple-element.66), channel_id=1, source_target_pairs={{0,4},{1,5},{2,6},{3,7},{4,0},{5,1},{6,2},{7,3},{8,12},{9,13},{10,... | collective-permute-start | bytes 589832 | tf_op jit(solution)/shard_map/ppermute | solution.py:24
  47.3 9.2 %collective-permute-start.22 = (bf16[3,64,256]{2,1,0:T(8,128)(2,1)S(1)}, bf16[3,64,256]{2,1,0:T(8,128)(2,1)S(1)}, u32[]{:S(2)}, u32[]{:S(2)}) collective-permute-start(bf16[3,64,256]{2,1,0:T(8,128)(2,1)S(1)} %fusion.16), channel_id=1, source_target_pairs={{0,16},{1,17},{2,18},{3,19},{4,20},{5,21},{6,22},{7,23},{8,24},{9,... | collective-permute-start | bytes 294920 | tf_op jit(solution)/shard_map/ppermute | solution.py:24
  50.8 5.0 %collective-permute-start.29 = (bf16[3,64,256]{2,1,0:T(8,128)(2,1)S(1)}, bf16[3,64,256]{2,1,0:T(8,128)(2,1)S(1)}, u32[]{:S(2)}, u32[]{:S(2)}) collective-permute-start(bf16[3,64,256]{2,1,0:T(8,128)(2,1)S(1)} %fusion.4), channel_id=1, source_target_pairs={{0,4},{1,5},{2,6},{3,7},{4,0},{5,1},{6,2},{7,3},{8,12},{9,13},{10,... | collective-permute-start | bytes 294920 | tf_op jit(solution)/shard_map/ppermute | solution.py:24
  53.3 7.1 %collective-permute-start.27 = (bf16[3,64,256]{2,1,0:T(8,128)(2,1)S(1)}, bf16[3,64,256]{2,1,0:T(8,128)(2,1)S(1)}, u32[]{:S(2)}, u32[]{:S(2)}) collective-permute-start(bf16[3,64,256]{2,1,0:T(8,128)(2,1)S(1)} %fusion.9), channel_id=1, source_target_pairs={{0,24},{1,25},{2,26},{3,27},{4,28},{5,29},{6,30},{7,31},{8,16},{9,... | collective-permute-start | bytes 294920 | tf_op jit(solution)/shard_map/ppermute | solution.py:24
  55.5 5.2 %collective-permute-start.25 = (bf16[3,64,256]{2,1,0:T(8,128)(2,1)S(1)}, bf16[3,64,256]{2,1,0:T(8,128)(2,1)S(1)}, u32[]{:S(2)}, u32[]{:S(2)}) collective-permute-start(bf16[3,64,256]{2,1,0:T(8,128)(2,1)S(1)} %fusion.10), channel_id=1, source_target_pairs={{0,2},{1,3},{2,0},{3,1},{4,6},{5,7},{6,4},{7,5},{8,10},{9,11},{10,... | collective-permute-start | bytes 294920 | tf_op jit(solution)/shard_map/ppermute | solution.py:24
  55.8 5.9 %collective-permute-start.30 = (bf16[3,64,256]{2,1,0:T(8,128)(2,1)S(1)}, bf16[3,64,256]{2,1,0:T(8,128)(2,1)S(1)}, u32[]{:S(2)}, u32[]{:S(2)}) collective-permute-start(bf16[3,64,256]{2,1,0:T(8,128)(2,1)S(1)} %fusion.6), channel_id=1, source_target_pairs={{0,8},{1,9},{2,10},{3,11},{4,12},{5,13},{6,14},{7,15},{8,0},{9,1},... | collective-permute-start | bytes 294920 | tf_op jit(solution)/shard_map/ppermute | solution.py:24
  62.0 6.7 %collective-permute-start.37 = (bf16[3,64,256]{2,1,0:T(8,128)(2,1)S(1)}, bf16[3,64,256]{2,1,0:T(8,128)(2,1)S(1)}, u32[]{:S(2)}, u32[]{:S(2)}) collective-permute-start(bf16[3,64,256]{2,1,0:T(8,128)(2,1)S(1)} %get-tuple-element.88.refs_0_), channel_id=1, source_target_pairs={{0,16},{1,17},{2,18},{3,19},{4,20},{5,21},{6,22},{7,23},{8,24},{9,... | collective-permute-start | bytes 294920 | tf_op jit(solution)/shard_map/ppermute | solution.py:24
  63.4 5.7 %collective-permute-start.34 = (bf16[3,64,256]{2,1,0:T(8,128)(2,1)S(1)}, bf16[3,64,256]{2,1,0:T(8,128)(2,1)S(1)}, u32[]{:S(2)}, u32[]{:S(2)}) collective-permute-start(bf16[3,64,256]{2,1,0:T(8,128)(2,1)S(1)} %get-tuple-element.88.refs_0_), channel_id=1, source_target_pairs={{0,8},{1,9},{2,10},{3,11},{4,12},{5,13},{6,14},{7,15},{8,0},{9,1},... | collective-permute-start | bytes 294920 | tf_op jit(solution)/shard_map/ppermute | solution.py:24
  65.9 5.7 %collective-permute-start.32 = (bf16[3,64,256]{2,1,0:T(8,128)(2,1)S(1)}, bf16[3,64,256]{2,1,0:T(8,128)(2,1)S(1)}, u32[]{:S(2)}, u32[]{:S(2)}) collective-permute-start(bf16[3,64,256]{2,1,0:T(8,128)(2,1)S(1)} %get-tuple-element.88.refs_0_), channel_id=1, source_target_pairs={{0,4},{1,5},{2,6},{3,7},{4,0},{5,1},{6,2},{7,3},{8,12},{9,13},{10,... | collective-permute-start | bytes 294920 | tf_op jit(solution)/shard_map/ppermute | solution.py:24
  65.9 5.7 %collective-permute-start.31 = (bf16[3,64,256]{2,1,0:T(8,128)(2,1)S(1)}, bf16[3,64,256]{2,1,0:T(8,128)(2,1)S(1)}, u32[]{:S(2)}, u32[]{:S(2)}) collective-permute-start(bf16[3,64,256]{2,1,0:T(8,128)(2,1)S(1)} %get-tuple-element.88.refs_0_), channel_id=1, source_target_pairs={{0,2},{1,3},{2,0},{3,1},{4,6},{5,7},{6,4},{7,5},{8,10},{9,11},{10,... | collective-permute-start | bytes 294920 | tf_op jit(solution)/shard_map/ppermute | solution.py:24
  68.8 4.6 %collective-permute-start.41 = (bf16[3,64,256]{2,1,0:T(8,128)(2,1)S(1)}, bf16[3,64,256]{2,1,0:T(8,128)(2,1)S(1)}, u32[]{:S(2)}, u32[]{:S(2)}) collective-permute-start(bf16[3,64,256]{2,1,0:T(8,128)(2,1)S(1)} %collective-permute-done.37.refs_8_), channel_id=1, source_target_pairs={{0,8},{1,9},{2,10},{3,11},{4,12},{5,13},{6,14},{7,15},{8,0},{9,1},... | collective-permute-start | bytes 294920 | tf_op jit(solution)/shard_map/ppermute | solution.py:24
  69.1 5.5 %collective-permute-start.35 = (bf16[3,64,256]{2,1,0:T(8,128)(2,1)S(1)}, bf16[3,64,256]{2,1,0:T(8,128)(2,1)S(1)}, u32[]{:S(2)}, u32[]{:S(2)}) collective-permute-start(bf16[3,64,256]{2,1,0:T(8,128)(2,1)S(1)} %collective-permute-done.34.refs_4_), channel_id=1, source_target_pairs={{0,2},{1,3},{2,0},{3,1},{4,6},{5,7},{6,4},{7,5},{8,10},{9,11},{10,... | collective-permute-start | bytes 294920 | tf_op jit(solution)/shard_map/ppermute | solution.py:24
  69.7 16.2 %copy-start = (bf16[1,256,1024]{2,1,0:T(8,128)(2,1)S(1)}, bf16[1,256,1024]{2,1,0:T(8,128)(2,1)}, u32[]{:S(2)}) copy-start(bf16[1,256,1024]{2,1,0:T(8,128)(2,1)} %param.14) | copy-start | bytes 1572868
  71.5 5.5 %collective-permute-start.36 = (bf16[3,64,256]{2,1,0:T(8,128)(2,1)S(1)}, bf16[3,64,256]{2,1,0:T(8,128)(2,1)S(1)}, u32[]{:S(2)}, u32[]{:S(2)}) collective-permute-start(bf16[3,64,256]{2,1,0:T(8,128)(2,1)S(1)} %collective-permute-done.34.refs_4_), channel_id=1, source_target_pairs={{0,4},{1,5},{2,6},{3,7},{4,0},{5,1},{6,2},{7,3},{8,12},{9,13},{10,... | collective-permute-start | bytes 294920 | tf_op jit(solution)/shard_map/ppermute | solution.py:24
  72.7 5.7 %collective-permute-start.38 = (bf16[3,64,256]{2,1,0:T(8,128)(2,1)S(1)}, bf16[3,64,256]{2,1,0:T(8,128)(2,1)S(1)}, u32[]{:S(2)}, u32[]{:S(2)}) collective-permute-start(bf16[3,64,256]{2,1,0:T(8,128)(2,1)S(1)} %collective-permute-done.37.refs_8_), channel_id=1, source_target_pairs={{0,2},{1,3},{2,0},{3,1},{4,6},{5,7},{6,4},{7,5},{8,10},{9,11},{10,... | collective-permute-start | bytes 294920 | tf_op jit(solution)/shard_map/ppermute | solution.py:24
  74.6 6.6 %collective-permute-start.44 = (bf16[3,64,256]{2,1,0:T(8,128)(2,1)S(1)}, bf16[3,64,256]{2,1,0:T(8,128)(2,1)S(1)}, u32[]{:S(2)}, u32[]{:S(2)}) collective-permute-start(bf16[3,64,256]{2,1,0:T(8,128)(2,1)S(1)} %collective-permute-done.41.refs_12_), channel_id=1, source_target_pairs={{0,4},{1,5},{2,6},{3,7},{4,0},{5,1},{6,2},{7,3},{8,12},{9,13},{10,... | collective-permute-start | bytes 294920 | tf_op jit(solution)/shard_map/ppermute | solution.py:24
  74.7 4.6 %collective-permute-start.42 = (bf16[3,64,256]{2,1,0:T(8,128)(2,1)S(1)}, bf16[3,64,256]{2,1,0:T(8,128)(2,1)S(1)}, u32[]{:S(2)}, u32[]{:S(2)}) collective-permute-start(bf16[3,64,256]{2,1,0:T(8,128)(2,1)S(1)} %collective-permute-done.41.refs_12_), channel_id=1, source_target_pairs={{0,2},{1,3},{2,0},{3,1},{4,6},{5,7},{6,4},{7,5},{8,10},{9,11},{10,... | collective-permute-start | bytes 294920 | tf_op jit(solution)/shard_map/ppermute | solution.py:24
  76.3 5.3 %collective-permute-start.33 = (bf16[3,64,256]{2,1,0:T(8,128)(2,1)S(1)}, bf16[3,64,256]{2,1,0:T(8,128)(2,1)S(1)}, u32[]{:S(2)}, u32[]{:S(2)}) collective-permute-start(bf16[3,64,256]{2,1,0:T(8,128)(2,1)S(1)} %collective-permute-done.31.refs_1_), channel_id=1, source_target_pairs={{0,4},{1,5},{2,6},{3,7},{4,0},{5,1},{6,2},{7,3},{8,12},{9,13},{10,... | collective-permute-start | bytes 294920 | tf_op jit(solution)/shard_map/ppermute | solution.py:24
  77.0 5.0 %collective-permute-start.40 = (bf16[3,64,256]{2,1,0:T(8,128)(2,1)S(1)}, bf16[3,64,256]{2,1,0:T(8,128)(2,1)S(1)}, u32[]{:S(2)}, u32[]{:S(2)}) collective-permute-start(bf16[3,64,256]{2,1,0:T(8,128)(2,1)S(1)} %collective-permute-done.37.refs_8_), channel_id=1, source_target_pairs={{0,4},{1,5},{2,6},{3,7},{4,0},{5,1},{6,2},{7,3},{8,12},{9,13},{10,... | collective-permute-start | bytes 294920 | tf_op jit(solution)/shard_map/ppermute | solution.py:24
  78.4 4.6 %collective-permute-start.39 = (bf16[3,64,256]{2,1,0:T(8,128)(2,1)S(1)}, bf16[3,64,256]{2,1,0:T(8,128)(2,1)S(1)}, u32[]{:S(2)}, u32[]{:S(2)}) collective-permute-start(bf16[3,64,256]{2,1,0:T(8,128)(2,1)S(1)} %collective-permute-done.36.refs_6_), channel_id=1, source_target_pairs={{0,2},{1,3},{2,0},{3,1},{4,6},{5,7},{6,4},{7,5},{8,10},{9,11},{10,... | collective-permute-start | bytes 294920 | tf_op jit(solution)/shard_map/ppermute | solution.py:24
  79.3 6.5 %collective-permute-start.43 = (bf16[3,64,256]{2,1,0:T(8,128)(2,1)S(1)}, bf16[3,64,256]{2,1,0:T(8,128)(2,1)S(1)}, u32[]{:S(2)}, u32[]{:S(2)}) collective-permute-start(bf16[3,64,256]{2,1,0:T(8,128)(2,1)S(1)} %collective-permute-done.38.refs_9_), channel_id=1, source_target_pairs={{0,4},{1,5},{2,6},{3,7},{4,0},{5,1},{6,2},{7,3},{8,12},{9,13},{10,... | collective-permute-start | bytes 294920 | tf_op jit(solution)/shard_map/ppermute | solution.py:24
  81.2 4.6 %collective-permute-start.45 = (bf16[3,64,256]{2,1,0:T(8,128)(2,1)S(1)}, bf16[3,64,256]{2,1,0:T(8,128)(2,1)S(1)}, u32[]{:S(2)}, u32[]{:S(2)}) collective-permute-start(bf16[3,64,256]{2,1,0:T(8,128)(2,1)S(1)} %collective-permute-done.44.refs_14_), channel_id=1, source_target_pairs={{0,2},{1,3},{2,0},{3,1},{4,6},{5,7},{6,4},{7,5},{8,10},{9,11},{10,... | collective-permute-start | bytes 294920 | tf_op jit(solution)/shard_map/ppermute | solution.py:24
  86.6 1.9 %collective-permute-start.46 = (f32[3,3,32,256]{3,2,1,0:T(8,128)S(1)}, f32[3,3,32,256]{3,2,1,0:T(8,128)S(1)}, u32[]{:S(2)}, u32[]{:S(2)}) collective-permute-start(f32[3,3,32,256]{3,2,1,0:T(8,128)S(1)} %get-tuple-element.85), channel_id=1, source_target_pairs={{0,1},{1,0},{2,3},{3,2},{4,5},{5,4},{6,7},{7,6},{8,9},{9,8},{10,11... | collective-permute-start | bytes 884744 | tf_op jit(solution)/shard_map/ppermute | solution.py:24
  86.7 2.7 %collective-permute-start.47 = (bf16[256,1024]{1,0:T(8,128)(2,1)S(1)}, bf16[256,1024]{1,0:T(8,128)(2,1)S(1)}, u32[]{:S(2)}, u32[]{:S(2)}) collective-permute-start(bf16[256,1024]{1,0:T(8,128)(2,1)S(1)} %get-tuple-element.84), channel_id=1, source_target_pairs={{0,1},{1,0},{2,3},{3,2},{4,5},{5,4},{6,7},{7,6},{8,9},{9,8},{10,11... | collective-permute-start | bytes 1572872 | tf_op jit(solution)/shard_map/ppermute | solution.py:24

commit v15 on v14

--- a/solution.py
+++ b/solution.py
@@ -213,7 +213,7 @@
     return lax.optimization_barrier((value,) + others)[0]
 
 
-def gather_chips(piece):
+def gather_chips(piece, *first):
     depth = lax.axis_size("dev") // Z_UNIT
     column = [piece] + [None] * (depth - 1)
     for top in reversed([1 << bit for bit in range(depth.bit_length() - 1)]):
@@ -225,7 +225,7 @@
     for zj in range(2, depth):
         top = 1 << zj.bit_length() - 1
         if zj != top:
-            column[zj] = hop(column[top], (zj - top) * Z_UNIT)
+            column[zj] = hop(after(column[top], *first), (zj - top) * Z_UNIT)
     along_y[1] = hop(after(column[1], along_x[0]), Y_STEP)
     for zj in range(2, depth, 2):
         along_x[zj] = hop(after(column[zj], along_x[zj - 2], along_y[zj - 2]), X_STEP)
@@ -286,15 +286,16 @@
 
     other_x = hop(old_rows, CORE)
     other_c = hop(old_cotangent, CORE)
-    theirs = hop(jnp.stack([partners(master), partners(first), partners(second)]), CORE)
+    their_master = hop(partners(master), CORE)
+    theirs = hop(jnp.stack([partners(first), partners(second)]), CORE)
     other_y = hop(new_rows, CORE)
     other_live = hop(live, CORE)
     x_turned, c_turned = transposed(old_rows, other_x, old_cotangent, other_c)
-    theirs, other_y, other_live, x_turned, c_turned = lax.optimization_barrier(
-        (theirs, other_y, other_live, x_turned, c_turned)
-    )
-    master_two = both_rows(mine(master), theirs[0])
-    pieces = gather_chips(master_two.astype(jnp.bfloat16))
+    their_master, other_y, other_live, x_turned, c_turned = lax.optimization_barrier(
+        (their_master, other_y, other_live, x_turned, c_turned)
+    )
+    master_two = both_rows(mine(master), their_master)
+    pieces = gather_chips(master_two.astype(jnp.bfloat16), theirs)
     *grads, matches = backward(
         old_slots[None],
         new_slots[None],
@@ -309,9 +310,10 @@
         c_turned,
     )
     theirs = after(theirs, grads[0])
-    first_two = both_rows(mine(first), theirs[1])
-    second_two = both_rows(mine(second), theirs[2])
+    first_two = both_rows(mine(first), theirs[0])
+    second_two = both_rows(mine(second), theirs[1])
     grad = reduce_chips(grads)
+    grad, is_own = lax.optimization_barrier((grad, matches == 1))
     updated = adam_update(master_two, first_two, second_two, grad)
 
     new_pieces = gather_chips(updated[0].astype(jnp.bfloat16))
@@ -323,7 +325,7 @@
     state = jnp.where(
         core == 0, jnp.stack([own_part, from_other], axis=1), jnp.stack([from_other, own_part], axis=1)
     )
-    new_outputs = jnp.where(matches == 1, own_out, hop(other_out, CORE))
+    new_outputs = jnp.where(is_own, own_out, hop(other_out, CORE))
     return (state[0], state[1], state[2], new_outputs[None])
 
 

time: 90.5 us -> 89.8 us (level)
  waiting for transfers between devices: 26.3 us -> 25.1 us
    ppermute x48 -> x49, waiting for transfers between devices: 26.3 us -> 25.1 us  [hop(): lax.ppermute(block, 'dev', [(low, low ^ mask) for low in range(count)])]
    dynamic_slice x1 -> x0, local copies, waits for them, and re-layouts: 0.96 us -> none  [partners(): return lax.dynamic_index_in_dim(state, 1 - core, 0, keepdims=False)]
    squeeze x1 -> x2, local copies, waits for them, and re-layouts: 1.06 us -> 2.01 us  [mine(): return lax.dynamic_index_in_dim(state, core, 0, keepdims=False)]
    ppermute x48 -> x49, starting transfers between devices: 52.1 us -> 52.6 us  [hop(): lax.ppermute(block, 'dev', [(low, low ^ mask) for low in range(count)])]
  transfers between devices with their start and end apart: 48 -> 49, of which waited for: 24 -> 23; matrix products, arithmetic and copies ran while one was open for 4% -> 4% of each run, Pallas kernels for 1% -> 1%
where the time goes in v15:
time: 89.8 us; the launch traced here: 89.6 us
  starting transfers between devices  52.6 us (59%)
  waiting for transfers between devices  25.1 us (28%)
  Pallas kernels  5.21 us (6%)
  local copies, waits for them, and re-layouts  2.92 us (3%)
  between operations  2.2 us (2%)
  other arithmetic  1.52 us (2%)
    ppermute x49, starting transfers between devices, hop(): lax.ppermute(block, 'dev', [(low, low ^ mask) for low in range(count)])  52.6 us
    ppermute x49, waiting for transfers between devices, hop(): lax.ppermute(block, 'dev', [(low, low ^ mask) for low in range(count)])  25.1 us
    pallas_call x1, Pallas kernels, backward(): pl.pallas_call(functools.partial(backward_kernel, count), out_shape=[one,...  3.18 us
    squeeze x2, local copies, waits for them, and re-layouts, mine(): return lax.dynamic_index_in_dim(state, core, 0, keepdims=False)  2.01 us
  transfers between devices with their start and end apart: 49, of which 23 were waited for; matrix products, arithmetic and copies ran while one was open for 4% of the time, Pallas kernels for 1%

profile of v15, /device:TPU:0, one launch (start us, length us, event | category | flops | bytes accessed | tf_op | source)
XLA Modules:
  0.0 89.6 jit_solution(17488443758096073301)
XLA Ops:
  0.7 0.5 collective-permute-start.3
  1.2 0.4 collective-permute-start.1
  1.8 1.0 %dynamic-slice_bitcast_fusion.4 = (f32[3,32,256]{2,1,0:T(8,128)S(1)}, f32[3,32,256]{2,1,0:T(8,128)S(1)}) fusion(f32[2,3,32,256]{3,2,1,0:T(8,128)} %param.9, s32[]{:T(128)S(6)} %select_n.47, s32[]{:T(128)S(6)} %select_n.48), kind=kLoop, calls=%fused_computation.52 | loop fusion | bytes 393224 | tf_op jit(solution)/shard_map/jit(dynamic_index_in_dim)/squeeze | solution.py:277
  2.7 0.5 collective-permute-start
  3.2 1.1 %dynamic-slice_bitcast_fusion.1 = (f32[3,32,256]{2,1,0:T(8,128)S(1)}, f32[1,3,32,256]{3,2,1,0:T(8,128)S(1)}, f32[1,3,32,256]{3,2,1,0:T(8,128)S(1)}, f32[3,32,256]{2,1,0:T(8,128)S(1)}) fusion(f32[2,3,32,256]{3,2,1,0:T(8,128)} %param.11, s32[]{:T(128)S(6)} %select_n.47, s32[]{:T(128)S(6)} %select_n.48, f32[2,3,32,256]{3,2,1,0:T(8,128)} %param.10), kind=kLoop, calls=%fused_computation.48 | loop fusion | bytes 786440 | tf_op jit(solution)/shard_map/jit(dynamic_index_in_dim)/squeeze | solution.py:277
  4.5 0.6 transpose_rows.1
  5.1 4.1 %collective-permute-start.12 = (bf16[3,64,256]{2,1,0:T(8,128)(2,1)S(1)}, bf16[3,64,256]{2,1,0:T(8,128)(2,1)S(1)}, u32[]{:S(2)}, u32[]{:S(2)}) collective-permute-start(bf16[3,64,256]{2,1,0:T(8,128)(2,1)S(1)} %fusion.17.refs_0_), channel_id=1, source_target_pairs={{0,16},{1,17},{2,18},{3,19},{4,20},{5,21},{6,22},{7,23},{8,24},{9,... | collective-permute-start | bytes 294920 | tf_op jit(solution)/shard_map/ppermute | solution.py:24
  9.2 1.6 %collective-permute-start.9 = (bf16[3,64,256]{2,1,0:T(8,128)(2,1)S(1)}, bf16[3,64,256]{2,1,0:T(8,128)(2,1)S(1)}, u32[]{:S(2)}, u32[]{:S(2)}) collective-permute-start(bf16[3,64,256]{2,1,0:T(8,128)(2,1)S(1)} %fusion.17.refs_0_), channel_id=1, source_target_pairs={{0,8},{1,9},{2,10},{3,11},{4,12},{5,13},{6,14},{7,15},{8,0},{9,1},... | collective-permute-start | bytes 294920 | tf_op jit(solution)/shard_map/ppermute | solution.py:24
  10.8 1.5 %collective-permute-start.6 = (bf16[3,64,256]{2,1,0:T(8,128)(2,1)S(1)}, bf16[3,64,256]{2,1,0:T(8,128)(2,1)S(1)}, u32[]{:S(2)}, u32[]{:S(2)}) collective-permute-start(bf16[3,64,256]{2,1,0:T(8,128)(2,1)S(1)} %fusion.17.refs_0_), channel_id=1, source_target_pairs={{0,2},{1,3},{2,0},{3,1},{4,6},{5,7},{6,4},{7,5},{8,10},{9,11},{10,... | collective-permute-start | bytes 294920 | tf_op jit(solution)/shard_map/ppermute | solution.py:24
  12.3 1.5 %collective-permute-start.7 = (bf16[3,64,256]{2,1,0:T(8,128)(2,1)S(1)}, bf16[3,64,256]{2,1,0:T(8,128)(2,1)S(1)}, u32[]{:S(2)}, u32[]{:S(2)}) collective-permute-start(bf16[3,64,256]{2,1,0:T(8,128)(2,1)S(1)} %fusion.17.refs_0_), channel_id=1, source_target_pairs={{0,4},{1,5},{2,6},{3,7},{4,0},{5,1},{6,2},{7,3},{8,12},{9,13},{10,... | collective-permute-start | bytes 294920 | tf_op jit(solution)/shard_map/ppermute | solution.py:24
  13.8 0.7 collective-permute-done.12.refs_8_
  14.5 0.6 collective-permute-start.16
  15.1 1.5 %collective-permute-start.10 = (bf16[3,64,256]{2,1,0:T(8,128)(2,1)S(1)}, bf16[3,64,256]{2,1,0:T(8,128)(2,1)S(1)}, u32[]{:S(2)}, u32[]{:S(2)}) collective-permute-start(bf16[3,64,256]{2,1,0:T(8,128)(2,1)S(1)} %collective-permute-done.9.refs_4_), channel_id=1, source_target_pairs={{0,2},{1,3},{2,0},{3,1},{4,6},{5,7},{6,4},{7,5},{8,10},{9,11},{10,... | collective-permute-start | bytes 294920 | tf_op jit(solution)/shard_map/ppermute | solution.py:24
  16.6 1.5 %collective-permute-start.11 = (bf16[3,64,256]{2,1,0:T(8,128)(2,1)S(1)}, bf16[3,64,256]{2,1,0:T(8,128)(2,1)S(1)}, u32[]{:S(2)}, u32[]{:S(2)}) collective-permute-start(bf16[3,64,256]{2,1,0:T(8,128)(2,1)S(1)} %collective-permute-done.9.refs_4_), channel_id=1, source_target_pairs={{0,4},{1,5},{2,6},{3,7},{4,0},{5,1},{6,2},{7,3},{8,12},{9,13},{10,... | collective-permute-start | bytes 294920 | tf_op jit(solution)/shard_map/ppermute | solution.py:24
  18.1 0.5 collective-permute-start.13
  18.7 0.4 collective-permute-done.16.refs_12_
  19.1 0.6 collective-permute-done.10.refs_5_
  19.7 2.3 %collective-permute-start.17 = (bf16[3,64,256]{2,1,0:T(8,128)(2,1)S(1)}, bf16[3,64,256]{2,1,0:T(8,128)(2,1)S(1)}, u32[]{:S(2)}, u32[]{:S(2)}) collective-permute-start(bf16[3,64,256]{2,1,0:T(8,128)(2,1)S(1)} %collective-permute-done.16.refs_12_), channel_id=1, source_target_pairs={{0,2},{1,3},{2,0},{3,1},{4,6},{5,7},{6,4},{7,5},{8,10},{9,11},{10,... | collective-permute-start | bytes 294920 | tf_op jit(solution)/shard_map/ppermute | solution.py:24
  22.0 1.6 %collective-permute-start.19 = (bf16[3,64,256]{2,1,0:T(8,128)(2,1)S(1)}, bf16[3,64,256]{2,1,0:T(8,128)(2,1)S(1)}, u32[]{:S(2)}, u32[]{:S(2)}) collective-permute-start(bf16[3,64,256]{2,1,0:T(8,128)(2,1)S(1)} %collective-permute-done.16.refs_12_), channel_id=1, source_target_pairs={{0,4},{1,5},{2,6},{3,7},{4,0},{5,1},{6,2},{7,3},{8,12},{9,13},{10,... | collective-permute-start | bytes 294920 | tf_op jit(solution)/shard_map/ppermute | solution.py:24
  24.0 1.6 %collective-permute-start.15 = (bf16[3,64,256]{2,1,0:T(8,128)(2,1)S(1)}, bf16[3,64,256]{2,1,0:T(8,128)(2,1)S(1)}, u32[]{:S(2)}, u32[]{:S(2)}) collective-permute-start(bf16[3,64,256]{2,1,0:T(8,128)(2,1)S(1)} %collective-permute-done.12.refs_8_), channel_id=1, source_target_pairs={{0,4},{1,5},{2,6},{3,7},{4,0},{5,1},{6,2},{7,3},{8,12},{9,13},{10,... | collective-permute-start | bytes 294920 | tf_op jit(solution)/shard_map/ppermute | solution.py:24
  25.6 0.5 collective-permute-start.14
  26.1 0.9 collective-permute-done.19.refs_14_
  27.0 0.7 collective-permute-start.20
  27.7 1.0 %collective-permute-start.18 = (bf16[3,64,256]{2,1,0:T(8,128)(2,1)S(1)}, bf16[3,64,256]{2,1,0:T(8,128)(2,1)S(1)}, u32[]{:S(2)}, u32[]{:S(2)}) collective-permute-start(bf16[3,64,256]{2,1,0:T(8,128)(2,1)S(1)} %collective-permute-done.13.refs_9_), channel_id=1, source_target_pairs={{0,4},{1,5},{2,6},{3,7},{4,0},{5,1},{6,2},{7,3},{8,12},{9,13},{10,... | collective-permute-start | bytes 294920 | tf_op jit(solution)/shard_map/ppermute | solution.py:24
  29.4 0.6 collective-permute-done.15.refs_10_
  30.3 1.3 %collective-permute-done.20.refs_15_ = bf16[3,64,256]{2,1,0:T(8,128)(2,1)S(1)} collective-permute-done((bf16[3,64,256]{2,1,0:T(8,128)(2,1)S(1)}, bf16[3,64,256]{2,1,0:T(8,128)(2,1)S(1)}, u32[]{:S(2)}, u32[]{:S(2)}) %collective-permute-start.20) | collective-permute-done | bytes 98336 | tf_op jit(solution)/shard_map/ppermute | solution.py:24
  31.6 0.7 collective-permute-done.18.refs_11_
  32.3 3.2 %slot_gradients.1 = (bf16[3,64,256]{2,1,0:T(8,128)(2,1)S(1)}, bf16[3,64,256]{2,1,0:T(8,128)(2,1)S(1)}, bf16[2,3,64,256]{3,2,1,0:T(8,128)(2,1)S(1)}, bf16[3,64,25...) custom-call(s32[1,32]{1,0:T(1,128)S(1)} %bitcast.86, ...), custom_call_target="tpu_custom_call" | custom-call | flops 1610612736 | bytes 7340032 | tf_op jit(solution)/shard_map/slot_gradients/pallas_call | solution.py:160
  35.5 1.0 %collective-permute-start.21 = (bf16[2,3,64,256]{3,2,1,0:T(8,128)(2,1)S(1)}, bf16[2,3,64,256]{3,2,1,0:T(8,128)(2,1)S(1)}, u32[]{:S(2)}, u32[]{:S(2)}) collective-permute-start(bf16[2,3,64,256]{3,2,1,0:T(8,128)(2,1)S(1)} %get-tuple-element.66), channel_id=1, source_target_pairs={{0,4},{1,5},{2,6},{3,7},{4,0},{5,1},{6,2},{7,3},{8,12},{9,13},{10,... | collective-permute-start | bytes 589832 | tf_op jit(solution)/shard_map/ppermute | solution.py:24
  36.5 2.0 %collective-permute-start.24 = (bf16[2,3,64,256]{3,2,1,0:T(8,128)(2,1)S(1)}, bf16[2,3,64,256]{3,2,1,0:T(8,128)(2,1)S(1)}, u32[]{:S(2)}, u32[]{:S(2)}) collective-permute-start(bf16[2,3,64,256]{3,2,1,0:T(8,128)(2,1)S(1)} %get-tuple-element.69), channel_id=1, source_target_pairs={{0,2},{1,3},{2,0},{3,1},{4,6},{5,7},{6,4},{7,5},{8,10},{9,11},{10,... | collective-permute-start | bytes 589832 | tf_op jit(solution)/shard_map/ppermute | solution.py:24
  38.5 3.5 %collective-permute-done.21 = bf16[2,3,64,256]{3,2,1,0:T(8,128)(2,1)S(1)} collective-permute-done((bf16[2,3,64,256]{3,2,1,0:T(8,128)(2,1)S(1)}, bf16[2,3,64,256]{3,2,1,0:T(8,128)(2,1)S(1)}, u32[]{:S(2)}, u32[]{:S(2)}) %collective-permute-start.21) | collective-permute-done | bytes 196640 | tf_op jit(solution)/shard_map/ppermute | solution.py:24
  42.1 1.5 %collective-permute-start.22 = (bf16[3,64,256]{2,1,0:T(8,128)(2,1)S(1)}, bf16[3,64,256]{2,1,0:T(8,128)(2,1)S(1)}, u32[]{:S(2)}, u32[]{:S(2)}) collective-permute-start(bf16[3,64,256]{2,1,0:T(8,128)(2,1)S(1)} %fusion.14), channel_id=1, source_target_pairs={{0,2},{1,3},{2,0},{3,1},{4,6},{5,7},{6,4},{7,5},{8,10},{9,11},{10,... | collective-permute-start | bytes 294920 | tf_op jit(solution)/shard_map/ppermute | solution.py:24
  43.7 2.5 %collective-permute-start.27 = (bf16[3,64,256]{2,1,0:T(8,128)(2,1)S(1)}, bf16[3,64,256]{2,1,0:T(8,128)(2,1)S(1)}, u32[]{:S(2)}, u32[]{:S(2)}) collective-permute-start(bf16[3,64,256]{2,1,0:T(8,128)(2,1)S(1)} %fusion.7), channel_id=1, source_target_pairs={{0,4},{1,5},{2,6},{3,7},{4,0},{5,1},{6,2},{7,3},{8,12},{9,13},{10,... | collective-permute-start | bytes 294920 | tf_op jit(solution)/shard_map/ppermute | solution.py:24
  46.3 0.5 collective-permute-done.22
  46.8 3.5 %collective-permute-start.23 = (bf16[3,64,256]{2,1,0:T(8,128)(2,1)S(1)}, bf16[3,64,256]{2,1,0:T(8,128)(2,1)S(1)}, u32[]{:S(2)}, u32[]{:S(2)}) collective-permute-start(bf16[3,64,256]{2,1,0:T(8,128)(2,1)S(1)} %fusion.16), channel_id=1, source_target_pairs={{0,16},{1,17},{2,18},{3,19},{4,20},{5,21},{6,22},{7,23},{8,24},{9,... | collective-permute-start | bytes 294920 | tf_op jit(solution)/shard_map/ppermute | solution.py:24
  50.4 2.4 %collective-permute-start.30 = (bf16[3,64,256]{2,1,0:T(8,128)(2,1)S(1)}, bf16[3,64,256]{2,1,0:T(8,128)(2,1)S(1)}, u32[]{:S(2)}, u32[]{:S(2)}) collective-permute-start(bf16[3,64,256]{2,1,0:T(8,128)(2,1)S(1)} %fusion.4), channel_id=1, source_target_pairs={{0,4},{1,5},{2,6},{3,7},{4,0},{5,1},{6,2},{7,3},{8,12},{9,13},{10,... | collective-permute-start | bytes 294920 | tf_op jit(solution)/shard_map/ppermute | solution.py:24
  52.8 2.3 %collective-permute-start.28 = (bf16[3,64,256]{2,1,0:T(8,128)(2,1)S(1)}, bf16[3,64,256]{2,1,0:T(8,128)(2,1)S(1)}, u32[]{:S(2)}, u32[]{:S(2)}) collective-permute-start(bf16[3,64,256]{2,1,0:T(8,128)(2,1)S(1)} %fusion.9), channel_id=1, source_target_pairs={{0,24},{1,25},{2,26},{3,27},{4,28},{5,29},{6,30},{7,31},{8,16},{9,... | collective-permute-start | bytes 294920 | tf_op jit(solution)/shard_map/ppermute | solution.py:24
  55.4 0.7 collective-permute-start.31
  56.7 3.3 %collective-permute-done.28 = bf16[3,64,256]{2,1,0:T(8,128)(2,1)S(1)} collective-permute-done((bf16[3,64,256]{2,1,0:T(8,128)(2,1)S(1)}, bf16[3,64,256]{2,1,0:T(8,128)(2,1)S(1)}, u32[]{:S(2)}, u32[]{:S(2)}) %collective-permute-start.28) | collective-permute-done | bytes 98336 | tf_op jit(solution)/shard_map/ppermute | solution.py:24
  60.3 1.0 %collective-permute-done.31 = bf16[3,64,256]{2,1,0:T(8,128)(2,1)S(1)} collective-permute-done((bf16[3,64,256]{2,1,0:T(8,128)(2,1)S(1)}, bf16[3,64,256]{2,1,0:T(8,128)(2,1)S(1)}, u32[]{:S(2)}, u32[]{:S(2)}) %collective-permute-start.31) | collective-permute-done | bytes 98336 | tf_op jit(solution)/shard_map/ppermute | solution.py:24
  61.6 1.4 %collective-permute-start.38 = (bf16[3,64,256]{2,1,0:T(8,128)(2,1)S(1)}, bf16[3,64,256]{2,1,0:T(8,128)(2,1)S(1)}, u32[]{:S(2)}, u32[]{:S(2)}) collective-permute-start(bf16[3,64,256]{2,1,0:T(8,128)(2,1)S(1)} %get-tuple-element.94.refs_0_), channel_id=1, source_target_pairs={{0,16},{1,17},{2,18},{3,19},{4,20},{5,21},{6,22},{7,23},{8,24},{9,... | collective-permute-start | bytes 294920 | tf_op jit(solution)/shard_map/ppermute | solution.py:24
  63.0 2.5 %collective-permute-start.35 = (bf16[3,64,256]{2,1,0:T(8,128)(2,1)S(1)}, bf16[3,64,256]{2,1,0:T(8,128)(2,1)S(1)}, u32[]{:S(2)}, u32[]{:S(2)}) collective-permute-start(bf16[3,64,256]{2,1,0:T(8,128)(2,1)S(1)} %get-tuple-element.94.refs_0_), channel_id=1, source_target_pairs={{0,8},{1,9},{2,10},{3,11},{4,12},{5,13},{6,14},{7,15},{8,0},{9,1},... | collective-permute-start | bytes 294920 | tf_op jit(solution)/shard_map/ppermute | solution.py:24
  65.5 1.1 %collective-permute-start.32 = (bf16[3,64,256]{2,1,0:T(8,128)(2,1)S(1)}, bf16[3,64,256]{2,1,0:T(8,128)(2,1)S(1)}, u32[]{:S(2)}, u32[]{:S(2)}) collective-permute-start(bf16[3,64,256]{2,1,0:T(8,128)(2,1)S(1)} %get-tuple-element.94.refs_0_), channel_id=1, source_target_pairs={{0,2},{1,3},{2,0},{3,1},{4,6},{5,7},{6,4},{7,5},{8,10},{9,11},{10,... | collective-permute-start | bytes 294920 | tf_op jit(solution)/shard_map/ppermute | solution.py:24
  66.6 1.8 %collective-permute-done.38.refs_8_ = bf16[3,64,256]{2,1,0:T(8,128)(2,1)S(1)} collective-permute-done((bf16[3,64,256]{2,1,0:T(8,128)(2,1)S(1)}, bf16[3,64,256]{2,1,0:T(8,128)(2,1)S(1)}, u32[]{:S(2)}, u32[]{:S(2)}) %collective-permute-start.38) | collective-permute-done | bytes 98336 | tf_op jit(solution)/shard_map/ppermute | solution.py:24
  68.7 0.6 collective-permute-start.36
  69.3 1.8 %collective-permute-done.33.refs_2_ = bf16[3,64,256]{2,1,0:T(8,128)(2,1)S(1)} collective-permute-done((bf16[3,64,256]{2,1,0:T(8,128)(2,1)S(1)}, bf16[3,64,256]{2,1,0:T(8,128)(2,1)S(1)}, u32[]{:S(2)}, u32[]{:S(2)}) %collective-permute-start.33) | collective-permute-done | bytes 98336 | tf_op jit(solution)/shard_map/ppermute | solution.py:24
  71.1 1.1 %collective-permute-start.37 = (bf16[3,64,256]{2,1,0:T(8,128)(2,1)S(1)}, bf16[3,64,256]{2,1,0:T(8,128)(2,1)S(1)}, u32[]{:S(2)}, u32[]{:S(2)}) collective-permute-start(bf16[3,64,256]{2,1,0:T(8,128)(2,1)S(1)} %collective-permute-done.35.refs_4_), channel_id=1, source_target_pairs={{0,4},{1,5},{2,6},{3,7},{4,0},{5,1},{6,2},{7,3},{8,12},{9,13},{10,... | collective-permute-start | bytes 294920 | tf_op jit(solution)/shard_map/ppermute | solution.py:24
  72.4 0.6 collective-permute-done.42.refs_12_
  73.0 1.2 %collective-permute-done.36.refs_5_ = bf16[3,64,256]{2,1,0:T(8,128)(2,1)S(1)} collective-permute-done((bf16[3,64,256]{2,1,0:T(8,128)(2,1)S(1)}, bf16[3,64,256]{2,1,0:T(8,128)(2,1)S(1)}, u32[]{:S(2)}, u32[]{:S(2)}) %collective-permute-start.36) | collective-permute-done | bytes 98336 | tf_op jit(solution)/shard_map/ppermute | solution.py:24
  74.4 1.5 %collective-permute-start.43 = (bf16[3,64,256]{2,1,0:T(8,128)(2,1)S(1)}, bf16[3,64,256]{2,1,0:T(8,128)(2,1)S(1)}, u32[]{:S(2)}, u32[]{:S(2)}) collective-permute-start(bf16[3,64,256]{2,1,0:T(8,128)(2,1)S(1)} %collective-permute-done.42.refs_12_), channel_id=1, source_target_pairs={{0,2},{1,3},{2,0},{3,1},{4,6},{5,7},{6,4},{7,5},{8,10},{9,11},{10,... | collective-permute-start | bytes 294920 | tf_op jit(solution)/shard_map/ppermute | solution.py:24
  75.9 0.7 collective-permute-start.34
  76.6 1.4 %collective-permute-start.41 = (bf16[3,64,256]{2,1,0:T(8,128)(2,1)S(1)}, bf16[3,64,256]{2,1,0:T(8,128)(2,1)S(1)}, u32[]{:S(2)}, u32[]{:S(2)}) collective-permute-start(bf16[3,64,256]{2,1,0:T(8,128)(2,1)S(1)} %collective-permute-done.38.refs_8_), channel_id=1, source_target_pairs={{0,4},{1,5},{2,6},{3,7},{4,0},{5,1},{6,2},{7,3},{8,12},{9,13},{10,... | collective-permute-start | bytes 294920 | tf_op jit(solution)/shard_map/ppermute | solution.py:24
  78.0 0.6 collective-permute-start.40
  78.6 0.4 collective-permute-done.43.refs_13_
  79.0 1.8 %collective-permute-start.44 = (bf16[3,64,256]{2,1,0:T(8,128)(2,1)S(1)}, bf16[3,64,256]{2,1,0:T(8,128)(2,1)S(1)}, u32[]{:S(2)}, u32[]{:S(2)}) collective-permute-start(bf16[3,64,256]{2,1,0:T(8,128)(2,1)S(1)} %collective-permute-done.39.refs_9_), channel_id=1, source_target_pairs={{0,4},{1,5},{2,6},{3,7},{4,0},{5,1},{6,2},{7,3},{8,12},{9,13},{10,... | collective-permute-start | bytes 294920 | tf_op jit(solution)/shard_map/ppermute | solution.py:24
  81.2 0.4 collective-permute-done.41.refs_10_
  81.6 1.0 %collective-permute-done.40.refs_7_ = bf16[3,64,256]{2,1,0:T(8,128)(2,1)S(1)} collective-permute-done((bf16[3,64,256]{2,1,0:T(8,128)(2,1)S(1)}, bf16[3,64,256]{2,1,0:T(8,128)(2,1)S(1)}, u32[]{:S(2)}, u32[]{:S(2)}) %collective-permute-start.40) | collective-permute-done | bytes 98336 | tf_op jit(solution)/shard_map/ppermute | solution.py:24
  82.6 2.9 %collective-permute-done.46.refs_15_ = bf16[3,64,256]{2,1,0:T(8,128)(2,1)S(1)} collective-permute-done((bf16[3,64,256]{2,1,0:T(8,128)(2,1)S(1)}, bf16[3,64,256]{2,1,0:T(8,128)(2,1)S(1)}, u32[]{:S(2)}, u32[]{:S(2)}) %collective-permute-start.46) | collective-permute-done | bytes 98336 | tf_op jit(solution)/shard_map/ppermute | solution.py:24
  85.5 0.8 other_outputs.1
  86.3 0.5 collective-permute-start.48
  86.8 0.7 own_outputs.1
  87.5 0.4 collective-permute-done.47
  87.9 0.8 slice_bitcast_fusion
  88.8 0.8 select_bitcast_fusion
  (68 shorter events, 3.4 us)
Async XLA Ops:
  0.6 3.9 %copy-start.1 = (bf16[1,256,1024]{2,1,0:T(8,128)(2,1)S(1)}, bf16[1,256,1024]{2,1,0:T(8,128)(2,1)}, u32[]{:S(2)}) copy-start(bf16[1,256,1024]{2,1,0:T(8,128)(2,1)} %param.12) | copy-start | bytes 1572868
  0.6 3.8 %copy-start.2 = (bf16[1,256,1024]{2,1,0:T(8,128)(2,1)S(1)}, bf16[1,256,1024]{2,1,0:T(8,128)(2,1)}, u32[]{:S(2)}) copy-start(bf16[1,256,1024]{2,1,0:T(8,128)(2,1)} %param.13) | copy-start | bytes 1572868
  0.7 3.7 %collective-permute-start.3 = (bf16[256,1024]{1,0:T(8,128)(2,1)}, bf16[256,1024]{1,0:T(8,128)(2,1)S(1)}, u32[]{:S(2)}, u32[]{:S(2)}) collective-permute-start(bf16[256,1024]{1,0:T(8,128)(2,1)} %bitcast.80), channel_id=1, source_target_pairs={{0,1},{1,0},{2,3},{3,2},{4,5},{5,4},{6,7},{7,6},{8,9},{9,8},{10,11... | collective-permute-start | bytes 1572872 | tf_op jit(solution)/shard_map/ppermute | solution.py:24
  1.2 3.3 %collective-permute-start.4 = (bf16[256,1024]{1,0:T(8,128)(2,1)}, bf16[256,1024]{1,0:T(8,128)(2,1)S(1)}, u32[]{:S(2)}, u32[]{:S(2)}) collective-permute-start(bf16[256,1024]{1,0:T(8,128)(2,1)} %bitcast.83), channel_id=1, source_target_pairs={{0,1},{1,0},{2,3},{3,2},{4,5},{5,4},{6,7},{7,6},{8,9},{9,8},{10,11... | collective-permute-start | bytes 1572872 | tf_op jit(solution)/shard_map/ppermute | solution.py:24
  1.2 3.9 %collective-permute-start.1 = (bf16[256,1024]{1,0:T(8,128)(2,1)}, bf16[256,1024]{1,0:T(8,128)(2,1)S(1)}, u32[]{:S(2)}, u32[]{:S(2)}) collective-permute-start(bf16[256,1024]{1,0:T(8,128)(2,1)} %bitcast.77), channel_id=1, source_target_pairs={{0,1},{1,0},{2,3},{3,2},{4,5},{5,4},{6,7},{7,6},{8,9},{9,8},{10,11... | collective-permute-start | bytes 1572872 | tf_op jit(solution)/shard_map/ppermute | solution.py:24
  1.7 3.4 %collective-permute-start.2 = (s32[1]{0:T(128)}, s32[1]{0:T(128)}, u32[]{:S(2)}, u32[]{:S(2)}) collective-permute-start(s32[1]{0:T(128)} %param.17), channel_id=1, source_target_pairs={{0,1},{1,0},{2,3},{3,2},{4,5},{5,4},{6,7},{7,6},{8,9},{9,8},{10,11... | collective-permute-start | bytes 20 | tf_op jit(solution)/shard_map/ppermute | solution.py:24
  2.7 2.4 %collective-permute-start = (f32[3,32,256]{2,1,0:T(8,128)S(1)}, f32[3,32,256]{2,1,0:T(8,128)S(1)}, u32[]{:S(2)}, u32[]{:S(2)}) collective-permute-start(f32[3,32,256]{2,1,0:T(8,128)S(1)} %get-tuple-element.109), channel_id=1, source_target_pairs={{0,1},{1,0},{2,3},{3,2},{4,5},{5,4},{6,7},{7,6},{8,9},{9,8},{10,11... | collective-permute-start | bytes 294920 | tf_op jit(solution)/shard_map/ppermute | solution.py:24
  4.3 28.0 %copy-start.3 = (s32[32]{0:T(128)S(1)}, s32[32]{0:T(128)}, u32[]{:S(2)}) copy-start(s32[32]{0:T(128)} %param.15) | copy-start | bytes 388
  4.3 28.0 %copy-start.4 = (s32[32]{0:T(128)S(1)}, s32[32]{0:T(128)}, u32[]{:S(2)}) copy-start(s32[32]{0:T(128)} %param.16) | copy-start | bytes 388
  4.3 9.5 %collective-permute-start.5 = (f32[2,3,32,256]{3,2,1,0:T(8,128)S(1)}, f32[2,3,32,256]{3,2,1,0:T(8,128)S(1)}, u32[]{:S(2)}, u32[]{:S(2)}) collective-permute-start(f32[2,3,32,256]{3,2,1,0:T(8,128)S(1)} %pad_maximum_fusion.1), channel_id=1, source_target_pairs={{0,1},{1,0},{2,3},{3,2},{4,5},{5,4},{6,7},{7,6},{8,9},{9,8},{10,11... | collective-permute-start | bytes 589832 | tf_op jit(solution)/shard_map/ppermute | solution.py:24
  5.1 9.3 %collective-permute-start.12 = (bf16[3,64,256]{2,1,0:T(8,128)(2,1)S(1)}, bf16[3,64,256]{2,1,0:T(8,128)(2,1)S(1)}, u32[]{:S(2)}, u32[]{:S(2)}) collective-permute-start(bf16[3,64,256]{2,1,0:T(8,128)(2,1)S(1)} %fusion.17.refs_0_), channel_id=1, source_target_pairs={{0,16},{1,17},{2,18},{3,19},{4,20},{5,21},{6,22},{7,23},{8,24},{9,... | collective-permute-start | bytes 294920 | tf_op jit(solution)/shard_map/ppermute | solution.py:24
  9.2 5.9 %collective-permute-start.9 = (bf16[3,64,256]{2,1,0:T(8,128)(2,1)S(1)}, bf16[3,64,256]{2,1,0:T(8,128)(2,1)S(1)}, u32[]{:S(2)}, u32[]{:S(2)}) collective-permute-start(bf16[3,64,256]{2,1,0:T(8,128)(2,1)S(1)} %fusion.17.refs_0_), channel_id=1, source_target_pairs={{0,8},{1,9},{2,10},{3,11},{4,12},{5,13},{6,14},{7,15},{8,0},{9,1},... | collective-permute-start | bytes 294920 | tf_op jit(solution)/shard_map/ppermute | solution.py:24
  10.8 5.8 %collective-permute-start.6 = (bf16[3,64,256]{2,1,0:T(8,128)(2,1)S(1)}, bf16[3,64,256]{2,1,0:T(8,128)(2,1)S(1)}, u32[]{:S(2)}, u32[]{:S(2)}) collective-permute-start(bf16[3,64,256]{2,1,0:T(8,128)(2,1)S(1)} %fusion.17.refs_0_), channel_id=1, source_target_pairs={{0,2},{1,3},{2,0},{3,1},{4,6},{5,7},{6,4},{7,5},{8,10},{9,11},{10,... | collective-permute-start | bytes 294920 | tf_op jit(solution)/shard_map/ppermute | solution.py:24
  12.3 5.8 %collective-permute-start.7 = (bf16[3,64,256]{2,1,0:T(8,128)(2,1)S(1)}, bf16[3,64,256]{2,1,0:T(8,128)(2,1)S(1)}, u32[]{:S(2)}, u32[]{:S(2)}) collective-permute-start(bf16[3,64,256]{2,1,0:T(8,128)(2,1)S(1)} %fusion.17.refs_0_), channel_id=1, source_target_pairs={{0,4},{1,5},{2,6},{3,7},{4,0},{5,1},{6,2},{7,3},{8,12},{9,13},{10,... | collective-permute-start | bytes 294920 | tf_op jit(solution)/shard_map/ppermute | solution.py:24
  14.5 4.6 %collective-permute-start.16 = (bf16[3,64,256]{2,1,0:T(8,128)(2,1)S(1)}, bf16[3,64,256]{2,1,0:T(8,128)(2,1)S(1)}, u32[]{:S(2)}, u32[]{:S(2)}) collective-permute-start(bf16[3,64,256]{2,1,0:T(8,128)(2,1)S(1)} %collective-permute-done.12.refs_8_), channel_id=1, source_target_pairs={{0,8},{1,9},{2,10},{3,11},{4,12},{5,13},{6,14},{7,15},{8,0},{9,1},... | collective-permute-start | bytes 294920 | tf_op jit(solution)/shard_map/ppermute | solution.py:24
  15.1 4.6 %collective-permute-start.10 = (bf16[3,64,256]{2,1,0:T(8,128)(2,1)S(1)}, bf16[3,64,256]{2,1,0:T(8,128)(2,1)S(1)}, u32[]{:S(2)}, u32[]{:S(2)}) collective-permute-start(bf16[3,64,256]{2,1,0:T(8,128)(2,1)S(1)} %collective-permute-done.9.refs_4_), channel_id=1, source_target_pairs={{0,2},{1,3},{2,0},{3,1},{4,6},{5,7},{6,4},{7,5},{8,10},{9,11},{10,... | collective-permute-start | bytes 294920 | tf_op jit(solution)/shard_map/ppermute | solution.py:24
  16.6 7.4 %collective-permute-start.11 = (bf16[3,64,256]{2,1,0:T(8,128)(2,1)S(1)}, bf16[3,64,256]{2,1,0:T(8,128)(2,1)S(1)}, u32[]{:S(2)}, u32[]{:S(2)}) collective-permute-start(bf16[3,64,256]{2,1,0:T(8,128)(2,1)S(1)} %collective-permute-done.9.refs_4_), channel_id=1, source_target_pairs={{0,4},{1,5},{2,6},{3,7},{4,0},{5,1},{6,2},{7,3},{8,12},{9,13},{10,... | collective-permute-start | bytes 294920 | tf_op jit(solution)/shard_map/ppermute | solution.py:24
  18.1 7.5 %collective-permute-start.13 = (bf16[3,64,256]{2,1,0:T(8,128)(2,1)S(1)}, bf16[3,64,256]{2,1,0:T(8,128)(2,1)S(1)}, u32[]{:S(2)}, u32[]{:S(2)}) collective-permute-start(bf16[3,64,256]{2,1,0:T(8,128)(2,1)S(1)} %collective-permute-done.12.refs_8_), channel_id=1, source_target_pairs={{0,2},{1,3},{2,0},{3,1},{4,6},{5,7},{6,4},{7,5},{8,10},{9,11},{10,... | collective-permute-start | bytes 294920 | tf_op jit(solution)/shard_map/ppermute | solution.py:24
  19.7 6.4 %collective-permute-start.17 = (bf16[3,64,256]{2,1,0:T(8,128)(2,1)S(1)}, bf16[3,64,256]{2,1,0:T(8,128)(2,1)S(1)}, u32[]{:S(2)}, u32[]{:S(2)}) collective-permute-start(bf16[3,64,256]{2,1,0:T(8,128)(2,1)S(1)} %collective-permute-done.16.refs_12_), channel_id=1, source_target_pairs={{0,2},{1,3},{2,0},{3,1},{4,6},{5,7},{6,4},{7,5},{8,10},{9,11},{10,... | collective-permute-start | bytes 294920 | tf_op jit(solution)/shard_map/ppermute | solution.py:24
  22.0 5.0 %collective-permute-start.19 = (bf16[3,64,256]{2,1,0:T(8,128)(2,1)S(1)}, bf16[3,64,256]{2,1,0:T(8,128)(2,1)S(1)}, u32[]{:S(2)}, u32[]{:S(2)}) collective-permute-start(bf16[3,64,256]{2,1,0:T(8,128)(2,1)S(1)} %collective-permute-done.16.refs_12_), channel_id=1, source_target_pairs={{0,4},{1,5},{2,6},{3,7},{4,0},{5,1},{6,2},{7,3},{8,12},{9,13},{10,... | collective-permute-start | bytes 294920 | tf_op jit(solution)/shard_map/ppermute | solution.py:24
  23.6 5.8 %collective-permute-start.8 = (bf16[3,64,256]{2,1,0:T(8,128)(2,1)S(1)}, bf16[3,64,256]{2,1,0:T(8,128)(2,1)S(1)}, u32[]{:S(2)}, u32[]{:S(2)}) collective-permute-start(bf16[3,64,256]{2,1,0:T(8,128)(2,1)S(1)} %collective-permute-done.6.refs_1_), channel_id=1, source_target_pairs={{0,4},{1,5},{2,6},{3,7},{4,0},{5,1},{6,2},{7,3},{8,12},{9,13},{10,... | collective-permute-start | bytes 294920 | tf_op jit(solution)/shard_map/ppermute | solution.py:24
  24.0 6.0 %collective-permute-start.15 = (bf16[3,64,256]{2,1,0:T(8,128)(2,1)S(1)}, bf16[3,64,256]{2,1,0:T(8,128)(2,1)S(1)}, u32[]{:S(2)}, u32[]{:S(2)}) collective-permute-start(bf16[3,64,256]{2,1,0:T(8,128)(2,1)S(1)} %collective-permute-done.12.refs_8_), channel_id=1, source_target_pairs={{0,4},{1,5},{2,6},{3,7},{4,0},{5,1},{6,2},{7,3},{8,12},{9,13},{10,... | collective-permute-start | bytes 294920 | tf_op jit(solution)/shard_map/ppermute | solution.py:24
  25.6 4.6 %collective-permute-start.14 = (bf16[3,64,256]{2,1,0:T(8,128)(2,1)S(1)}, bf16[3,64,256]{2,1,0:T(8,128)(2,1)S(1)}, u32[]{:S(2)}, u32[]{:S(2)}) collective-permute-start(bf16[3,64,256]{2,1,0:T(8,128)(2,1)S(1)} %collective-permute-done.11.refs_6_), channel_id=1, source_target_pairs={{0,2},{1,3},{2,0},{3,1},{4,6},{5,7},{6,4},{7,5},{8,10},{9,11},{10,... | collective-permute-start | bytes 294920 | tf_op jit(solution)/shard_map/ppermute | solution.py:24
  27.0 4.6 %collective-permute-start.20 = (bf16[3,64,256]{2,1,0:T(8,128)(2,1)S(1)}, bf16[3,64,256]{2,1,0:T(8,128)(2,1)S(1)}, u32[]{:S(2)}, u32[]{:S(2)}) collective-permute-start(bf16[3,64,256]{2,1,0:T(8,128)(2,1)S(1)} %collective-permute-done.19.refs_14_), channel_id=1, source_target_pairs={{0,2},{1,3},{2,0},{3,1},{4,6},{5,7},{6,4},{7,5},{8,10},{9,11},{10,... | collective-permute-start | bytes 294920 | tf_op jit(solution)/shard_map/ppermute | solution.py:24
  27.7 4.6 %collective-permute-start.18 = (bf16[3,64,256]{2,1,0:T(8,128)(2,1)S(1)}, bf16[3,64,256]{2,1,0:T(8,128)(2,1)S(1)}, u32[]{:S(2)}, u32[]{:S(2)}) collective-permute-start(bf16[3,64,256]{2,1,0:T(8,128)(2,1)S(1)} %collective-permute-done.13.refs_9_), channel_id=1, source_target_pairs={{0,4},{1,5},{2,6},{3,7},{4,0},{5,1},{6,2},{7,3},{8,12},{9,13},{10,... | collective-permute-start | bytes 294920 | tf_op jit(solution)/shard_map/ppermute | solution.py:24
  35.5 6.6 %collective-permute-start.21 = (bf16[2,3,64,256]{3,2,1,0:T(8,128)(2,1)S(1)}, bf16[2,3,64,256]{3,2,1,0:T(8,128)(2,1)S(1)}, u32[]{:S(2)}, u32[]{:S(2)}) collective-permute-start(bf16[2,3,64,256]{3,2,1,0:T(8,128)(2,1)S(1)} %get-tuple-element.66), channel_id=1, source_target_pairs={{0,4},{1,5},{2,6},{3,7},{4,0},{5,1},{6,2},{7,3},{8,12},{9,13},{10,... | collective-permute-start | bytes 589832 | tf_op jit(solution)/shard_map/ppermute | solution.py:24
  36.5 7.1 %collective-permute-start.24 = (bf16[2,3,64,256]{3,2,1,0:T(8,128)(2,1)S(1)}, bf16[2,3,64,256]{3,2,1,0:T(8,128)(2,1)S(1)}, u32[]{:S(2)}, u32[]{:S(2)}) collective-permute-start(bf16[2,3,64,256]{3,2,1,0:T(8,128)(2,1)S(1)} %get-tuple-element.69), channel_id=1, source_target_pairs={{0,2},{1,3},{2,0},{3,1},{4,6},{5,7},{6,4},{7,5},{8,10},{9,11},{10,... | collective-permute-start | bytes 589832 | tf_op jit(solution)/shard_map/ppermute | solution.py:24
  38.5 7.8 %collective-permute-start.29 = (bf16[2,3,64,256]{3,2,1,0:T(8,128)(2,1)S(1)}, bf16[2,3,64,256]{3,2,1,0:T(8,128)(2,1)S(1)}, u32[]{:S(2)}, u32[]{:S(2)}) collective-permute-start(bf16[2,3,64,256]{3,2,1,0:T(8,128)(2,1)S(1)} %get-tuple-element.77), channel_id=1, source_target_pairs={{0,2},{1,3},{2,0},{3,1},{4,6},{5,7},{6,4},{7,5},{8,10},{9,11},{10,... | collective-permute-start | bytes 589832 | tf_op jit(solution)/shard_map/ppermute | solution.py:24
  42.1 4.7 %collective-permute-start.22 = (bf16[3,64,256]{2,1,0:T(8,128)(2,1)S(1)}, bf16[3,64,256]{2,1,0:T(8,128)(2,1)S(1)}, u32[]{:S(2)}, u32[]{:S(2)}) collective-permute-start(bf16[3,64,256]{2,1,0:T(8,128)(2,1)S(1)} %fusion.14), channel_id=1, source_target_pairs={{0,2},{1,3},{2,0},{3,1},{4,6},{5,7},{6,4},{7,5},{8,10},{9,11},{10,... | collective-permute-start | bytes 294920 | tf_op jit(solution)/shard_map/ppermute | solution.py:24
  43.7 9.1 %collective-permute-start.27 = (bf16[3,64,256]{2,1,0:T(8,128)(2,1)S(1)}, bf16[3,64,256]{2,1,0:T(8,128)(2,1)S(1)}, u32[]{:S(2)}, u32[]{:S(2)}) collective-permute-start(bf16[3,64,256]{2,1,0:T(8,128)(2,1)S(1)} %fusion.7), channel_id=1, source_target_pairs={{0,4},{1,5},{2,6},{3,7},{4,0},{5,1},{6,2},{7,3},{8,12},{9,13},{10,... | collective-permute-start | bytes 294920 | tf_op jit(solution)/shard_map/ppermute | solution.py:24
  46.2 6.6 %collective-permute-start.25 = (bf16[2,3,64,256]{3,2,1,0:T(8,128)(2,1)S(1)}, bf16[2,3,64,256]{3,2,1,0:T(8,128)(2,1)S(1)}, u32[]{:S(2)}, u32[]{:S(2)}) collective-permute-start(bf16[2,3,64,256]{3,2,1,0:T(8,128)(2,1)S(1)} %get-tuple-element.70), channel_id=1, source_target_pairs={{0,4},{1,5},{2,6},{3,7},{4,0},{5,1},{6,2},{7,3},{8,12},{9,13},{10,... | collective-permute-start | bytes 589832 | tf_op jit(solution)/shard_map/ppermute | solution.py:24
  46.8 9.9 %collective-permute-start.23 = (bf16[3,64,256]{2,1,0:T(8,128)(2,1)S(1)}, bf16[3,64,256]{2,1,0:T(8,128)(2,1)S(1)}, u32[]{:S(2)}, u32[]{:S(2)}) collective-permute-start(bf16[3,64,256]{2,1,0:T(8,128)(2,1)S(1)} %fusion.16), channel_id=1, source_target_pairs={{0,16},{1,17},{2,18},{3,19},{4,20},{5,21},{6,22},{7,23},{8,24},{9,... | collective-permute-start | bytes 294920 | tf_op jit(solution)/shard_map/ppermute | solution.py:24
  50.4 5.0 %collective-permute-start.30 = (bf16[3,64,256]{2,1,0:T(8,128)(2,1)S(1)}, bf16[3,64,256]{2,1,0:T(8,128)(2,1)S(1)}, u32[]{:S(2)}, u32[]{:S(2)}) collective-permute-start(bf16[3,64,256]{2,1,0:T(8,128)(2,1)S(1)} %fusion.4), channel_id=1, source_target_pairs={{0,4},{1,5},{2,6},{3,7},{4,0},{5,1},{6,2},{7,3},{8,12},{9,13},{10,... | collective-permute-start | bytes 294920 | tf_op jit(solution)/shard_map/ppermute | solution.py:24
  52.8 7.2 %collective-permute-start.28 = (bf16[3,64,256]{2,1,0:T(8,128)(2,1)S(1)}, bf16[3,64,256]{2,1,0:T(8,128)(2,1)S(1)}, u32[]{:S(2)}, u32[]{:S(2)}) collective-permute-start(bf16[3,64,256]{2,1,0:T(8,128)(2,1)S(1)} %fusion.9), channel_id=1, source_target_pairs={{0,24},{1,25},{2,26},{3,27},{4,28},{5,29},{6,30},{7,31},{8,16},{9,... | collective-permute-start | bytes 294920 | tf_op jit(solution)/shard_map/ppermute | solution.py:24
  55.1 5.2 %collective-permute-start.26 = (bf16[3,64,256]{2,1,0:T(8,128)(2,1)S(1)}, bf16[3,64,256]{2,1,0:T(8,128)(2,1)S(1)}, u32[]{:S(2)}, u32[]{:S(2)}) collective-permute-start(bf16[3,64,256]{2,1,0:T(8,128)(2,1)S(1)} %fusion.10), channel_id=1, source_target_pairs={{0,2},{1,3},{2,0},{3,1},{4,6},{5,7},{6,4},{7,5},{8,10},{9,11},{10,... | collective-permute-start | bytes 294920 | tf_op jit(solution)/shard_map/ppermute | solution.py:24
  55.4 5.9 %collective-permute-start.31 = (bf16[3,64,256]{2,1,0:T(8,128)(2,1)S(1)}, bf16[3,64,256]{2,1,0:T(8,128)(2,1)S(1)}, u32[]{:S(2)}, u32[]{:S(2)}) collective-permute-start(bf16[3,64,256]{2,1,0:T(8,128)(2,1)S(1)} %fusion.6), channel_id=1, source_target_pairs={{0,8},{1,9},{2,10},{3,11},{4,12},{5,13},{6,14},{7,15},{8,0},{9,1},... | collective-permute-start | bytes 294920 | tf_op jit(solution)/shard_map/ppermute | solution.py:24
  61.6 23.8 %copy-start = (bf16[1,256,1024]{2,1,0:T(8,128)(2,1)S(1)}, bf16[1,256,1024]{2,1,0:T(8,128)(2,1)}, u32[]{:S(2)}) copy-start(bf16[1,256,1024]{2,1,0:T(8,128)(2,1)} %param.14) | copy-start | bytes 1572868
  61.6 6.7 %collective-permute-start.38 = (bf16[3,64,256]{2,1,0:T(8,128)(2,1)S(1)}, bf16[3,64,256]{2,1,0:T(8,128)(2,1)S(1)}, u32[]{:S(2)}, u32[]{:S(2)}) collective-permute-start(bf16[3,64,256]{2,1,0:T(8,128)(2,1)S(1)} %get-tuple-element.94.refs_0_), channel_id=1, source_target_pairs={{0,16},{1,17},{2,18},{3,19},{4,20},{5,21},{6,22},{7,23},{8,24},{9,... | collective-permute-start | bytes 294920 | tf_op jit(solution)/shard_map/ppermute | solution.py:24
  63.0 5.7 %collective-permute-start.35 = (bf16[3,64,256]{2,1,0:T(8,128)(2,1)S(1)}, bf16[3,64,256]{2,1,0:T(8,128)(2,1)S(1)}, u32[]{:S(2)}, u32[]{:S(2)}) collective-permute-start(bf16[3,64,256]{2,1,0:T(8,128)(2,1)S(1)} %get-tuple-element.94.refs_0_), channel_id=1, source_target_pairs={{0,8},{1,9},{2,10},{3,11},{4,12},{5,13},{6,14},{7,15},{8,0},{9,1},... | collective-permute-start | bytes 294920 | tf_op jit(solution)/shard_map/ppermute | solution.py:24
  65.5 5.7 %collective-permute-start.33 = (bf16[3,64,256]{2,1,0:T(8,128)(2,1)S(1)}, bf16[3,64,256]{2,1,0:T(8,128)(2,1)S(1)}, u32[]{:S(2)}, u32[]{:S(2)}) collective-permute-start(bf16[3,64,256]{2,1,0:T(8,128)(2,1)S(1)} %get-tuple-element.94.refs_0_), channel_id=1, source_target_pairs={{0,4},{1,5},{2,6},{3,7},{4,0},{5,1},{6,2},{7,3},{8,12},{9,13},{10,... | collective-permute-start | bytes 294920 | tf_op jit(solution)/shard_map/ppermute | solution.py:24
  65.5 5.7 %collective-permute-start.32 = (bf16[3,64,256]{2,1,0:T(8,128)(2,1)S(1)}, bf16[3,64,256]{2,1,0:T(8,128)(2,1)S(1)}, u32[]{:S(2)}, u32[]{:S(2)}) collective-permute-start(bf16[3,64,256]{2,1,0:T(8,128)(2,1)S(1)} %get-tuple-element.94.refs_0_), channel_id=1, source_target_pairs={{0,2},{1,3},{2,0},{3,1},{4,6},{5,7},{6,4},{7,5},{8,10},{9,11},{10,... | collective-permute-start | bytes 294920 | tf_op jit(solution)/shard_map/ppermute | solution.py:24
  68.4 4.6 %collective-permute-start.42 = (bf16[3,64,256]{2,1,0:T(8,128)(2,1)S(1)}, bf16[3,64,256]{2,1,0:T(8,128)(2,1)S(1)}, u32[]{:S(2)}, u32[]{:S(2)}) collective-permute-start(bf16[3,64,256]{2,1,0:T(8,128)(2,1)S(1)} %collective-permute-done.38.refs_8_), channel_id=1, source_target_pairs={{0,8},{1,9},{2,10},{3,11},{4,12},{5,13},{6,14},{7,15},{8,0},{9,1},... | collective-permute-start | bytes 294920 | tf_op jit(solution)/shard_map/ppermute | solution.py:24
  68.7 5.5 %collective-permute-start.36 = (bf16[3,64,256]{2,1,0:T(8,128)(2,1)S(1)}, bf16[3,64,256]{2,1,0:T(8,128)(2,1)S(1)}, u32[]{:S(2)}, u32[]{:S(2)}) collective-permute-start(bf16[3,64,256]{2,1,0:T(8,128)(2,1)S(1)} %collective-permute-done.35.refs_4_), channel_id=1, source_target_pairs={{0,2},{1,3},{2,0},{3,1},{4,6},{5,7},{6,4},{7,5},{8,10},{9,11},{10,... | collective-permute-start | bytes 294920 | tf_op jit(solution)/shard_map/ppermute | solution.py:24
  71.1 5.5 %collective-permute-start.37 = (bf16[3,64,256]{2,1,0:T(8,128)(2,1)S(1)}, bf16[3,64,256]{2,1,0:T(8,128)(2,1)S(1)}, u32[]{:S(2)}, u32[]{:S(2)}) collective-permute-start(bf16[3,64,256]{2,1,0:T(8,128)(2,1)S(1)} %collective-permute-done.35.refs_4_), channel_id=1, source_target_pairs={{0,4},{1,5},{2,6},{3,7},{4,0},{5,1},{6,2},{7,3},{8,12},{9,13},{10,... | collective-permute-start | bytes 294920 | tf_op jit(solution)/shard_map/ppermute | solution.py:24
  72.3 5.7 %collective-permute-start.39 = (bf16[3,64,256]{2,1,0:T(8,128)(2,1)S(1)}, bf16[3,64,256]{2,1,0:T(8,128)(2,1)S(1)}, u32[]{:S(2)}, u32[]{:S(2)}) collective-permute-start(bf16[3,64,256]{2,1,0:T(8,128)(2,1)S(1)} %collective-permute-done.38.refs_8_), channel_id=1, source_target_pairs={{0,2},{1,3},{2,0},{3,1},{4,6},{5,7},{6,4},{7,5},{8,10},{9,11},{10,... | collective-permute-start | bytes 294920 | tf_op jit(solution)/shard_map/ppermute | solution.py:24
  74.2 6.6 %collective-permute-start.45 = (bf16[3,64,256]{2,1,0:T(8,128)(2,1)S(1)}, bf16[3,64,256]{2,1,0:T(8,128)(2,1)S(1)}, u32[]{:S(2)}, u32[]{:S(2)}) collective-permute-start(bf16[3,64,256]{2,1,0:T(8,128)(2,1)S(1)} %collective-permute-done.42.refs_12_), channel_id=1, source_target_pairs={{0,4},{1,5},{2,6},{3,7},{4,0},{5,1},{6,2},{7,3},{8,12},{9,13},{10,... | collective-permute-start | bytes 294920 | tf_op jit(solution)/shard_map/ppermute | solution.py:24
  74.4 4.6 %collective-permute-start.43 = (bf16[3,64,256]{2,1,0:T(8,128)(2,1)S(1)}, bf16[3,64,256]{2,1,0:T(8,128)(2,1)S(1)}, u32[]{:S(2)}, u32[]{:S(2)}) collective-permute-start(bf16[3,64,256]{2,1,0:T(8,128)(2,1)S(1)} %collective-permute-done.42.refs_12_), channel_id=1, source_target_pairs={{0,2},{1,3},{2,0},{3,1},{4,6},{5,7},{6,4},{7,5},{8,10},{9,11},{10,... | collective-permute-start | bytes 294920 | tf_op jit(solution)/shard_map/ppermute | solution.py:24
  75.9 5.3 %collective-permute-start.34 = (bf16[3,64,256]{2,1,0:T(8,128)(2,1)S(1)}, bf16[3,64,256]{2,1,0:T(8,128)(2,1)S(1)}, u32[]{:S(2)}, u32[]{:S(2)}) collective-permute-start(bf16[3,64,256]{2,1,0:T(8,128)(2,1)S(1)} %collective-permute-done.32.refs_1_), channel_id=1, source_target_pairs={{0,4},{1,5},{2,6},{3,7},{4,0},{5,1},{6,2},{7,3},{8,12},{9,13},{10,... | collective-permute-start | bytes 294920 | tf_op jit(solution)/shard_map/ppermute | solution.py:24
  76.6 5.0 %collective-permute-start.41 = (bf16[3,64,256]{2,1,0:T(8,128)(2,1)S(1)}, bf16[3,64,256]{2,1,0:T(8,128)(2,1)S(1)}, u32[]{:S(2)}, u32[]{:S(2)}) collective-permute-start(bf16[3,64,256]{2,1,0:T(8,128)(2,1)S(1)} %collective-permute-done.38.refs_8_), channel_id=1, source_target_pairs={{0,4},{1,5},{2,6},{3,7},{4,0},{5,1},{6,2},{7,3},{8,12},{9,13},{10,... | collective-permute-start | bytes 294920 | tf_op jit(solution)/shard_map/ppermute | solution.py:24
  78.0 4.6 %collective-permute-start.40 = (bf16[3,64,256]{2,1,0:T(8,128)(2,1)S(1)}, bf16[3,64,256]{2,1,0:T(8,128)(2,1)S(1)}, u32[]{:S(2)}, u32[]{:S(2)}) collective-permute-start(bf16[3,64,256]{2,1,0:T(8,128)(2,1)S(1)} %collective-permute-done.37.refs_6_), channel_id=1, source_target_pairs={{0,2},{1,3},{2,0},{3,1},{4,6},{5,7},{6,4},{7,5},{8,10},{9,11},{10,... | collective-permute-start | bytes 294920 | tf_op jit(solution)/shard_map/ppermute | solution.py:24
  79.0 6.5 %collective-permute-start.44 = (bf16[3,64,256]{2,1,0:T(8,128)(2,1)S(1)}, bf16[3,64,256]{2,1,0:T(8,128)(2,1)S(1)}, u32[]{:S(2)}, u32[]{:S(2)}) collective-permute-start(bf16[3,64,256]{2,1,0:T(8,128)(2,1)S(1)} %collective-permute-done.39.refs_9_), channel_id=1, source_target_pairs={{0,4},{1,5},{2,6},{3,7},{4,0},{5,1},{6,2},{7,3},{8,12},{9,13},{10,... | collective-permute-start | bytes 294920 | tf_op jit(solution)/shard_map/ppermute | solution.py:24
  80.8 4.6 %collective-permute-start.46 = (bf16[3,64,256]{2,1,0:T(8,128)(2,1)S(1)}, bf16[3,64,256]{2,1,0:T(8,128)(2,1)S(1)}, u32[]{:S(2)}, u32[]{:S(2)}) collective-permute-start(bf16[3,64,256]{2,1,0:T(8,128)(2,1)S(1)} %collective-permute-done.45.refs_14_), channel_id=1, source_target_pairs={{0,2},{1,3},{2,0},{3,1},{4,6},{5,7},{6,4},{7,5},{8,10},{9,11},{10,... | collective-permute-start | bytes 294920 | tf_op jit(solution)/shard_map/ppermute | solution.py:24
  86.2 1.6 %collective-permute-start.47 = (f32[3,3,32,256]{3,2,1,0:T(8,128)S(1)}, f32[3,3,32,256]{3,2,1,0:T(8,128)S(1)}, u32[]{:S(2)}, u32[]{:S(2)}) collective-permute-start(f32[3,3,32,256]{3,2,1,0:T(8,128)S(1)} %get-tuple-element.91), channel_id=1, source_target_pairs={{0,1},{1,0},{2,3},{3,2},{4,5},{5,4},{6,7},{7,6},{8,9},{9,8},{10,11... | collective-permute-start | bytes 884744 | tf_op jit(solution)/shard_map/ppermute | solution.py:24
  86.3 2.5 %collective-permute-start.48 = (bf16[256,1024]{1,0:T(8,128)(2,1)S(1)}, bf16[256,1024]{1,0:T(8,128)(2,1)S(1)}, u32[]{:S(2)}, u32[]{:S(2)}) collective-permute-start(bf16[256,1024]{1,0:T(8,128)(2,1)S(1)} %get-tuple-element.90), channel_id=1, source_target_pairs={{0,1},{1,0},{2,3},{3,2},{4,5},{5,4},{6,7},{7,6},{8,9},{9,8},{10,11... | collective-permute-start | bytes 1572872 | tf_op jit(solution)/shard_map/ppermute | solution.py:24

commit v16 on v15

--- a/solution.py
+++ b/solution.py
@@ -290,10 +290,10 @@
     theirs = hop(jnp.stack([partners(first), partners(second)]), CORE)
     other_y = hop(new_rows, CORE)
     other_live = hop(live, CORE)
+    their_master, other_x, other_c, other_y, other_live = lax.optimization_barrier(
+        (their_master, other_x, other_c, other_y, other_live)
+    )
     x_turned, c_turned = transposed(old_rows, other_x, old_cotangent, other_c)
-    their_master, other_y, other_live, x_turned, c_turned = lax.optimization_barrier(
-        (their_master, other_y, other_live, x_turned, c_turned)
-    )
     master_two = both_rows(mine(master), their_master)
     pieces = gather_chips(master_two.astype(jnp.bfloat16), theirs)
     *grads, matches = backward(

time: 89.8 us -> 89.2 us (level)
  transfers between devices with their start and end apart: 49 -> 49, of which waited for: 23 -> 22; matrix products, arithmetic and copies ran while one was open for 4% -> 4% of each run, Pallas kernels for 1% -> 1%
where the time goes in v16:
time: 89.2 us; the launch traced here: 89 us
  starting transfers between devices  52.7 us (59%)
  waiting for transfers between devices  24.5 us (27%)
  Pallas kernels  5.21 us (6%)
  local copies, waits for them, and re-layouts  2.92 us (3%)
  between operations  2.2 us (2%)
  other arithmetic  1.52 us (2%)
    ppermute x49, starting transfers between devices, hop(): lax.ppermute(block, 'dev', [(low, low ^ mask) for low in range(count)])  52.7 us
    ppermute x49, waiting for transfers between devices, hop(): lax.ppermute(block, 'dev', [(low, low ^ mask) for low in range(count)])  24.5 us
    pallas_call x1, Pallas kernels, backward(): pl.pallas_call(functools.partial(backward_kernel, count), out_shape=[one,...  3.18 us
    squeeze x2, local copies, waits for them, and re-layouts, mine(): return lax.dynamic_index_in_dim(state, core, 0, keepdims=False)  2.01 us
  transfers between devices with their start and end apart: 49, of which 22 were waited for; matrix products, arithmetic and copies ran while one was open for 4% of the time, Pallas kernels for 1%

profile of v16, /device:TPU:0, one launch (start us, length us, event | category | flops | bytes accessed | tf_op | source)
XLA Modules:
  0.0 89.0 jit_solution(17256808846577199822)
XLA Ops:
  0.7 0.5 collective-permute-start.1
  1.2 0.4 collective-permute-start.3
  1.8 1.0 %dynamic-slice_bitcast_fusion.4 = (f32[3,32,256]{2,1,0:T(8,128)S(1)}, f32[3,32,256]{2,1,0:T(8,128)S(1)}) fusion(f32[2,3,32,256]{3,2,1,0:T(8,128)} %param.9, s32[]{:T(128)S(6)} %select_n.47, s32[]{:T(128)S(6)} %select_n.48), kind=kLoop, calls=%fused_computation.52 | loop fusion | bytes 393224 | tf_op jit(solution)/shard_map/jit(dynamic_index_in_dim)/squeeze | solution.py:277
  2.7 0.5 collective-permute-start
  3.2 1.1 %dynamic-slice_bitcast_fusion.1 = (f32[3,32,256]{2,1,0:T(8,128)S(1)}, f32[1,3,32,256]{3,2,1,0:T(8,128)S(1)}, f32[1,3,32,256]{3,2,1,0:T(8,128)S(1)}, f32[3,32,256]{2,1,0:T(8,128)S(1)}) fusion(f32[2,3,32,256]{3,2,1,0:T(8,128)} %param.11, s32[]{:T(128)S(6)} %select_n.47, s32[]{:T(128)S(6)} %select_n.48, f32[2,3,32,256]{3,2,1,0:T(8,128)} %param.10), kind=kLoop, calls=%fused_computation.48 | loop fusion | bytes 786440 | tf_op jit(solution)/shard_map/jit(dynamic_index_in_dim)/squeeze | solution.py:277
  4.5 4.1 %collective-permute-start.12 = (bf16[3,64,256]{2,1,0:T(8,128)(2,1)S(1)}, bf16[3,64,256]{2,1,0:T(8,128)(2,1)S(1)}, u32[]{:S(2)}, u32[]{:S(2)}) collective-permute-start(bf16[3,64,256]{2,1,0:T(8,128)(2,1)S(1)} %fusion.17.refs_0_), channel_id=1, source_target_pairs={{0,16},{1,17},{2,18},{3,19},{4,20},{5,21},{6,22},{7,23},{8,24},{9,... | collective-permute-start | bytes 294920 | tf_op jit(solution)/shard_map/ppermute | solution.py:24
  8.6 1.6 %collective-permute-start.9 = (bf16[3,64,256]{2,1,0:T(8,128)(2,1)S(1)}, bf16[3,64,256]{2,1,0:T(8,128)(2,1)S(1)}, u32[]{:S(2)}, u32[]{:S(2)}) collective-permute-start(bf16[3,64,256]{2,1,0:T(8,128)(2,1)S(1)} %fusion.17.refs_0_), channel_id=1, source_target_pairs={{0,8},{1,9},{2,10},{3,11},{4,12},{5,13},{6,14},{7,15},{8,0},{9,1},... | collective-permute-start | bytes 294920 | tf_op jit(solution)/shard_map/ppermute | solution.py:24
  10.2 1.5 %collective-permute-start.6 = (bf16[3,64,256]{2,1,0:T(8,128)(2,1)S(1)}, bf16[3,64,256]{2,1,0:T(8,128)(2,1)S(1)}, u32[]{:S(2)}, u32[]{:S(2)}) collective-permute-start(bf16[3,64,256]{2,1,0:T(8,128)(2,1)S(1)} %fusion.17.refs_0_), channel_id=1, source_target_pairs={{0,2},{1,3},{2,0},{3,1},{4,6},{5,7},{6,4},{7,5},{8,10},{9,11},{10,... | collective-permute-start | bytes 294920 | tf_op jit(solution)/shard_map/ppermute | solution.py:24
  11.7 1.5 %collective-permute-start.7 = (bf16[3,64,256]{2,1,0:T(8,128)(2,1)S(1)}, bf16[3,64,256]{2,1,0:T(8,128)(2,1)S(1)}, u32[]{:S(2)}, u32[]{:S(2)}) collective-permute-start(bf16[3,64,256]{2,1,0:T(8,128)(2,1)S(1)} %fusion.17.refs_0_), channel_id=1, source_target_pairs={{0,4},{1,5},{2,6},{3,7},{4,0},{5,1},{6,2},{7,3},{8,12},{9,13},{10,... | collective-permute-start | bytes 294920 | tf_op jit(solution)/shard_map/ppermute | solution.py:24
  13.2 0.7 collective-permute-done.12.refs_8_
  13.9 0.6 collective-permute-start.16
  14.5 1.5 %collective-permute-start.10 = (bf16[3,64,256]{2,1,0:T(8,128)(2,1)S(1)}, bf16[3,64,256]{2,1,0:T(8,128)(2,1)S(1)}, u32[]{:S(2)}, u32[]{:S(2)}) collective-permute-start(bf16[3,64,256]{2,1,0:T(8,128)(2,1)S(1)} %collective-permute-done.9.refs_4_), channel_id=1, source_target_pairs={{0,2},{1,3},{2,0},{3,1},{4,6},{5,7},{6,4},{7,5},{8,10},{9,11},{10,... | collective-permute-start | bytes 294920 | tf_op jit(solution)/shard_map/ppermute | solution.py:24
  16.0 1.5 %collective-permute-start.11 = (bf16[3,64,256]{2,1,0:T(8,128)(2,1)S(1)}, bf16[3,64,256]{2,1,0:T(8,128)(2,1)S(1)}, u32[]{:S(2)}, u32[]{:S(2)}) collective-permute-start(bf16[3,64,256]{2,1,0:T(8,128)(2,1)S(1)} %collective-permute-done.9.refs_4_), channel_id=1, source_target_pairs={{0,4},{1,5},{2,6},{3,7},{4,0},{5,1},{6,2},{7,3},{8,12},{9,13},{10,... | collective-permute-start | bytes 294920 | tf_op jit(solution)/shard_map/ppermute | solution.py:24
  17.5 0.5 collective-permute-start.13
  18.0 0.4 collective-permute-done.16.refs_12_
  18.5 0.6 collective-permute-done.10.refs_5_
  19.1 2.3 %collective-permute-start.17 = (bf16[3,64,256]{2,1,0:T(8,128)(2,1)S(1)}, bf16[3,64,256]{2,1,0:T(8,128)(2,1)S(1)}, u32[]{:S(2)}, u32[]{:S(2)}) collective-permute-start(bf16[3,64,256]{2,1,0:T(8,128)(2,1)S(1)} %collective-permute-done.16.refs_12_), channel_id=1, source_target_pairs={{0,2},{1,3},{2,0},{3,1},{4,6},{5,7},{6,4},{7,5},{8,10},{9,11},{10,... | collective-permute-start | bytes 294920 | tf_op jit(solution)/shard_map/ppermute | solution.py:24
  21.4 1.6 %collective-permute-start.19 = (bf16[3,64,256]{2,1,0:T(8,128)(2,1)S(1)}, bf16[3,64,256]{2,1,0:T(8,128)(2,1)S(1)}, u32[]{:S(2)}, u32[]{:S(2)}) collective-permute-start(bf16[3,64,256]{2,1,0:T(8,128)(2,1)S(1)} %collective-permute-done.16.refs_12_), channel_id=1, source_target_pairs={{0,4},{1,5},{2,6},{3,7},{4,0},{5,1},{6,2},{7,3},{8,12},{9,13},{10,... | collective-permute-start | bytes 294920 | tf_op jit(solution)/shard_map/ppermute | solution.py:24
  23.0 0.4 collective-permute-start.8
  23.4 1.6 %collective-permute-start.15 = (bf16[3,64,256]{2,1,0:T(8,128)(2,1)S(1)}, bf16[3,64,256]{2,1,0:T(8,128)(2,1)S(1)}, u32[]{:S(2)}, u32[]{:S(2)}) collective-permute-start(bf16[3,64,256]{2,1,0:T(8,128)(2,1)S(1)} %collective-permute-done.12.refs_8_), channel_id=1, source_target_pairs={{0,4},{1,5},{2,6},{3,7},{4,0},{5,1},{6,2},{7,3},{8,12},{9,13},{10,... | collective-permute-start | bytes 294920 | tf_op jit(solution)/shard_map/ppermute | solution.py:24
  25.0 0.5 collective-permute-start.14
  25.5 0.9 collective-permute-done.19.refs_14_
  26.4 0.7 collective-permute-start.20
  27.1 1.0 %collective-permute-start.18 = (bf16[3,64,256]{2,1,0:T(8,128)(2,1)S(1)}, bf16[3,64,256]{2,1,0:T(8,128)(2,1)S(1)}, u32[]{:S(2)}, u32[]{:S(2)}) collective-permute-start(bf16[3,64,256]{2,1,0:T(8,128)(2,1)S(1)} %collective-permute-done.13.refs_9_), channel_id=1, source_target_pairs={{0,4},{1,5},{2,6},{3,7},{4,0},{5,1},{6,2},{7,3},{8,12},{9,13},{10,... | collective-permute-start | bytes 294920 | tf_op jit(solution)/shard_map/ppermute | solution.py:24
  28.8 0.6 transpose_rows.1
  29.6 1.3 %collective-permute-done.20.refs_15_ = bf16[3,64,256]{2,1,0:T(8,128)(2,1)S(1)} collective-permute-done((bf16[3,64,256]{2,1,0:T(8,128)(2,1)S(1)}, bf16[3,64,256]{2,1,0:T(8,128)(2,1)S(1)}, u32[]{:S(2)}, u32[]{:S(2)}) %collective-permute-start.20) | collective-permute-done | bytes 98336 | tf_op jit(solution)/shard_map/ppermute | solution.py:24
  31.0 0.7 collective-permute-done.18.refs_11_
  31.7 3.2 %slot_gradients.1 = (bf16[3,64,256]{2,1,0:T(8,128)(2,1)S(1)}, bf16[3,64,256]{2,1,0:T(8,128)(2,1)S(1)}, bf16[2,3,64,256]{3,2,1,0:T(8,128)(2,1)S(1)}, bf16[3,64,25...) custom-call(s32[1,32]{1,0:T(1,128)S(1)} %bitcast.86, ...), custom_call_target="tpu_custom_call" | custom-call | flops 1610612736 | bytes 7340032 | tf_op jit(solution)/shard_map/slot_gradients/pallas_call | solution.py:160
  34.9 1.0 %collective-permute-start.21 = (bf16[2,3,64,256]{3,2,1,0:T(8,128)(2,1)S(1)}, bf16[2,3,64,256]{3,2,1,0:T(8,128)(2,1)S(1)}, u32[]{:S(2)}, u32[]{:S(2)}) collective-permute-start(bf16[2,3,64,256]{3,2,1,0:T(8,128)(2,1)S(1)} %get-tuple-element.66), channel_id=1, source_target_pairs={{0,4},{1,5},{2,6},{3,7},{4,0},{5,1},{6,2},{7,3},{8,12},{9,13},{10,... | collective-permute-start | bytes 589832 | tf_op jit(solution)/shard_map/ppermute | solution.py:24
  35.9 2.0 %collective-permute-start.24 = (bf16[2,3,64,256]{3,2,1,0:T(8,128)(2,1)S(1)}, bf16[2,3,64,256]{3,2,1,0:T(8,128)(2,1)S(1)}, u32[]{:S(2)}, u32[]{:S(2)}) collective-permute-start(bf16[2,3,64,256]{3,2,1,0:T(8,128)(2,1)S(1)} %get-tuple-element.69), channel_id=1, source_target_pairs={{0,2},{1,3},{2,0},{3,1},{4,6},{5,7},{6,4},{7,5},{8,10},{9,11},{10,... | collective-permute-start | bytes 589832 | tf_op jit(solution)/shard_map/ppermute | solution.py:24
  37.9 3.5 %collective-permute-done.21 = bf16[2,3,64,256]{3,2,1,0:T(8,128)(2,1)S(1)} collective-permute-done((bf16[2,3,64,256]{3,2,1,0:T(8,128)(2,1)S(1)}, bf16[2,3,64,256]{3,2,1,0:T(8,128)(2,1)S(1)}, u32[]{:S(2)}, u32[]{:S(2)}) %collective-permute-start.21) | collective-permute-done | bytes 196640 | tf_op jit(solution)/shard_map/ppermute | solution.py:24
  41.5 1.5 %collective-permute-start.22 = (bf16[3,64,256]{2,1,0:T(8,128)(2,1)S(1)}, bf16[3,64,256]{2,1,0:T(8,128)(2,1)S(1)}, u32[]{:S(2)}, u32[]{:S(2)}) collective-permute-start(bf16[3,64,256]{2,1,0:T(8,128)(2,1)S(1)} %fusion.14), channel_id=1, source_target_pairs={{0,2},{1,3},{2,0},{3,1},{4,6},{5,7},{6,4},{7,5},{8,10},{9,11},{10,... | collective-permute-start | bytes 294920 | tf_op jit(solution)/shard_map/ppermute | solution.py:24
  43.0 2.5 %collective-permute-start.27 = (bf16[3,64,256]{2,1,0:T(8,128)(2,1)S(1)}, bf16[3,64,256]{2,1,0:T(8,128)(2,1)S(1)}, u32[]{:S(2)}, u32[]{:S(2)}) collective-permute-start(bf16[3,64,256]{2,1,0:T(8,128)(2,1)S(1)} %fusion.7), channel_id=1, source_target_pairs={{0,4},{1,5},{2,6},{3,7},{4,0},{5,1},{6,2},{7,3},{8,12},{9,13},{10,... | collective-permute-start | bytes 294920 | tf_op jit(solution)/shard_map/ppermute | solution.py:24
  45.7 0.5 collective-permute-done.22
  46.2 3.5 %collective-permute-start.23 = (bf16[3,64,256]{2,1,0:T(8,128)(2,1)S(1)}, bf16[3,64,256]{2,1,0:T(8,128)(2,1)S(1)}, u32[]{:S(2)}, u32[]{:S(2)}) collective-permute-start(bf16[3,64,256]{2,1,0:T(8,128)(2,1)S(1)} %fusion.16), channel_id=1, source_target_pairs={{0,16},{1,17},{2,18},{3,19},{4,20},{5,21},{6,22},{7,23},{8,24},{9,... | collective-permute-start | bytes 294920 | tf_op jit(solution)/shard_map/ppermute | solution.py:24
  49.7 2.4 %collective-permute-start.30 = (bf16[3,64,256]{2,1,0:T(8,128)(2,1)S(1)}, bf16[3,64,256]{2,1,0:T(8,128)(2,1)S(1)}, u32[]{:S(2)}, u32[]{:S(2)}) collective-permute-start(bf16[3,64,256]{2,1,0:T(8,128)(2,1)S(1)} %fusion.4), channel_id=1, source_target_pairs={{0,4},{1,5},{2,6},{3,7},{4,0},{5,1},{6,2},{7,3},{8,12},{9,13},{10,... | collective-permute-start | bytes 294920 | tf_op jit(solution)/shard_map/ppermute | solution.py:24
  52.2 2.3 %collective-permute-start.28 = (bf16[3,64,256]{2,1,0:T(8,128)(2,1)S(1)}, bf16[3,64,256]{2,1,0:T(8,128)(2,1)S(1)}, u32[]{:S(2)}, u32[]{:S(2)}) collective-permute-start(bf16[3,64,256]{2,1,0:T(8,128)(2,1)S(1)} %fusion.9), channel_id=1, source_target_pairs={{0,24},{1,25},{2,26},{3,27},{4,28},{5,29},{6,30},{7,31},{8,16},{9,... | collective-permute-start | bytes 294920 | tf_op jit(solution)/shard_map/ppermute | solution.py:24
  54.8 0.7 collective-permute-start.31
  56.1 3.3 %collective-permute-done.28 = bf16[3,64,256]{2,1,0:T(8,128)(2,1)S(1)} collective-permute-done((bf16[3,64,256]{2,1,0:T(8,128)(2,1)S(1)}, bf16[3,64,256]{2,1,0:T(8,128)(2,1)S(1)}, u32[]{:S(2)}, u32[]{:S(2)}) %collective-permute-start.28) | collective-permute-done | bytes 98336 | tf_op jit(solution)/shard_map/ppermute | solution.py:24
  59.7 1.0 %collective-permute-done.31 = bf16[3,64,256]{2,1,0:T(8,128)(2,1)S(1)} collective-permute-done((bf16[3,64,256]{2,1,0:T(8,128)(2,1)S(1)}, bf16[3,64,256]{2,1,0:T(8,128)(2,1)S(1)}, u32[]{:S(2)}, u32[]{:S(2)}) %collective-permute-start.31) | collective-permute-done | bytes 98336 | tf_op jit(solution)/shard_map/ppermute | solution.py:24
  61.0 1.4 %collective-permute-start.38 = (bf16[3,64,256]{2,1,0:T(8,128)(2,1)S(1)}, bf16[3,64,256]{2,1,0:T(8,128)(2,1)S(1)}, u32[]{:S(2)}, u32[]{:S(2)}) collective-permute-start(bf16[3,64,256]{2,1,0:T(8,128)(2,1)S(1)} %get-tuple-element.94.refs_0_), channel_id=1, source_target_pairs={{0,16},{1,17},{2,18},{3,19},{4,20},{5,21},{6,22},{7,23},{8,24},{9,... | collective-permute-start | bytes 294920 | tf_op jit(solution)/shard_map/ppermute | solution.py:24
  62.4 2.5 %collective-permute-start.35 = (bf16[3,64,256]{2,1,0:T(8,128)(2,1)S(1)}, bf16[3,64,256]{2,1,0:T(8,128)(2,1)S(1)}, u32[]{:S(2)}, u32[]{:S(2)}) collective-permute-start(bf16[3,64,256]{2,1,0:T(8,128)(2,1)S(1)} %get-tuple-element.94.refs_0_), channel_id=1, source_target_pairs={{0,8},{1,9},{2,10},{3,11},{4,12},{5,13},{6,14},{7,15},{8,0},{9,1},... | collective-permute-start | bytes 294920 | tf_op jit(solution)/shard_map/ppermute | solution.py:24
  64.9 1.1 %collective-permute-start.32 = (bf16[3,64,256]{2,1,0:T(8,128)(2,1)S(1)}, bf16[3,64,256]{2,1,0:T(8,128)(2,1)S(1)}, u32[]{:S(2)}, u32[]{:S(2)}) collective-permute-start(bf16[3,64,256]{2,1,0:T(8,128)(2,1)S(1)} %get-tuple-element.94.refs_0_), channel_id=1, source_target_pairs={{0,2},{1,3},{2,0},{3,1},{4,6},{5,7},{6,4},{7,5},{8,10},{9,11},{10,... | collective-permute-start | bytes 294920 | tf_op jit(solution)/shard_map/ppermute | solution.py:24
  65.9 1.8 %collective-permute-done.38.refs_8_ = bf16[3,64,256]{2,1,0:T(8,128)(2,1)S(1)} collective-permute-done((bf16[3,64,256]{2,1,0:T(8,128)(2,1)S(1)}, bf16[3,64,256]{2,1,0:T(8,128)(2,1)S(1)}, u32[]{:S(2)}, u32[]{:S(2)}) %collective-permute-start.38) | collective-permute-done | bytes 98336 | tf_op jit(solution)/shard_map/ppermute | solution.py:24
  68.1 0.6 collective-permute-start.36
  68.7 1.9 %collective-permute-done.33.refs_2_ = bf16[3,64,256]{2,1,0:T(8,128)(2,1)S(1)} collective-permute-done((bf16[3,64,256]{2,1,0:T(8,128)(2,1)S(1)}, bf16[3,64,256]{2,1,0:T(8,128)(2,1)S(1)}, u32[]{:S(2)}, u32[]{:S(2)}) %collective-permute-start.33) | collective-permute-done | bytes 98336 | tf_op jit(solution)/shard_map/ppermute | solution.py:24
  70.6 1.1 %collective-permute-start.37 = (bf16[3,64,256]{2,1,0:T(8,128)(2,1)S(1)}, bf16[3,64,256]{2,1,0:T(8,128)(2,1)S(1)}, u32[]{:S(2)}, u32[]{:S(2)}) collective-permute-start(bf16[3,64,256]{2,1,0:T(8,128)(2,1)S(1)} %collective-permute-done.35.refs_4_), channel_id=1, source_target_pairs={{0,4},{1,5},{2,6},{3,7},{4,0},{5,1},{6,2},{7,3},{8,12},{9,13},{10,... | collective-permute-start | bytes 294920 | tf_op jit(solution)/shard_map/ppermute | solution.py:24
  71.8 0.6 collective-permute-done.42.refs_12_
  72.4 1.2 %collective-permute-done.36.refs_5_ = bf16[3,64,256]{2,1,0:T(8,128)(2,1)S(1)} collective-permute-done((bf16[3,64,256]{2,1,0:T(8,128)(2,1)S(1)}, bf16[3,64,256]{2,1,0:T(8,128)(2,1)S(1)}, u32[]{:S(2)}, u32[]{:S(2)}) %collective-permute-start.36) | collective-permute-done | bytes 98336 | tf_op jit(solution)/shard_map/ppermute | solution.py:24
  73.8 1.4 %collective-permute-start.43 = (bf16[3,64,256]{2,1,0:T(8,128)(2,1)S(1)}, bf16[3,64,256]{2,1,0:T(8,128)(2,1)S(1)}, u32[]{:S(2)}, u32[]{:S(2)}) collective-permute-start(bf16[3,64,256]{2,1,0:T(8,128)(2,1)S(1)} %collective-permute-done.42.refs_12_), channel_id=1, source_target_pairs={{0,2},{1,3},{2,0},{3,1},{4,6},{5,7},{6,4},{7,5},{8,10},{9,11},{10,... | collective-permute-start | bytes 294920 | tf_op jit(solution)/shard_map/ppermute | solution.py:24
  75.3 0.7 collective-permute-start.34
  76.0 1.4 %collective-permute-start.41 = (bf16[3,64,256]{2,1,0:T(8,128)(2,1)S(1)}, bf16[3,64,256]{2,1,0:T(8,128)(2,1)S(1)}, u32[]{:S(2)}, u32[]{:S(2)}) collective-permute-start(bf16[3,64,256]{2,1,0:T(8,128)(2,1)S(1)} %collective-permute-done.38.refs_8_), channel_id=1, source_target_pairs={{0,4},{1,5},{2,6},{3,7},{4,0},{5,1},{6,2},{7,3},{8,12},{9,13},{10,... | collective-permute-start | bytes 294920 | tf_op jit(solution)/shard_map/ppermute | solution.py:24
  77.4 0.6 collective-permute-start.40
  77.9 0.4 collective-permute-done.43.refs_13_
  78.4 1.8 %collective-permute-start.44 = (bf16[3,64,256]{2,1,0:T(8,128)(2,1)S(1)}, bf16[3,64,256]{2,1,0:T(8,128)(2,1)S(1)}, u32[]{:S(2)}, u32[]{:S(2)}) collective-permute-start(bf16[3,64,256]{2,1,0:T(8,128)(2,1)S(1)} %collective-permute-done.39.refs_9_), channel_id=1, source_target_pairs={{0,4},{1,5},{2,6},{3,7},{4,0},{5,1},{6,2},{7,3},{8,12},{9,13},{10,... | collective-permute-start | bytes 294920 | tf_op jit(solution)/shard_map/ppermute | solution.py:24
  80.5 0.5 collective-permute-done.41.refs_10_
  81.0 1.0 %collective-permute-done.40.refs_7_ = bf16[3,64,256]{2,1,0:T(8,128)(2,1)S(1)} collective-permute-done((bf16[3,64,256]{2,1,0:T(8,128)(2,1)S(1)}, bf16[3,64,256]{2,1,0:T(8,128)(2,1)S(1)}, u32[]{:S(2)}, u32[]{:S(2)}) %collective-permute-start.40) | collective-permute-done | bytes 98336 | tf_op jit(solution)/shard_map/ppermute | solution.py:24
  82.0 2.8 %collective-permute-done.46.refs_15_ = bf16[3,64,256]{2,1,0:T(8,128)(2,1)S(1)} collective-permute-done((bf16[3,64,256]{2,1,0:T(8,128)(2,1)S(1)}, bf16[3,64,256]{2,1,0:T(8,128)(2,1)S(1)}, u32[]{:S(2)}, u32[]{:S(2)}) %collective-permute-start.46) | collective-permute-done | bytes 98336 | tf_op jit(solution)/shard_map/ppermute | solution.py:24
  84.8 0.8 other_outputs.1
  85.7 0.5 collective-permute-start.48
  86.2 0.7 own_outputs.1
  86.8 0.4 collective-permute-done.47
  87.3 0.8 slice_bitcast_fusion
  88.1 0.8 select_bitcast_fusion
  (68 shorter events, 3.1 us)
Async XLA Ops:
  0.6 28.1 %copy-start.1 = (bf16[1,256,1024]{2,1,0:T(8,128)(2,1)S(1)}, bf16[1,256,1024]{2,1,0:T(8,128)(2,1)}, u32[]{:S(2)}) copy-start(bf16[1,256,1024]{2,1,0:T(8,128)(2,1)} %param.12) | copy-start | bytes 1572868
  0.6 28.1 %copy-start.2 = (bf16[1,256,1024]{2,1,0:T(8,128)(2,1)S(1)}, bf16[1,256,1024]{2,1,0:T(8,128)(2,1)}, u32[]{:S(2)}) copy-start(bf16[1,256,1024]{2,1,0:T(8,128)(2,1)} %param.13) | copy-start | bytes 1572868
  0.7 3.8 %collective-permute-start.1 = (bf16[256,1024]{1,0:T(8,128)(2,1)}, bf16[256,1024]{1,0:T(8,128)(2,1)S(1)}, u32[]{:S(2)}, u32[]{:S(2)}) collective-permute-start(bf16[256,1024]{1,0:T(8,128)(2,1)} %bitcast.80), channel_id=1, source_target_pairs={{0,1},{1,0},{2,3},{3,2},{4,5},{5,4},{6,7},{7,6},{8,9},{9,8},{10,11... | collective-permute-start | bytes 1572872 | tf_op jit(solution)/shard_map/ppermute | solution.py:24
  1.2 3.3 %collective-permute-start.2 = (bf16[256,1024]{1,0:T(8,128)(2,1)}, bf16[256,1024]{1,0:T(8,128)(2,1)S(1)}, u32[]{:S(2)}, u32[]{:S(2)}) collective-permute-start(bf16[256,1024]{1,0:T(8,128)(2,1)} %bitcast.83), channel_id=1, source_target_pairs={{0,1},{1,0},{2,3},{3,2},{4,5},{5,4},{6,7},{7,6},{8,9},{9,8},{10,11... | collective-permute-start | bytes 1572872 | tf_op jit(solution)/shard_map/ppermute | solution.py:24
  1.2 3.2 %collective-permute-start.3 = (bf16[256,1024]{1,0:T(8,128)(2,1)}, bf16[256,1024]{1,0:T(8,128)(2,1)S(1)}, u32[]{:S(2)}, u32[]{:S(2)}) collective-permute-start(bf16[256,1024]{1,0:T(8,128)(2,1)} %bitcast.77), channel_id=1, source_target_pairs={{0,1},{1,0},{2,3},{3,2},{4,5},{5,4},{6,7},{7,6},{8,9},{9,8},{10,11... | collective-permute-start | bytes 1572872 | tf_op jit(solution)/shard_map/ppermute | solution.py:24
  1.7 2.6 %collective-permute-start.4 = (s32[1]{0:T(128)}, s32[1]{0:T(128)}, u32[]{:S(2)}, u32[]{:S(2)}) collective-permute-start(s32[1]{0:T(128)} %param.17), channel_id=1, source_target_pairs={{0,1},{1,0},{2,3},{3,2},{4,5},{5,4},{6,7},{7,6},{8,9},{9,8},{10,11... | collective-permute-start | bytes 20 | tf_op jit(solution)/shard_map/ppermute | solution.py:24
  2.7 1.8 %collective-permute-start = (f32[3,32,256]{2,1,0:T(8,128)S(1)}, f32[3,32,256]{2,1,0:T(8,128)S(1)}, u32[]{:S(2)}, u32[]{:S(2)}) collective-permute-start(f32[3,32,256]{2,1,0:T(8,128)S(1)} %get-tuple-element.109), channel_id=1, source_target_pairs={{0,1},{1,0},{2,3},{3,2},{4,5},{5,4},{6,7},{7,6},{8,9},{9,8},{10,11... | collective-permute-start | bytes 294920 | tf_op jit(solution)/shard_map/ppermute | solution.py:24
  4.3 27.4 %copy-start.3 = (s32[32]{0:T(128)S(1)}, s32[32]{0:T(128)}, u32[]{:S(2)}) copy-start(s32[32]{0:T(128)} %param.15) | copy-start | bytes 388
  4.3 27.4 %copy-start.4 = (s32[32]{0:T(128)S(1)}, s32[32]{0:T(128)}, u32[]{:S(2)}) copy-start(s32[32]{0:T(128)} %param.16) | copy-start | bytes 388
  4.3 8.9 %collective-permute-start.5 = (f32[2,3,32,256]{3,2,1,0:T(8,128)S(1)}, f32[2,3,32,256]{3,2,1,0:T(8,128)S(1)}, u32[]{:S(2)}, u32[]{:S(2)}) collective-permute-start(f32[2,3,32,256]{3,2,1,0:T(8,128)S(1)} %pad_maximum_fusion.1), channel_id=1, source_target_pairs={{0,1},{1,0},{2,3},{3,2},{4,5},{5,4},{6,7},{7,6},{8,9},{9,8},{10,11... | collective-permute-start | bytes 589832 | tf_op jit(solution)/shard_map/ppermute | solution.py:24
  4.5 9.3 %collective-permute-start.12 = (bf16[3,64,256]{2,1,0:T(8,128)(2,1)S(1)}, bf16[3,64,256]{2,1,0:T(8,128)(2,1)S(1)}, u32[]{:S(2)}, u32[]{:S(2)}) collective-permute-start(bf16[3,64,256]{2,1,0:T(8,128)(2,1)S(1)} %fusion.17.refs_0_), channel_id=1, source_target_pairs={{0,16},{1,17},{2,18},{3,19},{4,20},{5,21},{6,22},{7,23},{8,24},{9,... | collective-permute-start | bytes 294920 | tf_op jit(solution)/shard_map/ppermute | solution.py:24
  8.6 5.9 %collective-permute-start.9 = (bf16[3,64,256]{2,1,0:T(8,128)(2,1)S(1)}, bf16[3,64,256]{2,1,0:T(8,128)(2,1)S(1)}, u32[]{:S(2)}, u32[]{:S(2)}) collective-permute-start(bf16[3,64,256]{2,1,0:T(8,128)(2,1)S(1)} %fusion.17.refs_0_), channel_id=1, source_target_pairs={{0,8},{1,9},{2,10},{3,11},{4,12},{5,13},{6,14},{7,15},{8,0},{9,1},... | collective-permute-start | bytes 294920 | tf_op jit(solution)/shard_map/ppermute | solution.py:24
  10.2 5.8 %collective-permute-start.6 = (bf16[3,64,256]{2,1,0:T(8,128)(2,1)S(1)}, bf16[3,64,256]{2,1,0:T(8,128)(2,1)S(1)}, u32[]{:S(2)}, u32[]{:S(2)}) collective-permute-start(bf16[3,64,256]{2,1,0:T(8,128)(2,1)S(1)} %fusion.17.refs_0_), channel_id=1, source_target_pairs={{0,2},{1,3},{2,0},{3,1},{4,6},{5,7},{6,4},{7,5},{8,10},{9,11},{10,... | collective-permute-start | bytes 294920 | tf_op jit(solution)/shard_map/ppermute | solution.py:24
  11.7 5.8 %collective-permute-start.7 = (bf16[3,64,256]{2,1,0:T(8,128)(2,1)S(1)}, bf16[3,64,256]{2,1,0:T(8,128)(2,1)S(1)}, u32[]{:S(2)}, u32[]{:S(2)}) collective-permute-start(bf16[3,64,256]{2,1,0:T(8,128)(2,1)S(1)} %fusion.17.refs_0_), channel_id=1, source_target_pairs={{0,4},{1,5},{2,6},{3,7},{4,0},{5,1},{6,2},{7,3},{8,12},{9,13},{10,... | collective-permute-start | bytes 294920 | tf_op jit(solution)/shard_map/ppermute | solution.py:24
  13.9 4.6 %collective-permute-start.16 = (bf16[3,64,256]{2,1,0:T(8,128)(2,1)S(1)}, bf16[3,64,256]{2,1,0:T(8,128)(2,1)S(1)}, u32[]{:S(2)}, u32[]{:S(2)}) collective-permute-start(bf16[3,64,256]{2,1,0:T(8,128)(2,1)S(1)} %collective-permute-done.12.refs_8_), channel_id=1, source_target_pairs={{0,8},{1,9},{2,10},{3,11},{4,12},{5,13},{6,14},{7,15},{8,0},{9,1},... | collective-permute-start | bytes 294920 | tf_op jit(solution)/shard_map/ppermute | solution.py:24
  14.5 4.6 %collective-permute-start.10 = (bf16[3,64,256]{2,1,0:T(8,128)(2,1)S(1)}, bf16[3,64,256]{2,1,0:T(8,128)(2,1)S(1)}, u32[]{:S(2)}, u32[]{:S(2)}) collective-permute-start(bf16[3,64,256]{2,1,0:T(8,128)(2,1)S(1)} %collective-permute-done.9.refs_4_), channel_id=1, source_target_pairs={{0,2},{1,3},{2,0},{3,1},{4,6},{5,7},{6,4},{7,5},{8,10},{9,11},{10,... | collective-permute-start | bytes 294920 | tf_op jit(solution)/shard_map/ppermute | solution.py:24
  16.0 7.4 %collective-permute-start.11 = (bf16[3,64,256]{2,1,0:T(8,128)(2,1)S(1)}, bf16[3,64,256]{2,1,0:T(8,128)(2,1)S(1)}, u32[]{:S(2)}, u32[]{:S(2)}) collective-permute-start(bf16[3,64,256]{2,1,0:T(8,128)(2,1)S(1)} %collective-permute-done.9.refs_4_), channel_id=1, source_target_pairs={{0,4},{1,5},{2,6},{3,7},{4,0},{5,1},{6,2},{7,3},{8,12},{9,13},{10,... | collective-permute-start | bytes 294920 | tf_op jit(solution)/shard_map/ppermute | solution.py:24
  17.5 7.5 %collective-permute-start.13 = (bf16[3,64,256]{2,1,0:T(8,128)(2,1)S(1)}, bf16[3,64,256]{2,1,0:T(8,128)(2,1)S(1)}, u32[]{:S(2)}, u32[]{:S(2)}) collective-permute-start(bf16[3,64,256]{2,1,0:T(8,128)(2,1)S(1)} %collective-permute-done.12.refs_8_), channel_id=1, source_target_pairs={{0,2},{1,3},{2,0},{3,1},{4,6},{5,7},{6,4},{7,5},{8,10},{9,11},{10,... | collective-permute-start | bytes 294920 | tf_op jit(solution)/shard_map/ppermute | solution.py:24
  19.1 6.4 %collective-permute-start.17 = (bf16[3,64,256]{2,1,0:T(8,128)(2,1)S(1)}, bf16[3,64,256]{2,1,0:T(8,128)(2,1)S(1)}, u32[]{:S(2)}, u32[]{:S(2)}) collective-permute-start(bf16[3,64,256]{2,1,0:T(8,128)(2,1)S(1)} %collective-permute-done.16.refs_12_), channel_id=1, source_target_pairs={{0,2},{1,3},{2,0},{3,1},{4,6},{5,7},{6,4},{7,5},{8,10},{9,11},{10,... | collective-permute-start | bytes 294920 | tf_op jit(solution)/shard_map/ppermute | solution.py:24
  21.4 5.0 %collective-permute-start.19 = (bf16[3,64,256]{2,1,0:T(8,128)(2,1)S(1)}, bf16[3,64,256]{2,1,0:T(8,128)(2,1)S(1)}, u32[]{:S(2)}, u32[]{:S(2)}) collective-permute-start(bf16[3,64,256]{2,1,0:T(8,128)(2,1)S(1)} %collective-permute-done.16.refs_12_), channel_id=1, source_target_pairs={{0,4},{1,5},{2,6},{3,7},{4,0},{5,1},{6,2},{7,3},{8,12},{9,13},{10,... | collective-permute-start | bytes 294920 | tf_op jit(solution)/shard_map/ppermute | solution.py:24
  23.0 6.4 %collective-permute-start.8 = (bf16[3,64,256]{2,1,0:T(8,128)(2,1)S(1)}, bf16[3,64,256]{2,1,0:T(8,128)(2,1)S(1)}, u32[]{:S(2)}, u32[]{:S(2)}) collective-permute-start(bf16[3,64,256]{2,1,0:T(8,128)(2,1)S(1)} %collective-permute-done.6.refs_1_), channel_id=1, source_target_pairs={{0,4},{1,5},{2,6},{3,7},{4,0},{5,1},{6,2},{7,3},{8,12},{9,13},{10,... | collective-permute-start | bytes 294920 | tf_op jit(solution)/shard_map/ppermute | solution.py:24
  23.4 6.0 %collective-permute-start.15 = (bf16[3,64,256]{2,1,0:T(8,128)(2,1)S(1)}, bf16[3,64,256]{2,1,0:T(8,128)(2,1)S(1)}, u32[]{:S(2)}, u32[]{:S(2)}) collective-permute-start(bf16[3,64,256]{2,1,0:T(8,128)(2,1)S(1)} %collective-permute-done.12.refs_8_), channel_id=1, source_target_pairs={{0,4},{1,5},{2,6},{3,7},{4,0},{5,1},{6,2},{7,3},{8,12},{9,13},{10,... | collective-permute-start | bytes 294920 | tf_op jit(solution)/shard_map/ppermute | solution.py:24
  25.0 4.6 %collective-permute-start.14 = (bf16[3,64,256]{2,1,0:T(8,128)(2,1)S(1)}, bf16[3,64,256]{2,1,0:T(8,128)(2,1)S(1)}, u32[]{:S(2)}, u32[]{:S(2)}) collective-permute-start(bf16[3,64,256]{2,1,0:T(8,128)(2,1)S(1)} %collective-permute-done.11.refs_6_), channel_id=1, source_target_pairs={{0,2},{1,3},{2,0},{3,1},{4,6},{5,7},{6,4},{7,5},{8,10},{9,11},{10,... | collective-permute-start | bytes 294920 | tf_op jit(solution)/shard_map/ppermute | solution.py:24
  26.4 4.6 %collective-permute-start.20 = (bf16[3,64,256]{2,1,0:T(8,128)(2,1)S(1)}, bf16[3,64,256]{2,1,0:T(8,128)(2,1)S(1)}, u32[]{:S(2)}, u32[]{:S(2)}) collective-permute-start(bf16[3,64,256]{2,1,0:T(8,128)(2,1)S(1)} %collective-permute-done.19.refs_14_), channel_id=1, source_target_pairs={{0,2},{1,3},{2,0},{3,1},{4,6},{5,7},{6,4},{7,5},{8,10},{9,11},{10,... | collective-permute-start | bytes 294920 | tf_op jit(solution)/shard_map/ppermute | solution.py:24
  27.1 4.6 %collective-permute-start.18 = (bf16[3,64,256]{2,1,0:T(8,128)(2,1)S(1)}, bf16[3,64,256]{2,1,0:T(8,128)(2,1)S(1)}, u32[]{:S(2)}, u32[]{:S(2)}) collective-permute-start(bf16[3,64,256]{2,1,0:T(8,128)(2,1)S(1)} %collective-permute-done.13.refs_9_), channel_id=1, source_target_pairs={{0,4},{1,5},{2,6},{3,7},{4,0},{5,1},{6,2},{7,3},{8,12},{9,13},{10,... | collective-permute-start | bytes 294920 | tf_op jit(solution)/shard_map/ppermute | solution.py:24
  34.9 6.6 %collective-permute-start.21 = (bf16[2,3,64,256]{3,2,1,0:T(8,128)(2,1)S(1)}, bf16[2,3,64,256]{3,2,1,0:T(8,128)(2,1)S(1)}, u32[]{:S(2)}, u32[]{:S(2)}) collective-permute-start(bf16[2,3,64,256]{3,2,1,0:T(8,128)(2,1)S(1)} %get-tuple-element.66), channel_id=1, source_target_pairs={{0,4},{1,5},{2,6},{3,7},{4,0},{5,1},{6,2},{7,3},{8,12},{9,13},{10,... | collective-permute-start | bytes 589832 | tf_op jit(solution)/shard_map/ppermute | solution.py:24
  35.9 7.1 %collective-permute-start.24 = (bf16[2,3,64,256]{3,2,1,0:T(8,128)(2,1)S(1)}, bf16[2,3,64,256]{3,2,1,0:T(8,128)(2,1)S(1)}, u32[]{:S(2)}, u32[]{:S(2)}) collective-permute-start(bf16[2,3,64,256]{3,2,1,0:T(8,128)(2,1)S(1)} %get-tuple-element.69), channel_id=1, source_target_pairs={{0,2},{1,3},{2,0},{3,1},{4,6},{5,7},{6,4},{7,5},{8,10},{9,11},{10,... | collective-permute-start | bytes 589832 | tf_op jit(solution)/shard_map/ppermute | solution.py:24
  37.9 7.8 %collective-permute-start.29 = (bf16[2,3,64,256]{3,2,1,0:T(8,128)(2,1)S(1)}, bf16[2,3,64,256]{3,2,1,0:T(8,128)(2,1)S(1)}, u32[]{:S(2)}, u32[]{:S(2)}) collective-permute-start(bf16[2,3,64,256]{3,2,1,0:T(8,128)(2,1)S(1)} %get-tuple-element.77), channel_id=1, source_target_pairs={{0,2},{1,3},{2,0},{3,1},{4,6},{5,7},{6,4},{7,5},{8,10},{9,11},{10,... | collective-permute-start | bytes 589832 | tf_op jit(solution)/shard_map/ppermute | solution.py:24
  41.5 4.7 %collective-permute-start.22 = (bf16[3,64,256]{2,1,0:T(8,128)(2,1)S(1)}, bf16[3,64,256]{2,1,0:T(8,128)(2,1)S(1)}, u32[]{:S(2)}, u32[]{:S(2)}) collective-permute-start(bf16[3,64,256]{2,1,0:T(8,128)(2,1)S(1)} %fusion.14), channel_id=1, source_target_pairs={{0,2},{1,3},{2,0},{3,1},{4,6},{5,7},{6,4},{7,5},{8,10},{9,11},{10,... | collective-permute-start | bytes 294920 | tf_op jit(solution)/shard_map/ppermute | solution.py:24
  43.0 9.1 %collective-permute-start.27 = (bf16[3,64,256]{2,1,0:T(8,128)(2,1)S(1)}, bf16[3,64,256]{2,1,0:T(8,128)(2,1)S(1)}, u32[]{:S(2)}, u32[]{:S(2)}) collective-permute-start(bf16[3,64,256]{2,1,0:T(8,128)(2,1)S(1)} %fusion.7), channel_id=1, source_target_pairs={{0,4},{1,5},{2,6},{3,7},{4,0},{5,1},{6,2},{7,3},{8,12},{9,13},{10,... | collective-permute-start | bytes 294920 | tf_op jit(solution)/shard_map/ppermute | solution.py:24
  45.6 6.6 %collective-permute-start.25 = (bf16[2,3,64,256]{3,2,1,0:T(8,128)(2,1)S(1)}, bf16[2,3,64,256]{3,2,1,0:T(8,128)(2,1)S(1)}, u32[]{:S(2)}, u32[]{:S(2)}) collective-permute-start(bf16[2,3,64,256]{3,2,1,0:T(8,128)(2,1)S(1)} %get-tuple-element.70), channel_id=1, source_target_pairs={{0,4},{1,5},{2,6},{3,7},{4,0},{5,1},{6,2},{7,3},{8,12},{9,13},{10,... | collective-permute-start | bytes 589832 | tf_op jit(solution)/shard_map/ppermute | solution.py:24
  46.2 9.9 %collective-permute-start.23 = (bf16[3,64,256]{2,1,0:T(8,128)(2,1)S(1)}, bf16[3,64,256]{2,1,0:T(8,128)(2,1)S(1)}, u32[]{:S(2)}, u32[]{:S(2)}) collective-permute-start(bf16[3,64,256]{2,1,0:T(8,128)(2,1)S(1)} %fusion.16), channel_id=1, source_target_pairs={{0,16},{1,17},{2,18},{3,19},{4,20},{5,21},{6,22},{7,23},{8,24},{9,... | collective-permute-start | bytes 294920 | tf_op jit(solution)/shard_map/ppermute | solution.py:24
  49.7 5.0 %collective-permute-start.30 = (bf16[3,64,256]{2,1,0:T(8,128)(2,1)S(1)}, bf16[3,64,256]{2,1,0:T(8,128)(2,1)S(1)}, u32[]{:S(2)}, u32[]{:S(2)}) collective-permute-start(bf16[3,64,256]{2,1,0:T(8,128)(2,1)S(1)} %fusion.4), channel_id=1, source_target_pairs={{0,4},{1,5},{2,6},{3,7},{4,0},{5,1},{6,2},{7,3},{8,12},{9,13},{10,... | collective-permute-start | bytes 294920 | tf_op jit(solution)/shard_map/ppermute | solution.py:24
  52.2 7.2 %collective-permute-start.28 = (bf16[3,64,256]{2,1,0:T(8,128)(2,1)S(1)}, bf16[3,64,256]{2,1,0:T(8,128)(2,1)S(1)}, u32[]{:S(2)}, u32[]{:S(2)}) collective-permute-start(bf16[3,64,256]{2,1,0:T(8,128)(2,1)S(1)} %fusion.9), channel_id=1, source_target_pairs={{0,24},{1,25},{2,26},{3,27},{4,28},{5,29},{6,30},{7,31},{8,16},{9,... | collective-permute-start | bytes 294920 | tf_op jit(solution)/shard_map/ppermute | solution.py:24
  54.5 5.2 %collective-permute-start.26 = (bf16[3,64,256]{2,1,0:T(8,128)(2,1)S(1)}, bf16[3,64,256]{2,1,0:T(8,128)(2,1)S(1)}, u32[]{:S(2)}, u32[]{:S(2)}) collective-permute-start(bf16[3,64,256]{2,1,0:T(8,128)(2,1)S(1)} %fusion.10), channel_id=1, source_target_pairs={{0,2},{1,3},{2,0},{3,1},{4,6},{5,7},{6,4},{7,5},{8,10},{9,11},{10,... | collective-permute-start | bytes 294920 | tf_op jit(solution)/shard_map/ppermute | solution.py:24
  54.8 5.9 %collective-permute-start.31 = (bf16[3,64,256]{2,1,0:T(8,128)(2,1)S(1)}, bf16[3,64,256]{2,1,0:T(8,128)(2,1)S(1)}, u32[]{:S(2)}, u32[]{:S(2)}) collective-permute-start(bf16[3,64,256]{2,1,0:T(8,128)(2,1)S(1)} %fusion.6), channel_id=1, source_target_pairs={{0,8},{1,9},{2,10},{3,11},{4,12},{5,13},{6,14},{7,15},{8,0},{9,1},... | collective-permute-start | bytes 294920 | tf_op jit(solution)/shard_map/ppermute | solution.py:24
  61.0 23.8 %copy-start = (bf16[1,256,1024]{2,1,0:T(8,128)(2,1)S(1)}, bf16[1,256,1024]{2,1,0:T(8,128)(2,1)}, u32[]{:S(2)}) copy-start(bf16[1,256,1024]{2,1,0:T(8,128)(2,1)} %param.14) | copy-start | bytes 1572868
  61.0 6.7 %collective-permute-start.38 = (bf16[3,64,256]{2,1,0:T(8,128)(2,1)S(1)}, bf16[3,64,256]{2,1,0:T(8,128)(2,1)S(1)}, u32[]{:S(2)}, u32[]{:S(2)}) collective-permute-start(bf16[3,64,256]{2,1,0:T(8,128)(2,1)S(1)} %get-tuple-element.94.refs_0_), channel_id=1, source_target_pairs={{0,16},{1,17},{2,18},{3,19},{4,20},{5,21},{6,22},{7,23},{8,24},{9,... | collective-permute-start | bytes 294920 | tf_op jit(solution)/shard_map/ppermute | solution.py:24
  62.4 5.7 %collective-permute-start.35 = (bf16[3,64,256]{2,1,0:T(8,128)(2,1)S(1)}, bf16[3,64,256]{2,1,0:T(8,128)(2,1)S(1)}, u32[]{:S(2)}, u32[]{:S(2)}) collective-permute-start(bf16[3,64,256]{2,1,0:T(8,128)(2,1)S(1)} %get-tuple-element.94.refs_0_), channel_id=1, source_target_pairs={{0,8},{1,9},{2,10},{3,11},{4,12},{5,13},{6,14},{7,15},{8,0},{9,1},... | collective-permute-start | bytes 294920 | tf_op jit(solution)/shard_map/ppermute | solution.py:24
  64.9 5.7 %collective-permute-start.33 = (bf16[3,64,256]{2,1,0:T(8,128)(2,1)S(1)}, bf16[3,64,256]{2,1,0:T(8,128)(2,1)S(1)}, u32[]{:S(2)}, u32[]{:S(2)}) collective-permute-start(bf16[3,64,256]{2,1,0:T(8,128)(2,1)S(1)} %get-tuple-element.94.refs_0_), channel_id=1, source_target_pairs={{0,4},{1,5},{2,6},{3,7},{4,0},{5,1},{6,2},{7,3},{8,12},{9,13},{10,... | collective-permute-start | bytes 294920 | tf_op jit(solution)/shard_map/ppermute | solution.py:24
  64.9 5.7 %collective-permute-start.32 = (bf16[3,64,256]{2,1,0:T(8,128)(2,1)S(1)}, bf16[3,64,256]{2,1,0:T(8,128)(2,1)S(1)}, u32[]{:S(2)}, u32[]{:S(2)}) collective-permute-start(bf16[3,64,256]{2,1,0:T(8,128)(2,1)S(1)} %get-tuple-element.94.refs_0_), channel_id=1, source_target_pairs={{0,2},{1,3},{2,0},{3,1},{4,6},{5,7},{6,4},{7,5},{8,10},{9,11},{10,... | collective-permute-start | bytes 294920 | tf_op jit(solution)/shard_map/ppermute | solution.py:24
  67.7 4.6 %collective-permute-start.42 = (bf16[3,64,256]{2,1,0:T(8,128)(2,1)S(1)}, bf16[3,64,256]{2,1,0:T(8,128)(2,1)S(1)}, u32[]{:S(2)}, u32[]{:S(2)}) collective-permute-start(bf16[3,64,256]{2,1,0:T(8,128)(2,1)S(1)} %collective-permute-done.38.refs_8_), channel_id=1, source_target_pairs={{0,8},{1,9},{2,10},{3,11},{4,12},{5,13},{6,14},{7,15},{8,0},{9,1},... | collective-permute-start | bytes 294920 | tf_op jit(solution)/shard_map/ppermute | solution.py:24
  68.1 5.5 %collective-permute-start.36 = (bf16[3,64,256]{2,1,0:T(8,128)(2,1)S(1)}, bf16[3,64,256]{2,1,0:T(8,128)(2,1)S(1)}, u32[]{:S(2)}, u32[]{:S(2)}) collective-permute-start(bf16[3,64,256]{2,1,0:T(8,128)(2,1)S(1)} %collective-permute-done.35.refs_4_), channel_id=1, source_target_pairs={{0,2},{1,3},{2,0},{3,1},{4,6},{5,7},{6,4},{7,5},{8,10},{9,11},{10,... | collective-permute-start | bytes 294920 | tf_op jit(solution)/shard_map/ppermute | solution.py:24
  70.6 5.4 %collective-permute-start.37 = (bf16[3,64,256]{2,1,0:T(8,128)(2,1)S(1)}, bf16[3,64,256]{2,1,0:T(8,128)(2,1)S(1)}, u32[]{:S(2)}, u32[]{:S(2)}) collective-permute-start(bf16[3,64,256]{2,1,0:T(8,128)(2,1)S(1)} %collective-permute-done.35.refs_4_), channel_id=1, source_target_pairs={{0,4},{1,5},{2,6},{3,7},{4,0},{5,1},{6,2},{7,3},{8,12},{9,13},{10,... | collective-permute-start | bytes 294920 | tf_op jit(solution)/shard_map/ppermute | solution.py:24
  71.6 5.7 %collective-permute-start.39 = (bf16[3,64,256]{2,1,0:T(8,128)(2,1)S(1)}, bf16[3,64,256]{2,1,0:T(8,128)(2,1)S(1)}, u32[]{:S(2)}, u32[]{:S(2)}) collective-permute-start(bf16[3,64,256]{2,1,0:T(8,128)(2,1)S(1)} %collective-permute-done.38.refs_8_), channel_id=1, source_target_pairs={{0,2},{1,3},{2,0},{3,1},{4,6},{5,7},{6,4},{7,5},{8,10},{9,11},{10,... | collective-permute-start | bytes 294920 | tf_op jit(solution)/shard_map/ppermute | solution.py:24
  73.6 6.6 %collective-permute-start.45 = (bf16[3,64,256]{2,1,0:T(8,128)(2,1)S(1)}, bf16[3,64,256]{2,1,0:T(8,128)(2,1)S(1)}, u32[]{:S(2)}, u32[]{:S(2)}) collective-permute-start(bf16[3,64,256]{2,1,0:T(8,128)(2,1)S(1)} %collective-permute-done.42.refs_12_), channel_id=1, source_target_pairs={{0,4},{1,5},{2,6},{3,7},{4,0},{5,1},{6,2},{7,3},{8,12},{9,13},{10,... | collective-permute-start | bytes 294920 | tf_op jit(solution)/shard_map/ppermute | solution.py:24
  73.8 4.6 %collective-permute-start.43 = (bf16[3,64,256]{2,1,0:T(8,128)(2,1)S(1)}, bf16[3,64,256]{2,1,0:T(8,128)(2,1)S(1)}, u32[]{:S(2)}, u32[]{:S(2)}) collective-permute-start(bf16[3,64,256]{2,1,0:T(8,128)(2,1)S(1)} %collective-permute-done.42.refs_12_), channel_id=1, source_target_pairs={{0,2},{1,3},{2,0},{3,1},{4,6},{5,7},{6,4},{7,5},{8,10},{9,11},{10,... | collective-permute-start | bytes 294920 | tf_op jit(solution)/shard_map/ppermute | solution.py:24
  75.3 5.3 %collective-permute-start.34 = (bf16[3,64,256]{2,1,0:T(8,128)(2,1)S(1)}, bf16[3,64,256]{2,1,0:T(8,128)(2,1)S(1)}, u32[]{:S(2)}, u32[]{:S(2)}) collective-permute-start(bf16[3,64,256]{2,1,0:T(8,128)(2,1)S(1)} %collective-permute-done.32.refs_1_), channel_id=1, source_target_pairs={{0,4},{1,5},{2,6},{3,7},{4,0},{5,1},{6,2},{7,3},{8,12},{9,13},{10,... | collective-permute-start | bytes 294920 | tf_op jit(solution)/shard_map/ppermute | solution.py:24
  76.0 5.0 %collective-permute-start.41 = (bf16[3,64,256]{2,1,0:T(8,128)(2,1)S(1)}, bf16[3,64,256]{2,1,0:T(8,128)(2,1)S(1)}, u32[]{:S(2)}, u32[]{:S(2)}) collective-permute-start(bf16[3,64,256]{2,1,0:T(8,128)(2,1)S(1)} %collective-permute-done.38.refs_8_), channel_id=1, source_target_pairs={{0,4},{1,5},{2,6},{3,7},{4,0},{5,1},{6,2},{7,3},{8,12},{9,13},{10,... | collective-permute-start | bytes 294920 | tf_op jit(solution)/shard_map/ppermute | solution.py:24
  77.4 4.6 %collective-permute-start.40 = (bf16[3,64,256]{2,1,0:T(8,128)(2,1)S(1)}, bf16[3,64,256]{2,1,0:T(8,128)(2,1)S(1)}, u32[]{:S(2)}, u32[]{:S(2)}) collective-permute-start(bf16[3,64,256]{2,1,0:T(8,128)(2,1)S(1)} %collective-permute-done.37.refs_6_), channel_id=1, source_target_pairs={{0,2},{1,3},{2,0},{3,1},{4,6},{5,7},{6,4},{7,5},{8,10},{9,11},{10,... | collective-permute-start | bytes 294920 | tf_op jit(solution)/shard_map/ppermute | solution.py:24
  78.4 6.4 %collective-permute-start.44 = (bf16[3,64,256]{2,1,0:T(8,128)(2,1)S(1)}, bf16[3,64,256]{2,1,0:T(8,128)(2,1)S(1)}, u32[]{:S(2)}, u32[]{:S(2)}) collective-permute-start(bf16[3,64,256]{2,1,0:T(8,128)(2,1)S(1)} %collective-permute-done.39.refs_9_), channel_id=1, source_target_pairs={{0,4},{1,5},{2,6},{3,7},{4,0},{5,1},{6,2},{7,3},{8,12},{9,13},{10,... | collective-permute-start | bytes 294920 | tf_op jit(solution)/shard_map/ppermute | solution.py:24
  80.2 4.6 %collective-permute-start.46 = (bf16[3,64,256]{2,1,0:T(8,128)(2,1)S(1)}, bf16[3,64,256]{2,1,0:T(8,128)(2,1)S(1)}, u32[]{:S(2)}, u32[]{:S(2)}) collective-permute-start(bf16[3,64,256]{2,1,0:T(8,128)(2,1)S(1)} %collective-permute-done.45.refs_14_), channel_id=1, source_target_pairs={{0,2},{1,3},{2,0},{3,1},{4,6},{5,7},{6,4},{7,5},{8,10},{9,11},{10,... | collective-permute-start | bytes 294920 | tf_op jit(solution)/shard_map/ppermute | solution.py:24
  85.6 1.6 %collective-permute-start.47 = (f32[3,3,32,256]{3,2,1,0:T(8,128)S(1)}, f32[3,3,32,256]{3,2,1,0:T(8,128)S(1)}, u32[]{:S(2)}, u32[]{:S(2)}) collective-permute-start(f32[3,3,32,256]{3,2,1,0:T(8,128)S(1)} %get-tuple-element.91), channel_id=1, source_target_pairs={{0,1},{1,0},{2,3},{3,2},{4,5},{5,4},{6,7},{7,6},{8,9},{9,8},{10,11... | collective-permute-start | bytes 884744 | tf_op jit(solution)/shard_map/ppermute | solution.py:24
  85.7 2.5 %collective-permute-start.48 = (bf16[256,1024]{1,0:T(8,128)(2,1)S(1)}, bf16[256,1024]{1,0:T(8,128)(2,1)S(1)}, u32[]{:S(2)}, u32[]{:S(2)}) collective-permute-start(bf16[256,1024]{1,0:T(8,128)(2,1)S(1)} %get-tuple-element.90), channel_id=1, source_target_pairs={{0,1},{1,0},{2,3},{3,2},{4,5},{5,4},{6,7},{7,6},{8,9},{9,8},{10,11... | collective-permute-start | bytes 1572872 | tf_op jit(solution)/shard_map/ppermute | solution.py:24

commit v17 on v16

--- a/solution.py
+++ b/solution.py
@@ -248,23 +248,22 @@
 
 def reduce_chips(pieces):
     depth = lax.axis_size("dev") // Z_UNIT
-    total, waiting, arrived, crossed = [], [], (), ()
+    total, waiting, arrived = [], [], ()
     for upper in reversed(range(1, depth, 2)):
         own_up, up_y, pair_x = pieces[3 * upper : 3 * upper + 3]
         own_low, low_x, pair_y = pieces[3 * upper - 3 : 3 * upper]
         got_x = hop(pair_x, X_STEP)
         got_y = hop(after(pair_y, *arrived), Y_STEP)
-        up_y = hop(after(add_all(up_y, got_x[0]).astype(jnp.bfloat16), *crossed), Y_STEP)
-        low_x = hop(after(add_all(low_x, got_y[0]).astype(jnp.bfloat16), *crossed), X_STEP)
-        arrived, crossed = (got_x,), (low_x,)
+        up_y = hop(add_all(up_y, got_x[0]).astype(jnp.bfloat16), Y_STEP)
+        low_x = hop(add_all(low_x, got_y[0]).astype(jnp.bfloat16), X_STEP)
+        arrived = (got_x,)
         low = [own_low, got_y[1], low_x]
         up = add_all(own_up, got_x[1], up_y).astype(jnp.bfloat16)
         if upper > 1:
-            total.append(hop(add_all(*low).astype(jnp.bfloat16), (upper - 1) * Z_UNIT))
-            waiting.append((up, upper * Z_UNIT))
+            waiting += [(add_all(*low).astype(jnp.bfloat16), (upper - 1) * Z_UNIT), (up, upper * Z_UNIT)]
         else:
             total += low
-            total += [hop(after(part, got_y), mask) for part, mask in waiting]
+            total += [hop(after(part, got_x if mask & Z_UNIT == 0 else got_y), mask) for part, mask in waiting]
             total.append(hop(up, Z_UNIT))
     return add_all(*total)
 

time: 89.2 us -> 88.4 us (level)
  waiting for transfers between devices: 24.5 us -> 20.5 us
  starting transfers between devices: 52.7 us -> 55.9 us
    ppermute x49, waiting for transfers between devices: 24.5 us -> 20.5 us  [hop(): lax.ppermute(block, 'dev', [(low, low ^ mask) for low in range(count)])]
    ppermute x49, starting transfers between devices: 52.7 us -> 55.9 us  [hop(): lax.ppermute(block, 'dev', [(low, low ^ mask) for low in range(count)])]
  transfers between devices with their start and end apart: 49 -> 49, of which waited for: 22 -> 19; matrix products, arithmetic and copies ran while one was open for 4% -> 4% of each run, Pallas kernels for 1% -> 1%
where the time goes in v17:
time: 88.4 us; the launch traced here: 88.2 us
  starting transfers between devices  55.9 us (63%)
  waiting for transfers between devices  20.5 us (23%)
  Pallas kernels  5.21 us (6%)
  local copies, waits for them, and re-layouts  2.92 us (3%)
  between operations  2.21 us (2%)
  other arithmetic  1.52 us (2%)
    ppermute x49, starting transfers between devices, hop(): lax.ppermute(block, 'dev', [(low, low ^ mask) for low in range(count)])  55.9 us
    ppermute x49, waiting for transfers between devices, hop(): lax.ppermute(block, 'dev', [(low, low ^ mask) for low in range(count)])  20.5 us
    pallas_call x1, Pallas kernels, backward(): pl.pallas_call(functools.partial(backward_kernel, count), out_shape=[one,...  3.18 us
    squeeze x2, local copies, waits for them, and re-layouts, mine(): return lax.dynamic_index_in_dim(state, core, 0, keepdims=False)  2.01 us
  transfers between devices with their start and end apart: 49, of which 19 were waited for; matrix products, arithmetic and copies ran while one was open for 4% of the time, Pallas kernels for 1%

profile of v17, /device:TPU:0, one launch (start us, length us, event | category | flops | bytes accessed | tf_op | source)
XLA Modules:
  0.0 88.2 jit_solution(4313872578517631071)
XLA Ops:
  0.7 0.5 collective-permute-start.1
  1.2 0.4 collective-permute-start.3
  1.8 1.0 %dynamic-slice_bitcast_fusion.4 = (f32[3,32,256]{2,1,0:T(8,128)S(1)}, f32[3,32,256]{2,1,0:T(8,128)S(1)}) fusion(f32[2,3,32,256]{3,2,1,0:T(8,128)} %param.9, s32[]{:T(128)S(6)} %select_n.47, s32[]{:T(128)S(6)} %select_n.48), kind=kLoop, calls=%fused_computation.53 | loop fusion | bytes 393224 | tf_op jit(solution)/shard_map/jit(dynamic_index_in_dim)/squeeze | solution.py:276
  2.7 0.5 collective-permute-start
  3.2 1.1 %dynamic-slice_bitcast_fusion.1 = (f32[3,32,256]{2,1,0:T(8,128)S(1)}, f32[1,3,32,256]{3,2,1,0:T(8,128)S(1)}, f32[1,3,32,256]{3,2,1,0:T(8,128)S(1)}, f32[3,32,256]{2,1,0:T(8,128)S(1)}) fusion(f32[2,3,32,256]{3,2,1,0:T(8,128)} %param.11, s32[]{:T(128)S(6)} %select_n.47, s32[]{:T(128)S(6)} %select_n.48, f32[2,3,32,256]{3,2,1,0:T(8,128)} %param.10), kind=kLoop, calls=%fused_computation.49 | loop fusion | bytes 786440 | tf_op jit(solution)/shard_map/jit(dynamic_index_in_dim)/squeeze | solution.py:276
  4.5 4.1 %collective-permute-start.12 = (bf16[3,64,256]{2,1,0:T(8,128)(2,1)S(1)}, bf16[3,64,256]{2,1,0:T(8,128)(2,1)S(1)}, u32[]{:S(2)}, u32[]{:S(2)}) collective-permute-start(bf16[3,64,256]{2,1,0:T(8,128)(2,1)S(1)} %fusion.18.refs_0_), channel_id=1, source_target_pairs={{0,16},{1,17},{2,18},{3,19},{4,20},{5,21},{6,22},{7,23},{8,24},{9,... | collective-permute-start | bytes 294920 | tf_op jit(solution)/shard_map/ppermute | solution.py:24
  8.6 1.6 %collective-permute-start.9 = (bf16[3,64,256]{2,1,0:T(8,128)(2,1)S(1)}, bf16[3,64,256]{2,1,0:T(8,128)(2,1)S(1)}, u32[]{:S(2)}, u32[]{:S(2)}) collective-permute-start(bf16[3,64,256]{2,1,0:T(8,128)(2,1)S(1)} %fusion.18.refs_0_), channel_id=1, source_target_pairs={{0,8},{1,9},{2,10},{3,11},{4,12},{5,13},{6,14},{7,15},{8,0},{9,1},... | collective-permute-start | bytes 294920 | tf_op jit(solution)/shard_map/ppermute | solution.py:24
  10.2 1.5 %collective-permute-start.6 = (bf16[3,64,256]{2,1,0:T(8,128)(2,1)S(1)}, bf16[3,64,256]{2,1,0:T(8,128)(2,1)S(1)}, u32[]{:S(2)}, u32[]{:S(2)}) collective-permute-start(bf16[3,64,256]{2,1,0:T(8,128)(2,1)S(1)} %fusion.18.refs_0_), channel_id=1, source_target_pairs={{0,2},{1,3},{2,0},{3,1},{4,6},{5,7},{6,4},{7,5},{8,10},{9,11},{10,... | collective-permute-start | bytes 294920 | tf_op jit(solution)/shard_map/ppermute | solution.py:24
  11.7 1.5 %collective-permute-start.7 = (bf16[3,64,256]{2,1,0:T(8,128)(2,1)S(1)}, bf16[3,64,256]{2,1,0:T(8,128)(2,1)S(1)}, u32[]{:S(2)}, u32[]{:S(2)}) collective-permute-start(bf16[3,64,256]{2,1,0:T(8,128)(2,1)S(1)} %fusion.18.refs_0_), channel_id=1, source_target_pairs={{0,4},{1,5},{2,6},{3,7},{4,0},{5,1},{6,2},{7,3},{8,12},{9,13},{10,... | collective-permute-start | bytes 294920 | tf_op jit(solution)/shard_map/ppermute | solution.py:24
  13.2 0.7 collective-permute-done.12.refs_8_
  13.9 0.6 collective-permute-start.16
  14.5 1.5 %collective-permute-start.10 = (bf16[3,64,256]{2,1,0:T(8,128)(2,1)S(1)}, bf16[3,64,256]{2,1,0:T(8,128)(2,1)S(1)}, u32[]{:S(2)}, u32[]{:S(2)}) collective-permute-start(bf16[3,64,256]{2,1,0:T(8,128)(2,1)S(1)} %collective-permute-done.9.refs_4_), channel_id=1, source_target_pairs={{0,2},{1,3},{2,0},{3,1},{4,6},{5,7},{6,4},{7,5},{8,10},{9,11},{10,... | collective-permute-start | bytes 294920 | tf_op jit(solution)/shard_map/ppermute | solution.py:24
  16.0 1.5 %collective-permute-start.11 = (bf16[3,64,256]{2,1,0:T(8,128)(2,1)S(1)}, bf16[3,64,256]{2,1,0:T(8,128)(2,1)S(1)}, u32[]{:S(2)}, u32[]{:S(2)}) collective-permute-start(bf16[3,64,256]{2,1,0:T(8,128)(2,1)S(1)} %collective-permute-done.9.refs_4_), channel_id=1, source_target_pairs={{0,4},{1,5},{2,6},{3,7},{4,0},{5,1},{6,2},{7,3},{8,12},{9,13},{10,... | collective-permute-start | bytes 294920 | tf_op jit(solution)/shard_map/ppermute | solution.py:24
  17.5 0.5 collective-permute-start.13
  18.0 0.4 collective-permute-done.16.refs_12_
  18.5 0.6 collective-permute-done.10.refs_5_
  19.1 2.3 %collective-permute-start.17 = (bf16[3,64,256]{2,1,0:T(8,128)(2,1)S(1)}, bf16[3,64,256]{2,1,0:T(8,128)(2,1)S(1)}, u32[]{:S(2)}, u32[]{:S(2)}) collective-permute-start(bf16[3,64,256]{2,1,0:T(8,128)(2,1)S(1)} %collective-permute-done.16.refs_12_), channel_id=1, source_target_pairs={{0,2},{1,3},{2,0},{3,1},{4,6},{5,7},{6,4},{7,5},{8,10},{9,11},{10,... | collective-permute-start | bytes 294920 | tf_op jit(solution)/shard_map/ppermute | solution.py:24
  21.4 1.6 %collective-permute-start.19 = (bf16[3,64,256]{2,1,0:T(8,128)(2,1)S(1)}, bf16[3,64,256]{2,1,0:T(8,128)(2,1)S(1)}, u32[]{:S(2)}, u32[]{:S(2)}) collective-permute-start(bf16[3,64,256]{2,1,0:T(8,128)(2,1)S(1)} %collective-permute-done.16.refs_12_), channel_id=1, source_target_pairs={{0,4},{1,5},{2,6},{3,7},{4,0},{5,1},{6,2},{7,3},{8,12},{9,13},{10,... | collective-permute-start | bytes 294920 | tf_op jit(solution)/shard_map/ppermute | solution.py:24
  23.4 1.6 %collective-permute-start.15 = (bf16[3,64,256]{2,1,0:T(8,128)(2,1)S(1)}, bf16[3,64,256]{2,1,0:T(8,128)(2,1)S(1)}, u32[]{:S(2)}, u32[]{:S(2)}) collective-permute-start(bf16[3,64,256]{2,1,0:T(8,128)(2,1)S(1)} %collective-permute-done.12.refs_8_), channel_id=1, source_target_pairs={{0,4},{1,5},{2,6},{3,7},{4,0},{5,1},{6,2},{7,3},{8,12},{9,13},{10,... | collective-permute-start | bytes 294920 | tf_op jit(solution)/shard_map/ppermute | solution.py:24
  25.0 0.5 collective-permute-start.14
  25.5 0.9 collective-permute-done.19.refs_14_
  26.4 0.7 collective-permute-start.20
  27.1 1.0 %collective-permute-start.18 = (bf16[3,64,256]{2,1,0:T(8,128)(2,1)S(1)}, bf16[3,64,256]{2,1,0:T(8,128)(2,1)S(1)}, u32[]{:S(2)}, u32[]{:S(2)}) collective-permute-start(bf16[3,64,256]{2,1,0:T(8,128)(2,1)S(1)} %collective-permute-done.13.refs_9_), channel_id=1, source_target_pairs={{0,4},{1,5},{2,6},{3,7},{4,0},{5,1},{6,2},{7,3},{8,12},{9,13},{10,... | collective-permute-start | bytes 294920 | tf_op jit(solution)/shard_map/ppermute | solution.py:24
  28.8 0.6 transpose_rows.1
  29.6 1.3 %collective-permute-done.20.refs_15_ = bf16[3,64,256]{2,1,0:T(8,128)(2,1)S(1)} collective-permute-done((bf16[3,64,256]{2,1,0:T(8,128)(2,1)S(1)}, bf16[3,64,256]{2,1,0:T(8,128)(2,1)S(1)}, u32[]{:S(2)}, u32[]{:S(2)}) %collective-permute-start.20) | collective-permute-done | bytes 98336 | tf_op jit(solution)/shard_map/ppermute | solution.py:24
  31.0 0.7 collective-permute-done.18.refs_11_
  31.7 3.2 %slot_gradients.1 = (bf16[3,64,256]{2,1,0:T(8,128)(2,1)S(1)}, bf16[3,64,256]{2,1,0:T(8,128)(2,1)S(1)}, bf16[2,3,64,256]{3,2,1,0:T(8,128)(2,1)S(1)}, bf16[3,64,25...) custom-call(s32[1,32]{1,0:T(1,128)S(1)} %bitcast.86, ...), custom_call_target="tpu_custom_call" | custom-call | flops 1610612736 | bytes 7340032 | tf_op jit(solution)/shard_map/slot_gradients/pallas_call | solution.py:160
  34.9 1.3 %collective-permute-start.21 = (bf16[2,3,64,256]{3,2,1,0:T(8,128)(2,1)S(1)}, bf16[2,3,64,256]{3,2,1,0:T(8,128)(2,1)S(1)}, u32[]{:S(2)}, u32[]{:S(2)}) collective-permute-start(bf16[2,3,64,256]{3,2,1,0:T(8,128)(2,1)S(1)} %get-tuple-element.65), channel_id=1, source_target_pairs={{0,2},{1,3},{2,0},{3,1},{4,6},{5,7},{6,4},{7,5},{8,10},{9,11},{10,... | collective-permute-start | bytes 589832 | tf_op jit(solution)/shard_map/ppermute | solution.py:24
  36.2 1.7 %collective-permute-start.24 = (bf16[2,3,64,256]{3,2,1,0:T(8,128)(2,1)S(1)}, bf16[2,3,64,256]{3,2,1,0:T(8,128)(2,1)S(1)}, u32[]{:S(2)}, u32[]{:S(2)}) collective-permute-start(bf16[2,3,64,256]{3,2,1,0:T(8,128)(2,1)S(1)} %get-tuple-element.69), channel_id=1, source_target_pairs={{0,4},{1,5},{2,6},{3,7},{4,0},{5,1},{6,2},{7,3},{8,12},{9,13},{10,... | collective-permute-start | bytes 589832 | tf_op jit(solution)/shard_map/ppermute | solution.py:24
  37.9 3.0 %collective-permute-done.21 = bf16[2,3,64,256]{3,2,1,0:T(8,128)(2,1)S(1)} collective-permute-done((bf16[2,3,64,256]{3,2,1,0:T(8,128)(2,1)S(1)}, bf16[2,3,64,256]{3,2,1,0:T(8,128)(2,1)S(1)}, u32[]{:S(2)}, u32[]{:S(2)}) %collective-permute-start.21) | collective-permute-done | bytes 196640 | tf_op jit(solution)/shard_map/ppermute | solution.py:24
  41.0 0.9 collective-permute-start.28
  41.8 1.2 %collective-permute-start.22 = (bf16[2,3,64,256]{3,2,1,0:T(8,128)(2,1)S(1)}, bf16[2,3,64,256]{3,2,1,0:T(8,128)(2,1)S(1)}, u32[]{:S(2)}, u32[]{:S(2)}) collective-permute-start(bf16[2,3,64,256]{3,2,1,0:T(8,128)(2,1)S(1)} %get-tuple-element.66), channel_id=1, source_target_pairs={{0,4},{1,5},{2,6},{3,7},{4,0},{5,1},{6,2},{7,3},{8,12},{9,13},{10,... | collective-permute-start | bytes 589832 | tf_op jit(solution)/shard_map/ppermute | solution.py:24
  43.0 1.0 %collective-permute-done.24 = bf16[2,3,64,256]{3,2,1,0:T(8,128)(2,1)S(1)} collective-permute-done((bf16[2,3,64,256]{3,2,1,0:T(8,128)(2,1)S(1)}, bf16[2,3,64,256]{3,2,1,0:T(8,128)(2,1)S(1)}, u32[]{:S(2)}, u32[]{:S(2)}) %collective-permute-start.24) | collective-permute-done | bytes 196640 | tf_op jit(solution)/shard_map/ppermute | solution.py:24
  44.0 0.7 collective-permute-start.25
  44.8 1.8 %collective-permute-start.30 = (bf16[3,64,256]{2,1,0:T(8,128)(2,1)S(1)}, bf16[3,64,256]{2,1,0:T(8,128)(2,1)S(1)}, u32[]{:S(2)}, u32[]{:S(2)}) collective-permute-start(bf16[3,64,256]{2,1,0:T(8,128)(2,1)S(1)} %fusion.4), channel_id=1, source_target_pairs={{0,4},{1,5},{2,6},{3,7},{4,0},{5,1},{6,2},{7,3},{8,12},{9,13},{10,... | collective-permute-start | bytes 294920 | tf_op jit(solution)/shard_map/ppermute | solution.py:24
  46.5 2.2 %collective-permute-done.25 = bf16[3,64,256]{2,1,0:T(8,128)(2,1)S(1)} collective-permute-done((bf16[3,64,256]{2,1,0:T(8,128)(2,1)S(1)}, bf16[3,64,256]{2,1,0:T(8,128)(2,1)S(1)}, u32[]{:S(2)}, u32[]{:S(2)}) %collective-permute-start.25) | collective-permute-done | bytes 98336 | tf_op jit(solution)/shard_map/ppermute | solution.py:24
  48.8 2.9 %collective-permute-start.27 = (bf16[3,64,256]{2,1,0:T(8,128)(2,1)S(1)}, bf16[3,64,256]{2,1,0:T(8,128)(2,1)S(1)}, u32[]{:S(2)}, u32[]{:S(2)}) collective-permute-start(bf16[3,64,256]{2,1,0:T(8,128)(2,1)S(1)} %fusion.12), channel_id=1, source_target_pairs={{0,16},{1,17},{2,18},{3,19},{4,20},{5,21},{6,22},{7,23},{8,24},{9,... | collective-permute-start | bytes 294920 | tf_op jit(solution)/shard_map/ppermute | solution.py:24
  51.7 0.9 %collective-permute-start.31 = (bf16[3,64,256]{2,1,0:T(8,128)(2,1)S(1)}, bf16[3,64,256]{2,1,0:T(8,128)(2,1)S(1)}, u32[]{:S(2)}, u32[]{:S(2)}) collective-permute-start(bf16[3,64,256]{2,1,0:T(8,128)(2,1)S(1)} %fusion.6), channel_id=1, source_target_pairs={{0,8},{1,9},{2,10},{3,11},{4,12},{5,13},{6,14},{7,15},{8,0},{9,1},... | collective-permute-start | bytes 294920 | tf_op jit(solution)/shard_map/ppermute | solution.py:24
  52.7 1.9 %collective-permute-start.29 = (bf16[3,64,256]{2,1,0:T(8,128)(2,1)S(1)}, bf16[3,64,256]{2,1,0:T(8,128)(2,1)S(1)}, u32[]{:S(2)}, u32[]{:S(2)}) collective-permute-start(bf16[3,64,256]{2,1,0:T(8,128)(2,1)S(1)} %fusion.9), channel_id=1, source_target_pairs={{0,24},{1,25},{2,26},{3,27},{4,28},{5,29},{6,30},{7,31},{8,16},{9,... | collective-permute-start | bytes 294920 | tf_op jit(solution)/shard_map/ppermute | solution.py:24
  54.7 1.9 %collective-permute-start.23 = (bf16[3,64,256]{2,1,0:T(8,128)(2,1)S(1)}, bf16[3,64,256]{2,1,0:T(8,128)(2,1)S(1)}, u32[]{:S(2)}, u32[]{:S(2)}) collective-permute-start(bf16[3,64,256]{2,1,0:T(8,128)(2,1)S(1)} %fusion.13), channel_id=1, source_target_pairs={{0,2},{1,3},{2,0},{3,1},{4,6},{5,7},{6,4},{7,5},{8,10},{9,11},{10,... | collective-permute-start | bytes 294920 | tf_op jit(solution)/shard_map/ppermute | solution.py:24
  57.3 3.0 %collective-permute-done.29 = bf16[3,64,256]{2,1,0:T(8,128)(2,1)S(1)} collective-permute-done((bf16[3,64,256]{2,1,0:T(8,128)(2,1)S(1)}, bf16[3,64,256]{2,1,0:T(8,128)(2,1)S(1)}, u32[]{:S(2)}, u32[]{:S(2)}) %collective-permute-start.29) | collective-permute-done | bytes 98336 | tf_op jit(solution)/shard_map/ppermute | solution.py:24
  60.6 1.6 %collective-permute-start.38 = (bf16[3,64,256]{2,1,0:T(8,128)(2,1)S(1)}, bf16[3,64,256]{2,1,0:T(8,128)(2,1)S(1)}, u32[]{:S(2)}, u32[]{:S(2)}) collective-permute-start(bf16[3,64,256]{2,1,0:T(8,128)(2,1)S(1)} %get-tuple-element.92.refs_0_), channel_id=1, source_target_pairs={{0,16},{1,17},{2,18},{3,19},{4,20},{5,21},{6,22},{7,23},{8,24},{9,... | collective-permute-start | bytes 294920 | tf_op jit(solution)/shard_map/ppermute | solution.py:24
  62.1 1.0 %collective-permute-start.35 = (bf16[3,64,256]{2,1,0:T(8,128)(2,1)S(1)}, bf16[3,64,256]{2,1,0:T(8,128)(2,1)S(1)}, u32[]{:S(2)}, u32[]{:S(2)}) collective-permute-start(bf16[3,64,256]{2,1,0:T(8,128)(2,1)S(1)} %get-tuple-element.92.refs_0_), channel_id=1, source_target_pairs={{0,8},{1,9},{2,10},{3,11},{4,12},{5,13},{6,14},{7,15},{8,0},{9,1},... | collective-permute-start | bytes 294920 | tf_op jit(solution)/shard_map/ppermute | solution.py:24
  63.1 2.8 %collective-permute-start.33 = (bf16[3,64,256]{2,1,0:T(8,128)(2,1)S(1)}, bf16[3,64,256]{2,1,0:T(8,128)(2,1)S(1)}, u32[]{:S(2)}, u32[]{:S(2)}) collective-permute-start(bf16[3,64,256]{2,1,0:T(8,128)(2,1)S(1)} %get-tuple-element.92.refs_0_), channel_id=1, source_target_pairs={{0,4},{1,5},{2,6},{3,7},{4,0},{5,1},{6,2},{7,3},{8,12},{9,13},{10,... | collective-permute-start | bytes 294920 | tf_op jit(solution)/shard_map/ppermute | solution.py:24
  65.9 1.0 %collective-permute-start.32 = (bf16[3,64,256]{2,1,0:T(8,128)(2,1)S(1)}, bf16[3,64,256]{2,1,0:T(8,128)(2,1)S(1)}, u32[]{:S(2)}, u32[]{:S(2)}) collective-permute-start(bf16[3,64,256]{2,1,0:T(8,128)(2,1)S(1)} %get-tuple-element.92.refs_0_), channel_id=1, source_target_pairs={{0,2},{1,3},{2,0},{3,1},{4,6},{5,7},{6,4},{7,5},{8,10},{9,11},{10,... | collective-permute-start | bytes 294920 | tf_op jit(solution)/shard_map/ppermute | solution.py:24
  67.3 1.1 %collective-permute-start.36 = (bf16[3,64,256]{2,1,0:T(8,128)(2,1)S(1)}, bf16[3,64,256]{2,1,0:T(8,128)(2,1)S(1)}, u32[]{:S(2)}, u32[]{:S(2)}) collective-permute-start(bf16[3,64,256]{2,1,0:T(8,128)(2,1)S(1)} %collective-permute-done.35.refs_4_), channel_id=1, source_target_pairs={{0,2},{1,3},{2,0},{3,1},{4,6},{5,7},{6,4},{7,5},{8,10},{9,11},{10,... | collective-permute-start | bytes 294920 | tf_op jit(solution)/shard_map/ppermute | solution.py:24
  68.5 1.1 %collective-permute-done.33.refs_2_ = bf16[3,64,256]{2,1,0:T(8,128)(2,1)S(1)} collective-permute-done((bf16[3,64,256]{2,1,0:T(8,128)(2,1)S(1)}, bf16[3,64,256]{2,1,0:T(8,128)(2,1)S(1)}, u32[]{:S(2)}, u32[]{:S(2)}) %collective-permute-start.33) | collective-permute-done | bytes 98336 | tf_op jit(solution)/shard_map/ppermute | solution.py:24
  69.6 1.5 %collective-permute-done.32.refs_1_ = bf16[3,64,256]{2,1,0:T(8,128)(2,1)S(1)} collective-permute-done((bf16[3,64,256]{2,1,0:T(8,128)(2,1)S(1)}, bf16[3,64,256]{2,1,0:T(8,128)(2,1)S(1)}, u32[]{:S(2)}, u32[]{:S(2)}) %collective-permute-start.32) | collective-permute-done | bytes 98336 | tf_op jit(solution)/shard_map/ppermute | solution.py:24
  71.1 0.6 collective-permute-start.37
  71.7 0.9 %collective-permute-start.39 = (bf16[3,64,256]{2,1,0:T(8,128)(2,1)S(1)}, bf16[3,64,256]{2,1,0:T(8,128)(2,1)S(1)}, u32[]{:S(2)}, u32[]{:S(2)}) collective-permute-start(bf16[3,64,256]{2,1,0:T(8,128)(2,1)S(1)} %collective-permute-done.38.refs_8_), channel_id=1, source_target_pairs={{0,2},{1,3},{2,0},{3,1},{4,6},{5,7},{6,4},{7,5},{8,10},{9,11},{10,... | collective-permute-start | bytes 294920 | tf_op jit(solution)/shard_map/ppermute | solution.py:24
  72.6 2.2 %collective-permute-start.45 = (bf16[3,64,256]{2,1,0:T(8,128)(2,1)S(1)}, bf16[3,64,256]{2,1,0:T(8,128)(2,1)S(1)}, u32[]{:S(2)}, u32[]{:S(2)}) collective-permute-start(bf16[3,64,256]{2,1,0:T(8,128)(2,1)S(1)} %collective-permute-done.42.refs_12_), channel_id=1, source_target_pairs={{0,4},{1,5},{2,6},{3,7},{4,0},{5,1},{6,2},{7,3},{8,12},{9,13},{10,... | collective-permute-start | bytes 294920 | tf_op jit(solution)/shard_map/ppermute | solution.py:24
  74.8 0.5 collective-permute-start.43
  75.3 1.5 %collective-permute-start.34 = (bf16[3,64,256]{2,1,0:T(8,128)(2,1)S(1)}, bf16[3,64,256]{2,1,0:T(8,128)(2,1)S(1)}, u32[]{:S(2)}, u32[]{:S(2)}) collective-permute-start(bf16[3,64,256]{2,1,0:T(8,128)(2,1)S(1)} %collective-permute-done.32.refs_1_), channel_id=1, source_target_pairs={{0,4},{1,5},{2,6},{3,7},{4,0},{5,1},{6,2},{7,3},{8,12},{9,13},{10,... | collective-permute-start | bytes 294920 | tf_op jit(solution)/shard_map/ppermute | solution.py:24
  76.8 0.6 collective-permute-start.41
  77.4 1.6 %collective-permute-start.40 = (bf16[3,64,256]{2,1,0:T(8,128)(2,1)S(1)}, bf16[3,64,256]{2,1,0:T(8,128)(2,1)S(1)}, u32[]{:S(2)}, u32[]{:S(2)}) collective-permute-start(bf16[3,64,256]{2,1,0:T(8,128)(2,1)S(1)} %collective-permute-done.37.refs_6_), channel_id=1, source_target_pairs={{0,2},{1,3},{2,0},{3,1},{4,6},{5,7},{6,4},{7,5},{8,10},{9,11},{10,... | collective-permute-start | bytes 294920 | tf_op jit(solution)/shard_map/ppermute | solution.py:24
  79.0 0.4 collective-permute-done.43.refs_13_
  79.4 1.9 %collective-permute-start.46 = (bf16[3,64,256]{2,1,0:T(8,128)(2,1)S(1)}, bf16[3,64,256]{2,1,0:T(8,128)(2,1)S(1)}, u32[]{:S(2)}, u32[]{:S(2)}) collective-permute-start(bf16[3,64,256]{2,1,0:T(8,128)(2,1)S(1)} %collective-permute-done.45.refs_14_), channel_id=1, source_target_pairs={{0,2},{1,3},{2,0},{3,1},{4,6},{5,7},{6,4},{7,5},{8,10},{9,11},{10,... | collective-permute-start | bytes 294920 | tf_op jit(solution)/shard_map/ppermute | solution.py:24
  81.5 0.6 collective-permute-done.40.refs_7_
  82.0 2.0 %collective-permute-done.46.refs_15_ = bf16[3,64,256]{2,1,0:T(8,128)(2,1)S(1)} collective-permute-done((bf16[3,64,256]{2,1,0:T(8,128)(2,1)S(1)}, bf16[3,64,256]{2,1,0:T(8,128)(2,1)S(1)}, u32[]{:S(2)}, u32[]{:S(2)}) %collective-permute-start.46) | collective-permute-done | bytes 98336 | tf_op jit(solution)/shard_map/ppermute | solution.py:24
  84.1 0.8 other_outputs.1
  84.9 0.5 collective-permute-start.48
  85.4 0.7 own_outputs.1
  86.5 0.8 slice_bitcast_fusion
  87.4 0.8 select_bitcast_fusion
  (68 shorter events, 2.7 us)
Async XLA Ops:
  0.6 28.1 %copy-start.1 = (bf16[1,256,1024]{2,1,0:T(8,128)(2,1)S(1)}, bf16[1,256,1024]{2,1,0:T(8,128)(2,1)}, u32[]{:S(2)}) copy-start(bf16[1,256,1024]{2,1,0:T(8,128)(2,1)} %param.12) | copy-start | bytes 1572868
  0.6 28.1 %copy-start.2 = (bf16[1,256,1024]{2,1,0:T(8,128)(2,1)S(1)}, bf16[1,256,1024]{2,1,0:T(8,128)(2,1)}, u32[]{:S(2)}) copy-start(bf16[1,256,1024]{2,1,0:T(8,128)(2,1)} %param.13) | copy-start | bytes 1572868
  0.7 3.8 %collective-permute-start.1 = (bf16[256,1024]{1,0:T(8,128)(2,1)}, bf16[256,1024]{1,0:T(8,128)(2,1)S(1)}, u32[]{:S(2)}, u32[]{:S(2)}) collective-permute-start(bf16[256,1024]{1,0:T(8,128)(2,1)} %bitcast.80), channel_id=1, source_target_pairs={{0,1},{1,0},{2,3},{3,2},{4,5},{5,4},{6,7},{7,6},{8,9},{9,8},{10,11... | collective-permute-start | bytes 1572872 | tf_op jit(solution)/shard_map/ppermute | solution.py:24
  1.2 3.3 %collective-permute-start.2 = (bf16[256,1024]{1,0:T(8,128)(2,1)}, bf16[256,1024]{1,0:T(8,128)(2,1)S(1)}, u32[]{:S(2)}, u32[]{:S(2)}) collective-permute-start(bf16[256,1024]{1,0:T(8,128)(2,1)} %bitcast.83), channel_id=1, source_target_pairs={{0,1},{1,0},{2,3},{3,2},{4,5},{5,4},{6,7},{7,6},{8,9},{9,8},{10,11... | collective-permute-start | bytes 1572872 | tf_op jit(solution)/shard_map/ppermute | solution.py:24
  1.2 3.2 %collective-permute-start.3 = (bf16[256,1024]{1,0:T(8,128)(2,1)}, bf16[256,1024]{1,0:T(8,128)(2,1)S(1)}, u32[]{:S(2)}, u32[]{:S(2)}) collective-permute-start(bf16[256,1024]{1,0:T(8,128)(2,1)} %bitcast.77), channel_id=1, source_target_pairs={{0,1},{1,0},{2,3},{3,2},{4,5},{5,4},{6,7},{7,6},{8,9},{9,8},{10,11... | collective-permute-start | bytes 1572872 | tf_op jit(solution)/shard_map/ppermute | solution.py:24
  1.7 2.6 %collective-permute-start.4 = (s32[1]{0:T(128)}, s32[1]{0:T(128)}, u32[]{:S(2)}, u32[]{:S(2)}) collective-permute-start(s32[1]{0:T(128)} %param.17), channel_id=1, source_target_pairs={{0,1},{1,0},{2,3},{3,2},{4,5},{5,4},{6,7},{7,6},{8,9},{9,8},{10,11... | collective-permute-start | bytes 20 | tf_op jit(solution)/shard_map/ppermute | solution.py:24
  2.7 1.8 %collective-permute-start = (f32[3,32,256]{2,1,0:T(8,128)S(1)}, f32[3,32,256]{2,1,0:T(8,128)S(1)}, u32[]{:S(2)}, u32[]{:S(2)}) collective-permute-start(f32[3,32,256]{2,1,0:T(8,128)S(1)} %get-tuple-element.107), channel_id=1, source_target_pairs={{0,1},{1,0},{2,3},{3,2},{4,5},{5,4},{6,7},{7,6},{8,9},{9,8},{10,11... | collective-permute-start | bytes 294920 | tf_op jit(solution)/shard_map/ppermute | solution.py:24
  4.3 27.4 %copy-start.3 = (s32[32]{0:T(128)S(1)}, s32[32]{0:T(128)}, u32[]{:S(2)}) copy-start(s32[32]{0:T(128)} %param.15) | copy-start | bytes 388
  4.3 27.4 %copy-start.4 = (s32[32]{0:T(128)S(1)}, s32[32]{0:T(128)}, u32[]{:S(2)}) copy-start(s32[32]{0:T(128)} %param.16) | copy-start | bytes 388
  4.3 8.9 %collective-permute-start.5 = (f32[2,3,32,256]{3,2,1,0:T(8,128)S(1)}, f32[2,3,32,256]{3,2,1,0:T(8,128)S(1)}, u32[]{:S(2)}, u32[]{:S(2)}) collective-permute-start(f32[2,3,32,256]{3,2,1,0:T(8,128)S(1)} %pad_maximum_fusion.1), channel_id=1, source_target_pairs={{0,1},{1,0},{2,3},{3,2},{4,5},{5,4},{6,7},{7,6},{8,9},{9,8},{10,11... | collective-permute-start | bytes 589832 | tf_op jit(solution)/shard_map/ppermute | solution.py:24
  4.5 9.3 %collective-permute-start.12 = (bf16[3,64,256]{2,1,0:T(8,128)(2,1)S(1)}, bf16[3,64,256]{2,1,0:T(8,128)(2,1)S(1)}, u32[]{:S(2)}, u32[]{:S(2)}) collective-permute-start(bf16[3,64,256]{2,1,0:T(8,128)(2,1)S(1)} %fusion.18.refs_0_), channel_id=1, source_target_pairs={{0,16},{1,17},{2,18},{3,19},{4,20},{5,21},{6,22},{7,23},{8,24},{9,... | collective-permute-start | bytes 294920 | tf_op jit(solution)/shard_map/ppermute | solution.py:24
  8.6 5.9 %collective-permute-start.9 = (bf16[3,64,256]{2,1,0:T(8,128)(2,1)S(1)}, bf16[3,64,256]{2,1,0:T(8,128)(2,1)S(1)}, u32[]{:S(2)}, u32[]{:S(2)}) collective-permute-start(bf16[3,64,256]{2,1,0:T(8,128)(2,1)S(1)} %fusion.18.refs_0_), channel_id=1, source_target_pairs={{0,8},{1,9},{2,10},{3,11},{4,12},{5,13},{6,14},{7,15},{8,0},{9,1},... | collective-permute-start | bytes 294920 | tf_op jit(solution)/shard_map/ppermute | solution.py:24
  10.2 5.8 %collective-permute-start.6 = (bf16[3,64,256]{2,1,0:T(8,128)(2,1)S(1)}, bf16[3,64,256]{2,1,0:T(8,128)(2,1)S(1)}, u32[]{:S(2)}, u32[]{:S(2)}) collective-permute-start(bf16[3,64,256]{2,1,0:T(8,128)(2,1)S(1)} %fusion.18.refs_0_), channel_id=1, source_target_pairs={{0,2},{1,3},{2,0},{3,1},{4,6},{5,7},{6,4},{7,5},{8,10},{9,11},{10,... | collective-permute-start | bytes 294920 | tf_op jit(solution)/shard_map/ppermute | solution.py:24
  11.7 5.8 %collective-permute-start.7 = (bf16[3,64,256]{2,1,0:T(8,128)(2,1)S(1)}, bf16[3,64,256]{2,1,0:T(8,128)(2,1)S(1)}, u32[]{:S(2)}, u32[]{:S(2)}) collective-permute-start(bf16[3,64,256]{2,1,0:T(8,128)(2,1)S(1)} %fusion.18.refs_0_), channel_id=1, source_target_pairs={{0,4},{1,5},{2,6},{3,7},{4,0},{5,1},{6,2},{7,3},{8,12},{9,13},{10,... | collective-permute-start | bytes 294920 | tf_op jit(solution)/shard_map/ppermute | solution.py:24
  13.9 4.6 %collective-permute-start.16 = (bf16[3,64,256]{2,1,0:T(8,128)(2,1)S(1)}, bf16[3,64,256]{2,1,0:T(8,128)(2,1)S(1)}, u32[]{:S(2)}, u32[]{:S(2)}) collective-permute-start(bf16[3,64,256]{2,1,0:T(8,128)(2,1)S(1)} %collective-permute-done.12.refs_8_), channel_id=1, source_target_pairs={{0,8},{1,9},{2,10},{3,11},{4,12},{5,13},{6,14},{7,15},{8,0},{9,1},... | collective-permute-start | bytes 294920 | tf_op jit(solution)/shard_map/ppermute | solution.py:24
  14.5 4.6 %collective-permute-start.10 = (bf16[3,64,256]{2,1,0:T(8,128)(2,1)S(1)}, bf16[3,64,256]{2,1,0:T(8,128)(2,1)S(1)}, u32[]{:S(2)}, u32[]{:S(2)}) collective-permute-start(bf16[3,64,256]{2,1,0:T(8,128)(2,1)S(1)} %collective-permute-done.9.refs_4_), channel_id=1, source_target_pairs={{0,2},{1,3},{2,0},{3,1},{4,6},{5,7},{6,4},{7,5},{8,10},{9,11},{10,... | collective-permute-start | bytes 294920 | tf_op jit(solution)/shard_map/ppermute | solution.py:24
  16.0 7.4 %collective-permute-start.11 = (bf16[3,64,256]{2,1,0:T(8,128)(2,1)S(1)}, bf16[3,64,256]{2,1,0:T(8,128)(2,1)S(1)}, u32[]{:S(2)}, u32[]{:S(2)}) collective-permute-start(bf16[3,64,256]{2,1,0:T(8,128)(2,1)S(1)} %collective-permute-done.9.refs_4_), channel_id=1, source_target_pairs={{0,4},{1,5},{2,6},{3,7},{4,0},{5,1},{6,2},{7,3},{8,12},{9,13},{10,... | collective-permute-start | bytes 294920 | tf_op jit(solution)/shard_map/ppermute | solution.py:24
  17.5 7.5 %collective-permute-start.13 = (bf16[3,64,256]{2,1,0:T(8,128)(2,1)S(1)}, bf16[3,64,256]{2,1,0:T(8,128)(2,1)S(1)}, u32[]{:S(2)}, u32[]{:S(2)}) collective-permute-start(bf16[3,64,256]{2,1,0:T(8,128)(2,1)S(1)} %collective-permute-done.12.refs_8_), channel_id=1, source_target_pairs={{0,2},{1,3},{2,0},{3,1},{4,6},{5,7},{6,4},{7,5},{8,10},{9,11},{10,... | collective-permute-start | bytes 294920 | tf_op jit(solution)/shard_map/ppermute | solution.py:24
  19.1 6.4 %collective-permute-start.17 = (bf16[3,64,256]{2,1,0:T(8,128)(2,1)S(1)}, bf16[3,64,256]{2,1,0:T(8,128)(2,1)S(1)}, u32[]{:S(2)}, u32[]{:S(2)}) collective-permute-start(bf16[3,64,256]{2,1,0:T(8,128)(2,1)S(1)} %collective-permute-done.16.refs_12_), channel_id=1, source_target_pairs={{0,2},{1,3},{2,0},{3,1},{4,6},{5,7},{6,4},{7,5},{8,10},{9,11},{10,... | collective-permute-start | bytes 294920 | tf_op jit(solution)/shard_map/ppermute | solution.py:24
  21.4 5.0 %collective-permute-start.19 = (bf16[3,64,256]{2,1,0:T(8,128)(2,1)S(1)}, bf16[3,64,256]{2,1,0:T(8,128)(2,1)S(1)}, u32[]{:S(2)}, u32[]{:S(2)}) collective-permute-start(bf16[3,64,256]{2,1,0:T(8,128)(2,1)S(1)} %collective-permute-done.16.refs_12_), channel_id=1, source_target_pairs={{0,4},{1,5},{2,6},{3,7},{4,0},{5,1},{6,2},{7,3},{8,12},{9,13},{10,... | collective-permute-start | bytes 294920 | tf_op jit(solution)/shard_map/ppermute | solution.py:24
  23.0 6.4 %collective-permute-start.8 = (bf16[3,64,256]{2,1,0:T(8,128)(2,1)S(1)}, bf16[3,64,256]{2,1,0:T(8,128)(2,1)S(1)}, u32[]{:S(2)}, u32[]{:S(2)}) collective-permute-start(bf16[3,64,256]{2,1,0:T(8,128)(2,1)S(1)} %collective-permute-done.6.refs_1_), channel_id=1, source_target_pairs={{0,4},{1,5},{2,6},{3,7},{4,0},{5,1},{6,2},{7,3},{8,12},{9,13},{10,... | collective-permute-start | bytes 294920 | tf_op jit(solution)/shard_map/ppermute | solution.py:24
  23.4 6.0 %collective-permute-start.15 = (bf16[3,64,256]{2,1,0:T(8,128)(2,1)S(1)}, bf16[3,64,256]{2,1,0:T(8,128)(2,1)S(1)}, u32[]{:S(2)}, u32[]{:S(2)}) collective-permute-start(bf16[3,64,256]{2,1,0:T(8,128)(2,1)S(1)} %collective-permute-done.12.refs_8_), channel_id=1, source_target_pairs={{0,4},{1,5},{2,6},{3,7},{4,0},{5,1},{6,2},{7,3},{8,12},{9,13},{10,... | collective-permute-start | bytes 294920 | tf_op jit(solution)/shard_map/ppermute | solution.py:24
  25.0 4.6 %collective-permute-start.14 = (bf16[3,64,256]{2,1,0:T(8,128)(2,1)S(1)}, bf16[3,64,256]{2,1,0:T(8,128)(2,1)S(1)}, u32[]{:S(2)}, u32[]{:S(2)}) collective-permute-start(bf16[3,64,256]{2,1,0:T(8,128)(2,1)S(1)} %collective-permute-done.11.refs_6_), channel_id=1, source_target_pairs={{0,2},{1,3},{2,0},{3,1},{4,6},{5,7},{6,4},{7,5},{8,10},{9,11},{10,... | collective-permute-start | bytes 294920 | tf_op jit(solution)/shard_map/ppermute | solution.py:24
  26.4 4.6 %collective-permute-start.20 = (bf16[3,64,256]{2,1,0:T(8,128)(2,1)S(1)}, bf16[3,64,256]{2,1,0:T(8,128)(2,1)S(1)}, u32[]{:S(2)}, u32[]{:S(2)}) collective-permute-start(bf16[3,64,256]{2,1,0:T(8,128)(2,1)S(1)} %collective-permute-done.19.refs_14_), channel_id=1, source_target_pairs={{0,2},{1,3},{2,0},{3,1},{4,6},{5,7},{6,4},{7,5},{8,10},{9,11},{10,... | collective-permute-start | bytes 294920 | tf_op jit(solution)/shard_map/ppermute | solution.py:24
  27.1 4.6 %collective-permute-start.18 = (bf16[3,64,256]{2,1,0:T(8,128)(2,1)S(1)}, bf16[3,64,256]{2,1,0:T(8,128)(2,1)S(1)}, u32[]{:S(2)}, u32[]{:S(2)}) collective-permute-start(bf16[3,64,256]{2,1,0:T(8,128)(2,1)S(1)} %collective-permute-done.13.refs_9_), channel_id=1, source_target_pairs={{0,4},{1,5},{2,6},{3,7},{4,0},{5,1},{6,2},{7,3},{8,12},{9,13},{10,... | collective-permute-start | bytes 294920 | tf_op jit(solution)/shard_map/ppermute | solution.py:24
  34.9 6.1 %collective-permute-start.21 = (bf16[2,3,64,256]{3,2,1,0:T(8,128)(2,1)S(1)}, bf16[2,3,64,256]{3,2,1,0:T(8,128)(2,1)S(1)}, u32[]{:S(2)}, u32[]{:S(2)}) collective-permute-start(bf16[2,3,64,256]{3,2,1,0:T(8,128)(2,1)S(1)} %get-tuple-element.65), channel_id=1, source_target_pairs={{0,2},{1,3},{2,0},{3,1},{4,6},{5,7},{6,4},{7,5},{8,10},{9,11},{10,... | collective-permute-start | bytes 589832 | tf_op jit(solution)/shard_map/ppermute | solution.py:24
  36.2 7.8 %collective-permute-start.24 = (bf16[2,3,64,256]{3,2,1,0:T(8,128)(2,1)S(1)}, bf16[2,3,64,256]{3,2,1,0:T(8,128)(2,1)S(1)}, u32[]{:S(2)}, u32[]{:S(2)}) collective-permute-start(bf16[2,3,64,256]{3,2,1,0:T(8,128)(2,1)S(1)} %get-tuple-element.69), channel_id=1, source_target_pairs={{0,4},{1,5},{2,6},{3,7},{4,0},{5,1},{6,2},{7,3},{8,12},{9,13},{10,... | collective-permute-start | bytes 589832 | tf_op jit(solution)/shard_map/ppermute | solution.py:24
  37.9 6.9 %collective-permute-start.26 = (bf16[2,3,64,256]{3,2,1,0:T(8,128)(2,1)S(1)}, bf16[2,3,64,256]{3,2,1,0:T(8,128)(2,1)S(1)}, u32[]{:S(2)}, u32[]{:S(2)}) collective-permute-start(bf16[2,3,64,256]{3,2,1,0:T(8,128)(2,1)S(1)} %get-tuple-element.71), channel_id=1, source_target_pairs={{0,2},{1,3},{2,0},{3,1},{4,6},{5,7},{6,4},{7,5},{8,10},{9,11},{10,... | collective-permute-start | bytes 589832 | tf_op jit(solution)/shard_map/ppermute | solution.py:24
  41.0 11.7 %collective-permute-start.28 = (bf16[3,64,256]{2,1,0:T(8,128)(2,1)S(1)}, bf16[3,64,256]{2,1,0:T(8,128)(2,1)S(1)}, u32[]{:S(2)}, u32[]{:S(2)}) collective-permute-start(bf16[3,64,256]{2,1,0:T(8,128)(2,1)S(1)} %fusion.7), channel_id=1, source_target_pairs={{0,4},{1,5},{2,6},{3,7},{4,0},{5,1},{6,2},{7,3},{8,12},{9,13},{10,... | collective-permute-start | bytes 294920 | tf_op jit(solution)/shard_map/ppermute | solution.py:24
  41.8 10.9 %collective-permute-start.22 = (bf16[2,3,64,256]{3,2,1,0:T(8,128)(2,1)S(1)}, bf16[2,3,64,256]{3,2,1,0:T(8,128)(2,1)S(1)}, u32[]{:S(2)}, u32[]{:S(2)}) collective-permute-start(bf16[2,3,64,256]{3,2,1,0:T(8,128)(2,1)S(1)} %get-tuple-element.66), channel_id=1, source_target_pairs={{0,4},{1,5},{2,6},{3,7},{4,0},{5,1},{6,2},{7,3},{8,12},{9,13},{10,... | collective-permute-start | bytes 589832 | tf_op jit(solution)/shard_map/ppermute | solution.py:24
  44.0 4.7 %collective-permute-start.25 = (bf16[3,64,256]{2,1,0:T(8,128)(2,1)S(1)}, bf16[3,64,256]{2,1,0:T(8,128)(2,1)S(1)}, u32[]{:S(2)}, u32[]{:S(2)}) collective-permute-start(bf16[3,64,256]{2,1,0:T(8,128)(2,1)S(1)} %fusion.10), channel_id=1, source_target_pairs={{0,2},{1,3},{2,0},{3,1},{4,6},{5,7},{6,4},{7,5},{8,10},{9,11},{10,... | collective-permute-start | bytes 294920 | tf_op jit(solution)/shard_map/ppermute | solution.py:24
  44.8 6.9 %collective-permute-start.30 = (bf16[3,64,256]{2,1,0:T(8,128)(2,1)S(1)}, bf16[3,64,256]{2,1,0:T(8,128)(2,1)S(1)}, u32[]{:S(2)}, u32[]{:S(2)}) collective-permute-start(bf16[3,64,256]{2,1,0:T(8,128)(2,1)S(1)} %fusion.4), channel_id=1, source_target_pairs={{0,4},{1,5},{2,6},{3,7},{4,0},{5,1},{6,2},{7,3},{8,12},{9,13},{10,... | collective-permute-start | bytes 294920 | tf_op jit(solution)/shard_map/ppermute | solution.py:24
  48.8 8.5 %collective-permute-start.27 = (bf16[3,64,256]{2,1,0:T(8,128)(2,1)S(1)}, bf16[3,64,256]{2,1,0:T(8,128)(2,1)S(1)}, u32[]{:S(2)}, u32[]{:S(2)}) collective-permute-start(bf16[3,64,256]{2,1,0:T(8,128)(2,1)S(1)} %fusion.12), channel_id=1, source_target_pairs={{0,16},{1,17},{2,18},{3,19},{4,20},{5,21},{6,22},{7,23},{8,24},{9,... | collective-permute-start | bytes 294920 | tf_op jit(solution)/shard_map/ppermute | solution.py:24
  51.7 5.5 %collective-permute-start.31 = (bf16[3,64,256]{2,1,0:T(8,128)(2,1)S(1)}, bf16[3,64,256]{2,1,0:T(8,128)(2,1)S(1)}, u32[]{:S(2)}, u32[]{:S(2)}) collective-permute-start(bf16[3,64,256]{2,1,0:T(8,128)(2,1)S(1)} %fusion.6), channel_id=1, source_target_pairs={{0,8},{1,9},{2,10},{3,11},{4,12},{5,13},{6,14},{7,15},{8,0},{9,1},... | collective-permute-start | bytes 294920 | tf_op jit(solution)/shard_map/ppermute | solution.py:24
  52.7 7.5 %collective-permute-start.29 = (bf16[3,64,256]{2,1,0:T(8,128)(2,1)S(1)}, bf16[3,64,256]{2,1,0:T(8,128)(2,1)S(1)}, u32[]{:S(2)}, u32[]{:S(2)}) collective-permute-start(bf16[3,64,256]{2,1,0:T(8,128)(2,1)S(1)} %fusion.9), channel_id=1, source_target_pairs={{0,24},{1,25},{2,26},{3,27},{4,28},{5,29},{6,30},{7,31},{8,16},{9,... | collective-permute-start | bytes 294920 | tf_op jit(solution)/shard_map/ppermute | solution.py:24
  54.7 5.6 %collective-permute-start.23 = (bf16[3,64,256]{2,1,0:T(8,128)(2,1)S(1)}, bf16[3,64,256]{2,1,0:T(8,128)(2,1)S(1)}, u32[]{:S(2)}, u32[]{:S(2)}) collective-permute-start(bf16[3,64,256]{2,1,0:T(8,128)(2,1)S(1)} %fusion.13), channel_id=1, source_target_pairs={{0,2},{1,3},{2,0},{3,1},{4,6},{5,7},{6,4},{7,5},{8,10},{9,11},{10,... | collective-permute-start | bytes 294920 | tf_op jit(solution)/shard_map/ppermute | solution.py:24
  60.6 23.5 %copy-start = (bf16[1,256,1024]{2,1,0:T(8,128)(2,1)S(1)}, bf16[1,256,1024]{2,1,0:T(8,128)(2,1)}, u32[]{:S(2)}) copy-start(bf16[1,256,1024]{2,1,0:T(8,128)(2,1)} %param.14) | copy-start | bytes 1572868
  60.6 6.7 %collective-permute-start.38 = (bf16[3,64,256]{2,1,0:T(8,128)(2,1)S(1)}, bf16[3,64,256]{2,1,0:T(8,128)(2,1)S(1)}, u32[]{:S(2)}, u32[]{:S(2)}) collective-permute-start(bf16[3,64,256]{2,1,0:T(8,128)(2,1)S(1)} %get-tuple-element.92.refs_0_), channel_id=1, source_target_pairs={{0,16},{1,17},{2,18},{3,19},{4,20},{5,21},{6,22},{7,23},{8,24},{9,... | collective-permute-start | bytes 294920 | tf_op jit(solution)/shard_map/ppermute | solution.py:24
  62.1 5.2 %collective-permute-start.35 = (bf16[3,64,256]{2,1,0:T(8,128)(2,1)S(1)}, bf16[3,64,256]{2,1,0:T(8,128)(2,1)S(1)}, u32[]{:S(2)}, u32[]{:S(2)}) collective-permute-start(bf16[3,64,256]{2,1,0:T(8,128)(2,1)S(1)} %get-tuple-element.92.refs_0_), channel_id=1, source_target_pairs={{0,8},{1,9},{2,10},{3,11},{4,12},{5,13},{6,14},{7,15},{8,0},{9,1},... | collective-permute-start | bytes 294920 | tf_op jit(solution)/shard_map/ppermute | solution.py:24
  63.1 6.5 %collective-permute-start.33 = (bf16[3,64,256]{2,1,0:T(8,128)(2,1)S(1)}, bf16[3,64,256]{2,1,0:T(8,128)(2,1)S(1)}, u32[]{:S(2)}, u32[]{:S(2)}) collective-permute-start(bf16[3,64,256]{2,1,0:T(8,128)(2,1)S(1)} %get-tuple-element.92.refs_0_), channel_id=1, source_target_pairs={{0,4},{1,5},{2,6},{3,7},{4,0},{5,1},{6,2},{7,3},{8,12},{9,13},{10,... | collective-permute-start | bytes 294920 | tf_op jit(solution)/shard_map/ppermute | solution.py:24
  65.9 5.2 %collective-permute-start.32 = (bf16[3,64,256]{2,1,0:T(8,128)(2,1)S(1)}, bf16[3,64,256]{2,1,0:T(8,128)(2,1)S(1)}, u32[]{:S(2)}, u32[]{:S(2)}) collective-permute-start(bf16[3,64,256]{2,1,0:T(8,128)(2,1)S(1)} %get-tuple-element.92.refs_0_), channel_id=1, source_target_pairs={{0,2},{1,3},{2,0},{3,1},{4,6},{5,7},{6,4},{7,5},{8,10},{9,11},{10,... | collective-permute-start | bytes 294920 | tf_op jit(solution)/shard_map/ppermute | solution.py:24
  67.2 5.4 %collective-permute-start.42 = (bf16[3,64,256]{2,1,0:T(8,128)(2,1)S(1)}, bf16[3,64,256]{2,1,0:T(8,128)(2,1)S(1)}, u32[]{:S(2)}, u32[]{:S(2)}) collective-permute-start(bf16[3,64,256]{2,1,0:T(8,128)(2,1)S(1)} %collective-permute-done.38.refs_8_), channel_id=1, source_target_pairs={{0,8},{1,9},{2,10},{3,11},{4,12},{5,13},{6,14},{7,15},{8,0},{9,1},... | collective-permute-start | bytes 294920 | tf_op jit(solution)/shard_map/ppermute | solution.py:24
  67.3 5.3 %collective-permute-start.36 = (bf16[3,64,256]{2,1,0:T(8,128)(2,1)S(1)}, bf16[3,64,256]{2,1,0:T(8,128)(2,1)S(1)}, u32[]{:S(2)}, u32[]{:S(2)}) collective-permute-start(bf16[3,64,256]{2,1,0:T(8,128)(2,1)S(1)} %collective-permute-done.35.refs_4_), channel_id=1, source_target_pairs={{0,2},{1,3},{2,0},{3,1},{4,6},{5,7},{6,4},{7,5},{8,10},{9,11},{10,... | collective-permute-start | bytes 294920 | tf_op jit(solution)/shard_map/ppermute | solution.py:24
  71.1 5.8 %collective-permute-start.37 = (bf16[3,64,256]{2,1,0:T(8,128)(2,1)S(1)}, bf16[3,64,256]{2,1,0:T(8,128)(2,1)S(1)}, u32[]{:S(2)}, u32[]{:S(2)}) collective-permute-start(bf16[3,64,256]{2,1,0:T(8,128)(2,1)S(1)} %collective-permute-done.35.refs_4_), channel_id=1, source_target_pairs={{0,4},{1,5},{2,6},{3,7},{4,0},{5,1},{6,2},{7,3},{8,12},{9,13},{10,... | collective-permute-start | bytes 294920 | tf_op jit(solution)/shard_map/ppermute | solution.py:24
  71.7 5.8 %collective-permute-start.39 = (bf16[3,64,256]{2,1,0:T(8,128)(2,1)S(1)}, bf16[3,64,256]{2,1,0:T(8,128)(2,1)S(1)}, u32[]{:S(2)}, u32[]{:S(2)}) collective-permute-start(bf16[3,64,256]{2,1,0:T(8,128)(2,1)S(1)} %collective-permute-done.38.refs_8_), channel_id=1, source_target_pairs={{0,2},{1,3},{2,0},{3,1},{4,6},{5,7},{6,4},{7,5},{8,10},{9,11},{10,... | collective-permute-start | bytes 294920 | tf_op jit(solution)/shard_map/ppermute | solution.py:24
  72.6 6.8 %collective-permute-start.45 = (bf16[3,64,256]{2,1,0:T(8,128)(2,1)S(1)}, bf16[3,64,256]{2,1,0:T(8,128)(2,1)S(1)}, u32[]{:S(2)}, u32[]{:S(2)}) collective-permute-start(bf16[3,64,256]{2,1,0:T(8,128)(2,1)S(1)} %collective-permute-done.42.refs_12_), channel_id=1, source_target_pairs={{0,4},{1,5},{2,6},{3,7},{4,0},{5,1},{6,2},{7,3},{8,12},{9,13},{10,... | collective-permute-start | bytes 294920 | tf_op jit(solution)/shard_map/ppermute | solution.py:24
  74.8 4.6 %collective-permute-start.43 = (bf16[3,64,256]{2,1,0:T(8,128)(2,1)S(1)}, bf16[3,64,256]{2,1,0:T(8,128)(2,1)S(1)}, u32[]{:S(2)}, u32[]{:S(2)}) collective-permute-start(bf16[3,64,256]{2,1,0:T(8,128)(2,1)S(1)} %collective-permute-done.42.refs_12_), channel_id=1, source_target_pairs={{0,2},{1,3},{2,0},{3,1},{4,6},{5,7},{6,4},{7,5},{8,10},{9,11},{10,... | collective-permute-start | bytes 294920 | tf_op jit(solution)/shard_map/ppermute | solution.py:24
  75.3 6.1 %collective-permute-start.34 = (bf16[3,64,256]{2,1,0:T(8,128)(2,1)S(1)}, bf16[3,64,256]{2,1,0:T(8,128)(2,1)S(1)}, u32[]{:S(2)}, u32[]{:S(2)}) collective-permute-start(bf16[3,64,256]{2,1,0:T(8,128)(2,1)S(1)} %collective-permute-done.32.refs_1_), channel_id=1, source_target_pairs={{0,4},{1,5},{2,6},{3,7},{4,0},{5,1},{6,2},{7,3},{8,12},{9,13},{10,... | collective-permute-start | bytes 294920 | tf_op jit(solution)/shard_map/ppermute | solution.py:24
  76.8 4.6 %collective-permute-start.41 = (bf16[3,64,256]{2,1,0:T(8,128)(2,1)S(1)}, bf16[3,64,256]{2,1,0:T(8,128)(2,1)S(1)}, u32[]{:S(2)}, u32[]{:S(2)}) collective-permute-start(bf16[3,64,256]{2,1,0:T(8,128)(2,1)S(1)} %collective-permute-done.38.refs_8_), channel_id=1, source_target_pairs={{0,4},{1,5},{2,6},{3,7},{4,0},{5,1},{6,2},{7,3},{8,12},{9,13},{10,... | collective-permute-start | bytes 294920 | tf_op jit(solution)/shard_map/ppermute | solution.py:24
  77.4 4.6 %collective-permute-start.40 = (bf16[3,64,256]{2,1,0:T(8,128)(2,1)S(1)}, bf16[3,64,256]{2,1,0:T(8,128)(2,1)S(1)}, u32[]{:S(2)}, u32[]{:S(2)}) collective-permute-start(bf16[3,64,256]{2,1,0:T(8,128)(2,1)S(1)} %collective-permute-done.37.refs_6_), channel_id=1, source_target_pairs={{0,2},{1,3},{2,0},{3,1},{4,6},{5,7},{6,4},{7,5},{8,10},{9,11},{10,... | collective-permute-start | bytes 294920 | tf_op jit(solution)/shard_map/ppermute | solution.py:24
  79.4 4.6 %collective-permute-start.44 = (bf16[3,64,256]{2,1,0:T(8,128)(2,1)S(1)}, bf16[3,64,256]{2,1,0:T(8,128)(2,1)S(1)}, u32[]{:S(2)}, u32[]{:S(2)}) collective-permute-start(bf16[3,64,256]{2,1,0:T(8,128)(2,1)S(1)} %collective-permute-done.39.refs_9_), channel_id=1, source_target_pairs={{0,4},{1,5},{2,6},{3,7},{4,0},{5,1},{6,2},{7,3},{8,12},{9,13},{10,... | collective-permute-start | bytes 294920 | tf_op jit(solution)/shard_map/ppermute | solution.py:24
  79.4 4.6 %collective-permute-start.46 = (bf16[3,64,256]{2,1,0:T(8,128)(2,1)S(1)}, bf16[3,64,256]{2,1,0:T(8,128)(2,1)S(1)}, u32[]{:S(2)}, u32[]{:S(2)}) collective-permute-start(bf16[3,64,256]{2,1,0:T(8,128)(2,1)S(1)} %collective-permute-done.45.refs_14_), channel_id=1, source_target_pairs={{0,2},{1,3},{2,0},{3,1},{4,6},{5,7},{6,4},{7,5},{8,10},{9,11},{10,... | collective-permute-start | bytes 294920 | tf_op jit(solution)/shard_map/ppermute | solution.py:24
  84.8 1.6 %collective-permute-start.47 = (f32[3,3,32,256]{3,2,1,0:T(8,128)S(1)}, f32[3,3,32,256]{3,2,1,0:T(8,128)S(1)}, u32[]{:S(2)}, u32[]{:S(2)}) collective-permute-start(f32[3,3,32,256]{3,2,1,0:T(8,128)S(1)} %get-tuple-element.89), channel_id=1, source_target_pairs={{0,1},{1,0},{2,3},{3,2},{4,5},{5,4},{6,7},{7,6},{8,9},{9,8},{10,11... | collective-permute-start | bytes 884744 | tf_op jit(solution)/shard_map/ppermute | solution.py:24
  84.9 2.5 %collective-permute-start.48 = (bf16[256,1024]{1,0:T(8,128)(2,1)S(1)}, bf16[256,1024]{1,0:T(8,128)(2,1)S(1)}, u32[]{:S(2)}, u32[]{:S(2)}) collective-permute-start(bf16[256,1024]{1,0:T(8,128)(2,1)S(1)} %get-tuple-element.88), channel_id=1, source_target_pairs={{0,1},{1,0},{2,3},{3,2},{4,5},{5,4},{6,7},{7,6},{8,9},{9,8},{10,11... | collective-permute-start | bytes 1572872 | tf_op jit(solution)/shard_map/ppermute | solution.py:24
